TPU v7x, 32 devices: a whole 2x2x4 slice. The times are simulated.
32 devices in a mesh: ctx: 4 (over z), tp: 4 (over y, x), fsdp: 2 (over core).
Axes of the slice: x: 2, y: 2, z: 4, core: 2. Of those that a mesh axis runs over, the one named last changes fastest.
Arguments:
- tokens: bfloat16 [2, 4096, 2048], P('fsdp', 'ctx'), may hold values from -6 to 6
- query_weight: bfloat16 [2048, 2048], P('fsdp', 'tp'), may hold values from -0.125 to 0.125
- key_weight: bfloat16 [2048, 2048], P('fsdp', 'tp'), may hold values from -0.125 to 0.125
- value_weight: bfloat16 [2048, 2048], P('fsdp', 'tp'), may hold values from -0.125 to 0.125
- gate_weight: bfloat16 [2048, 2048], P('fsdp', 'tp'), may hold values from -0.125 to 0.125
- out_weight: bfloat16 [2048, 2048], P('tp', 'fsdp'), may hold values from -0.125 to 0.125
- log_decay: float32 [2, 4096, 8], P('fsdp', 'ctx', 'tp'), may hold values from -1 to 0
Outputs:
- mixed: bfloat16 [2, 4096, 2048], P('fsdp', 'ctx', 'tp')
All inputs are finite; a program needn't handle non-finite values.
Results may differ from a plain program's by a relative error of at most 0.013.
Values may be sent and summed in bfloat16 or wider, within the bound.
No kernel may reach another device: no remote copies, remote signals or barrier semaphores. Data moves between devices by JAX's collectives and lax.ppermute only.
A program may use at most 128 MiB of HBM per device.

v0:
```python
import jax
import jax.numpy as jnp
from jax import lax
from jax.sharding import PartitionSpec as P

DH = 256
BLOCK = 512


def entering(value, axis, join, neutral):
    count, mine = (lax.axis_size(axis), lax.axis_index(axis))
    pieces = jax.tree.map(lambda part: lax.all_gather(part, axis), value)
    running = jax.tree.map(
        lambda part, zero: jnp.full_like(part, 0) + jnp.asarray(zero, part.dtype), value, neutral
    )

    def hop(position, running):
        longer = join(running, jax.tree.map(lambda part: part[position], pieces))
        return jax.tree.map(lambda new, old: jnp.where(position < mine, new, old), longer, running)

    return lax.fori_loop(0, count - 1, hop, running)


def rotate(values, positions):
    half_dim = values.shape[-1] // 2
    index_row = jnp.arange(half_dim).astype(jnp.float32)
    frequency = jnp.power(jnp.float32(10000.0), -index_row / half_dim)
    angles = positions[:, None] * frequency[None, :]
    cosine = jnp.concatenate([jnp.cos(angles), jnp.cos(angles)], axis=-1)[:, None, :]
    sine_part = jnp.concatenate([jnp.sin(angles), jnp.sin(angles)], axis=-1)[:, None, :]
    turned = jnp.concatenate([-values[..., half_dim:], values[..., :half_dim]], axis=-1)
    return values * cosine + turned * sine_part


def group_norm(retained):
    center = retained - jnp.mean(retained, axis=-1, keepdims=True)
    spread = jnp.mean(center * center, axis=-1, keepdims=True)
    return center * lax.rsqrt(spread + 1e-05)


def combine(earlier, later):
    return (earlier[0] + later[0], jnp.exp(later[0])[:, None, None] * earlier[1] + later[1])


def on_device(tokens, query_weight, key_weight, value_weight, gate_weight, out_weight, log_decay):
    token_rows = tokens[0]
    row_count = token_rows.shape[0]
    col_count = query_weight.shape[1]
    head_count = col_count // DH
    block_count = row_count // BLOCK

    def add_rows(shard_rows):
        return jnp.dot(token_rows, shard_rows, preferred_element_type=jnp.float32)

    query_proj = add_rows(lax.all_gather(query_weight, "fsdp", axis=0, tiled=True))
    key_proj = add_rows(lax.all_gather(key_weight, "fsdp", axis=0, tiled=True))
    value_proj = add_rows(lax.all_gather(value_weight, "fsdp", axis=0, tiled=True))
    gate_proj = add_rows(lax.all_gather(gate_weight, "fsdp", axis=0, tiled=True))
    offset = lax.axis_index("ctx") * row_count
    positions = (offset + jnp.arange(row_count)).astype(jnp.float32)
    block_shape = (block_count, BLOCK, head_count, DH)
    queries = (
        rotate(query_proj.reshape(row_count, head_count, DH), positions)
        .astype(jnp.bfloat16)
        .reshape(block_shape)
    )
    keys_block = (
        rotate(key_proj.reshape(row_count, head_count, DH), positions)
        .astype(jnp.bfloat16)
        .reshape(block_shape)
    )
    values_block = value_proj.astype(jnp.bfloat16).reshape(block_shape)
    gate_values = gate_proj.astype(jnp.bfloat16)
    cumulative = jnp.cumsum(log_decay[0].reshape(block_count, BLOCK, head_count), axis=1)
    scores = jnp.einsum("cthd,cshd->chts", queries, keys_block, preferred_element_type=jnp.float32)
    leading = jnp.transpose(cumulative, (0, 2, 1))
    differ = leading[:, :, :, None] - leading[:, :, None, :]
    causal = jnp.arange(BLOCK)[:, None] >= jnp.arange(BLOCK)[None, :]
    weights = jnp.where(causal, jnp.exp(jnp.where(causal, differ, 0.0)), 0.0)
    mixed_weights = (scores * weights).astype(jnp.bfloat16)
    intra_part = jnp.einsum(
        "chts,cshd->cthd", mixed_weights, values_block, preferred_element_type=jnp.float32
    )
    ending = cumulative[:, -1, :]
    weighted = keys_block.astype(jnp.float32) * jnp.exp(ending[:, None, :] - cumulative)[..., None]
    updates = jnp.einsum(
        "cshd,cshe->chde",
        weighted,
        values_block.astype(jnp.float32),
        precision=lax.Precision.HIGHEST,
    )
    device_total = jnp.sum(ending, axis=0)
    device_state = updates[0]
    block_index = 1
    device_state = jnp.exp(ending[block_index])[:, None, None] * device_state + updates[block_index]
    incoming = entering(
        (device_total, device_state),
        "ctx",
        combine,
        (jnp.zeros_like(device_total), jnp.zeros_like(device_state)),
    )
    carried = incoming[1]
    prior_states = []
    for block_index in range(block_count):
        prior_states.append(carried)
        carried = jnp.exp(ending[block_index])[:, None, None] * carried + updates[block_index]
    prior_stack = jnp.stack(prior_states)
    inter_part = jnp.exp(cumulative)[..., None] * jnp.einsum(
        "cthd,chde->cthe", queries.astype(jnp.float32), prior_stack, precision=lax.Precision.HIGHEST
    )
    retained = (intra_part + inter_part).reshape(row_count, head_count, DH)
    normed = group_norm(retained).reshape(row_count, col_count)
    hidden = (jax.nn.silu(gate_values.astype(jnp.float32)) * normed).astype(jnp.bfloat16)
    column_block = lax.all_gather(out_weight, "fsdp", axis=1, tiled=True)
    own_columns = lax.all_to_all(column_block, "tp", split_axis=1, concat_axis=0, tiled=True)
    every_head = lax.all_gather(hidden, "tp", axis=1, tiled=True)
    result = jnp.dot(every_head, own_columns, preferred_element_type=jnp.float32).astype(
        jnp.bfloat16
    )
    return result[None]


def solution(mesh):
    in_specs = (
        P("fsdp", "ctx", None),
        P("fsdp", "tp"),
        P("fsdp", "tp"),
        P("fsdp", "tp"),
        P("fsdp", "tp"),
        P("tp", "fsdp"),
        P("fsdp", "ctx", "tp"),
    )
    out_specs = P("fsdp", "ctx", "tp")
    return jax.shard_map(
        on_device, mesh=mesh, in_specs=in_specs, out_specs=out_specs, check_vma=False
    )
```

profile of v0, /device:TPU:24, one launch (start us, length us, event | category | flops | bytes accessed | tf_op | source)
XLA Modules:
  0.0 211.2 jit_solution(7667421544391426512)
XLA Ops:
  8.9 1.2 reduce-window.6
  11.2 1.9 multiply_cosine_fusion
  13.3 7.5 %all-gather.15.cloned.1.call-done = bf16[2048,512]{1,0:T(8,128)(2,1)} async-done(((bf16[1024,512]{1,0:T(8,128)(2,1)}), bf16[2048,512]{1,0:T(8,128)(2,1)}) %all-gather.15.cloned.1.call-update) | async-done | bytes 2097168 | tf_op jit(solution)/shard_map/all_gather | solution.py:56
  20.8 4.0 %copy.86 = bf16[512,2048]{1,0:T(8,128)(2,1)} copy(bf16[512,2048]{0,1:T(8,128)(2,1)} %bitcast.85) | data formatting | bytes 4194304 | tf_op jit(solution)/shard_map/dot_general | solution.py:53
  24.7 9.4 %all-gather.13.cloned.1.call-done = bf16[2048,512]{1,0:T(8,128)(2,1)} async-done(((bf16[1024,512]{1,0:T(8,128)(2,1)}), bf16[2048,512]{1,0:T(8,128)(2,1)}) %all-gather.13.cloned.1.call-update) | async-done | bytes 2097168 | tf_op jit(solution)/shard_map/all_gather | solution.py:55
  34.1 4.0 %copy.85 = bf16[512,2048]{1,0:T(8,128)(2,1)} copy(bf16[512,2048]{0,1:T(8,128)(2,1)} %bitcast.86) | data formatting | bytes 4194304 | tf_op jit(solution)/shard_map/dot_general | solution.py:53
  38.1 5.4 %fusion.1 = f32[1024,2,256]{2,0,1:T(8,128)S(1)} fusion(bf16[2,256,2048]{2,1,0:T(8,128)(2,1)} %bitcast.90, bf16[1,1024,2048]{2,1,0:T(8,128)(2,1)} %param.9), kind=kOutput, calls=%fused_computation.3 | convolution fusion | flops 2147483648 | bytes 8388608 | tf_op jit(solution)/shard_map/dot_general | solution.py:53
  43.5 2.4 %fusion.3 = f32[1024,2,256]{2,0,1:T(8,128)S(1)} fusion(bf16[2,256,2048]{2,1,0:T(8,128)(2,1)S(1)} %bitcast.92, bf16[1,1024,2048]{2,1,0:T(8,128)(2,1)S(1)} %copy-done.6), kind=kOutput, calls=%fused_computation.5 | convolution fusion | flops 2147483648 | bytes 8388608 | tf_op jit(solution)/shard_map/dot_general | solution.py:53
  46.1 1.6 fusion.14
  48.3 5.2 %fusion.25 = bf16[1024,512]{1,0:T(8,128)(2,1)S(1)} fusion(bf16[2048,512]{1,0:T(8,128)(2,1)} %all-gather.11.cloned.1.call-done, bf16[1,1024,2048]{2,1,0:T(8,128)(2,1)} %param.9), kind=kOutput, calls=%fused_computation.32 | convolution fusion | flops 2148007936 | bytes 7340032 | tf_op jit(solution)/shard_map/dot_general | solution.py:53
  53.8 1.3 fusion.18
  55.0 0.9 slice_add_fusion
  57.2 1.4 copy.98
  60.2 8.2 %all-reduce = f32[8]{0:T(128)S(1)} all-reduce(f32[8]{0:T(128)S(1)} %dynamic-update-slice), channel_id=2, replica_groups=mesh['ctx'=4,'tp'=4,'fsdp'=2] {'ctx'}, use_global_device_ids=true, to_apply=%add | all-reduce | flops 8 | bytes 64
  68.5 5.0 %fusion.28 = f32[2,2,256,512]{3,2,1,0:T(8,128)} fusion(bf16[2,512,2,256]{1,3,2,0:T(8,128)(2,1)S(1)} %copy.91, f32[2,2,512]{2,1,0:T(2,128)S(1)} %reduce_window_sum.24, pred[512,512]{1,0:T(8,128)(4,1)S(1)} %iota_compare_fusion, bf16[2,512,2,256]{3,2,1,0:T(2,128)(2,1)} %copy-done.1, bf16[2,512,2,256]{3,1,0,2:T(8,128)(2,1)} %bitcast.82), kind=kOutput, calls=%fused_computation.34 | convolution fusion | flops 1078984704 | bytes 5513216 | tf_op jit(solution)/shard_map/chts,cshd->cthd/dot_general | solution.py:81
  73.5 27.5 %all-gather.17.cloned.1.call-done = f32[4,2,256,256]{3,2,1,0:T(8,128)} async-done(((f32[1,2,256,256]{3,2,1,0:T(8,128)}), f32[4,2,256,256]{3,2,1,0:T(8,128)}) %all-gather.17.cloned.1.call-update) | async-done | bytes 2097168 | tf_op jit(solution)/shard_map/all_gather | solution.py:12
  100.9 3.6 %while.14 = (s32[]{:T(128)}, f32[2,256,256]{2,1,0:T(8,128)S(1)}, s32[]{:T(128)}, f32[4,2]{1,0:T(4,128)S(1)}, f32[4,2,256,256]{3,2,1,0:T(8,128)}, /*index=5*/s32[]{:T(128)}, s32[]{:T(128)}) while((s32[]{:T(128)}, f32[2,256,256]{2,1,0:T(8,128)S(1)}, s32[]{:T(128)}, f32[4,2]{1,0:T(4,128)S(1)}, f32[4,2,256,256]{3,2,1,0:T(8,128)}, ...), condition=%wide.region_4.5_spmd.clone, body=%wide.region_3.4_spmd.clone.sunk | while | flops 524292 | bytes 1572993 | solution.py:21
  101.0 1.2 fusion.55
  102.2 1.2 fusion.55
  103.4 1.2 fusion.55
  104.7 1.1 copy-done.2
  105.8 3.6 %fusion.46 = (f32[2,512,2]{1,2,0:T(2,128)S(1)}, f32[2,512,2,256]{1,3,2,0:T(8,128)S(1)}) fusion(bf16[2,512,2,256]{3,1,0,2:T(8,128)(2,1)S(1)} %bitcast.83, f32[1,2,256,256]{3,2,1,0:T(8,128)S(1)} %fusion.41, f32[1,2,256,256]{3,2,1,0:T(8,128)S(1)} %bitcast.76, f32[2,512,2]{1,2,0:T(2,128)S(1)} %get-tuple-element.138, f32[2,2,256,512]{3,2,1,0:T(8,128)} %fusion.28), kind=kOutput, calls=%fused_computation.70 | convolution fusion | flops 1612445696 | bytes 6307840 | tf_op jit(solution)/shard_map/cthd,chde->cthe/dot_general | solution.py:108
  109.4 2.4 %copy.95 = f32[2,512,2,256]{3,2,1,0:T(2,128)} copy(f32[2,512,2,256]{1,3,2,0:T(8,128)S(1)} %get-tuple-element.143) | data formatting | bytes 4194304 | tf_op jit(solution)/shard_map/add | solution.py:111
  112.3 1.2 mul.152
  114.0 1.2 sub.45
  115.2 1.5 copy.103
  117.6 1.5 copy.102
  119.1 7.8 %fusion.21 = bf16[1024,512]{1,0:T(8,128)(2,1)} fusion(f32[1024,512]{1,0:T(8,128)S(1)} %bitcast.87, f32[1024,512]{1,0:T(8,128)} %bitcast.89, f32[1024,512]{1,0:T(8,128)} %bitcast.88, bf16[2048,512]{1,0:T(8,128)(2,1)} %all-gather.9.cloned.1.call-done, bf16[1,1024,2048]{2,1,0:T(8,128)(2,1)} %param.9), kind=kOutput, calls=%fused_computation.30 | convolution fusion | flops 2152726528 | bytes 13631488 | tf_op jit(solution)/shard_map/dot_general | solution.py:53
  127.5 40.9 %all_to_all.19 = bf16[512,4,512]{0,2,1:T(8,128)(2,1)S(1)} all-to-all(bf16[512,4,512]{0,2,1:T(8,128)(2,1)} %bitcast.84), channel_id=1, replica_groups=mesh['ctx'=4,'tp'=4,'fsdp'=2] {'tp'}, dimensions={1} | all-to-all | bytes 4194304 | tf_op jit(solution)/shard_map/all_to_all | solution.py:115
  168.4 2.4 %copy.99 = bf16[4,512,512]{2,1,0:T(8,128)(2,1)} copy(bf16[4,512,512]{1,2,0:T(8,128)(2,1)S(1)} %bitcast.80) | data formatting | bytes 4194304 | tf_op jit(solution)/shard_map/all_to_all | solution.py:115
  170.8 27.4 %all-gather.19.cloned.1.call-done = bf16[1024,2048]{1,0:T(8,128)(2,1)} async-done(((bf16[1024,512]{1,0:T(8,128)(2,1)}), bf16[1024,2048]{1,0:T(8,128)(2,1)}) %all-gather.19.cloned.1.call-update) | async-done | bytes 4194320 | tf_op jit(solution)/shard_map/all_gather | solution.py:116
  198.2 6.2 %fusion.31 = bf16[1,1024,512]{2,1,0:T(8,128)(2,1)} fusion(bf16[1024,2048]{1,0:T(8,128)(2,1)} %all-gather.19.cloned.1.call-done, bf16[2048,512]{1,0:T(8,128)(2,1)} %bitcast.91), kind=kOutput, calls=%fused_computation.35 | convolution fusion | flops 2148007936 | bytes 7340032 | tf_op jit(solution)/shard_map/dot_general | solution.py:117
  (64 shorter events, 9.5 us)
Async XLA Ops:
  6.5 2.3 %copy-start.5 = (f32[1,1024,2]{1,2,0:T(2,128)S(1)}, f32[1,1024,2]{1,2,0:T(2,128)}, u32[]{:S(2)}) copy-start(f32[1,1024,2]{1,2,0:T(2,128)} %param.15) | copy-start | bytes 24580
  6.5 14.2 %all-gather.15.cloned.1.call-start = ((), (), s32[]{:S(2)}) async-start(), calls=%async_computation.4 | async-start | bytes 3145728 | tf_op jit(solution)/shard_map/all_gather | solution.py:56
  7.3 26.8 %all-gather.13.cloned.1.call-start = ((), (), s32[]{:S(2)}) async-start(), calls=%async_computation.3 | async-start | bytes 3145728 | tf_op jit(solution)/shard_map/all_gather | solution.py:55
  8.0 40.2 %all-gather.11.cloned.1.call-start = ((), (), s32[]{:S(2)}) async-start(), calls=%async_computation.2 | async-start | bytes 3145728 | tf_op jit(solution)/shard_map/all_gather | solution.py:57
  8.7 92.2 %all-gather.17.cloned.1.call-start = ((), (), s32[]{:S(2)}) async-start(), calls=%async_computation.5 | async-start | bytes 2621440 | tf_op jit(solution)/shard_map/all_gather | solution.py:12
  38.1 5.4 %copy-start.3 = (bf16[512,2048]{1,0:T(8,128)(2,1)S(1)}, bf16[512,2048]{1,0:T(8,128)(2,1)}, u32[]{:S(2)}) copy-start(bf16[512,2048]{1,0:T(8,128)(2,1)} %copy.85) | copy-start | bytes 6291460
  38.1 5.4 %copy-start.6 = (bf16[1,1024,2048]{2,1,0:T(8,128)(2,1)S(1)}, bf16[1,1024,2048]{2,1,0:T(8,128)(2,1)}, u32[]{:S(2)}) copy-start(bf16[1,1024,2048]{2,1,0:T(8,128)(2,1)} %param.9) | copy-start | bytes 12582916
  53.8 2.2 %copy-start.1 = (bf16[2,512,2,256]{3,2,1,0:T(2,128)(2,1)}, bf16[2,512,2,256]{3,2,1,0:T(2,128)(2,1)S(1)}, u32[]{:S(2)}) copy-start(bf16[2,512,2,256]{3,2,1,0:T(2,128)(2,1)S(1)} %reshape.123) | copy-start | bytes 3145732
  56.0 1.2 copy-start.4
  56.0 2.7 %copy-start.7 = (u32[32]{0:T(128)S(1)}, u32[32]{0:T(128)}, u32[]{:S(2)}) copy-start(u32[32]{0:T(128)} %constant.55) | copy-start | bytes 388
  56.0 63.1 %all-gather.9.cloned.1.call-start = ((), (), s32[]{:S(2)}) async-start(), calls=%async_computation.1 | async-start | bytes 3145728 | tf_op jit(solution)/shard_map/all_gather | solution.py:58
  56.6 70.9 %all-gather.21.cloned.1.call-start = ((), (), s32[]{:S(2)}) async-start(), calls=%async_computation.7 | async-start | bytes 3145728 | tf_op jit(solution)/shard_map/all_gather | solution.py:114
  58.6 139.6 %all-gather.19.cloned.1.call-start = ((), (), s32[]{:S(2)}) async-start(), calls=%async_computation.6 | async-start | bytes 5242880 | tf_op jit(solution)/shard_map/all_gather | solution.py:116
  104.6 1.2 copy-start.2
  115.2 2.3 %copy-start = (f32[2,512,2,256]{3,2,1,0:T(2,128)S(1)}, f32[2,512,2,256]{3,2,1,0:T(2,128)}, u32[]{:S(2)}) copy-start(f32[2,512,2,256]{3,2,1,0:T(2,128)} %copy.95) | copy-start | bytes 6291460
Sparse Core Ops, SparseCore 0:
  8.9 11.8 all-gather.14
  22.3 11.7 all-gather.12
  35.6 11.7 all-gather.10
  56.1 44.7 all-gather.16
  102.3 11.9 all-gather.8
  115.7 11.7 all-gather.20
  129.3 68.8 all-gather.18
where the time goes:
time: 214 us; the launch traced here: 211 us
  waiting for transfers between devices  75 us (35%)
  blocking collectives  49.1 us (23%)
  matrix products  36.6 us (17%)
  local copies, waits for them, and re-layouts  24.8 us (12%)
  between operations  14.4 us (7%)
  other arithmetic  10.8 us (5%)
    all_to_all x1, blocking collectives, on_device(): lax.all_to_all(column_block, 'tp', split_axis=1, concat_axis=0, tiled=True)  40.9 us
    all_gather x1, waiting for transfers between devices, entering(): pieces = jax.tree.map(lambda part: lax.all_gather(part, axis), value)  27.5 us
    all_gather x1, waiting for transfers between devices, on_device(): every_head = lax.all_gather(hidden, 'tp', axis=1, tiled=True)  27.4 us
    dot_general x4, matrix products, add_rows(): return jnp.dot(token_rows, shard_rows, preferred_element_type=jnp.float32)  20.7 us
    all_gather x1, waiting for transfers between devices, on_device(): lax.all_gather(query_weight, 'fsdp', axis=0, tiled=True)  9.36 us
    unnamed x1, blocking collectives  8.19 us
    dot_general x2, local copies, waits for them, and re-layouts, add_rows(): return jnp.dot(token_rows, shard_rows, preferred_element_type=jnp.float32)  7.96 us
    unnamed x23, local copies, waits for them, and re-layouts  7.72 us
  transfers between devices with their start and end apart: 7, of which 5 were waited for; matrix products, arithmetic and copies ran while one was open for 27% of the time, Pallas kernels for 0%

commit v1 on v0

v1 whole, which is shorter than its diff:
```python
import functools

import jax
import jax.numpy as jnp
from jax import lax
from jax.experimental import pallas as pl
from jax.experimental.pallas import tpu as pltpu
from jax.sharding import PartitionSpec as P

DH = 256
BLOCK = 512
VMEM_LIMIT = 40 * 1024 * 1024
F32 = jnp.float32
BF16 = jnp.bfloat16


def mm(left, right):
    return jnp.dot(left, right, preferred_element_type=F32)


def mm_nt(left, right):
    return lax.dot_general(left, right, (((1,), (1,)), ((), ())), preferred_element_type=F32)


def mm_tn(left, right):
    return lax.dot_general(left, right, (((0,), (0,)), ((), ())), preferred_element_type=F32)


def swap(value, axis, mask):
    size = lax.axis_size(axis)
    return lax.ppermute(value, axis, [(place, place ^ mask) for place in range(size)])


def rotated(values, cosine, sine):
    half = DH // 2
    parts = []
    for start in range(0, values.shape[1], DH):
        low = values[:, start : start + half]
        high = values[:, start + half : start + DH]
        parts.append((low * cosine - high * sine).astype(BF16))
        parts.append((high * cosine + low * sine).astype(BF16))
    return jnp.concatenate(parts, axis=1)


def key_value_kernel(
    heads, other, x, wk, wv, acc_k, acc_v, cosine, sine, decay, k_out, v_out, before_out, state_out, sent_out
):
    block = pl.program_id(0)

    @pl.when(block == 0)
    def _():
        state_out[...] = jnp.zeros_like(state_out)

    keys = rotated(acc_k[...] + mm(x[...], wk[...]), cosine[...], sine[...])
    values = (acc_v[...] + mm(x[...], wv[...])).astype(BF16)
    k_out[...] = keys
    v_out[...] = values
    columns = decay[...].T
    for head in range(heads):
        span = slice(head * DH, (head + 1) * DH)
        ending = columns[BLOCK - 1 : BLOCK, head : head + 1]
        faded = jnp.exp(ending - columns[:, head : head + 1])
        weighted = (keys[:, span].astype(F32) * faded).astype(BF16)
        old = state_out[head]
        before_out[0, head] = old.astype(BF16)
        state_out[head] = jnp.exp(ending) * old + mm_tn(weighted, values[:, span])
    sent_out[...] = state_out[...].astype(BF16)


def query_gate_kernel(heads, other, x, wq, wg, acc_q, acc_g, cosine, sine, decay, k, v, q_out, g_out, intra_out):
    queries = rotated(acc_q[...] + mm(x[...], wq[...]), cosine[...], sine[...])
    q_out[...] = queries
    g_out[...] = (acc_g[...] + mm(x[...], wg[...])).astype(BF16)
    columns = decay[...].T
    rows = decay[...]
    part = BLOCK // 2
    for head in range(heads):
        span = slice(head * DH, (head + 1) * DH)
        for piece in range(2):
            first, last = piece * part, (piece + 1) * part
            scores = mm_nt(queries[first:last, span], k[:last, span])
            differ = columns[first:last, head : head + 1] - rows[head : head + 1, :last]
            place_t = lax.broadcasted_iota(jnp.int32, (part, last), 0) + first
            place_s = lax.broadcasted_iota(jnp.int32, (part, last), 1)
            causal = place_t >= place_s
            weights = jnp.where(causal, jnp.exp(jnp.where(causal, differ, 0.0)), 0.0)
            intra_out[first:last, span] = mm((scores * weights).astype(BF16), v[:last, span])


def hidden_kernel(heads, block, scale, q, gate, intra, decay, entering, before, out):
    columns = decay[...].T
    for head in range(heads):
        span = slice(head * DH, (head + 1) * DH)
        prior = scale[block, head] * entering[head].astype(F32) + before[0, head].astype(F32)
        inter = jnp.exp(columns[:, head : head + 1]) * mm(q[:, span], prior.astype(BF16))
        retained = intra[:, span] + inter
        center = retained - jnp.mean(retained, axis=1, keepdims=True)
        spread = jnp.mean(center * center, axis=1, keepdims=True)
        value = gate[:, span].astype(F32)
        silu = value / (1.0 + jnp.exp(-value))
        out[:, span] = (silu * center * lax.rsqrt(spread + 1e-5)).astype(BF16)


def params(*semantics):
    return pltpu.CompilerParams(vmem_limit_bytes=VMEM_LIMIT, dimension_semantics=semantics)


def cost(flops, bytes_accessed, transcendentals=0):
    return pl.CostEstimate(flops=flops, bytes_accessed=bytes_accessed, transcendentals=transcendentals)


def turn_tables(row_count, width):
    half = width // 2
    fine = 32
    index_row = jnp.arange(half).astype(F32)
    frequency = jnp.power(F32(10000.0), -index_row / half)
    offset = lax.axis_index("ctx") * row_count
    coarse_at = (offset + fine * jnp.arange(row_count // fine)).astype(F32)
    fine_at = jnp.arange(fine).astype(F32)
    coarse = coarse_at[:, None] * frequency[None, :]
    small = fine_at[:, None] * frequency[None, :]
    cos_c, sin_c = jnp.cos(coarse)[:, None, :], jnp.sin(coarse)[:, None, :]
    cos_f, sin_f = jnp.cos(small)[None], jnp.sin(small)[None]
    cosine = (cos_c * cos_f - sin_c * sin_f).reshape(row_count, half)
    sine = (sin_c * cos_f + cos_c * sin_f).reshape(row_count, half)
    return cosine, sine


def on_device(tokens, query_weight, key_weight, value_weight, gate_weight, out_weight, log_decay):
    x = tokens[0]
    rows, width = x.shape
    part, cols = query_weight.shape
    heads = cols // DH
    blocks = rows // BLOCK
    ctx = lax.axis_size("ctx")
    core = lax.axis_index("fsdp")
    place = lax.axis_index("tp")

    key_far = swap(key_weight, "fsdp", 1)
    value_far = swap(value_weight, "fsdp", 1)
    query_far = swap(query_weight, "fsdp", 1)
    gate_far = swap(gate_weight, "fsdp", 1)
    out_far = swap(out_weight, "fsdp", 1)

    lower = (jnp.arange(BLOCK)[:, None] <= jnp.arange(BLOCK)[None, :]).astype(F32)
    per_block = log_decay[0].T.reshape(heads * blocks, BLOCK)
    sums = jnp.dot(per_block, lower, precision=lax.Precision.HIGHEST).reshape(heads, blocks, BLOCK)
    ending = sums[:, :, -1]
    decay_rows = jnp.pad(sums.reshape(heads, rows), ((0, 8 - heads), (0, 0)))
    earlier = jnp.cumsum(ending, axis=1) - ending
    block_scale = jnp.exp(earlier).T
    total = jnp.sum(ending, axis=1)

    cosine, sine = turn_tables(rows, DH)

    x_own = lax.dynamic_slice_in_dim(x, core * part, part, axis=1)
    acc_k = mm(x_own, key_weight)
    acc_v = mm(x_own, value_weight)
    acc_q = mm(x_own, query_weight)
    acc_g = mm(x_own, gate_weight)

    other = (1 - core).astype(jnp.int32).reshape(1)
    whole_w = pl.BlockSpec((part, cols), lambda b, o: (0, 0))
    rows_spec = pl.BlockSpec((BLOCK, cols), lambda b, o: (b, 0))
    turn_spec = pl.BlockSpec((BLOCK, DH // 2), lambda b, o: (b, 0))
    decay_spec = pl.BlockSpec((8, BLOCK), lambda b, o: (0, b))
    x_spec = pl.BlockSpec((BLOCK, part), lambda b, o: (b, o[0]))
    state_spec = pl.BlockSpec((heads, DH, DH), lambda b, o: (0, 0, 0))

    keys, values, before, state, sent = pl.pallas_call(
        functools.partial(key_value_kernel, heads),
        grid_spec=pltpu.PrefetchScalarGridSpec(
            num_scalar_prefetch=1,
            grid=(blocks,),
            in_specs=[x_spec, whole_w, whole_w, rows_spec, rows_spec, turn_spec, turn_spec, decay_spec],
            out_specs=[
                rows_spec,
                rows_spec,
                pl.BlockSpec((1, heads, DH, DH), lambda b, o: (b, 0, 0, 0)),
                state_spec,
                state_spec,
            ],
        ),
        out_shape=[
            jax.ShapeDtypeStruct((rows, cols), BF16),
            jax.ShapeDtypeStruct((rows, cols), BF16),
            jax.ShapeDtypeStruct((blocks, heads, DH, DH), BF16),
            jax.ShapeDtypeStruct((heads, DH, DH), F32),
            jax.ShapeDtypeStruct((heads, DH, DH), BF16),
        ],
        compiler_params=params("arbitrary"),
        cost_estimate=cost(4 * rows * part * cols, 12 << 20),
        name="key_value",
    )(other, x, key_far, value_far, acc_k, acc_v, cosine, sine, decay_rows)

    entering = jnp.zeros_like(state)
    entering_log = jnp.zeros_like(total)
    window, window_log, message = state, total, sent
    hop = 1
    while hop < ctx:
        pairs = [(source, source + hop) for source in range(ctx - hop)]
        got = lax.ppermute(message, "ctx", pairs).astype(F32)
        entering = entering + jnp.exp(entering_log)[:, None, None] * got
        if 2 * hop < ctx:
            got_log = lax.ppermute(window_log, "ctx", pairs)
            window = window + jnp.exp(window_log)[:, None, None] * got
            message = window.astype(BF16)
            entering_log = entering_log + got_log
            window_log = window_log + got_log
        hop *= 2
    entering = entering.astype(BF16)

    queries, gates, intra = pl.pallas_call(
        functools.partial(query_gate_kernel, heads),
        grid_spec=pltpu.PrefetchScalarGridSpec(
            num_scalar_prefetch=1,
            grid=(blocks,),
            in_specs=[
                x_spec, whole_w, whole_w, rows_spec, rows_spec, turn_spec, turn_spec, decay_spec, rows_spec, rows_spec,
            ],
            out_specs=[rows_spec, rows_spec, rows_spec],
        ),
        out_shape=[
            jax.ShapeDtypeStruct((rows, cols), BF16),
            jax.ShapeDtypeStruct((rows, cols), BF16),
            jax.ShapeDtypeStruct((rows, cols), F32),
        ],
        compiler_params=params("arbitrary"),
        cost_estimate=cost(4 * rows * part * cols + 4 * rows * BLOCK * cols, 16 << 20, rows * BLOCK * heads),
        name="query_gate",
    )(other, x, query_far, gate_far, acc_q, acc_g, cosine, sine, decay_rows, keys, values)

    out_rows = jnp.where(
        core == 0,
        jnp.concatenate([out_weight, out_far], axis=1),
        jnp.concatenate([out_far, out_weight], axis=1),
    )

    def out_columns(at):
        return lax.dynamic_slice_in_dim(out_rows, at * cols, cols, axis=1)

    masks = (1, 2)
    mine = out_columns(place)
    across = [out_columns(place ^ mask) for mask in masks]
    diagonal = out_columns(place ^ (masks[0] | masks[1]))
    gathered_rows = []
    for index, mask in enumerate(masks):
        both = jnp.concatenate([across[index], diagonal], axis=1)
        gathered_rows.append(swap(both, "tp", mask))

    def hidden_rows(block):
        at = pl.BlockSpec((BLOCK, cols), lambda i: (block, 0))
        return pl.pallas_call(
            functools.partial(hidden_kernel, heads, block),
            grid=(1,),
            in_specs=[
                pl.BlockSpec(memory_space=pltpu.SMEM),
                at,
                at,
                at,
                pl.BlockSpec((8, BLOCK), lambda i: (0, block)),
                pl.BlockSpec((heads, DH, DH), lambda i: (0, 0, 0)),
                pl.BlockSpec((1, heads, DH, DH), lambda i: (block, 0, 0, 0)),
            ],
            out_specs=pl.BlockSpec((BLOCK, cols), lambda i: (0, 0)),
            out_shape=jax.ShapeDtypeStruct((BLOCK, cols), BF16),
            compiler_params=params("arbitrary"),
            cost_estimate=cost(2 * BLOCK * DH * cols, 4 << 20, BLOCK * cols),
            name="hidden",
        )(block_scale, queries, gates, intra, decay_rows, entering, before)

    hidden = [hidden_rows(block) for block in range(blocks)]
    outs = []
    for block in range(blocks):
        gather_at, sum_at = block % 2, 1 - block % 2
        far = swap(hidden[block], "tp", masks[gather_at])
        far_weight = gathered_rows[gather_at]
        give = mm(hidden[block], across[sum_at]) + mm(far, far_weight[:, cols:])
        keep = mm(hidden[block], mine) + mm(far, far_weight[:, :cols])
        got = swap(give.astype(BF16), "tp", masks[sum_at])
        outs.append((keep + got.astype(F32)).astype(BF16))
    return jnp.concatenate(outs, axis=0)[None]


def solution(mesh):
    in_specs = (
        P("fsdp", "ctx", None),
        P("fsdp", "tp"),
        P("fsdp", "tp"),
        P("fsdp", "tp"),
        P("fsdp", "tp"),
        P("tp", "fsdp"),
        P("fsdp", "ctx", "tp"),
    )
    out_specs = P("fsdp", "ctx", "tp")
    return jax.shard_map(
        on_device, mesh=mesh, in_specs=in_specs, out_specs=out_specs, check_vma=False
    )
```

time: 214 us -> 109 us (0.51)
  blocking collectives: 49.1 us -> 0 us
  waiting for transfers between devices: 75 us -> 45.4 us
  local copies, waits for them, and re-layouts: 24.8 us -> 6.49 us
  Pallas kernels: 0 us -> 14.6 us
  matrix products: 36.6 us -> 22.6 us
  between operations: 14.4 us -> 0.47 us
  starting transfers between devices: 0.42 us -> 12.5 us
  other arithmetic: 10.8 us -> 5.86 us
    all_gather x7 -> x0, waiting for transfers between devices: 72.3 us -> none  [the longest x1 27.5 us: entering(): pieces = jax.tree.map(lambda part: lax.all_gather(part, axis), value)]
    ppermute x0 -> x14, waiting for transfers between devices: none -> 45.4 us  [the longest x11 31.8 us: swap(): lax.ppermute(value, axis, [(place, place ^ mask) for place in range(size)])]
    all_to_all x1 -> x0, blocking collectives: 40.9 us -> none  [on_device(): lax.all_to_all(column_block, 'tp', split_axis=1, concat_axis=0, tiled=True)]
    pallas_call x0 -> x4, Pallas kernels: none -> 14.6 us  [the longest x1 5.72 us: on_device(): pl.pallas_call(functools.partial(query_gate_kernel, heads), grid_spec=plt...]
    dot_general x8 -> x13, matrix products: 36.6 us -> 22.6 us  [the longest x12 22.3 us: mm(): return jnp.dot(left, right, preferred_element_type=F32)]
    ppermute x0 -> x14, starting transfers between devices: none -> 12.5 us  [the longest x11 8.49 us: swap(): lax.ppermute(value, axis, [(place, place ^ mask) for place in range(size)])]
    unnamed x1 -> x0, blocking collectives: 8.19 us -> none
    dot_general x2 -> x0, local copies, waits for them, and re-layouts: 7.96 us -> none  [add_rows(): return jnp.dot(token_rows, shard_rows, preferred_element_type=jnp.float32)]
  transfers between devices with their start and end apart: 7 -> 14, of which waited for: 5 -> 6; matrix products, arithmetic and copies ran while one was open for 27% -> 26% of each run, Pallas kernels for 0% -> 14%
where the time goes in v1:
time: 109 us; the launch traced here: 108 us
  waiting for transfers between devices  45.4 us (42%)
  matrix products  22.6 us (21%)
  Pallas kernels  14.6 us (13%)
  starting transfers between devices  12.5 us (11%)
  local copies, waits for them, and re-layouts  6.49 us (6%)
  other arithmetic  5.86 us (5%)
    ppermute x11, waiting for transfers between devices, swap(): lax.ppermute(value, axis, [(place, place ^ mask) for place in range(size)])  31.8 us
    dot_general x12, matrix products, mm(): return jnp.dot(left, right, preferred_element_type=F32)  22.3 us
    ppermute x2, waiting for transfers between devices, on_device(): got = lax.ppermute(message, 'ctx', pairs).astype(F32)  13.6 us
    ppermute x11, starting transfers between devices, swap(): lax.ppermute(value, axis, [(place, place ^ mask) for place in range(size)])  8.49 us
    pallas_call x1, Pallas kernels, on_device(): pl.pallas_call(functools.partial(query_gate_kernel, heads), grid_spec=plt...  5.72 us
    unnamed x38, local copies, waits for them, and re-layouts  5.42 us
    pallas_call x1, Pallas kernels, on_device(): pl.pallas_call(functools.partial(key_value_kernel, heads), grid_spec=pltp...  5.17 us
    pallas_call x2, Pallas kernels, hidden_rows(): pl.pallas_call(functools.partial(hidden_kernel, heads, block), grid=(1,),...  3.75 us
  transfers between devices with their start and end apart: 14, of which 6 were waited for; matrix products, arithmetic and copies ran while one was open for 26% of the time, Pallas kernels for 14%

profile of v1, /device:TPU:24, one launch (start us, length us, event | category | flops | bytes accessed | tf_op | source)
XLA Modules:
  0.0 108.0 jit_solution(14807868419089544262)
XLA Ops:
  1.7 1.3 %collective-permute-start.5 = (f32[2]{0:T(128)S(1)}, f32[2]{0:T(128)S(1)}, u32[]{:S(2)}, u32[]{:S(2)}) collective-permute-start(f32[2]{0:T(128)S(1)} %get-tuple-element.28), channel_id=1, source_target_pairs={{0,8},{8,16},{16,24},{1,9},{9,17},{17,25},{2,10},{10,18},{18,26},{... | collective-permute-start | bytes 32 | tf_op jit(solution)/shard_map/ppermute | solution.py:205
  3.6 3.3 %fusion.acc_v = f32[1024,512]{1,0:T(8,128)S(1)} fusion(bf16[1024,512]{1,0:T(8,128)(2,1)} %param.10, bf16[1,1024,2048]{2,1,0:T(8,128)(2,1)} %param.7, s32[]{:T(128)S(6)} %select_n.23), kind=kOutput, calls=%fused_computation.1 | convolution fusion | flops 1073741824 | bytes 5242884 | tf_op jit(solution)/shard_map/dot_general | solution.py:18
  7.0 2.6 %fusion.2.acc_k = f32[1024,512]{1,0:T(8,128)} fusion(bf16[1024,512]{1,0:T(8,128)(2,1)S(1)} %copy-done.18, bf16[1,1024,2048]{2,1,0:T(8,128)(2,1)S(1)} %copy-done.9, s32[]{:T(128)S(6)} %select_n.23), kind=kOutput, calls=%fused_computation.3 | convolution fusion | flops 1073741824 | bytes 5242884 | tf_op jit(solution)/shard_map/dot_general | solution.py:18
  10.1 4.6 %fusion.6.acc_q = f32[1024,512]{1,0:T(8,128)} fusion(bf16[1024,512]{1,0:T(8,128)(2,1)} %param.8, bf16[1,1024,2048]{2,1,0:T(8,128)(2,1)} %param.7, s32[]{:T(128)S(6)} %select_n.23), kind=kOutput, calls=%fused_computation.7 | convolution fusion | flops 1073741824 | bytes 5242884 | tf_op jit(solution)/shard_map/dot_general | solution.py:18
  14.7 3.9 %fusion.4.acc_g = f32[1024,512]{1,0:T(8,128)} fusion(bf16[1024,512]{1,0:T(8,128)(2,1)} %param.11, bf16[1,1024,2048]{2,1,0:T(8,128)(2,1)S(1)} %copy-done.10, s32[]{:T(128)S(6)} %select_n.23), kind=kOutput, calls=%fused_computation.5 | convolution fusion | flops 1073741824 | bytes 5242884 | tf_op jit(solution)/shard_map/dot_general | solution.py:18
  18.8 1.6 %copy-done.8 = f32[1024,512]{1,0:T(8,128)S(1)} copy-done((f32[1024,512]{1,0:T(8,128)S(1)}, f32[1024,512]{1,0:T(8,128)}, u32[]{:S(2)}) %copy-start.8) | copy-done | bytes 2097176
  20.4 5.2 %key_value.1 = (bf16[1024,512]{1,0:T(8,128)(2,1)S(1)}, bf16[1024,512]{1,0:T(8,128)(2,1)S(1)}, bf16[2,2,256,256]{3,2,1,0:T(8,128)(2,1)S(1)}, f32[2,256,256]{2,1,0:T(8,128)S(1)}, bf16[2,256,256]{2,1,0:T(8,128)(2,1)S(1)}) custom-call(s32[1]{0:T(128)} %bitcast.5.other, bf16[1024,2048]{1,0:T(8,128)(2,1)} %bitcast.44, ...), custom_call_target="tpu_custom_call" | custom-call | flops 2147483648 | bytes 12582912 | tf_op jit(solution)/shard_map/key_value/pallas_call | solution.py:170
  25.6 1.3 %collective-permute-start.4 = (bf16[2,256,256]{2,1,0:T(8,128)(2,1)S(1)}, bf16[2,256,256]{2,1,0:T(8,128)(2,1)S(1)}, u32[]{:S(2)}, u32[]{:S(2)}) collective-permute-start(bf16[2,256,256]{2,1,0:T(8,128)(2,1)S(1)} %get-tuple-element.18), channel_id=1, source_target_pairs={{0,8},{8,16},{16,24},{1,9},{9,17},{17,25},{2,10},{10,18},{18,26},{... | collective-permute-start | bytes 786440 | tf_op jit(solution)/shard_map/ppermute | solution.py:202
  26.9 2.3 %maximum_select_fusion = bf16[512,2048]{1,0:T(8,128)(2,1)S(1)} fusion(bf16[512,1024]{1,0:T(8,128)(2,1)} %collective-permute-done.7, bf16[512,1024]{1,0:T(8,128)(2,1)S(1)} %copy-done.17, pred[]{:T(512)S(6)} %eq.3), kind=kLoop, calls=%fused_computation | loop fusion | flops 9437184 | bytes 4194305 | tf_op jit(solution)/shard_map/jit(_where)/select_n | solution.py:233
  29.4 1.7 %pad_maximum_fusion.1 = (bf16[512,1024]{1,0:T(8,128)(2,1)}, bf16[512,1024]{1,0:T(8,128)(2,1)}) fusion(bf16[512,512]{1,0:T(8,128)(2,1)S(1)} %get-tuple-element.23, bf16[512,512]{1,0:T(8,128)(2,1)S(1)} %get-tuple-element.21, bf16[512,512]{1,0:T(8,128)(2,1)S(1)} %get-tuple-element.22), kind=kLoop, calls=%fused_computation.24 | loop fusion | flops 3670016 | bytes 3670016 | tf_op jit(solution)/shard_map/concatenate | solution.py:248
  31.2 1.5 %collective-permute-start.9 = (bf16[512,1024]{1,0:T(8,128)(2,1)}, bf16[512,1024]{1,0:T(8,128)(2,1)}, u32[]{:S(2)}, u32[]{:S(2)}) collective-permute-start(bf16[512,1024]{1,0:T(8,128)(2,1)} %get-tuple-element.24), channel_id=1, source_target_pairs={{0,2},{2,0},{4,6},{6,4},{1,3},{3,1},{5,7},{7,5},{8,10},{10,8},{12,... | collective-permute-start | bytes 3145736 | tf_op jit(solution)/shard_map/ppermute | solution.py:31
  32.7 4.3 %collective-permute-done.4 = bf16[2,256,256]{2,1,0:T(8,128)(2,1)S(1)} collective-permute-done((bf16[2,256,256]{2,1,0:T(8,128)(2,1)S(1)}, bf16[2,256,256]{2,1,0:T(8,128)(2,1)S(1)}, u32[]{:S(2)}, u32[]{:S(2)}) %collective-permute-start.4) | collective-permute-done | bytes 262176 | tf_op jit(solution)/shard_map/ppermute | solution.py:202
  37.2 1.5 %collective-permute-start.6 = (bf16[2,256,256]{2,1,0:T(8,128)(2,1)S(1)}, bf16[2,256,256]{2,1,0:T(8,128)(2,1)S(1)}, u32[]{:S(2)}, u32[]{:S(2)}) collective-permute-start(bf16[2,256,256]{2,1,0:T(8,128)(2,1)S(1)} %fusion.19), channel_id=1, source_target_pairs={{0,16},{8,24},{1,17},{9,25},{2,18},{10,26},{3,19},{11,27},{4,20},{... | collective-permute-start | bytes 786440 | tf_op jit(solution)/shard_map/ppermute | solution.py:202
  38.7 5.7 %query_gate.1 = (bf16[1024,512]{1,0:T(8,128)(2,1)S(1)}, bf16[1024,512]{1,0:T(8,128)(2,1)S(1)}, f32[1024,512]{1,0:T(8,128)S(1)}) custom-call(s32[1]{0:T(128)} %bitcast.5.other, bf16[1024,2048]{1,0:T(8,128)(2,1)} %bitcast.45, bf16[1024,512]{1,0:T(8,128)(2,1)} %collective-permute-done.wq, bf16[1024,512]{1,0:T(8,128)(2,1)} %collective-permute-done.1.wg, ...), custom_call_target="tpu_custom_call" | custom-call | flops 3221225472 | bytes 16777216 | tf_op jit(solution)/shard_map/query_gate/pallas_call | solution.py:213
  44.4 9.3 %collective-permute-done.6 = bf16[2,256,256]{2,1,0:T(8,128)(2,1)S(1)} collective-permute-done((bf16[2,256,256]{2,1,0:T(8,128)(2,1)S(1)}, bf16[2,256,256]{2,1,0:T(8,128)(2,1)S(1)}, u32[]{:S(2)}, u32[]{:S(2)}) %collective-permute-start.6) | collective-permute-done | bytes 262176 | tf_op jit(solution)/shard_map/ppermute | solution.py:202
  53.9 1.9 %hidden.2 = bf16[512,512]{1,0:T(8,128)(2,1)S(1)} custom-call(f32[2,2]{1,0:T(2,128)S(1)} %exponential_bitcast_fusion.scale, bf16[1024,512]{1,0:T(8,128)(2,1)S(1)} %get-tuple-element.15.q, bf16[1024,512]{1,0:T(8,128)(2,1)S(1)} %get-tuple-element.16.gate, f32[1024,512]{1,0:T(8,128)S(1)} %get-tuple-element.17.intra, f32[8,1024]{1,0:T(8,128)S(1)} %pad.4.decay, ...), custom_call_target="tpu_custom_call" | custom-call | flops 134217728 | bytes 4194304 | tf_op jit(solution)/shard_map/hidden/pallas_call | solution.py:253
  55.8 1.5 %collective-permute-start.8 = (bf16[512,512]{1,0:T(8,128)(2,1)S(1)}, bf16[512,512]{1,0:T(8,128)(2,1)}, u32[]{:S(2)}, u32[]{:S(2)}) collective-permute-start(bf16[512,512]{1,0:T(8,128)(2,1)S(1)} %hidden.2), channel_id=1, source_target_pairs={{0,2},{2,0},{4,6},{6,4},{1,3},{3,1},{5,7},{7,5},{8,10},{10,8},{12,... | collective-permute-start | bytes 1572872 | tf_op jit(solution)/shard_map/ppermute | solution.py:31
  57.4 1.5 %collective-permute-start.12 = (bf16[512,1024]{1,0:T(8,128)(2,1)}, bf16[512,1024]{1,0:T(8,128)(2,1)}, u32[]{:S(2)}, u32[]{:S(2)}) collective-permute-start(bf16[512,1024]{1,0:T(8,128)(2,1)} %get-tuple-element.25), channel_id=1, source_target_pairs={{0,4},{2,6},{4,0},{6,2},{1,5},{3,7},{5,1},{7,3},{8,12},{10,14},{12... | collective-permute-start | bytes 3145736 | tf_op jit(solution)/shard_map/ppermute | solution.py:31
  58.9 1.2 %copy-done.1 = bf16[1024,512]{1,0:T(8,128)(2,1)S(1)} copy-done((bf16[1024,512]{1,0:T(8,128)(2,1)S(1)}, bf16[1024,512]{1,0:T(8,128)(2,1)}, u32[]{:S(2)}) %copy-start.1) | copy-done | bytes 1048600
  60.1 1.2 %copy-done.3 = bf16[1024,512]{1,0:T(8,128)(2,1)S(1)} copy-done((bf16[1024,512]{1,0:T(8,128)(2,1)S(1)}, bf16[1024,512]{1,0:T(8,128)(2,1)}, u32[]{:S(2)}) %copy-start.3) | copy-done | bytes 1048600
  61.3 1.0 copy-done.5
  62.4 1.9 %hidden.3 = bf16[512,512]{1,0:T(8,128)(2,1)S(1)} custom-call(f32[2,2]{1,0:T(2,128)S(1)} %exponential_bitcast_fusion.scale, bf16[1024,512]{1,0:T(8,128)(2,1)S(1)} %copy-done.1, bf16[1024,512]{1,0:T(8,128)(2,1)S(1)} %copy-done.3, f32[1024,512]{1,0:T(8,128)S(1)} %get-tuple-element.17.intra, f32[8,1024]{1,0:T(8,128)S(1)} %pad.4.decay, ...), custom_call_target="tpu_custom_call" | custom-call | flops 134217728 | bytes 4194304 | tf_op jit(solution)/shard_map/hidden/pallas_call | solution.py:253
  64.8 4.1 %collective-permute-done.8 = bf16[512,512]{1,0:T(8,128)(2,1)} collective-permute-done((bf16[512,512]{1,0:T(8,128)(2,1)S(1)}, bf16[512,512]{1,0:T(8,128)(2,1)}, u32[]{:S(2)}, u32[]{:S(2)}) %collective-permute-start.8) | collective-permute-done | bytes 524320 | tf_op jit(solution)/shard_map/ppermute | solution.py:31
  68.9 1.6 %fusion.25 = f32[512,512]{1,0:T(8,128)S(1)} fusion(bf16[512,512]{1,0:T(8,128)(2,1)} %collective-permute-done.8, bf16[512,1024]{1,0:T(8,128)(2,1)} %collective-permute-done.9), kind=kOutput, calls=%fused_computation.37 | convolution fusion | flops 268435456 | bytes 2097152 | tf_op jit(solution)/shard_map/dot_general | solution.py:18
  71.0 1.6 %collective-permute-start.10 = (bf16[512,512]{1,0:T(8,128)(2,1)S(1)}, bf16[512,512]{1,0:T(8,128)(2,1)S(1)}, u32[]{:S(2)}, u32[]{:S(2)}) collective-permute-start(bf16[512,512]{1,0:T(8,128)(2,1)S(1)} %fusion.16), channel_id=1, source_target_pairs={{0,4},{2,6},{4,0},{6,2},{1,5},{3,7},{5,1},{7,3},{8,12},{10,14},{12... | collective-permute-start | bytes 1572872 | tf_op jit(solution)/shard_map/ppermute | solution.py:31
  72.6 22.3 %collective-permute-done.11 = bf16[512,512]{1,0:T(8,128)(2,1)S(1)} collective-permute-done((bf16[512,512]{1,0:T(8,128)(2,1)S(1)}, bf16[512,512]{1,0:T(8,128)(2,1)S(1)}, u32[]{:S(2)}, u32[]{:S(2)}) %collective-permute-start.11) | collective-permute-done | bytes 524320 | tf_op jit(solution)/shard_map/ppermute | solution.py:31
  94.9 1.5 %fusion.21 = f32[512,512]{1,0:T(8,128)S(1)} fusion(bf16[512,512]{1,0:T(8,128)(2,1)S(1)} %collective-permute-done.11, bf16[512,1024]{1,0:T(8,128)(2,1)} %collective-permute-done.12), kind=kOutput, calls=%fused_computation.33 | convolution fusion | flops 268435456 | bytes 2097152 | tf_op jit(solution)/shard_map/dot_general | solution.py:18
  97.5 1.7 %fusion.27 = f32[512,512]{1,0:T(8,128)S(1)} fusion(bf16[512,512]{1,0:T(8,128)(2,1)} %collective-permute-done.8, bf16[512,1024]{1,0:T(8,128)(2,1)} %collective-permute-done.9), kind=kOutput, calls=%fused_computation.39 | convolution fusion | flops 268435456 | bytes 2097152 | tf_op jit(solution)/shard_map/dot_general | solution.py:18
  99.1 1.5 %fusion.23 = f32[512,512]{1,0:T(8,128)S(1)} fusion(bf16[512,512]{1,0:T(8,128)(2,1)S(1)} %collective-permute-done.11, bf16[512,1024]{1,0:T(8,128)(2,1)} %collective-permute-done.12), kind=kOutput, calls=%fused_computation.35 | convolution fusion | flops 268435456 | bytes 2097152 | tf_op jit(solution)/shard_map/dot_general | solution.py:18
  100.6 3.3 %collective-permute-done.10 = bf16[512,512]{1,0:T(8,128)(2,1)S(1)} collective-permute-done((bf16[512,512]{1,0:T(8,128)(2,1)S(1)}, bf16[512,512]{1,0:T(8,128)(2,1)S(1)}, u32[]{:S(2)}, u32[]{:S(2)}) %collective-permute-start.10) | collective-permute-done | bytes 524320 | tf_op jit(solution)/shard_map/ppermute | solution.py:31
  104.4 2.1 %collective-permute-done.13 = bf16[512,512]{1,0:T(8,128)(2,1)S(1)} collective-permute-done((bf16[512,512]{1,0:T(8,128)(2,1)S(1)}, bf16[512,512]{1,0:T(8,128)(2,1)S(1)}, u32[]{:S(2)}, u32[]{:S(2)}) %collective-permute-start.13) | collective-permute-done | bytes 524320 | tf_op jit(solution)/shard_map/ppermute | solution.py:31
  106.9 1.0 maximum_bitcast_fusion
  (71 shorter events, 6.7 us)
Async XLA Ops:
  0.0 18.8 %collective-permute-start.2 = (bf16[1024,512]{1,0:T(8,128)(2,1)}, bf16[1024,512]{1,0:T(8,128)(2,1)}, u32[]{:S(2)}, u32[]{:S(2)}) collective-permute-start(bf16[1024,512]{1,0:T(8,128)(2,1)} %param.9), channel_id=1, source_target_pairs={{0,1},{1,0},{2,3},{3,2},{4,5},{5,4},{6,7},{7,6},{8,9},{9,8},{10,11... | collective-permute-start | bytes 3145736 | tf_op jit(solution)/shard_map/ppermute | solution.py:31
  0.0 18.8 %collective-permute-start.3 = (bf16[1024,512]{1,0:T(8,128)(2,1)}, bf16[1024,512]{1,0:T(8,128)(2,1)}, u32[]{:S(2)}, u32[]{:S(2)}) collective-permute-start(bf16[1024,512]{1,0:T(8,128)(2,1)} %param.10), channel_id=1, source_target_pairs={{0,1},{1,0},{2,3},{3,2},{4,5},{5,4},{6,7},{7,6},{8,9},{9,8},{10,11... | collective-permute-start | bytes 3145736 | tf_op jit(solution)/shard_map/ppermute | solution.py:31
  1.7 16.9 %collective-permute-start.5 = (f32[2]{0:T(128)S(1)}, f32[2]{0:T(128)S(1)}, u32[]{:S(2)}, u32[]{:S(2)}) collective-permute-start(f32[2]{0:T(128)S(1)} %get-tuple-element.28), channel_id=1, source_target_pairs={{0,8},{8,16},{16,24},{1,9},{9,17},{17,25},{2,10},{10,18},{18,26},{... | collective-permute-start | bytes 32 | tf_op jit(solution)/shard_map/ppermute | solution.py:205
  3.0 35.6 %collective-permute-start = (bf16[1024,512]{1,0:T(8,128)(2,1)}, bf16[1024,512]{1,0:T(8,128)(2,1)}, u32[]{:S(2)}, u32[]{:S(2)}) collective-permute-start(bf16[1024,512]{1,0:T(8,128)(2,1)} %param.8), channel_id=1, source_target_pairs={{0,1},{1,0},{2,3},{3,2},{4,5},{5,4},{6,7},{7,6},{8,9},{9,8},{10,11... | collective-permute-start | bytes 3145736 | tf_op jit(solution)/shard_map/ppermute | solution.py:31
  3.1 23.8 %collective-permute-start.7 = (bf16[512,1024]{1,0:T(8,128)(2,1)}, bf16[512,1024]{1,0:T(8,128)(2,1)}, u32[]{:S(2)}, u32[]{:S(2)}) collective-permute-start(bf16[512,1024]{1,0:T(8,128)(2,1)} %param.12), channel_id=1, source_target_pairs={{0,1},{1,0},{2,3},{3,2},{4,5},{5,4},{6,7},{7,6},{8,9},{9,8},{10,11... | collective-permute-start | bytes 3145736 | tf_op jit(solution)/shard_map/ppermute | solution.py:31
  3.6 3.3 %copy-start.9 = (bf16[1,1024,2048]{2,1,0:T(8,128)(2,1)S(1)}, bf16[1,1024,2048]{2,1,0:T(8,128)(2,1)}, u32[]{:S(2)}) copy-start(bf16[1,1024,2048]{2,1,0:T(8,128)(2,1)} %param.7) | copy-start | bytes 12582916
  3.6 3.4 %copy-start.18 = (bf16[1024,512]{1,0:T(8,128)(2,1)S(1)}, bf16[1024,512]{1,0:T(8,128)(2,1)}, u32[]{:S(2)}) copy-start(bf16[1024,512]{1,0:T(8,128)(2,1)} %param.9) | copy-start | bytes 3145732
  10.1 4.6 %copy-start.10 = (bf16[1,1024,2048]{2,1,0:T(8,128)(2,1)S(1)}, bf16[1,1024,2048]{2,1,0:T(8,128)(2,1)}, u32[]{:S(2)}) copy-start(bf16[1,1024,2048]{2,1,0:T(8,128)(2,1)} %param.7) | copy-start | bytes 12582916
  18.6 20.1 %collective-permute-start.1 = (bf16[1024,512]{1,0:T(8,128)(2,1)}, bf16[1024,512]{1,0:T(8,128)(2,1)}, u32[]{:S(2)}, u32[]{:S(2)}) collective-permute-start(bf16[1024,512]{1,0:T(8,128)(2,1)} %param.11), channel_id=1, source_target_pairs={{0,1},{1,0},{2,3},{3,2},{4,5},{5,4},{6,7},{7,6},{8,9},{9,8},{10,11... | collective-permute-start | bytes 3145736 | tf_op jit(solution)/shard_map/ppermute | solution.py:31
  18.8 1.6 %copy-start.8 = (f32[1024,512]{1,0:T(8,128)S(1)}, f32[1024,512]{1,0:T(8,128)}, u32[]{:S(2)}) copy-start(f32[1024,512]{1,0:T(8,128)} %fusion.2.acc_k) | copy-start | bytes 6291460
  20.4 6.5 %copy-start.17 = (bf16[512,1024]{1,0:T(8,128)(2,1)S(1)}, bf16[512,1024]{1,0:T(8,128)(2,1)}, u32[]{:S(2)}) copy-start(bf16[512,1024]{1,0:T(8,128)(2,1)} %param.12) | copy-start | bytes 3145732
  25.5 28.4 %copy-start.4 = (bf16[2,2,256,256]{3,2,1,0:T(8,128)(2,1)}, bf16[2,2,256,256]{3,2,1,0:T(8,128)(2,1)S(1)}, u32[]{:S(2)}) copy-start(bf16[2,2,256,256]{3,2,1,0:T(8,128)(2,1)S(1)} %get-tuple-element.20.before) | copy-start | bytes 1572868
  25.6 11.4 %collective-permute-start.4 = (bf16[2,256,256]{2,1,0:T(8,128)(2,1)S(1)}, bf16[2,256,256]{2,1,0:T(8,128)(2,1)S(1)}, u32[]{:S(2)}, u32[]{:S(2)}) collective-permute-start(bf16[2,256,256]{2,1,0:T(8,128)(2,1)S(1)} %get-tuple-element.18), channel_id=1, source_target_pairs={{0,8},{8,16},{16,24},{1,9},{9,17},{17,25},{2,10},{10,18},{18,26},{... | collective-permute-start | bytes 786440 | tf_op jit(solution)/shard_map/ppermute | solution.py:202
  29.2 2.0 %copy-start.11 = (bf16[512,2048]{1,0:T(8,128)(2,1)}, bf16[512,2048]{1,0:T(8,128)(2,1)S(1)}, u32[]{:S(2)}) copy-start(bf16[512,2048]{1,0:T(8,128)(2,1)S(1)} %maximum_select_fusion) | copy-start | bytes 6291460
  29.4 7.7 %copy-start.13 = (bf16[512,512]{1,0:T(8,128)(2,1)}, bf16[512,512]{1,0:T(8,128)(2,1)S(1)}, u32[]{:S(2)}) copy-start(bf16[512,512]{1,0:T(8,128)(2,1)S(1)} %get-tuple-element.21) | copy-start | bytes 1572868
  29.4 7.7 %copy-start.15 = (bf16[512,512]{1,0:T(8,128)(2,1)}, bf16[512,512]{1,0:T(8,128)(2,1)S(1)}, u32[]{:S(2)}) copy-start(bf16[512,512]{1,0:T(8,128)(2,1)S(1)} %get-tuple-element.22) | copy-start | bytes 1572868
  29.4 9.2 %copy-start.6 = (f32[1024,512]{1,0:T(8,128)S(1)}, f32[1024,512]{1,0:T(8,128)}, u32[]{:S(2)}) copy-start(f32[1024,512]{1,0:T(8,128)} %fusion.6.acc_q) | copy-start | bytes 6291460
  29.4 9.2 %copy-start.7 = (f32[1024,512]{1,0:T(8,128)S(1)}, f32[1024,512]{1,0:T(8,128)}, u32[]{:S(2)}) copy-start(f32[1024,512]{1,0:T(8,128)} %fusion.4.acc_g) | copy-start | bytes 6291460
  31.2 37.7 %collective-permute-start.9 = (bf16[512,1024]{1,0:T(8,128)(2,1)}, bf16[512,1024]{1,0:T(8,128)(2,1)}, u32[]{:S(2)}, u32[]{:S(2)}) collective-permute-start(bf16[512,1024]{1,0:T(8,128)(2,1)} %get-tuple-element.24), channel_id=1, source_target_pairs={{0,2},{2,0},{4,6},{6,4},{1,3},{3,1},{5,7},{7,5},{8,10},{10,8},{12,... | collective-permute-start | bytes 3145736 | tf_op jit(solution)/shard_map/ppermute | solution.py:31
  37.2 16.6 %collective-permute-start.6 = (bf16[2,256,256]{2,1,0:T(8,128)(2,1)S(1)}, bf16[2,256,256]{2,1,0:T(8,128)(2,1)S(1)}, u32[]{:S(2)}, u32[]{:S(2)}) collective-permute-start(bf16[2,256,256]{2,1,0:T(8,128)(2,1)S(1)} %fusion.19), channel_id=1, source_target_pairs={{0,16},{8,24},{1,17},{9,25},{2,18},{10,26},{3,19},{11,27},{4,20},{... | collective-permute-start | bytes 786440 | tf_op jit(solution)/shard_map/ppermute | solution.py:202
  44.4 11.4 %copy-start = (bf16[1024,512]{1,0:T(8,128)(2,1)}, bf16[1024,512]{1,0:T(8,128)(2,1)S(1)}, u32[]{:S(2)}) copy-start(bf16[1024,512]{1,0:T(8,128)(2,1)S(1)} %get-tuple-element.15.q) | copy-start | bytes 3145732
  44.4 11.4 %copy-start.2 = (bf16[1024,512]{1,0:T(8,128)(2,1)}, bf16[1024,512]{1,0:T(8,128)(2,1)S(1)}, u32[]{:S(2)}) copy-start(bf16[1024,512]{1,0:T(8,128)(2,1)S(1)} %get-tuple-element.16.gate) | copy-start | bytes 3145732
  55.8 13.1 %collective-permute-start.8 = (bf16[512,512]{1,0:T(8,128)(2,1)S(1)}, bf16[512,512]{1,0:T(8,128)(2,1)}, u32[]{:S(2)}, u32[]{:S(2)}) collective-permute-start(bf16[512,512]{1,0:T(8,128)(2,1)S(1)} %hidden.2), channel_id=1, source_target_pairs={{0,2},{2,0},{4,6},{6,4},{1,3},{3,1},{5,7},{7,5},{8,10},{10,8},{12,... | collective-permute-start | bytes 1572872 | tf_op jit(solution)/shard_map/ppermute | solution.py:31
  57.4 37.5 %collective-permute-start.12 = (bf16[512,1024]{1,0:T(8,128)(2,1)}, bf16[512,1024]{1,0:T(8,128)(2,1)}, u32[]{:S(2)}, u32[]{:S(2)}) collective-permute-start(bf16[512,1024]{1,0:T(8,128)(2,1)} %get-tuple-element.25), channel_id=1, source_target_pairs={{0,4},{2,6},{4,0},{6,2},{1,5},{3,7},{5,1},{7,3},{8,12},{10,14},{12... | collective-permute-start | bytes 3145736 | tf_op jit(solution)/shard_map/ppermute | solution.py:31
  58.9 1.2 %copy-start.1 = (bf16[1024,512]{1,0:T(8,128)(2,1)S(1)}, bf16[1024,512]{1,0:T(8,128)(2,1)}, u32[]{:S(2)}) copy-start(bf16[1024,512]{1,0:T(8,128)(2,1)} %copy-done) | copy-start | bytes 3145732
  60.1 1.2 %copy-start.3 = (bf16[1024,512]{1,0:T(8,128)(2,1)S(1)}, bf16[1024,512]{1,0:T(8,128)(2,1)}, u32[]{:S(2)}) copy-start(bf16[1024,512]{1,0:T(8,128)(2,1)} %copy-done.2) | copy-start | bytes 3145732
  64.3 6.3 %copy-start.16 = (bf16[512,512]{1,0:T(8,128)(2,1)S(1)}, bf16[512,512]{1,0:T(8,128)(2,1)}, u32[]{:S(2)}) copy-start(bf16[512,512]{1,0:T(8,128)(2,1)} %copy-done.15) | copy-start | bytes 1572868
  64.3 30.6 %collective-permute-start.11 = (bf16[512,512]{1,0:T(8,128)(2,1)S(1)}, bf16[512,512]{1,0:T(8,128)(2,1)S(1)}, u32[]{:S(2)}, u32[]{:S(2)}) collective-permute-start(bf16[512,512]{1,0:T(8,128)(2,1)S(1)} %hidden.3), channel_id=1, source_target_pairs={{0,4},{2,6},{4,0},{6,2},{1,5},{3,7},{5,1},{7,3},{8,12},{10,14},{12... | collective-permute-start | bytes 1572872 | tf_op jit(solution)/shard_map/ppermute | solution.py:31
  70.6 25.8 %copy-start.14 = (bf16[512,512]{1,0:T(8,128)(2,1)S(1)}, bf16[512,512]{1,0:T(8,128)(2,1)}, u32[]{:S(2)}) copy-start(bf16[512,512]{1,0:T(8,128)(2,1)} %copy-done.13) | copy-start | bytes 1572868
  71.0 32.9 %collective-permute-start.10 = (bf16[512,512]{1,0:T(8,128)(2,1)S(1)}, bf16[512,512]{1,0:T(8,128)(2,1)S(1)}, u32[]{:S(2)}, u32[]{:S(2)}) collective-permute-start(bf16[512,512]{1,0:T(8,128)(2,1)S(1)} %fusion.16), channel_id=1, source_target_pairs={{0,4},{2,6},{4,0},{6,2},{1,5},{3,7},{5,1},{7,3},{8,12},{10,14},{12... | collective-permute-start | bytes 1572872 | tf_op jit(solution)/shard_map/ppermute | solution.py:31
  96.8 7.1 %copy-start.12 = (bf16[512,2048]{1,0:T(8,128)(2,1)S(1)}, bf16[512,2048]{1,0:T(8,128)(2,1)}, u32[]{:S(2)}) copy-start(bf16[512,2048]{1,0:T(8,128)(2,1)} %copy-done.11) | copy-start | bytes 6291460
  96.9 9.6 %collective-permute-start.13 = (bf16[512,512]{1,0:T(8,128)(2,1)S(1)}, bf16[512,512]{1,0:T(8,128)(2,1)S(1)}, u32[]{:S(2)}, u32[]{:S(2)}) collective-permute-start(bf16[512,512]{1,0:T(8,128)(2,1)S(1)} %fusion.17), channel_id=1, source_target_pairs={{0,2},{2,0},{4,6},{6,4},{1,3},{3,1},{5,7},{7,5},{8,10},{10,8},{12,... | collective-permute-start | bytes 1572872 | tf_op jit(solution)/shard_map/ppermute | solution.py:31
  (1 other events, 1.0 us)

commit v2 on v1

v2 whole, which is shorter than its diff:
```python
import functools

import jax
import jax.numpy as jnp
from jax import lax
from jax.experimental import pallas as pl
from jax.experimental.pallas import tpu as pltpu
from jax.sharding import PartitionSpec as P

DH = 256
BLOCK = 512
TILE = 256
FINE = 32
VMEM_LIMIT = 14 * 1024 * 1024
F32 = jnp.float32
BF16 = jnp.bfloat16


def mm(left, right):
    return jnp.dot(left, right, preferred_element_type=F32)


def mm_nt(left, right):
    return lax.dot_general(left, right, (((1,), (1,)), ((), ())), preferred_element_type=F32)


def mm_tn(left, right):
    return lax.dot_general(left, right, (((0,), (0,)), ((), ())), preferred_element_type=F32)


def swap(value, axis, mask):
    size = lax.axis_size(axis)
    return lax.ppermute(value, axis, [(place, place ^ mask) for place in range(size)])


def kernel_call(kernel, outs, operands, scalars, name, flops, transcendentals=0):
    arrays = [pltpu.with_memory_space_constraint(array, pltpu.VMEM) for array in operands]
    moved = sum(array.size * array.dtype.itemsize for array in operands)
    return pl.pallas_call(
        kernel,
        in_specs=[pl.BlockSpec(memory_space=pltpu.SMEM)] * len(scalars)
        + [pl.BlockSpec(memory_space=pltpu.VMEM)] * len(operands),
        out_specs=[pl.BlockSpec(memory_space=pltpu.VMEM)] * len(outs),
        out_shape=[pltpu.VMEM(shape, dtype) for shape, dtype in outs],
        compiler_params=pltpu.CompilerParams(vmem_limit_bytes=VMEM_LIMIT),
        cost_estimate=pl.CostEstimate(
            flops=flops, bytes_accessed=moved, transcendentals=transcendentals
        ),
        name=name,
    )(*scalars, *arrays)


def turned(values, cosine, sine):
    half = DH // 2
    parts = []
    for start in range(0, values.shape[1], DH):
        low = values[:, start : start + half]
        high = values[:, start + half : start + DH]
        parts.append((low * cosine - high * sine).astype(BF16))
        parts.append((high * cosine + low * sine).astype(BF16))
    return jnp.concatenate(parts, axis=1)


def angles(coarse, fine, first, count):
    at = first // FINE
    far = coarse[:, pl.ds(at, count // FINE), :]
    near = fine[...]
    cos_c, sin_c = far[0][:, None, :], far[1][:, None, :]
    cos_f, sin_f = near[0][None], near[1][None]
    cosine = cos_c * cos_f - sin_c * sin_f
    sine = sin_c * cos_f + cos_c * sin_f
    return cosine.reshape(count, DH // 2), sine.reshape(count, DH // 2)


def half_of(x, first, count, index, part):
    return x[pl.ds(first, count), pl.ds(pl.multiple_of(index * part, part), part)]


def key_value_own_kernel(where, x, wk, wv, acc_k, acc_v):
    part = wk.shape[0]
    core = where[0]

    def step(tile, carry):
        first = pl.multiple_of(tile * TILE, TILE)
        rows = half_of(x, first, TILE, core, part)
        acc_k[pl.ds(first, TILE), :] = mm(rows, wk[...])
        acc_v[pl.ds(first, TILE), :] = mm(rows, wv[...])
        return carry

    lax.fori_loop(0, x.shape[0] // TILE, step, 0)


def key_value_kernel(
    heads, where, x, wk, wv, acc_k, acc_v, coarse, fine, decay, k_out, v_out, before_out, state_out, sent_out
):
    part = wk.shape[0]
    far = 1 - where[0]
    state_out[...] = jnp.zeros_like(state_out)

    def block_step(block, carry):
        start = pl.multiple_of(block * BLOCK, BLOCK)
        columns = decay[:, pl.ds(start, BLOCK)].T
        ending = columns[BLOCK - 1 : BLOCK, :]
        faded = jnp.exp(ending - columns)
        updates = [None] * heads
        for piece in range(BLOCK // TILE):
            first = pl.multiple_of(start + piece * TILE, TILE)
            at = pl.ds(first, TILE)
            rows = half_of(x, first, TILE, far, part)
            cosine, sine = angles(coarse, fine, first, TILE)
            keys = turned(acc_k[at, :] + mm(rows, wk[...]), cosine, sine)
            values = (acc_v[at, :] + mm(rows, wv[...])).astype(BF16)
            k_out[at, :] = keys
            v_out[at, :] = values
            for head in range(heads):
                span = slice(head * DH, (head + 1) * DH)
                fade = faded[piece * TILE : (piece + 1) * TILE, head : head + 1]
                weighted = (keys[:, span].astype(F32) * fade).astype(BF16)
                update = mm_tn(weighted, values[:, span])
                updates[head] = update if piece == 0 else updates[head] + update
        for head in range(heads):
            old = state_out[head]
            before_out[block, head] = old.astype(BF16)
            state_out[head] = jnp.exp(ending[:, head : head + 1]) * old + updates[head]
        return carry

    lax.fori_loop(0, x.shape[0] // BLOCK, block_step, 0)
    sent_out[...] = state_out[...].astype(BF16)


def query_gate_kernel(
    heads, where, x, wq, wq_far, wg, wg_far, coarse, fine, decay, k, v, q_out, g_out, intra_out
):
    part = wq.shape[0]
    core = where[0]

    def block_step(block, carry):
        start = pl.multiple_of(block * BLOCK, BLOCK)
        lines = decay[:, pl.ds(start, BLOCK)]
        columns = lines.T
        for piece in range(BLOCK // TILE):
            low, last = piece * TILE, (piece + 1) * TILE
            first = pl.multiple_of(start + low, TILE)
            at = pl.ds(first, TILE)
            own = half_of(x, first, TILE, core, part)
            far = half_of(x, first, TILE, 1 - core, part)
            cosine, sine = angles(coarse, fine, first, TILE)
            queries = turned(mm(own, wq[...]) + mm(far, wq_far[...]), cosine, sine)
            q_out[at, :] = queries
            g_out[at, :] = (mm(own, wg[...]) + mm(far, wg_far[...])).astype(BF16)
            place_t = lax.broadcasted_iota(jnp.int32, (TILE, last), 0) + low
            place_s = lax.broadcasted_iota(jnp.int32, (TILE, last), 1)
            causal = place_t >= place_s
            for head in range(heads):
                span = slice(head * DH, (head + 1) * DH)
                scores = mm_nt(queries[:, span], k[pl.ds(start, last), span])
                differ = columns[low:last, head : head + 1] - lines[head : head + 1, :last]
                weights = jnp.where(causal, jnp.exp(jnp.where(causal, differ, 0.0)), 0.0)
                intra_out[at, span] = mm((scores * weights).astype(BF16), v[pl.ds(start, last), span])
        return carry

    lax.fori_loop(0, x.shape[0] // BLOCK, block_step, 0)


def hidden_kernel(heads, block, scale, q, gate, intra, decay, entering, before, out):
    start = block * BLOCK
    columns = jnp.exp(decay[:, start : start + BLOCK].T)
    for head in range(heads):
        span = slice(head * DH, (head + 1) * DH)
        prior = scale[block, head] * entering[head].astype(F32) + before[block, head].astype(F32)
        prior = prior.astype(BF16)
        for low in range(0, BLOCK, TILE):
            at = slice(start + low, start + low + TILE)
            inter = columns[low : low + TILE, head : head + 1] * mm(q[at, span], prior)
            retained = intra[at, span] + inter
            center = retained - jnp.mean(retained, axis=1, keepdims=True)
            spread = jnp.mean(center * center, axis=1, keepdims=True)
            value = gate[at, span].astype(F32)
            silu = value / (1.0 + jnp.exp(-value))
            out[low : low + TILE, span] = (silu * center * lax.rsqrt(spread + 1e-5)).astype(BF16)


def column_of(first, second, is_first, index, cols):
    at = pl.ds(pl.multiple_of(index * cols, cols), cols)
    return jnp.where(is_first, first[:, at], second[:, at])


def product_kernel(parts, where, *refs):
    out = refs[-1]
    cols = out.shape[1]
    total = None
    for number, (half, index) in enumerate(parts):
        rows, first, second = refs[3 * number : 3 * number + 3]
        weight = column_of(first, second, where[half] == 1, where[index], cols)
        term = mm(rows[...], weight)
        total = term if total is None else total + term
    out[...] = total.astype(out.dtype)


def finish_kernel(*refs):
    out = refs[-1]
    count = (len(refs) - 1) // 2
    for block in range(count):
        value = refs[2 * block][...] + refs[2 * block + 1][...].astype(F32)
        out[0, block * BLOCK : (block + 1) * BLOCK, :] = value.astype(BF16)


def turn_tables(row_count):
    half = DH // 2
    index_row = jnp.arange(half).astype(F32)
    frequency = jnp.power(F32(10000.0), -index_row / half)
    offset = lax.axis_index("ctx") * row_count
    coarse_at = (offset + FINE * jnp.arange(row_count // FINE)).astype(F32)
    fine_at = jnp.arange(FINE).astype(F32)
    coarse = coarse_at[:, None] * frequency[None, :]
    fine = fine_at[:, None] * frequency[None, :]
    return jnp.stack([jnp.cos(coarse), jnp.sin(coarse)]), jnp.stack([jnp.cos(fine), jnp.sin(fine)])


def on_device(tokens, query_weight, key_weight, value_weight, gate_weight, out_weight, log_decay):
    x = tokens[0]
    rows, width = x.shape
    part, cols = query_weight.shape
    heads = cols // DH
    blocks = rows // BLOCK
    ctx = lax.axis_size("ctx")
    tp, cores = lax.axis_size("tp"), lax.axis_size("fsdp")
    core = lax.axis_index("fsdp")
    place = lax.axis_index("tp")
    assert tp == 4 and cores == 2
    high, low = place // 2, place % 2
    near_mask, far_mask = 1, 2

    key_far = swap(key_weight, "fsdp", 1)
    value_far = swap(value_weight, "fsdp", 1)
    near_first = swap(out_weight, "tp", near_mask)
    high_pairs = [
        ((at ^ far_mask) * cores + at // 2, at * cores + at // 2) for at in range(tp)
    ]
    high_pass = lax.ppermute(out_weight, ("tp", "fsdp"), high_pairs)
    query_far = swap(query_weight, "fsdp", 1)
    gate_far = swap(gate_weight, "fsdp", 1)
    own_second = swap(out_weight, "fsdp", 1)
    near_second = swap(near_first, "fsdp", 1)
    core_pairs = [(at * cores + at // 2, at * cores + 1 - at // 2) for at in range(tp)]
    high_other = lax.ppermute(high_pass, ("tp", "fsdp"), core_pairs)

    lower = (jnp.arange(BLOCK)[:, None] <= jnp.arange(BLOCK)[None, :]).astype(F32)
    per_block = log_decay[0].T.reshape(heads * blocks, BLOCK)
    sums = jnp.dot(per_block, lower, precision=lax.Precision.HIGHEST).reshape(heads, blocks, BLOCK)
    ending = sums[:, :, -1]
    decay_rows = jnp.pad(sums.reshape(heads, rows), ((0, 8 - heads), (0, 0)))
    earlier = jnp.cumsum(ending, axis=1) - ending
    block_scale = jnp.exp(earlier).T
    total = jnp.sum(ending, axis=1)
    coarse, fine = turn_tables(rows)

    same_half = (core == high).astype(jnp.int32)
    where = jnp.stack([core, same_half, 1 - same_half, low, 1 - low]).astype(jnp.int32)
    at_same, at_other, at_low, at_flip = 1, 2, 3, 4
    product = 2 * rows * part * cols

    acc_k, acc_v = kernel_call(
        key_value_own_kernel,
        [((rows, cols), F32)] * 2,
        [x, key_weight, value_weight],
        [where],
        "key_value_own",
        2 * product,
    )
    keys, values, before, state, sent = kernel_call(
        functools.partial(key_value_kernel, heads),
        [
            ((rows, cols), BF16),
            ((rows, cols), BF16),
            ((blocks, heads, DH, DH), BF16),
            ((heads, DH, DH), F32),
            ((heads, DH, DH), BF16),
        ],
        [x, key_far, value_far, acc_k, acc_v, coarse, fine, decay_rows],
        [where],
        "key_value",
        2 * product,
    )

    entering = jnp.zeros_like(state)
    entering_log = jnp.zeros_like(total)
    window, window_log, message = state, total, sent
    hop = 1
    while hop < ctx:
        pairs = [(source, source + hop) for source in range(ctx - hop)]
        got = lax.ppermute(message, "ctx", pairs).astype(F32)
        entering = entering + jnp.exp(entering_log)[:, None, None] * got
        if 2 * hop < ctx:
            got_log = lax.ppermute(window_log, "ctx", pairs)
            window = window + jnp.exp(window_log)[:, None, None] * got
            message = window.astype(BF16)
            entering_log = entering_log + got_log
            window_log = window_log + got_log
        hop *= 2
    entering = entering.astype(BF16)

    queries, gates, intra = kernel_call(
        functools.partial(query_gate_kernel, heads),
        [((rows, cols), BF16), ((rows, cols), BF16), ((rows, cols), F32)],
        [x, query_weight, query_far, gate_weight, gate_far, coarse, fine, decay_rows, keys, values],
        [where],
        "query_gate",
        4 * product + 4 * rows * BLOCK * cols,
        rows * BLOCK * heads,
    )

    hidden = [
        kernel_call(
            functools.partial(hidden_kernel, heads, block),
            [((BLOCK, cols), BF16)],
            [queries, gates, intra, decay_rows, entering, before],
            [block_scale],
            "hidden",
            2 * BLOCK * DH * cols,
            BLOCK * cols,
        )[0]
        for block in range(blocks)
    ]
    own_pair = (out_weight, own_second)
    plans = [
        (near_mask, far_mask, (near_first, near_second), (at_other, at_low), (at_same, at_low)),
        (far_mask, near_mask, (high_pass, high_other), (at_same, at_flip), (at_same, at_low)),
    ]
    keeps = []
    for block in range(blocks):
        gather_at, sum_at, pair, give_at, keep_at = plans[block % 2]
        far = swap(hidden[block], "tp", gather_at)
        flops = 4 * BLOCK * cols * cols

        def product_of(at, dtype, name):
            return kernel_call(
                functools.partial(product_kernel, (at, at)),
                [((BLOCK, cols), dtype)],
                [hidden[block], *own_pair, far, *pair],
                [where],
                name,
                flops,
            )[0]

        give = product_of(give_at, BF16, "give")
        keep = product_of(keep_at, F32, "keep")
        keeps += [keep, swap(give, "tp", sum_at)]
    arrays = [pltpu.with_memory_space_constraint(array, pltpu.VMEM) for array in keeps]
    return pl.pallas_call(
        finish_kernel,
        in_specs=[pl.BlockSpec(memory_space=pltpu.VMEM)] * len(arrays),
        out_specs=pl.BlockSpec(memory_space=pltpu.VMEM),
        out_shape=jax.ShapeDtypeStruct((1, rows, cols), BF16),
        compiler_params=pltpu.CompilerParams(vmem_limit_bytes=VMEM_LIMIT),
        name="finish",
    )(*arrays)


def solution(mesh):
    in_specs = (
        P("fsdp", "ctx", None),
        P("fsdp", "tp"),
        P("fsdp", "tp"),
        P("fsdp", "tp"),
        P("fsdp", "tp"),
        P("tp", "fsdp"),
        P("fsdp", "ctx", "tp"),
    )
    out_specs = P("fsdp", "ctx", "tp")
    return jax.shard_map(
        on_device, mesh=mesh, in_specs=in_specs, out_specs=out_specs, check_vma=False
    )
```

time: 109 us -> 104 us (0.954)
  the two profiles are of different devices: /device:TPU:24 before, /device:TPU:0 now
where the time goes in v2:
time: 104 us; the launch traced here: 103 us
  starting transfers between devices  26 us (25%)
  local copies, waits for them, and re-layouts  25.8 us (25%)
  Pallas kernels  25.4 us (24%)
  waiting for transfers between devices  22.8 us (22%)
  other arithmetic  2.77 us (3%)
    unnamed x44, local copies, waits for them, and re-layouts  25.5 us
    pallas_call x9, Pallas kernels, kernel_call(): pl.pallas_call(kernel, in_specs=[pl.BlockSpec(memory_space=pltpu.SMEM)] *...  24.2 us
    ppermute x11, waiting for transfers between devices, swap(): lax.ppermute(value, axis, [(place, place ^ mask) for place in range(size)])  20.7 us
    ppermute x2, starting transfers between devices, on_device(): got = lax.ppermute(message, 'ctx', pairs).astype(F32)  9.69 us
    ppermute x11, starting transfers between devices, swap(): lax.ppermute(value, axis, [(place, place ^ mask) for place in range(size)])  9.1 us
    ppermute x1, starting transfers between devices, on_device(): got_log = lax.ppermute(window_log, 'ctx', pairs)  3.47 us
    ppermute x1, starting transfers between devices, on_device(): high_other = lax.ppermute(high_pass, ('tp', 'fsdp'), core_pairs)  2.45 us
  transfers between devices with their start and end apart: 16, of which 5 were waited for; matrix products, arithmetic and copies ran while one was open for 3% of the time, Pallas kernels for 23%

profile of v2, /device:TPU:0, one launch (start us, length us, event | category | flops | bytes accessed | tf_op | source)
XLA Modules:
  0.0 103.2 jit_solution(4460155914476632972)
XLA Ops:
  0.5 1.3 %collective-permute-start.13 = (bf16[512,1024]{1,0:T(8,128)(2,1)}, bf16[512,1024]{1,0:T(8,128)(2,1)S(1)}, u32[]{:S(2)}, u32[]{:S(2)}) collective-permute-start(bf16[512,1024]{1,0:T(8,128)(2,1)} %refs_1_.7), channel_id=1, source_target_pairs={{4,0},{6,2},{1,5},{3,7},{12,8},{14,10},{9,13},{11,15},{20,16},{22,... | collective-permute-start | bytes 3145736 | tf_op jit(solution)/shard_map/ppermute | solution.py:240
  1.7 2.6 %collective-permute-start.9 = (bf16[512,1024]{1,0:T(8,128)(2,1)}, bf16[512,1024]{1,0:T(8,128)(2,1)S(1)}, u32[]{:S(2)}, u32[]{:S(2)}) collective-permute-start(bf16[512,1024]{1,0:T(8,128)(2,1)} %refs_1_.7), channel_id=1, source_target_pairs={{0,2},{2,0},{4,6},{6,4},{1,3},{3,1},{5,7},{7,5},{8,10},{10,8},{12,... | collective-permute-start | bytes 3145736 | tf_op jit(solution)/shard_map/ppermute | solution.py:33
  4.3 2.1 %collective-permute-start.3 = (bf16[1024,512]{1,0:T(8,128)(2,1)}, bf16[1024,512]{1,0:T(8,128)(2,1)}, u32[]{:S(2)}, u32[]{:S(2)}) collective-permute-start(bf16[1024,512]{1,0:T(8,128)(2,1)} %wv.1), channel_id=1, source_target_pairs={{0,1},{1,0},{2,3},{3,2},{4,5},{5,4},{6,7},{7,6},{8,9},{9,8},{10,11... | collective-permute-start | bytes 3145736 | tf_op jit(solution)/shard_map/ppermute | solution.py:33
  6.5 2.2 %copy-done.1 = bf16[1,1024,2048]{2,1,0:T(8,128)(2,1)S(1)} copy-done((bf16[1,1024,2048]{2,1,0:T(8,128)(2,1)S(1)}, bf16[1,1024,2048]{2,1,0:T(8,128)(2,1)}, u32[]{:S(2)}) %copy-start.1) | copy-done | bytes 4194328
  8.7 1.2 %copy-done.13 = bf16[1024,512]{1,0:T(8,128)(2,1)S(1)} copy-done((bf16[1024,512]{1,0:T(8,128)(2,1)S(1)}, bf16[1024,512]{1,0:T(8,128)(2,1)}, u32[]{:S(2)}) %copy-start.13) | copy-done | bytes 1048600
  9.9 1.2 %copy-done.14 = bf16[1024,512]{1,0:T(8,128)(2,1)S(1)} copy-done((bf16[1024,512]{1,0:T(8,128)(2,1)S(1)}, bf16[1024,512]{1,0:T(8,128)(2,1)}, u32[]{:S(2)}) %copy-start.14) | copy-done | bytes 1048600
  11.2 3.4 %key_value_own.1 = (f32[1024,512]{1,0:T(8,128)S(1)}, f32[1024,512]{1,0:T(8,128)S(1)}) custom-call(s32[5]{0:T(128)S(1)} %stack.33.where, bf16[1024,2048]{1,0:T(8,128)(2,1)S(1)} %bitcast.17, bf16[1024,512]{1,0:T(8,128)(2,1)S(1)} %copy-done.13, bf16[1024,512]{1,0:T(8,128)(2,1)S(1)} %copy-done.14), custom_call_target="tpu_custom_call" | custom-call | flops 2147483648 | bytes 6291456 | tf_op jit(solution)/shard_map/key_value_own/pallas_call | solution.py:39
  14.6 1.4 %copy-done.6 = f32[1024,512]{1,0:T(8,128)} copy-done((f32[1024,512]{1,0:T(8,128)}, f32[1024,512]{1,0:T(8,128)S(1)}, u32[]{:S(2)}) %copy-start.6) | copy-done | bytes 2097176
  15.9 1.3 %copy-done.8 = f32[1024,512]{1,0:T(8,128)} copy-done((f32[1024,512]{1,0:T(8,128)}, f32[1024,512]{1,0:T(8,128)S(1)}, u32[]{:S(2)}) %copy-start.8) | copy-done | bytes 2097176
  19.5 3.5 %collective-permute-start.5 = (f32[2]{0:T(128)S(1)}, f32[2]{0:T(128)S(1)}, u32[]{:S(2)}, u32[]{:S(2)}) collective-permute-start(f32[2]{0:T(128)S(1)} %get-tuple-element.25), channel_id=1, source_target_pairs={{0,8},{8,16},{16,24},{1,9},{9,17},{17,25},{2,10},{10,18},{18,26},{... | collective-permute-start | bytes 32 | tf_op jit(solution)/shard_map/ppermute | solution.py:295
  23.0 2.2 %copy-done.2 = bf16[1,1024,2048]{2,1,0:T(8,128)(2,1)S(1)} copy-done((bf16[1,1024,2048]{2,1,0:T(8,128)(2,1)S(1)}, bf16[1,1024,2048]{2,1,0:T(8,128)(2,1)}, u32[]{:S(2)}) %copy-start.2) | copy-done | bytes 4194328
  25.2 1.6 %copy-done.7 = f32[1024,512]{1,0:T(8,128)S(1)} copy-done((f32[1024,512]{1,0:T(8,128)S(1)}, f32[1024,512]{1,0:T(8,128)}, u32[]{:S(2)}) %copy-start.7) | copy-done | bytes 2097176
  26.8 1.6 %copy-done.9 = f32[1024,512]{1,0:T(8,128)S(1)} copy-done((f32[1024,512]{1,0:T(8,128)S(1)}, f32[1024,512]{1,0:T(8,128)}, u32[]{:S(2)}) %copy-start.9) | copy-done | bytes 2097176
  28.4 1.2 %copy-done.11 = bf16[1024,512]{1,0:T(8,128)(2,1)S(1)} copy-done((bf16[1024,512]{1,0:T(8,128)(2,1)S(1)}, bf16[1024,512]{1,0:T(8,128)(2,1)}, u32[]{:S(2)}) %copy-start.11) | copy-done | bytes 1048600
  29.6 4.7 %key_value.1 = (bf16[1024,512]{1,0:T(8,128)(2,1)S(1)}, bf16[1024,512]{1,0:T(8,128)(2,1)S(1)}, bf16[2,2,256,256]{3,2,1,0:T(8,128)(2,1)S(1)}, f32[2,256,256]{2,1,0:T(8,128)S(1)}, bf16[2,256,256]{2,1,0:T(8,128)(2,1)S(1)}) custom-call(s32[5]{0:T(128)S(1)} %stack.33.where, bf16[1024,2048]{1,0:T(8,128)(2,1)S(1)} %bitcast.18, bf16[1024,512]{1,0:T(8,128)(2,1)S(1)} %copy-done.11, ...), custom_call_target="tpu_custom_call" | custom-call | flops 2147483648 | bytes 10584064 | tf_op jit(solution)/shard_map/key_value/pallas_call | solution.py:39
  37.8 4.2 %collective-permute-start.4 = (bf16[2,256,256]{2,1,0:T(8,128)(2,1)S(1)}, bf16[2,256,256]{2,1,0:T(8,128)(2,1)}, u32[]{:S(2)}, u32[]{:S(2)}) collective-permute-start(bf16[2,256,256]{2,1,0:T(8,128)(2,1)S(1)} %get-tuple-element.22), channel_id=1, source_target_pairs={{0,8},{8,16},{16,24},{1,9},{9,17},{17,25},{2,10},{10,18},{18,26},{... | collective-permute-start | bytes 786440 | tf_op jit(solution)/shard_map/ppermute | solution.py:292
  42.3 2.4 %collective-permute-start.14 = (bf16[512,1024]{1,0:T(8,128)(2,1)S(1)}, bf16[512,1024]{1,0:T(8,128)(2,1)S(1)}, u32[]{:S(2)}, u32[]{:S(2)}) collective-permute-start(bf16[512,1024]{1,0:T(8,128)(2,1)S(1)} %collective-permute-done.13.refs_4_), channel_id=1, source_target_pairs={{0,1},{2,3},{5,4},{7,6},{8,9},{10,11},{13,12},{15,14},{16,17},{18,... | collective-permute-start | bytes 3145736 | tf_op jit(solution)/shard_map/ppermute | solution.py:246
  44.7 2.0 %collective-permute-done.4 = bf16[2,256,256]{2,1,0:T(8,128)(2,1)} collective-permute-done((bf16[2,256,256]{2,1,0:T(8,128)(2,1)S(1)}, bf16[2,256,256]{2,1,0:T(8,128)(2,1)}, u32[]{:S(2)}, u32[]{:S(2)}) %collective-permute-start.4) | collective-permute-done | bytes 262176 | tf_op jit(solution)/shard_map/ppermute | solution.py:292
  46.8 1.2 %fusion.1 = bf16[2,256,256]{2,1,0:T(8,128)(2,1)S(1)} fusion(f32[2,256,256]{2,1,0:T(8,128)} %copy-done.12, bf16[2,256,256]{2,1,0:T(8,128)(2,1)} %collective-permute-done.4, f32[2]{0:T(128)S(1)} %exp.15), kind=kLoop, calls=%fused_computation.5 | loop fusion | flops 524288 | bytes 1048584 | tf_op jit(solution)/shard_map/convert_element_type | solution.py:297
  48.0 5.5 %collective-permute-start.6 = (bf16[2,256,256]{2,1,0:T(8,128)(2,1)S(1)}, bf16[2,256,256]{2,1,0:T(8,128)(2,1)S(1)}, u32[]{:S(2)}, u32[]{:S(2)}) collective-permute-start(bf16[2,256,256]{2,1,0:T(8,128)(2,1)S(1)} %fusion.1), channel_id=1, source_target_pairs={{0,16},{8,24},{1,17},{9,25},{2,18},{10,26},{3,19},{11,27},{4,20},{... | collective-permute-start | bytes 786440 | tf_op jit(solution)/shard_map/ppermute | solution.py:292
  53.6 2.2 %copy-done.3 = bf16[1,1024,2048]{2,1,0:T(8,128)(2,1)S(1)} copy-done((bf16[1,1024,2048]{2,1,0:T(8,128)(2,1)S(1)}, bf16[1,1024,2048]{2,1,0:T(8,128)(2,1)}, u32[]{:S(2)}) %copy-start.3) | copy-done | bytes 4194328
  59.4 1.2 %copy-done.20 = bf16[1024,512]{1,0:T(8,128)(2,1)S(1)} copy-done((bf16[1024,512]{1,0:T(8,128)(2,1)S(1)}, bf16[1024,512]{1,0:T(8,128)(2,1)}, u32[]{:S(2)}) %copy-start.20) | copy-done | bytes 1048600
  60.6 7.5 %query_gate.1 = (bf16[1024,512]{1,0:T(8,128)(2,1)S(1)}, bf16[1024,512]{1,0:T(8,128)(2,1)S(1)}, f32[1024,512]{1,0:T(8,128)S(1)}) custom-call(s32[5]{0:T(128)S(1)} %stack.33.where, bf16[1024,2048]{1,0:T(8,128)(2,1)S(1)} %bitcast.19, bf16[1024,512]{1,0:T(8,128)(2,1)S(1)} %copy-done.15, bf16[1024,512]{1,0:T(8,128)(2,1)} %collective-permute-done.wq_far, ...), custom_call_target="tpu_custom_call" | custom-call | flops 5368709120 | bytes 10584064 | tf_op jit(solution)/shard_map/query_gate/pallas_call | solution.py:39
  69.3 1.7 %hidden.3.refs_0_ = bf16[512,512]{1,0:T(8,128)(2,1)S(1)} custom-call(f32[2,2]{1,0:T(2,128)S(1)} %exponential_bitcast_fusion.scale, bf16[1024,512]{1,0:T(8,128)(2,1)S(1)} %get-tuple-element.19.q, bf16[1024,512]{1,0:T(8,128)(2,1)S(1)} %get-tuple-element.20.gate, f32[1024,512]{1,0:T(8,128)S(1)} %get-tuple-element.21.intra, f32[8,1024]{1,0:T(8,128)S(1)} %pad.4.decay, ...), custom_call_target="tpu_custom_call" | custom-call | flops 134217728 | bytes 5013504 | tf_op jit(solution)/shard_map/hidden/pallas_call | solution.py:39
  72.1 1.7 %hidden.2.refs_0_ = bf16[512,512]{1,0:T(8,128)(2,1)S(1)} custom-call(f32[2,2]{1,0:T(2,128)S(1)} %exponential_bitcast_fusion.scale, bf16[1024,512]{1,0:T(8,128)(2,1)S(1)} %get-tuple-element.19.q, bf16[1024,512]{1,0:T(8,128)(2,1)S(1)} %get-tuple-element.20.gate, f32[1024,512]{1,0:T(8,128)S(1)} %get-tuple-element.21.intra, f32[8,1024]{1,0:T(8,128)S(1)} %pad.4.decay, ...), custom_call_target="tpu_custom_call" | custom-call | flops 134217728 | bytes 5013504 | tf_op jit(solution)/shard_map/hidden/pallas_call | solution.py:39
  74.5 10.6 %collective-permute-done.12.refs_3_ = bf16[512,512]{1,0:T(8,128)(2,1)S(1)} collective-permute-done((bf16[512,512]{1,0:T(8,128)(2,1)S(1)}, bf16[512,512]{1,0:T(8,128)(2,1)S(1)}, u32[]{:S(2)}, u32[]{:S(2)}) %collective-permute-start.12) | collective-permute-done | bytes 524320 | tf_op jit(solution)/shard_map/ppermute | solution.py:33
  85.1 1.3 %give.3 = bf16[512,512]{1,0:T(8,128)(2,1)S(1)} custom-call(s32[5]{0:T(128)S(1)} %stack.33.where, bf16[512,512]{1,0:T(8,128)(2,1)S(1)} %hidden.3.refs_0_, bf16[512,1024]{1,0:T(8,128)(2,1)S(1)} %copy-done, bf16[512,1024]{1,0:T(8,128)(2,1)S(1)} %collective-permute-done.7.refs_2_, bf16[512,512]{1,0:T(8,128)(2,1)S(1)} %collective-permute-done.12.refs_3_, ...), custom_call_target="tpu_custom_call" | custom-call | flops 536870912 | bytes 5242880 | tf_op jit(solution)/shard_map/give/pallas_call | solution.py:39
  87.7 1.3 %give.2 = bf16[512,512]{1,0:T(8,128)(2,1)S(1)} custom-call(s32[5]{0:T(128)S(1)} %stack.33.where, bf16[512,512]{1,0:T(8,128)(2,1)S(1)} %hidden.2.refs_0_, bf16[512,1024]{1,0:T(8,128)(2,1)S(1)} %copy-done, bf16[512,1024]{1,0:T(8,128)(2,1)S(1)} %collective-permute-done.7.refs_2_, bf16[512,512]{1,0:T(8,128)(2,1)S(1)} %collective-permute-done.8.refs_3_, ...), custom_call_target="tpu_custom_call" | custom-call | flops 536870912 | bytes 5242880 | tf_op jit(solution)/shard_map/give/pallas_call | solution.py:39
  90.1 1.3 %keep.3.refs_2_ = f32[512,512]{1,0:T(8,128)S(1)} custom-call(s32[5]{0:T(128)S(1)} %stack.33.where, bf16[512,512]{1,0:T(8,128)(2,1)S(1)} %hidden.3.refs_0_, bf16[512,1024]{1,0:T(8,128)(2,1)S(1)} %copy-done, bf16[512,1024]{1,0:T(8,128)(2,1)S(1)} %collective-permute-done.7.refs_2_, bf16[512,512]{1,0:T(8,128)(2,1)S(1)} %collective-permute-done.12.refs_3_, ...), custom_call_target="tpu_custom_call" | custom-call | flops 536870912 | bytes 5242880 | tf_op jit(solution)/shard_map/keep/pallas_call | solution.py:39
  91.3 1.3 %keep.2.refs_0_ = f32[512,512]{1,0:T(8,128)S(1)} custom-call(s32[5]{0:T(128)S(1)} %stack.33.where, bf16[512,512]{1,0:T(8,128)(2,1)S(1)} %hidden.2.refs_0_, bf16[512,1024]{1,0:T(8,128)(2,1)S(1)} %copy-done, bf16[512,1024]{1,0:T(8,128)(2,1)S(1)} %collective-permute-done.7.refs_2_, bf16[512,512]{1,0:T(8,128)(2,1)S(1)} %collective-permute-done.8.refs_3_, ...), custom_call_target="tpu_custom_call" | custom-call | flops 536870912 | bytes 5242880 | tf_op jit(solution)/shard_map/keep/pallas_call | solution.py:39
  92.6 7.1 %collective-permute-done.15.refs_3_ = bf16[512,512]{1,0:T(8,128)(2,1)S(1)} collective-permute-done((bf16[512,512]{1,0:T(8,128)(2,1)S(1)}, bf16[512,512]{1,0:T(8,128)(2,1)S(1)}, u32[]{:S(2)}, u32[]{:S(2)}) %collective-permute-start.15) | collective-permute-done | bytes 524320 | tf_op jit(solution)/shard_map/ppermute | solution.py:33
  99.7 2.3 %collective-permute-done.11.refs_1_ = bf16[512,512]{1,0:T(8,128)(2,1)S(1)} collective-permute-done((bf16[512,512]{1,0:T(8,128)(2,1)S(1)}, bf16[512,512]{1,0:T(8,128)(2,1)S(1)}, u32[]{:S(2)}, u32[]{:S(2)}) %collective-permute-start.11) | collective-permute-done | bytes 524320 | tf_op jit(solution)/shard_map/ppermute | solution.py:33
  (73 shorter events, 16.6 us)
Async XLA Ops:
  0.0 17.9 %collective-permute-start.2 = (bf16[1024,512]{1,0:T(8,128)(2,1)}, bf16[1024,512]{1,0:T(8,128)(2,1)S(1)}, u32[]{:S(2)}, u32[]{:S(2)}) collective-permute-start(bf16[1024,512]{1,0:T(8,128)(2,1)} %wk.1), channel_id=1, source_target_pairs={{0,1},{1,0},{2,3},{3,2},{4,5},{5,4},{6,7},{7,6},{8,9},{9,8},{10,11... | collective-permute-start | bytes 3145736 | tf_op jit(solution)/shard_map/ppermute | solution.py:33
  0.5 41.7 %collective-permute-start.13 = (bf16[512,1024]{1,0:T(8,128)(2,1)}, bf16[512,1024]{1,0:T(8,128)(2,1)S(1)}, u32[]{:S(2)}, u32[]{:S(2)}) collective-permute-start(bf16[512,1024]{1,0:T(8,128)(2,1)} %refs_1_.7), channel_id=1, source_target_pairs={{4,0},{6,2},{1,5},{3,7},{12,8},{14,10},{9,13},{11,15},{20,16},{22,... | collective-permute-start | bytes 3145736 | tf_op jit(solution)/shard_map/ppermute | solution.py:240
  1.7 40.5 %collective-permute-start.9 = (bf16[512,1024]{1,0:T(8,128)(2,1)}, bf16[512,1024]{1,0:T(8,128)(2,1)S(1)}, u32[]{:S(2)}, u32[]{:S(2)}) collective-permute-start(bf16[512,1024]{1,0:T(8,128)(2,1)} %refs_1_.7), channel_id=1, source_target_pairs={{0,2},{2,0},{4,6},{6,4},{1,3},{3,1},{5,7},{7,5},{8,10},{10,8},{12,... | collective-permute-start | bytes 3145736 | tf_op jit(solution)/shard_map/ppermute | solution.py:33
  4.3 15.2 %collective-permute-start.3 = (bf16[1024,512]{1,0:T(8,128)(2,1)}, bf16[1024,512]{1,0:T(8,128)(2,1)}, u32[]{:S(2)}, u32[]{:S(2)}) collective-permute-start(bf16[1024,512]{1,0:T(8,128)(2,1)} %wv.1), channel_id=1, source_target_pairs={{0,1},{1,0},{2,3},{3,2},{4,5},{5,4},{6,7},{7,6},{8,9},{9,8},{10,11... | collective-permute-start | bytes 3145736 | tf_op jit(solution)/shard_map/ppermute | solution.py:33
  6.4 41.6 %collective-permute-start = (bf16[1024,512]{1,0:T(8,128)(2,1)}, bf16[1024,512]{1,0:T(8,128)(2,1)}, u32[]{:S(2)}, u32[]{:S(2)}) collective-permute-start(bf16[1024,512]{1,0:T(8,128)(2,1)} %wq.1), channel_id=1, source_target_pairs={{0,1},{1,0},{2,3},{3,2},{4,5},{5,4},{6,7},{7,6},{8,9},{9,8},{10,11... | collective-permute-start | bytes 3145736 | tf_op jit(solution)/shard_map/ppermute | solution.py:33
  6.5 2.2 %copy-start.1 = (bf16[1,1024,2048]{2,1,0:T(8,128)(2,1)S(1)}, bf16[1,1024,2048]{2,1,0:T(8,128)(2,1)}, u32[]{:S(2)}) copy-start(bf16[1,1024,2048]{2,1,0:T(8,128)(2,1)} %param.7) | copy-start | bytes 12582916
  8.7 1.2 %copy-start.13 = (bf16[1024,512]{1,0:T(8,128)(2,1)S(1)}, bf16[1024,512]{1,0:T(8,128)(2,1)}, u32[]{:S(2)}) copy-start(bf16[1024,512]{1,0:T(8,128)(2,1)} %wk.1) | copy-start | bytes 3145732
  9.9 1.2 %copy-start.14 = (bf16[1024,512]{1,0:T(8,128)(2,1)S(1)}, bf16[1024,512]{1,0:T(8,128)(2,1)}, u32[]{:S(2)}) copy-start(bf16[1024,512]{1,0:T(8,128)(2,1)} %wv.1) | copy-start | bytes 3145732
  11.2 6.1 %copy-start.21 = (f32[1,1024,2]{1,2,0:T(2,128)S(1)}, f32[1,1024,2]{1,2,0:T(2,128)}, u32[]{:S(2)}) copy-start(f32[1,1024,2]{1,2,0:T(2,128)} %param.13) | copy-start | bytes 24580
  14.6 1.4 %copy-start.6 = (f32[1024,512]{1,0:T(8,128)}, f32[1024,512]{1,0:T(8,128)S(1)}, u32[]{:S(2)}) copy-start(f32[1024,512]{1,0:T(8,128)S(1)} %get-tuple-element.15.acc_k) | copy-start | bytes 6291460
  15.9 1.3 %copy-start.8 = (f32[1024,512]{1,0:T(8,128)}, f32[1024,512]{1,0:T(8,128)S(1)}, u32[]{:S(2)}) copy-start(f32[1024,512]{1,0:T(8,128)S(1)} %get-tuple-element.16.acc_v) | copy-start | bytes 6291460
  18.8 34.7 %collective-permute-start.1 = (bf16[1024,512]{1,0:T(8,128)(2,1)}, bf16[1024,512]{1,0:T(8,128)(2,1)}, u32[]{:S(2)}, u32[]{:S(2)}) collective-permute-start(bf16[1024,512]{1,0:T(8,128)(2,1)} %wg.1), channel_id=1, source_target_pairs={{0,1},{1,0},{2,3},{3,2},{4,5},{5,4},{6,7},{7,6},{8,9},{9,8},{10,11... | collective-permute-start | bytes 3145736 | tf_op jit(solution)/shard_map/ppermute | solution.py:33
  19.5 18.3 %collective-permute-start.5 = (f32[2]{0:T(128)S(1)}, f32[2]{0:T(128)S(1)}, u32[]{:S(2)}, u32[]{:S(2)}) collective-permute-start(f32[2]{0:T(128)S(1)} %get-tuple-element.25), channel_id=1, source_target_pairs={{0,8},{8,16},{16,24},{1,9},{9,17},{17,25},{2,10},{10,18},{18,26},{... | collective-permute-start | bytes 32 | tf_op jit(solution)/shard_map/ppermute | solution.py:295
  23.0 2.2 %copy-start.2 = (bf16[1,1024,2048]{2,1,0:T(8,128)(2,1)S(1)}, bf16[1,1024,2048]{2,1,0:T(8,128)(2,1)}, u32[]{:S(2)}) copy-start(bf16[1,1024,2048]{2,1,0:T(8,128)(2,1)} %param.7) | copy-start | bytes 12582916
  25.2 1.6 %copy-start.7 = (f32[1024,512]{1,0:T(8,128)S(1)}, f32[1024,512]{1,0:T(8,128)}, u32[]{:S(2)}) copy-start(f32[1024,512]{1,0:T(8,128)} %copy-done.6) | copy-start | bytes 6291460
  26.8 1.6 %copy-start.9 = (f32[1024,512]{1,0:T(8,128)S(1)}, f32[1024,512]{1,0:T(8,128)}, u32[]{:S(2)}) copy-start(f32[1024,512]{1,0:T(8,128)} %copy-done.8) | copy-start | bytes 6291460
  28.4 1.2 %copy-start.11 = (bf16[1024,512]{1,0:T(8,128)(2,1)S(1)}, bf16[1024,512]{1,0:T(8,128)(2,1)}, u32[]{:S(2)}) copy-start(bf16[1024,512]{1,0:T(8,128)(2,1)} %copy-done.10) | copy-start | bytes 3145732
  29.6 12.6 %copy-start = (bf16[512,1024]{1,0:T(8,128)(2,1)S(1)}, bf16[512,1024]{1,0:T(8,128)(2,1)}, u32[]{:S(2)}) copy-start(bf16[512,1024]{1,0:T(8,128)(2,1)} %refs_1_.7) | copy-start | bytes 3145732
  37.8 8.9 %collective-permute-start.4 = (bf16[2,256,256]{2,1,0:T(8,128)(2,1)S(1)}, bf16[2,256,256]{2,1,0:T(8,128)(2,1)}, u32[]{:S(2)}, u32[]{:S(2)}) collective-permute-start(bf16[2,256,256]{2,1,0:T(8,128)(2,1)S(1)} %get-tuple-element.22), channel_id=1, source_target_pairs={{0,8},{8,16},{16,24},{1,9},{9,17},{17,25},{2,10},{10,18},{18,26},{... | collective-permute-start | bytes 786440 | tf_op jit(solution)/shard_map/ppermute | solution.py:292
  42.2 32.3 %collective-permute-start.7 = (bf16[512,1024]{1,0:T(8,128)(2,1)S(1)}, bf16[512,1024]{1,0:T(8,128)(2,1)S(1)}, u32[]{:S(2)}, u32[]{:S(2)}) collective-permute-start(bf16[512,1024]{1,0:T(8,128)(2,1)S(1)} %copy-done), channel_id=1, source_target_pairs={{0,1},{1,0},{2,3},{3,2},{4,5},{5,4},{6,7},{7,6},{8,9},{9,8},{10,11... | collective-permute-start | bytes 3145736 | tf_op jit(solution)/shard_map/ppermute | solution.py:33
  42.3 42.9 %collective-permute-start.14 = (bf16[512,1024]{1,0:T(8,128)(2,1)S(1)}, bf16[512,1024]{1,0:T(8,128)(2,1)S(1)}, u32[]{:S(2)}, u32[]{:S(2)}) collective-permute-start(bf16[512,1024]{1,0:T(8,128)(2,1)S(1)} %collective-permute-done.13.refs_4_), channel_id=1, source_target_pairs={{0,1},{2,3},{5,4},{7,6},{8,9},{10,11},{13,12},{15,14},{16,17},{18,... | collective-permute-start | bytes 3145736 | tf_op jit(solution)/shard_map/ppermute | solution.py:246
  46.8 41.0 %collective-permute-start.10 = (bf16[512,1024]{1,0:T(8,128)(2,1)S(1)}, bf16[512,1024]{1,0:T(8,128)(2,1)S(1)}, u32[]{:S(2)}, u32[]{:S(2)}) collective-permute-start(bf16[512,1024]{1,0:T(8,128)(2,1)S(1)} %collective-permute-done.9.refs_4_), channel_id=1, source_target_pairs={{0,1},{1,0},{2,3},{3,2},{4,5},{5,4},{6,7},{7,6},{8,9},{9,8},{10,11... | collective-permute-start | bytes 3145736 | tf_op jit(solution)/shard_map/ppermute | solution.py:33
  48.0 20.1 %collective-permute-start.6 = (bf16[2,256,256]{2,1,0:T(8,128)(2,1)S(1)}, bf16[2,256,256]{2,1,0:T(8,128)(2,1)S(1)}, u32[]{:S(2)}, u32[]{:S(2)}) collective-permute-start(bf16[2,256,256]{2,1,0:T(8,128)(2,1)S(1)} %fusion.1), channel_id=1, source_target_pairs={{0,16},{8,24},{1,17},{9,25},{2,18},{10,26},{3,19},{11,27},{4,20},{... | collective-permute-start | bytes 786440 | tf_op jit(solution)/shard_map/ppermute | solution.py:292
  53.6 2.2 %copy-start.3 = (bf16[1,1024,2048]{2,1,0:T(8,128)(2,1)S(1)}, bf16[1,1024,2048]{2,1,0:T(8,128)(2,1)}, u32[]{:S(2)}) copy-start(bf16[1,1024,2048]{2,1,0:T(8,128)(2,1)} %param.7) | copy-start | bytes 12582916
  55.7 1.2 %copy-start.15 = (bf16[1024,512]{1,0:T(8,128)(2,1)S(1)}, bf16[1024,512]{1,0:T(8,128)(2,1)}, u32[]{:S(2)}) copy-start(bf16[1024,512]{1,0:T(8,128)(2,1)} %wq.1) | copy-start | bytes 3145732
  57.0 1.2 %copy-start.16 = (bf16[1024,512]{1,0:T(8,128)(2,1)S(1)}, bf16[1024,512]{1,0:T(8,128)(2,1)}, u32[]{:S(2)}) copy-start(bf16[1024,512]{1,0:T(8,128)(2,1)} %wg.1) | copy-start | bytes 3145732
  59.4 1.2 %copy-start.20 = (bf16[1024,512]{1,0:T(8,128)(2,1)S(1)}, bf16[1024,512]{1,0:T(8,128)(2,1)}, u32[]{:S(2)}) copy-start(bf16[1024,512]{1,0:T(8,128)(2,1)} %copy-done.19) | copy-start | bytes 3145732
  60.6 8.6 %copy-start.5 = (bf16[2,2,256,256]{3,2,1,0:T(8,128)(2,1)S(1)}, bf16[2,2,256,256]{3,2,1,0:T(8,128)(2,1)}, u32[]{:S(2)}) copy-start(bf16[2,2,256,256]{3,2,1,0:T(8,128)(2,1)} %copy-done.4) | copy-start | bytes 1572868
  71.0 14.1 %collective-permute-start.12 = (bf16[512,512]{1,0:T(8,128)(2,1)S(1)}, bf16[512,512]{1,0:T(8,128)(2,1)S(1)}, u32[]{:S(2)}, u32[]{:S(2)}) collective-permute-start(bf16[512,512]{1,0:T(8,128)(2,1)S(1)} %hidden.3.refs_0_), channel_id=1, source_target_pairs={{0,4},{2,6},{4,0},{6,2},{1,5},{3,7},{5,1},{7,3},{8,12},{10,14},{12... | collective-permute-start | bytes 1572872 | tf_op jit(solution)/shard_map/ppermute | solution.py:33
  73.9 13.8 %collective-permute-start.8 = (bf16[512,512]{1,0:T(8,128)(2,1)S(1)}, bf16[512,512]{1,0:T(8,128)(2,1)S(1)}, u32[]{:S(2)}, u32[]{:S(2)}) collective-permute-start(bf16[512,512]{1,0:T(8,128)(2,1)S(1)} %hidden.2.refs_0_), channel_id=1, source_target_pairs={{0,2},{2,0},{4,6},{6,4},{1,3},{3,1},{5,7},{7,5},{8,10},{10,8},{12,... | collective-permute-start | bytes 1572872 | tf_op jit(solution)/shard_map/ppermute | solution.py:33
  86.4 13.3 %collective-permute-start.15 = (bf16[512,512]{1,0:T(8,128)(2,1)S(1)}, bf16[512,512]{1,0:T(8,128)(2,1)S(1)}, u32[]{:S(2)}, u32[]{:S(2)}) collective-permute-start(bf16[512,512]{1,0:T(8,128)(2,1)S(1)} %give.3), channel_id=1, source_target_pairs={{0,2},{2,0},{4,6},{6,4},{1,3},{3,1},{5,7},{7,5},{8,10},{10,8},{12,... | collective-permute-start | bytes 1572872 | tf_op jit(solution)/shard_map/ppermute | solution.py:33
  89.0 13.0 %collective-permute-start.11 = (bf16[512,512]{1,0:T(8,128)(2,1)S(1)}, bf16[512,512]{1,0:T(8,128)(2,1)S(1)}, u32[]{:S(2)}, u32[]{:S(2)}) collective-permute-start(bf16[512,512]{1,0:T(8,128)(2,1)S(1)} %give.2), channel_id=1, source_target_pairs={{0,4},{2,6},{4,0},{6,2},{1,5},{3,7},{5,1},{7,3},{8,12},{10,14},{12... | collective-permute-start | bytes 1572872 | tf_op jit(solution)/shard_map/ppermute | solution.py:33
  (6 other events, 5.8 us)

commit v3 on v2

v3 whole, which is shorter than its diff:
```python
import functools
import math

import jax
import jax.numpy as jnp
from jax import lax
from jax.experimental import pallas as pl
from jax.experimental.pallas import tpu as pltpu
from jax.sharding import PartitionSpec as P

DH = 256
BLOCK = 512
TILE = 256
FINE = 32
EXTRA = 16
VMEM_LIMIT = 14 * 1024 * 1024
F32 = jnp.float32
BF16 = jnp.bfloat16


def mm(left, right):
    return jnp.dot(left, right, preferred_element_type=F32)


def mm_nt(left, right):
    return lax.dot_general(left, right, (((1,), (1,)), ((), ())), preferred_element_type=F32)


def mm_tn(left, right):
    return lax.dot_general(left, right, (((0,), (0,)), ((), ())), preferred_element_type=F32)


def swap(value, axis, mask):
    size = lax.axis_size(axis)
    return lax.ppermute(value, axis, [(place, place ^ mask) for place in range(size)])


def kernel_call(kernel, outs, operands, name, flops, transcendentals=0):
    arrays = [pltpu.with_memory_space_constraint(array, pltpu.VMEM) for array in operands]
    moved = sum(array.size * array.dtype.itemsize for array in operands)
    return pl.pallas_call(
        kernel,
        in_specs=[pl.BlockSpec(memory_space=pltpu.VMEM)] * len(operands),
        out_specs=[pl.BlockSpec(memory_space=pltpu.VMEM)] * len(outs),
        out_shape=[pltpu.VMEM(shape, dtype) for shape, dtype in outs],
        compiler_params=pltpu.CompilerParams(vmem_limit_bytes=VMEM_LIMIT),
        cost_estimate=pl.CostEstimate(
            flops=flops, bytes_accessed=moved, transcendentals=transcendentals
        ),
        name=name,
    )(*arrays)


def turned(values, cosine, sine):
    half = DH // 2
    parts = []
    for start in range(0, values.shape[1], DH):
        low = values[:, start : start + half]
        high = values[:, start + half : start + DH]
        parts.append((low * cosine - high * sine).astype(BF16))
        parts.append((high * cosine + low * sine).astype(BF16))
    return jnp.concatenate(parts, axis=1)


def angles(coarse, fine, first, count):
    at = first // FINE
    far = coarse[:, pl.ds(at, count // FINE), :]
    near = fine[...]
    cos_c, sin_c = far[0][:, None, :], far[1][:, None, :]
    cos_f, sin_f = near[0][None], near[1][None]
    cosine = cos_c * cos_f - sin_c * sin_f
    sine = sin_c * cos_f + cos_c * sin_f
    return cosine.reshape(count, DH // 2), sine.reshape(count, DH // 2)


def half_of(x, first, count, index, part):
    return x[pl.ds(first, count), pl.ds(pl.multiple_of(index * part, part), part)]


def decay_sums(log_decay, decay):
    heads, rows = log_decay.shape
    place_s = lax.broadcasted_iota(jnp.int32, (BLOCK, BLOCK), 0)
    place_t = lax.broadcasted_iota(jnp.int32, (BLOCK, BLOCK), 1)
    upper = jnp.where(place_s <= place_t, 1.0, 0.0).astype(BF16)
    value = jnp.concatenate([log_decay[...], jnp.zeros((8 - heads, rows), F32)], axis=0)
    parts = []
    for _ in range(3):
        parts.append(value.astype(BF16))
        value = value - parts[-1].astype(F32)
    stacked = jnp.concatenate([part.astype(F32) for part in parts], axis=0).astype(BF16)
    for start in range(0, rows, BLOCK):
        sums = mm(stacked[:, start : start + BLOCK], upper)
        decay[:, start : start + BLOCK] = sums[:8] + sums[8:16] + sums[16:]


def angle_tables(coarse, fine):
    half = DH // 2

    def fill(table, start, stride):
        count = table.shape[1]
        place = lax.broadcasted_iota(jnp.int32, (count, half), 0) * stride + start
        index = lax.broadcasted_iota(jnp.int32, (count, half), 1).astype(F32)
        angle = place.astype(F32) * jnp.exp(index * (-math.log(10000.0) / half))
        table[0] = jnp.cos(angle)
        table[1] = jnp.sin(angle)

    fill(coarse, lax.axis_index("ctx") * coarse.shape[1] * FINE, FINE)
    fill(fine, 0, 1)


def key_value_own_kernel(x, wk, wv, log_decay, acc_k, acc_v, decay, coarse, fine):
    part = wk.shape[0]
    core = lax.axis_index("fsdp")

    def step(tile, carry):
        first = pl.multiple_of(tile * TILE, TILE)
        rows = half_of(x, first, TILE, core, part)
        acc_k[pl.ds(first, TILE), :] = mm(rows, wk[...])
        acc_v[pl.ds(first, TILE), :] = mm(rows, wv[...])
        return carry

    lax.fori_loop(0, x.shape[0] // TILE, step, 0)
    decay_sums(log_decay, decay)
    angle_tables(coarse, fine)


def pack_message(message, states, logs):
    heads = len(states)
    place = lax.broadcasted_iota(jnp.int32, (EXTRA, DH), 0)
    tail = jnp.zeros((EXTRA, DH), F32)
    for head in range(heads):
        message[head * DH : (head + 1) * DH, :] = states[head].astype(BF16)
        rest = logs[head]
        for number in range(3):
            piece = rest.astype(BF16).astype(F32)
            tail = jnp.where(place == 3 * head + number, piece, tail)
            rest = rest - piece
    message[heads * DH :, :] = tail.astype(BF16)


def message_log(message, heads, head):
    tail = message[heads * DH :, :].astype(F32)
    return tail[3 * head : 3 * head + 1] + tail[3 * head + 1 : 3 * head + 2] + tail[3 * head + 2 : 3 * head + 3]


def key_value_kernel(
    heads, x, wk, wv, acc_k, acc_v, decay, coarse, fine, k_out, v_out, before_out, state_out, message
):
    part = wk.shape[0]
    far = 1 - lax.axis_index("fsdp")
    state_out[...] = jnp.zeros_like(state_out)

    def block_step(block, totals):
        start = pl.multiple_of(block * BLOCK, BLOCK)
        columns = decay[:, pl.ds(start, BLOCK)].T
        ending = columns[BLOCK - 1 : BLOCK, :]
        faded = jnp.exp(ending - columns)
        updates = [None] * heads
        for piece in range(BLOCK // TILE):
            first = pl.multiple_of(start + piece * TILE, TILE)
            at = pl.ds(first, TILE)
            rows = half_of(x, first, TILE, far, part)
            cosine, sine = angles(coarse, fine, first, TILE)
            keys = turned(acc_k[at, :] + mm(rows, wk[...]), cosine, sine)
            values = (acc_v[at, :] + mm(rows, wv[...])).astype(BF16)
            k_out[at, :] = keys
            v_out[at, :] = values
            for head in range(heads):
                span = slice(head * DH, (head + 1) * DH)
                fade = faded[piece * TILE : (piece + 1) * TILE, head : head + 1]
                weighted = (keys[:, span].astype(F32) * fade).astype(BF16)
                update = mm_tn(weighted, values[:, span])
                updates[head] = update if piece == 0 else updates[head] + update
        for head in range(heads):
            span = slice(head * DH, (head + 1) * DH)
            old = state_out[span, :]
            before_out[block, span, :] = old.astype(BF16)
            state_out[span, :] = jnp.exp(ending[:, head : head + 1]) * old + updates[head]
        return totals + ending

    totals = lax.fori_loop(0, x.shape[0] // BLOCK, block_step, jnp.zeros((1, 8), F32))
    states = [state_out[head * DH : (head + 1) * DH, :] for head in range(heads)]
    pack_message(message, states, [totals[:, head : head + 1] for head in range(heads)])


def combine_kernel(heads, first, decay, *refs):
    if first:
        state, got, window, entering, message = refs
    else:
        state, old_message, old_entering, got, window, entering, message = refs
    states, logs = [], []
    for head in range(heads):
        span = slice(head * DH, (head + 1) * DH)
        arrived = got[span, :].astype(F32)
        arrived_log = message_log(got, heads, head)[:, :1]
        if first:
            ends = [decay[head : head + 1, end - 1 : end] for end in range(BLOCK, decay.shape[1] + 1, BLOCK)]
            window_log = functools.reduce(lambda a, b: a + b, ends)
            entering[span, :] = arrived
            entering_log = arrived_log
        else:
            window_log = message_log(old_message, heads, head)[:, :1]
            before_log = old_entering[heads * DH + head : heads * DH + head + 1, :1]
            entering[span, :] = old_entering[span, :] + jnp.exp(before_log) * arrived
            entering_log = before_log + arrived_log
        entering[heads * DH + head : heads * DH + head + 1, :] = jnp.broadcast_to(entering_log, (1, DH))
        new = state[span, :] + jnp.exp(window_log) * arrived
        window[span, :] = new
        states.append(new)
        logs.append(window_log + arrived_log)
    pack_message(message, states, logs)


def query_gate_kernel(
    heads, x, wq, wq_far, wg, wg_far, decay, coarse, fine, k, v, q_out, g_out, intra_out
):
    part = wq.shape[0]
    core = lax.axis_index("fsdp")

    def block_step(block, carry):
        start = pl.multiple_of(block * BLOCK, BLOCK)
        lines = decay[:, pl.ds(start, BLOCK)]
        columns = lines.T
        for piece in range(BLOCK // TILE):
            low, last = piece * TILE, (piece + 1) * TILE
            first = pl.multiple_of(start + low, TILE)
            at = pl.ds(first, TILE)
            own = half_of(x, first, TILE, core, part)
            far = half_of(x, first, TILE, 1 - core, part)
            cosine, sine = angles(coarse, fine, first, TILE)
            queries = turned(mm(own, wq[...]) + mm(far, wq_far[...]), cosine, sine)
            q_out[at, :] = queries
            g_out[at, :] = (mm(own, wg[...]) + mm(far, wg_far[...])).astype(BF16)
            place_t = lax.broadcasted_iota(jnp.int32, (TILE, last), 0) + low
            place_s = lax.broadcasted_iota(jnp.int32, (TILE, last), 1)
            causal = place_t >= place_s
            for head in range(heads):
                span = slice(head * DH, (head + 1) * DH)
                scores = mm_nt(queries[:, span], k[pl.ds(start, last), span])
                differ = columns[low:last, head : head + 1] - lines[head : head + 1, :last]
                weights = jnp.where(causal, jnp.exp(jnp.where(causal, differ, 0.0)), 0.0)
                intra_out[at, span] = mm((scores * weights).astype(BF16), v[pl.ds(start, last), span])
        return carry

    lax.fori_loop(0, x.shape[0] // BLOCK, block_step, 0)


def hidden_kernel(heads, start, q, gate, intra, decay, entering, got, before, out):
    block, low = start // BLOCK, start % BLOCK
    lines = decay[:, start : start + TILE]
    columns = jnp.exp(lines.T)
    at = slice(start, start + TILE)
    for head in range(heads):
        span = slice(head * DH, (head + 1) * DH)
        entering_log = entering[heads * DH + head : heads * DH + head + 1, :1]
        state = entering[span, :] + jnp.exp(entering_log) * got[span, :].astype(F32)
        scale_log = jnp.zeros((1, 1), F32)
        for earlier in range(block):
            end = (earlier + 1) * BLOCK
            scale_log = scale_log + decay[head : head + 1, end - 1 : end]
        prior = (jnp.exp(scale_log) * state + before[block, span, :].astype(F32)).astype(BF16)
        inter = columns[:, head : head + 1] * mm(q[at, span], prior)
        retained = intra[at, span] + inter
        center = retained - jnp.mean(retained, axis=1, keepdims=True)
        spread = jnp.mean(center * center, axis=1, keepdims=True)
        value = gate[at, span].astype(F32)
        silu = value / (1.0 + jnp.exp(-value))
        out[:, span] = (silu * center * lax.rsqrt(spread + 1e-5)).astype(BF16)


def column_of(first, second, is_first, index, cols):
    at = pl.ds(pl.multiple_of(index * cols, cols), cols)
    return jnp.where(is_first, first[:, at], second[:, at])


def product_kernel(by_low, flip, *refs):
    out = refs[-1]
    cols = out.shape[1]
    place, core = lax.axis_index("tp"), lax.axis_index("fsdp")
    high, low = place // 2, place % 2
    if by_low:
        wanted_high, wanted_low = (1 - high if flip else high), low
    else:
        wanted_high, wanted_low = high, (1 - low if flip else low)
    own, own_first, own_second, far, far_first, far_second = refs[:-1]
    own_weight = column_of(own_first, own_second, core == wanted_high, wanted_low, cols)
    if by_low:
        far_weight = jnp.where(core == wanted_high, far_first[...], far_second[...])
    else:
        far_weight = column_of(far_first, far_second, core == high, wanted_low, cols)
    out[...] = (mm(own[...], own_weight) + mm(far[...], far_weight)).astype(out.dtype)


def slice_kernel(weight, out):
    cols = out.shape[1]
    low = lax.axis_index("tp") % 2
    out[...] = weight[:, pl.ds(pl.multiple_of((1 - low) * cols, cols), cols)]


def finish_kernel(*refs):
    out = refs[-1]
    for number in range((len(refs) - 1) // 2):
        value = refs[2 * number][...] + refs[2 * number + 1][...].astype(F32)
        out[0, number * TILE : (number + 1) * TILE, :] = value.astype(BF16)


def after(value, *others):
    return lax.optimization_barrier((value, *others))[0]


def on_device(tokens, query_weight, key_weight, value_weight, gate_weight, out_weight, log_decay):
    x = tokens[0]
    rows, width = x.shape
    part, cols = query_weight.shape
    heads = cols // DH
    blocks = rows // BLOCK
    ctx, tp, cores = lax.axis_size("ctx"), lax.axis_size("tp"), lax.axis_size("fsdp")
    assert tp == 4 and cores == 2 and ctx > 2
    near_mask, far_mask = 1, 2
    product = 2 * rows * part * cols
    tables = [((2, rows // FINE, DH // 2), F32), ((2, FINE, DH // 2), F32)]

    key_far = swap(key_weight, "fsdp", 1)
    value_far = swap(value_weight, "fsdp", 1)

    acc_k, acc_v, decay, coarse, fine = kernel_call(
        key_value_own_kernel,
        [((rows, cols), F32)] * 2 + [((8, rows), F32)] + tables,
        [x, key_weight, value_weight, log_decay[0].T],
        "key_value_own",
        2 * product,
    )
    state_shape = (heads * DH, DH)
    message_shape = (heads * DH + EXTRA, DH)
    keys, values, before, state, message = kernel_call(
        functools.partial(key_value_kernel, heads),
        [
            ((rows, cols), BF16),
            ((rows, cols), BF16),
            ((blocks, *state_shape), BF16),
            (state_shape, F32),
            (message_shape, BF16),
        ],
        [x, key_far, value_far, acc_k, acc_v, decay, coarse, fine],
        "key_value",
        2 * product,
    )

    window, entering, hop = state, None, 1
    while hop < ctx:
        pairs = [(source, source + hop) for source in range(ctx - hop)]
        got = lax.ppermute(message, "ctx", pairs)
        hop *= 2
        if hop < ctx:
            held = [decay, window] + ([] if entering is None else [message, entering]) + [got]
            window, entering, message = kernel_call(
                functools.partial(combine_kernel, heads, entering is None),
                [(state_shape, F32), (message_shape, F32), (message_shape, BF16)],
                held,
                "combine",
                0,
            )

    query_far = swap(query_weight, "fsdp", 1)
    gate_far = swap(gate_weight, "fsdp", 1)
    [for_near] = kernel_call(slice_kernel, [((cols, cols), BF16)], [out_weight], "near_columns", 0)
    near_first = swap(for_near, "tp", near_mask)
    near_second = swap(near_first, "fsdp", 1)
    high_pairs = [((at ^ far_mask) * cores + at // 2, at * cores + at // 2) for at in range(tp)]
    core_pairs = [(at * cores + at // 2, at * cores + 1 - at // 2) for at in range(tp)]
    high_pass = lax.ppermute(out_weight, ("tp", "fsdp"), high_pairs)
    high_other = lax.ppermute(high_pass, ("tp", "fsdp"), core_pairs)
    own_second = swap(out_weight, "fsdp", 1)

    queries, gates, intra = kernel_call(
        functools.partial(query_gate_kernel, heads),
        [((rows, cols), BF16), ((rows, cols), BF16), ((rows, cols), F32)],
        [x, query_weight, query_far, gate_weight, gate_far, decay, coarse, fine, keys, values],
        "query_gate",
        4 * product + 4 * rows * BLOCK * cols,
        rows * BLOCK * heads,
    )

    starts = list(range(0, rows, TILE))
    order = [start for pair in zip(starts[: len(starts) // 2], starts[len(starts) // 2 :]) for start in pair]
    pieces = {}
    for start in order:
        by_low = start < rows // 2
        [hidden] = kernel_call(
            functools.partial(hidden_kernel, heads, start),
            [((TILE, cols), BF16)],
            [queries, gates, intra, decay, entering, got, before],
            "hidden",
            2 * TILE * DH * cols,
            TILE * cols,
        )
        pieces[start] = hidden, swap(hidden, "tp", near_mask if by_low else far_mask)
    sums = {}
    for start in order:
        by_low = start < rows // 2
        hidden, far = pieces[start]
        pair = (near_first, near_second) if by_low else (high_pass, high_other)

        def product_of(flip, dtype, name):
            return kernel_call(
                functools.partial(product_kernel, by_low, flip),
                [((TILE, cols), dtype)],
                [hidden, out_weight, own_second, far, *pair],
                name,
                4 * TILE * cols * cols,
            )[0]

        give = product_of(True, BF16, "give")
        keep = product_of(False, F32, "keep")
        sums[start] = keep, swap(give, "tp", far_mask if by_low else near_mask)
    arrays = [
        pltpu.with_memory_space_constraint(array, pltpu.VMEM) for start in starts for array in sums[start]
    ]
    return pl.pallas_call(
        finish_kernel,
        in_specs=[pl.BlockSpec(memory_space=pltpu.VMEM)] * len(arrays),
        out_specs=pl.BlockSpec(memory_space=pltpu.VMEM),
        out_shape=jax.ShapeDtypeStruct((1, rows, cols), BF16),
        compiler_params=pltpu.CompilerParams(vmem_limit_bytes=VMEM_LIMIT),
        name="finish",
    )(*arrays)


def solution(mesh):
    in_specs = (
        P("fsdp", "ctx", None),
        P("fsdp", "tp"),
        P("fsdp", "tp"),
        P("fsdp", "tp"),
        P("fsdp", "tp"),
        P("tp", "fsdp"),
        P("fsdp", "ctx", "tp"),
    )
    out_specs = P("fsdp", "ctx", "tp")
    return jax.shard_map(
        on_device, mesh=mesh, in_specs=in_specs, out_specs=out_specs, check_vma=False
    )
```

time: 104 us -> 81.8 us (0.79)
  the two profiles are of different devices: /device:TPU:0 before, /device:TPU:24 now
where the time goes in v3:
time: 81.8 us; the launch traced here: 81.1 us
  Pallas kernels  31.9 us (39%)
  waiting for transfers between devices  24.8 us (30%)
  starting transfers between devices  18.8 us (23%)
  local copies, waits for them, and re-layouts  5.35 us (7%)
    pallas_call x17, Pallas kernels, kernel_call(): pl.pallas_call(kernel, in_specs=[pl.BlockSpec(memory_space=pltpu.VMEM)] *...  30.7 us
    ppermute x2, waiting for transfers between devices, on_device(): got = lax.ppermute(message, 'ctx', pairs)  17.1 us
    ppermute x15, starting transfers between devices, swap(): lax.ppermute(value, axis, [(place, place ^ mask) for place in range(size)])  13.3 us
    ppermute x15, waiting for transfers between devices, swap(): lax.ppermute(value, axis, [(place, place ^ mask) for place in range(size)])  7.61 us
    unnamed x14, local copies, waits for them, and re-layouts  5.35 us
    ppermute x2, starting transfers between devices, on_device(): got = lax.ppermute(message, 'ctx', pairs)  2.56 us
    ppermute x1, starting transfers between devices, on_device(): high_other = lax.ppermute(high_pass, ('tp', 'fsdp'), core_pairs)  1.68 us
  transfers between devices with their start and end apart: 19, of which 6 were waited for; matrix products, arithmetic and copies ran while one was open for 0% of the time, Pallas kernels for 38%

profile of v3, /device:TPU:24, one launch (start us, length us, event | category | flops | bytes accessed | tf_op | source)
XLA Modules:
  0.0 81.1 jit_solution(2210490577143120897)
XLA Ops:
  0.5 1.3 %collective-permute-start.14 = (bf16[512,1024]{1,0:T(8,128)(2,1)}, bf16[512,1024]{1,0:T(8,128)(2,1)S(1)}, u32[]{:S(2)}, u32[]{:S(2)}) collective-permute-start(bf16[512,1024]{1,0:T(8,128)(2,1)} %refs_1_.15), channel_id=1, source_target_pairs={{4,0},{6,2},{1,5},{3,7},{12,8},{14,10},{9,13},{11,15},{20,16},{22,... | collective-permute-start | bytes 3145736 | tf_op jit(solution)/shard_map/ppermute | solution.py:371
  1.8 2.0 %collective-permute-start = (bf16[1024,512]{1,0:T(8,128)(2,1)}, bf16[1024,512]{1,0:T(8,128)(2,1)S(1)}, u32[]{:S(2)}, u32[]{:S(2)}) collective-permute-start(bf16[1024,512]{1,0:T(8,128)(2,1)} %wq.1), channel_id=1, source_target_pairs={{0,1},{1,0},{2,3},{3,2},{4,5},{5,4},{6,7},{7,6},{8,9},{9,8},{10,11... | collective-permute-start | bytes 3145736 | tf_op jit(solution)/shard_map/ppermute | solution.py:35
  3.9 1.3 %near_columns.1 = bf16[512,512]{1,0:T(8,128)(2,1)S(1)} custom-call(bf16[512,1024]{1,0:T(8,128)(2,1)} %refs_1_.15), custom_call_target="tpu_custom_call" | custom-call | bytes 1048576 | tf_op jit(solution)/shard_map/near_columns/pallas_call | solution.py:41
  5.1 1.6 %collective-permute-start.8 = (bf16[512,512]{1,0:T(8,128)(2,1)S(1)}, bf16[512,512]{1,0:T(8,128)(2,1)S(1)}, u32[]{:S(2)}, u32[]{:S(2)}) collective-permute-start(bf16[512,512]{1,0:T(8,128)(2,1)S(1)} %near_columns.1), channel_id=1, source_target_pairs={{0,2},{2,0},{4,6},{6,4},{1,3},{3,1},{5,7},{7,5},{8,10},{10,8},{12,... | collective-permute-start | bytes 1572872 | tf_op jit(solution)/shard_map/ppermute | solution.py:35
  6.9 2.2 %copy-done = bf16[1,1024,2048]{2,1,0:T(8,128)(2,1)S(1)} copy-done((bf16[1,1024,2048]{2,1,0:T(8,128)(2,1)S(1)}, bf16[1,1024,2048]{2,1,0:T(8,128)(2,1)}, u32[]{:S(2)}) %copy-start) | copy-done | bytes 4194328
  9.1 1.2 %copy-done.2 = bf16[1024,512]{1,0:T(8,128)(2,1)S(1)} copy-done((bf16[1024,512]{1,0:T(8,128)(2,1)S(1)}, bf16[1024,512]{1,0:T(8,128)(2,1)}, u32[]{:S(2)}) %copy-start.2) | copy-done | bytes 1048600
  10.3 1.2 %copy-done.3 = bf16[1024,512]{1,0:T(8,128)(2,1)S(1)} copy-done((bf16[1024,512]{1,0:T(8,128)(2,1)S(1)}, bf16[1024,512]{1,0:T(8,128)(2,1)}, u32[]{:S(2)}) %copy-start.3) | copy-done | bytes 1048600
  12.2 3.2 %key_value_own.1 = (f32[1024,512]{1,0:T(8,128)S(1)}, f32[1024,512]{1,0:T(8,128)S(1)}, f32[8,1024]{1,0:T(8,128)S(1)}, f32[2,32,128]{2,1,0:T(8,128)S(1)}, f32[2,32,128]{2,1,0:T(8,128)S(1)}) custom-call(bf16[1024,2048]{1,0:T(8,128)(2,1)S(1)} %bitcast.4, bf16[1024,512]{1,0:T(8,128)(2,1)S(1)} %copy-done.2, bf16[1024,512]{1,0:T(8,128)(2,1)S(1)} %copy-done.3, ...), custom_call_target="tpu_custom_call" | custom-call | flops 2147483648 | bytes 6299648 | tf_op jit(solution)/shard_map/key_value_own/pallas_call | solution.py:41
  15.4 3.4 %key_value.1 = (bf16[1024,512]{1,0:T(8,128)(2,1)S(1)}, bf16[1024,512]{1,0:T(8,128)(2,1)S(1)}, bf16[2,512,256]{2,1,0:T(8,128)(2,1)S(1)}, f32[512,256]{1,0:T(8,128)S(1)}, bf16[528,256]{1,0:T(8,128)(2,1)S(1)}) custom-call(bf16[1024,2048]{1,0:T(8,128)(2,1)S(1)} %bitcast.5, bf16[1024,512]{1,0:T(8,128)(2,1)S(1)} %collective-permute-done.2.wk, ...), custom_call_target="tpu_custom_call" | custom-call | flops 2147483648 | bytes 10584064 | tf_op jit(solution)/shard_map/key_value/pallas_call | solution.py:41
  19.5 1.3 %collective-permute-start.4 = (bf16[528,256]{1,0:T(8,128)(2,1)S(1)}, bf16[528,256]{1,0:T(8,128)(2,1)S(1)}, u32[]{:S(2)}, u32[]{:S(2)}) collective-permute-start(bf16[528,256]{1,0:T(8,128)(2,1)S(1)} %get-tuple-element.31), channel_id=1, source_target_pairs={{0,8},{8,16},{16,24},{1,9},{9,17},{17,25},{2,10},{10,18},{18,26},{... | collective-permute-start | bytes 811016 | tf_op jit(solution)/shard_map/ppermute | solution.py:352
  20.8 1.7 %collective-permute-start.15 = (bf16[512,1024]{1,0:T(8,128)(2,1)S(1)}, bf16[512,1024]{1,0:T(8,128)(2,1)S(1)}, u32[]{:S(2)}, u32[]{:S(2)}) collective-permute-start(bf16[512,1024]{1,0:T(8,128)(2,1)S(1)} %collective-permute-done.14.refs_4_), channel_id=1, source_target_pairs={{0,1},{2,3},{5,4},{7,6},{8,9},{10,11},{13,12},{15,14},{16,17},{18,... | collective-permute-start | bytes 3145736 | tf_op jit(solution)/shard_map/ppermute | solution.py:372
  22.5 7.0 %collective-permute-done.4.refs_1_ = bf16[528,256]{1,0:T(8,128)(2,1)S(1)} collective-permute-done((bf16[528,256]{1,0:T(8,128)(2,1)S(1)}, bf16[528,256]{1,0:T(8,128)(2,1)S(1)}, u32[]{:S(2)}, u32[]{:S(2)}) %collective-permute-start.4) | collective-permute-done | bytes 270368 | tf_op jit(solution)/shard_map/ppermute | solution.py:352
  30.5 1.3 %collective-permute-start.5 = (bf16[528,256]{1,0:T(8,128)(2,1)S(1)}, bf16[528,256]{1,0:T(8,128)(2,1)S(1)}, u32[]{:S(2)}, u32[]{:S(2)}) collective-permute-start(bf16[528,256]{1,0:T(8,128)(2,1)S(1)} %get-tuple-element.33), channel_id=1, source_target_pairs={{0,16},{8,24},{1,17},{9,25},{2,18},{10,26},{3,19},{11,27},{4,20},{... | collective-permute-start | bytes 811016 | tf_op jit(solution)/shard_map/ppermute | solution.py:352
  31.8 5.9 %query_gate.1 = (bf16[1024,512]{1,0:T(8,128)(2,1)S(1)}, bf16[1024,512]{1,0:T(8,128)(2,1)S(1)}, f32[1024,512]{1,0:T(8,128)S(1)}) custom-call(bf16[1024,2048]{1,0:T(8,128)(2,1)S(1)} %bitcast.6, bf16[1024,512]{1,0:T(8,128)(2,1)S(1)} %copy-done.4, bf16[1024,512]{1,0:T(8,128)(2,1)S(1)} %collective-permute-done.wq_far, bf16[1024,512]{1,0:T(8,128)(2,1)S(1)} %copy-done.5, ...), custom_call_target="tpu_custom_call" | custom-call | flops 5368709120 | bytes 10584064 | tf_op jit(solution)/shard_map/query_gate/pallas_call | solution.py:41
  37.7 10.1 %collective-permute-done.5.got = bf16[528,256]{1,0:T(8,128)(2,1)S(1)} collective-permute-done((bf16[528,256]{1,0:T(8,128)(2,1)S(1)}, bf16[528,256]{1,0:T(8,128)(2,1)S(1)}, u32[]{:S(2)}, u32[]{:S(2)}) %collective-permute-start.5) | collective-permute-done | bytes 270368 | tf_op jit(solution)/shard_map/ppermute | solution.py:352
  48.5 1.5 %collective-permute-start.11 = (bf16[256,512]{1,0:T(8,128)(2,1)S(1)}, bf16[256,512]{1,0:T(8,128)(2,1)S(1)}, u32[]{:S(2)}, u32[]{:S(2)}) collective-permute-start(bf16[256,512]{1,0:T(8,128)(2,1)S(1)} %hidden.5.refs_0_), channel_id=1, source_target_pairs={{0,2},{2,0},{4,6},{6,4},{1,3},{3,1},{5,7},{7,5},{8,10},{10,8},{12,... | collective-permute-start | bytes 786440 | tf_op jit(solution)/shard_map/ppermute | solution.py:35
  52.0 1.3 %collective-permute-start.17 = (bf16[256,512]{1,0:T(8,128)(2,1)S(1)}, bf16[256,512]{1,0:T(8,128)(2,1)S(1)}, u32[]{:S(2)}, u32[]{:S(2)}) collective-permute-start(bf16[256,512]{1,0:T(8,128)(2,1)S(1)} %hidden.7.refs_0_), channel_id=1, source_target_pairs={{0,4},{2,6},{4,0},{6,2},{1,5},{3,7},{5,1},{7,3},{8,12},{10,14},{12... | collective-permute-start | bytes 786440 | tf_op jit(solution)/shard_map/ppermute | solution.py:35
  54.9 2.9 %collective-permute-done.11.refs_3_ = bf16[256,512]{1,0:T(8,128)(2,1)S(1)} collective-permute-done((bf16[256,512]{1,0:T(8,128)(2,1)S(1)}, bf16[256,512]{1,0:T(8,128)(2,1)S(1)}, u32[]{:S(2)}, u32[]{:S(2)}) %collective-permute-start.11) | collective-permute-done | bytes 262176 | tf_op jit(solution)/shard_map/ppermute | solution.py:35
  57.7 1.7 %give.5 = bf16[256,512]{1,0:T(8,128)(2,1)S(1)} custom-call(bf16[256,512]{1,0:T(8,128)(2,1)S(1)} %hidden.5.refs_0_, bf16[512,1024]{1,0:T(8,128)(2,1)} %refs_1_.15, bf16[512,1024]{1,0:T(8,128)(2,1)S(1)} %collective-permute-done.6.refs_2_, bf16[256,512]{1,0:T(8,128)(2,1)S(1)} %collective-permute-done.11.refs_3_, ...), custom_call_target="tpu_custom_call" | custom-call | flops 268435456 | bytes 3670016 | tf_op jit(solution)/shard_map/give/pallas_call | solution.py:41
  59.4 1.3 %collective-permute-start.12 = (bf16[256,512]{1,0:T(8,128)(2,1)S(1)}, bf16[256,512]{1,0:T(8,128)(2,1)S(1)}, u32[]{:S(2)}, u32[]{:S(2)}) collective-permute-start(bf16[256,512]{1,0:T(8,128)(2,1)S(1)} %give.5), channel_id=1, source_target_pairs={{0,4},{2,6},{4,0},{6,2},{1,5},{3,7},{5,1},{7,3},{8,12},{10,14},{12... | collective-permute-start | bytes 786440 | tf_op jit(solution)/shard_map/ppermute | solution.py:35
  60.7 1.8 %collective-permute-done.7.refs_3_ = bf16[256,512]{1,0:T(8,128)(2,1)S(1)} collective-permute-done((bf16[256,512]{1,0:T(8,128)(2,1)S(1)}, bf16[256,512]{1,0:T(8,128)(2,1)S(1)}, u32[]{:S(2)}, u32[]{:S(2)}) %collective-permute-start.7) | collective-permute-done | bytes 262176 | tf_op jit(solution)/shard_map/ppermute | solution.py:35
  62.5 1.7 %give.4 = bf16[256,512]{1,0:T(8,128)(2,1)S(1)} custom-call(bf16[256,512]{1,0:T(8,128)(2,1)S(1)} %hidden.4.refs_0_, bf16[512,1024]{1,0:T(8,128)(2,1)} %refs_1_.15, bf16[512,1024]{1,0:T(8,128)(2,1)S(1)} %collective-permute-done.6.refs_2_, bf16[256,512]{1,0:T(8,128)(2,1)S(1)} %collective-permute-done.7.refs_3_, ...), custom_call_target="tpu_custom_call" | custom-call | flops 268435456 | bytes 3670016 | tf_op jit(solution)/shard_map/give/pallas_call | solution.py:41
  64.2 1.3 %collective-permute-start.10 = (bf16[256,512]{1,0:T(8,128)(2,1)S(1)}, bf16[256,512]{1,0:T(8,128)(2,1)S(1)}, u32[]{:S(2)}, u32[]{:S(2)}) collective-permute-start(bf16[256,512]{1,0:T(8,128)(2,1)S(1)} %give.4), channel_id=1, source_target_pairs={{0,4},{2,6},{4,0},{6,2},{1,5},{3,7},{5,1},{7,3},{8,12},{10,14},{12... | collective-permute-start | bytes 786440 | tf_op jit(solution)/shard_map/ppermute | solution.py:35
  65.4 1.7 %give.7 = bf16[256,512]{1,0:T(8,128)(2,1)S(1)} custom-call(bf16[256,512]{1,0:T(8,128)(2,1)S(1)} %hidden.7.refs_0_, bf16[512,1024]{1,0:T(8,128)(2,1)} %refs_1_.15, bf16[512,1024]{1,0:T(8,128)(2,1)S(1)} %collective-permute-done.6.refs_2_, bf16[256,512]{1,0:T(8,128)(2,1)S(1)} %collective-permute-done.17.refs_3_, ...), custom_call_target="tpu_custom_call" | custom-call | flops 268435456 | bytes 4718592 | tf_op jit(solution)/shard_map/give/pallas_call | solution.py:41
  67.8 1.7 %give.6 = bf16[256,512]{1,0:T(8,128)(2,1)S(1)} custom-call(bf16[256,512]{1,0:T(8,128)(2,1)S(1)} %hidden.6.refs_0_, bf16[512,1024]{1,0:T(8,128)(2,1)} %refs_1_.15, bf16[512,1024]{1,0:T(8,128)(2,1)S(1)} %collective-permute-done.6.refs_2_, bf16[256,512]{1,0:T(8,128)(2,1)S(1)} %collective-permute-done.13.refs_3_, ...), custom_call_target="tpu_custom_call" | custom-call | flops 268435456 | bytes 4718592 | tf_op jit(solution)/shard_map/give/pallas_call | solution.py:41
  69.5 1.4 %collective-permute-start.16 = (bf16[256,512]{1,0:T(8,128)(2,1)S(1)}, bf16[256,512]{1,0:T(8,128)(2,1)S(1)}, u32[]{:S(2)}, u32[]{:S(2)}) collective-permute-start(bf16[256,512]{1,0:T(8,128)(2,1)S(1)} %give.6), channel_id=1, source_target_pairs={{0,2},{2,0},{4,6},{6,4},{1,3},{3,1},{5,7},{7,5},{8,10},{10,8},{12,... | collective-permute-start | bytes 786440 | tf_op jit(solution)/shard_map/ppermute | solution.py:35
  71.0 1.7 %keep.5.refs_2_ = f32[256,512]{1,0:T(8,128)S(1)} custom-call(bf16[256,512]{1,0:T(8,128)(2,1)S(1)} %hidden.5.refs_0_, bf16[512,1024]{1,0:T(8,128)(2,1)} %refs_1_.15, bf16[512,1024]{1,0:T(8,128)(2,1)S(1)} %collective-permute-done.6.refs_2_, bf16[256,512]{1,0:T(8,128)(2,1)S(1)} %collective-permute-done.11.refs_3_, ...), custom_call_target="tpu_custom_call" | custom-call | flops 268435456 | bytes 3670016 | tf_op jit(solution)/shard_map/keep/pallas_call | solution.py:41
  72.6 1.7 %keep.4.refs_0_ = f32[256,512]{1,0:T(8,128)S(1)} custom-call(bf16[256,512]{1,0:T(8,128)(2,1)S(1)} %hidden.4.refs_0_, bf16[512,1024]{1,0:T(8,128)(2,1)} %refs_1_.15, bf16[512,1024]{1,0:T(8,128)(2,1)S(1)} %collective-permute-done.6.refs_2_, bf16[256,512]{1,0:T(8,128)(2,1)S(1)} %collective-permute-done.7.refs_3_, ...), custom_call_target="tpu_custom_call" | custom-call | flops 268435456 | bytes 3670016 | tf_op jit(solution)/shard_map/keep/pallas_call | solution.py:41
  74.3 1.7 %keep.7.refs_6_ = f32[256,512]{1,0:T(8,128)S(1)} custom-call(bf16[256,512]{1,0:T(8,128)(2,1)S(1)} %hidden.7.refs_0_, bf16[512,1024]{1,0:T(8,128)(2,1)} %refs_1_.15, bf16[512,1024]{1,0:T(8,128)(2,1)S(1)} %collective-permute-done.6.refs_2_, bf16[256,512]{1,0:T(8,128)(2,1)S(1)} %collective-permute-done.17.refs_3_, ...), custom_call_target="tpu_custom_call" | custom-call | flops 268435456 | bytes 4718592 | tf_op jit(solution)/shard_map/keep/pallas_call | solution.py:41
  76.0 1.7 %keep.6.refs_4_ = f32[256,512]{1,0:T(8,128)S(1)} custom-call(bf16[256,512]{1,0:T(8,128)(2,1)S(1)} %hidden.6.refs_0_, bf16[512,1024]{1,0:T(8,128)(2,1)} %refs_1_.15, bf16[512,1024]{1,0:T(8,128)(2,1)S(1)} %collective-permute-done.6.refs_2_, bf16[256,512]{1,0:T(8,128)(2,1)S(1)} %collective-permute-done.13.refs_3_, ...), custom_call_target="tpu_custom_call" | custom-call | flops 268435456 | bytes 4718592 | tf_op jit(solution)/shard_map/keep/pallas_call | solution.py:41
  77.7 2.3 %collective-permute-done.16.refs_5_ = bf16[256,512]{1,0:T(8,128)(2,1)S(1)} collective-permute-done((bf16[256,512]{1,0:T(8,128)(2,1)S(1)}, bf16[256,512]{1,0:T(8,128)(2,1)S(1)}, u32[]{:S(2)}, u32[]{:S(2)}) %collective-permute-start.16) | collective-permute-done | bytes 262176 | tf_op jit(solution)/shard_map/ppermute | solution.py:35
  80.0 1.1 %finish.1 = bf16[1,1024,512]{2,1,0:T(8,128)(2,1)} custom-call(f32[256,512]{1,0:T(8,128)S(1)} %keep.4.refs_0_, bf16[256,512]{1,0:T(8,128)(2,1)S(1)} %collective-permute-done.10.refs_1_, f32[256,512]{1,0:T(8,128)S(1)} %keep.5.refs_2_, bf16[256,512]{1,0:T(8,128)(2,1)S(1)} %collective-permute-done.12.refs_3_, f32[256,512]{1,0:T(8,128)S(1)} %keep.6.refs_4_, ...), custom_call_target="tpu_custom_call" | custom-call | tf_op jit(solution)/shard_map/finish/pallas_call | solution.py:419
  (38 shorter events, 8.1 us)
Async XLA Ops:
  0.0 5.1 %collective-permute-start.2 = (bf16[1024,512]{1,0:T(8,128)(2,1)}, bf16[1024,512]{1,0:T(8,128)(2,1)S(1)}, u32[]{:S(2)}, u32[]{:S(2)}) collective-permute-start(bf16[1024,512]{1,0:T(8,128)(2,1)} %wk.1), channel_id=1, source_target_pairs={{0,1},{1,0},{2,3},{3,2},{4,5},{5,4},{6,7},{7,6},{8,9},{9,8},{10,11... | collective-permute-start | bytes 3145736 | tf_op jit(solution)/shard_map/ppermute | solution.py:35
  0.0 6.7 %collective-permute-start.3 = (bf16[1024,512]{1,0:T(8,128)(2,1)}, bf16[1024,512]{1,0:T(8,128)(2,1)S(1)}, u32[]{:S(2)}, u32[]{:S(2)}) collective-permute-start(bf16[1024,512]{1,0:T(8,128)(2,1)} %wv.1), channel_id=1, source_target_pairs={{0,1},{1,0},{2,3},{3,2},{4,5},{5,4},{6,7},{7,6},{8,9},{9,8},{10,11... | collective-permute-start | bytes 3145736 | tf_op jit(solution)/shard_map/ppermute | solution.py:35
  0.5 20.3 %collective-permute-start.14 = (bf16[512,1024]{1,0:T(8,128)(2,1)}, bf16[512,1024]{1,0:T(8,128)(2,1)S(1)}, u32[]{:S(2)}, u32[]{:S(2)}) collective-permute-start(bf16[512,1024]{1,0:T(8,128)(2,1)} %refs_1_.15), channel_id=1, source_target_pairs={{4,0},{6,2},{1,5},{3,7},{12,8},{14,10},{9,13},{11,15},{20,16},{22,... | collective-permute-start | bytes 3145736 | tf_op jit(solution)/shard_map/ppermute | solution.py:371
  1.8 28.7 %collective-permute-start = (bf16[1024,512]{1,0:T(8,128)(2,1)}, bf16[1024,512]{1,0:T(8,128)(2,1)S(1)}, u32[]{:S(2)}, u32[]{:S(2)}) collective-permute-start(bf16[1024,512]{1,0:T(8,128)(2,1)} %wq.1), channel_id=1, source_target_pairs={{0,1},{1,0},{2,3},{3,2},{4,5},{5,4},{6,7},{7,6},{8,9},{9,8},{10,11... | collective-permute-start | bytes 3145736 | tf_op jit(solution)/shard_map/ppermute | solution.py:35
  3.8 28.0 %collective-permute-start.1 = (bf16[1024,512]{1,0:T(8,128)(2,1)}, bf16[1024,512]{1,0:T(8,128)(2,1)S(1)}, u32[]{:S(2)}, u32[]{:S(2)}) collective-permute-start(bf16[1024,512]{1,0:T(8,128)(2,1)} %wg.1), channel_id=1, source_target_pairs={{0,1},{1,0},{2,3},{3,2},{4,5},{5,4},{6,7},{7,6},{8,9},{9,8},{10,11... | collective-permute-start | bytes 3145736 | tf_op jit(solution)/shard_map/ppermute | solution.py:35
  5.1 14.3 %collective-permute-start.8 = (bf16[512,512]{1,0:T(8,128)(2,1)S(1)}, bf16[512,512]{1,0:T(8,128)(2,1)S(1)}, u32[]{:S(2)}, u32[]{:S(2)}) collective-permute-start(bf16[512,512]{1,0:T(8,128)(2,1)S(1)} %near_columns.1), channel_id=1, source_target_pairs={{0,2},{2,0},{4,6},{6,4},{1,3},{3,1},{5,7},{7,5},{8,10},{10,8},{12,... | collective-permute-start | bytes 1572872 | tf_op jit(solution)/shard_map/ppermute | solution.py:35
  6.7 45.3 %collective-permute-start.6 = (bf16[512,1024]{1,0:T(8,128)(2,1)}, bf16[512,1024]{1,0:T(8,128)(2,1)S(1)}, u32[]{:S(2)}, u32[]{:S(2)}) collective-permute-start(bf16[512,1024]{1,0:T(8,128)(2,1)} %refs_1_.15), channel_id=1, source_target_pairs={{0,1},{1,0},{2,3},{3,2},{4,5},{5,4},{6,7},{7,6},{8,9},{9,8},{10,11... | collective-permute-start | bytes 3145736 | tf_op jit(solution)/shard_map/ppermute | solution.py:35
  6.9 2.2 %copy-start = (bf16[1,1024,2048]{2,1,0:T(8,128)(2,1)S(1)}, bf16[1,1024,2048]{2,1,0:T(8,128)(2,1)}, u32[]{:S(2)}) copy-start(bf16[1,1024,2048]{2,1,0:T(8,128)(2,1)} %param.7) | copy-start | bytes 12582916
  9.1 1.2 %copy-start.2 = (bf16[1024,512]{1,0:T(8,128)(2,1)S(1)}, bf16[1024,512]{1,0:T(8,128)(2,1)}, u32[]{:S(2)}) copy-start(bf16[1024,512]{1,0:T(8,128)(2,1)} %wk.1) | copy-start | bytes 3145732
  10.3 1.2 %copy-start.3 = (bf16[1024,512]{1,0:T(8,128)(2,1)S(1)}, bf16[1024,512]{1,0:T(8,128)(2,1)}, u32[]{:S(2)}) copy-start(bf16[1024,512]{1,0:T(8,128)(2,1)} %wv.1) | copy-start | bytes 3145732
  11.5 0.7 copy-start.6
  15.4 16.4 %copy-start.1 = (bf16[1,1024,2048]{2,1,0:T(8,128)(2,1)S(1)}, bf16[1,1024,2048]{2,1,0:T(8,128)(2,1)}, u32[]{:S(2)}) copy-start(bf16[1,1024,2048]{2,1,0:T(8,128)(2,1)} %param.7) | copy-start | bytes 12582916
  15.4 16.4 %copy-start.4 = (bf16[1024,512]{1,0:T(8,128)(2,1)S(1)}, bf16[1024,512]{1,0:T(8,128)(2,1)}, u32[]{:S(2)}) copy-start(bf16[1024,512]{1,0:T(8,128)(2,1)} %wq.1) | copy-start | bytes 3145732
  15.4 16.4 %copy-start.5 = (bf16[1024,512]{1,0:T(8,128)(2,1)S(1)}, bf16[1024,512]{1,0:T(8,128)(2,1)}, u32[]{:S(2)}) copy-start(bf16[1024,512]{1,0:T(8,128)(2,1)} %wg.1) | copy-start | bytes 3145732
  19.5 10.0 %collective-permute-start.4 = (bf16[528,256]{1,0:T(8,128)(2,1)S(1)}, bf16[528,256]{1,0:T(8,128)(2,1)S(1)}, u32[]{:S(2)}, u32[]{:S(2)}) collective-permute-start(bf16[528,256]{1,0:T(8,128)(2,1)S(1)} %get-tuple-element.31), channel_id=1, source_target_pairs={{0,8},{8,16},{16,24},{1,9},{9,17},{17,25},{2,10},{10,18},{18,26},{... | collective-permute-start | bytes 811016 | tf_op jit(solution)/shard_map/ppermute | solution.py:352
  20.8 44.7 %collective-permute-start.15 = (bf16[512,1024]{1,0:T(8,128)(2,1)S(1)}, bf16[512,1024]{1,0:T(8,128)(2,1)S(1)}, u32[]{:S(2)}, u32[]{:S(2)}) collective-permute-start(bf16[512,1024]{1,0:T(8,128)(2,1)S(1)} %collective-permute-done.14.refs_4_), channel_id=1, source_target_pairs={{0,1},{2,3},{5,4},{7,6},{8,9},{10,11},{13,12},{15,14},{16,17},{18,... | collective-permute-start | bytes 3145736 | tf_op jit(solution)/shard_map/ppermute | solution.py:372
  29.5 24.5 %collective-permute-start.9 = (bf16[512,512]{1,0:T(8,128)(2,1)S(1)}, bf16[512,512]{1,0:T(8,128)(2,1)S(1)}, u32[]{:S(2)}, u32[]{:S(2)}) collective-permute-start(bf16[512,512]{1,0:T(8,128)(2,1)S(1)} %collective-permute-done.8.refs_4_), channel_id=1, source_target_pairs={{0,1},{1,0},{2,3},{3,2},{4,5},{5,4},{6,7},{7,6},{8,9},{9,8},{10,11... | collective-permute-start | bytes 1572872 | tf_op jit(solution)/shard_map/ppermute | solution.py:35
  30.5 17.4 %collective-permute-start.5 = (bf16[528,256]{1,0:T(8,128)(2,1)S(1)}, bf16[528,256]{1,0:T(8,128)(2,1)S(1)}, u32[]{:S(2)}, u32[]{:S(2)}) collective-permute-start(bf16[528,256]{1,0:T(8,128)(2,1)S(1)} %get-tuple-element.33), channel_id=1, source_target_pairs={{0,16},{8,24},{1,17},{9,25},{2,18},{10,26},{3,19},{11,27},{4,20},{... | collective-permute-start | bytes 811016 | tf_op jit(solution)/shard_map/ppermute | solution.py:352
  48.5 9.2 %collective-permute-start.11 = (bf16[256,512]{1,0:T(8,128)(2,1)S(1)}, bf16[256,512]{1,0:T(8,128)(2,1)S(1)}, u32[]{:S(2)}, u32[]{:S(2)}) collective-permute-start(bf16[256,512]{1,0:T(8,128)(2,1)S(1)} %hidden.5.refs_0_), channel_id=1, source_target_pairs={{0,2},{2,0},{4,6},{6,4},{1,3},{3,1},{5,7},{7,5},{8,10},{10,8},{12,... | collective-permute-start | bytes 786440 | tf_op jit(solution)/shard_map/ppermute | solution.py:35
  50.7 11.8 %collective-permute-start.7 = (bf16[256,512]{1,0:T(8,128)(2,1)S(1)}, bf16[256,512]{1,0:T(8,128)(2,1)S(1)}, u32[]{:S(2)}, u32[]{:S(2)}) collective-permute-start(bf16[256,512]{1,0:T(8,128)(2,1)S(1)} %hidden.4.refs_0_), channel_id=1, source_target_pairs={{0,2},{2,0},{4,6},{6,4},{1,3},{3,1},{5,7},{7,5},{8,10},{10,8},{12,... | collective-permute-start | bytes 786440 | tf_op jit(solution)/shard_map/ppermute | solution.py:35
  52.0 13.4 %collective-permute-start.17 = (bf16[256,512]{1,0:T(8,128)(2,1)S(1)}, bf16[256,512]{1,0:T(8,128)(2,1)S(1)}, u32[]{:S(2)}, u32[]{:S(2)}) collective-permute-start(bf16[256,512]{1,0:T(8,128)(2,1)S(1)} %hidden.7.refs_0_), channel_id=1, source_target_pairs={{0,4},{2,6},{4,0},{6,2},{1,5},{3,7},{5,1},{7,3},{8,12},{10,14},{12... | collective-permute-start | bytes 786440 | tf_op jit(solution)/shard_map/ppermute | solution.py:35
  54.0 13.8 %collective-permute-start.13 = (bf16[256,512]{1,0:T(8,128)(2,1)S(1)}, bf16[256,512]{1,0:T(8,128)(2,1)S(1)}, u32[]{:S(2)}, u32[]{:S(2)}) collective-permute-start(bf16[256,512]{1,0:T(8,128)(2,1)S(1)} %hidden.6.refs_0_), channel_id=1, source_target_pairs={{0,4},{2,6},{4,0},{6,2},{1,5},{3,7},{5,1},{7,3},{8,12},{10,14},{12... | collective-permute-start | bytes 786440 | tf_op jit(solution)/shard_map/ppermute | solution.py:35
  59.4 18.3 %collective-permute-start.12 = (bf16[256,512]{1,0:T(8,128)(2,1)S(1)}, bf16[256,512]{1,0:T(8,128)(2,1)S(1)}, u32[]{:S(2)}, u32[]{:S(2)}) collective-permute-start(bf16[256,512]{1,0:T(8,128)(2,1)S(1)} %give.5), channel_id=1, source_target_pairs={{0,4},{2,6},{4,0},{6,2},{1,5},{3,7},{5,1},{7,3},{8,12},{10,14},{12... | collective-permute-start | bytes 786440 | tf_op jit(solution)/shard_map/ppermute | solution.py:35
  64.2 13.5 %collective-permute-start.10 = (bf16[256,512]{1,0:T(8,128)(2,1)S(1)}, bf16[256,512]{1,0:T(8,128)(2,1)S(1)}, u32[]{:S(2)}, u32[]{:S(2)}) collective-permute-start(bf16[256,512]{1,0:T(8,128)(2,1)S(1)} %give.4), channel_id=1, source_target_pairs={{0,4},{2,6},{4,0},{6,2},{1,5},{3,7},{5,1},{7,3},{8,12},{10,14},{12... | collective-permute-start | bytes 786440 | tf_op jit(solution)/shard_map/ppermute | solution.py:35
  67.1 10.6 %collective-permute-start.18 = (bf16[256,512]{1,0:T(8,128)(2,1)S(1)}, bf16[256,512]{1,0:T(8,128)(2,1)S(1)}, u32[]{:S(2)}, u32[]{:S(2)}) collective-permute-start(bf16[256,512]{1,0:T(8,128)(2,1)S(1)} %give.7), channel_id=1, source_target_pairs={{0,2},{2,0},{4,6},{6,4},{1,3},{3,1},{5,7},{7,5},{8,10},{10,8},{12,... | collective-permute-start | bytes 786440 | tf_op jit(solution)/shard_map/ppermute | solution.py:35
  69.5 10.4 %collective-permute-start.16 = (bf16[256,512]{1,0:T(8,128)(2,1)S(1)}, bf16[256,512]{1,0:T(8,128)(2,1)S(1)}, u32[]{:S(2)}, u32[]{:S(2)}) collective-permute-start(bf16[256,512]{1,0:T(8,128)(2,1)S(1)} %give.6), channel_id=1, source_target_pairs={{0,2},{2,0},{4,6},{6,4},{1,3},{3,1},{5,7},{7,5},{8,10},{10,8},{12,... | collective-permute-start | bytes 786440 | tf_op jit(solution)/shard_map/ppermute | solution.py:35

commit v4 on v3

v4 whole, which is shorter than its diff:
```python
import functools
import math

import jax
import jax.numpy as jnp
from jax import lax
from jax.experimental import pallas as pl
from jax.experimental.pallas import tpu as pltpu
from jax.sharding import PartitionSpec as P

DH = 256
BLOCK = 512
TILE = 256
FINE = 32
EXTRA = 16
VMEM_LIMIT = 14 * 1024 * 1024
F32 = jnp.float32
BF16 = jnp.bfloat16


def mm(left, right):
    return jnp.dot(left, right, preferred_element_type=F32)


def mm_nt(left, right):
    return lax.dot_general(left, right, (((1,), (1,)), ((), ())), preferred_element_type=F32)


def mm_tn(left, right):
    return lax.dot_general(left, right, (((0,), (0,)), ((), ())), preferred_element_type=F32)


def swap(value, axis, mask):
    size = lax.axis_size(axis)
    return lax.ppermute(value, axis, [(place, place ^ mask) for place in range(size)])


def kernel_call(kernel, outs, operands, name):
    arrays = [pltpu.with_memory_space_constraint(array, pltpu.VMEM) for array in operands]
    return pl.pallas_call(
        kernel,
        in_specs=[pl.BlockSpec(memory_space=pltpu.VMEM)] * len(operands),
        out_specs=[pl.BlockSpec(memory_space=pltpu.VMEM)] * len(outs),
        out_shape=[pltpu.VMEM(shape, dtype) for shape, dtype in outs],
        compiler_params=pltpu.CompilerParams(vmem_limit_bytes=VMEM_LIMIT),
        cost_estimate=pl.CostEstimate(
            flops=1, bytes_accessed=1, transcendentals=0
        ),
        name=name,
    )(*arrays)


def turned(values, cosine, sine):
    half = DH // 2
    parts = []
    for start in range(0, values.shape[1], DH):
        low = values[:, start : start + half]
        high = values[:, start + half : start + DH]
        parts.append((low * cosine - high * sine).astype(BF16))
        parts.append((high * cosine + low * sine).astype(BF16))
    return jnp.concatenate(parts, axis=1)


def angles(coarse, fine, first, count):
    at = first // FINE
    far = coarse[:, pl.ds(at, count // FINE), :]
    near = fine[...]
    cos_c, sin_c = far[0][:, None, :], far[1][:, None, :]
    cos_f, sin_f = near[0][None], near[1][None]
    cosine = cos_c * cos_f - sin_c * sin_f
    sine = sin_c * cos_f + cos_c * sin_f
    return cosine.reshape(count, DH // 2), sine.reshape(count, DH // 2)


def half_of(x, first, count, index, part):
    return x[pl.ds(first, count), pl.ds(pl.multiple_of(index * part, part), part)]


def decay_sums(log_decay, decay):
    heads, rows = log_decay.shape
    place_s = lax.broadcasted_iota(jnp.int32, (BLOCK, BLOCK), 0)
    place_t = lax.broadcasted_iota(jnp.int32, (BLOCK, BLOCK), 1)
    upper = jnp.where(place_s <= place_t, 1.0, 0.0).astype(BF16)
    value = jnp.concatenate([log_decay[...], jnp.zeros((8 - heads, rows), F32)], axis=0)
    parts = []
    for _ in range(3):
        parts.append(value.astype(BF16))
        value = value - parts[-1].astype(F32)
    stacked = jnp.concatenate([part.astype(F32) for part in parts], axis=0).astype(BF16)
    for start in range(0, rows, BLOCK):
        sums = mm(stacked[:, start : start + BLOCK], upper)
        decay[:, start : start + BLOCK] = sums[:8] + sums[8:16] + sums[16:]


def angle_tables(coarse, fine):
    half = DH // 2

    def fill(table, start, stride):
        count = table.shape[1]
        place = lax.broadcasted_iota(jnp.int32, (count, half), 0) * stride + start
        index = lax.broadcasted_iota(jnp.int32, (count, half), 1).astype(F32)
        angle = place.astype(F32) * jnp.exp(index * (-math.log(10000.0) / half))
        table[0] = jnp.cos(angle)
        table[1] = jnp.sin(angle)

    fill(coarse, lax.axis_index("ctx") * coarse.shape[1] * FINE, FINE)
    fill(fine, 0, 1)


def key_value_own_kernel(
    x_far, wk_far, wv_far, wq_far, wg_far, wo_far, log_decay_far,
    x, acc_k, acc_v, decay, coarse, fine, wqg, wo, near_columns, wk, wv, log_decay, arrived,
):
    rows, part = x.shape[0], wk.shape[0]
    core = lax.axis_index("fsdp")
    low = lax.axis_index("tp") % 2
    steps = rows // TILE
    cols = near_columns.shape[1]
    copies = []

    def load(source, target):
        copy = pltpu.make_async_copy(source, target, arrived.at[len(copies)])
        copies.append(copy)
        copy.start()
        return copy

    def load_x(tile, half):
        at = (pl.ds(tile * TILE, TILE), pl.ds(pl.multiple_of(half * part, part), part))
        return load(x_far.at[at], x.at[at])

    logs = load(log_decay_far, log_decay)
    first = [load(wk_far, wk), load_x(0, core)]
    value = load(wv_far, wv)
    own = [load_x(tile, core) for tile in range(1, steps)]
    weight = load(wo_far, wo)
    rest = [load_x(tile, 1 - core) for tile in range(steps)]
    rest += [load(wq_far, wqg.at[pl.ds(0, part)]), load(wg_far, wqg.at[pl.ds(part, part)])]
    angle_tables(coarse, fine)
    logs.wait()
    decay_sums(log_decay, decay)
    for tile in range(steps):
        at = slice(tile * TILE, (tile + 1) * TILE)
        for copy in first if tile == 0 else [own[tile - 1]]:
            copy.wait()
        block = half_of(x, tile * TILE, TILE, core, part)
        acc_k[at, :] = mm(block, wk[...])
        if tile == 0:
            value.wait()
        acc_v[at, :] = mm(block, wv[...])
    weight.wait()
    near_columns[...] = wo[:, pl.ds(pl.multiple_of((1 - low) * cols, cols), cols)]
    for copy in rest:
        copy.wait()


def pack_message(message, states, logs):
    heads = len(states)
    place = lax.broadcasted_iota(jnp.int32, (EXTRA, DH), 0)
    tail = jnp.zeros((EXTRA, DH), F32)
    for head in range(heads):
        message[head * DH : (head + 1) * DH, :] = states[head].astype(BF16)
        rest = logs[head]
        for number in range(3):
            piece = rest.astype(BF16).astype(F32)
            tail = jnp.where(place == 3 * head + number, piece, tail)
            rest = rest - piece
    message[heads * DH :, :] = tail.astype(BF16)


def message_log(message, heads, head):
    tail = message[heads * DH :, :].astype(F32)
    return tail[3 * head : 3 * head + 1] + tail[3 * head + 1 : 3 * head + 2] + tail[3 * head + 2 : 3 * head + 3]


def key_value_kernel(
    heads, x, wk, wv, acc_k, acc_v, decay, coarse, fine, k_out, v_out, before_out, state_out, message
):
    part = wk.shape[0]
    far = 1 - lax.axis_index("fsdp")
    state_out[...] = jnp.zeros_like(state_out)

    def block_step(block, totals):
        start = pl.multiple_of(block * BLOCK, BLOCK)
        columns = decay[:, pl.ds(start, BLOCK)].T
        ending = columns[BLOCK - 1 : BLOCK, :]
        faded = jnp.exp(ending - columns)
        updates = [None] * heads
        for piece in range(BLOCK // TILE):
            first = pl.multiple_of(start + piece * TILE, TILE)
            at = pl.ds(first, TILE)
            rows = half_of(x, first, TILE, far, part)
            cosine, sine = angles(coarse, fine, first, TILE)
            keys = turned(acc_k[at, :] + mm(rows, wk[...]), cosine, sine)
            values = (acc_v[at, :] + mm(rows, wv[...])).astype(BF16)
            k_out[at, :] = keys
            v_out[at, :] = values
            for head in range(heads):
                span = slice(head * DH, (head + 1) * DH)
                fade = faded[piece * TILE : (piece + 1) * TILE, head : head + 1]
                weighted = (keys[:, span].astype(F32) * fade).astype(BF16)
                update = mm_tn(weighted, values[:, span])
                updates[head] = update if piece == 0 else updates[head] + update
        for head in range(heads):
            span = slice(head * DH, (head + 1) * DH)
            old = state_out[span, :]
            before_out[block, span, :] = old.astype(BF16)
            state_out[span, :] = jnp.exp(ending[:, head : head + 1]) * old + updates[head]
        return totals + ending

    totals = lax.fori_loop(0, x.shape[0] // BLOCK, block_step, jnp.zeros((1, 8), F32))
    states = [state_out[head * DH : (head + 1) * DH, :] for head in range(heads)]
    pack_message(message, states, [totals[:, head : head + 1] for head in range(heads)])


def combine_kernel(heads, first, ins, decay, state, *refs):
    if not first:
        old_message, old_entering = refs[:2]
        refs = refs[2:]
    arrivals = refs[:ins]
    window, entering, message = refs[ins:]
    states, logs = [], []
    for head in range(heads):
        span = slice(head * DH, (head + 1) * DH)
        arrived = functools.reduce(lambda a, b: a + b, [got[span, :].astype(F32) for got in arrivals])
        arrived_log = functools.reduce(
            lambda a, b: a + b, [message_log(got, heads, head)[:, :1] for got in arrivals]
        )
        if first:
            ends = [decay[head : head + 1, end - 1 : end] for end in range(BLOCK, decay.shape[1] + 1, BLOCK)]
            window_log = functools.reduce(lambda a, b: a + b, ends)
            entering[span, :] = arrived
            entering_log = arrived_log
        else:
            window_log = message_log(old_message, heads, head)[:, :1]
            before_log = old_entering[heads * DH + head : heads * DH + head + 1, :1]
            entering[span, :] = old_entering[span, :] + jnp.exp(before_log) * arrived
            entering_log = before_log + arrived_log
        entering[heads * DH + head : heads * DH + head + 1, :] = jnp.broadcast_to(entering_log, (1, DH))
        new = state[span, :] + jnp.exp(window_log) * arrived
        window[span, :] = new
        states.append(new)
        logs.append(window_log + arrived_log)
    pack_message(message, states, logs)


def query_gate_kernel(
    heads, block, x, wqg, wqg_far, decay, coarse, fine, k, v, q_out, g_out, intra_out
):
    part = wqg.shape[0] // 2
    core = lax.axis_index("fsdp")
    start = block * BLOCK
    lines = decay[:, start : start + BLOCK]
    columns = lines.T

    def project(piece, carry):
        first = pl.multiple_of(start + piece * TILE, TILE)
        at = pl.ds(pl.multiple_of(piece * TILE, TILE), TILE)
        own = half_of(x, first, TILE, core, part)
        far = half_of(x, first, TILE, 1 - core, part)
        cosine, sine = angles(coarse, fine, first, TILE)
        q_out[at, :] = turned(mm(own, wqg[:part, :]) + mm(far, wqg_far[:part, :]), cosine, sine)
        g_out[at, :] = (mm(own, wqg[part:, :]) + mm(far, wqg_far[part:, :])).astype(BF16)
        return carry

    lax.fori_loop(0, BLOCK // TILE, project, 0)
    for piece in range(BLOCK // TILE):
        low, last = piece * TILE, (piece + 1) * TILE
        place_t = lax.broadcasted_iota(jnp.int32, (TILE, last), 0) + low
        place_s = lax.broadcasted_iota(jnp.int32, (TILE, last), 1)
        causal = place_t >= place_s
        for head in range(heads):
            span = slice(head * DH, (head + 1) * DH)
            scores = mm_nt(q_out[low:last, span], k[start : start + last, span])
            differ = columns[low:last, head : head + 1] - lines[head : head + 1, :last]
            weights = jnp.where(causal, jnp.exp(jnp.where(causal, differ, 0.0)), 0.0)
            intra_out[low:last, span] = mm((scores * weights).astype(BF16), v[start : start + last, span])


def hidden_kernel(heads, starts, ins, decay, entering, before, *refs):
    arrivals, projected, outs = refs[:ins], refs[ins : -len(starts)], refs[-len(starts) :]
    for head in range(heads):
        span = slice(head * DH, (head + 1) * DH)
        entering_log = entering[heads * DH + head : heads * DH + head + 1, :1]
        got = functools.reduce(lambda a, b: a + b, [ref[span, :].astype(F32) for ref in arrivals])
        state = entering[span, :] + jnp.exp(entering_log) * got
        for start, out in zip(starts, outs):
            block = start // BLOCK
            q, gate, intra = projected[3 * block : 3 * block + 3]
            at = slice(start % BLOCK, start % BLOCK + TILE)
            column = jnp.exp(decay[:, start : start + TILE].T[:, head : head + 1])
            scale_log = jnp.zeros((1, 1), F32)
            for earlier in range(block):
                end = (earlier + 1) * BLOCK
                scale_log = scale_log + decay[head : head + 1, end - 1 : end]
            prior = (jnp.exp(scale_log) * state + before[block, span, :].astype(F32)).astype(BF16)
            retained = intra[at, span] + column * mm(q[at, span], prior)
            center = retained - jnp.mean(retained, axis=1, keepdims=True)
            spread = jnp.mean(center * center, axis=1, keepdims=True)
            value = gate[at, span].astype(F32)
            silu = value / (1.0 + jnp.exp(-value))
            out[:, span] = (silu * center * lax.rsqrt(spread + 1e-5)).astype(BF16)


def arrange_kernel(near_first, near_second, high_first, high_second, low_out, high_out):
    cols = near_first.shape[1]
    place, core = lax.axis_index("tp"), lax.axis_index("fsdp")
    high, low = place // 2, place % 2
    here = core == high
    mine = pl.ds(pl.multiple_of(low * cols, cols), cols)
    flipped = pl.ds(pl.multiple_of((1 - low) * cols, cols), cols)
    low_out[:, :cols] = jnp.where(here, near_second[...], near_first[...])
    low_out[:, cols:] = jnp.where(here, near_first[...], near_second[...])
    high_out[:, :cols] = jnp.where(here, high_first[:, flipped], high_second[:, flipped])
    high_out[:, cols:] = jnp.where(here, high_first[:, mine], high_second[:, mine])


def own_kernel(order, own_first, own_second, *refs):
    pieces, outs = refs[: len(order)], refs[len(order) :]
    cols = pieces[0].shape[1]
    place, core = lax.axis_index("tp"), lax.axis_index("fsdp")
    high, low = place // 2, place % 2
    here = core == high
    mine = pl.ds(pl.multiple_of(low * cols, cols), cols)
    flipped = pl.ds(pl.multiple_of((1 - low) * cols, cols), cols)
    keep = jnp.where(here, own_first[:, mine], own_second[:, mine])
    gives = [
        jnp.where(here, own_second[:, mine], own_first[:, mine]),
        jnp.where(here, own_first[:, flipped], own_second[:, flipped]),
    ]
    for (half, number), piece in zip(order, pieces):
        at = slice(number * TILE, (number + 1) * TILE)
        outs[half][at, :cols] = mm(piece[...], gives[half])
        outs[half][at, cols:] = mm(piece[...], keep)


def give_kernel(number, own, far, weight, out):
    cols = out.shape[1]
    at = slice(number * TILE, (number + 1) * TILE)
    out[...] = (own[at, :cols] + mm(far[...], weight[:, :cols])).astype(BF16)


def keep_kernel(order, *refs):
    count = len(order)
    fars, owns, weights, outs = refs[:count], refs[count : count + 2], refs[count + 2 : count + 4], refs[count + 4 :]
    for (half, number), far in zip(order, fars):
        cols = far.shape[1]
        at = slice(number * TILE, (number + 1) * TILE)
        outs[half][at, :] = owns[half][at, cols:] + mm(far[...], weights[half][:, cols:])


def finish_kernel(order, *refs):
    gots, keeps, out = refs[: len(order)], refs[len(order) : -1], refs[-1]
    for (half, number), got in zip(order, gots):
        keep = keeps[half]
        at = slice(number * TILE, (number + 1) * TILE)
        value = keep[at, :] + got[...].astype(F32)
        start = half * keep.shape[0] + number * TILE
        out[0, start : start + TILE, :] = value.astype(BF16)


def after(value, *others):
    return lax.optimization_barrier((value, *others))[0]


def on_device(tokens, query_weight, key_weight, value_weight, gate_weight, out_weight, log_decay):
    x = tokens[0]
    rows, width = x.shape
    part, cols = query_weight.shape
    heads = cols // DH
    blocks = rows // BLOCK
    ctx, tp, cores = lax.axis_size("ctx"), lax.axis_size("tp"), lax.axis_size("fsdp")
    assert tp == 4 and cores == 2 and ctx > 2
    near_mask, far_mask = 1, 2
    tables = [((2, rows // FINE, DH // 2), F32), ((2, FINE, DH // 2), F32)]

    key_far = swap(key_weight, "fsdp", 1)
    value_far = swap(value_weight, "fsdp", 1)

    own_outs = [((rows, width), BF16), ((rows, cols), F32), ((rows, cols), F32), ((8, rows), F32)] + tables
    own_outs += [((2 * part, cols), BF16), (out_weight.shape, BF16), ((cols, cols), BF16)]
    loaded = (x, key_weight, value_weight, query_weight, gate_weight, out_weight, log_decay[0].T)
    in_hbm = [pltpu.with_memory_space_constraint(array, pltpu.HBM) for array in loaded]
    x, acc_k, acc_v, decay, coarse, fine, own_qg, out_weight, for_near = pl.pallas_call(
        key_value_own_kernel,
        in_specs=[pl.BlockSpec(memory_space=pltpu.HBM)] * len(in_hbm),
        out_specs=[pl.BlockSpec(memory_space=pltpu.VMEM)] * len(own_outs),
        out_shape=[pltpu.VMEM(shape, dtype) for shape, dtype in own_outs],
        scratch_shapes=[
            pltpu.VMEM((part, cols), BF16),
            pltpu.VMEM((part, cols), BF16),
            pltpu.VMEM((heads, rows), F32),
            pltpu.SemaphoreType.DMA((2 * (rows // TILE) + 6,)),
        ],
        compiler_params=pltpu.CompilerParams(vmem_limit_bytes=VMEM_LIMIT),
        cost_estimate=pl.CostEstimate(flops=1, bytes_accessed=1, transcendentals=0),
        name="key_value_own",
    )(*in_hbm)
    state_shape = (heads * DH, DH)
    message_shape = (heads * DH + EXTRA, DH)
    keys, values, before, state, message = kernel_call(
        functools.partial(key_value_kernel, heads),
        [
            ((rows, cols), BF16),
            ((rows, cols), BF16),
            ((blocks, *state_shape), BF16),
            (state_shape, F32),
            (message_shape, BF16),
        ],
        [x, key_far, value_far, acc_k, acc_v, decay, coarse, fine],
        "key_value",
    )

    far_qg = swap(after(own_qg, message), "fsdp", 1)

    def query_gate(block, decay):
        return kernel_call(
            functools.partial(query_gate_kernel, heads, block),
            [((BLOCK, cols), BF16), ((BLOCK, cols), BF16), ((BLOCK, cols), F32)],
            [x, own_qg, far_qg, decay, coarse, fine, keys, values],
            "query_gate",
        )

    near_first = swap(after(for_near, message), "tp", near_mask)
    high_pairs = [((at ^ far_mask) * cores + at // 2, at * cores + at // 2) for at in range(tp)]
    core_pairs = [(at * cores + at // 2, at * cores + 1 - at // 2) for at in range(tp)]
    late_weight = after(out_weight, message)
    high_pass = lax.ppermute(late_weight, ("tp", "fsdp"), high_pairs)
    own_second = swap(late_weight, "fsdp", 1)

    projected = [query_gate(0, decay)]
    window, entering, hop, early = state, None, 1, None
    held = after(decay, *projected[0])
    while True:
        grown = hop // 2
        late = [(source, source + hop) for source in range(grown, ctx - hop)]
        arrivals = [lax.ppermute(message, "ctx", late)] + ([early] if early is not None else [])
        if 2 * hop >= ctx:
            break
        unchanged = [(source, source + 2 * hop) for source in range(hop) if source + 2 * hop < ctx]
        early = lax.ppermute(message, "ctx", unchanged)
        old = [] if entering is None else [message, entering]
        window, entering, message = kernel_call(
            functools.partial(combine_kernel, heads, entering is None, len(arrivals)),
            [(state_shape, F32), (message_shape, F32), (message_shape, BF16)],
            [held, window, *old, *arrivals],
            "combine",
        )
        hop *= 2

    held = after(decay, message, near_first, *arrivals[1:])
    for block in range(1, blocks):
        projected.append(query_gate(block, held))
    projected = [array for arrays in projected for array in arrays]

    count = rows // 2 // TILE
    masks = (near_mask, far_mask)
    hidden, far = [[], []], [[], []]
    for number in range(count):
        held = after(decay, pair[0]) if number else decay
        pair = kernel_call(
            functools.partial(hidden_kernel, heads, [(half * count + number) * TILE for half in range(2)], len(arrivals)),
            [((TILE, cols), BF16)] * 2,
            [held, entering, before, *arrivals, *projected],
            "hidden",
        )
        for half in range(2):
            hidden[half].append(pair[half])
            far[half].append(swap(pair[half], "tp", masks[half]))
    near_second = swap(after(near_first, hidden[0][-1]), "fsdp", 1)
    high_other = lax.ppermute(after(high_pass, hidden[0][-1]), ("tp", "fsdp"), core_pairs)
    weights = kernel_call(
        arrange_kernel,
        [((cols, 2 * cols), BF16)] * 2,
        [near_first, near_second, high_pass, high_other],
        "arrange",
    )
    order = [(half, number) for number in reversed(range(count)) for half in (1, 0)]
    owns = kernel_call(
        functools.partial(own_kernel, order),
        [((count * TILE, 2 * cols), F32)] * 2,
        [out_weight, own_second, *(hidden[half][number] for half, number in order)],
        "own_products",
    )
    gots = []
    for half, number in order:
        [give] = kernel_call(
            functools.partial(give_kernel, number),
            [((TILE, cols), BF16)],
            [owns[half], far[half][number], weights[half]],
            "give",
        )
        gots.append(swap(give, "tp", masks[1 - half]))
    keeps = kernel_call(
        functools.partial(keep_kernel, order),
        [((count * TILE, cols), F32)] * 2,
        [*(far[half][number] for half, number in order), *owns, *weights],
        "keep",
    )
    arrays = [pltpu.with_memory_space_constraint(array, pltpu.VMEM) for array in (*gots, *keeps)]
    return pl.pallas_call(
        functools.partial(finish_kernel, order),
        in_specs=[pl.BlockSpec(memory_space=pltpu.VMEM)] * len(arrays),
        out_specs=pl.BlockSpec(memory_space=pltpu.VMEM),
        out_shape=jax.ShapeDtypeStruct((1, rows, cols), BF16),
        compiler_params=pltpu.CompilerParams(vmem_limit_bytes=VMEM_LIMIT),
        name="finish",
    )(*arrays)


def solution(mesh):
    in_specs = (
        P("fsdp", "ctx", None),
        P("fsdp", "tp"),
        P("fsdp", "tp"),
        P("fsdp", "tp"),
        P("fsdp", "tp"),
        P("tp", "fsdp"),
        P("fsdp", "ctx", "tp"),
    )
    out_specs = P("fsdp", "ctx", "tp")
    return jax.shard_map(
        on_device, mesh=mesh, in_specs=in_specs, out_specs=out_specs, check_vma=False
    )
```

time: 81.8 us -> 66.4 us (0.81)
  Pallas kernels: 31.9 us -> 23.5 us
  local copies, waits for them, and re-layouts: 5.35 us -> 0 us
  waiting for transfers between devices: 24.8 us -> 20.7 us
  starting transfers between devices: 18.8 us -> 21.3 us
    pallas_call x17 -> x13, Pallas kernels: 30.7 us -> 17.8 us  [kernel_call(): pl.pallas_call(kernel, in_specs=[pl.BlockSpec(memory_space=pltpu.VMEM)] *...]
    ppermute x4 -> x5, waiting for transfers between devices: 17.1 us -> 6.89 us  [the longest x2 6.88 us: on_device(): lax.ppermute(message, 'ctx', late)]
    ppermute x15 -> x14, waiting for transfers between devices: 7.61 us -> 13.8 us  [swap(): lax.ppermute(value, axis, [(place, place ^ mask) for place in range(size)])]
    unnamed x14 -> x0, local copies, waits for them, and re-layouts: 5.35 us -> none
    pallas_call x1 -> x2, Pallas kernels: 1.14 us -> 5.71 us  [the longest x1 4.57 us: on_device(): pl.pallas_call(key_value_own_kernel, in_specs=[pl.BlockSpec(memory_space=...]
    ppermute x4 -> x5, starting transfers between devices: 5.52 us -> 7.09 us  [the longest x2 2.57 us: on_device(): lax.ppermute(message, 'ctx', late)]
    ppermute x15 -> x14, starting transfers between devices: 13.3 us -> 14.2 us  [swap(): lax.ppermute(value, axis, [(place, place ^ mask) for place in range(size)])]
  transfers between devices with their start and end apart: 19 -> 19, of which waited for: 6 -> 7; matrix products, arithmetic and copies ran while one was open for 0% -> 0% of each run, Pallas kernels for 38% -> 29%
where the time goes in v4:
time: 66.4 us; the launch traced here: 65.8 us
  Pallas kernels  23.5 us (35%)
  starting transfers between devices  21.3 us (32%)
  waiting for transfers between devices  20.7 us (31%)
    pallas_call x13, Pallas kernels, kernel_call(): pl.pallas_call(kernel, in_specs=[pl.BlockSpec(memory_space=pltpu.VMEM)] *...  17.8 us
    ppermute x14, starting transfers between devices, swap(): lax.ppermute(value, axis, [(place, place ^ mask) for place in range(size)])  14.2 us
    ppermute x14, waiting for transfers between devices, swap(): lax.ppermute(value, axis, [(place, place ^ mask) for place in range(size)])  13.8 us
    ppermute x2, waiting for transfers between devices, on_device(): lax.ppermute(message, 'ctx', late)  6.88 us
    pallas_call x1, Pallas kernels, on_device(): pl.pallas_call(key_value_own_kernel, in_specs=[pl.BlockSpec(memory_space=...  4.57 us
    ppermute x2, starting transfers between devices, on_device(): lax.ppermute(message, 'ctx', late)  2.57 us
    ppermute x1, starting transfers between devices, on_device(): lax.ppermute(after(high_pass, hidden[0][-1]), ('tp', 'fsdp'), core_pairs)  2.56 us
  transfers between devices with their start and end apart: 19, of which 7 were waited for; matrix products, arithmetic and copies ran while one was open for 0% of the time, Pallas kernels for 29%

profile of v4, /device:TPU:24, one launch (start us, length us, event | category | flops | bytes accessed | tf_op | source)
XLA Modules:
  0.0 65.8 jit_solution(11410827148045936661)
XLA Ops:
  0.5 4.6 %key_value_own.1 = (bf16[1024,2048]{1,0:T(8,128)(2,1)S(1)}, f32[1024,512]{1,0:T(8,128)S(1)}, f32[1024,512]{1,0:T(8,128)S(1)}, f32[8,1024]{1,0:T(8,128)S(1)}, f32...) custom-call(bf16[1024,2048]{1,0:T(8,128)(2,1)} %bitcast.4, ...), custom_call_target="tpu_custom_call" | custom-call | flops 1 | bytes 1 | tf_op jit(solution)/shard_map/key_value_own/pallas_call | solution.py:383
  5.1 3.3 %key_value.1 = (bf16[1024,512]{1,0:T(8,128)(2,1)S(1)}, bf16[1024,512]{1,0:T(8,128)(2,1)S(1)}, bf16[2,512,256]{2,1,0:T(8,128)(2,1)S(1)}, f32[512,256]{1,0:T(8,128)S(1)}, bf16[528,256]{1,0:T(8,128)(2,1)S(1)}) custom-call(bf16[1024,2048]{1,0:T(8,128)(2,1)S(1)} %get-tuple-element.46.x, bf16[1024,512]{1,0:T(8,128)(2,1)S(1)} %collective-permute-done.wk, ...), custom_call_target="tpu_custom_call" | custom-call | flops 1 | bytes 1 | tf_op jit(solution)/shard_map/key_value/pallas_call | solution.py:40
  8.5 1.3 %collective-permute-start.10 = (bf16[512,1024]{1,0:T(8,128)(2,1)S(1)}, bf16[512,1024]{1,0:T(8,128)(2,1)S(1)}, u32[]{:S(2)}, u32[]{:S(2)}) collective-permute-start(bf16[512,1024]{1,0:T(8,128)(2,1)S(1)} %get-tuple-element.53.own_first), channel_id=1, source_target_pairs={{4,0},{6,2},{1,5},{3,7},{12,8},{14,10},{9,13},{11,15},{20,16},{22,... | collective-permute-start | bytes 3145736 | tf_op jit(solution)/shard_map/ppermute | solution.py:427
  9.8 1.3 %collective-permute-start.4 = (bf16[528,256]{1,0:T(8,128)(2,1)S(1)}, bf16[528,256]{1,0:T(8,128)(2,1)S(1)}, u32[]{:S(2)}, u32[]{:S(2)}) collective-permute-start(bf16[528,256]{1,0:T(8,128)(2,1)S(1)} %get-tuple-element.52), channel_id=1, source_target_pairs={{0,8},{8,16},{16,24},{1,9},{9,17},{17,25},{2,10},{10,18},{18,26},{... | collective-permute-start | bytes 811016 | tf_op jit(solution)/shard_map/ppermute | solution.py:436
  11.1 1.6 %collective-permute-start.7 = (bf16[512,512]{1,0:T(8,128)(2,1)S(1)}, bf16[512,512]{1,0:T(8,128)(2,1)S(1)}, u32[]{:S(2)}, u32[]{:S(2)}) collective-permute-start(bf16[512,512]{1,0:T(8,128)(2,1)S(1)} %get-tuple-element.67), channel_id=1, source_target_pairs={{0,2},{2,0},{4,6},{6,4},{1,3},{3,1},{5,7},{7,5},{8,10},{10,8},{12,... | collective-permute-start | bytes 1572872 | tf_op jit(solution)/shard_map/ppermute | solution.py:35
  12.7 0.7 %collective-permute-start.6 = (bf16[528,256]{1,0:T(8,128)(2,1)S(1)}, bf16[528,256]{1,0:T(8,128)(2,1)S(1)}, u32[]{:S(2)}, u32[]{:S(2)}) collective-permute-start(bf16[528,256]{1,0:T(8,128)(2,1)S(1)} %get-tuple-element.52), channel_id=1, source_target_pairs={{0,16},{1,17},{2,18},{3,19},{4,20},{5,21},{6,22},{7,23}} | collective-permute-start | bytes 811016 | tf_op jit(solution)/shard_map/ppermute | solution.py:440
  13.4 3.5 %query_gate.2 = (bf16[512,512]{1,0:T(8,128)(2,1)S(1)}, bf16[512,512]{1,0:T(8,128)(2,1)S(1)}, f32[512,512]{1,0:T(8,128)S(1)}) custom-call(bf16[1024,2048]{1,0:T(8,128)(2,1)S(1)} %get-tuple-element.46.x, bf16[2048,512]{1,0:T(8,128)(2,1)S(1)} %get-tuple-element.55.wqg, bf16[2048,512]{1,0:T(8,128)(2,1)S(1)} %collective-permute-done.3.wqg_far, ...), custom_call_target="tpu_custom_call" | custom-call | flops 1 | bytes 1 | tf_op jit(solution)/shard_map/query_gate/pallas_call | solution.py:40
  16.9 2.7 %collective-permute-done.4.refs_0_ = bf16[528,256]{1,0:T(8,128)(2,1)S(1)} collective-permute-done((bf16[528,256]{1,0:T(8,128)(2,1)S(1)}, bf16[528,256]{1,0:T(8,128)(2,1)S(1)}, u32[]{:S(2)}, u32[]{:S(2)}) %collective-permute-start.4) | collective-permute-done | bytes 270368 | tf_op jit(solution)/shard_map/ppermute | solution.py:436
  19.6 1.0 %combine.1 = (f32[512,256]{1,0:T(8,128)}, f32[528,256]{1,0:T(8,128)S(1)}, bf16[528,256]{1,0:T(8,128)(2,1)S(1)}) custom-call(f32[8,1024]{1,0:T(8,128)S(1)} %get-tuple-element.73.decay, f32[512,256]{1,0:T(8,128)S(1)} %get-tuple-element.62.state, bf16[528,256]{1,0:T(8,128)(2,1)S(1)} %collective-permute-done.4.refs_0_), custom_call_target="tpu_custom_call" | custom-call | flops 1 | bytes 1 | tf_op jit(solution)/shard_map/combine/pallas_call | solution.py:40
  20.6 1.3 %collective-permute-start.5 = (bf16[528,256]{1,0:T(8,128)(2,1)S(1)}, bf16[528,256]{1,0:T(8,128)(2,1)S(1)}, u32[]{:S(2)}, u32[]{:S(2)}) collective-permute-start(bf16[528,256]{1,0:T(8,128)(2,1)S(1)} %get-tuple-element.65), channel_id=1, source_target_pairs={{8,24},{9,25},{10,26},{11,27},{12,28},{13,29},{14,30},{15,31}} | collective-permute-start | bytes 811016 | tf_op jit(solution)/shard_map/ppermute | solution.py:436
  21.9 1.7 %collective-permute-start.2 = (bf16[512,1024]{1,0:T(8,128)(2,1)S(1)}, bf16[512,1024]{1,0:T(8,128)(2,1)S(1)}, u32[]{:S(2)}, u32[]{:S(2)}) collective-permute-start(bf16[512,1024]{1,0:T(8,128)(2,1)S(1)} %get-tuple-element.53.own_first), channel_id=1, source_target_pairs={{0,1},{1,0},{2,3},{3,2},{4,5},{5,4},{6,7},{7,6},{8,9},{9,8},{10,11... | collective-permute-start | bytes 3145736 | tf_op jit(solution)/shard_map/ppermute | solution.py:35
  23.6 0.9 %collective-permute-done.7.near_first = bf16[512,512]{1,0:T(8,128)(2,1)S(1)} collective-permute-done((bf16[512,512]{1,0:T(8,128)(2,1)S(1)}, bf16[512,512]{1,0:T(8,128)(2,1)S(1)}, u32[]{:S(2)}, u32[]{:S(2)}) %collective-permute-start.7) | collective-permute-done | bytes 524320 | tf_op jit(solution)/shard_map/ppermute | solution.py:35
  24.5 3.5 %query_gate.3 = (bf16[512,512]{1,0:T(8,128)(2,1)S(1)}, bf16[512,512]{1,0:T(8,128)(2,1)S(1)}, f32[512,512]{1,0:T(8,128)S(1)}) custom-call(bf16[1024,2048]{1,0:T(8,128)(2,1)S(1)} %get-tuple-element.46.x, bf16[2048,512]{1,0:T(8,128)(2,1)S(1)} %get-tuple-element.55.wqg, bf16[2048,512]{1,0:T(8,128)(2,1)S(1)} %collective-permute-done.3.wqg_far, ...), custom_call_target="tpu_custom_call" | custom-call | flops 1 | bytes 1 | tf_op jit(solution)/shard_map/query_gate/pallas_call | solution.py:40
  28.0 4.2 %collective-permute-done.5.refs_0_ = bf16[528,256]{1,0:T(8,128)(2,1)S(1)} collective-permute-done((bf16[528,256]{1,0:T(8,128)(2,1)S(1)}, bf16[528,256]{1,0:T(8,128)(2,1)S(1)}, u32[]{:S(2)}, u32[]{:S(2)}) %collective-permute-start.5) | collective-permute-done | bytes 270368 | tf_op jit(solution)/shard_map/ppermute | solution.py:436
  32.2 1.5 %hidden.2 = (bf16[256,512]{1,0:T(8,128)(2,1)S(1)}, bf16[256,512]{1,0:T(8,128)(2,1)S(1)}) custom-call(f32[8,1024]{1,0:T(8,128)S(1)} %get-tuple-element.73.decay, f32[528,256]{1,0:T(8,128)S(1)} %get-tuple-element.63.entering, bf16[2,512,256]{2,1,0:T(8,128)(2,1)S(1)} %get-tuple-element.64.before, bf16[528,256]{1,0:T(8,128)(2,1)S(1)} %collective-permute-done.5.refs_0_, ...), custom_call_target="tpu_custom_call" | custom-call | flops 1 | bytes 1 | tf_op jit(solution)/shard_map/hidden/pallas_call | solution.py:40
  33.7 1.5 %hidden.3 = (bf16[256,512]{1,0:T(8,128)(2,1)S(1)}, bf16[256,512]{1,0:T(8,128)(2,1)S(1)}) custom-call(f32[8,1024]{1,0:T(8,128)S(1)} %get-tuple-element.73.decay, f32[528,256]{1,0:T(8,128)S(1)} %get-tuple-element.63.entering, bf16[2,512,256]{2,1,0:T(8,128)(2,1)S(1)} %get-tuple-element.64.before, bf16[528,256]{1,0:T(8,128)(2,1)S(1)} %collective-permute-done.5.refs_0_, ...), custom_call_target="tpu_custom_call" | custom-call | flops 1 | bytes 1 | tf_op jit(solution)/shard_map/hidden/pallas_call | solution.py:40
  35.2 2.6 %collective-permute-start.11 = (bf16[512,1024]{1,0:T(8,128)(2,1)S(1)}, bf16[512,1024]{1,0:T(8,128)(2,1)S(1)}, u32[]{:S(2)}, u32[]{:S(2)}) collective-permute-start(bf16[512,1024]{1,0:T(8,128)(2,1)S(1)} %collective-permute-done.10.high_first), channel_id=1, source_target_pairs={{0,1},{2,3},{5,4},{7,6},{8,9},{10,11},{13,12},{15,14},{16,17},{18,... | collective-permute-start | bytes 3145736 | tf_op jit(solution)/shard_map/ppermute | solution.py:470
  37.8 1.6 %collective-permute-start.17 = (bf16[256,512]{1,0:T(8,128)(2,1)S(1)}, bf16[256,512]{1,0:T(8,128)(2,1)S(1)}, u32[]{:S(2)}, u32[]{:S(2)}) collective-permute-start(bf16[256,512]{1,0:T(8,128)(2,1)S(1)} %get-tuple-element.72.refs_3_), channel_id=1, source_target_pairs={{0,2},{2,0},{4,6},{6,4},{1,3},{3,1},{5,7},{7,5},{8,10},{10,8},{12,... | collective-permute-start | bytes 786440 | tf_op jit(solution)/shard_map/ppermute | solution.py:35
  39.4 1.4 %collective-permute-start.15 = (bf16[256,512]{1,0:T(8,128)(2,1)S(1)}, bf16[256,512]{1,0:T(8,128)(2,1)S(1)}, u32[]{:S(2)}, u32[]{:S(2)}) collective-permute-start(bf16[256,512]{1,0:T(8,128)(2,1)S(1)} %get-tuple-element.76.refs_2_), channel_id=1, source_target_pairs={{0,4},{2,6},{4,0},{6,2},{1,5},{3,7},{5,1},{7,3},{8,12},{10,14},{12... | collective-permute-start | bytes 786440 | tf_op jit(solution)/shard_map/ppermute | solution.py:35
  40.8 0.5 collective-permute-start.13
  41.4 0.6 collective-permute-start.8
  42.0 1.3 %own_products.1 = (f32[512,1024]{1,0:T(8,128)S(1)}, f32[512,1024]{1,0:T(8,128)S(1)}) custom-call(bf16[512,1024]{1,0:T(8,128)(2,1)S(1)} %get-tuple-element.53.own_first, bf16[512,1024]{1,0:T(8,128)(2,1)S(1)} %collective-permute-done.2.own_second, bf16[256,512]{1,0:T(8,128)(2,1)S(1)} %get-tuple-element.74.refs_0_, ...), custom_call_target="tpu_custom_call" | custom-call | flops 1 | bytes 1 | tf_op jit(solution)/shard_map/own_products/pallas_call | solution.py:40
  43.5 3.5 %collective-permute-done.17.far.refs_3_ = bf16[256,512]{1,0:T(8,128)(2,1)S(1)} collective-permute-done((bf16[256,512]{1,0:T(8,128)(2,1)S(1)}, bf16[256,512]{1,0:T(8,128)(2,1)S(1)}, u32[]{:S(2)}, u32[]{:S(2)}) %collective-permute-start.17) | collective-permute-done | bytes 262176 | tf_op jit(solution)/shard_map/ppermute | solution.py:35
  47.3 1.6 %collective-permute-start.18 = (bf16[256,512]{1,0:T(8,128)(2,1)S(1)}, bf16[256,512]{1,0:T(8,128)(2,1)S(1)}, u32[]{:S(2)}, u32[]{:S(2)}) collective-permute-start(bf16[256,512]{1,0:T(8,128)(2,1)S(1)} %give.7), channel_id=1, source_target_pairs={{0,4},{2,6},{4,0},{6,2},{1,5},{3,7},{5,1},{7,3},{8,12},{10,14},{12... | collective-permute-start | bytes 786440 | tf_op jit(solution)/shard_map/ppermute | solution.py:35
  49.2 1.6 %collective-permute-start.16 = (bf16[256,512]{1,0:T(8,128)(2,1)S(1)}, bf16[256,512]{1,0:T(8,128)(2,1)S(1)}, u32[]{:S(2)}, u32[]{:S(2)}) collective-permute-start(bf16[256,512]{1,0:T(8,128)(2,1)S(1)} %give.6), channel_id=1, source_target_pairs={{0,2},{2,0},{4,6},{6,4},{1,3},{3,1},{5,7},{7,5},{8,10},{10,8},{12,... | collective-permute-start | bytes 786440 | tf_op jit(solution)/shard_map/ppermute | solution.py:35
  50.7 1.9 %collective-permute-done.13.far.refs_1_ = bf16[256,512]{1,0:T(8,128)(2,1)S(1)} collective-permute-done((bf16[256,512]{1,0:T(8,128)(2,1)S(1)}, bf16[256,512]{1,0:T(8,128)(2,1)S(1)}, u32[]{:S(2)}, u32[]{:S(2)}) %collective-permute-start.13) | collective-permute-done | bytes 262176 | tf_op jit(solution)/shard_map/ppermute | solution.py:35
  52.9 1.6 %collective-permute-start.14 = (bf16[256,512]{1,0:T(8,128)(2,1)S(1)}, bf16[256,512]{1,0:T(8,128)(2,1)S(1)}, u32[]{:S(2)}, u32[]{:S(2)}) collective-permute-start(bf16[256,512]{1,0:T(8,128)(2,1)S(1)} %give.5), channel_id=1, source_target_pairs={{0,4},{2,6},{4,0},{6,2},{1,5},{3,7},{5,1},{7,3},{8,12},{10,14},{12... | collective-permute-start | bytes 786440 | tf_op jit(solution)/shard_map/ppermute | solution.py:35
  54.8 1.6 %collective-permute-start.12 = (bf16[256,512]{1,0:T(8,128)(2,1)S(1)}, bf16[256,512]{1,0:T(8,128)(2,1)S(1)}, u32[]{:S(2)}, u32[]{:S(2)}) collective-permute-start(bf16[256,512]{1,0:T(8,128)(2,1)S(1)} %give.4), channel_id=1, source_target_pairs={{0,2},{2,0},{4,6},{6,4},{1,3},{3,1},{5,7},{7,5},{8,10},{10,8},{12,... | collective-permute-start | bytes 786440 | tf_op jit(solution)/shard_map/ppermute | solution.py:35
  56.4 0.7 %keep.1 = (f32[512,512]{1,0:T(8,128)S(1)}, f32[512,512]{1,0:T(8,128)S(1)}) custom-call(bf16[256,512]{1,0:T(8,128)(2,1)S(1)} %collective-permute-done.8.far.refs_0_, bf16[256,512]{1,0:T(8,128)(2,1)S(1)} %collective-permute-done.13.far.refs_1_, bf16[256,512]{1,0:T(8,128)(2,1)S(1)} %collective-permute-done.15.far.refs_2_, ...), custom_call_target="tpu_custom_call" | custom-call | flops 1 | bytes 1 | tf_op jit(solution)/shard_map/keep/pallas_call | solution.py:40
  57.1 2.7 %collective-permute-done.18.refs_3_ = bf16[256,512]{1,0:T(8,128)(2,1)S(1)} collective-permute-done((bf16[256,512]{1,0:T(8,128)(2,1)S(1)}, bf16[256,512]{1,0:T(8,128)(2,1)S(1)}, u32[]{:S(2)}, u32[]{:S(2)}) %collective-permute-start.18) | collective-permute-done | bytes 262176 | tf_op jit(solution)/shard_map/ppermute | solution.py:35
  59.8 4.8 %collective-permute-done.14.refs_1_ = bf16[256,512]{1,0:T(8,128)(2,1)S(1)} collective-permute-done((bf16[256,512]{1,0:T(8,128)(2,1)S(1)}, bf16[256,512]{1,0:T(8,128)(2,1)S(1)}, u32[]{:S(2)}, u32[]{:S(2)}) %collective-permute-start.14) | collective-permute-done | bytes 262176 | tf_op jit(solution)/shard_map/ppermute | solution.py:35
  64.6 1.1 %finish.1 = bf16[1,1024,512]{2,1,0:T(8,128)(2,1)} custom-call(bf16[256,512]{1,0:T(8,128)(2,1)S(1)} %collective-permute-done.12.refs_0_, bf16[256,512]{1,0:T(8,128)(2,1)S(1)} %collective-permute-done.14.refs_1_, bf16[256,512]{1,0:T(8,128)(2,1)S(1)} %collective-permute-done.16.refs_2_, bf16[256,512]{1,0:T(8,128)(2,1)S(1)} %collective-permute-done.18.refs_3_, ...), custom_call_target="tpu_custom_call" | custom-call | tf_op jit(solution)/shard_map/finish/pallas_call | solution.py:500
  (21 shorter events, 2.1 us)
Async XLA Ops:
  0.0 5.1 %collective-permute-start = (bf16[1024,512]{1,0:T(8,128)(2,1)}, bf16[1024,512]{1,0:T(8,128)(2,1)S(1)}, u32[]{:S(2)}, u32[]{:S(2)}) collective-permute-start(bf16[1024,512]{1,0:T(8,128)(2,1)} %wk_far.1), channel_id=1, source_target_pairs={{0,1},{1,0},{2,3},{3,2},{4,5},{5,4},{6,7},{7,6},{8,9},{9,8},{10,11... | collective-permute-start | bytes 3145736 | tf_op jit(solution)/shard_map/ppermute | solution.py:35
  0.0 5.1 %collective-permute-start.1 = (bf16[1024,512]{1,0:T(8,128)(2,1)}, bf16[1024,512]{1,0:T(8,128)(2,1)S(1)}, u32[]{:S(2)}, u32[]{:S(2)}) collective-permute-start(bf16[1024,512]{1,0:T(8,128)(2,1)} %wv_far.1), channel_id=1, source_target_pairs={{0,1},{1,0},{2,3},{3,2},{4,5},{5,4},{6,7},{7,6},{8,9},{9,8},{10,11... | collective-permute-start | bytes 3145736 | tf_op jit(solution)/shard_map/ppermute | solution.py:35
  8.5 4.9 %collective-permute-start.3 = (bf16[2048,512]{1,0:T(8,128)(2,1)S(1)}, bf16[2048,512]{1,0:T(8,128)(2,1)S(1)}, u32[]{:S(2)}, u32[]{:S(2)}) collective-permute-start(bf16[2048,512]{1,0:T(8,128)(2,1)S(1)} %get-tuple-element.55.wqg), channel_id=1, source_target_pairs={{0,1},{1,0},{2,3},{3,2},{4,5},{5,4},{6,7},{7,6},{8,9},{9,8},{10,11... | collective-permute-start | bytes 6291464 | tf_op jit(solution)/shard_map/ppermute | solution.py:35
  8.5 26.6 %collective-permute-start.10 = (bf16[512,1024]{1,0:T(8,128)(2,1)S(1)}, bf16[512,1024]{1,0:T(8,128)(2,1)S(1)}, u32[]{:S(2)}, u32[]{:S(2)}) collective-permute-start(bf16[512,1024]{1,0:T(8,128)(2,1)S(1)} %get-tuple-element.53.own_first), channel_id=1, source_target_pairs={{4,0},{6,2},{1,5},{3,7},{12,8},{14,10},{9,13},{11,15},{20,16},{22,... | collective-permute-start | bytes 3145736 | tf_op jit(solution)/shard_map/ppermute | solution.py:427
  9.8 9.8 %collective-permute-start.4 = (bf16[528,256]{1,0:T(8,128)(2,1)S(1)}, bf16[528,256]{1,0:T(8,128)(2,1)S(1)}, u32[]{:S(2)}, u32[]{:S(2)}) collective-permute-start(bf16[528,256]{1,0:T(8,128)(2,1)S(1)} %get-tuple-element.52), channel_id=1, source_target_pairs={{0,8},{8,16},{16,24},{1,9},{9,17},{17,25},{2,10},{10,18},{18,26},{... | collective-permute-start | bytes 811016 | tf_op jit(solution)/shard_map/ppermute | solution.py:436
  11.1 13.4 %collective-permute-start.7 = (bf16[512,512]{1,0:T(8,128)(2,1)S(1)}, bf16[512,512]{1,0:T(8,128)(2,1)S(1)}, u32[]{:S(2)}, u32[]{:S(2)}) collective-permute-start(bf16[512,512]{1,0:T(8,128)(2,1)S(1)} %get-tuple-element.67), channel_id=1, source_target_pairs={{0,2},{2,0},{4,6},{6,4},{1,3},{3,1},{5,7},{7,5},{8,10},{10,8},{12,... | collective-permute-start | bytes 1572872 | tf_op jit(solution)/shard_map/ppermute | solution.py:35
  12.7 10.9 %collective-permute-start.6 = (bf16[528,256]{1,0:T(8,128)(2,1)S(1)}, bf16[528,256]{1,0:T(8,128)(2,1)S(1)}, u32[]{:S(2)}, u32[]{:S(2)}) collective-permute-start(bf16[528,256]{1,0:T(8,128)(2,1)S(1)} %get-tuple-element.52), channel_id=1, source_target_pairs={{0,16},{1,17},{2,18},{3,19},{4,20},{5,21},{6,22},{7,23}} | collective-permute-start | bytes 811016 | tf_op jit(solution)/shard_map/ppermute | solution.py:440
  20.6 11.6 %collective-permute-start.5 = (bf16[528,256]{1,0:T(8,128)(2,1)S(1)}, bf16[528,256]{1,0:T(8,128)(2,1)S(1)}, u32[]{:S(2)}, u32[]{:S(2)}) collective-permute-start(bf16[528,256]{1,0:T(8,128)(2,1)S(1)} %get-tuple-element.65), channel_id=1, source_target_pairs={{8,24},{9,25},{10,26},{11,27},{12,28},{13,29},{14,30},{15,31}} | collective-permute-start | bytes 811016 | tf_op jit(solution)/shard_map/ppermute | solution.py:436
  21.9 18.9 %collective-permute-start.2 = (bf16[512,1024]{1,0:T(8,128)(2,1)S(1)}, bf16[512,1024]{1,0:T(8,128)(2,1)S(1)}, u32[]{:S(2)}, u32[]{:S(2)}) collective-permute-start(bf16[512,1024]{1,0:T(8,128)(2,1)S(1)} %get-tuple-element.53.own_first), channel_id=1, source_target_pairs={{0,1},{1,0},{2,3},{3,2},{4,5},{5,4},{6,7},{7,6},{8,9},{9,8},{10,11... | collective-permute-start | bytes 3145736 | tf_op jit(solution)/shard_map/ppermute | solution.py:35
  35.2 8.1 %collective-permute-start.11 = (bf16[512,1024]{1,0:T(8,128)(2,1)S(1)}, bf16[512,1024]{1,0:T(8,128)(2,1)S(1)}, u32[]{:S(2)}, u32[]{:S(2)}) collective-permute-start(bf16[512,1024]{1,0:T(8,128)(2,1)S(1)} %collective-permute-done.10.high_first), channel_id=1, source_target_pairs={{0,1},{2,3},{5,4},{7,6},{8,9},{10,11},{13,12},{15,14},{16,17},{18,... | collective-permute-start | bytes 3145736 | tf_op jit(solution)/shard_map/ppermute | solution.py:470
  37.7 3.6 %collective-permute-start.9 = (bf16[512,512]{1,0:T(8,128)(2,1)S(1)}, bf16[512,512]{1,0:T(8,128)(2,1)S(1)}, u32[]{:S(2)}, u32[]{:S(2)}) collective-permute-start(bf16[512,512]{1,0:T(8,128)(2,1)S(1)} %collective-permute-done.7.near_first), channel_id=1, source_target_pairs={{0,1},{1,0},{2,3},{3,2},{4,5},{5,4},{6,7},{7,6},{8,9},{9,8},{10,11... | collective-permute-start | bytes 1572872 | tf_op jit(solution)/shard_map/ppermute | solution.py:35
  37.8 9.2 %collective-permute-start.17 = (bf16[256,512]{1,0:T(8,128)(2,1)S(1)}, bf16[256,512]{1,0:T(8,128)(2,1)S(1)}, u32[]{:S(2)}, u32[]{:S(2)}) collective-permute-start(bf16[256,512]{1,0:T(8,128)(2,1)S(1)} %get-tuple-element.72.refs_3_), channel_id=1, source_target_pairs={{0,2},{2,0},{4,6},{6,4},{1,3},{3,1},{5,7},{7,5},{8,10},{10,8},{12,... | collective-permute-start | bytes 786440 | tf_op jit(solution)/shard_map/ppermute | solution.py:35
  39.4 9.5 %collective-permute-start.15 = (bf16[256,512]{1,0:T(8,128)(2,1)S(1)}, bf16[256,512]{1,0:T(8,128)(2,1)S(1)}, u32[]{:S(2)}, u32[]{:S(2)}) collective-permute-start(bf16[256,512]{1,0:T(8,128)(2,1)S(1)} %get-tuple-element.76.refs_2_), channel_id=1, source_target_pairs={{0,4},{2,6},{4,0},{6,2},{1,5},{3,7},{5,1},{7,3},{8,12},{10,14},{12... | collective-permute-start | bytes 786440 | tf_op jit(solution)/shard_map/ppermute | solution.py:35
  40.8 11.8 %collective-permute-start.13 = (bf16[256,512]{1,0:T(8,128)(2,1)S(1)}, bf16[256,512]{1,0:T(8,128)(2,1)S(1)}, u32[]{:S(2)}, u32[]{:S(2)}) collective-permute-start(bf16[256,512]{1,0:T(8,128)(2,1)S(1)} %get-tuple-element.75.refs_1_), channel_id=1, source_target_pairs={{0,2},{2,0},{4,6},{6,4},{1,3},{3,1},{5,7},{7,5},{8,10},{10,8},{12,... | collective-permute-start | bytes 786440 | tf_op jit(solution)/shard_map/ppermute | solution.py:35
  41.4 13.1 %collective-permute-start.8 = (bf16[256,512]{1,0:T(8,128)(2,1)S(1)}, bf16[256,512]{1,0:T(8,128)(2,1)S(1)}, u32[]{:S(2)}, u32[]{:S(2)}) collective-permute-start(bf16[256,512]{1,0:T(8,128)(2,1)S(1)} %get-tuple-element.74.refs_0_), channel_id=1, source_target_pairs={{0,4},{2,6},{4,0},{6,2},{1,5},{3,7},{5,1},{7,3},{8,12},{10,14},{12... | collective-permute-start | bytes 786440 | tf_op jit(solution)/shard_map/ppermute | solution.py:35
  47.3 12.5 %collective-permute-start.18 = (bf16[256,512]{1,0:T(8,128)(2,1)S(1)}, bf16[256,512]{1,0:T(8,128)(2,1)S(1)}, u32[]{:S(2)}, u32[]{:S(2)}) collective-permute-start(bf16[256,512]{1,0:T(8,128)(2,1)S(1)} %give.7), channel_id=1, source_target_pairs={{0,4},{2,6},{4,0},{6,2},{1,5},{3,7},{5,1},{7,3},{8,12},{10,14},{12... | collective-permute-start | bytes 786440 | tf_op jit(solution)/shard_map/ppermute | solution.py:35
  49.2 10.6 %collective-permute-start.16 = (bf16[256,512]{1,0:T(8,128)(2,1)S(1)}, bf16[256,512]{1,0:T(8,128)(2,1)S(1)}, u32[]{:S(2)}, u32[]{:S(2)}) collective-permute-start(bf16[256,512]{1,0:T(8,128)(2,1)S(1)} %give.6), channel_id=1, source_target_pairs={{0,2},{2,0},{4,6},{6,4},{1,3},{3,1},{5,7},{7,5},{8,10},{10,8},{12,... | collective-permute-start | bytes 786440 | tf_op jit(solution)/shard_map/ppermute | solution.py:35
  52.9 11.7 %collective-permute-start.14 = (bf16[256,512]{1,0:T(8,128)(2,1)S(1)}, bf16[256,512]{1,0:T(8,128)(2,1)S(1)}, u32[]{:S(2)}, u32[]{:S(2)}) collective-permute-start(bf16[256,512]{1,0:T(8,128)(2,1)S(1)} %give.5), channel_id=1, source_target_pairs={{0,4},{2,6},{4,0},{6,2},{1,5},{3,7},{5,1},{7,3},{8,12},{10,14},{12... | collective-permute-start | bytes 786440 | tf_op jit(solution)/shard_map/ppermute | solution.py:35
  54.8 9.8 %collective-permute-start.12 = (bf16[256,512]{1,0:T(8,128)(2,1)S(1)}, bf16[256,512]{1,0:T(8,128)(2,1)S(1)}, u32[]{:S(2)}, u32[]{:S(2)}) collective-permute-start(bf16[256,512]{1,0:T(8,128)(2,1)S(1)} %give.4), channel_id=1, source_target_pairs={{0,2},{2,0},{4,6},{6,4},{1,3},{3,1},{5,7},{7,5},{8,10},{10,8},{12,... | collective-permute-start | bytes 786440 | tf_op jit(solution)/shard_map/ppermute | solution.py:35

commit v5 on v4

v5 whole, which is shorter than its diff:
```python
import functools
import math

import jax
import jax.numpy as jnp
from jax import lax
from jax.experimental import pallas as pl
from jax.experimental.pallas import tpu as pltpu
from jax.sharding import PartitionSpec as P

DH = 256
BLOCK = 512
TILE = 256
FINE = 32
EXTRA = 16
VMEM_LIMIT = 14 * 1024 * 1024
F32 = jnp.float32
BF16 = jnp.bfloat16


def mm(left, right):
    return jnp.dot(left, right, preferred_element_type=F32)


def mm_nt(left, right):
    return lax.dot_general(left, right, (((1,), (1,)), ((), ())), preferred_element_type=F32)


def mm_tn(left, right):
    return lax.dot_general(left, right, (((0,), (0,)), ((), ())), preferred_element_type=F32)


def swap(value, axis, mask):
    size = lax.axis_size(axis)
    return lax.ppermute(value, axis, [(place, place ^ mask) for place in range(size)])


def kernel_call(kernel, outs, operands, name):
    arrays = [pltpu.with_memory_space_constraint(array, pltpu.VMEM) for array in operands]
    return pl.pallas_call(
        kernel,
        in_specs=[pl.BlockSpec(memory_space=pltpu.VMEM)] * len(operands),
        out_specs=[pl.BlockSpec(memory_space=pltpu.VMEM)] * len(outs),
        out_shape=[pltpu.VMEM(shape, dtype) for shape, dtype in outs],
        compiler_params=pltpu.CompilerParams(vmem_limit_bytes=VMEM_LIMIT),
        cost_estimate=pl.CostEstimate(
            flops=1, bytes_accessed=1, transcendentals=0
        ),
        name=name,
    )(*arrays)


def loading_call(kernel, outs, loaded, operands, scratch, loads, name):
    arrays = [pltpu.with_memory_space_constraint(array, pltpu.HBM) for array in loaded]
    arrays += [pltpu.with_memory_space_constraint(array, pltpu.VMEM) for array in operands]
    return pl.pallas_call(
        kernel,
        in_specs=[pl.BlockSpec(memory_space=pltpu.HBM)] * len(loaded)
        + [pl.BlockSpec(memory_space=pltpu.VMEM)] * len(operands),
        out_specs=[pl.BlockSpec(memory_space=pltpu.VMEM)] * len(outs),
        out_shape=[pltpu.VMEM(shape, dtype) for shape, dtype in outs],
        scratch_shapes=[*scratch, pltpu.SemaphoreType.DMA((loads,))],
        compiler_params=pltpu.CompilerParams(vmem_limit_bytes=VMEM_LIMIT),
        cost_estimate=pl.CostEstimate(flops=1, bytes_accessed=1, transcendentals=0),
        name=name,
    )(*arrays)


def turned(values, cosine, sine):
    half = DH // 2
    parts = []
    for start in range(0, values.shape[1], DH):
        low = values[:, start : start + half]
        high = values[:, start + half : start + DH]
        parts.append((low * cosine - high * sine).astype(BF16))
        parts.append((high * cosine + low * sine).astype(BF16))
    return jnp.concatenate(parts, axis=1)


def angles(coarse, fine, first, count):
    at = first // FINE
    far = coarse[:, pl.ds(at, count // FINE), :]
    near = fine[...]
    cos_c, sin_c = far[0][:, None, :], far[1][:, None, :]
    cos_f, sin_f = near[0][None], near[1][None]
    cosine = cos_c * cos_f - sin_c * sin_f
    sine = sin_c * cos_f + cos_c * sin_f
    return cosine.reshape(count, DH // 2), sine.reshape(count, DH // 2)


def decay_sums(log_decay, decay):
    heads, rows = log_decay.shape
    place_s = lax.broadcasted_iota(jnp.int32, (BLOCK, BLOCK), 0)
    place_t = lax.broadcasted_iota(jnp.int32, (BLOCK, BLOCK), 1)
    upper = jnp.where(place_s <= place_t, 1.0, 0.0).astype(BF16)
    value = jnp.concatenate([log_decay[...], jnp.zeros((8 - heads, rows), F32)], axis=0)
    parts = []
    for _ in range(3):
        parts.append(value.astype(BF16))
        value = value - parts[-1].astype(F32)
    stacked = jnp.concatenate([part.astype(F32) for part in parts], axis=0).astype(BF16)
    for start in range(0, rows, BLOCK):
        sums = mm(stacked[:, start : start + BLOCK], upper)
        decay[:, start : start + BLOCK] = sums[:8] + sums[8:16] + sums[16:]


def angle_tables(coarse, fine):
    half = DH // 2

    def fill(table, start, stride):
        count = table.shape[1]
        place = lax.broadcasted_iota(jnp.int32, (count, half), 0) * stride + start
        index = lax.broadcasted_iota(jnp.int32, (count, half), 1).astype(F32)
        angle = place.astype(F32) * jnp.exp(index * (-math.log(10000.0) / half))
        table[0] = jnp.cos(angle)
        table[1] = jnp.sin(angle)

    fill(coarse, lax.axis_index("ctx") * coarse.shape[1] * FINE, FINE)
    fill(fine, 0, 1)


class Loads:
    def __init__(self, arrived):
        self.arrived, self.count = arrived, 0

    def start(self, source, target):
        copy = pltpu.make_async_copy(source, target, self.arrived.at[self.count])
        self.count += 1
        copy.start()
        return copy


def half_tiles(x_far, x, half, loads):
    rows, part = x.shape
    columns = pl.ds(pl.multiple_of(half * part, part), part)
    return [
        functools.partial(loads.start, x_far.at[pl.ds(at, TILE), columns], x.at[pl.ds(at, TILE)])
        for at in range(0, rows, TILE)
    ]


def key_value_own_kernel(
    x_far, wk_far, wv_far, log_decay_far, wo_far, wq_far, wg_far,
    x, acc_k, acc_v, decay, coarse, fine, wo, wq, wg, wk, wv, log_decay, arrived,
):
    loads = Loads(arrived)
    tiles = half_tiles(x_far, x, lax.axis_index("fsdp"), loads)
    logs = loads.start(log_decay_far, log_decay)
    key, first = loads.start(wk_far, wk), tiles[0]()
    value = loads.start(wv_far, wv)
    rest = [tile() for tile in tiles[1:]]
    others = [loads.start(wo_far, wo), loads.start(wq_far, wq), loads.start(wg_far, wg)]
    angle_tables(coarse, fine)
    logs.wait()
    decay_sums(log_decay, decay)
    key.wait()
    for number, copy in enumerate([first, *rest]):
        at = slice(number * TILE, (number + 1) * TILE)
        copy.wait()
        acc_k[at, :] = mm(x[at, :], wk[...])
        if number == 0:
            value.wait()
        acc_v[at, :] = mm(x[at, :], wv[...])
    for copy in others:
        copy.wait()


def pack_message(message, state, log):
    place = lax.broadcasted_iota(jnp.int32, (EXTRA, DH), 0)
    tail = jnp.zeros((EXTRA, DH), F32)
    message[:DH, :] = state.astype(BF16)
    for number in range(3):
        piece = log.astype(BF16).astype(F32)
        tail = jnp.where(place == number, piece, tail)
        log = log - piece
    message[DH:, :] = tail.astype(BF16)


def message_log(message):
    tail = message[DH:, :].astype(F32)
    return (tail[:1] + tail[1:2] + tail[2:3])[:, :1]


def key_value_kernel(
    heads, x_far, wk, wv, acc_k, acc_v, decay, coarse, fine, x, k_out, v_out, before_out, *refs
):
    states, messages, arrived = refs[:heads], refs[heads : 2 * heads], refs[-1]
    loads = Loads(arrived)
    tiles = [tile() for tile in half_tiles(x_far, x, 1 - lax.axis_index("fsdp"), loads)]
    totals, blocks = 0.0, x.shape[0] // BLOCK
    for block in range(blocks):
        start = block * BLOCK
        columns = decay[:, start : start + BLOCK].T
        ending = columns[BLOCK - 1 : BLOCK, :]
        totals = totals + ending
        faded = jnp.exp(ending - columns)
        updates = [None] * heads
        for piece in range(BLOCK // TILE):
            first = start + piece * TILE
            at = slice(first, first + TILE)
            tiles[first // TILE].wait()
            cosine, sine = angles(coarse, fine, first, TILE)
            keys = turned(acc_k[at, :] + mm(x[at, :], wk[...]), cosine, sine)
            values = (acc_v[at, :] + mm(x[at, :], wv[...])).astype(BF16)
            k_out[at, :] = keys
            v_out[at, :] = values
            for head in range(heads):
                span = slice(head * DH, (head + 1) * DH)
                fade = faded[piece * TILE : (piece + 1) * TILE, head : head + 1]
                weighted = (keys[:, span].astype(F32) * fade).astype(BF16)
                update = mm_tn(weighted, values[:, span])
                updates[head] = update if piece == 0 else updates[head] + update
        for head in range(heads):
            span = slice(head * DH, (head + 1) * DH)
            old = states[head][...] if block else jnp.zeros((DH, DH), F32)
            before_out[block, span, :] = old.astype(BF16)
            new = jnp.exp(ending[:, head : head + 1]) * old + updates[head]
            states[head][...] = new
            if block == blocks - 1:
                pack_message(messages[head], new, totals[:, head : head + 1])


def combine_kernel(hop, first, window, sent, *refs):
    if first:
        got, new_window, new_entering, message = refs
    else:
        entering, got, new_window, new_entering, message = refs
    upper = (lax.axis_index("ctx") // hop) % 2 == 1
    arrived = got[:DH, :].astype(F32)
    window_log, arrived_log = message_log(sent), message_log(got)
    if first:
        new_entering[:DH, :] = jnp.where(upper, arrived, 0.0)
        entering_log = jnp.zeros((1, 1), F32)
    else:
        entering_log = entering[DH : DH + 1, :1]
        new_entering[:DH, :] = entering[:DH, :] + jnp.where(upper, jnp.exp(entering_log), 0.0) * arrived
    entering_log = entering_log + jnp.where(upper, arrived_log, 0.0)
    new_entering[DH:, :] = jnp.broadcast_to(entering_log, (8, DH))
    own_fade = jnp.where(upper, 1.0, jnp.exp(arrived_log))
    arrived_fade = jnp.where(upper, jnp.exp(window_log), 1.0)
    joined = own_fade * window[...] + arrived_fade * arrived
    new_window[...] = joined
    pack_message(message, joined, window_log + arrived_log)


def query_gate_kernel(
    heads, block, x_own, x_other, wq, wq_far, wg, wg_far, decay, coarse, fine, k, v, q_out, g_out, intra_out
):
    start = block * BLOCK
    lines = decay[:, start : start + BLOCK]
    columns = lines.T

    def project(piece, carry):
        first = pl.multiple_of(start + piece * TILE, TILE)
        at = pl.ds(pl.multiple_of(piece * TILE, TILE), TILE)
        own, far = x_own[pl.ds(first, TILE), :], x_other[pl.ds(first, TILE), :]
        cosine, sine = angles(coarse, fine, first, TILE)
        q_out[at, :] = turned(mm(own, wq[...]) + mm(far, wq_far[...]), cosine, sine)
        g_out[at, :] = (mm(own, wg[...]) + mm(far, wg_far[...])).astype(BF16)
        return carry

    lax.fori_loop(0, BLOCK // TILE, project, 0)
    for piece in range(BLOCK // TILE):
        low, last = piece * TILE, (piece + 1) * TILE
        place_t = lax.broadcasted_iota(jnp.int32, (TILE, last), 0) + low
        place_s = lax.broadcasted_iota(jnp.int32, (TILE, last), 1)
        causal = place_t >= place_s
        for head in range(heads):
            span = slice(head * DH, (head + 1) * DH)
            scores = mm_nt(q_out[low:last, span], k[start : start + last, span])
            differ = columns[low:last, head : head + 1] - lines[head : head + 1, :last]
            weights = jnp.where(causal, jnp.exp(jnp.where(causal, differ, 0.0)), 0.0)
            intra_out[low:last, span] = mm((scores * weights).astype(BF16), v[start : start + last, span])


def hidden_kernel(heads, hop, starts, decay, before, *refs):
    refs, token = refs[:-1], refs[-1]
    token[...] = jnp.zeros_like(token)
    entering, arrivals, projected, outs = (
        refs[:heads], refs[heads : 2 * heads], refs[2 * heads : -len(starts)], refs[-len(starts) :]
    )
    upper = (lax.axis_index("ctx") // hop) % 2 == 1
    for head in range(heads):
        span = slice(head * DH, (head + 1) * DH)
        fade = jnp.where(upper, jnp.exp(entering[head][DH : DH + 1, :1]), 0.0)
        state = entering[head][:DH, :] + fade * arrivals[head][:DH, :].astype(F32)
        for start, out in zip(starts, outs):
            block = start // BLOCK
            q, gate, intra = projected[3 * block : 3 * block + 3]
            at = slice(start % BLOCK, start % BLOCK + TILE)
            column = jnp.exp(decay[:, start : start + TILE].T[:, head : head + 1])
            scale_log = jnp.zeros((1, 1), F32)
            for earlier in range(block):
                end = (earlier + 1) * BLOCK
                scale_log = scale_log + decay[head : head + 1, end - 1 : end]
            prior = (jnp.exp(scale_log) * state + before[block, span, :].astype(F32)).astype(BF16)
            retained = intra[at, span] + column * mm(q[at, span], prior)
            center = retained - jnp.mean(retained, axis=1, keepdims=True)
            spread = jnp.mean(center * center, axis=1, keepdims=True)
            value = gate[at, span].astype(F32)
            silu = value / (1.0 + jnp.exp(-value))
            out[:, span] = (silu * center * lax.rsqrt(spread + 1e-5)).astype(BF16)


def arrange_kernel(near_first, near_second, high_first, high_second, low_out, high_out):
    cols = near_first.shape[1]
    place, core = lax.axis_index("tp"), lax.axis_index("fsdp")
    high, low = place // 2, place % 2
    here = core == high
    same = core == low
    low_out[:, :cols] = jnp.where(here, near_second[...], near_first[...])
    low_out[:, cols:] = jnp.where(here, near_first[...], near_second[...])
    high_out[:, :cols] = jnp.where(same, high_second[...], high_first[...])
    high_out[:, cols:] = jnp.where(same, high_first[...], high_second[...])


def columns_kernel(own_first, own_second, near, high_out):
    cols = near.shape[1]
    place, core = lax.axis_index("tp"), lax.axis_index("fsdp")
    high, low = place // 2, place % 2
    near[...] = own_first[:, pl.ds(pl.multiple_of((1 - low) * cols, cols), cols)]
    at = pl.ds(pl.multiple_of(core * cols, cols), cols)
    high_out[...] = jnp.where(core == high, own_second[:, at], own_first[:, at])


def own_kernel(order, own_first, own_second, *refs):
    pieces, outs = refs[: len(order)], refs[len(order) :]
    cols = pieces[0].shape[1]
    place, core = lax.axis_index("tp"), lax.axis_index("fsdp")
    high, low = place // 2, place % 2
    here = core == high
    mine = pl.ds(pl.multiple_of(low * cols, cols), cols)
    flipped = pl.ds(pl.multiple_of((1 - low) * cols, cols), cols)
    keep = jnp.where(here, own_first[:, mine], own_second[:, mine])
    gives = [
        jnp.where(here, own_second[:, mine], own_first[:, mine]),
        jnp.where(here, own_first[:, flipped], own_second[:, flipped]),
    ]
    for (half, number), piece in zip(order, pieces):
        at = slice(number * TILE, (number + 1) * TILE)
        outs[half][at, :cols] = mm(piece[...], gives[half])
        outs[half][at, cols:] = mm(piece[...], keep)


def give_kernel(number, own, far, weight, out):
    cols = out.shape[1]
    at = slice(number * TILE, (number + 1) * TILE)
    out[...] = (own[at, :cols] + mm(far[...], weight[:, :cols])).astype(BF16)


def keep_kernel(order, *refs):
    count = len(order)
    fars, owns, weights, outs = refs[:count], refs[count : count + 2], refs[count + 2 : count + 4], refs[count + 4 :]
    for (half, number), far in zip(order, fars):
        cols = far.shape[1]
        at = slice(number * TILE, (number + 1) * TILE)
        outs[half][at, :] = owns[half][at, cols:] + mm(far[...], weights[half][:, cols:])


def finish_kernel(order, *refs):
    gots, keeps, out = refs[: len(order)], refs[len(order) : -1], refs[-1]
    for (half, number), got in zip(order, gots):
        keep = keeps[half]
        at = slice(number * TILE, (number + 1) * TILE)
        value = keep[at, :] + got[...].astype(F32)
        start = half * keep.shape[0] + number * TILE
        out[0, start : start + TILE, :] = value.astype(BF16)


def after(value, *others):
    return lax.optimization_barrier((value, *others))[0]


def on_device(tokens, query_weight, key_weight, value_weight, gate_weight, out_weight, log_decay):
    x = tokens[0]
    rows, width = x.shape
    part, cols = query_weight.shape
    heads = cols // DH
    blocks = rows // BLOCK
    ctx, tp, cores = lax.axis_size("ctx"), lax.axis_size("tp"), lax.axis_size("fsdp")
    assert tp == 4 and cores == 2 and ctx >= 4 and ctx & (ctx - 1) == 0
    near_mask, far_mask = 1, 2
    tables = [((2, rows // FINE, DH // 2), F32), ((2, FINE, DH // 2), F32)]

    key_far = swap(key_weight, "fsdp", 1)
    value_far = swap(value_weight, "fsdp", 1)

    x_own, acc_k, acc_v, decay, coarse, fine, out_first, own_q, own_g = loading_call(
        key_value_own_kernel,
        [((rows, part), BF16), ((rows, cols), F32), ((rows, cols), F32), ((8, rows), F32)]
        + tables
        + [(out_weight.shape, BF16), ((part, cols), BF16), ((part, cols), BF16)],
        [x, key_weight, value_weight, log_decay[0].T, out_weight, query_weight, gate_weight],
        [],
        [pltpu.VMEM((part, cols), BF16)] * 2 + [pltpu.VMEM((heads, rows), F32)],
        rows // TILE + 6,
        "key_value_own",
    )
    message_shape, state_shape = (DH + EXTRA, DH), (DH, DH)
    x_other, keys, values, before, *states = loading_call(
        functools.partial(key_value_kernel, heads),
        [
            ((rows, part), BF16),
            ((rows, cols), BF16),
            ((rows, cols), BF16),
            ((blocks, heads * DH, DH), BF16),
        ]
        + [(state_shape, F32)] * heads
        + [(message_shape, BF16)] * heads,
        [x],
        [key_far, value_far, acc_k, acc_v, decay, coarse, fine],
        [],
        rows // TILE,
        "key_value",
    )
    windows, messages = states[:heads], states[heads:]
    last_message = messages[-1]

    entering = [None] * heads
    hop = 1
    while True:
        arrivals = [swap(message, "ctx", hop) for message in messages]
        if 2 * hop >= ctx:
            break
        for head in range(heads):
            old = [] if entering[head] is None else [entering[head]]
            windows[head], entering[head], messages[head] = kernel_call(
                functools.partial(combine_kernel, hop, not old),
                [(state_shape, F32), ((DH + 8, DH), F32), (message_shape, BF16)],
                [windows[head], messages[head], *old, arrivals[head]],
                "combine",
            )
        hop *= 2

    far_q, far_g = swap(own_q, "fsdp", 1), swap(own_g, "fsdp", 1)
    own_second = swap(out_first, "fsdp", 1)
    for_near, for_high = kernel_call(
        columns_kernel,
        [((cols, cols), BF16)] * 2,
        [after(out_first, last_message), own_second],
        "columns",
    )
    near_first = swap(for_near, "tp", near_mask)
    high_first = swap(for_high, "tp", far_mask)

    held, projected = after(decay, *messages), []
    for block in range(blocks):
        projected += kernel_call(
            functools.partial(query_gate_kernel, heads, block),
            [((BLOCK, cols), BF16), ((BLOCK, cols), BF16), ((BLOCK, cols), F32)],
            [x_own, x_other, own_q, far_q, own_g, far_g, held, coarse, fine, keys, values],
            "query_gate",
        )
    count = rows // 2 // TILE
    masks = (near_mask, far_mask)
    hidden, far = [[], []], [[], []]
    for number in range(count):
        held = after(decay, swap(pair[2], "fsdp", 1)) if number else decay
        pair = kernel_call(
            functools.partial(hidden_kernel, heads, hop, [(half * count + number) * TILE for half in range(2)]),
            [((TILE, cols), BF16)] * 2 + [((16, 128), BF16)],
            [held, before, *entering, *arrivals, *projected],
            "hidden",
        )
        if number == 0:
            near_second = swap(after(near_first, pair[0]), "fsdp", 1)
            high_second = swap(after(high_first, pair[0]), "fsdp", 1)
        for half in range(2):
            hidden[half].append(pair[half])
            far[half].append(swap(pair[half], "tp", masks[half]))
    weights = kernel_call(
        arrange_kernel,
        [((cols, 2 * cols), BF16)] * 2,
        [near_first, near_second, high_first, high_second],
        "arrange",
    )
    order = [(half, number) for number in reversed(range(count)) for half in (1, 0)]
    owns = kernel_call(
        functools.partial(own_kernel, order),
        [((count * TILE, 2 * cols), F32)] * 2,
        [out_first, own_second, *(hidden[half][number] for half, number in order)],
        "own_products",
    )
    gots = []
    for half, number in order:
        [give] = kernel_call(
            functools.partial(give_kernel, number),
            [((TILE, cols), BF16)],
            [owns[half], far[half][number], weights[half]],
            "give",
        )
        gots.append(swap(give, "tp", masks[1 - half]))
    keeps = kernel_call(
        functools.partial(keep_kernel, order),
        [((count * TILE, cols), F32)] * 2,
        [*(far[half][number] for half, number in order), *owns, *weights],
        "keep",
    )
    arrays = [pltpu.with_memory_space_constraint(array, pltpu.VMEM) for array in (*gots, *keeps)]
    return pl.pallas_call(
        functools.partial(finish_kernel, order),
        in_specs=[pl.BlockSpec(memory_space=pltpu.VMEM)] * len(arrays),
        out_specs=pl.BlockSpec(memory_space=pltpu.VMEM),
        out_shape=jax.ShapeDtypeStruct((1, rows, cols), BF16),
        compiler_params=pltpu.CompilerParams(vmem_limit_bytes=VMEM_LIMIT),
        name="finish",
    )(*arrays)


def solution(mesh):
    in_specs = (
        P("fsdp", "ctx", None),
        P("fsdp", "tp"),
        P("fsdp", "tp"),
        P("fsdp", "tp"),
        P("fsdp", "tp"),
        P("tp", "fsdp"),
        P("fsdp", "ctx", "tp"),
    )
    out_specs = P("fsdp", "ctx", "tp")
    return jax.shard_map(
        on_device, mesh=mesh, in_specs=in_specs, out_specs=out_specs, check_vma=False
    )
```

time: 66.4 us -> 66.8 us (level)
  the two profiles are of different devices: /device:TPU:24 before, /device:TPU:0 now
where the time goes in v5:
time: 66.8 us; the launch traced here: 66.6 us
  Pallas kernels  25.9 us (39%)
  waiting for transfers between devices  22.1 us (33%)
  starting transfers between devices  18.5 us (28%)
    ppermute x21, waiting for transfers between devices, swap(): lax.ppermute(value, axis, [(place, place ^ mask) for place in range(size)])  22.1 us
    ppermute x21, starting transfers between devices, swap(): lax.ppermute(value, axis, [(place, place ^ mask) for place in range(size)])  18.5 us
    pallas_call x14, Pallas kernels, kernel_call(): pl.pallas_call(kernel, in_specs=[pl.BlockSpec(memory_space=pltpu.VMEM)] *...  15.7 us
    pallas_call x2, Pallas kernels, loading_call(): pl.pallas_call(kernel, in_specs=[pl.BlockSpec(memory_space=pltpu.HBM)] *...  9.05 us
  transfers between devices with their start and end apart: 21, of which 9 were waited for; matrix products, arithmetic and copies ran while one was open for 0% of the time, Pallas kernels for 37%

profile of v5, /device:TPU:0, one launch (start us, length us, event | category | flops | bytes accessed | tf_op | source)
XLA Modules:
  0.0 66.6 jit_solution(2584653213185963705)
XLA Ops:
  0.5 4.5 %key_value_own.1 = (bf16[1024,1024]{1,0:T(8,128)(2,1)S(1)}, f32[1024,512]{1,0:T(8,128)S(1)}, f32[1024,512]{1,0:T(8,128)S(1)}, f32[8,1024]{1,0:T(8,128)S(1)}, f32...) custom-call(bf16[1024,2048]{1,0:T(8,128)(2,1)} %bitcast.4, ...), custom_call_target="tpu_custom_call" | custom-call | flops 1 | bytes 1 | tf_op jit(solution)/shard_map/key_value_own/pallas_call | solution.py:56
  5.0 0.5 collective-permute-start
  6.0 4.6 %key_value.1 = (bf16[1024,1024]{1,0:T(8,128)(2,1)S(1)}, bf16[1024,512]{1,0:T(8,128)(2,1)S(1)}, bf16[1024,512]{1,0:T(8,128)(2,1)S(1)}, bf16[2,512,256]{2,1,0:T(8,...) custom-call(bf16[1024,2048]{1,0:T(8,128)(2,1)} %bitcast.5, ...), custom_call_target="tpu_custom_call" | custom-call | flops 1 | bytes 1 | tf_op jit(solution)/shard_map/key_value/pallas_call | solution.py:56
  10.7 2.7 %collective-permute-start.12 = (bf16[512,512]{1,0:T(8,128)(2,1)S(1)}, bf16[512,512]{1,0:T(8,128)(2,1)S(1)}, u32[]{:S(2)}, u32[]{:S(2)}) collective-permute-start(bf16[512,512]{1,0:T(8,128)(2,1)S(1)} %get-tuple-element.84), channel_id=1, source_target_pairs={{0,4},{2,6},{4,0},{6,2},{1,5},{3,7},{5,1},{7,3},{8,12},{10,14},{12... | collective-permute-start | bytes 1572872 | tf_op jit(solution)/shard_map/ppermute | solution.py:35
  13.4 1.6 %collective-permute-start.4 = (bf16[272,256]{1,0:T(8,128)(2,1)S(1)}, bf16[272,256]{1,0:T(8,128)(2,1)S(1)}, u32[]{:S(2)}, u32[]{:S(2)}) collective-permute-start(bf16[272,256]{1,0:T(8,128)(2,1)S(1)} %get-tuple-element.59.sent), channel_id=1, source_target_pairs={{0,8},{8,0},{16,24},{24,16},{1,9},{9,1},{17,25},{25,17},{2,10},{10... | collective-permute-start | bytes 417800 | tf_op jit(solution)/shard_map/ppermute | solution.py:35
  15.4 4.5 %collective-permute-done.4.refs_0_ = bf16[272,256]{1,0:T(8,128)(2,1)S(1)} collective-permute-done((bf16[272,256]{1,0:T(8,128)(2,1)S(1)}, bf16[272,256]{1,0:T(8,128)(2,1)S(1)}, u32[]{:S(2)}, u32[]{:S(2)}) %collective-permute-start.4) | collective-permute-done | bytes 139296 | tf_op jit(solution)/shard_map/ppermute | solution.py:35
  19.9 1.5 %collective-permute-start.10 = (bf16[512,512]{1,0:T(8,128)(2,1)S(1)}, bf16[512,512]{1,0:T(8,128)(2,1)S(1)}, u32[]{:S(2)}, u32[]{:S(2)}) collective-permute-start(bf16[512,512]{1,0:T(8,128)(2,1)S(1)} %get-tuple-element.82), channel_id=1, source_target_pairs={{0,2},{2,0},{4,6},{6,4},{1,3},{3,1},{5,7},{7,5},{8,10},{10,8},{12,... | collective-permute-start | bytes 1572872 | tf_op jit(solution)/shard_map/ppermute | solution.py:35
  21.4 0.8 %combine.3 = (f32[256,256]{1,0:T(8,128)}, f32[264,256]{1,0:T(8,128)S(1)}, bf16[272,256]{1,0:T(8,128)(2,1)S(1)}) custom-call(f32[256,256]{1,0:T(8,128)S(1)} %get-tuple-element.58.window, bf16[272,256]{1,0:T(8,128)(2,1)S(1)} %get-tuple-element.59.sent, bf16[272,256]{1,0:T(8,128)(2,1)S(1)} %collective-permute-done.4.refs_0_), custom_call_target="tpu_custom_call" | custom-call | flops 1 | bytes 1 | tf_op jit(solution)/shard_map/combine/pallas_call | solution.py:40
  22.2 2.6 %collective-permute-start.6 = (bf16[272,256]{1,0:T(8,128)(2,1)S(1)}, bf16[272,256]{1,0:T(8,128)(2,1)S(1)}, u32[]{:S(2)}, u32[]{:S(2)}) collective-permute-start(bf16[272,256]{1,0:T(8,128)(2,1)S(1)} %get-tuple-element.62), channel_id=1, source_target_pairs={{0,16},{8,24},{16,0},{24,8},{1,17},{9,25},{17,1},{25,9},{2,18},{10... | collective-permute-start | bytes 417800 | tf_op jit(solution)/shard_map/ppermute | solution.py:35
  24.8 0.8 %combine.2 = (f32[256,256]{1,0:T(8,128)}, f32[264,256]{1,0:T(8,128)S(1)}, bf16[272,256]{1,0:T(8,128)(2,1)S(1)}) custom-call(f32[256,256]{1,0:T(8,128)S(1)} %get-tuple-element.55.window, bf16[272,256]{1,0:T(8,128)(2,1)S(1)} %get-tuple-element.56.sent, bf16[272,256]{1,0:T(8,128)(2,1)S(1)} %collective-permute-done.3.refs_0_), custom_call_target="tpu_custom_call" | custom-call | flops 1 | bytes 1 | tf_op jit(solution)/shard_map/combine/pallas_call | solution.py:40
  26.0 3.7 %query_gate.3 = (bf16[512,512]{1,0:T(8,128)(2,1)S(1)}, bf16[512,512]{1,0:T(8,128)(2,1)S(1)}, f32[512,512]{1,0:T(8,128)S(1)}) custom-call(bf16[1024,1024]{1,0:T(8,128)(2,1)S(1)} %get-tuple-element.63.x_own, bf16[1024,1024]{1,0:T(8,128)(2,1)S(1)} %get-tuple-element.64.x_other, bf16[1024,512]{1,0:T(8,128)(2,1)S(1)} %get-tuple-element.65.wq, ...), custom_call_target="tpu_custom_call" | custom-call | flops 1 | bytes 1 | tf_op jit(solution)/shard_map/query_gate/pallas_call | solution.py:40
  29.6 3.5 %query_gate.2 = (bf16[512,512]{1,0:T(8,128)(2,1)S(1)}, bf16[512,512]{1,0:T(8,128)(2,1)S(1)}, f32[512,512]{1,0:T(8,128)S(1)}) custom-call(bf16[1024,1024]{1,0:T(8,128)(2,1)S(1)} %get-tuple-element.63.x_own, bf16[1024,1024]{1,0:T(8,128)(2,1)S(1)} %get-tuple-element.64.x_other, bf16[1024,512]{1,0:T(8,128)(2,1)S(1)} %get-tuple-element.65.wq, ...), custom_call_target="tpu_custom_call" | custom-call | flops 1 | bytes 1 | tf_op jit(solution)/shard_map/query_gate/pallas_call | solution.py:40
  33.1 1.9 %collective-permute-done.6.refs_3_ = bf16[272,256]{1,0:T(8,128)(2,1)S(1)} collective-permute-done((bf16[272,256]{1,0:T(8,128)(2,1)S(1)}, bf16[272,256]{1,0:T(8,128)(2,1)S(1)}, u32[]{:S(2)}, u32[]{:S(2)}) %collective-permute-start.6) | collective-permute-done | bytes 139296 | tf_op jit(solution)/shard_map/ppermute | solution.py:35
  35.1 1.8 %collective-permute-done.5.refs_2_ = bf16[272,256]{1,0:T(8,128)(2,1)S(1)} collective-permute-done((bf16[272,256]{1,0:T(8,128)(2,1)S(1)}, bf16[272,256]{1,0:T(8,128)(2,1)S(1)}, u32[]{:S(2)}, u32[]{:S(2)}) %collective-permute-start.5) | collective-permute-done | bytes 139296 | tf_op jit(solution)/shard_map/ppermute | solution.py:35
  36.9 1.7 %hidden.3 = (bf16[256,512]{1,0:T(8,128)(2,1)S(1)}, bf16[256,512]{1,0:T(8,128)(2,1)S(1)}, bf16[16,128]{1,0:T(8,128)(2,1)}) custom-call(f32[8,1024]{1,0:T(8,128)S(1)} %get-tuple-element.67.decay, bf16[2,512,256]{2,1,0:T(8,128)(2,1)S(1)} %get-tuple-element.54.before, f32[264,256]{1,0:T(8,128)S(1)} %get-tuple-element.57.refs_0_, ...), custom_call_target="tpu_custom_call" | custom-call | flops 1 | bytes 1 | tf_op jit(solution)/shard_map/hidden/pallas_call | solution.py:40
  38.6 0.5 collective-permute-start.11
  39.1 1.5 %collective-permute-start.19 = (bf16[256,512]{1,0:T(8,128)(2,1)S(1)}, bf16[256,512]{1,0:T(8,128)(2,1)S(1)}, u32[]{:S(2)}, u32[]{:S(2)}) collective-permute-start(bf16[256,512]{1,0:T(8,128)(2,1)S(1)} %get-tuple-element.79.refs_3_), channel_id=1, source_target_pairs={{0,2},{2,0},{4,6},{6,4},{1,3},{3,1},{5,7},{7,5},{8,10},{10,8},{12,... | collective-permute-start | bytes 786440 | tf_op jit(solution)/shard_map/ppermute | solution.py:35
  40.6 0.5 collective-permute-start.17
  41.1 1.7 %hidden.2 = (bf16[256,512]{1,0:T(8,128)(2,1)S(1)}, bf16[256,512]{1,0:T(8,128)(2,1)S(1)}, bf16[16,128]{1,0:T(8,128)(2,1)}) custom-call(f32[8,1024]{1,0:T(8,128)S(1)} %get-tuple-element.67.decay, bf16[2,512,256]{2,1,0:T(8,128)(2,1)S(1)} %get-tuple-element.54.before, f32[264,256]{1,0:T(8,128)S(1)} %get-tuple-element.57.refs_0_, ...), custom_call_target="tpu_custom_call" | custom-call | flops 1 | bytes 1 | tf_op jit(solution)/shard_map/hidden/pallas_call | solution.py:40
  42.8 0.7 %collective-permute-start.15 = (bf16[256,512]{1,0:T(8,128)(2,1)S(1)}, bf16[256,512]{1,0:T(8,128)(2,1)S(1)}, u32[]{:S(2)}, u32[]{:S(2)}) collective-permute-start(bf16[256,512]{1,0:T(8,128)(2,1)S(1)} %get-tuple-element.77.refs_1_), channel_id=1, source_target_pairs={{0,2},{2,0},{4,6},{6,4},{1,3},{3,1},{5,7},{7,5},{8,10},{10,8},{12,... | collective-permute-start | bytes 786440 | tf_op jit(solution)/shard_map/ppermute | solution.py:35
  43.5 1.4 %collective-permute-start.9 = (bf16[256,512]{1,0:T(8,128)(2,1)S(1)}, bf16[256,512]{1,0:T(8,128)(2,1)S(1)}, u32[]{:S(2)}, u32[]{:S(2)}) collective-permute-start(bf16[256,512]{1,0:T(8,128)(2,1)S(1)} %get-tuple-element.76.refs_0_), channel_id=1, source_target_pairs={{0,4},{2,6},{4,0},{6,2},{1,5},{3,7},{5,1},{7,3},{8,12},{10,14},{12... | collective-permute-start | bytes 786440 | tf_op jit(solution)/shard_map/ppermute | solution.py:35
  44.9 1.3 %own_products.1 = (f32[512,1024]{1,0:T(8,128)S(1)}, f32[512,1024]{1,0:T(8,128)S(1)}) custom-call(bf16[512,1024]{1,0:T(8,128)(2,1)S(1)} %get-tuple-element.81.own_first, bf16[512,1024]{1,0:T(8,128)(2,1)S(1)} %collective-permute-done.own_second, bf16[256,512]{1,0:T(8,128)(2,1)S(1)} %get-tuple-element.76.refs_0_, ...), custom_call_target="tpu_custom_call" | custom-call | flops 1 | bytes 1 | tf_op jit(solution)/shard_map/own_products/pallas_call | solution.py:40
  46.4 1.9 %collective-permute-done.19.far.refs_3_ = bf16[256,512]{1,0:T(8,128)(2,1)S(1)} collective-permute-done((bf16[256,512]{1,0:T(8,128)(2,1)S(1)}, bf16[256,512]{1,0:T(8,128)(2,1)S(1)}, u32[]{:S(2)}, u32[]{:S(2)}) %collective-permute-start.19) | collective-permute-done | bytes 262176 | tf_op jit(solution)/shard_map/ppermute | solution.py:35
  48.6 0.7 %collective-permute-start.20 = (bf16[256,512]{1,0:T(8,128)(2,1)S(1)}, bf16[256,512]{1,0:T(8,128)(2,1)S(1)}, u32[]{:S(2)}, u32[]{:S(2)}) collective-permute-start(bf16[256,512]{1,0:T(8,128)(2,1)S(1)} %give.7), channel_id=1, source_target_pairs={{0,4},{2,6},{4,0},{6,2},{1,5},{3,7},{5,1},{7,3},{8,12},{10,14},{12... | collective-permute-start | bytes 786440 | tf_op jit(solution)/shard_map/ppermute | solution.py:35
  50.1 0.9 %collective-permute-start.18 = (bf16[256,512]{1,0:T(8,128)(2,1)S(1)}, bf16[256,512]{1,0:T(8,128)(2,1)S(1)}, u32[]{:S(2)}, u32[]{:S(2)}) collective-permute-start(bf16[256,512]{1,0:T(8,128)(2,1)S(1)} %give.6), channel_id=1, source_target_pairs={{0,2},{2,0},{4,6},{6,4},{1,3},{3,1},{5,7},{7,5},{8,10},{10,8},{12,... | collective-permute-start | bytes 786440 | tf_op jit(solution)/shard_map/ppermute | solution.py:35
  51.0 2.9 %collective-permute-done.15.far.refs_1_ = bf16[256,512]{1,0:T(8,128)(2,1)S(1)} collective-permute-done((bf16[256,512]{1,0:T(8,128)(2,1)S(1)}, bf16[256,512]{1,0:T(8,128)(2,1)S(1)}, u32[]{:S(2)}, u32[]{:S(2)}) %collective-permute-start.15) | collective-permute-done | bytes 262176 | tf_op jit(solution)/shard_map/ppermute | solution.py:35
  54.2 0.7 %collective-permute-start.16 = (bf16[256,512]{1,0:T(8,128)(2,1)S(1)}, bf16[256,512]{1,0:T(8,128)(2,1)S(1)}, u32[]{:S(2)}, u32[]{:S(2)}) collective-permute-start(bf16[256,512]{1,0:T(8,128)(2,1)S(1)} %give.5), channel_id=1, source_target_pairs={{0,4},{2,6},{4,0},{6,2},{1,5},{3,7},{5,1},{7,3},{8,12},{10,14},{12... | collective-permute-start | bytes 786440 | tf_op jit(solution)/shard_map/ppermute | solution.py:35
  55.7 0.9 %collective-permute-start.14 = (bf16[256,512]{1,0:T(8,128)(2,1)S(1)}, bf16[256,512]{1,0:T(8,128)(2,1)S(1)}, u32[]{:S(2)}, u32[]{:S(2)}) collective-permute-start(bf16[256,512]{1,0:T(8,128)(2,1)S(1)} %give.4), channel_id=1, source_target_pairs={{0,2},{2,0},{4,6},{6,4},{1,3},{3,1},{5,7},{7,5},{8,10},{10,8},{12,... | collective-permute-start | bytes 786440 | tf_op jit(solution)/shard_map/ppermute | solution.py:35
  56.6 0.7 %keep.1 = (f32[512,512]{1,0:T(8,128)S(1)}, f32[512,512]{1,0:T(8,128)S(1)}) custom-call(bf16[256,512]{1,0:T(8,128)(2,1)S(1)} %collective-permute-done.9.far.refs_0_, bf16[256,512]{1,0:T(8,128)(2,1)S(1)} %collective-permute-done.15.far.refs_1_, bf16[256,512]{1,0:T(8,128)(2,1)S(1)} %collective-permute-done.17.far.refs_2_, ...), custom_call_target="tpu_custom_call" | custom-call | flops 1 | bytes 1 | tf_op jit(solution)/shard_map/keep/pallas_call | solution.py:40
  57.3 3.7 %collective-permute-done.20.refs_3_ = bf16[256,512]{1,0:T(8,128)(2,1)S(1)} collective-permute-done((bf16[256,512]{1,0:T(8,128)(2,1)S(1)}, bf16[256,512]{1,0:T(8,128)(2,1)S(1)}, u32[]{:S(2)}, u32[]{:S(2)}) %collective-permute-start.20) | collective-permute-done | bytes 262176 | tf_op jit(solution)/shard_map/ppermute | solution.py:35
  61.0 4.4 %collective-permute-done.16.refs_1_ = bf16[256,512]{1,0:T(8,128)(2,1)S(1)} collective-permute-done((bf16[256,512]{1,0:T(8,128)(2,1)S(1)}, bf16[256,512]{1,0:T(8,128)(2,1)S(1)}, u32[]{:S(2)}, u32[]{:S(2)}) %collective-permute-start.16) | collective-permute-done | bytes 262176 | tf_op jit(solution)/shard_map/ppermute | solution.py:35
  65.4 1.1 %finish.1 = bf16[1,1024,512]{2,1,0:T(8,128)(2,1)} custom-call(bf16[256,512]{1,0:T(8,128)(2,1)S(1)} %collective-permute-done.14.refs_0_, bf16[256,512]{1,0:T(8,128)(2,1)S(1)} %collective-permute-done.16.refs_1_, bf16[256,512]{1,0:T(8,128)(2,1)S(1)} %collective-permute-done.18.refs_2_, bf16[256,512]{1,0:T(8,128)(2,1)S(1)} %collective-permute-done.20.refs_3_, ...), custom_call_target="tpu_custom_call" | custom-call | tf_op jit(solution)/shard_map/finish/pallas_call | solution.py:500
  (27 shorter events, 4.3 us)
Async XLA Ops:
  0.0 6.0 %collective-permute-start.1 = (bf16[1024,512]{1,0:T(8,128)(2,1)}, bf16[1024,512]{1,0:T(8,128)(2,1)S(1)}, u32[]{:S(2)}, u32[]{:S(2)}) collective-permute-start(bf16[1024,512]{1,0:T(8,128)(2,1)} %wk_far.1), channel_id=1, source_target_pairs={{0,1},{1,0},{2,3},{3,2},{4,5},{5,4},{6,7},{7,6},{8,9},{9,8},{10,11... | collective-permute-start | bytes 3145736 | tf_op jit(solution)/shard_map/ppermute | solution.py:35
  0.5 5.6 %collective-permute-start.2 = (bf16[1024,512]{1,0:T(8,128)(2,1)}, bf16[1024,512]{1,0:T(8,128)(2,1)S(1)}, u32[]{:S(2)}, u32[]{:S(2)}) collective-permute-start(bf16[1024,512]{1,0:T(8,128)(2,1)} %wv_far.1), channel_id=1, source_target_pairs={{0,1},{1,0},{2,3},{3,2},{4,5},{5,4},{6,7},{7,6},{8,9},{9,8},{10,11... | collective-permute-start | bytes 3145736 | tf_op jit(solution)/shard_map/ppermute | solution.py:35
  5.0 5.6 %collective-permute-start = (bf16[512,1024]{1,0:T(8,128)(2,1)S(1)}, bf16[512,1024]{1,0:T(8,128)(2,1)S(1)}, u32[]{:S(2)}, u32[]{:S(2)}) collective-permute-start(bf16[512,1024]{1,0:T(8,128)(2,1)S(1)} %get-tuple-element.81.own_first), channel_id=1, source_target_pairs={{0,1},{1,0},{2,3},{3,2},{4,5},{5,4},{6,7},{7,6},{8,9},{9,8},{10,11... | collective-permute-start | bytes 3145736 | tf_op jit(solution)/shard_map/ppermute | solution.py:35
  5.5 20.1 %collective-permute-start.7 = (bf16[1024,512]{1,0:T(8,128)(2,1)S(1)}, bf16[1024,512]{1,0:T(8,128)(2,1)S(1)}, u32[]{:S(2)}, u32[]{:S(2)}) collective-permute-start(bf16[1024,512]{1,0:T(8,128)(2,1)S(1)} %get-tuple-element.65.wq), channel_id=1, source_target_pairs={{0,1},{1,0},{2,3},{3,2},{4,5},{5,4},{6,7},{7,6},{8,9},{9,8},{10,11... | collective-permute-start | bytes 3145736 | tf_op jit(solution)/shard_map/ppermute | solution.py:35
  5.6 20.3 %collective-permute-start.8 = (bf16[1024,512]{1,0:T(8,128)(2,1)S(1)}, bf16[1024,512]{1,0:T(8,128)(2,1)S(1)}, u32[]{:S(2)}, u32[]{:S(2)}) collective-permute-start(bf16[1024,512]{1,0:T(8,128)(2,1)S(1)} %get-tuple-element.66.wg), channel_id=1, source_target_pairs={{0,1},{1,0},{2,3},{3,2},{4,5},{5,4},{6,7},{7,6},{8,9},{9,8},{10,11... | collective-permute-start | bytes 3145736 | tf_op jit(solution)/shard_map/ppermute | solution.py:35
  10.7 27.8 %collective-permute-start.12 = (bf16[512,512]{1,0:T(8,128)(2,1)S(1)}, bf16[512,512]{1,0:T(8,128)(2,1)S(1)}, u32[]{:S(2)}, u32[]{:S(2)}) collective-permute-start(bf16[512,512]{1,0:T(8,128)(2,1)S(1)} %get-tuple-element.84), channel_id=1, source_target_pairs={{0,4},{2,6},{4,0},{6,2},{1,5},{3,7},{5,1},{7,3},{8,12},{10,14},{12... | collective-permute-start | bytes 1572872 | tf_op jit(solution)/shard_map/ppermute | solution.py:35
  13.4 6.5 %collective-permute-start.4 = (bf16[272,256]{1,0:T(8,128)(2,1)S(1)}, bf16[272,256]{1,0:T(8,128)(2,1)S(1)}, u32[]{:S(2)}, u32[]{:S(2)}) collective-permute-start(bf16[272,256]{1,0:T(8,128)(2,1)S(1)} %get-tuple-element.59.sent), channel_id=1, source_target_pairs={{0,8},{8,0},{16,24},{24,16},{1,9},{9,1},{17,25},{25,17},{2,10},{10... | collective-permute-start | bytes 417800 | tf_op jit(solution)/shard_map/ppermute | solution.py:35
  15.0 7.2 %collective-permute-start.3 = (bf16[272,256]{1,0:T(8,128)(2,1)S(1)}, bf16[272,256]{1,0:T(8,128)(2,1)S(1)}, u32[]{:S(2)}, u32[]{:S(2)}) collective-permute-start(bf16[272,256]{1,0:T(8,128)(2,1)S(1)} %get-tuple-element.56.sent), channel_id=1, source_target_pairs={{0,8},{8,0},{16,24},{24,16},{1,9},{9,1},{17,25},{25,17},{2,10},{10... | collective-permute-start | bytes 417800 | tf_op jit(solution)/shard_map/ppermute | solution.py:35
  19.9 18.7 %collective-permute-start.10 = (bf16[512,512]{1,0:T(8,128)(2,1)S(1)}, bf16[512,512]{1,0:T(8,128)(2,1)S(1)}, u32[]{:S(2)}, u32[]{:S(2)}) collective-permute-start(bf16[512,512]{1,0:T(8,128)(2,1)S(1)} %get-tuple-element.82), channel_id=1, source_target_pairs={{0,2},{2,0},{4,6},{6,4},{1,3},{3,1},{5,7},{7,5},{8,10},{10,8},{12,... | collective-permute-start | bytes 1572872 | tf_op jit(solution)/shard_map/ppermute | solution.py:35
  22.2 12.9 %collective-permute-start.6 = (bf16[272,256]{1,0:T(8,128)(2,1)S(1)}, bf16[272,256]{1,0:T(8,128)(2,1)S(1)}, u32[]{:S(2)}, u32[]{:S(2)}) collective-permute-start(bf16[272,256]{1,0:T(8,128)(2,1)S(1)} %get-tuple-element.62), channel_id=1, source_target_pairs={{0,16},{8,24},{16,0},{24,8},{1,17},{9,25},{17,1},{25,9},{2,18},{10... | collective-permute-start | bytes 417800 | tf_op jit(solution)/shard_map/ppermute | solution.py:35
  25.6 11.3 %collective-permute-start.5 = (bf16[272,256]{1,0:T(8,128)(2,1)S(1)}, bf16[272,256]{1,0:T(8,128)(2,1)S(1)}, u32[]{:S(2)}, u32[]{:S(2)}) collective-permute-start(bf16[272,256]{1,0:T(8,128)(2,1)S(1)} %get-tuple-element.61), channel_id=1, source_target_pairs={{0,16},{8,24},{16,0},{24,8},{1,17},{9,25},{17,1},{25,9},{2,18},{10... | collective-permute-start | bytes 417800 | tf_op jit(solution)/shard_map/ppermute | solution.py:35
  38.6 4.9 %collective-permute-start.13 = (bf16[512,512]{1,0:T(8,128)(2,1)S(1)}, bf16[512,512]{1,0:T(8,128)(2,1)S(1)}, u32[]{:S(2)}, u32[]{:S(2)}) collective-permute-start(bf16[512,512]{1,0:T(8,128)(2,1)S(1)} %collective-permute-done.12.high_first), channel_id=1, source_target_pairs={{0,1},{1,0},{2,3},{3,2},{4,5},{5,4},{6,7},{7,6},{8,9},{9,8},{10,11... | collective-permute-start | bytes 1572872 | tf_op jit(solution)/shard_map/ppermute | solution.py:35
  38.6 7.5 %collective-permute-start.11 = (bf16[512,512]{1,0:T(8,128)(2,1)S(1)}, bf16[512,512]{1,0:T(8,128)(2,1)S(1)}, u32[]{:S(2)}, u32[]{:S(2)}) collective-permute-start(bf16[512,512]{1,0:T(8,128)(2,1)S(1)} %collective-permute-done.10.near_first), channel_id=1, source_target_pairs={{0,1},{1,0},{2,3},{3,2},{4,5},{5,4},{6,7},{7,6},{8,9},{9,8},{10,11... | collective-permute-start | bytes 1572872 | tf_op jit(solution)/shard_map/ppermute | solution.py:35
  39.1 9.2 %collective-permute-start.19 = (bf16[256,512]{1,0:T(8,128)(2,1)S(1)}, bf16[256,512]{1,0:T(8,128)(2,1)S(1)}, u32[]{:S(2)}, u32[]{:S(2)}) collective-permute-start(bf16[256,512]{1,0:T(8,128)(2,1)S(1)} %get-tuple-element.79.refs_3_), channel_id=1, source_target_pairs={{0,2},{2,0},{4,6},{6,4},{1,3},{3,1},{5,7},{7,5},{8,10},{10,8},{12,... | collective-permute-start | bytes 786440 | tf_op jit(solution)/shard_map/ppermute | solution.py:35
  40.6 9.2 %collective-permute-start.17 = (bf16[256,512]{1,0:T(8,128)(2,1)S(1)}, bf16[256,512]{1,0:T(8,128)(2,1)S(1)}, u32[]{:S(2)}, u32[]{:S(2)}) collective-permute-start(bf16[256,512]{1,0:T(8,128)(2,1)S(1)} %get-tuple-element.78.refs_2_), channel_id=1, source_target_pairs={{0,4},{2,6},{4,0},{6,2},{1,5},{3,7},{5,1},{7,3},{8,12},{10,14},{12... | collective-permute-start | bytes 786440 | tf_op jit(solution)/shard_map/ppermute | solution.py:35
  42.8 11.1 %collective-permute-start.15 = (bf16[256,512]{1,0:T(8,128)(2,1)S(1)}, bf16[256,512]{1,0:T(8,128)(2,1)S(1)}, u32[]{:S(2)}, u32[]{:S(2)}) collective-permute-start(bf16[256,512]{1,0:T(8,128)(2,1)S(1)} %get-tuple-element.77.refs_1_), channel_id=1, source_target_pairs={{0,2},{2,0},{4,6},{6,4},{1,3},{3,1},{5,7},{7,5},{8,10},{10,8},{12,... | collective-permute-start | bytes 786440 | tf_op jit(solution)/shard_map/ppermute | solution.py:35
  43.5 11.9 %collective-permute-start.9 = (bf16[256,512]{1,0:T(8,128)(2,1)S(1)}, bf16[256,512]{1,0:T(8,128)(2,1)S(1)}, u32[]{:S(2)}, u32[]{:S(2)}) collective-permute-start(bf16[256,512]{1,0:T(8,128)(2,1)S(1)} %get-tuple-element.76.refs_0_), channel_id=1, source_target_pairs={{0,4},{2,6},{4,0},{6,2},{1,5},{3,7},{5,1},{7,3},{8,12},{10,14},{12... | collective-permute-start | bytes 786440 | tf_op jit(solution)/shard_map/ppermute | solution.py:35
  48.6 12.5 %collective-permute-start.20 = (bf16[256,512]{1,0:T(8,128)(2,1)S(1)}, bf16[256,512]{1,0:T(8,128)(2,1)S(1)}, u32[]{:S(2)}, u32[]{:S(2)}) collective-permute-start(bf16[256,512]{1,0:T(8,128)(2,1)S(1)} %give.7), channel_id=1, source_target_pairs={{0,4},{2,6},{4,0},{6,2},{1,5},{3,7},{5,1},{7,3},{8,12},{10,14},{12... | collective-permute-start | bytes 786440 | tf_op jit(solution)/shard_map/ppermute | solution.py:35
  50.1 10.9 %collective-permute-start.18 = (bf16[256,512]{1,0:T(8,128)(2,1)S(1)}, bf16[256,512]{1,0:T(8,128)(2,1)S(1)}, u32[]{:S(2)}, u32[]{:S(2)}) collective-permute-start(bf16[256,512]{1,0:T(8,128)(2,1)S(1)} %give.6), channel_id=1, source_target_pairs={{0,2},{2,0},{4,6},{6,4},{1,3},{3,1},{5,7},{7,5},{8,10},{10,8},{12,... | collective-permute-start | bytes 786440 | tf_op jit(solution)/shard_map/ppermute | solution.py:35
  54.2 11.3 %collective-permute-start.16 = (bf16[256,512]{1,0:T(8,128)(2,1)S(1)}, bf16[256,512]{1,0:T(8,128)(2,1)S(1)}, u32[]{:S(2)}, u32[]{:S(2)}) collective-permute-start(bf16[256,512]{1,0:T(8,128)(2,1)S(1)} %give.5), channel_id=1, source_target_pairs={{0,4},{2,6},{4,0},{6,2},{1,5},{3,7},{5,1},{7,3},{8,12},{10,14},{12... | collective-permute-start | bytes 786440 | tf_op jit(solution)/shard_map/ppermute | solution.py:35
  55.7 9.7 %collective-permute-start.14 = (bf16[256,512]{1,0:T(8,128)(2,1)S(1)}, bf16[256,512]{1,0:T(8,128)(2,1)S(1)}, u32[]{:S(2)}, u32[]{:S(2)}) collective-permute-start(bf16[256,512]{1,0:T(8,128)(2,1)S(1)} %give.4), channel_id=1, source_target_pairs={{0,2},{2,0},{4,6},{6,4},{1,3},{3,1},{5,7},{7,5},{8,10},{10,8},{12,... | collective-permute-start | bytes 786440 | tf_op jit(solution)/shard_map/ppermute | solution.py:35

commit v6 on v5

--- a/solution.py
+++ b/solution.py
@@ -130,75 +130,107 @@
         return copy
 
 
-def half_tiles(x_far, x, half, loads):
-    rows, part = x.shape
-    columns = pl.ds(pl.multiple_of(half * part, part), part)
-    return [
-        functools.partial(loads.start, x_far.at[pl.ds(at, TILE), columns], x.at[pl.ds(at, TILE)])
-        for at in range(0, rows, TILE)
-    ]
-
-
 def key_value_own_kernel(
-    x_far, wk_far, wv_far, log_decay_far, wo_far, wq_far, wg_far,
-    x, acc_k, acc_v, decay, coarse, fine, wo, wq, wg, wk, wv, log_decay, arrived,
+    x_far, wk_far, wv_far, log_decay_far, wo_far,
+    x_own, x_other, acc_k, acc_v, decay, coarse, fine, wo, wk, wv, log_decay, arrived,
 ):
+    rows, part = x_own.shape
+    core = lax.axis_index("fsdp")
     loads = Loads(arrived)
-    tiles = half_tiles(x_far, x, lax.axis_index("fsdp"), loads)
+
+    def tile(x, half, number):
+        at = pl.ds(number * TILE, TILE)
+        columns = pl.ds(pl.multiple_of(half * part, part), part)
+        return loads.start(x_far.at[at, columns], x.at[at])
+
+    count = rows // TILE
     logs = loads.start(log_decay_far, log_decay)
-    key, first = loads.start(wk_far, wk), tiles[0]()
+    key, tiles = loads.start(wk_far, wk), [tile(x_own, core, 0)]
     value = loads.start(wv_far, wv)
-    rest = [tile() for tile in tiles[1:]]
-    others = [loads.start(wo_far, wo), loads.start(wq_far, wq), loads.start(wg_far, wg)]
     angle_tables(coarse, fine)
     logs.wait()
     decay_sums(log_decay, decay)
     key.wait()
-    for number, copy in enumerate([first, *rest]):
+    others = []
+    for number in range(count):
         at = slice(number * TILE, (number + 1) * TILE)
-        copy.wait()
-        acc_k[at, :] = mm(x[at, :], wk[...])
+        tiles[number].wait()
+        if number == 0:
+            tiles += [tile(x_own, core, later) for later in range(1, count)]
+        else:
+            others += [tile(x_other, 1 - core, later) for later in range(count) if later % (count - 1) == number - 1]
+            if number == count - 1:
+                others.append(loads.start(wo_far, wo))
+        acc_k[at, :] = mm(x_own[at, :], wk[...])
         if number == 0:
             value.wait()
-        acc_v[at, :] = mm(x[at, :], wv[...])
+        acc_v[at, :] = mm(x_own[at, :], wv[...])
     for copy in others:
         copy.wait()
 
 
-def pack_message(message, state, log):
+def pack_message(message, states, logs):
+    heads = len(states)
     place = lax.broadcasted_iota(jnp.int32, (EXTRA, DH), 0)
     tail = jnp.zeros((EXTRA, DH), F32)
-    message[:DH, :] = state.astype(BF16)
-    for number in range(3):
-        piece = log.astype(BF16).astype(F32)
-        tail = jnp.where(place == number, piece, tail)
-        log = log - piece
-    message[DH:, :] = tail.astype(BF16)
-
-
-def message_log(message):
-    tail = message[DH:, :].astype(F32)
-    return (tail[:1] + tail[1:2] + tail[2:3])[:, :1]
+    for head in range(heads):
+        message[head * DH : (head + 1) * DH, :] = states[head].astype(BF16)
+        rest = logs[head]
+        for number in range(3):
+            piece = rest.astype(BF16).astype(F32)
+            tail = jnp.where(place == 3 * head + number, piece, tail)
+            rest = rest - piece
+    message[heads * DH :, :] = tail.astype(BF16)
+
+
+def message_log(message, heads, head):
+    tail = message[heads * DH :, :].astype(F32)
+    return (tail[3 * head : 3 * head + 1] + tail[3 * head + 1 : 3 * head + 2] + tail[3 * head + 2 : 3 * head + 3])[:, :1]
+
+
+def exchanges(ctx, hop):
+    lower = range(ctx - hop)
+    early = [at for at in lower if at < hop // 2]
+    even = [at for at in lower if at >= hop // 2 and at // hop % 2 == 0]
+    odd = [at for at in lower if at // hop % 2 == 1]
+    return early, even, odd
+
+
+def is_upper(lowers, hop):
+    place = lax.axis_index("ctx")
+    found = place < 0
+    for lower in lowers:
+        found = jnp.logical_or(found, place == lower + hop)
+    return found
+
+
+def arrived_state(arrivals, sets, hop, span):
+    parts = [jnp.where(is_upper(lowers, hop), ref[span, :].astype(F32), 0.0) for ref, lowers in zip(arrivals, sets)]
+    return functools.reduce(lambda a, b: a + b, parts)
+
+
+def arrived_log(arrivals, sets, hop, heads, head):
+    parts = [jnp.where(is_upper(lowers, hop), message_log(ref, heads, head), 0.0) for ref, lowers in zip(arrivals, sets)]
+    return functools.reduce(lambda a, b: a + b, parts)
 
 
 def key_value_kernel(
-    heads, x_far, wk, wv, acc_k, acc_v, decay, coarse, fine, x, k_out, v_out, before_out, *refs
+    heads, wq_far, wg_far, x, wk, wv, acc_k, acc_v, decay, coarse, fine,
+    wq, wg, k_out, v_out, before_out, state_out, message, arrived,
 ):
-    states, messages, arrived = refs[:heads], refs[heads : 2 * heads], refs[-1]
     loads = Loads(arrived)
-    tiles = [tile() for tile in half_tiles(x_far, x, 1 - lax.axis_index("fsdp"), loads)]
-    totals, blocks = 0.0, x.shape[0] // BLOCK
-    for block in range(blocks):
-        start = block * BLOCK
-        columns = decay[:, start : start + BLOCK].T
+    others = [loads.start(wq_far, wq), loads.start(wg_far, wg)]
+    state_out[...] = jnp.zeros_like(state_out)
+
+    def block_step(block, totals):
+        start = pl.multiple_of(block * BLOCK, BLOCK)
+        columns = decay[:, pl.ds(start, BLOCK)].T
         ending = columns[BLOCK - 1 : BLOCK, :]
-        totals = totals + ending
         faded = jnp.exp(ending - columns)
         updates = [None] * heads
         for piece in range(BLOCK // TILE):
-            first = start + piece * TILE
-            at = slice(first, first + TILE)
-            tiles[first // TILE].wait()
+            first = pl.multiple_of(start + piece * TILE, TILE)
+            at = pl.ds(first, TILE)
             cosine, sine = angles(coarse, fine, first, TILE)
             keys = turned(acc_k[at, :] + mm(x[at, :], wk[...]), cosine, sine)
             values = (acc_v[at, :] + mm(x[at, :], wv[...])).astype(BF16)
@@ -212,35 +244,43 @@
                 updates[head] = update if piece == 0 else updates[head] + update
         for head in range(heads):
             span = slice(head * DH, (head + 1) * DH)
-            old = states[head][...] if block else jnp.zeros((DH, DH), F32)
+            old = state_out[span, :]
             before_out[block, span, :] = old.astype(BF16)
-            new = jnp.exp(ending[:, head : head + 1]) * old + updates[head]
-            states[head][...] = new
-            if block == blocks - 1:
-                pack_message(messages[head], new, totals[:, head : head + 1])
-
-
-def combine_kernel(hop, first, window, sent, *refs):
-    if first:
-        got, new_window, new_entering, message = refs
-    else:
-        entering, got, new_window, new_entering, message = refs
-    upper = (lax.axis_index("ctx") // hop) % 2 == 1
-    arrived = got[:DH, :].astype(F32)
-    window_log, arrived_log = message_log(sent), message_log(got)
-    if first:
-        new_entering[:DH, :] = jnp.where(upper, arrived, 0.0)
-        entering_log = jnp.zeros((1, 1), F32)
-    else:
-        entering_log = entering[DH : DH + 1, :1]
-        new_entering[:DH, :] = entering[:DH, :] + jnp.where(upper, jnp.exp(entering_log), 0.0) * arrived
-    entering_log = entering_log + jnp.where(upper, arrived_log, 0.0)
-    new_entering[DH:, :] = jnp.broadcast_to(entering_log, (8, DH))
-    own_fade = jnp.where(upper, 1.0, jnp.exp(arrived_log))
-    arrived_fade = jnp.where(upper, jnp.exp(window_log), 1.0)
-    joined = own_fade * window[...] + arrived_fade * arrived
-    new_window[...] = joined
-    pack_message(message, joined, window_log + arrived_log)
+            state_out[span, :] = jnp.exp(ending[:, head : head + 1]) * old + updates[head]
+        return totals + ending
+
+    totals = lax.fori_loop(0, x.shape[0] // BLOCK, block_step, jnp.zeros((1, 8), F32))
+    states = [state_out[head * DH : (head + 1) * DH, :] for head in range(heads)]
+    pack_message(message, states, [totals[:, head : head + 1] for head in range(heads)])
+    for copy in others:
+        copy.wait()
+
+
+def combine_kernel(heads, hop, sets, first, state, sent, *refs):
+    if not first:
+        old_entering, refs = refs[0], refs[1:]
+    arrivals = refs[: len(sets)]
+    window, entering, message = refs[len(sets) :]
+    states, logs = [], []
+    for head in range(heads):
+        span = slice(head * DH, (head + 1) * DH)
+        row = slice(heads * DH + head, heads * DH + head + 1)
+        arrived = arrived_state(arrivals, sets, hop, span)
+        log = arrived_log(arrivals, sets, hop, heads, head)
+        window_log = message_log(sent, heads, head)
+        if first:
+            entering[span, :] = arrived
+            entering_log = log
+        else:
+            before_log = old_entering[row, :1]
+            entering[span, :] = old_entering[span, :] + jnp.exp(before_log) * arrived
+            entering_log = before_log + log
+        entering[row, :] = jnp.broadcast_to(entering_log, (1, DH))
+        new = state[span, :] + jnp.exp(window_log) * arrived
+        window[span, :] = new
+        states.append(new)
+        logs.append(window_log + log)
+    pack_message(message, states, logs)
 
 
 def query_gate_kernel(
@@ -273,17 +313,14 @@
             intra_out[low:last, span] = mm((scores * weights).astype(BF16), v[start : start + last, span])
 
 
-def hidden_kernel(heads, hop, starts, decay, before, *refs):
-    refs, token = refs[:-1], refs[-1]
+def hidden_kernel(heads, hop, sets, starts, decay, before, entering, *refs):
+    arrivals, refs, token = refs[: len(sets)], refs[len(sets) : -1], refs[-1]
+    projected, outs = refs[: -len(starts)], refs[-len(starts) :]
     token[...] = jnp.zeros_like(token)
-    entering, arrivals, projected, outs = (
-        refs[:heads], refs[heads : 2 * heads], refs[2 * heads : -len(starts)], refs[-len(starts) :]
-    )
-    upper = (lax.axis_index("ctx") // hop) % 2 == 1
     for head in range(heads):
         span = slice(head * DH, (head + 1) * DH)
-        fade = jnp.where(upper, jnp.exp(entering[head][DH : DH + 1, :1]), 0.0)
-        state = entering[head][:DH, :] + fade * arrivals[head][:DH, :].astype(F32)
+        entering_log = entering[heads * DH + head : heads * DH + head + 1, :1]
+        state = entering[span, :] + jnp.exp(entering_log) * arrived_state(arrivals, sets, hop, span)
         for start, out in zip(starts, outs):
             block = start // BLOCK
             q, gate, intra = projected[3 * block : 3 * block + 3]
@@ -385,51 +422,54 @@
     key_far = swap(key_weight, "fsdp", 1)
     value_far = swap(value_weight, "fsdp", 1)
 
-    x_own, acc_k, acc_v, decay, coarse, fine, out_first, own_q, own_g = loading_call(
+    x_own, x_other, acc_k, acc_v, decay, coarse, fine, out_first = loading_call(
         key_value_own_kernel,
-        [((rows, part), BF16), ((rows, cols), F32), ((rows, cols), F32), ((8, rows), F32)]
+        [((rows, part), BF16)] * 2
+        + [((rows, cols), F32)] * 2
+        + [((8, rows), F32)]
         + tables
-        + [(out_weight.shape, BF16), ((part, cols), BF16), ((part, cols), BF16)],
-        [x, key_weight, value_weight, log_decay[0].T, out_weight, query_weight, gate_weight],
+        + [(out_weight.shape, BF16)],
+        [x, key_weight, value_weight, log_decay[0].T, out_weight],
         [],
         [pltpu.VMEM((part, cols), BF16)] * 2 + [pltpu.VMEM((heads, rows), F32)],
-        rows // TILE + 6,
+        2 * (rows // TILE) + 4,
         "key_value_own",
     )
-    message_shape, state_shape = (DH + EXTRA, DH), (DH, DH)
-    x_other, keys, values, before, *states = loading_call(
+    state_shape, message_shape = (heads * DH, DH), (heads * DH + EXTRA, DH)
+    own_q, own_g, keys, values, before, window, message = loading_call(
         functools.partial(key_value_kernel, heads),
-        [
-            ((rows, part), BF16),
-            ((rows, cols), BF16),
-            ((rows, cols), BF16),
-            ((blocks, heads * DH, DH), BF16),
-        ]
-        + [(state_shape, F32)] * heads
-        + [(message_shape, BF16)] * heads,
-        [x],
-        [key_far, value_far, acc_k, acc_v, decay, coarse, fine],
+        [((part, cols), BF16)] * 2
+        + [((rows, cols), BF16)] * 2
+        + [((blocks, heads * DH, DH), BF16), (state_shape, F32), (message_shape, BF16)],
+        [query_weight, gate_weight],
+        [x_other, key_far, value_far, acc_k, acc_v, decay, coarse, fine],
         [],
-        rows // TILE,
+        2,
         "key_value",
     )
-    windows, messages = states[:heads], states[heads:]
-    last_message = messages[-1]
-
-    entering = [None] * heads
-    hop = 1
+
+    def exchange(message, lowers, hop):
+        return lax.ppermute(
+            message, "ctx", [pair for at in lowers for pair in ((at, at + hop), (at + hop, at))]
+        )
+
+    entering, hop, early, last_message = None, 1, [], message
     while True:
-        arrivals = [swap(message, "ctx", hop) for message in messages]
+        first_set, *later_sets = exchanges(ctx, hop)
+        later_sets = [lowers for lowers in later_sets if lowers]
+        sets = later_sets + ([first_set] if first_set else [])
+        arrivals = [exchange(message, lowers, hop) for lowers in later_sets] + early
         if 2 * hop >= ctx:
             break
-        for head in range(heads):
-            old = [] if entering[head] is None else [entering[head]]
-            windows[head], entering[head], messages[head] = kernel_call(
-                functools.partial(combine_kernel, hop, not old),
-                [(state_shape, F32), ((DH + 8, DH), F32), (message_shape, BF16)],
-                [windows[head], messages[head], *old, arrivals[head]],
-                "combine",
-            )
+        unchanged = exchanges(ctx, 2 * hop)[0]
+        early = [exchange(message, unchanged, 2 * hop)]
+        old = [] if entering is None else [entering]
+        window, entering, message = kernel_call(
+            functools.partial(combine_kernel, heads, hop, sets, entering is None),
+            [(state_shape, F32), ((heads * DH + 8, DH), F32), (message_shape, BF16)],
+            [window, message, *old, *arrivals],
+            "combine",
+        )
         hop *= 2
 
     far_q, far_g = swap(own_q, "fsdp", 1), swap(own_g, "fsdp", 1)
@@ -443,7 +483,7 @@
     near_first = swap(for_near, "tp", near_mask)
     high_first = swap(for_high, "tp", far_mask)
 
-    held, projected = after(decay, *messages), []
+    held, projected = after(decay, message), []
     for block in range(blocks):
         projected += kernel_call(
             functools.partial(query_gate_kernel, heads, block),
@@ -457,9 +497,9 @@
     for number in range(count):
         held = after(decay, swap(pair[2], "fsdp", 1)) if number else decay
         pair = kernel_call(
-            functools.partial(hidden_kernel, heads, hop, [(half * count + number) * TILE for half in range(2)]),
+            functools.partial(hidden_kernel, heads, hop, sets, [(half * count + number) * TILE for half in range(2)]),
             [((TILE, cols), BF16)] * 2 + [((16, 128), BF16)],
-            [held, before, *entering, *arrivals, *projected],
+            [held, before, entering, *arrivals, *projected],
             "hidden",
         )
         if number == 0:

time: 66.8 us -> 68.2 us (1.021)
  starting transfers between devices: 18.5 us -> 23.9 us
  waiting for transfers between devices: 22.1 us -> 18.9 us
  Pallas kernels: 25.9 us -> 25.1 us
    ppermute x21 -> x17, waiting for transfers between devices: 22.1 us -> 12.5 us  [swap(): lax.ppermute(value, axis, [(place, place ^ mask) for place in range(size)])]
    ppermute x0 -> x4, starting transfers between devices: none -> 8.81 us  [exchange(): lax.ppermute(message, 'ctx', [pair for at in lowers for pair in ((at, at...]
    ppermute x0 -> x4, waiting for transfers between devices: none -> 6.35 us  [exchange(): lax.ppermute(message, 'ctx', [pair for at in lowers for pair in ((at, at...]
    ppermute x21 -> x17, starting transfers between devices: 18.5 us -> 15.1 us  [swap(): lax.ppermute(value, axis, [(place, place ^ mask) for place in range(size)])]
    pallas_call x14 -> x13, Pallas kernels: 15.7 us -> 15 us  [kernel_call(): pl.pallas_call(kernel, in_specs=[pl.BlockSpec(memory_space=pltpu.VMEM)] *...]
  transfers between devices with their start and end apart: 21 -> 21, of which waited for: 9 -> 7; matrix products, arithmetic and copies ran while one was open for 0% -> 0% of each run, Pallas kernels for 37% -> 35%
where the time goes in v6:
time: 68.2 us; the launch traced here: 68 us
  Pallas kernels  25.1 us (37%)
  starting transfers between devices  23.9 us (35%)
  waiting for transfers between devices  18.9 us (28%)
    ppermute x17, starting transfers between devices, swap(): lax.ppermute(value, axis, [(place, place ^ mask) for place in range(size)])  15.1 us
    pallas_call x13, Pallas kernels, kernel_call(): pl.pallas_call(kernel, in_specs=[pl.BlockSpec(memory_space=pltpu.VMEM)] *...  15 us
    ppermute x17, waiting for transfers between devices, swap(): lax.ppermute(value, axis, [(place, place ^ mask) for place in range(size)])  12.5 us
    pallas_call x2, Pallas kernels, loading_call(): pl.pallas_call(kernel, in_specs=[pl.BlockSpec(memory_space=pltpu.HBM)] *...  8.83 us
    ppermute x4, starting transfers between devices, exchange(): lax.ppermute(message, 'ctx', [pair for at in lowers for pair in ((at, at...  8.81 us
    ppermute x4, waiting for transfers between devices, exchange(): lax.ppermute(message, 'ctx', [pair for at in lowers for pair in ((at, at...  6.35 us
  transfers between devices with their start and end apart: 21, of which 7 were waited for; matrix products, arithmetic and copies ran while one was open for 0% of the time, Pallas kernels for 35%

profile of v6, /device:TPU:0, one launch (start us, length us, event | category | flops | bytes accessed | tf_op | source)
XLA Modules:
  0.0 68.0 jit_solution(11352108534388811608)
XLA Ops:
  0.5 5.5 %key_value_own.1 = (bf16[1024,1024]{1,0:T(8,128)(2,1)S(1)}, bf16[1024,1024]{1,0:T(8,128)(2,1)S(1)}, f32[1024,512]{1,0:T(8,128)S(1)}, f32[1024,512]{1,0:T(8,128)S...) custom-call(bf16[1024,2048]{1,0:T(8,128)(2,1)} %bitcast.4, ...), custom_call_target="tpu_custom_call" | custom-call | flops 1 | bytes 1 | tf_op jit(solution)/shard_map/key_value_own/pallas_call | solution.py:56
  6.0 0.5 collective-permute-start
  6.5 3.4 %key_value.1 = (bf16[1024,512]{1,0:T(8,128)(2,1)S(1)}, bf16[1024,512]{1,0:T(8,128)(2,1)S(1)}, bf16[1024,512]{1,0:T(8,128)(2,1)S(1)}, bf16[1024,512]{1,0:T(8,128)...) custom-call(bf16[1024,512]{1,0:T(8,128)(2,1)} %wq_far.1, ...), custom_call_target="tpu_custom_call" | custom-call | flops 1 | bytes 1 | tf_op jit(solution)/shard_map/key_value/pallas_call | solution.py:56
  10.5 2.6 %collective-permute-start.3 = (bf16[528,256]{1,0:T(8,128)(2,1)S(1)}, bf16[528,256]{1,0:T(8,128)(2,1)S(1)}, u32[]{:S(2)}, u32[]{:S(2)}) collective-permute-start(bf16[528,256]{1,0:T(8,128)(2,1)S(1)} %get-tuple-element.53.sent), channel_id=1, source_target_pairs={{0,8},{8,0},{16,24},{24,16},{1,9},{9,1},{17,25},{25,17},{2,10},{10... | collective-permute-start | bytes 811016 | tf_op jit(solution)/shard_map/ppermute | solution.py:452
  13.1 0.7 collective-permute-start.4
  13.9 1.6 %collective-permute-start.12 = (bf16[512,512]{1,0:T(8,128)(2,1)S(1)}, bf16[512,512]{1,0:T(8,128)(2,1)S(1)}, u32[]{:S(2)}, u32[]{:S(2)}) collective-permute-start(bf16[512,512]{1,0:T(8,128)(2,1)S(1)} %get-tuple-element.76), channel_id=1, source_target_pairs={{0,4},{2,6},{4,0},{6,2},{1,5},{3,7},{5,1},{7,3},{8,12},{10,14},{12... | collective-permute-start | bytes 1572872 | tf_op jit(solution)/shard_map/ppermute | solution.py:35
  15.5 4.7 %collective-permute-done.3.refs_0_ = bf16[528,256]{1,0:T(8,128)(2,1)S(1)} collective-permute-done((bf16[528,256]{1,0:T(8,128)(2,1)S(1)}, bf16[528,256]{1,0:T(8,128)(2,1)S(1)}, u32[]{:S(2)}, u32[]{:S(2)}) %collective-permute-start.3) | collective-permute-done | bytes 270368 | tf_op jit(solution)/shard_map/ppermute | solution.py:452
  20.2 4.7 %collective-permute-start.6 = (bf16[528,256]{1,0:T(8,128)(2,1)S(1)}, bf16[528,256]{1,0:T(8,128)(2,1)S(1)}, u32[]{:S(2)}, u32[]{:S(2)}) collective-permute-start(bf16[528,256]{1,0:T(8,128)(2,1)S(1)} %get-tuple-element.53.sent), channel_id=1, source_target_pairs={{0,16},{16,0},{1,17},{17,1},{2,18},{18,2},{3,19},{19,3},{4,20},{20... | collective-permute-start | bytes 811016 | tf_op jit(solution)/shard_map/ppermute | solution.py:452
  24.9 1.0 %combine.1 = (f32[512,256]{1,0:T(8,128)}, f32[520,256]{1,0:T(8,128)S(1)}, bf16[528,256]{1,0:T(8,128)(2,1)S(1)}) custom-call(f32[512,256]{1,0:T(8,128)S(1)} %get-tuple-element.52.state, bf16[528,256]{1,0:T(8,128)(2,1)S(1)} %get-tuple-element.53.sent, bf16[528,256]{1,0:T(8,128)(2,1)S(1)} %collective-permute-done.3.refs_0_, ...), custom_call_target="tpu_custom_call" | custom-call | flops 1 | bytes 1 | tf_op jit(solution)/shard_map/combine/pallas_call | solution.py:40
  25.9 0.8 %collective-permute-start.5 = (bf16[528,256]{1,0:T(8,128)(2,1)S(1)}, bf16[528,256]{1,0:T(8,128)(2,1)S(1)}, u32[]{:S(2)}, u32[]{:S(2)}) collective-permute-start(bf16[528,256]{1,0:T(8,128)(2,1)S(1)} %get-tuple-element.55), channel_id=1, source_target_pairs={{8,24},{24,8},{9,25},{25,9},{10,26},{26,10},{11,27},{27,11},{12,28... | collective-permute-start | bytes 811016 | tf_op jit(solution)/shard_map/ppermute | solution.py:452
  26.7 1.6 %collective-permute-start.10 = (bf16[512,512]{1,0:T(8,128)(2,1)S(1)}, bf16[512,512]{1,0:T(8,128)(2,1)S(1)}, u32[]{:S(2)}, u32[]{:S(2)}) collective-permute-start(bf16[512,512]{1,0:T(8,128)(2,1)S(1)} %get-tuple-element.74), channel_id=1, source_target_pairs={{0,2},{2,0},{4,6},{6,4},{1,3},{3,1},{5,7},{7,5},{8,10},{10,8},{12,... | collective-permute-start | bytes 1572872 | tf_op jit(solution)/shard_map/ppermute | solution.py:35
  28.3 3.5 %query_gate.3 = (bf16[512,512]{1,0:T(8,128)(2,1)S(1)}, bf16[512,512]{1,0:T(8,128)(2,1)S(1)}, f32[512,512]{1,0:T(8,128)S(1)}) custom-call(bf16[1024,1024]{1,0:T(8,128)(2,1)S(1)} %get-tuple-element.56.x_own, bf16[1024,1024]{1,0:T(8,128)(2,1)S(1)} %get-tuple-element.46.x.x_other, bf16[1024,512]{1,0:T(8,128)(2,1)S(1)} %get-tuple-element.57.wq, ...), custom_call_target="tpu_custom_call" | custom-call | flops 1 | bytes 1 | tf_op jit(solution)/shard_map/query_gate/pallas_call | solution.py:40
  31.8 3.5 %query_gate.2 = (bf16[512,512]{1,0:T(8,128)(2,1)S(1)}, bf16[512,512]{1,0:T(8,128)(2,1)S(1)}, f32[512,512]{1,0:T(8,128)S(1)}) custom-call(bf16[1024,1024]{1,0:T(8,128)(2,1)S(1)} %get-tuple-element.56.x_own, bf16[1024,1024]{1,0:T(8,128)(2,1)S(1)} %get-tuple-element.46.x.x_other, bf16[1024,512]{1,0:T(8,128)(2,1)S(1)} %get-tuple-element.57.wq, ...), custom_call_target="tpu_custom_call" | custom-call | flops 1 | bytes 1 | tf_op jit(solution)/shard_map/query_gate/pallas_call | solution.py:40
  35.3 1.7 %collective-permute-done.6.refs_1_ = bf16[528,256]{1,0:T(8,128)(2,1)S(1)} collective-permute-done((bf16[528,256]{1,0:T(8,128)(2,1)S(1)}, bf16[528,256]{1,0:T(8,128)(2,1)S(1)}, u32[]{:S(2)}, u32[]{:S(2)}) %collective-permute-start.6) | collective-permute-done | bytes 270368 | tf_op jit(solution)/shard_map/ppermute | solution.py:452
  37.0 1.7 %hidden.3 = (bf16[256,512]{1,0:T(8,128)(2,1)S(1)}, bf16[256,512]{1,0:T(8,128)(2,1)S(1)}, bf16[16,128]{1,0:T(8,128)(2,1)}) custom-call(f32[8,1024]{1,0:T(8,128)S(1)} %get-tuple-element.59.decay, bf16[2,512,256]{2,1,0:T(8,128)(2,1)S(1)} %get-tuple-element.51.before, f32[520,256]{1,0:T(8,128)S(1)} %get-tuple-element.54.entering, ...), custom_call_target="tpu_custom_call" | custom-call | flops 1 | bytes 1 | tf_op jit(solution)/shard_map/hidden/pallas_call | solution.py:40
  38.7 1.3 %collective-permute-done.10.near_first = bf16[512,512]{1,0:T(8,128)(2,1)S(1)} collective-permute-done((bf16[512,512]{1,0:T(8,128)(2,1)S(1)}, bf16[512,512]{1,0:T(8,128)(2,1)S(1)}, u32[]{:S(2)}, u32[]{:S(2)}) %collective-permute-start.10) | collective-permute-done | bytes 524320 | tf_op jit(solution)/shard_map/ppermute | solution.py:35
  40.0 1.5 %collective-permute-start.19 = (bf16[256,512]{1,0:T(8,128)(2,1)S(1)}, bf16[256,512]{1,0:T(8,128)(2,1)S(1)}, u32[]{:S(2)}, u32[]{:S(2)}) collective-permute-start(bf16[256,512]{1,0:T(8,128)(2,1)S(1)} %get-tuple-element.71.refs_3_), channel_id=1, source_target_pairs={{0,2},{2,0},{4,6},{6,4},{1,3},{3,1},{5,7},{7,5},{8,10},{10,8},{12,... | collective-permute-start | bytes 786440 | tf_op jit(solution)/shard_map/ppermute | solution.py:35
  41.5 1.5 %collective-permute-start.17 = (bf16[256,512]{1,0:T(8,128)(2,1)S(1)}, bf16[256,512]{1,0:T(8,128)(2,1)S(1)}, u32[]{:S(2)}, u32[]{:S(2)}) collective-permute-start(bf16[256,512]{1,0:T(8,128)(2,1)S(1)} %get-tuple-element.70.refs_2_), channel_id=1, source_target_pairs={{0,4},{2,6},{4,0},{6,2},{1,5},{3,7},{5,1},{7,3},{8,12},{10,14},{12... | collective-permute-start | bytes 786440 | tf_op jit(solution)/shard_map/ppermute | solution.py:35
  43.0 1.7 %hidden.2 = (bf16[256,512]{1,0:T(8,128)(2,1)S(1)}, bf16[256,512]{1,0:T(8,128)(2,1)S(1)}, bf16[16,128]{1,0:T(8,128)(2,1)}) custom-call(f32[8,1024]{1,0:T(8,128)S(1)} %get-tuple-element.59.decay, bf16[2,512,256]{2,1,0:T(8,128)(2,1)S(1)} %get-tuple-element.51.before, f32[520,256]{1,0:T(8,128)S(1)} %get-tuple-element.54.entering, ...), custom_call_target="tpu_custom_call" | custom-call | flops 1 | bytes 1 | tf_op jit(solution)/shard_map/hidden/pallas_call | solution.py:40
  44.8 0.5 collective-permute-start.15
  45.3 0.5 collective-permute-start.9
  45.8 1.3 %own_products.1 = (f32[512,1024]{1,0:T(8,128)S(1)}, f32[512,1024]{1,0:T(8,128)S(1)}) custom-call(bf16[512,1024]{1,0:T(8,128)(2,1)S(1)} %get-tuple-element.73.own_first, bf16[512,1024]{1,0:T(8,128)(2,1)S(1)} %collective-permute-done.own_second, bf16[256,512]{1,0:T(8,128)(2,1)S(1)} %get-tuple-element.68.refs_0_, ...), custom_call_target="tpu_custom_call" | custom-call | flops 1 | bytes 1 | tf_op jit(solution)/shard_map/own_products/pallas_call | solution.py:40
  47.4 1.8 %collective-permute-done.19.far.refs_3_ = bf16[256,512]{1,0:T(8,128)(2,1)S(1)} collective-permute-done((bf16[256,512]{1,0:T(8,128)(2,1)S(1)}, bf16[256,512]{1,0:T(8,128)(2,1)S(1)}, u32[]{:S(2)}, u32[]{:S(2)}) %collective-permute-start.19) | collective-permute-done | bytes 262176 | tf_op jit(solution)/shard_map/ppermute | solution.py:35
  49.4 1.6 %collective-permute-start.20 = (bf16[256,512]{1,0:T(8,128)(2,1)S(1)}, bf16[256,512]{1,0:T(8,128)(2,1)S(1)}, u32[]{:S(2)}, u32[]{:S(2)}) collective-permute-start(bf16[256,512]{1,0:T(8,128)(2,1)S(1)} %give.7), channel_id=1, source_target_pairs={{0,4},{2,6},{4,0},{6,2},{1,5},{3,7},{5,1},{7,3},{8,12},{10,14},{12... | collective-permute-start | bytes 786440 | tf_op jit(solution)/shard_map/ppermute | solution.py:35
  51.3 1.6 %collective-permute-start.18 = (bf16[256,512]{1,0:T(8,128)(2,1)S(1)}, bf16[256,512]{1,0:T(8,128)(2,1)S(1)}, u32[]{:S(2)}, u32[]{:S(2)}) collective-permute-start(bf16[256,512]{1,0:T(8,128)(2,1)S(1)} %give.6), channel_id=1, source_target_pairs={{0,2},{2,0},{4,6},{6,4},{1,3},{3,1},{5,7},{7,5},{8,10},{10,8},{12,... | collective-permute-start | bytes 786440 | tf_op jit(solution)/shard_map/ppermute | solution.py:35
  52.9 1.9 %collective-permute-done.15.far.refs_1_ = bf16[256,512]{1,0:T(8,128)(2,1)S(1)} collective-permute-done((bf16[256,512]{1,0:T(8,128)(2,1)S(1)}, bf16[256,512]{1,0:T(8,128)(2,1)S(1)}, u32[]{:S(2)}, u32[]{:S(2)}) %collective-permute-start.15) | collective-permute-done | bytes 262176 | tf_op jit(solution)/shard_map/ppermute | solution.py:35
  55.0 1.6 %collective-permute-start.16 = (bf16[256,512]{1,0:T(8,128)(2,1)S(1)}, bf16[256,512]{1,0:T(8,128)(2,1)S(1)}, u32[]{:S(2)}, u32[]{:S(2)}) collective-permute-start(bf16[256,512]{1,0:T(8,128)(2,1)S(1)} %give.5), channel_id=1, source_target_pairs={{0,4},{2,6},{4,0},{6,2},{1,5},{3,7},{5,1},{7,3},{8,12},{10,14},{12... | collective-permute-start | bytes 786440 | tf_op jit(solution)/shard_map/ppermute | solution.py:35
  56.9 1.6 %collective-permute-start.14 = (bf16[256,512]{1,0:T(8,128)(2,1)S(1)}, bf16[256,512]{1,0:T(8,128)(2,1)S(1)}, u32[]{:S(2)}, u32[]{:S(2)}) collective-permute-start(bf16[256,512]{1,0:T(8,128)(2,1)S(1)} %give.4), channel_id=1, source_target_pairs={{0,2},{2,0},{4,6},{6,4},{1,3},{3,1},{5,7},{7,5},{8,10},{10,8},{12,... | collective-permute-start | bytes 786440 | tf_op jit(solution)/shard_map/ppermute | solution.py:35
  58.5 0.7 %keep.1 = (f32[512,512]{1,0:T(8,128)S(1)}, f32[512,512]{1,0:T(8,128)S(1)}) custom-call(bf16[256,512]{1,0:T(8,128)(2,1)S(1)} %collective-permute-done.9.far.refs_0_, bf16[256,512]{1,0:T(8,128)(2,1)S(1)} %collective-permute-done.15.far.refs_1_, bf16[256,512]{1,0:T(8,128)(2,1)S(1)} %collective-permute-done.17.far.refs_2_, ...), custom_call_target="tpu_custom_call" | custom-call | flops 1 | bytes 1 | tf_op jit(solution)/shard_map/keep/pallas_call | solution.py:40
  59.2 2.7 %collective-permute-done.20.refs_3_ = bf16[256,512]{1,0:T(8,128)(2,1)S(1)} collective-permute-done((bf16[256,512]{1,0:T(8,128)(2,1)S(1)}, bf16[256,512]{1,0:T(8,128)(2,1)S(1)}, u32[]{:S(2)}, u32[]{:S(2)}) %collective-permute-start.20) | collective-permute-done | bytes 262176 | tf_op jit(solution)/shard_map/ppermute | solution.py:35
  61.9 4.9 %collective-permute-done.16.refs_1_ = bf16[256,512]{1,0:T(8,128)(2,1)S(1)} collective-permute-done((bf16[256,512]{1,0:T(8,128)(2,1)S(1)}, bf16[256,512]{1,0:T(8,128)(2,1)S(1)}, u32[]{:S(2)}, u32[]{:S(2)}) %collective-permute-start.16) | collective-permute-done | bytes 262176 | tf_op jit(solution)/shard_map/ppermute | solution.py:35
  66.8 1.2 %finish.1 = bf16[1,1024,512]{2,1,0:T(8,128)(2,1)} custom-call(bf16[256,512]{1,0:T(8,128)(2,1)S(1)} %collective-permute-done.14.refs_0_, bf16[256,512]{1,0:T(8,128)(2,1)S(1)} %collective-permute-done.16.refs_1_, bf16[256,512]{1,0:T(8,128)(2,1)S(1)} %collective-permute-done.18.refs_2_, bf16[256,512]{1,0:T(8,128)(2,1)S(1)} %collective-permute-done.20.refs_3_, ...), custom_call_target="tpu_custom_call" | custom-call | tf_op jit(solution)/shard_map/finish/pallas_call | solution.py:540
  (26 shorter events, 2.7 us)
Async XLA Ops:
  0.0 6.5 %collective-permute-start.1 = (bf16[1024,512]{1,0:T(8,128)(2,1)}, bf16[1024,512]{1,0:T(8,128)(2,1)S(1)}, u32[]{:S(2)}, u32[]{:S(2)}) collective-permute-start(bf16[1024,512]{1,0:T(8,128)(2,1)} %wk_far.1), channel_id=1, source_target_pairs={{0,1},{1,0},{2,3},{3,2},{4,5},{5,4},{6,7},{7,6},{8,9},{9,8},{10,11... | collective-permute-start | bytes 3145736 | tf_op jit(solution)/shard_map/ppermute | solution.py:35
  0.5 6.0 %collective-permute-start.2 = (bf16[1024,512]{1,0:T(8,128)(2,1)}, bf16[1024,512]{1,0:T(8,128)(2,1)S(1)}, u32[]{:S(2)}, u32[]{:S(2)}) collective-permute-start(bf16[1024,512]{1,0:T(8,128)(2,1)} %wv_far.1), channel_id=1, source_target_pairs={{0,1},{1,0},{2,3},{3,2},{4,5},{5,4},{6,7},{7,6},{8,9},{9,8},{10,11... | collective-permute-start | bytes 3145736 | tf_op jit(solution)/shard_map/ppermute | solution.py:35
  6.0 7.8 %collective-permute-start = (bf16[512,1024]{1,0:T(8,128)(2,1)S(1)}, bf16[512,1024]{1,0:T(8,128)(2,1)S(1)}, u32[]{:S(2)}, u32[]{:S(2)}) collective-permute-start(bf16[512,1024]{1,0:T(8,128)(2,1)S(1)} %get-tuple-element.73.own_first), channel_id=1, source_target_pairs={{0,1},{1,0},{2,3},{3,2},{4,5},{5,4},{6,7},{7,6},{8,9},{9,8},{10,11... | collective-permute-start | bytes 3145736 | tf_op jit(solution)/shard_map/ppermute | solution.py:35
  9.9 16.9 %collective-permute-start.7 = (bf16[1024,512]{1,0:T(8,128)(2,1)S(1)}, bf16[1024,512]{1,0:T(8,128)(2,1)S(1)}, u32[]{:S(2)}, u32[]{:S(2)}) collective-permute-start(bf16[1024,512]{1,0:T(8,128)(2,1)S(1)} %get-tuple-element.57.wq), channel_id=1, source_target_pairs={{0,1},{1,0},{2,3},{3,2},{4,5},{5,4},{6,7},{7,6},{8,9},{9,8},{10,11... | collective-permute-start | bytes 3145736 | tf_op jit(solution)/shard_map/ppermute | solution.py:35
  10.0 18.3 %collective-permute-start.8 = (bf16[1024,512]{1,0:T(8,128)(2,1)S(1)}, bf16[1024,512]{1,0:T(8,128)(2,1)S(1)}, u32[]{:S(2)}, u32[]{:S(2)}) collective-permute-start(bf16[1024,512]{1,0:T(8,128)(2,1)S(1)} %get-tuple-element.58.wg), channel_id=1, source_target_pairs={{0,1},{1,0},{2,3},{3,2},{4,5},{5,4},{6,7},{7,6},{8,9},{9,8},{10,11... | collective-permute-start | bytes 3145736 | tf_op jit(solution)/shard_map/ppermute | solution.py:35
  10.5 9.7 %collective-permute-start.3 = (bf16[528,256]{1,0:T(8,128)(2,1)S(1)}, bf16[528,256]{1,0:T(8,128)(2,1)S(1)}, u32[]{:S(2)}, u32[]{:S(2)}) collective-permute-start(bf16[528,256]{1,0:T(8,128)(2,1)S(1)} %get-tuple-element.53.sent), channel_id=1, source_target_pairs={{0,8},{8,0},{16,24},{24,16},{1,9},{9,1},{17,25},{25,17},{2,10},{10... | collective-permute-start | bytes 811016 | tf_op jit(solution)/shard_map/ppermute | solution.py:452
  13.1 11.8 %collective-permute-start.4 = (bf16[528,256]{1,0:T(8,128)(2,1)S(1)}, bf16[528,256]{1,0:T(8,128)(2,1)S(1)}, u32[]{:S(2)}, u32[]{:S(2)}) collective-permute-start(bf16[528,256]{1,0:T(8,128)(2,1)S(1)} %get-tuple-element.53.sent), channel_id=1, source_target_pairs={{8,16},{16,8},{9,17},{17,9},{10,18},{18,10},{11,19},{19,11},{12,20... | collective-permute-start | bytes 811016 | tf_op jit(solution)/shard_map/ppermute | solution.py:452
  13.9 24.8 %collective-permute-start.12 = (bf16[512,512]{1,0:T(8,128)(2,1)S(1)}, bf16[512,512]{1,0:T(8,128)(2,1)S(1)}, u32[]{:S(2)}, u32[]{:S(2)}) collective-permute-start(bf16[512,512]{1,0:T(8,128)(2,1)S(1)} %get-tuple-element.76), channel_id=1, source_target_pairs={{0,4},{2,6},{4,0},{6,2},{1,5},{3,7},{5,1},{7,3},{8,12},{10,14},{12... | collective-permute-start | bytes 1572872 | tf_op jit(solution)/shard_map/ppermute | solution.py:35
  20.2 16.8 %collective-permute-start.6 = (bf16[528,256]{1,0:T(8,128)(2,1)S(1)}, bf16[528,256]{1,0:T(8,128)(2,1)S(1)}, u32[]{:S(2)}, u32[]{:S(2)}) collective-permute-start(bf16[528,256]{1,0:T(8,128)(2,1)S(1)} %get-tuple-element.53.sent), channel_id=1, source_target_pairs={{0,16},{16,0},{1,17},{17,1},{2,18},{18,2},{3,19},{19,3},{4,20},{20... | collective-permute-start | bytes 811016 | tf_op jit(solution)/shard_map/ppermute | solution.py:452
  25.9 11.1 %collective-permute-start.5 = (bf16[528,256]{1,0:T(8,128)(2,1)S(1)}, bf16[528,256]{1,0:T(8,128)(2,1)S(1)}, u32[]{:S(2)}, u32[]{:S(2)}) collective-permute-start(bf16[528,256]{1,0:T(8,128)(2,1)S(1)} %get-tuple-element.55), channel_id=1, source_target_pairs={{8,24},{24,8},{9,25},{25,9},{10,26},{26,10},{11,27},{27,11},{12,28... | collective-permute-start | bytes 811016 | tf_op jit(solution)/shard_map/ppermute | solution.py:452
  26.7 13.3 %collective-permute-start.10 = (bf16[512,512]{1,0:T(8,128)(2,1)S(1)}, bf16[512,512]{1,0:T(8,128)(2,1)S(1)}, u32[]{:S(2)}, u32[]{:S(2)}) collective-permute-start(bf16[512,512]{1,0:T(8,128)(2,1)S(1)} %get-tuple-element.74), channel_id=1, source_target_pairs={{0,2},{2,0},{4,6},{6,4},{1,3},{3,1},{5,7},{7,5},{8,10},{10,8},{12,... | collective-permute-start | bytes 1572872 | tf_op jit(solution)/shard_map/ppermute | solution.py:35
  38.7 6.6 %collective-permute-start.13 = (bf16[512,512]{1,0:T(8,128)(2,1)S(1)}, bf16[512,512]{1,0:T(8,128)(2,1)S(1)}, u32[]{:S(2)}, u32[]{:S(2)}) collective-permute-start(bf16[512,512]{1,0:T(8,128)(2,1)S(1)} %collective-permute-done.12.high_first), channel_id=1, source_target_pairs={{0,1},{1,0},{2,3},{3,2},{4,5},{5,4},{6,7},{7,6},{8,9},{9,8},{10,11... | collective-permute-start | bytes 1572872 | tf_op jit(solution)/shard_map/ppermute | solution.py:35
  40.0 7.1 %collective-permute-start.11 = (bf16[512,512]{1,0:T(8,128)(2,1)S(1)}, bf16[512,512]{1,0:T(8,128)(2,1)S(1)}, u32[]{:S(2)}, u32[]{:S(2)}) collective-permute-start(bf16[512,512]{1,0:T(8,128)(2,1)S(1)} %collective-permute-done.10.near_first), channel_id=1, source_target_pairs={{0,1},{1,0},{2,3},{3,2},{4,5},{5,4},{6,7},{7,6},{8,9},{9,8},{10,11... | collective-permute-start | bytes 1572872 | tf_op jit(solution)/shard_map/ppermute | solution.py:35
  40.0 9.1 %collective-permute-start.19 = (bf16[256,512]{1,0:T(8,128)(2,1)S(1)}, bf16[256,512]{1,0:T(8,128)(2,1)S(1)}, u32[]{:S(2)}, u32[]{:S(2)}) collective-permute-start(bf16[256,512]{1,0:T(8,128)(2,1)S(1)} %get-tuple-element.71.refs_3_), channel_id=1, source_target_pairs={{0,2},{2,0},{4,6},{6,4},{1,3},{3,1},{5,7},{7,5},{8,10},{10,8},{12,... | collective-permute-start | bytes 786440 | tf_op jit(solution)/shard_map/ppermute | solution.py:35
  41.5 9.5 %collective-permute-start.17 = (bf16[256,512]{1,0:T(8,128)(2,1)S(1)}, bf16[256,512]{1,0:T(8,128)(2,1)S(1)}, u32[]{:S(2)}, u32[]{:S(2)}) collective-permute-start(bf16[256,512]{1,0:T(8,128)(2,1)S(1)} %get-tuple-element.70.refs_2_), channel_id=1, source_target_pairs={{0,4},{2,6},{4,0},{6,2},{1,5},{3,7},{5,1},{7,3},{8,12},{10,14},{12... | collective-permute-start | bytes 786440 | tf_op jit(solution)/shard_map/ppermute | solution.py:35
  44.8 10.0 %collective-permute-start.15 = (bf16[256,512]{1,0:T(8,128)(2,1)S(1)}, bf16[256,512]{1,0:T(8,128)(2,1)S(1)}, u32[]{:S(2)}, u32[]{:S(2)}) collective-permute-start(bf16[256,512]{1,0:T(8,128)(2,1)S(1)} %get-tuple-element.69.refs_1_), channel_id=1, source_target_pairs={{0,2},{2,0},{4,6},{6,4},{1,3},{3,1},{5,7},{7,5},{8,10},{10,8},{12,... | collective-permute-start | bytes 786440 | tf_op jit(solution)/shard_map/ppermute | solution.py:35
  45.3 11.3 %collective-permute-start.9 = (bf16[256,512]{1,0:T(8,128)(2,1)S(1)}, bf16[256,512]{1,0:T(8,128)(2,1)S(1)}, u32[]{:S(2)}, u32[]{:S(2)}) collective-permute-start(bf16[256,512]{1,0:T(8,128)(2,1)S(1)} %get-tuple-element.68.refs_0_), channel_id=1, source_target_pairs={{0,4},{2,6},{4,0},{6,2},{1,5},{3,7},{5,1},{7,3},{8,12},{10,14},{12... | collective-permute-start | bytes 786440 | tf_op jit(solution)/shard_map/ppermute | solution.py:35
  49.4 12.5 %collective-permute-start.20 = (bf16[256,512]{1,0:T(8,128)(2,1)S(1)}, bf16[256,512]{1,0:T(8,128)(2,1)S(1)}, u32[]{:S(2)}, u32[]{:S(2)}) collective-permute-start(bf16[256,512]{1,0:T(8,128)(2,1)S(1)} %give.7), channel_id=1, source_target_pairs={{0,4},{2,6},{4,0},{6,2},{1,5},{3,7},{5,1},{7,3},{8,12},{10,14},{12... | collective-permute-start | bytes 786440 | tf_op jit(solution)/shard_map/ppermute | solution.py:35
  51.3 10.6 %collective-permute-start.18 = (bf16[256,512]{1,0:T(8,128)(2,1)S(1)}, bf16[256,512]{1,0:T(8,128)(2,1)S(1)}, u32[]{:S(2)}, u32[]{:S(2)}) collective-permute-start(bf16[256,512]{1,0:T(8,128)(2,1)S(1)} %give.6), channel_id=1, source_target_pairs={{0,2},{2,0},{4,6},{6,4},{1,3},{3,1},{5,7},{7,5},{8,10},{10,8},{12,... | collective-permute-start | bytes 786440 | tf_op jit(solution)/shard_map/ppermute | solution.py:35
  55.0 11.8 %collective-permute-start.16 = (bf16[256,512]{1,0:T(8,128)(2,1)S(1)}, bf16[256,512]{1,0:T(8,128)(2,1)S(1)}, u32[]{:S(2)}, u32[]{:S(2)}) collective-permute-start(bf16[256,512]{1,0:T(8,128)(2,1)S(1)} %give.5), channel_id=1, source_target_pairs={{0,4},{2,6},{4,0},{6,2},{1,5},{3,7},{5,1},{7,3},{8,12},{10,14},{12... | collective-permute-start | bytes 786440 | tf_op jit(solution)/shard_map/ppermute | solution.py:35
  56.9 9.9 %collective-permute-start.14 = (bf16[256,512]{1,0:T(8,128)(2,1)S(1)}, bf16[256,512]{1,0:T(8,128)(2,1)S(1)}, u32[]{:S(2)}, u32[]{:S(2)}) collective-permute-start(bf16[256,512]{1,0:T(8,128)(2,1)S(1)} %give.4), channel_id=1, source_target_pairs={{0,2},{2,0},{4,6},{6,4},{1,3},{3,1},{5,7},{7,5},{8,10},{10,8},{12,... | collective-permute-start | bytes 786440 | tf_op jit(solution)/shard_map/ppermute | solution.py:35

commit v7 on v6

--- a/solution.py
+++ b/solution.py
@@ -131,36 +131,28 @@
 
 
 def key_value_own_kernel(
-    x_far, wk_far, wv_far, log_decay_far, wo_far,
-    x_own, x_other, acc_k, acc_v, decay, coarse, fine, wo, wk, wv, log_decay, arrived,
+    x_far, wk_far, wv_far, log_decay_far, x_own, x_other, acc_k, acc_v, decay, coarse, fine, wk, wv, log_decay, arrived
 ):
     rows, part = x_own.shape
     core = lax.axis_index("fsdp")
     loads = Loads(arrived)
 
-    def tile(x, half, number):
-        at = pl.ds(number * TILE, TILE)
+    def tile(x, half, start):
         columns = pl.ds(pl.multiple_of(half * part, part), part)
-        return loads.start(x_far.at[at, columns], x.at[at])
-
-    count = rows // TILE
+        return loads.start(x_far.at[pl.ds(start, TILE), columns], x.at[pl.ds(start, TILE)])
+
     logs = loads.start(log_decay_far, log_decay)
     key, tiles = loads.start(wk_far, wk), [tile(x_own, core, 0)]
     value = loads.start(wv_far, wv)
+    tiles += [tile(x_own, core, start) for start in range(TILE, rows, TILE)]
+    others = [tile(x_other, 1 - core, start) for start in range(0, rows, TILE)]
     angle_tables(coarse, fine)
     logs.wait()
     decay_sums(log_decay, decay)
     key.wait()
-    others = []
-    for number in range(count):
+    for number, copy in enumerate(tiles):
         at = slice(number * TILE, (number + 1) * TILE)
-        tiles[number].wait()
-        if number == 0:
-            tiles += [tile(x_own, core, later) for later in range(1, count)]
-        else:
-            others += [tile(x_other, 1 - core, later) for later in range(count) if later % (count - 1) == number - 1]
-            if number == count - 1:
-                others.append(loads.start(wo_far, wo))
+        copy.wait()
         acc_k[at, :] = mm(x_own[at, :], wk[...])
         if number == 0:
             value.wait()
@@ -190,6 +182,8 @@
 
 def exchanges(ctx, hop):
     lower = range(ctx - hop)
+    if hop == 1:
+        return [], list(lower), []
     early = [at for at in lower if at < hop // 2]
     even = [at for at in lower if at >= hop // 2 and at // hop % 2 == 0]
     odd = [at for at in lower if at // hop % 2 == 1]
@@ -215,11 +209,11 @@
 
 
 def key_value_kernel(
-    heads, wq_far, wg_far, x, wk, wv, acc_k, acc_v, decay, coarse, fine,
-    wq, wg, k_out, v_out, before_out, state_out, message, arrived,
+    heads, wo_far, wq_far, wg_far, x, wk, wv, acc_k, acc_v, decay, coarse, fine,
+    wo, wq, wg, k_out, v_out, before_out, state_out, message, arrived,
 ):
     loads = Loads(arrived)
-    others = [loads.start(wq_far, wq), loads.start(wg_far, wg)]
+    others = [loads.start(wo_far, wo), loads.start(wq_far, wq), loads.start(wg_far, wg)]
     state_out[...] = jnp.zeros_like(state_out)
 
     def block_step(block, totals):
@@ -422,36 +416,37 @@
     key_far = swap(key_weight, "fsdp", 1)
     value_far = swap(value_weight, "fsdp", 1)
 
-    x_own, x_other, acc_k, acc_v, decay, coarse, fine, out_first = loading_call(
+    x_own, x_other, acc_k, acc_v, decay, coarse, fine = loading_call(
         key_value_own_kernel,
         [((rows, part), BF16)] * 2
         + [((rows, cols), F32)] * 2
         + [((8, rows), F32)]
-        + tables
-        + [(out_weight.shape, BF16)],
-        [x, key_weight, value_weight, log_decay[0].T, out_weight],
+        + tables,
+        [x, key_weight, value_weight, log_decay[0].T],
         [],
         [pltpu.VMEM((part, cols), BF16)] * 2 + [pltpu.VMEM((heads, rows), F32)],
-        2 * (rows // TILE) + 4,
+        2 * (rows // TILE) + 3,
         "key_value_own",
     )
     state_shape, message_shape = (heads * DH, DH), (heads * DH + EXTRA, DH)
-    own_q, own_g, keys, values, before, window, message = loading_call(
+    out_first, own_q, own_g, keys, values, before, window, message = loading_call(
         functools.partial(key_value_kernel, heads),
-        [((part, cols), BF16)] * 2
+        [(out_weight.shape, BF16)]
+        + [((part, cols), BF16)] * 2
         + [((rows, cols), BF16)] * 2
         + [((blocks, heads * DH, DH), BF16), (state_shape, F32), (message_shape, BF16)],
-        [query_weight, gate_weight],
+        [out_weight, query_weight, gate_weight],
         [x_other, key_far, value_far, acc_k, acc_v, decay, coarse, fine],
         [],
-        2,
+        3,
         "key_value",
     )
 
     def exchange(message, lowers, hop):
-        return lax.ppermute(
-            message, "ctx", [pair for at in lowers for pair in ((at, at + hop), (at + hop, at))]
-        )
+        pairs = [(at, at + hop) for at in lowers]
+        if hop > 1:
+            pairs += [(upper, at) for at, upper in pairs]
+        return lax.ppermute(message, "ctx", pairs)
 
     entering, hop, early, last_message = None, 1, [], message
     while True:
@@ -483,8 +478,10 @@
     near_first = swap(for_near, "tp", near_mask)
     high_first = swap(for_high, "tp", far_mask)
 
-    held, projected = after(decay, message), []
+    held, projected = after(decay, message, *early), []
     for block in range(blocks):
+        if block == blocks - 1 and early:
+            held = after(held, *early, high_first, near_first)
         projected += kernel_call(
             functools.partial(query_gate_kernel, heads, block),
             [((BLOCK, cols), BF16), ((BLOCK, cols), BF16), ((BLOCK, cols), F32)],
@@ -502,7 +499,7 @@
             [held, before, entering, *arrivals, *projected],
             "hidden",
         )
-        if number == 0:
+        if number == 1:
             near_second = swap(after(near_first, pair[0]), "fsdp", 1)
             high_second = swap(after(high_first, pair[0]), "fsdp", 1)
         for half in range(2):

time: 68.2 us -> 68.3 us (level)
  the two profiles are of different devices: /device:TPU:0 before, /device:TPU:18 now
where the time goes in v7:
time: 68.3 us; the launch traced here: 68 us
  waiting for transfers between devices  26.3 us (39%)
  Pallas kernels  24 us (35%)
  starting transfers between devices  17.5 us (26%)
    ppermute x17, waiting for transfers between devices, swap(): lax.ppermute(value, axis, [(place, place ^ mask) for place in range(size)])  17.3 us
    pallas_call x13, Pallas kernels, kernel_call(): pl.pallas_call(kernel, in_specs=[pl.BlockSpec(memory_space=pltpu.VMEM)] *...  15 us
    ppermute x17, starting transfers between devices, swap(): lax.ppermute(value, axis, [(place, place ^ mask) for place in range(size)])  10.9 us
    ppermute x3, waiting for transfers between devices, exchange(): return lax.ppermute(message, 'ctx', pairs)  9.02 us
    pallas_call x2, Pallas kernels, loading_call(): pl.pallas_call(kernel, in_specs=[pl.BlockSpec(memory_space=pltpu.HBM)] *...  7.88 us
    ppermute x3, starting transfers between devices, exchange(): return lax.ppermute(message, 'ctx', pairs)  6.58 us
  transfers between devices with their start and end apart: 20, of which 8 were waited for; matrix products, arithmetic and copies ran while one was open for 0% of the time, Pallas kernels for 26%

profile of v7, /device:TPU:18, one launch (start us, length us, event | category | flops | bytes accessed | tf_op | source)
XLA Modules:
  0.0 68.0 jit_solution(8453672232091282871)
XLA Ops:
  0.0 0.5 collective-permute-start.1
  0.5 4.5 %key_value_own.1 = (bf16[1024,1024]{1,0:T(8,128)(2,1)S(1)}, bf16[1024,1024]{1,0:T(8,128)(2,1)S(1)}, f32[1024,512]{1,0:T(8,128)S(1)}, f32[1024,512]{1,0:T(8,128)S...) custom-call(bf16[1024,2048]{1,0:T(8,128)(2,1)} %bitcast.4, ...), custom_call_target="tpu_custom_call" | custom-call | flops 1 | bytes 1 | tf_op jit(solution)/shard_map/key_value_own/pallas_call | solution.py:56
  5.0 3.4 %key_value.1 = (bf16[512,1024]{1,0:T(8,128)(2,1)S(1)}, bf16[1024,512]{1,0:T(8,128)(2,1)S(1)}, bf16[1024,512]{1,0:T(8,128)(2,1)S(1)}, bf16[1024,512]{1,0:T(8,128)...) custom-call(bf16[512,1024]{1,0:T(8,128)(2,1)} %wo_far.1, ...), custom_call_target="tpu_custom_call" | custom-call | flops 1 | bytes 1 | tf_op jit(solution)/shard_map/key_value/pallas_call | solution.py:56
  9.1 3.5 %collective-permute-start.3 = (bf16[528,256]{1,0:T(8,128)(2,1)S(1)}, bf16[528,256]{1,0:T(8,128)(2,1)S(1)}, u32[]{:S(2)}, u32[]{:S(2)}) collective-permute-start(bf16[528,256]{1,0:T(8,128)(2,1)S(1)} %get-tuple-element.54.sent), channel_id=1, source_target_pairs={{0,8},{8,16},{16,24},{1,9},{9,17},{17,25},{2,10},{10,18},{18,26},{... | collective-permute-start | bytes 811016 | tf_op jit(solution)/shard_map/ppermute | solution.py:449
  12.6 2.3 %collective-permute-start.5 = (bf16[528,256]{1,0:T(8,128)(2,1)S(1)}, bf16[528,256]{1,0:T(8,128)(2,1)S(1)}, u32[]{:S(2)}, u32[]{:S(2)}) collective-permute-start(bf16[528,256]{1,0:T(8,128)(2,1)S(1)} %get-tuple-element.54.sent), channel_id=1, source_target_pairs={{0,16},{16,0},{1,17},{17,1},{2,18},{18,2},{3,19},{19,3},{4,20},{20... | collective-permute-start | bytes 811016 | tf_op jit(solution)/shard_map/ppermute | solution.py:449
  15.0 1.6 %collective-permute-start.8 = (bf16[512,512]{1,0:T(8,128)(2,1)S(1)}, bf16[512,512]{1,0:T(8,128)(2,1)S(1)}, u32[]{:S(2)}, u32[]{:S(2)}) collective-permute-start(bf16[512,512]{1,0:T(8,128)(2,1)S(1)} %get-tuple-element.67), channel_id=1, source_target_pairs={{0,4},{2,6},{4,0},{6,2},{1,5},{3,7},{5,1},{7,3},{8,12},{10,14},{12... | collective-permute-start | bytes 1572872 | tf_op jit(solution)/shard_map/ppermute | solution.py:35
  16.6 9.0 %collective-permute-done.3.refs_0_ = bf16[528,256]{1,0:T(8,128)(2,1)S(1)} collective-permute-done((bf16[528,256]{1,0:T(8,128)(2,1)S(1)}, bf16[528,256]{1,0:T(8,128)(2,1)S(1)}, u32[]{:S(2)}, u32[]{:S(2)}) %collective-permute-start.3) | collective-permute-done | bytes 270368 | tf_op jit(solution)/shard_map/ppermute | solution.py:449
  25.6 0.5 collective-permute-start.9
  26.1 0.9 %combine.1 = (f32[512,256]{1,0:T(8,128)}, f32[520,256]{1,0:T(8,128)S(1)}, bf16[528,256]{1,0:T(8,128)(2,1)S(1)}) custom-call(f32[512,256]{1,0:T(8,128)S(1)} %get-tuple-element.53.state, bf16[528,256]{1,0:T(8,128)(2,1)S(1)} %get-tuple-element.54.sent, bf16[528,256]{1,0:T(8,128)(2,1)S(1)} %collective-permute-done.3.refs_0_), custom_call_target="tpu_custom_call" | custom-call | flops 1 | bytes 1 | tf_op jit(solution)/shard_map/combine/pallas_call | solution.py:40
  27.1 0.8 %collective-permute-start.4 = (bf16[528,256]{1,0:T(8,128)(2,1)S(1)}, bf16[528,256]{1,0:T(8,128)(2,1)S(1)}, u32[]{:S(2)}, u32[]{:S(2)}) collective-permute-start(bf16[528,256]{1,0:T(8,128)(2,1)S(1)} %get-tuple-element.56), channel_id=1, source_target_pairs={{8,24},{24,8},{9,25},{25,9},{10,26},{26,10},{11,27},{27,11},{12,28... | collective-permute-start | bytes 811016 | tf_op jit(solution)/shard_map/ppermute | solution.py:449
  28.0 3.5 %query_gate.2 = (bf16[512,512]{1,0:T(8,128)(2,1)S(1)}, bf16[512,512]{1,0:T(8,128)(2,1)S(1)}, f32[512,512]{1,0:T(8,128)S(1)}) custom-call(bf16[1024,1024]{1,0:T(8,128)(2,1)S(1)} %get-tuple-element.57.x_own, bf16[1024,1024]{1,0:T(8,128)(2,1)S(1)} %get-tuple-element.45.x.x_other, bf16[1024,512]{1,0:T(8,128)(2,1)S(1)} %get-tuple-element.58.wq, ...), custom_call_target="tpu_custom_call" | custom-call | flops 1 | bytes 1 | tf_op jit(solution)/shard_map/query_gate/pallas_call | solution.py:40
  31.5 3.3 %collective-permute-done.9.near_first = bf16[512,512]{1,0:T(8,128)(2,1)S(1)} collective-permute-done((bf16[512,512]{1,0:T(8,128)(2,1)S(1)}, bf16[512,512]{1,0:T(8,128)(2,1)S(1)}, u32[]{:S(2)}, u32[]{:S(2)}) %collective-permute-start.9) | collective-permute-done | bytes 524320 | tf_op jit(solution)/shard_map/ppermute | solution.py:35
  34.8 3.5 %query_gate.3 = (bf16[512,512]{1,0:T(8,128)(2,1)S(1)}, bf16[512,512]{1,0:T(8,128)(2,1)S(1)}, f32[512,512]{1,0:T(8,128)S(1)}) custom-call(bf16[1024,1024]{1,0:T(8,128)(2,1)S(1)} %get-tuple-element.57.x_own, bf16[1024,1024]{1,0:T(8,128)(2,1)S(1)} %get-tuple-element.45.x.x_other, bf16[1024,512]{1,0:T(8,128)(2,1)S(1)} %get-tuple-element.58.wq, ...), custom_call_target="tpu_custom_call" | custom-call | flops 1 | bytes 1 | tf_op jit(solution)/shard_map/query_gate/pallas_call | solution.py:40
  38.3 1.7 %hidden.2 = (bf16[256,512]{1,0:T(8,128)(2,1)S(1)}, bf16[256,512]{1,0:T(8,128)(2,1)S(1)}, bf16[16,128]{1,0:T(8,128)(2,1)}) custom-call(f32[8,1024]{1,0:T(8,128)S(1)} %get-tuple-element.69.decay, bf16[2,512,256]{2,1,0:T(8,128)(2,1)S(1)} %get-tuple-element.52.before, f32[520,256]{1,0:T(8,128)S(1)} %get-tuple-element.55.entering, ...), custom_call_target="tpu_custom_call" | custom-call | flops 1 | bytes 1 | tf_op jit(solution)/shard_map/hidden/pallas_call | solution.py:40
  40.0 0.5 collective-permute-start.12
  40.5 1.5 %collective-permute-start.10 = (bf16[256,512]{1,0:T(8,128)(2,1)S(1)}, bf16[256,512]{1,0:T(8,128)(2,1)S(1)}, u32[]{:S(2)}, u32[]{:S(2)}) collective-permute-start(bf16[256,512]{1,0:T(8,128)(2,1)S(1)} %get-tuple-element.73.refs_0_), channel_id=1, source_target_pairs={{0,4},{2,6},{4,0},{6,2},{1,5},{3,7},{5,1},{7,3},{8,12},{10,14},{12... | collective-permute-start | bytes 786440 | tf_op jit(solution)/shard_map/ppermute | solution.py:35
  42.1 0.5 collective-permute-start.14
  42.6 1.7 %hidden.3 = (bf16[256,512]{1,0:T(8,128)(2,1)S(1)}, bf16[256,512]{1,0:T(8,128)(2,1)S(1)}, bf16[16,128]{1,0:T(8,128)(2,1)}) custom-call(f32[8,1024]{1,0:T(8,128)S(1)} %get-tuple-element.69.decay, bf16[2,512,256]{2,1,0:T(8,128)(2,1)S(1)} %get-tuple-element.52.before, f32[520,256]{1,0:T(8,128)S(1)} %get-tuple-element.55.entering, ...), custom_call_target="tpu_custom_call" | custom-call | flops 1 | bytes 1 | tf_op jit(solution)/shard_map/hidden/pallas_call | solution.py:40
  44.8 1.5 %collective-permute-start.18 = (bf16[256,512]{1,0:T(8,128)(2,1)S(1)}, bf16[256,512]{1,0:T(8,128)(2,1)S(1)}, u32[]{:S(2)}, u32[]{:S(2)}) collective-permute-start(bf16[256,512]{1,0:T(8,128)(2,1)S(1)} %get-tuple-element.76.refs_3_), channel_id=1, source_target_pairs={{0,2},{2,0},{4,6},{6,4},{1,3},{3,1},{5,7},{7,5},{8,10},{10,8},{12,... | collective-permute-start | bytes 786440 | tf_op jit(solution)/shard_map/ppermute | solution.py:35
  46.3 1.3 %own_products.1 = (f32[512,1024]{1,0:T(8,128)S(1)}, f32[512,1024]{1,0:T(8,128)S(1)}) custom-call(bf16[512,1024]{1,0:T(8,128)(2,1)S(1)} %get-tuple-element.66.own_first, bf16[512,1024]{1,0:T(8,128)(2,1)S(1)} %collective-permute-done.2.own_second, bf16[256,512]{1,0:T(8,128)(2,1)S(1)} %get-tuple-element.73.refs_0_, ...), custom_call_target="tpu_custom_call" | custom-call | flops 1 | bytes 1 | tf_op jit(solution)/shard_map/own_products/pallas_call | solution.py:40
  47.9 1.8 %collective-permute-done.10.far.refs_0_ = bf16[256,512]{1,0:T(8,128)(2,1)S(1)} collective-permute-done((bf16[256,512]{1,0:T(8,128)(2,1)S(1)}, bf16[256,512]{1,0:T(8,128)(2,1)S(1)}, u32[]{:S(2)}, u32[]{:S(2)}) %collective-permute-start.10) | collective-permute-done | bytes 262176 | tf_op jit(solution)/shard_map/ppermute | solution.py:35
  50.0 0.6 collective-permute-start.13
  50.6 0.7 collective-permute-done.14.far.refs_1_
  51.6 0.9 %collective-permute-start.15 = (bf16[256,512]{1,0:T(8,128)(2,1)S(1)}, bf16[256,512]{1,0:T(8,128)(2,1)S(1)}, u32[]{:S(2)}, u32[]{:S(2)}) collective-permute-start(bf16[256,512]{1,0:T(8,128)(2,1)S(1)} %give.5), channel_id=1, source_target_pairs={{0,4},{2,6},{4,0},{6,2},{1,5},{3,7},{5,1},{7,3},{8,12},{10,14},{12... | collective-permute-start | bytes 786440 | tf_op jit(solution)/shard_map/ppermute | solution.py:35
  52.5 2.8 %collective-permute-done.16.far.refs_2_ = bf16[256,512]{1,0:T(8,128)(2,1)S(1)} collective-permute-done((bf16[256,512]{1,0:T(8,128)(2,1)S(1)}, bf16[256,512]{1,0:T(8,128)(2,1)S(1)}, u32[]{:S(2)}, u32[]{:S(2)}) %collective-permute-start.16) | collective-permute-done | bytes 262176 | tf_op jit(solution)/shard_map/ppermute | solution.py:35
  55.6 0.6 collective-permute-start.17
  56.2 0.7 collective-permute-done.18.far.refs_3_
  57.2 0.9 %collective-permute-start.19 = (bf16[256,512]{1,0:T(8,128)(2,1)S(1)}, bf16[256,512]{1,0:T(8,128)(2,1)S(1)}, u32[]{:S(2)}, u32[]{:S(2)}) collective-permute-start(bf16[256,512]{1,0:T(8,128)(2,1)S(1)} %give.7), channel_id=1, source_target_pairs={{0,4},{2,6},{4,0},{6,2},{1,5},{3,7},{5,1},{7,3},{8,12},{10,14},{12... | collective-permute-start | bytes 786440 | tf_op jit(solution)/shard_map/ppermute | solution.py:35
  58.1 0.7 %keep.1 = (f32[512,512]{1,0:T(8,128)S(1)}, f32[512,512]{1,0:T(8,128)S(1)}) custom-call(bf16[256,512]{1,0:T(8,128)(2,1)S(1)} %collective-permute-done.10.far.refs_0_, bf16[256,512]{1,0:T(8,128)(2,1)S(1)} %collective-permute-done.14.far.refs_1_, bf16[256,512]{1,0:T(8,128)(2,1)S(1)} %collective-permute-done.16.far.refs_2_, ...), custom_call_target="tpu_custom_call" | custom-call | flops 1 | bytes 1 | tf_op jit(solution)/shard_map/keep/pallas_call | solution.py:40
  58.8 3.7 %collective-permute-done.13.refs_0_ = bf16[256,512]{1,0:T(8,128)(2,1)S(1)} collective-permute-done((bf16[256,512]{1,0:T(8,128)(2,1)S(1)}, bf16[256,512]{1,0:T(8,128)(2,1)S(1)}, u32[]{:S(2)}, u32[]{:S(2)}) %collective-permute-start.13) | collective-permute-done | bytes 262176 | tf_op jit(solution)/shard_map/ppermute | solution.py:35
  62.5 4.3 %collective-permute-done.17.refs_2_ = bf16[256,512]{1,0:T(8,128)(2,1)S(1)} collective-permute-done((bf16[256,512]{1,0:T(8,128)(2,1)S(1)}, bf16[256,512]{1,0:T(8,128)(2,1)S(1)}, u32[]{:S(2)}, u32[]{:S(2)}) %collective-permute-start.17) | collective-permute-done | bytes 262176 | tf_op jit(solution)/shard_map/ppermute | solution.py:35
  66.9 1.1 %finish.1 = bf16[1,1024,512]{2,1,0:T(8,128)(2,1)} custom-call(bf16[256,512]{1,0:T(8,128)(2,1)S(1)} %collective-permute-done.13.refs_0_, bf16[256,512]{1,0:T(8,128)(2,1)S(1)} %collective-permute-done.15.refs_1_, bf16[256,512]{1,0:T(8,128)(2,1)S(1)} %collective-permute-done.17.refs_2_, bf16[256,512]{1,0:T(8,128)(2,1)S(1)} %collective-permute-done.19.refs_3_, ...), custom_call_target="tpu_custom_call" | custom-call | tf_op jit(solution)/shard_map/finish/pallas_call | solution.py:537
  (24 shorter events, 2.8 us)
Async XLA Ops:
  0.0 5.0 %collective-permute-start = (bf16[1024,512]{1,0:T(8,128)(2,1)}, bf16[1024,512]{1,0:T(8,128)(2,1)S(1)}, u32[]{:S(2)}, u32[]{:S(2)}) collective-permute-start(bf16[1024,512]{1,0:T(8,128)(2,1)} %wk_far.1), channel_id=1, source_target_pairs={{0,1},{1,0},{2,3},{3,2},{4,5},{5,4},{6,7},{7,6},{8,9},{9,8},{10,11... | collective-permute-start | bytes 3145736 | tf_op jit(solution)/shard_map/ppermute | solution.py:35
  0.0 5.0 %collective-permute-start.1 = (bf16[1024,512]{1,0:T(8,128)(2,1)}, bf16[1024,512]{1,0:T(8,128)(2,1)S(1)}, u32[]{:S(2)}, u32[]{:S(2)}) collective-permute-start(bf16[1024,512]{1,0:T(8,128)(2,1)} %wv_far.1), channel_id=1, source_target_pairs={{0,1},{1,0},{2,3},{3,2},{4,5},{5,4},{6,7},{7,6},{8,9},{9,8},{10,11... | collective-permute-start | bytes 3145736 | tf_op jit(solution)/shard_map/ppermute | solution.py:35
  8.4 6.4 %collective-permute-start.2 = (bf16[512,1024]{1,0:T(8,128)(2,1)S(1)}, bf16[512,1024]{1,0:T(8,128)(2,1)S(1)}, u32[]{:S(2)}, u32[]{:S(2)}) collective-permute-start(bf16[512,1024]{1,0:T(8,128)(2,1)S(1)} %get-tuple-element.66.own_first), channel_id=1, source_target_pairs={{0,1},{1,0},{2,3},{3,2},{4,5},{5,4},{6,7},{7,6},{8,9},{9,8},{10,11... | collective-permute-start | bytes 3145736 | tf_op jit(solution)/shard_map/ppermute | solution.py:35
  8.5 19.4 %collective-permute-start.6 = (bf16[1024,512]{1,0:T(8,128)(2,1)S(1)}, bf16[1024,512]{1,0:T(8,128)(2,1)S(1)}, u32[]{:S(2)}, u32[]{:S(2)}) collective-permute-start(bf16[1024,512]{1,0:T(8,128)(2,1)S(1)} %get-tuple-element.58.wq), channel_id=1, source_target_pairs={{0,1},{1,0},{2,3},{3,2},{4,5},{5,4},{6,7},{7,6},{8,9},{9,8},{10,11... | collective-permute-start | bytes 3145736 | tf_op jit(solution)/shard_map/ppermute | solution.py:35
  9.0 18.9 %collective-permute-start.7 = (bf16[1024,512]{1,0:T(8,128)(2,1)S(1)}, bf16[1024,512]{1,0:T(8,128)(2,1)S(1)}, u32[]{:S(2)}, u32[]{:S(2)}) collective-permute-start(bf16[1024,512]{1,0:T(8,128)(2,1)S(1)} %get-tuple-element.59.wg), channel_id=1, source_target_pairs={{0,1},{1,0},{2,3},{3,2},{4,5},{5,4},{6,7},{7,6},{8,9},{9,8},{10,11... | collective-permute-start | bytes 3145736 | tf_op jit(solution)/shard_map/ppermute | solution.py:35
  9.1 16.5 %collective-permute-start.3 = (bf16[528,256]{1,0:T(8,128)(2,1)S(1)}, bf16[528,256]{1,0:T(8,128)(2,1)S(1)}, u32[]{:S(2)}, u32[]{:S(2)}) collective-permute-start(bf16[528,256]{1,0:T(8,128)(2,1)S(1)} %get-tuple-element.54.sent), channel_id=1, source_target_pairs={{0,8},{8,16},{16,24},{1,9},{9,17},{17,25},{2,10},{10,18},{18,26},{... | collective-permute-start | bytes 811016 | tf_op jit(solution)/shard_map/ppermute | solution.py:449
  12.6 14.5 %collective-permute-start.5 = (bf16[528,256]{1,0:T(8,128)(2,1)S(1)}, bf16[528,256]{1,0:T(8,128)(2,1)S(1)}, u32[]{:S(2)}, u32[]{:S(2)}) collective-permute-start(bf16[528,256]{1,0:T(8,128)(2,1)S(1)} %get-tuple-element.54.sent), channel_id=1, source_target_pairs={{0,16},{16,0},{1,17},{17,1},{2,18},{18,2},{3,19},{19,3},{4,20},{20... | collective-permute-start | bytes 811016 | tf_op jit(solution)/shard_map/ppermute | solution.py:449
  15.0 16.5 %collective-permute-start.8 = (bf16[512,512]{1,0:T(8,128)(2,1)S(1)}, bf16[512,512]{1,0:T(8,128)(2,1)S(1)}, u32[]{:S(2)}, u32[]{:S(2)}) collective-permute-start(bf16[512,512]{1,0:T(8,128)(2,1)S(1)} %get-tuple-element.67), channel_id=1, source_target_pairs={{0,4},{2,6},{4,0},{6,2},{1,5},{3,7},{5,1},{7,3},{8,12},{10,14},{12... | collective-permute-start | bytes 1572872 | tf_op jit(solution)/shard_map/ppermute | solution.py:35
  25.6 9.2 %collective-permute-start.9 = (bf16[512,512]{1,0:T(8,128)(2,1)S(1)}, bf16[512,512]{1,0:T(8,128)(2,1)S(1)}, u32[]{:S(2)}, u32[]{:S(2)}) collective-permute-start(bf16[512,512]{1,0:T(8,128)(2,1)S(1)} %get-tuple-element.68), channel_id=1, source_target_pairs={{0,2},{2,0},{4,6},{6,4},{1,3},{3,1},{5,7},{7,5},{8,10},{10,8},{12,... | collective-permute-start | bytes 1572872 | tf_op jit(solution)/shard_map/ppermute | solution.py:35
  27.1 11.2 %collective-permute-start.4 = (bf16[528,256]{1,0:T(8,128)(2,1)S(1)}, bf16[528,256]{1,0:T(8,128)(2,1)S(1)}, u32[]{:S(2)}, u32[]{:S(2)}) collective-permute-start(bf16[528,256]{1,0:T(8,128)(2,1)S(1)} %get-tuple-element.56), channel_id=1, source_target_pairs={{8,24},{24,8},{9,25},{25,9},{10,26},{26,10},{11,27},{27,11},{12,28... | collective-permute-start | bytes 811016 | tf_op jit(solution)/shard_map/ppermute | solution.py:449
  40.0 4.8 %collective-permute-start.11 = (bf16[512,512]{1,0:T(8,128)(2,1)S(1)}, bf16[512,512]{1,0:T(8,128)(2,1)S(1)}, u32[]{:S(2)}, u32[]{:S(2)}) collective-permute-start(bf16[512,512]{1,0:T(8,128)(2,1)S(1)} %collective-permute-done.9.near_first), channel_id=1, source_target_pairs={{0,1},{1,0},{2,3},{3,2},{4,5},{5,4},{6,7},{7,6},{8,9},{9,8},{10,11... | collective-permute-start | bytes 1572872 | tf_op jit(solution)/shard_map/ppermute | solution.py:35
  40.0 7.6 %collective-permute-start.12 = (bf16[512,512]{1,0:T(8,128)(2,1)S(1)}, bf16[512,512]{1,0:T(8,128)(2,1)S(1)}, u32[]{:S(2)}, u32[]{:S(2)}) collective-permute-start(bf16[512,512]{1,0:T(8,128)(2,1)S(1)} %collective-permute-done.8.high_first), channel_id=1, source_target_pairs={{0,1},{1,0},{2,3},{3,2},{4,5},{5,4},{6,7},{7,6},{8,9},{9,8},{10,11... | collective-permute-start | bytes 1572872 | tf_op jit(solution)/shard_map/ppermute | solution.py:35
  40.5 9.2 %collective-permute-start.10 = (bf16[256,512]{1,0:T(8,128)(2,1)S(1)}, bf16[256,512]{1,0:T(8,128)(2,1)S(1)}, u32[]{:S(2)}, u32[]{:S(2)}) collective-permute-start(bf16[256,512]{1,0:T(8,128)(2,1)S(1)} %get-tuple-element.73.refs_0_), channel_id=1, source_target_pairs={{0,4},{2,6},{4,0},{6,2},{1,5},{3,7},{5,1},{7,3},{8,12},{10,14},{12... | collective-permute-start | bytes 786440 | tf_op jit(solution)/shard_map/ppermute | solution.py:35
  42.1 9.2 %collective-permute-start.14 = (bf16[256,512]{1,0:T(8,128)(2,1)S(1)}, bf16[256,512]{1,0:T(8,128)(2,1)S(1)}, u32[]{:S(2)}, u32[]{:S(2)}) collective-permute-start(bf16[256,512]{1,0:T(8,128)(2,1)S(1)} %get-tuple-element.74.refs_1_), channel_id=1, source_target_pairs={{0,2},{2,0},{4,6},{6,4},{1,3},{3,1},{5,7},{7,5},{8,10},{10,8},{12,... | collective-permute-start | bytes 786440 | tf_op jit(solution)/shard_map/ppermute | solution.py:35
  44.3 11.0 %collective-permute-start.16 = (bf16[256,512]{1,0:T(8,128)(2,1)S(1)}, bf16[256,512]{1,0:T(8,128)(2,1)S(1)}, u32[]{:S(2)}, u32[]{:S(2)}) collective-permute-start(bf16[256,512]{1,0:T(8,128)(2,1)S(1)} %get-tuple-element.75.refs_2_), channel_id=1, source_target_pairs={{0,4},{2,6},{4,0},{6,2},{1,5},{3,7},{5,1},{7,3},{8,12},{10,14},{12... | collective-permute-start | bytes 786440 | tf_op jit(solution)/shard_map/ppermute | solution.py:35
  44.8 12.1 %collective-permute-start.18 = (bf16[256,512]{1,0:T(8,128)(2,1)S(1)}, bf16[256,512]{1,0:T(8,128)(2,1)S(1)}, u32[]{:S(2)}, u32[]{:S(2)}) collective-permute-start(bf16[256,512]{1,0:T(8,128)(2,1)S(1)} %get-tuple-element.76.refs_3_), channel_id=1, source_target_pairs={{0,2},{2,0},{4,6},{6,4},{1,3},{3,1},{5,7},{7,5},{8,10},{10,8},{12,... | collective-permute-start | bytes 786440 | tf_op jit(solution)/shard_map/ppermute | solution.py:35
  50.0 12.5 %collective-permute-start.13 = (bf16[256,512]{1,0:T(8,128)(2,1)S(1)}, bf16[256,512]{1,0:T(8,128)(2,1)S(1)}, u32[]{:S(2)}, u32[]{:S(2)}) collective-permute-start(bf16[256,512]{1,0:T(8,128)(2,1)S(1)} %give.4), channel_id=1, source_target_pairs={{0,2},{2,0},{4,6},{6,4},{1,3},{3,1},{5,7},{7,5},{8,10},{10,8},{12,... | collective-permute-start | bytes 786440 | tf_op jit(solution)/shard_map/ppermute | solution.py:35
  51.6 10.9 %collective-permute-start.15 = (bf16[256,512]{1,0:T(8,128)(2,1)S(1)}, bf16[256,512]{1,0:T(8,128)(2,1)S(1)}, u32[]{:S(2)}, u32[]{:S(2)}) collective-permute-start(bf16[256,512]{1,0:T(8,128)(2,1)S(1)} %give.5), channel_id=1, source_target_pairs={{0,4},{2,6},{4,0},{6,2},{1,5},{3,7},{5,1},{7,3},{8,12},{10,14},{12... | collective-permute-start | bytes 786440 | tf_op jit(solution)/shard_map/ppermute | solution.py:35
  55.6 11.2 %collective-permute-start.17 = (bf16[256,512]{1,0:T(8,128)(2,1)S(1)}, bf16[256,512]{1,0:T(8,128)(2,1)S(1)}, u32[]{:S(2)}, u32[]{:S(2)}) collective-permute-start(bf16[256,512]{1,0:T(8,128)(2,1)S(1)} %give.6), channel_id=1, source_target_pairs={{0,2},{2,0},{4,6},{6,4},{1,3},{3,1},{5,7},{7,5},{8,10},{10,8},{12,... | collective-permute-start | bytes 786440 | tf_op jit(solution)/shard_map/ppermute | solution.py:35
  57.2 9.7 %collective-permute-start.19 = (bf16[256,512]{1,0:T(8,128)(2,1)S(1)}, bf16[256,512]{1,0:T(8,128)(2,1)S(1)}, u32[]{:S(2)}, u32[]{:S(2)}) collective-permute-start(bf16[256,512]{1,0:T(8,128)(2,1)S(1)} %give.7), channel_id=1, source_target_pairs={{0,4},{2,6},{4,0},{6,2},{1,5},{3,7},{5,1},{7,3},{8,12},{10,14},{12... | collective-permute-start | bytes 786440 | tf_op jit(solution)/shard_map/ppermute | solution.py:35

commit v8 on v7

--- a/solution.py
+++ b/solution.py
@@ -13,6 +13,7 @@
 TILE = 256
 FINE = 32
 EXTRA = 16
+IN_FLIGHT = 5
 VMEM_LIMIT = 14 * 1024 * 1024
 F32 = jnp.float32
 BF16 = jnp.bfloat16
@@ -131,7 +132,8 @@
 
 
 def key_value_own_kernel(
-    x_far, wk_far, wv_far, log_decay_far, x_own, x_other, acc_k, acc_v, decay, coarse, fine, wk, wv, log_decay, arrived
+    x_far, wk_far, wv_far, log_decay_far, wo_far,
+    x_own, x_other, acc_k, acc_v, decay, coarse, fine, wo, wk, wv, log_decay, arrived,
 ):
     rows, part = x_own.shape
     core = lax.axis_index("fsdp")
@@ -139,26 +141,43 @@
 
     def tile(x, half, start):
         columns = pl.ds(pl.multiple_of(half * part, part), part)
-        return loads.start(x_far.at[pl.ds(start, TILE), columns], x.at[pl.ds(start, TILE)])
-
-    logs = loads.start(log_decay_far, log_decay)
-    key, tiles = loads.start(wk_far, wk), [tile(x_own, core, 0)]
-    value = loads.start(wv_far, wv)
-    tiles += [tile(x_own, core, start) for start in range(TILE, rows, TILE)]
-    others = [tile(x_other, 1 - core, start) for start in range(0, rows, TILE)]
+        return functools.partial(loads.start, x_far.at[pl.ds(start, TILE), columns], x.at[pl.ds(start, TILE)])
+
+    starts = range(0, rows, TILE)
+    half = part // 2
+    queue = [functools.partial(loads.start, log_decay_far, log_decay)]
+    queue += [functools.partial(loads.start, wk_far.at[pl.ds(at, half)], wk.at[pl.ds(at, half)]) for at in (0, half)]
+    queue += [tile(x_own, core, start) for start in starts]
+    queue += [functools.partial(loads.start, wv_far.at[pl.ds(at, half)], wv.at[pl.ds(at, half)]) for at in (0, half)]
+    queue += [tile(x_other, 1 - core, start) for start in starts]
+    queue += [functools.partial(loads.start, wo_far, wo)]
+    flight, done = [], 0
+
+    def fill(limit):
+        while len(flight) < min(len(queue), done + limit):
+            flight.append(queue[len(flight)]())
+
+    def need(count):
+        nonlocal done
+        while done < count:
+            flight[done].wait()
+            done += 1
+            fill(IN_FLIGHT)
+
+    fill(IN_FLIGHT)
     angle_tables(coarse, fine)
-    logs.wait()
+    need(1)
     decay_sums(log_decay, decay)
-    key.wait()
-    for number, copy in enumerate(tiles):
-        at = slice(number * TILE, (number + 1) * TILE)
-        copy.wait()
+    for number, start in enumerate(starts):
+        need(4 + number)
+        at = slice(start, start + TILE)
         acc_k[at, :] = mm(x_own[at, :], wk[...])
-        if number == 0:
-            value.wait()
+    need(5 + len(starts))
+    for start in starts:
+        at = slice(start, start + TILE)
         acc_v[at, :] = mm(x_own[at, :], wv[...])
-    for copy in others:
-        copy.wait()
+        need(min(len(queue), done + 2))
+    need(len(queue))
 
 
 def pack_message(message, states, logs):
@@ -209,11 +228,12 @@
 
 
 def key_value_kernel(
-    heads, wo_far, wq_far, wg_far, x, wk, wv, acc_k, acc_v, decay, coarse, fine,
-    wo, wq, wg, k_out, v_out, before_out, state_out, message, arrived,
+    heads, wq_far, wg_far, x, wk, wv, acc_k, acc_v, decay, coarse, fine, wqg,
+    k_out, v_out, before_out, state_out, message, arrived,
 ):
     loads = Loads(arrived)
-    others = [loads.start(wo_far, wo), loads.start(wq_far, wq), loads.start(wg_far, wg)]
+    part = wk.shape[0]
+    others = [loads.start(far, wqg.at[pl.ds(at, part)]) for far, at in ((wq_far, 0), (wg_far, part))]
     state_out[...] = jnp.zeros_like(state_out)
 
     def block_step(block, totals):
@@ -278,8 +298,9 @@
 
 
 def query_gate_kernel(
-    heads, block, x_own, x_other, wq, wq_far, wg, wg_far, decay, coarse, fine, k, v, q_out, g_out, intra_out
+    heads, block, x_own, x_other, wqg, wqg_far, decay, coarse, fine, k, v, q_out, g_out, intra_out
 ):
+    part = x_own.shape[1]
     start = block * BLOCK
     lines = decay[:, start : start + BLOCK]
     columns = lines.T
@@ -289,8 +310,8 @@
         at = pl.ds(pl.multiple_of(piece * TILE, TILE), TILE)
         own, far = x_own[pl.ds(first, TILE), :], x_other[pl.ds(first, TILE), :]
         cosine, sine = angles(coarse, fine, first, TILE)
-        q_out[at, :] = turned(mm(own, wq[...]) + mm(far, wq_far[...]), cosine, sine)
-        g_out[at, :] = (mm(own, wg[...]) + mm(far, wg_far[...])).astype(BF16)
+        q_out[at, :] = turned(mm(own, wqg[:part, :]) + mm(far, wqg_far[:part, :]), cosine, sine)
+        g_out[at, :] = (mm(own, wqg[part:, :]) + mm(far, wqg_far[part:, :])).astype(BF16)
         return carry
 
     lax.fori_loop(0, BLOCK // TILE, project, 0)
@@ -333,25 +354,30 @@
             out[:, span] = (silu * center * lax.rsqrt(spread + 1e-5)).astype(BF16)
 
 
-def arrange_kernel(near_first, near_second, high_first, high_second, low_out, high_out):
-    cols = near_first.shape[1]
+def columns_kernel(first, second, out):
+    cols = out.shape[1] // 2
     place, core = lax.axis_index("tp"), lax.axis_index("fsdp")
     high, low = place // 2, place % 2
-    here = core == high
-    same = core == low
-    low_out[:, :cols] = jnp.where(here, near_second[...], near_first[...])
-    low_out[:, cols:] = jnp.where(here, near_first[...], near_second[...])
-    high_out[:, :cols] = jnp.where(same, high_second[...], high_first[...])
-    high_out[:, cols:] = jnp.where(same, high_first[...], high_second[...])
-
-
-def columns_kernel(own_first, own_second, near, high_out):
-    cols = near.shape[1]
+
+    @pl.when(core == 0)
+    def _():
+        at = pl.ds(pl.multiple_of((1 - low) * cols, cols), cols)
+        out[:, :cols] = first[:, at]
+        out[:, cols:] = second[:, at]
+
+    @pl.when(core == 1)
+    def _():
+        out[...] = jnp.where(high == 0, first[...], second[...])
+
+
+def arrange_kernel(mine, other, low_out, high_out):
+    cols = mine.shape[1] // 2
     place, core = lax.axis_index("tp"), lax.axis_index("fsdp")
-    high, low = place // 2, place % 2
-    near[...] = own_first[:, pl.ds(pl.multiple_of((1 - low) * cols, cols), cols)]
-    at = pl.ds(pl.multiple_of(core * cols, cols), cols)
-    high_out[...] = jnp.where(core == high, own_second[:, at], own_first[:, at])
+    for gathered, bit, out in ((core == 0, place // 2, low_out), (core == 1, place % 2, high_out)):
+        give = pl.ds(pl.multiple_of((1 - bit) * cols, cols), cols)
+        keep = pl.ds(pl.multiple_of(bit * cols, cols), cols)
+        out[:, :cols] = jnp.where(gathered, mine[:, give], other[:, give])
+        out[:, cols:] = jnp.where(gathered, mine[:, keep], other[:, keep])
 
 
 def own_kernel(order, own_first, own_second, *refs):
@@ -416,29 +442,29 @@
     key_far = swap(key_weight, "fsdp", 1)
     value_far = swap(value_weight, "fsdp", 1)
 
-    x_own, x_other, acc_k, acc_v, decay, coarse, fine = loading_call(
+    x_own, x_other, acc_k, acc_v, decay, coarse, fine, out_first = loading_call(
         key_value_own_kernel,
         [((rows, part), BF16)] * 2
         + [((rows, cols), F32)] * 2
         + [((8, rows), F32)]
-        + tables,
-        [x, key_weight, value_weight, log_decay[0].T],
+        + tables
+        + [(out_weight.shape, BF16)],
+        [x, key_weight, value_weight, log_decay[0].T, out_weight],
         [],
         [pltpu.VMEM((part, cols), BF16)] * 2 + [pltpu.VMEM((heads, rows), F32)],
-        2 * (rows // TILE) + 3,
+        2 * (rows // TILE) + 6,
         "key_value_own",
     )
     state_shape, message_shape = (heads * DH, DH), (heads * DH + EXTRA, DH)
-    out_first, own_q, own_g, keys, values, before, window, message = loading_call(
+    own_qg, keys, values, before, window, message = loading_call(
         functools.partial(key_value_kernel, heads),
-        [(out_weight.shape, BF16)]
-        + [((part, cols), BF16)] * 2
+        [((2 * part, cols), BF16)]
         + [((rows, cols), BF16)] * 2
         + [((blocks, heads * DH, DH), BF16), (state_shape, F32), (message_shape, BF16)],
-        [out_weight, query_weight, gate_weight],
+        [query_weight, gate_weight],
         [x_other, key_far, value_far, acc_k, acc_v, decay, coarse, fine],
         [],
-        3,
+        2,
         "key_value",
     )
 
@@ -448,7 +474,7 @@
             pairs += [(upper, at) for at, upper in pairs]
         return lax.ppermute(message, "ctx", pairs)
 
-    entering, hop, early, last_message = None, 1, [], message
+    entering, hop, early, message_sent = None, 1, [], message
     while True:
         first_set, *later_sets = exchanges(ctx, hop)
         later_sets = [lowers for lowers in later_sets if lowers]
@@ -467,25 +493,25 @@
         )
         hop *= 2
 
-    far_q, far_g = swap(own_q, "fsdp", 1), swap(own_g, "fsdp", 1)
+    far_qg = swap(own_qg, "fsdp", 1)
     own_second = swap(out_first, "fsdp", 1)
-    for_near, for_high = kernel_call(
+    [for_partner] = kernel_call(
         columns_kernel,
-        [((cols, cols), BF16)] * 2,
-        [after(out_first, last_message), own_second],
+        [(out_weight.shape, BF16)],
+        [out_first, own_second],
         "columns",
     )
-    near_first = swap(for_near, "tp", near_mask)
-    high_first = swap(for_high, "tp", far_mask)
-
-    held, projected = after(decay, message, *early), []
+    pairs = [(at * cores + at_core, (at ^ mask) * cores + at_core) for at in range(tp) for at_core, mask in enumerate((near_mask, far_mask))]
+    out_mine = lax.ppermute(for_partner, ("tp", "fsdp"), pairs)
+
+    held, projected = after(decay, message), []
     for block in range(blocks):
         if block == blocks - 1 and early:
-            held = after(held, *early, high_first, near_first)
+            held = after(held, *early, out_mine)
         projected += kernel_call(
             functools.partial(query_gate_kernel, heads, block),
             [((BLOCK, cols), BF16), ((BLOCK, cols), BF16), ((BLOCK, cols), F32)],
-            [x_own, x_other, own_q, far_q, own_g, far_g, held, coarse, fine, keys, values],
+            [x_own, x_other, own_qg, far_qg, held, coarse, fine, keys, values],
             "query_gate",
         )
     count = rows // 2 // TILE
@@ -500,15 +526,14 @@
             "hidden",
         )
         if number == 1:
-            near_second = swap(after(near_first, pair[0]), "fsdp", 1)
-            high_second = swap(after(high_first, pair[0]), "fsdp", 1)
+            out_other = swap(after(out_mine, pair[0]), "fsdp", 1)
         for half in range(2):
             hidden[half].append(pair[half])
             far[half].append(swap(pair[half], "tp", masks[half]))
     weights = kernel_call(
         arrange_kernel,
         [((cols, 2 * cols), BF16)] * 2,
-        [near_first, near_second, high_first, high_second],
+        [out_mine, out_other],
         "arrange",
     )
     order = [(half, number) for number in reversed(range(count)) for half in (1, 0)]

time: 68.3 us -> 65.1 us (0.953)
  waiting for transfers between devices: 26.3 us -> 24 us
  starting transfers between devices: 17.5 us -> 16 us
  Pallas kernels: 24 us -> 24.8 us
    ppermute x17 -> x13, waiting for transfers between devices: 17.3 us -> 12.9 us  [swap(): lax.ppermute(value, axis, [(place, place ^ mask) for place in range(size)])]
    ppermute x17 -> x13, starting transfers between devices: 10.9 us -> 8.82 us  [swap(): lax.ppermute(value, axis, [(place, place ^ mask) for place in range(size)])]
    ppermute x3, waiting for transfers between devices: 9.02 us -> 11.1 us  [exchange(): return lax.ppermute(message, 'ctx', pairs)]
    pallas_call x2, Pallas kernels: 7.88 us -> 8.65 us  [loading_call(): pl.pallas_call(kernel, in_specs=[pl.BlockSpec(memory_space=pltpu.HBM)] *...]
  transfers between devices with their start and end apart: 20 -> 17, of which waited for: 8 -> 5; matrix products, arithmetic and copies ran while one was open for 0% -> 0% of each run, Pallas kernels for 26% -> 34%
where the time goes in v8:
time: 65.1 us; the launch traced here: 64.9 us
  Pallas kernels  24.8 us (38%)
  waiting for transfers between devices  24 us (37%)
  starting transfers between devices  16 us (25%)
    pallas_call x13, Pallas kernels, kernel_call(): pl.pallas_call(kernel, in_specs=[pl.BlockSpec(memory_space=pltpu.VMEM)] *...  15 us
    ppermute x13, waiting for transfers between devices, swap(): lax.ppermute(value, axis, [(place, place ^ mask) for place in range(size)])  12.9 us
    ppermute x3, waiting for transfers between devices, exchange(): return lax.ppermute(message, 'ctx', pairs)  11.1 us
    ppermute x13, starting transfers between devices, swap(): lax.ppermute(value, axis, [(place, place ^ mask) for place in range(size)])  8.82 us
    pallas_call x2, Pallas kernels, loading_call(): pl.pallas_call(kernel, in_specs=[pl.BlockSpec(memory_space=pltpu.HBM)] *...  8.65 us
    ppermute x3, starting transfers between devices, exchange(): return lax.ppermute(message, 'ctx', pairs)  6.57 us
  transfers between devices with their start and end apart: 17, of which 5 were waited for; matrix products, arithmetic and copies ran while one was open for 0% of the time, Pallas kernels for 34%

profile of v8, /device:TPU:18, one launch (start us, length us, event | category | flops | bytes accessed | tf_op | source)
XLA Modules:
  0.0 64.9 jit_solution(17568053552238091527)
XLA Ops:
  0.0 0.5 collective-permute-start.2
  0.5 5.3 %key_value_own.1 = (bf16[1024,1024]{1,0:T(8,128)(2,1)S(1)}, bf16[1024,1024]{1,0:T(8,128)(2,1)S(1)}, f32[1024,512]{1,0:T(8,128)S(1)}, f32[1024,512]{1,0:T(8,128)S...) custom-call(bf16[1024,2048]{1,0:T(8,128)(2,1)} %bitcast.4, ...), custom_call_target="tpu_custom_call" | custom-call | flops 1 | bytes 1 | tf_op jit(solution)/shard_map/key_value_own/pallas_call | solution.py:57
  5.9 3.4 %key_value.1 = (bf16[2048,512]{1,0:T(8,128)(2,1)S(1)}, bf16[1024,512]{1,0:T(8,128)(2,1)S(1)}, bf16[1024,512]{1,0:T(8,128)(2,1)S(1)}, bf16[2,512,256]{2,1,0:T(8,1...) custom-call(bf16[1024,512]{1,0:T(8,128)(2,1)} %wq_far.1, bf16[1024,512]{1,0:T(8,128)(2,1)} %wg_far.1, ...), custom_call_target="tpu_custom_call" | custom-call | flops 1 | bytes 1 | tf_op jit(solution)/shard_map/key_value/pallas_call | solution.py:57
  9.3 0.5 collective-permute-start.6
  9.9 0.6 collective-permute-start.7
  10.5 3.5 %collective-permute-start.3 = (bf16[528,256]{1,0:T(8,128)(2,1)S(1)}, bf16[528,256]{1,0:T(8,128)(2,1)S(1)}, u32[]{:S(2)}, u32[]{:S(2)}) collective-permute-start(bf16[528,256]{1,0:T(8,128)(2,1)S(1)} %get-tuple-element.49.sent), channel_id=1, source_target_pairs={{0,8},{8,16},{16,24},{1,9},{9,17},{17,25},{2,10},{10,18},{18,26},{... | collective-permute-start | bytes 811016 | tf_op jit(solution)/shard_map/ppermute | solution.py:475
  14.0 2.2 %collective-permute-start.5 = (bf16[528,256]{1,0:T(8,128)(2,1)S(1)}, bf16[528,256]{1,0:T(8,128)(2,1)S(1)}, u32[]{:S(2)}, u32[]{:S(2)}) collective-permute-start(bf16[528,256]{1,0:T(8,128)(2,1)S(1)} %get-tuple-element.49.sent), channel_id=1, source_target_pairs={{0,16},{16,0},{1,17},{17,1},{2,18},{18,2},{3,19},{19,3},{4,20},{20... | collective-permute-start | bytes 811016 | tf_op jit(solution)/shard_map/ppermute | solution.py:475
  16.2 11.1 %collective-permute-done.3.refs_0_ = bf16[528,256]{1,0:T(8,128)(2,1)S(1)} collective-permute-done((bf16[528,256]{1,0:T(8,128)(2,1)S(1)}, bf16[528,256]{1,0:T(8,128)(2,1)S(1)}, u32[]{:S(2)}, u32[]{:S(2)}) %collective-permute-start.3) | collective-permute-done | bytes 270368 | tf_op jit(solution)/shard_map/ppermute | solution.py:475
  27.3 0.9 %combine.1 = (f32[512,256]{1,0:T(8,128)}, f32[520,256]{1,0:T(8,128)S(1)}, bf16[528,256]{1,0:T(8,128)(2,1)S(1)}) custom-call(f32[512,256]{1,0:T(8,128)S(1)} %get-tuple-element.48.state, bf16[528,256]{1,0:T(8,128)(2,1)S(1)} %get-tuple-element.49.sent, bf16[528,256]{1,0:T(8,128)(2,1)S(1)} %collective-permute-done.3.refs_0_), custom_call_target="tpu_custom_call" | custom-call | flops 1 | bytes 1 | tf_op jit(solution)/shard_map/combine/pallas_call | solution.py:41
  28.3 0.8 %collective-permute-start.4 = (bf16[528,256]{1,0:T(8,128)(2,1)S(1)}, bf16[528,256]{1,0:T(8,128)(2,1)S(1)}, u32[]{:S(2)}, u32[]{:S(2)}) collective-permute-start(bf16[528,256]{1,0:T(8,128)(2,1)S(1)} %get-tuple-element.51), channel_id=1, source_target_pairs={{8,24},{24,8},{9,25},{25,9},{10,26},{26,10},{11,27},{27,11},{12,28... | collective-permute-start | bytes 811016 | tf_op jit(solution)/shard_map/ppermute | solution.py:475
  29.2 3.5 %query_gate.2 = (bf16[512,512]{1,0:T(8,128)(2,1)S(1)}, bf16[512,512]{1,0:T(8,128)(2,1)S(1)}, f32[512,512]{1,0:T(8,128)S(1)}) custom-call(bf16[1024,1024]{1,0:T(8,128)(2,1)S(1)} %get-tuple-element.52.x_own, bf16[1024,1024]{1,0:T(8,128)(2,1)S(1)} %get-tuple-element.42.x.x_other, bf16[2048,512]{1,0:T(8,128)(2,1)S(1)} %get-tuple-element.53.wqg, ...), custom_call_target="tpu_custom_call" | custom-call | flops 1 | bytes 1 | tf_op jit(solution)/shard_map/query_gate/pallas_call | solution.py:41
  32.7 3.5 %query_gate.3 = (bf16[512,512]{1,0:T(8,128)(2,1)S(1)}, bf16[512,512]{1,0:T(8,128)(2,1)S(1)}, f32[512,512]{1,0:T(8,128)S(1)}) custom-call(bf16[1024,1024]{1,0:T(8,128)(2,1)S(1)} %get-tuple-element.52.x_own, bf16[1024,1024]{1,0:T(8,128)(2,1)S(1)} %get-tuple-element.42.x.x_other, bf16[2048,512]{1,0:T(8,128)(2,1)S(1)} %get-tuple-element.53.wqg, ...), custom_call_target="tpu_custom_call" | custom-call | flops 1 | bytes 1 | tf_op jit(solution)/shard_map/query_gate/pallas_call | solution.py:41
  36.2 1.7 %hidden.2 = (bf16[256,512]{1,0:T(8,128)(2,1)S(1)}, bf16[256,512]{1,0:T(8,128)(2,1)S(1)}, bf16[16,128]{1,0:T(8,128)(2,1)}) custom-call(f32[8,1024]{1,0:T(8,128)S(1)} %get-tuple-element.60.decay, bf16[2,512,256]{2,1,0:T(8,128)(2,1)S(1)} %get-tuple-element.47.before, f32[520,256]{1,0:T(8,128)S(1)} %get-tuple-element.50.entering, ...), custom_call_target="tpu_custom_call" | custom-call | flops 1 | bytes 1 | tf_op jit(solution)/shard_map/hidden/pallas_call | solution.py:41
  37.9 0.5 collective-permute-start.8
  38.4 0.5 collective-permute-start.11
  39.0 1.7 %hidden.3 = (bf16[256,512]{1,0:T(8,128)(2,1)S(1)}, bf16[256,512]{1,0:T(8,128)(2,1)S(1)}, bf16[16,128]{1,0:T(8,128)(2,1)}) custom-call(f32[8,1024]{1,0:T(8,128)S(1)} %get-tuple-element.60.decay, bf16[2,512,256]{2,1,0:T(8,128)(2,1)S(1)} %get-tuple-element.47.before, f32[520,256]{1,0:T(8,128)S(1)} %get-tuple-element.50.entering, ...), custom_call_target="tpu_custom_call" | custom-call | flops 1 | bytes 1 | tf_op jit(solution)/shard_map/hidden/pallas_call | solution.py:41
  40.7 1.5 %collective-permute-start.13 = (bf16[256,512]{1,0:T(8,128)(2,1)S(1)}, bf16[256,512]{1,0:T(8,128)(2,1)S(1)}, u32[]{:S(2)}, u32[]{:S(2)}) collective-permute-start(bf16[256,512]{1,0:T(8,128)(2,1)S(1)} %get-tuple-element.66.refs_2_), channel_id=1, source_target_pairs={{0,4},{2,6},{4,0},{6,2},{1,5},{3,7},{5,1},{7,3},{8,12},{10,14},{12... | collective-permute-start | bytes 786440 | tf_op jit(solution)/shard_map/ppermute | solution.py:36
  42.2 1.5 %collective-permute-start.15 = (bf16[256,512]{1,0:T(8,128)(2,1)S(1)}, bf16[256,512]{1,0:T(8,128)(2,1)S(1)}, u32[]{:S(2)}, u32[]{:S(2)}) collective-permute-start(bf16[256,512]{1,0:T(8,128)(2,1)S(1)} %get-tuple-element.67.refs_3_), channel_id=1, source_target_pairs={{0,2},{2,0},{4,6},{6,4},{1,3},{3,1},{5,7},{7,5},{8,10},{10,8},{12,... | collective-permute-start | bytes 786440 | tf_op jit(solution)/shard_map/ppermute | solution.py:36
  43.7 1.3 %own_products.1 = (f32[512,1024]{1,0:T(8,128)S(1)}, f32[512,1024]{1,0:T(8,128)S(1)}) custom-call(bf16[512,1024]{1,0:T(8,128)(2,1)S(1)} %get-tuple-element.40.first.own_first, bf16[512,1024]{1,0:T(8,128)(2,1)S(1)} %collective-permute-done.second.own_second, bf16[256,512]{1,0:T(8,128)(2,1)S(1)} %get-tuple-element.64.refs_0_, ...), custom_call_target="tpu_custom_call" | custom-call | flops 1 | bytes 1 | tf_op jit(solution)/shard_map/own_products/pallas_call | solution.py:41
  45.3 1.7 %collective-permute-done.8.far.refs_0_ = bf16[256,512]{1,0:T(8,128)(2,1)S(1)} collective-permute-done((bf16[256,512]{1,0:T(8,128)(2,1)S(1)}, bf16[256,512]{1,0:T(8,128)(2,1)S(1)}, u32[]{:S(2)}, u32[]{:S(2)}) %collective-permute-start.8) | collective-permute-done | bytes 262176 | tf_op jit(solution)/shard_map/ppermute | solution.py:36
  47.0 0.3 give.4
  47.3 0.6 collective-permute-start.10
  47.9 0.3 give.5
  48.2 1.2 %collective-permute-start.12 = (bf16[256,512]{1,0:T(8,128)(2,1)S(1)}, bf16[256,512]{1,0:T(8,128)(2,1)S(1)}, u32[]{:S(2)}, u32[]{:S(2)}) collective-permute-start(bf16[256,512]{1,0:T(8,128)(2,1)S(1)} %give.5), channel_id=1, source_target_pairs={{0,4},{2,6},{4,0},{6,2},{1,5},{3,7},{5,1},{7,3},{8,12},{10,14},{12... | collective-permute-start | bytes 786440 | tf_op jit(solution)/shard_map/ppermute | solution.py:36
  49.5 3.2 %collective-permute-done.13.far.refs_2_ = bf16[256,512]{1,0:T(8,128)(2,1)S(1)} collective-permute-done((bf16[256,512]{1,0:T(8,128)(2,1)S(1)}, bf16[256,512]{1,0:T(8,128)(2,1)S(1)}, u32[]{:S(2)}, u32[]{:S(2)}) %collective-permute-start.13) | collective-permute-done | bytes 262176 | tf_op jit(solution)/shard_map/ppermute | solution.py:36
  53.0 0.6 collective-permute-start.14
  53.6 0.3 give.7
  53.9 1.2 %collective-permute-start.16 = (bf16[256,512]{1,0:T(8,128)(2,1)S(1)}, bf16[256,512]{1,0:T(8,128)(2,1)S(1)}, u32[]{:S(2)}, u32[]{:S(2)}) collective-permute-start(bf16[256,512]{1,0:T(8,128)(2,1)S(1)} %give.7), channel_id=1, source_target_pairs={{0,4},{2,6},{4,0},{6,2},{1,5},{3,7},{5,1},{7,3},{8,12},{10,14},{12... | collective-permute-start | bytes 786440 | tf_op jit(solution)/shard_map/ppermute | solution.py:36
  55.1 0.7 %keep.1 = (f32[512,512]{1,0:T(8,128)S(1)}, f32[512,512]{1,0:T(8,128)S(1)}) custom-call(bf16[256,512]{1,0:T(8,128)(2,1)S(1)} %collective-permute-done.8.far.refs_0_, bf16[256,512]{1,0:T(8,128)(2,1)S(1)} %collective-permute-done.11.far.refs_1_, bf16[256,512]{1,0:T(8,128)(2,1)S(1)} %collective-permute-done.13.far.refs_2_, ...), custom_call_target="tpu_custom_call" | custom-call | flops 1 | bytes 1 | tf_op jit(solution)/shard_map/keep/pallas_call | solution.py:41
  55.8 3.0 %collective-permute-done.10.refs_0_ = bf16[256,512]{1,0:T(8,128)(2,1)S(1)} collective-permute-done((bf16[256,512]{1,0:T(8,128)(2,1)S(1)}, bf16[256,512]{1,0:T(8,128)(2,1)S(1)}, u32[]{:S(2)}, u32[]{:S(2)}) %collective-permute-start.10) | collective-permute-done | bytes 262176 | tf_op jit(solution)/shard_map/ppermute | solution.py:36
  58.8 4.9 %collective-permute-done.14.refs_2_ = bf16[256,512]{1,0:T(8,128)(2,1)S(1)} collective-permute-done((bf16[256,512]{1,0:T(8,128)(2,1)S(1)}, bf16[256,512]{1,0:T(8,128)(2,1)S(1)}, u32[]{:S(2)}, u32[]{:S(2)}) %collective-permute-start.14) | collective-permute-done | bytes 262176 | tf_op jit(solution)/shard_map/ppermute | solution.py:36
  63.7 1.1 %finish.1 = bf16[1,1024,512]{2,1,0:T(8,128)(2,1)} custom-call(bf16[256,512]{1,0:T(8,128)(2,1)S(1)} %collective-permute-done.10.refs_0_, bf16[256,512]{1,0:T(8,128)(2,1)S(1)} %collective-permute-done.12.refs_1_, bf16[256,512]{1,0:T(8,128)(2,1)S(1)} %collective-permute-done.14.refs_2_, bf16[256,512]{1,0:T(8,128)(2,1)S(1)} %collective-permute-done.16.refs_3_, ...), custom_call_target="tpu_custom_call" | custom-call | tf_op jit(solution)/shard_map/finish/pallas_call | solution.py:562
  (18 shorter events, 0.8 us)
Async XLA Ops:
  0.0 5.9 %collective-permute-start.1 = (bf16[1024,512]{1,0:T(8,128)(2,1)}, bf16[1024,512]{1,0:T(8,128)(2,1)S(1)}, u32[]{:S(2)}, u32[]{:S(2)}) collective-permute-start(bf16[1024,512]{1,0:T(8,128)(2,1)} %wk_far.1), channel_id=1, source_target_pairs={{0,1},{1,0},{2,3},{3,2},{4,5},{5,4},{6,7},{7,6},{8,9},{9,8},{10,11... | collective-permute-start | bytes 3145736 | tf_op jit(solution)/shard_map/ppermute | solution.py:36
  0.0 5.9 %collective-permute-start.2 = (bf16[1024,512]{1,0:T(8,128)(2,1)}, bf16[1024,512]{1,0:T(8,128)(2,1)S(1)}, u32[]{:S(2)}, u32[]{:S(2)}) collective-permute-start(bf16[1024,512]{1,0:T(8,128)(2,1)} %wv_far.1), channel_id=1, source_target_pairs={{0,1},{1,0},{2,3},{3,2},{4,5},{5,4},{6,7},{7,6},{8,9},{9,8},{10,11... | collective-permute-start | bytes 3145736 | tf_op jit(solution)/shard_map/ppermute | solution.py:36
  5.8 4.0 %collective-permute-start = (bf16[512,1024]{1,0:T(8,128)(2,1)S(1)}, bf16[512,1024]{1,0:T(8,128)(2,1)S(1)}, u32[]{:S(2)}, u32[]{:S(2)}) collective-permute-start(bf16[512,1024]{1,0:T(8,128)(2,1)S(1)} %get-tuple-element.40.first.own_first), channel_id=1, source_target_pairs={{0,1},{1,0},{2,3},{3,2},{4,5},{5,4},{6,7},{7,6},{8,9},{9,8},{10,11... | collective-permute-start | bytes 3145736 | tf_op jit(solution)/shard_map/ppermute | solution.py:36
  9.3 19.9 %collective-permute-start.6 = (bf16[2048,512]{1,0:T(8,128)(2,1)S(1)}, bf16[2048,512]{1,0:T(8,128)(2,1)S(1)}, u32[]{:S(2)}, u32[]{:S(2)}) collective-permute-start(bf16[2048,512]{1,0:T(8,128)(2,1)S(1)} %get-tuple-element.53.wqg), channel_id=1, source_target_pairs={{0,1},{1,0},{2,3},{3,2},{4,5},{5,4},{6,7},{7,6},{8,9},{9,8},{10,11... | collective-permute-start | bytes 6291464 | tf_op jit(solution)/shard_map/ppermute | solution.py:36
  9.9 19.2 %collective-permute-start.7 = (bf16[512,1024]{1,0:T(8,128)(2,1)S(1)}, bf16[512,1024]{1,0:T(8,128)(2,1)S(1)}, u32[]{:S(2)}, u32[]{:S(2)}) collective-permute-start(bf16[512,1024]{1,0:T(8,128)(2,1)S(1)} %columns.1), channel_id=1, source_target_pairs={{0,2},{1,5},{2,0},{3,7},{4,6},{5,1},{6,4},{7,3},{8,10},{9,13},{10,... | collective-permute-start | bytes 3145736 | tf_op jit(solution)/shard_map/ppermute | solution.py:505
  10.5 16.8 %collective-permute-start.3 = (bf16[528,256]{1,0:T(8,128)(2,1)S(1)}, bf16[528,256]{1,0:T(8,128)(2,1)S(1)}, u32[]{:S(2)}, u32[]{:S(2)}) collective-permute-start(bf16[528,256]{1,0:T(8,128)(2,1)S(1)} %get-tuple-element.49.sent), channel_id=1, source_target_pairs={{0,8},{8,16},{16,24},{1,9},{9,17},{17,25},{2,10},{10,18},{18,26},{... | collective-permute-start | bytes 811016 | tf_op jit(solution)/shard_map/ppermute | solution.py:475
  14.0 15.2 %collective-permute-start.5 = (bf16[528,256]{1,0:T(8,128)(2,1)S(1)}, bf16[528,256]{1,0:T(8,128)(2,1)S(1)}, u32[]{:S(2)}, u32[]{:S(2)}) collective-permute-start(bf16[528,256]{1,0:T(8,128)(2,1)S(1)} %get-tuple-element.49.sent), channel_id=1, source_target_pairs={{0,16},{16,0},{1,17},{17,1},{2,18},{18,2},{3,19},{19,3},{4,20},{20... | collective-permute-start | bytes 811016 | tf_op jit(solution)/shard_map/ppermute | solution.py:475
  28.3 7.9 %collective-permute-start.4 = (bf16[528,256]{1,0:T(8,128)(2,1)S(1)}, bf16[528,256]{1,0:T(8,128)(2,1)S(1)}, u32[]{:S(2)}, u32[]{:S(2)}) collective-permute-start(bf16[528,256]{1,0:T(8,128)(2,1)S(1)} %get-tuple-element.51), channel_id=1, source_target_pairs={{8,24},{24,8},{9,25},{25,9},{10,26},{26,10},{11,27},{27,11},{12,28... | collective-permute-start | bytes 811016 | tf_op jit(solution)/shard_map/ppermute | solution.py:475
  37.9 7.1 %collective-permute-start.9 = (bf16[512,1024]{1,0:T(8,128)(2,1)S(1)}, bf16[512,1024]{1,0:T(8,128)(2,1)S(1)}, u32[]{:S(2)}, u32[]{:S(2)}) collective-permute-start(bf16[512,1024]{1,0:T(8,128)(2,1)S(1)} %collective-permute-done.7.mine), channel_id=1, source_target_pairs={{0,1},{1,0},{2,3},{3,2},{4,5},{5,4},{6,7},{7,6},{8,9},{9,8},{10,11... | collective-permute-start | bytes 3145736 | tf_op jit(solution)/shard_map/ppermute | solution.py:36
  37.9 9.1 %collective-permute-start.8 = (bf16[256,512]{1,0:T(8,128)(2,1)S(1)}, bf16[256,512]{1,0:T(8,128)(2,1)S(1)}, u32[]{:S(2)}, u32[]{:S(2)}) collective-permute-start(bf16[256,512]{1,0:T(8,128)(2,1)S(1)} %get-tuple-element.64.refs_0_), channel_id=1, source_target_pairs={{0,4},{2,6},{4,0},{6,2},{1,5},{3,7},{5,1},{7,3},{8,12},{10,14},{12... | collective-permute-start | bytes 786440 | tf_op jit(solution)/shard_map/ppermute | solution.py:36
  38.4 9.5 %collective-permute-start.11 = (bf16[256,512]{1,0:T(8,128)(2,1)S(1)}, bf16[256,512]{1,0:T(8,128)(2,1)S(1)}, u32[]{:S(2)}, u32[]{:S(2)}) collective-permute-start(bf16[256,512]{1,0:T(8,128)(2,1)S(1)} %get-tuple-element.65.refs_1_), channel_id=1, source_target_pairs={{0,2},{2,0},{4,6},{6,4},{1,3},{3,1},{5,7},{7,5},{8,10},{10,8},{12,... | collective-permute-start | bytes 786440 | tf_op jit(solution)/shard_map/ppermute | solution.py:36
  40.7 11.9 %collective-permute-start.13 = (bf16[256,512]{1,0:T(8,128)(2,1)S(1)}, bf16[256,512]{1,0:T(8,128)(2,1)S(1)}, u32[]{:S(2)}, u32[]{:S(2)}) collective-permute-start(bf16[256,512]{1,0:T(8,128)(2,1)S(1)} %get-tuple-element.66.refs_2_), channel_id=1, source_target_pairs={{0,4},{2,6},{4,0},{6,2},{1,5},{3,7},{5,1},{7,3},{8,12},{10,14},{12... | collective-permute-start | bytes 786440 | tf_op jit(solution)/shard_map/ppermute | solution.py:36
  42.2 11.3 %collective-permute-start.15 = (bf16[256,512]{1,0:T(8,128)(2,1)S(1)}, bf16[256,512]{1,0:T(8,128)(2,1)S(1)}, u32[]{:S(2)}, u32[]{:S(2)}) collective-permute-start(bf16[256,512]{1,0:T(8,128)(2,1)S(1)} %get-tuple-element.67.refs_3_), channel_id=1, source_target_pairs={{0,2},{2,0},{4,6},{6,4},{1,3},{3,1},{5,7},{7,5},{8,10},{10,8},{12,... | collective-permute-start | bytes 786440 | tf_op jit(solution)/shard_map/ppermute | solution.py:36
  47.3 11.5 %collective-permute-start.10 = (bf16[256,512]{1,0:T(8,128)(2,1)S(1)}, bf16[256,512]{1,0:T(8,128)(2,1)S(1)}, u32[]{:S(2)}, u32[]{:S(2)}) collective-permute-start(bf16[256,512]{1,0:T(8,128)(2,1)S(1)} %give.4), channel_id=1, source_target_pairs={{0,2},{2,0},{4,6},{6,4},{1,3},{3,1},{5,7},{7,5},{8,10},{10,8},{12,... | collective-permute-start | bytes 786440 | tf_op jit(solution)/shard_map/ppermute | solution.py:36
  48.2 10.6 %collective-permute-start.12 = (bf16[256,512]{1,0:T(8,128)(2,1)S(1)}, bf16[256,512]{1,0:T(8,128)(2,1)S(1)}, u32[]{:S(2)}, u32[]{:S(2)}) collective-permute-start(bf16[256,512]{1,0:T(8,128)(2,1)S(1)} %give.5), channel_id=1, source_target_pairs={{0,4},{2,6},{4,0},{6,2},{1,5},{3,7},{5,1},{7,3},{8,12},{10,14},{12... | collective-permute-start | bytes 786440 | tf_op jit(solution)/shard_map/ppermute | solution.py:36
  53.0 10.8 %collective-permute-start.14 = (bf16[256,512]{1,0:T(8,128)(2,1)S(1)}, bf16[256,512]{1,0:T(8,128)(2,1)S(1)}, u32[]{:S(2)}, u32[]{:S(2)}) collective-permute-start(bf16[256,512]{1,0:T(8,128)(2,1)S(1)} %give.6), channel_id=1, source_target_pairs={{0,2},{2,0},{4,6},{6,4},{1,3},{3,1},{5,7},{7,5},{8,10},{10,8},{12,... | collective-permute-start | bytes 786440 | tf_op jit(solution)/shard_map/ppermute | solution.py:36
  53.9 9.9 %collective-permute-start.16 = (bf16[256,512]{1,0:T(8,128)(2,1)S(1)}, bf16[256,512]{1,0:T(8,128)(2,1)S(1)}, u32[]{:S(2)}, u32[]{:S(2)}) collective-permute-start(bf16[256,512]{1,0:T(8,128)(2,1)S(1)} %give.7), channel_id=1, source_target_pairs={{0,4},{2,6},{4,0},{6,2},{1,5},{3,7},{5,1},{7,3},{8,12},{10,14},{12... | collective-permute-start | bytes 786440 | tf_op jit(solution)/shard_map/ppermute | solution.py:36

commit v9 on v8

--- a/solution.py
+++ b/solution.py
@@ -13,7 +13,6 @@
 TILE = 256
 FINE = 32
 EXTRA = 16
-IN_FLIGHT = 5
 VMEM_LIMIT = 14 * 1024 * 1024
 F32 = jnp.float32
 BF16 = jnp.bfloat16
@@ -105,19 +104,33 @@
         decay[:, start : start + BLOCK] = sums[:8] + sums[8:16] + sums[16:]
 
 
+def turn(first, second):
+    (cos_a, sin_a), (cos_b, sin_b) = first, second
+    return cos_a * cos_b - sin_a * sin_b, sin_a * cos_b + cos_a * sin_b
+
+
+def joined(first, second):
+    return tuple(jnp.concatenate(pair, axis=0) for pair in zip(first, second))
+
+
 def angle_tables(coarse, fine):
-    half = DH // 2
-
-    def fill(table, start, stride):
-        count = table.shape[1]
-        place = lax.broadcasted_iota(jnp.int32, (count, half), 0) * stride + start
-        index = lax.broadcasted_iota(jnp.int32, (count, half), 1).astype(F32)
-        angle = place.astype(F32) * jnp.exp(index * (-math.log(10000.0) / half))
-        table[0] = jnp.cos(angle)
-        table[1] = jnp.sin(angle)
-
-    fill(coarse, lax.axis_index("ctx") * coarse.shape[1] * FINE, FINE)
-    fill(fine, 0, 1)
+    half, seeds = DH // 2, 8
+    index = lax.broadcasted_iota(jnp.int32, (seeds, half), 1).astype(F32)
+    frequency = jnp.exp(index * (-math.log(10000.0) / half))
+    place = lax.broadcasted_iota(jnp.int32, (seeds, half), 0).astype(F32)
+    offset = (lax.axis_index("ctx") * (coarse.shape[1] * FINE)).astype(F32)
+    near = jnp.cos(place * frequency), jnp.sin(place * frequency)
+    base = jnp.cos(offset * frequency), jnp.sin(offset * frequency)
+    step = turn([part[seeds - 1 : seeds] for part in near], [part[1:2] for part in near])
+    while near[0].shape[0] < FINE:
+        near = joined(near, turn(near, step))
+        step = turn(step, step)
+    far = tuple(part[:1] for part in base)
+    while far[0].shape[0] < coarse.shape[1]:
+        far = joined(far, turn(far, step))
+        step = turn(step, step)
+    for table, parts in ((coarse, far), (fine, near)):
+        table[0], table[1] = (part[: table.shape[1]] for part in parts)
 
 
 class Loads:
@@ -132,8 +145,8 @@
 
 
 def key_value_own_kernel(
-    x_far, wk_far, wv_far, log_decay_far, wo_far,
-    x_own, x_other, acc_k, acc_v, decay, coarse, fine, wo, wk, wv, log_decay, arrived,
+    x_far, wk_far, wv_far, log_decay_far, wo_far, wq_far, wg_far,
+    x_own, x_other, acc_k, acc_v, decay, coarse, fine, wo, wq, wg, wk, wv, log_decay, arrived,
 ):
     rows, part = x_own.shape
     core = lax.axis_index("fsdp")
@@ -141,43 +154,28 @@
 
     def tile(x, half, start):
         columns = pl.ds(pl.multiple_of(half * part, part), part)
-        return functools.partial(loads.start, x_far.at[pl.ds(start, TILE), columns], x.at[pl.ds(start, TILE)])
+        return loads.start(x_far.at[pl.ds(start, TILE), columns], x.at[pl.ds(start, TILE)])
 
     starts = range(0, rows, TILE)
-    half = part // 2
-    queue = [functools.partial(loads.start, log_decay_far, log_decay)]
-    queue += [functools.partial(loads.start, wk_far.at[pl.ds(at, half)], wk.at[pl.ds(at, half)]) for at in (0, half)]
-    queue += [tile(x_own, core, start) for start in starts]
-    queue += [functools.partial(loads.start, wv_far.at[pl.ds(at, half)], wv.at[pl.ds(at, half)]) for at in (0, half)]
-    queue += [tile(x_other, 1 - core, start) for start in starts]
-    queue += [functools.partial(loads.start, wo_far, wo)]
-    flight, done = [], 0
-
-    def fill(limit):
-        while len(flight) < min(len(queue), done + limit):
-            flight.append(queue[len(flight)]())
-
-    def need(count):
-        nonlocal done
-        while done < count:
-            flight[done].wait()
-            done += 1
-            fill(IN_FLIGHT)
-
-    fill(IN_FLIGHT)
+    logs, key = loads.start(log_decay_far, log_decay), loads.start(wk_far, wk)
+    tiles = [tile(x_own, core, start) for start in starts]
+    value = loads.start(wv_far, wv)
+    others = [tile(x_other, 1 - core, start) for start in starts]
+    others += [loads.start(wo_far, wo), loads.start(wq_far, wq), loads.start(wg_far, wg)]
     angle_tables(coarse, fine)
-    need(1)
+    logs.wait()
     decay_sums(log_decay, decay)
-    for number, start in enumerate(starts):
-        need(4 + number)
+    key.wait()
+    for copy, start in zip(tiles, starts):
         at = slice(start, start + TILE)
+        copy.wait()
         acc_k[at, :] = mm(x_own[at, :], wk[...])
-    need(5 + len(starts))
+    value.wait()
     for start in starts:
         at = slice(start, start + TILE)
         acc_v[at, :] = mm(x_own[at, :], wv[...])
-        need(min(len(queue), done + 2))
-    need(len(queue))
+    for copy in others:
+        copy.wait()
 
 
 def pack_message(message, states, logs):
@@ -228,12 +226,8 @@
 
 
 def key_value_kernel(
-    heads, wq_far, wg_far, x, wk, wv, acc_k, acc_v, decay, coarse, fine, wqg,
-    k_out, v_out, before_out, state_out, message, arrived,
+    heads, x, wk, wv, acc_k, acc_v, decay, coarse, fine, k_out, v_out, before_out, state_out, message
 ):
-    loads = Loads(arrived)
-    part = wk.shape[0]
-    others = [loads.start(far, wqg.at[pl.ds(at, part)]) for far, at in ((wq_far, 0), (wg_far, part))]
     state_out[...] = jnp.zeros_like(state_out)
 
     def block_step(block, totals):
@@ -266,8 +260,6 @@
     totals = lax.fori_loop(0, x.shape[0] // BLOCK, block_step, jnp.zeros((1, 8), F32))
     states = [state_out[head * DH : (head + 1) * DH, :] for head in range(heads)]
     pack_message(message, states, [totals[:, head : head + 1] for head in range(heads)])
-    for copy in others:
-        copy.wait()
 
 
 def combine_kernel(heads, hop, sets, first, state, sent, *refs):
@@ -298,9 +290,8 @@
 
 
 def query_gate_kernel(
-    heads, block, x_own, x_other, wqg, wqg_far, decay, coarse, fine, k, v, q_out, g_out, intra_out
+    heads, block, x_own, x_other, wq, wq_far, wg, wg_far, decay, coarse, fine, k, v, q_out, g_out, intra_out
 ):
-    part = x_own.shape[1]
     start = block * BLOCK
     lines = decay[:, start : start + BLOCK]
     columns = lines.T
@@ -310,8 +301,8 @@
         at = pl.ds(pl.multiple_of(piece * TILE, TILE), TILE)
         own, far = x_own[pl.ds(first, TILE), :], x_other[pl.ds(first, TILE), :]
         cosine, sine = angles(coarse, fine, first, TILE)
-        q_out[at, :] = turned(mm(own, wqg[:part, :]) + mm(far, wqg_far[:part, :]), cosine, sine)
-        g_out[at, :] = (mm(own, wqg[part:, :]) + mm(far, wqg_far[part:, :])).astype(BF16)
+        q_out[at, :] = turned(mm(own, wq[...]) + mm(far, wq_far[...]), cosine, sine)
+        g_out[at, :] = (mm(own, wg[...]) + mm(far, wg_far[...])).astype(BF16)
         return carry
 
     lax.fori_loop(0, BLOCK // TILE, project, 0)
@@ -442,31 +433,36 @@
     key_far = swap(key_weight, "fsdp", 1)
     value_far = swap(value_weight, "fsdp", 1)
 
-    x_own, x_other, acc_k, acc_v, decay, coarse, fine, out_first = loading_call(
+    x_own, x_other, acc_k, acc_v, decay, coarse, fine, out_first, own_q, own_g = loading_call(
         key_value_own_kernel,
         [((rows, part), BF16)] * 2
         + [((rows, cols), F32)] * 2
         + [((8, rows), F32)]
         + tables
-        + [(out_weight.shape, BF16)],
-        [x, key_weight, value_weight, log_decay[0].T, out_weight],
+        + [(out_weight.shape, BF16), ((part, cols), BF16), ((part, cols), BF16)],
+        [x, key_weight, value_weight, log_decay[0].T, out_weight, query_weight, gate_weight],
         [],
         [pltpu.VMEM((part, cols), BF16)] * 2 + [pltpu.VMEM((heads, rows), F32)],
         2 * (rows // TILE) + 6,
         "key_value_own",
     )
     state_shape, message_shape = (heads * DH, DH), (heads * DH + EXTRA, DH)
-    own_qg, keys, values, before, window, message = loading_call(
+    keys, values, before, window, message = kernel_call(
         functools.partial(key_value_kernel, heads),
-        [((2 * part, cols), BF16)]
-        + [((rows, cols), BF16)] * 2
+        [((rows, cols), BF16)] * 2
         + [((blocks, heads * DH, DH), BF16), (state_shape, F32), (message_shape, BF16)],
-        [query_weight, gate_weight],
         [x_other, key_far, value_far, acc_k, acc_v, decay, coarse, fine],
-        [],
-        2,
         "key_value",
     )
+    far_q, far_g = swap(own_q, "fsdp", 1), swap(own_g, "fsdp", 1)
+
+    def query_gate(block, decay):
+        return kernel_call(
+            functools.partial(query_gate_kernel, heads, block),
+            [((BLOCK, cols), BF16), ((BLOCK, cols), BF16), ((BLOCK, cols), F32)],
+            [x_own, x_other, own_q, far_q, own_g, far_g, decay, coarse, fine, keys, values],
+            "query_gate",
+        )
 
     def exchange(message, lowers, hop):
         pairs = [(at, at + hop) for at in lowers]
@@ -474,7 +470,9 @@
             pairs += [(upper, at) for at, upper in pairs]
         return lax.ppermute(message, "ctx", pairs)
 
-    entering, hop, early, message_sent = None, 1, [], message
+    projected = list(query_gate(0, decay))
+    window = after(window, projected[0])
+    entering, hop, early, first_message = None, 1, [], message
     while True:
         first_set, *later_sets = exchanges(ctx, hop)
         later_sets = [lowers for lowers in later_sets if lowers]
@@ -493,27 +491,20 @@
         )
         hop *= 2
 
-    far_qg = swap(own_qg, "fsdp", 1)
     own_second = swap(out_first, "fsdp", 1)
     [for_partner] = kernel_call(
         columns_kernel,
         [(out_weight.shape, BF16)],
-        [out_first, own_second],
+        [after(out_first, first_message), own_second],
         "columns",
     )
     pairs = [(at * cores + at_core, (at ^ mask) * cores + at_core) for at in range(tp) for at_core, mask in enumerate((near_mask, far_mask))]
     out_mine = lax.ppermute(for_partner, ("tp", "fsdp"), pairs)
 
-    held, projected = after(decay, message), []
-    for block in range(blocks):
-        if block == blocks - 1 and early:
-            held = after(held, *early, out_mine)
-        projected += kernel_call(
-            functools.partial(query_gate_kernel, heads, block),
-            [((BLOCK, cols), BF16), ((BLOCK, cols), BF16), ((BLOCK, cols), F32)],
-            [x_own, x_other, own_qg, far_qg, held, coarse, fine, keys, values],
-            "query_gate",
-        )
+    held = after(decay, message, *early)
+    for block in range(1, blocks):
+        projected += query_gate(block, held)
+
     count = rows // 2 // TILE
     masks = (near_mask, far_mask)
     hidden, far = [[], []], [[], []]
@@ -525,7 +516,7 @@
             [held, before, entering, *arrivals, *projected],
             "hidden",
         )
-        if number == 1:
+        if number == 0:
             out_other = swap(after(out_mine, pair[0]), "fsdp", 1)
         for half in range(2):
             hidden[half].append(pair[half])

time: 65.1 us -> 63.4 us (0.974)
  the two profiles are of different devices: /device:TPU:18 before, /device:TPU:24 now
where the time goes in v9:
time: 63.4 us; the launch traced here: 62.9 us
  waiting for transfers between devices  25 us (39%)
  Pallas kernels  24.1 us (38%)
  starting transfers between devices  13.7 us (22%)
    pallas_call x14, Pallas kernels, kernel_call(): pl.pallas_call(kernel, in_specs=[pl.BlockSpec(memory_space=pltpu.VMEM)] *...  18.4 us
    ppermute x14, waiting for transfers between devices, swap(): lax.ppermute(value, axis, [(place, place ^ mask) for place in range(size)])  16.2 us
    ppermute x3, waiting for transfers between devices, exchange(): return lax.ppermute(message, 'ctx', pairs)  8.89 us
    ppermute x14, starting transfers between devices, swap(): lax.ppermute(value, axis, [(place, place ^ mask) for place in range(size)])  7.03 us
    ppermute x3, starting transfers between devices, exchange(): return lax.ppermute(message, 'ctx', pairs)  5.08 us
    pallas_call x1, Pallas kernels, loading_call(): pl.pallas_call(kernel, in_specs=[pl.BlockSpec(memory_space=pltpu.HBM)] *...  4.54 us
    ppermute x1, starting transfers between devices, on_device(): out_mine = lax.ppermute(for_partner, ('tp', 'fsdp'), pairs)  1.56 us
  transfers between devices with their start and end apart: 18, of which 8 were waited for; matrix products, arithmetic and copies ran while one was open for 0% of the time, Pallas kernels for 36%

profile of v9, /device:TPU:24, one launch (start us, length us, event | category | flops | bytes accessed | tf_op | source)
XLA Modules:
  0.0 62.9 jit_solution(96654354050250074)
XLA Ops:
  0.0 0.5 collective-permute-start.2
  0.5 4.5 %key_value_own.1 = (bf16[1024,1024]{1,0:T(8,128)(2,1)S(1)}, bf16[1024,1024]{1,0:T(8,128)(2,1)S(1)}, f32[1024,512]{1,0:T(8,128)S(1)}, f32[1024,512]{1,0:T(8,128)S...) custom-call(bf16[1024,2048]{1,0:T(8,128)(2,1)} %bitcast.4, ...), custom_call_target="tpu_custom_call" | custom-call | flops 1 | bytes 1 | tf_op jit(solution)/shard_map/key_value_own/pallas_call | solution.py:56
  5.1 0.5 collective-permute-start.3
  5.7 3.4 %key_value.1 = (bf16[1024,512]{1,0:T(8,128)(2,1)S(1)}, bf16[1024,512]{1,0:T(8,128)(2,1)S(1)}, bf16[2,512,256]{2,1,0:T(8,128)(2,1)S(1)}, f32[512,256]{1,0:T(8,128)S(1)}, bf16[528,256]{1,0:T(8,128)(2,1)S(1)}) custom-call(bf16[1024,1024]{1,0:T(8,128)(2,1)S(1)} %get-tuple-element.44.x.x_other, bf16[1024,512]{1,0:T(8,128)(2,1)S(1)} %collective-permute-done.1.wk, ...), custom_call_target="tpu_custom_call" | custom-call | flops 1 | bytes 1 | tf_op jit(solution)/shard_map/key_value/pallas_call | solution.py:40
  9.2 1.6 %collective-permute-start.9 = (bf16[512,1024]{1,0:T(8,128)(2,1)S(1)}, bf16[512,1024]{1,0:T(8,128)(2,1)S(1)}, u32[]{:S(2)}, u32[]{:S(2)}) collective-permute-start(bf16[512,1024]{1,0:T(8,128)(2,1)S(1)} %columns.1), channel_id=1, source_target_pairs={{0,2},{1,5},{2,0},{3,7},{4,6},{5,1},{6,4},{7,3},{8,10},{9,13},{10,... | collective-permute-start | bytes 3145736 | tf_op jit(solution)/shard_map/ppermute | solution.py:502
  10.7 1.3 %collective-permute-start.5 = (bf16[528,256]{1,0:T(8,128)(2,1)S(1)}, bf16[528,256]{1,0:T(8,128)(2,1)S(1)}, u32[]{:S(2)}, u32[]{:S(2)}) collective-permute-start(bf16[528,256]{1,0:T(8,128)(2,1)S(1)} %get-tuple-element.58.sent), channel_id=1, source_target_pairs={{0,8},{8,16},{16,24},{1,9},{9,17},{17,25},{2,10},{10,18},{18,26},{... | collective-permute-start | bytes 811016 | tf_op jit(solution)/shard_map/ppermute | solution.py:471
  12.0 0.7 %collective-permute-start.7 = (bf16[528,256]{1,0:T(8,128)(2,1)S(1)}, bf16[528,256]{1,0:T(8,128)(2,1)S(1)}, u32[]{:S(2)}, u32[]{:S(2)}) collective-permute-start(bf16[528,256]{1,0:T(8,128)(2,1)S(1)} %get-tuple-element.58.sent), channel_id=1, source_target_pairs={{0,16},{16,0},{1,17},{17,1},{2,18},{18,2},{3,19},{19,3},{4,20},{20... | collective-permute-start | bytes 811016 | tf_op jit(solution)/shard_map/ppermute | solution.py:471
  12.7 3.5 %query_gate.2 = (bf16[512,512]{1,0:T(8,128)(2,1)S(1)}, bf16[512,512]{1,0:T(8,128)(2,1)S(1)}, f32[512,512]{1,0:T(8,128)S(1)}) custom-call(bf16[1024,1024]{1,0:T(8,128)(2,1)S(1)} %get-tuple-element.51.x_own, bf16[1024,1024]{1,0:T(8,128)(2,1)S(1)} %get-tuple-element.44.x.x_other, bf16[1024,512]{1,0:T(8,128)(2,1)S(1)} %get-tuple-element.52.wq, ...), custom_call_target="tpu_custom_call" | custom-call | flops 1 | bytes 1 | tf_op jit(solution)/shard_map/query_gate/pallas_call | solution.py:40
  16.3 5.0 %collective-permute-done.5.refs_0_ = bf16[528,256]{1,0:T(8,128)(2,1)S(1)} collective-permute-done((bf16[528,256]{1,0:T(8,128)(2,1)S(1)}, bf16[528,256]{1,0:T(8,128)(2,1)S(1)}, u32[]{:S(2)}, u32[]{:S(2)}) %collective-permute-start.5) | collective-permute-done | bytes 270368 | tf_op jit(solution)/shard_map/ppermute | solution.py:471
  21.2 0.9 %combine.1 = (f32[512,256]{1,0:T(8,128)}, f32[520,256]{1,0:T(8,128)S(1)}, bf16[528,256]{1,0:T(8,128)(2,1)S(1)}) custom-call(f32[512,256]{1,0:T(8,128)S(1)} %get-tuple-element.57.state, bf16[528,256]{1,0:T(8,128)(2,1)S(1)} %get-tuple-element.58.sent, bf16[528,256]{1,0:T(8,128)(2,1)S(1)} %collective-permute-done.5.refs_0_), custom_call_target="tpu_custom_call" | custom-call | flops 1 | bytes 1 | tf_op jit(solution)/shard_map/combine/pallas_call | solution.py:40
  22.2 3.1 %collective-permute-start.6 = (bf16[528,256]{1,0:T(8,128)(2,1)S(1)}, bf16[528,256]{1,0:T(8,128)(2,1)S(1)}, u32[]{:S(2)}, u32[]{:S(2)}) collective-permute-start(bf16[528,256]{1,0:T(8,128)(2,1)S(1)} %get-tuple-element.60), channel_id=1, source_target_pairs={{8,24},{24,8},{9,25},{25,9},{10,26},{26,10},{11,27},{27,11},{12,28... | collective-permute-start | bytes 811016 | tf_op jit(solution)/shard_map/ppermute | solution.py:471
  25.3 3.5 %query_gate.3 = (bf16[512,512]{1,0:T(8,128)(2,1)S(1)}, bf16[512,512]{1,0:T(8,128)(2,1)S(1)}, f32[512,512]{1,0:T(8,128)S(1)}) custom-call(bf16[1024,1024]{1,0:T(8,128)(2,1)S(1)} %get-tuple-element.51.x_own, bf16[1024,1024]{1,0:T(8,128)(2,1)S(1)} %get-tuple-element.44.x.x_other, bf16[1024,512]{1,0:T(8,128)(2,1)S(1)} %get-tuple-element.52.wq, ...), custom_call_target="tpu_custom_call" | custom-call | flops 1 | bytes 1 | tf_op jit(solution)/shard_map/query_gate/pallas_call | solution.py:40
  28.8 3.9 %collective-permute-done.6.refs_0_ = bf16[528,256]{1,0:T(8,128)(2,1)S(1)} collective-permute-done((bf16[528,256]{1,0:T(8,128)(2,1)S(1)}, bf16[528,256]{1,0:T(8,128)(2,1)S(1)}, u32[]{:S(2)}, u32[]{:S(2)}) %collective-permute-start.6) | collective-permute-done | bytes 270368 | tf_op jit(solution)/shard_map/ppermute | solution.py:471
  32.7 1.7 %hidden.3 = (bf16[256,512]{1,0:T(8,128)(2,1)S(1)}, bf16[256,512]{1,0:T(8,128)(2,1)S(1)}, bf16[16,128]{1,0:T(8,128)(2,1)}) custom-call(f32[8,1024]{1,0:T(8,128)S(1)} %get-tuple-element.63.decay, bf16[2,512,256]{2,1,0:T(8,128)(2,1)S(1)} %get-tuple-element.49.before, f32[520,256]{1,0:T(8,128)S(1)} %get-tuple-element.59.entering, ...), custom_call_target="tpu_custom_call" | custom-call | flops 1 | bytes 1 | tf_op jit(solution)/shard_map/hidden/pallas_call | solution.py:40
  34.5 2.0 %collective-permute-start.16 = (bf16[256,512]{1,0:T(8,128)(2,1)S(1)}, bf16[256,512]{1,0:T(8,128)(2,1)S(1)}, u32[]{:S(2)}, u32[]{:S(2)}) collective-permute-start(bf16[256,512]{1,0:T(8,128)(2,1)S(1)} %get-tuple-element.70.refs_3_), channel_id=1, source_target_pairs={{0,2},{2,0},{4,6},{6,4},{1,3},{3,1},{5,7},{7,5},{8,10},{10,8},{12,... | collective-permute-start | bytes 786440 | tf_op jit(solution)/shard_map/ppermute | solution.py:35
  36.5 1.7 %hidden.2 = (bf16[256,512]{1,0:T(8,128)(2,1)S(1)}, bf16[256,512]{1,0:T(8,128)(2,1)S(1)}, bf16[16,128]{1,0:T(8,128)(2,1)}) custom-call(f32[8,1024]{1,0:T(8,128)S(1)} %get-tuple-element.63.decay, bf16[2,512,256]{2,1,0:T(8,128)(2,1)S(1)} %get-tuple-element.49.before, f32[520,256]{1,0:T(8,128)S(1)} %get-tuple-element.59.entering, ...), custom_call_target="tpu_custom_call" | custom-call | flops 1 | bytes 1 | tf_op jit(solution)/shard_map/hidden/pallas_call | solution.py:40
  38.2 0.5 collective-permute-start.12
  38.7 1.6 %collective-permute-start.8 = (bf16[256,512]{1,0:T(8,128)(2,1)S(1)}, bf16[256,512]{1,0:T(8,128)(2,1)S(1)}, u32[]{:S(2)}, u32[]{:S(2)}) collective-permute-start(bf16[256,512]{1,0:T(8,128)(2,1)S(1)} %get-tuple-element.67.refs_0_), channel_id=1, source_target_pairs={{0,4},{2,6},{4,0},{6,2},{1,5},{3,7},{5,1},{7,3},{8,12},{10,14},{12... | collective-permute-start | bytes 786440 | tf_op jit(solution)/shard_map/ppermute | solution.py:35
  40.3 1.3 %own_products.1 = (f32[512,1024]{1,0:T(8,128)S(1)}, f32[512,1024]{1,0:T(8,128)S(1)}) custom-call(bf16[512,1024]{1,0:T(8,128)(2,1)S(1)} %get-tuple-element.72.own_first.first, bf16[512,1024]{1,0:T(8,128)(2,1)S(1)} %collective-permute-done.own_second.second, bf16[256,512]{1,0:T(8,128)(2,1)S(1)} %get-tuple-element.67.refs_0_, ...), custom_call_target="tpu_custom_call" | custom-call | flops 1 | bytes 1 | tf_op jit(solution)/shard_map/own_products/pallas_call | solution.py:40
  41.9 1.7 %collective-permute-done.16.far.refs_3_ = bf16[256,512]{1,0:T(8,128)(2,1)S(1)} collective-permute-done((bf16[256,512]{1,0:T(8,128)(2,1)S(1)}, bf16[256,512]{1,0:T(8,128)(2,1)S(1)}, u32[]{:S(2)}, u32[]{:S(2)}) %collective-permute-start.16) | collective-permute-done | bytes 262176 | tf_op jit(solution)/shard_map/ppermute | solution.py:35
  44.0 0.5 collective-permute-start.17
  44.4 1.2 %collective-permute-done.14.far.refs_2_ = bf16[256,512]{1,0:T(8,128)(2,1)S(1)} collective-permute-done((bf16[256,512]{1,0:T(8,128)(2,1)S(1)}, bf16[256,512]{1,0:T(8,128)(2,1)S(1)}, u32[]{:S(2)}, u32[]{:S(2)}) %collective-permute-start.14) | collective-permute-done | bytes 262176 | tf_op jit(solution)/shard_map/ppermute | solution.py:35
  45.6 0.3 give.6
  45.9 0.4 collective-permute-start.15
  46.4 2.9 %collective-permute-done.12.far.refs_1_ = bf16[256,512]{1,0:T(8,128)(2,1)S(1)} collective-permute-done((bf16[256,512]{1,0:T(8,128)(2,1)S(1)}, bf16[256,512]{1,0:T(8,128)(2,1)S(1)}, u32[]{:S(2)}, u32[]{:S(2)}) %collective-permute-start.12) | collective-permute-done | bytes 262176 | tf_op jit(solution)/shard_map/ppermute | solution.py:35
  49.6 0.5 collective-permute-start.13
  50.1 1.2 %collective-permute-done.8.far.refs_0_ = bf16[256,512]{1,0:T(8,128)(2,1)S(1)} collective-permute-done((bf16[256,512]{1,0:T(8,128)(2,1)S(1)}, bf16[256,512]{1,0:T(8,128)(2,1)S(1)}, u32[]{:S(2)}, u32[]{:S(2)}) %collective-permute-start.8) | collective-permute-done | bytes 262176 | tf_op jit(solution)/shard_map/ppermute | solution.py:35
  51.6 0.4 collective-permute-start.11
  52.0 0.7 %keep.1 = (f32[512,512]{1,0:T(8,128)S(1)}, f32[512,512]{1,0:T(8,128)S(1)}) custom-call(bf16[256,512]{1,0:T(8,128)(2,1)S(1)} %collective-permute-done.8.far.refs_0_, bf16[256,512]{1,0:T(8,128)(2,1)S(1)} %collective-permute-done.12.far.refs_1_, bf16[256,512]{1,0:T(8,128)(2,1)S(1)} %collective-permute-done.14.far.refs_2_, ...), custom_call_target="tpu_custom_call" | custom-call | flops 1 | bytes 1 | tf_op jit(solution)/shard_map/keep/pallas_call | solution.py:40
  52.7 4.2 %collective-permute-done.17.refs_3_ = bf16[256,512]{1,0:T(8,128)(2,1)S(1)} collective-permute-done((bf16[256,512]{1,0:T(8,128)(2,1)S(1)}, bf16[256,512]{1,0:T(8,128)(2,1)S(1)}, u32[]{:S(2)}, u32[]{:S(2)}) %collective-permute-start.17) | collective-permute-done | bytes 262176 | tf_op jit(solution)/shard_map/ppermute | solution.py:35
  56.9 4.9 %collective-permute-done.13.refs_1_ = bf16[256,512]{1,0:T(8,128)(2,1)S(1)} collective-permute-done((bf16[256,512]{1,0:T(8,128)(2,1)S(1)}, bf16[256,512]{1,0:T(8,128)(2,1)S(1)}, u32[]{:S(2)}, u32[]{:S(2)}) %collective-permute-start.13) | collective-permute-done | bytes 262176 | tf_op jit(solution)/shard_map/ppermute | solution.py:35
  61.8 1.1 %finish.1 = bf16[1,1024,512]{2,1,0:T(8,128)(2,1)} custom-call(bf16[256,512]{1,0:T(8,128)(2,1)S(1)} %collective-permute-done.11.refs_0_, bf16[256,512]{1,0:T(8,128)(2,1)S(1)} %collective-permute-done.13.refs_1_, bf16[256,512]{1,0:T(8,128)(2,1)S(1)} %collective-permute-done.15.refs_2_, bf16[256,512]{1,0:T(8,128)(2,1)S(1)} %collective-permute-done.17.refs_3_, ...), custom_call_target="tpu_custom_call" | custom-call | tf_op jit(solution)/shard_map/finish/pallas_call | solution.py:553
  (20 shorter events, 1.5 us)
Async XLA Ops:
  0.0 5.7 %collective-permute-start.1 = (bf16[1024,512]{1,0:T(8,128)(2,1)}, bf16[1024,512]{1,0:T(8,128)(2,1)S(1)}, u32[]{:S(2)}, u32[]{:S(2)}) collective-permute-start(bf16[1024,512]{1,0:T(8,128)(2,1)} %wk_far.1), channel_id=1, source_target_pairs={{0,1},{1,0},{2,3},{3,2},{4,5},{5,4},{6,7},{7,6},{8,9},{9,8},{10,11... | collective-permute-start | bytes 3145736 | tf_op jit(solution)/shard_map/ppermute | solution.py:35
  0.0 5.7 %collective-permute-start.2 = (bf16[1024,512]{1,0:T(8,128)(2,1)}, bf16[1024,512]{1,0:T(8,128)(2,1)S(1)}, u32[]{:S(2)}, u32[]{:S(2)}) collective-permute-start(bf16[1024,512]{1,0:T(8,128)(2,1)} %wv_far.1), channel_id=1, source_target_pairs={{0,1},{1,0},{2,3},{3,2},{4,5},{5,4},{6,7},{7,6},{8,9},{9,8},{10,11... | collective-permute-start | bytes 3145736 | tf_op jit(solution)/shard_map/ppermute | solution.py:35
  5.1 4.0 %collective-permute-start = (bf16[512,1024]{1,0:T(8,128)(2,1)S(1)}, bf16[512,1024]{1,0:T(8,128)(2,1)S(1)}, u32[]{:S(2)}, u32[]{:S(2)}) collective-permute-start(bf16[512,1024]{1,0:T(8,128)(2,1)S(1)} %get-tuple-element.72.own_first.first), channel_id=1, source_target_pairs={{0,1},{1,0},{2,3},{3,2},{4,5},{5,4},{6,7},{7,6},{8,9},{9,8},{10,11... | collective-permute-start | bytes 3145736 | tf_op jit(solution)/shard_map/ppermute | solution.py:35
  5.1 7.6 %collective-permute-start.3 = (bf16[1024,512]{1,0:T(8,128)(2,1)S(1)}, bf16[1024,512]{1,0:T(8,128)(2,1)S(1)}, u32[]{:S(2)}, u32[]{:S(2)}) collective-permute-start(bf16[1024,512]{1,0:T(8,128)(2,1)S(1)} %get-tuple-element.52.wq), channel_id=1, source_target_pairs={{0,1},{1,0},{2,3},{3,2},{4,5},{5,4},{6,7},{7,6},{8,9},{9,8},{10,11... | collective-permute-start | bytes 3145736 | tf_op jit(solution)/shard_map/ppermute | solution.py:35
  5.6 7.1 %collective-permute-start.4 = (bf16[1024,512]{1,0:T(8,128)(2,1)S(1)}, bf16[1024,512]{1,0:T(8,128)(2,1)S(1)}, u32[]{:S(2)}, u32[]{:S(2)}) collective-permute-start(bf16[1024,512]{1,0:T(8,128)(2,1)S(1)} %get-tuple-element.53.wg), channel_id=1, source_target_pairs={{0,1},{1,0},{2,3},{3,2},{4,5},{5,4},{6,7},{7,6},{8,9},{9,8},{10,11... | collective-permute-start | bytes 3145736 | tf_op jit(solution)/shard_map/ppermute | solution.py:35
  9.2 25.3 %collective-permute-start.9 = (bf16[512,1024]{1,0:T(8,128)(2,1)S(1)}, bf16[512,1024]{1,0:T(8,128)(2,1)S(1)}, u32[]{:S(2)}, u32[]{:S(2)}) collective-permute-start(bf16[512,1024]{1,0:T(8,128)(2,1)S(1)} %columns.1), channel_id=1, source_target_pairs={{0,2},{1,5},{2,0},{3,7},{4,6},{5,1},{6,4},{7,3},{8,10},{9,13},{10,... | collective-permute-start | bytes 3145736 | tf_op jit(solution)/shard_map/ppermute | solution.py:502
  10.7 10.5 %collective-permute-start.5 = (bf16[528,256]{1,0:T(8,128)(2,1)S(1)}, bf16[528,256]{1,0:T(8,128)(2,1)S(1)}, u32[]{:S(2)}, u32[]{:S(2)}) collective-permute-start(bf16[528,256]{1,0:T(8,128)(2,1)S(1)} %get-tuple-element.58.sent), channel_id=1, source_target_pairs={{0,8},{8,16},{16,24},{1,9},{9,17},{17,25},{2,10},{10,18},{18,26},{... | collective-permute-start | bytes 811016 | tf_op jit(solution)/shard_map/ppermute | solution.py:471
  12.0 13.3 %collective-permute-start.7 = (bf16[528,256]{1,0:T(8,128)(2,1)S(1)}, bf16[528,256]{1,0:T(8,128)(2,1)S(1)}, u32[]{:S(2)}, u32[]{:S(2)}) collective-permute-start(bf16[528,256]{1,0:T(8,128)(2,1)S(1)} %get-tuple-element.58.sent), channel_id=1, source_target_pairs={{0,16},{16,0},{1,17},{17,1},{2,18},{18,2},{3,19},{19,3},{4,20},{20... | collective-permute-start | bytes 811016 | tf_op jit(solution)/shard_map/ppermute | solution.py:471
  22.2 10.6 %collective-permute-start.6 = (bf16[528,256]{1,0:T(8,128)(2,1)S(1)}, bf16[528,256]{1,0:T(8,128)(2,1)S(1)}, u32[]{:S(2)}, u32[]{:S(2)}) collective-permute-start(bf16[528,256]{1,0:T(8,128)(2,1)S(1)} %get-tuple-element.60), channel_id=1, source_target_pairs={{8,24},{24,8},{9,25},{25,9},{10,26},{26,10},{11,27},{27,11},{12,28... | collective-permute-start | bytes 811016 | tf_op jit(solution)/shard_map/ppermute | solution.py:471
  34.5 7.1 %collective-permute-start.10 = (bf16[512,1024]{1,0:T(8,128)(2,1)S(1)}, bf16[512,1024]{1,0:T(8,128)(2,1)S(1)}, u32[]{:S(2)}, u32[]{:S(2)}) collective-permute-start(bf16[512,1024]{1,0:T(8,128)(2,1)S(1)} %collective-permute-done.9.mine), channel_id=1, source_target_pairs={{0,1},{1,0},{2,3},{3,2},{4,5},{5,4},{6,7},{7,6},{8,9},{9,8},{10,11... | collective-permute-start | bytes 3145736 | tf_op jit(solution)/shard_map/ppermute | solution.py:35
  34.5 9.2 %collective-permute-start.16 = (bf16[256,512]{1,0:T(8,128)(2,1)S(1)}, bf16[256,512]{1,0:T(8,128)(2,1)S(1)}, u32[]{:S(2)}, u32[]{:S(2)}) collective-permute-start(bf16[256,512]{1,0:T(8,128)(2,1)S(1)} %get-tuple-element.70.refs_3_), channel_id=1, source_target_pairs={{0,2},{2,0},{4,6},{6,4},{1,3},{3,1},{5,7},{7,5},{8,10},{10,8},{12,... | collective-permute-start | bytes 786440 | tf_op jit(solution)/shard_map/ppermute | solution.py:35
  36.5 9.1 %collective-permute-start.14 = (bf16[256,512]{1,0:T(8,128)(2,1)S(1)}, bf16[256,512]{1,0:T(8,128)(2,1)S(1)}, u32[]{:S(2)}, u32[]{:S(2)}) collective-permute-start(bf16[256,512]{1,0:T(8,128)(2,1)S(1)} %get-tuple-element.69.refs_2_), channel_id=1, source_target_pairs={{0,4},{2,6},{4,0},{6,2},{1,5},{3,7},{5,1},{7,3},{8,12},{10,14},{12... | collective-permute-start | bytes 786440 | tf_op jit(solution)/shard_map/ppermute | solution.py:35
  38.2 11.0 %collective-permute-start.12 = (bf16[256,512]{1,0:T(8,128)(2,1)S(1)}, bf16[256,512]{1,0:T(8,128)(2,1)S(1)}, u32[]{:S(2)}, u32[]{:S(2)}) collective-permute-start(bf16[256,512]{1,0:T(8,128)(2,1)S(1)} %get-tuple-element.68.refs_1_), channel_id=1, source_target_pairs={{0,2},{2,0},{4,6},{6,4},{1,3},{3,1},{5,7},{7,5},{8,10},{10,8},{12,... | collective-permute-start | bytes 786440 | tf_op jit(solution)/shard_map/ppermute | solution.py:35
  38.7 12.5 %collective-permute-start.8 = (bf16[256,512]{1,0:T(8,128)(2,1)S(1)}, bf16[256,512]{1,0:T(8,128)(2,1)S(1)}, u32[]{:S(2)}, u32[]{:S(2)}) collective-permute-start(bf16[256,512]{1,0:T(8,128)(2,1)S(1)} %get-tuple-element.67.refs_0_), channel_id=1, source_target_pairs={{0,4},{2,6},{4,0},{6,2},{1,5},{3,7},{5,1},{7,3},{8,12},{10,14},{12... | collective-permute-start | bytes 786440 | tf_op jit(solution)/shard_map/ppermute | solution.py:35
  44.0 12.9 %collective-permute-start.17 = (bf16[256,512]{1,0:T(8,128)(2,1)S(1)}, bf16[256,512]{1,0:T(8,128)(2,1)S(1)}, u32[]{:S(2)}, u32[]{:S(2)}) collective-permute-start(bf16[256,512]{1,0:T(8,128)(2,1)S(1)} %give.7), channel_id=1, source_target_pairs={{0,4},{2,6},{4,0},{6,2},{1,5},{3,7},{5,1},{7,3},{8,12},{10,14},{12... | collective-permute-start | bytes 786440 | tf_op jit(solution)/shard_map/ppermute | solution.py:35
  45.9 10.9 %collective-permute-start.15 = (bf16[256,512]{1,0:T(8,128)(2,1)S(1)}, bf16[256,512]{1,0:T(8,128)(2,1)S(1)}, u32[]{:S(2)}, u32[]{:S(2)}) collective-permute-start(bf16[256,512]{1,0:T(8,128)(2,1)S(1)} %give.6), channel_id=1, source_target_pairs={{0,2},{2,0},{4,6},{6,4},{1,3},{3,1},{5,7},{7,5},{8,10},{10,8},{12,... | collective-permute-start | bytes 786440 | tf_op jit(solution)/shard_map/ppermute | solution.py:35
  49.6 12.2 %collective-permute-start.13 = (bf16[256,512]{1,0:T(8,128)(2,1)S(1)}, bf16[256,512]{1,0:T(8,128)(2,1)S(1)}, u32[]{:S(2)}, u32[]{:S(2)}) collective-permute-start(bf16[256,512]{1,0:T(8,128)(2,1)S(1)} %give.5), channel_id=1, source_target_pairs={{0,4},{2,6},{4,0},{6,2},{1,5},{3,7},{5,1},{7,3},{8,12},{10,14},{12... | collective-permute-start | bytes 786440 | tf_op jit(solution)/shard_map/ppermute | solution.py:35
  51.6 10.2 %collective-permute-start.11 = (bf16[256,512]{1,0:T(8,128)(2,1)S(1)}, bf16[256,512]{1,0:T(8,128)(2,1)S(1)}, u32[]{:S(2)}, u32[]{:S(2)}) collective-permute-start(bf16[256,512]{1,0:T(8,128)(2,1)S(1)} %give.4), channel_id=1, source_target_pairs={{0,2},{2,0},{4,6},{6,4},{1,3},{3,1},{5,7},{7,5},{8,10},{10,8},{12,... | collective-permute-start | bytes 786440 | tf_op jit(solution)/shard_map/ppermute | solution.py:35

commit v10 on v9

--- a/solution.py
+++ b/solution.py
@@ -153,10 +153,11 @@
     loads = Loads(arrived)
 
     def tile(x, half, start):
+        at = pl.ds(start, BLOCK)
         columns = pl.ds(pl.multiple_of(half * part, part), part)
-        return loads.start(x_far.at[pl.ds(start, TILE), columns], x.at[pl.ds(start, TILE)])
-
-    starts = range(0, rows, TILE)
+        return loads.start(x_far.at[at, columns], x.at[at])
+
+    starts = range(0, rows, BLOCK)
     logs, key = loads.start(log_decay_far, log_decay), loads.start(wk_far, wk)
     tiles = [tile(x_own, core, start) for start in starts]
     value = loads.start(wv_far, wv)
@@ -167,12 +168,12 @@
     decay_sums(log_decay, decay)
     key.wait()
     for copy, start in zip(tiles, starts):
-        at = slice(start, start + TILE)
+        at = slice(start, start + BLOCK)
         copy.wait()
         acc_k[at, :] = mm(x_own[at, :], wk[...])
     value.wait()
     for start in starts:
-        at = slice(start, start + TILE)
+        at = slice(start, start + BLOCK)
         acc_v[at, :] = mm(x_own[at, :], wv[...])
     for copy in others:
         copy.wait()
@@ -235,26 +236,18 @@
         columns = decay[:, pl.ds(start, BLOCK)].T
         ending = columns[BLOCK - 1 : BLOCK, :]
         faded = jnp.exp(ending - columns)
-        updates = [None] * heads
-        for piece in range(BLOCK // TILE):
-            first = pl.multiple_of(start + piece * TILE, TILE)
-            at = pl.ds(first, TILE)
-            cosine, sine = angles(coarse, fine, first, TILE)
-            keys = turned(acc_k[at, :] + mm(x[at, :], wk[...]), cosine, sine)
-            values = (acc_v[at, :] + mm(x[at, :], wv[...])).astype(BF16)
-            k_out[at, :] = keys
-            v_out[at, :] = values
-            for head in range(heads):
-                span = slice(head * DH, (head + 1) * DH)
-                fade = faded[piece * TILE : (piece + 1) * TILE, head : head + 1]
-                weighted = (keys[:, span].astype(F32) * fade).astype(BF16)
-                update = mm_tn(weighted, values[:, span])
-                updates[head] = update if piece == 0 else updates[head] + update
+        at = pl.ds(start, BLOCK)
+        cosine, sine = angles(coarse, fine, start, BLOCK)
+        keys = turned(acc_k[at, :] + mm(x[at, :], wk[...]), cosine, sine)
+        k_out[at, :] = keys
+        values = (acc_v[at, :] + mm(x[at, :], wv[...])).astype(BF16)
+        v_out[at, :] = values
         for head in range(heads):
             span = slice(head * DH, (head + 1) * DH)
+            weighted = (keys[:, span].astype(F32) * faded[:, head : head + 1]).astype(BF16)
             old = state_out[span, :]
             before_out[block, span, :] = old.astype(BF16)
-            state_out[span, :] = jnp.exp(ending[:, head : head + 1]) * old + updates[head]
+            state_out[span, :] = jnp.exp(ending[:, head : head + 1]) * old + mm_tn(weighted, values[:, span])
         return totals + ending
 
     totals = lax.fori_loop(0, x.shape[0] // BLOCK, block_step, jnp.zeros((1, 8), F32))
@@ -296,16 +289,10 @@
     lines = decay[:, start : start + BLOCK]
     columns = lines.T
 
-    def project(piece, carry):
-        first = pl.multiple_of(start + piece * TILE, TILE)
-        at = pl.ds(pl.multiple_of(piece * TILE, TILE), TILE)
-        own, far = x_own[pl.ds(first, TILE), :], x_other[pl.ds(first, TILE), :]
-        cosine, sine = angles(coarse, fine, first, TILE)
-        q_out[at, :] = turned(mm(own, wq[...]) + mm(far, wq_far[...]), cosine, sine)
-        g_out[at, :] = (mm(own, wg[...]) + mm(far, wg_far[...])).astype(BF16)
-        return carry
-
-    lax.fori_loop(0, BLOCK // TILE, project, 0)
+    at = slice(start, start + BLOCK)
+    cosine, sine = angles(coarse, fine, start, BLOCK)
+    q_out[...] = turned(mm(x_own[at, :], wq[...]) + mm(x_other[at, :], wq_far[...]), cosine, sine)
+    g_out[...] = (mm(x_own[at, :], wg[...]) + mm(x_other[at, :], wg_far[...])).astype(BF16)
     for piece in range(BLOCK // TILE):
         low, last = piece * TILE, (piece + 1) * TILE
         place_t = lax.broadcasted_iota(jnp.int32, (TILE, last), 0) + low
@@ -443,7 +430,7 @@
         [x, key_weight, value_weight, log_decay[0].T, out_weight, query_weight, gate_weight],
         [],
         [pltpu.VMEM((part, cols), BF16)] * 2 + [pltpu.VMEM((heads, rows), F32)],
-        2 * (rows // TILE) + 6,
+        2 * (rows // BLOCK) + 6,
         "key_value_own",
     )
     state_shape, message_shape = (heads * DH, DH), (heads * DH + EXTRA, DH)

time: 63.4 us -> 63.3 us (level)
  Pallas kernels: 24.1 us -> 22.9 us
  waiting for transfers between devices: 25 us -> 26.2 us
    ppermute x3, waiting for transfers between devices: 8.89 us -> 10 us  [exchange(): return lax.ppermute(message, 'ctx', pairs)]
    pallas_call x14, Pallas kernels: 18.4 us -> 17.4 us  [kernel_call(): pl.pallas_call(kernel, in_specs=[pl.BlockSpec(memory_space=pltpu.VMEM)] *...]
  transfers between devices with their start and end apart: 18 -> 18, of which waited for: 8 -> 8; matrix products, arithmetic and copies ran while one was open for 0% -> 0% of each run, Pallas kernels for 36% -> 35%
where the time goes in v10:
time: 63.3 us; the launch traced here: 62.9 us
  waiting for transfers between devices  26.2 us (41%)
  Pallas kernels  22.9 us (36%)
  starting transfers between devices  13.7 us (22%)
    pallas_call x14, Pallas kernels, kernel_call(): pl.pallas_call(kernel, in_specs=[pl.BlockSpec(memory_space=pltpu.VMEM)] *...  17.4 us
    ppermute x14, waiting for transfers between devices, swap(): lax.ppermute(value, axis, [(place, place ^ mask) for place in range(size)])  16.1 us
    ppermute x3, waiting for transfers between devices, exchange(): return lax.ppermute(message, 'ctx', pairs)  10 us
    ppermute x14, starting transfers between devices, swap(): lax.ppermute(value, axis, [(place, place ^ mask) for place in range(size)])  7.05 us
    ppermute x3, starting transfers between devices, exchange(): return lax.ppermute(message, 'ctx', pairs)  5.08 us
    pallas_call x1, Pallas kernels, loading_call(): pl.pallas_call(kernel, in_specs=[pl.BlockSpec(memory_space=pltpu.HBM)] *...  4.35 us
    ppermute x1, starting transfers between devices, on_device(): out_mine = lax.ppermute(for_partner, ('tp', 'fsdp'), pairs)  1.56 us
  transfers between devices with their start and end apart: 18, of which 8 were waited for; matrix products, arithmetic and copies ran while one was open for 0% of the time, Pallas kernels for 35%

profile of v10, /device:TPU:24, one launch (start us, length us, event | category | flops | bytes accessed | tf_op | source)
XLA Modules:
  0.0 62.9 jit_solution(12700780699197149329)
XLA Ops:
  0.0 0.5 collective-permute-start.2
  0.5 4.3 %key_value_own.1 = (bf16[1024,1024]{1,0:T(8,128)(2,1)S(1)}, bf16[1024,1024]{1,0:T(8,128)(2,1)S(1)}, f32[1024,512]{1,0:T(8,128)S(1)}, f32[1024,512]{1,0:T(8,128)S...) custom-call(bf16[1024,2048]{1,0:T(8,128)(2,1)} %bitcast.4, ...), custom_call_target="tpu_custom_call" | custom-call | flops 1 | bytes 1 | tf_op jit(solution)/shard_map/key_value_own/pallas_call | solution.py:56
  4.9 0.5 collective-permute-start.3
  5.5 3.5 %key_value.1 = (bf16[1024,512]{1,0:T(8,128)(2,1)S(1)}, bf16[1024,512]{1,0:T(8,128)(2,1)S(1)}, bf16[2,512,256]{2,1,0:T(8,128)(2,1)S(1)}, f32[512,256]{1,0:T(8,128)S(1)}, bf16[528,256]{1,0:T(8,128)(2,1)S(1)}) custom-call(bf16[1024,1024]{1,0:T(8,128)(2,1)S(1)} %get-tuple-element.44.x.x_other, bf16[1024,512]{1,0:T(8,128)(2,1)S(1)} %collective-permute-done.1.wk, ...), custom_call_target="tpu_custom_call" | custom-call | flops 1 | bytes 1 | tf_op jit(solution)/shard_map/key_value/pallas_call | solution.py:40
  9.1 1.6 %collective-permute-start.9 = (bf16[512,1024]{1,0:T(8,128)(2,1)S(1)}, bf16[512,1024]{1,0:T(8,128)(2,1)S(1)}, u32[]{:S(2)}, u32[]{:S(2)}) collective-permute-start(bf16[512,1024]{1,0:T(8,128)(2,1)S(1)} %columns.1), channel_id=1, source_target_pairs={{0,2},{1,5},{2,0},{3,7},{4,6},{5,1},{6,4},{7,3},{8,10},{9,13},{10,... | collective-permute-start | bytes 3145736 | tf_op jit(solution)/shard_map/ppermute | solution.py:489
  10.7 1.3 %collective-permute-start.5 = (bf16[528,256]{1,0:T(8,128)(2,1)S(1)}, bf16[528,256]{1,0:T(8,128)(2,1)S(1)}, u32[]{:S(2)}, u32[]{:S(2)}) collective-permute-start(bf16[528,256]{1,0:T(8,128)(2,1)S(1)} %get-tuple-element.58.sent), channel_id=1, source_target_pairs={{0,8},{8,16},{16,24},{1,9},{9,17},{17,25},{2,10},{10,18},{18,26},{... | collective-permute-start | bytes 811016 | tf_op jit(solution)/shard_map/ppermute | solution.py:458
  12.0 0.7 %collective-permute-start.7 = (bf16[528,256]{1,0:T(8,128)(2,1)S(1)}, bf16[528,256]{1,0:T(8,128)(2,1)S(1)}, u32[]{:S(2)}, u32[]{:S(2)}) collective-permute-start(bf16[528,256]{1,0:T(8,128)(2,1)S(1)} %get-tuple-element.58.sent), channel_id=1, source_target_pairs={{0,16},{16,0},{1,17},{17,1},{2,18},{18,2},{3,19},{19,3},{4,20},{20... | collective-permute-start | bytes 811016 | tf_op jit(solution)/shard_map/ppermute | solution.py:458
  12.7 2.9 %query_gate.2 = (bf16[512,512]{1,0:T(8,128)(2,1)S(1)}, bf16[512,512]{1,0:T(8,128)(2,1)S(1)}, f32[512,512]{1,0:T(8,128)S(1)}) custom-call(bf16[1024,1024]{1,0:T(8,128)(2,1)S(1)} %get-tuple-element.51.x_own, bf16[1024,1024]{1,0:T(8,128)(2,1)S(1)} %get-tuple-element.44.x.x_other, bf16[1024,512]{1,0:T(8,128)(2,1)S(1)} %get-tuple-element.52.wq, ...), custom_call_target="tpu_custom_call" | custom-call | flops 1 | bytes 1 | tf_op jit(solution)/shard_map/query_gate/pallas_call | solution.py:40
  15.6 5.5 %collective-permute-done.5.refs_0_ = bf16[528,256]{1,0:T(8,128)(2,1)S(1)} collective-permute-done((bf16[528,256]{1,0:T(8,128)(2,1)S(1)}, bf16[528,256]{1,0:T(8,128)(2,1)S(1)}, u32[]{:S(2)}, u32[]{:S(2)}) %collective-permute-start.5) | collective-permute-done | bytes 270368 | tf_op jit(solution)/shard_map/ppermute | solution.py:458
  21.2 0.9 %combine.1 = (f32[512,256]{1,0:T(8,128)}, f32[520,256]{1,0:T(8,128)S(1)}, bf16[528,256]{1,0:T(8,128)(2,1)S(1)}) custom-call(f32[512,256]{1,0:T(8,128)S(1)} %get-tuple-element.57.state, bf16[528,256]{1,0:T(8,128)(2,1)S(1)} %get-tuple-element.58.sent, bf16[528,256]{1,0:T(8,128)(2,1)S(1)} %collective-permute-done.5.refs_0_), custom_call_target="tpu_custom_call" | custom-call | flops 1 | bytes 1 | tf_op jit(solution)/shard_map/combine/pallas_call | solution.py:40
  22.1 3.1 %collective-permute-start.6 = (bf16[528,256]{1,0:T(8,128)(2,1)S(1)}, bf16[528,256]{1,0:T(8,128)(2,1)S(1)}, u32[]{:S(2)}, u32[]{:S(2)}) collective-permute-start(bf16[528,256]{1,0:T(8,128)(2,1)S(1)} %get-tuple-element.60), channel_id=1, source_target_pairs={{8,24},{24,8},{9,25},{25,9},{10,26},{26,10},{11,27},{27,11},{12,28... | collective-permute-start | bytes 811016 | tf_op jit(solution)/shard_map/ppermute | solution.py:458
  25.3 2.9 %query_gate.3 = (bf16[512,512]{1,0:T(8,128)(2,1)S(1)}, bf16[512,512]{1,0:T(8,128)(2,1)S(1)}, f32[512,512]{1,0:T(8,128)S(1)}) custom-call(bf16[1024,1024]{1,0:T(8,128)(2,1)S(1)} %get-tuple-element.51.x_own, bf16[1024,1024]{1,0:T(8,128)(2,1)S(1)} %get-tuple-element.44.x.x_other, bf16[1024,512]{1,0:T(8,128)(2,1)S(1)} %get-tuple-element.52.wq, ...), custom_call_target="tpu_custom_call" | custom-call | flops 1 | bytes 1 | tf_op jit(solution)/shard_map/query_gate/pallas_call | solution.py:40
  28.2 4.5 %collective-permute-done.6.refs_0_ = bf16[528,256]{1,0:T(8,128)(2,1)S(1)} collective-permute-done((bf16[528,256]{1,0:T(8,128)(2,1)S(1)}, bf16[528,256]{1,0:T(8,128)(2,1)S(1)}, u32[]{:S(2)}, u32[]{:S(2)}) %collective-permute-start.6) | collective-permute-done | bytes 270368 | tf_op jit(solution)/shard_map/ppermute | solution.py:458
  32.7 1.7 %hidden.3 = (bf16[256,512]{1,0:T(8,128)(2,1)S(1)}, bf16[256,512]{1,0:T(8,128)(2,1)S(1)}, bf16[16,128]{1,0:T(8,128)(2,1)}) custom-call(f32[8,1024]{1,0:T(8,128)S(1)} %get-tuple-element.63.decay, bf16[2,512,256]{2,1,0:T(8,128)(2,1)S(1)} %get-tuple-element.49.before, f32[520,256]{1,0:T(8,128)S(1)} %get-tuple-element.59.entering, ...), custom_call_target="tpu_custom_call" | custom-call | flops 1 | bytes 1 | tf_op jit(solution)/shard_map/hidden/pallas_call | solution.py:40
  34.4 2.0 %collective-permute-start.16 = (bf16[256,512]{1,0:T(8,128)(2,1)S(1)}, bf16[256,512]{1,0:T(8,128)(2,1)S(1)}, u32[]{:S(2)}, u32[]{:S(2)}) collective-permute-start(bf16[256,512]{1,0:T(8,128)(2,1)S(1)} %get-tuple-element.70.refs_3_), channel_id=1, source_target_pairs={{0,2},{2,0},{4,6},{6,4},{1,3},{3,1},{5,7},{7,5},{8,10},{10,8},{12,... | collective-permute-start | bytes 786440 | tf_op jit(solution)/shard_map/ppermute | solution.py:35
  36.4 1.7 %hidden.2 = (bf16[256,512]{1,0:T(8,128)(2,1)S(1)}, bf16[256,512]{1,0:T(8,128)(2,1)S(1)}, bf16[16,128]{1,0:T(8,128)(2,1)}) custom-call(f32[8,1024]{1,0:T(8,128)S(1)} %get-tuple-element.63.decay, bf16[2,512,256]{2,1,0:T(8,128)(2,1)S(1)} %get-tuple-element.49.before, f32[520,256]{1,0:T(8,128)S(1)} %get-tuple-element.59.entering, ...), custom_call_target="tpu_custom_call" | custom-call | flops 1 | bytes 1 | tf_op jit(solution)/shard_map/hidden/pallas_call | solution.py:40
  38.2 0.5 collective-permute-start.12
  38.7 1.6 %collective-permute-start.8 = (bf16[256,512]{1,0:T(8,128)(2,1)S(1)}, bf16[256,512]{1,0:T(8,128)(2,1)S(1)}, u32[]{:S(2)}, u32[]{:S(2)}) collective-permute-start(bf16[256,512]{1,0:T(8,128)(2,1)S(1)} %get-tuple-element.67.refs_0_), channel_id=1, source_target_pairs={{0,4},{2,6},{4,0},{6,2},{1,5},{3,7},{5,1},{7,3},{8,12},{10,14},{12... | collective-permute-start | bytes 786440 | tf_op jit(solution)/shard_map/ppermute | solution.py:35
  40.3 1.3 %own_products.1 = (f32[512,1024]{1,0:T(8,128)S(1)}, f32[512,1024]{1,0:T(8,128)S(1)}) custom-call(bf16[512,1024]{1,0:T(8,128)(2,1)S(1)} %get-tuple-element.72.own_first.first, bf16[512,1024]{1,0:T(8,128)(2,1)S(1)} %collective-permute-done.own_second.second, bf16[256,512]{1,0:T(8,128)(2,1)S(1)} %get-tuple-element.67.refs_0_, ...), custom_call_target="tpu_custom_call" | custom-call | flops 1 | bytes 1 | tf_op jit(solution)/shard_map/own_products/pallas_call | solution.py:40
  41.9 1.7 %collective-permute-done.16.far.refs_3_ = bf16[256,512]{1,0:T(8,128)(2,1)S(1)} collective-permute-done((bf16[256,512]{1,0:T(8,128)(2,1)S(1)}, bf16[256,512]{1,0:T(8,128)(2,1)S(1)}, u32[]{:S(2)}, u32[]{:S(2)}) %collective-permute-start.16) | collective-permute-done | bytes 262176 | tf_op jit(solution)/shard_map/ppermute | solution.py:35
  43.6 0.3 give.7
  43.9 0.5 collective-permute-start.17
  44.4 1.2 %collective-permute-done.14.far.refs_2_ = bf16[256,512]{1,0:T(8,128)(2,1)S(1)} collective-permute-done((bf16[256,512]{1,0:T(8,128)(2,1)S(1)}, bf16[256,512]{1,0:T(8,128)(2,1)S(1)}, u32[]{:S(2)}, u32[]{:S(2)}) %collective-permute-start.14) | collective-permute-done | bytes 262176 | tf_op jit(solution)/shard_map/ppermute | solution.py:35
  45.9 0.4 collective-permute-start.15
  46.3 2.9 %collective-permute-done.12.far.refs_1_ = bf16[256,512]{1,0:T(8,128)(2,1)S(1)} collective-permute-done((bf16[256,512]{1,0:T(8,128)(2,1)S(1)}, bf16[256,512]{1,0:T(8,128)(2,1)S(1)}, u32[]{:S(2)}, u32[]{:S(2)}) %collective-permute-start.12) | collective-permute-done | bytes 262176 | tf_op jit(solution)/shard_map/ppermute | solution.py:35
  49.5 0.5 collective-permute-start.13
  50.0 1.2 %collective-permute-done.8.far.refs_0_ = bf16[256,512]{1,0:T(8,128)(2,1)S(1)} collective-permute-done((bf16[256,512]{1,0:T(8,128)(2,1)S(1)}, bf16[256,512]{1,0:T(8,128)(2,1)S(1)}, u32[]{:S(2)}, u32[]{:S(2)}) %collective-permute-start.8) | collective-permute-done | bytes 262176 | tf_op jit(solution)/shard_map/ppermute | solution.py:35
  51.5 0.4 collective-permute-start.11
  51.9 0.7 %keep.1 = (f32[512,512]{1,0:T(8,128)S(1)}, f32[512,512]{1,0:T(8,128)S(1)}) custom-call(bf16[256,512]{1,0:T(8,128)(2,1)S(1)} %collective-permute-done.8.far.refs_0_, bf16[256,512]{1,0:T(8,128)(2,1)S(1)} %collective-permute-done.12.far.refs_1_, bf16[256,512]{1,0:T(8,128)(2,1)S(1)} %collective-permute-done.14.far.refs_2_, ...), custom_call_target="tpu_custom_call" | custom-call | flops 1 | bytes 1 | tf_op jit(solution)/shard_map/keep/pallas_call | solution.py:40
  52.6 4.2 %collective-permute-done.17.refs_3_ = bf16[256,512]{1,0:T(8,128)(2,1)S(1)} collective-permute-done((bf16[256,512]{1,0:T(8,128)(2,1)S(1)}, bf16[256,512]{1,0:T(8,128)(2,1)S(1)}, u32[]{:S(2)}, u32[]{:S(2)}) %collective-permute-start.17) | collective-permute-done | bytes 262176 | tf_op jit(solution)/shard_map/ppermute | solution.py:35
  56.8 4.9 %collective-permute-done.13.refs_1_ = bf16[256,512]{1,0:T(8,128)(2,1)S(1)} collective-permute-done((bf16[256,512]{1,0:T(8,128)(2,1)S(1)}, bf16[256,512]{1,0:T(8,128)(2,1)S(1)}, u32[]{:S(2)}, u32[]{:S(2)}) %collective-permute-start.13) | collective-permute-done | bytes 262176 | tf_op jit(solution)/shard_map/ppermute | solution.py:35
  61.7 1.1 %finish.1 = bf16[1,1024,512]{2,1,0:T(8,128)(2,1)} custom-call(bf16[256,512]{1,0:T(8,128)(2,1)S(1)} %collective-permute-done.11.refs_0_, bf16[256,512]{1,0:T(8,128)(2,1)S(1)} %collective-permute-done.13.refs_1_, bf16[256,512]{1,0:T(8,128)(2,1)S(1)} %collective-permute-done.15.refs_2_, bf16[256,512]{1,0:T(8,128)(2,1)S(1)} %collective-permute-done.17.refs_3_, ...), custom_call_target="tpu_custom_call" | custom-call | tf_op jit(solution)/shard_map/finish/pallas_call | solution.py:540
  (20 shorter events, 1.5 us)
Async XLA Ops:
  0.0 5.5 %collective-permute-start.1 = (bf16[1024,512]{1,0:T(8,128)(2,1)}, bf16[1024,512]{1,0:T(8,128)(2,1)S(1)}, u32[]{:S(2)}, u32[]{:S(2)}) collective-permute-start(bf16[1024,512]{1,0:T(8,128)(2,1)} %wk_far.1), channel_id=1, source_target_pairs={{0,1},{1,0},{2,3},{3,2},{4,5},{5,4},{6,7},{7,6},{8,9},{9,8},{10,11... | collective-permute-start | bytes 3145736 | tf_op jit(solution)/shard_map/ppermute | solution.py:35
  0.0 5.5 %collective-permute-start.2 = (bf16[1024,512]{1,0:T(8,128)(2,1)}, bf16[1024,512]{1,0:T(8,128)(2,1)S(1)}, u32[]{:S(2)}, u32[]{:S(2)}) collective-permute-start(bf16[1024,512]{1,0:T(8,128)(2,1)} %wv_far.1), channel_id=1, source_target_pairs={{0,1},{1,0},{2,3},{3,2},{4,5},{5,4},{6,7},{7,6},{8,9},{9,8},{10,11... | collective-permute-start | bytes 3145736 | tf_op jit(solution)/shard_map/ppermute | solution.py:35
  4.9 4.1 %collective-permute-start = (bf16[512,1024]{1,0:T(8,128)(2,1)S(1)}, bf16[512,1024]{1,0:T(8,128)(2,1)S(1)}, u32[]{:S(2)}, u32[]{:S(2)}) collective-permute-start(bf16[512,1024]{1,0:T(8,128)(2,1)S(1)} %get-tuple-element.72.own_first.first), channel_id=1, source_target_pairs={{0,1},{1,0},{2,3},{3,2},{4,5},{5,4},{6,7},{7,6},{8,9},{9,8},{10,11... | collective-permute-start | bytes 3145736 | tf_op jit(solution)/shard_map/ppermute | solution.py:35
  4.9 7.7 %collective-permute-start.3 = (bf16[1024,512]{1,0:T(8,128)(2,1)S(1)}, bf16[1024,512]{1,0:T(8,128)(2,1)S(1)}, u32[]{:S(2)}, u32[]{:S(2)}) collective-permute-start(bf16[1024,512]{1,0:T(8,128)(2,1)S(1)} %get-tuple-element.52.wq), channel_id=1, source_target_pairs={{0,1},{1,0},{2,3},{3,2},{4,5},{5,4},{6,7},{7,6},{8,9},{9,8},{10,11... | collective-permute-start | bytes 3145736 | tf_op jit(solution)/shard_map/ppermute | solution.py:35
  5.4 7.2 %collective-permute-start.4 = (bf16[1024,512]{1,0:T(8,128)(2,1)S(1)}, bf16[1024,512]{1,0:T(8,128)(2,1)S(1)}, u32[]{:S(2)}, u32[]{:S(2)}) collective-permute-start(bf16[1024,512]{1,0:T(8,128)(2,1)S(1)} %get-tuple-element.53.wg), channel_id=1, source_target_pairs={{0,1},{1,0},{2,3},{3,2},{4,5},{5,4},{6,7},{7,6},{8,9},{9,8},{10,11... | collective-permute-start | bytes 3145736 | tf_op jit(solution)/shard_map/ppermute | solution.py:35
  9.1 25.3 %collective-permute-start.9 = (bf16[512,1024]{1,0:T(8,128)(2,1)S(1)}, bf16[512,1024]{1,0:T(8,128)(2,1)S(1)}, u32[]{:S(2)}, u32[]{:S(2)}) collective-permute-start(bf16[512,1024]{1,0:T(8,128)(2,1)S(1)} %columns.1), channel_id=1, source_target_pairs={{0,2},{1,5},{2,0},{3,7},{4,6},{5,1},{6,4},{7,3},{8,10},{9,13},{10,... | collective-permute-start | bytes 3145736 | tf_op jit(solution)/shard_map/ppermute | solution.py:489
  10.7 10.5 %collective-permute-start.5 = (bf16[528,256]{1,0:T(8,128)(2,1)S(1)}, bf16[528,256]{1,0:T(8,128)(2,1)S(1)}, u32[]{:S(2)}, u32[]{:S(2)}) collective-permute-start(bf16[528,256]{1,0:T(8,128)(2,1)S(1)} %get-tuple-element.58.sent), channel_id=1, source_target_pairs={{0,8},{8,16},{16,24},{1,9},{9,17},{17,25},{2,10},{10,18},{18,26},{... | collective-permute-start | bytes 811016 | tf_op jit(solution)/shard_map/ppermute | solution.py:458
  12.0 13.3 %collective-permute-start.7 = (bf16[528,256]{1,0:T(8,128)(2,1)S(1)}, bf16[528,256]{1,0:T(8,128)(2,1)S(1)}, u32[]{:S(2)}, u32[]{:S(2)}) collective-permute-start(bf16[528,256]{1,0:T(8,128)(2,1)S(1)} %get-tuple-element.58.sent), channel_id=1, source_target_pairs={{0,16},{16,0},{1,17},{17,1},{2,18},{18,2},{3,19},{19,3},{4,20},{20... | collective-permute-start | bytes 811016 | tf_op jit(solution)/shard_map/ppermute | solution.py:458
  22.1 10.6 %collective-permute-start.6 = (bf16[528,256]{1,0:T(8,128)(2,1)S(1)}, bf16[528,256]{1,0:T(8,128)(2,1)S(1)}, u32[]{:S(2)}, u32[]{:S(2)}) collective-permute-start(bf16[528,256]{1,0:T(8,128)(2,1)S(1)} %get-tuple-element.60), channel_id=1, source_target_pairs={{8,24},{24,8},{9,25},{25,9},{10,26},{26,10},{11,27},{27,11},{12,28... | collective-permute-start | bytes 811016 | tf_op jit(solution)/shard_map/ppermute | solution.py:458
  34.4 7.1 %collective-permute-start.10 = (bf16[512,1024]{1,0:T(8,128)(2,1)S(1)}, bf16[512,1024]{1,0:T(8,128)(2,1)S(1)}, u32[]{:S(2)}, u32[]{:S(2)}) collective-permute-start(bf16[512,1024]{1,0:T(8,128)(2,1)S(1)} %collective-permute-done.9.mine), channel_id=1, source_target_pairs={{0,1},{1,0},{2,3},{3,2},{4,5},{5,4},{6,7},{7,6},{8,9},{9,8},{10,11... | collective-permute-start | bytes 3145736 | tf_op jit(solution)/shard_map/ppermute | solution.py:35
  34.4 9.2 %collective-permute-start.16 = (bf16[256,512]{1,0:T(8,128)(2,1)S(1)}, bf16[256,512]{1,0:T(8,128)(2,1)S(1)}, u32[]{:S(2)}, u32[]{:S(2)}) collective-permute-start(bf16[256,512]{1,0:T(8,128)(2,1)S(1)} %get-tuple-element.70.refs_3_), channel_id=1, source_target_pairs={{0,2},{2,0},{4,6},{6,4},{1,3},{3,1},{5,7},{7,5},{8,10},{10,8},{12,... | collective-permute-start | bytes 786440 | tf_op jit(solution)/shard_map/ppermute | solution.py:35
  36.4 9.1 %collective-permute-start.14 = (bf16[256,512]{1,0:T(8,128)(2,1)S(1)}, bf16[256,512]{1,0:T(8,128)(2,1)S(1)}, u32[]{:S(2)}, u32[]{:S(2)}) collective-permute-start(bf16[256,512]{1,0:T(8,128)(2,1)S(1)} %get-tuple-element.69.refs_2_), channel_id=1, source_target_pairs={{0,4},{2,6},{4,0},{6,2},{1,5},{3,7},{5,1},{7,3},{8,12},{10,14},{12... | collective-permute-start | bytes 786440 | tf_op jit(solution)/shard_map/ppermute | solution.py:35
  38.2 11.0 %collective-permute-start.12 = (bf16[256,512]{1,0:T(8,128)(2,1)S(1)}, bf16[256,512]{1,0:T(8,128)(2,1)S(1)}, u32[]{:S(2)}, u32[]{:S(2)}) collective-permute-start(bf16[256,512]{1,0:T(8,128)(2,1)S(1)} %get-tuple-element.68.refs_1_), channel_id=1, source_target_pairs={{0,2},{2,0},{4,6},{6,4},{1,3},{3,1},{5,7},{7,5},{8,10},{10,8},{12,... | collective-permute-start | bytes 786440 | tf_op jit(solution)/shard_map/ppermute | solution.py:35
  38.7 12.5 %collective-permute-start.8 = (bf16[256,512]{1,0:T(8,128)(2,1)S(1)}, bf16[256,512]{1,0:T(8,128)(2,1)S(1)}, u32[]{:S(2)}, u32[]{:S(2)}) collective-permute-start(bf16[256,512]{1,0:T(8,128)(2,1)S(1)} %get-tuple-element.67.refs_0_), channel_id=1, source_target_pairs={{0,4},{2,6},{4,0},{6,2},{1,5},{3,7},{5,1},{7,3},{8,12},{10,14},{12... | collective-permute-start | bytes 786440 | tf_op jit(solution)/shard_map/ppermute | solution.py:35
  43.9 12.9 %collective-permute-start.17 = (bf16[256,512]{1,0:T(8,128)(2,1)S(1)}, bf16[256,512]{1,0:T(8,128)(2,1)S(1)}, u32[]{:S(2)}, u32[]{:S(2)}) collective-permute-start(bf16[256,512]{1,0:T(8,128)(2,1)S(1)} %give.7), channel_id=1, source_target_pairs={{0,4},{2,6},{4,0},{6,2},{1,5},{3,7},{5,1},{7,3},{8,12},{10,14},{12... | collective-permute-start | bytes 786440 | tf_op jit(solution)/shard_map/ppermute | solution.py:35
  45.9 10.9 %collective-permute-start.15 = (bf16[256,512]{1,0:T(8,128)(2,1)S(1)}, bf16[256,512]{1,0:T(8,128)(2,1)S(1)}, u32[]{:S(2)}, u32[]{:S(2)}) collective-permute-start(bf16[256,512]{1,0:T(8,128)(2,1)S(1)} %give.6), channel_id=1, source_target_pairs={{0,2},{2,0},{4,6},{6,4},{1,3},{3,1},{5,7},{7,5},{8,10},{10,8},{12,... | collective-permute-start | bytes 786440 | tf_op jit(solution)/shard_map/ppermute | solution.py:35
  49.5 12.2 %collective-permute-start.13 = (bf16[256,512]{1,0:T(8,128)(2,1)S(1)}, bf16[256,512]{1,0:T(8,128)(2,1)S(1)}, u32[]{:S(2)}, u32[]{:S(2)}) collective-permute-start(bf16[256,512]{1,0:T(8,128)(2,1)S(1)} %give.5), channel_id=1, source_target_pairs={{0,4},{2,6},{4,0},{6,2},{1,5},{3,7},{5,1},{7,3},{8,12},{10,14},{12... | collective-permute-start | bytes 786440 | tf_op jit(solution)/shard_map/ppermute | solution.py:35
  51.5 10.2 %collective-permute-start.11 = (bf16[256,512]{1,0:T(8,128)(2,1)S(1)}, bf16[256,512]{1,0:T(8,128)(2,1)S(1)}, u32[]{:S(2)}, u32[]{:S(2)}) collective-permute-start(bf16[256,512]{1,0:T(8,128)(2,1)S(1)} %give.4), channel_id=1, source_target_pairs={{0,2},{2,0},{4,6},{6,4},{1,3},{3,1},{5,7},{7,5},{8,10},{10,8},{12,... | collective-permute-start | bytes 786440 | tf_op jit(solution)/shard_map/ppermute | solution.py:35

commit v11 on v10

--- a/solution.py
+++ b/solution.py
@@ -163,15 +163,17 @@
     value = loads.start(wv_far, wv)
     others = [tile(x_other, 1 - core, start) for start in starts]
     others += [loads.start(wo_far, wo), loads.start(wq_far, wq), loads.start(wg_far, wg)]
-    angle_tables(coarse, fine)
-    logs.wait()
-    decay_sums(log_decay, decay)
     key.wait()
-    for copy, start in zip(tiles, starts):
+    tiles[0].wait()
+    for number, start in enumerate(starts):
         at = slice(start, start + BLOCK)
-        copy.wait()
+        if number:
+            tiles[number].wait()
         acc_k[at, :] = mm(x_own[at, :], wk[...])
     value.wait()
+    logs.wait()
+    angle_tables(coarse, fine)
+    decay_sums(log_decay, decay)
     for start in starts:
         at = slice(start, start + BLOCK)
         acc_v[at, :] = mm(x_own[at, :], wv[...])
@@ -231,12 +233,13 @@
 ):
     state_out[...] = jnp.zeros_like(state_out)
 
-    def block_step(block, totals):
-        start = pl.multiple_of(block * BLOCK, BLOCK)
-        columns = decay[:, pl.ds(start, BLOCK)].T
+    totals = jnp.zeros((1, 8), F32)
+    for block in range(x.shape[0] // BLOCK):
+        start = block * BLOCK
+        columns = decay[:, slice(start, start + BLOCK)].T
         ending = columns[BLOCK - 1 : BLOCK, :]
         faded = jnp.exp(ending - columns)
-        at = pl.ds(start, BLOCK)
+        at = slice(start, start + BLOCK)
         cosine, sine = angles(coarse, fine, start, BLOCK)
         keys = turned(acc_k[at, :] + mm(x[at, :], wk[...]), cosine, sine)
         k_out[at, :] = keys
@@ -248,9 +251,7 @@
             old = state_out[span, :]
             before_out[block, span, :] = old.astype(BF16)
             state_out[span, :] = jnp.exp(ending[:, head : head + 1]) * old + mm_tn(weighted, values[:, span])
-        return totals + ending
-
-    totals = lax.fori_loop(0, x.shape[0] // BLOCK, block_step, jnp.zeros((1, 8), F32))
+        totals = totals + ending
     states = [state_out[head * DH : (head + 1) * DH, :] for head in range(heads)]
     pack_message(message, states, [totals[:, head : head + 1] for head in range(heads)])
 
@@ -292,7 +293,8 @@
     at = slice(start, start + BLOCK)
     cosine, sine = angles(coarse, fine, start, BLOCK)
     q_out[...] = turned(mm(x_own[at, :], wq[...]) + mm(x_other[at, :], wq_far[...]), cosine, sine)
-    g_out[...] = (mm(x_own[at, :], wg[...]) + mm(x_other[at, :], wg_far[...])).astype(BF16)
+    gates = (mm(x_own[at, :], wg[...]) + mm(x_other[at, :], wg_far[...])).astype(BF16).astype(F32)
+    g_out[...] = gates / (1.0 + jnp.exp(-gates))
     for piece in range(BLOCK // TILE):
         low, last = piece * TILE, (piece + 1) * TILE
         place_t = lax.broadcasted_iota(jnp.int32, (TILE, last), 0) + low
@@ -327,9 +329,7 @@
             retained = intra[at, span] + column * mm(q[at, span], prior)
             center = retained - jnp.mean(retained, axis=1, keepdims=True)
             spread = jnp.mean(center * center, axis=1, keepdims=True)
-            value = gate[at, span].astype(F32)
-            silu = value / (1.0 + jnp.exp(-value))
-            out[:, span] = (silu * center * lax.rsqrt(spread + 1e-5)).astype(BF16)
+            out[:, span] = (gate[at, span] * center * lax.rsqrt(spread + 1e-5)).astype(BF16)
 
 
 def columns_kernel(first, second, out):
@@ -393,13 +393,18 @@
 
 
 def finish_kernel(order, *refs):
-    gots, keeps, out = refs[: len(order)], refs[len(order) : -1], refs[-1]
-    for (half, number), got in zip(order, gots):
+    count = len(order)
+    gots, keeps, out, ready, written = refs[:count], refs[count : count + 2], refs[-3], refs[-2], refs[-1]
+    copies = []
+    for slot, ((half, number), got) in enumerate(zip(order, gots)):
         keep = keeps[half]
         at = slice(number * TILE, (number + 1) * TILE)
-        value = keep[at, :] + got[...].astype(F32)
+        ready[slot] = (keep[at, :] + got[...].astype(F32)).astype(BF16)
         start = half * keep.shape[0] + number * TILE
-        out[0, start : start + TILE, :] = value.astype(BF16)
+        copies.append(pltpu.make_async_copy(ready.at[slot], out.at[0, pl.ds(start, TILE)], written.at[slot]))
+        copies[-1].start()
+    for copy in copies:
+        copy.wait()
 
 
 def after(value, *others):
@@ -446,7 +451,7 @@
     def query_gate(block, decay):
         return kernel_call(
             functools.partial(query_gate_kernel, heads, block),
-            [((BLOCK, cols), BF16), ((BLOCK, cols), BF16), ((BLOCK, cols), F32)],
+            [((BLOCK, cols), BF16), ((BLOCK, cols), F32), ((BLOCK, cols), F32)],
             [x_own, x_other, own_q, far_q, own_g, far_g, decay, coarse, fine, keys, values],
             "query_gate",
         )
@@ -536,15 +541,25 @@
         [*(far[half][number] for half, number in order), *owns, *weights],
         "keep",
     )
-    arrays = [pltpu.with_memory_space_constraint(array, pltpu.VMEM) for array in (*gots, *keeps)]
-    return pl.pallas_call(
-        functools.partial(finish_kernel, order),
-        in_specs=[pl.BlockSpec(memory_space=pltpu.VMEM)] * len(arrays),
-        out_specs=pl.BlockSpec(memory_space=pltpu.VMEM),
-        out_shape=jax.ShapeDtypeStruct((1, rows, cols), BF16),
-        compiler_params=pltpu.CompilerParams(vmem_limit_bytes=VMEM_LIMIT),
-        name="finish",
-    )(*arrays)
+    result = None
+    for part_order, part_gots in ((order[2:], gots[2:]), (order[:2], gots[:2])):
+        arrays = [pltpu.with_memory_space_constraint(array, pltpu.VMEM) for array in (*part_gots, *keeps)]
+        held = [] if result is None else [result]
+        result = pl.pallas_call(
+            functools.partial(finish_kernel, part_order),
+            in_specs=[pl.BlockSpec(memory_space=pltpu.VMEM)] * len(arrays)
+            + [pl.BlockSpec(memory_space=pltpu.HBM)] * len(held),
+            out_specs=pl.BlockSpec(memory_space=pltpu.HBM),
+            out_shape=jax.ShapeDtypeStruct((1, rows, cols), BF16),
+            input_output_aliases={len(arrays): 0} if held else {},
+            scratch_shapes=[
+                pltpu.VMEM((len(part_order), TILE, cols), BF16),
+                pltpu.SemaphoreType.DMA((len(part_order),)),
+            ],
+            compiler_params=pltpu.CompilerParams(vmem_limit_bytes=VMEM_LIMIT),
+            name="finish",
+        )(*arrays, *held)
+    return result
 
 
 def solution(mesh):

time: 63.3 us -> 62.9 us (level)
  waiting for transfers between devices: 26.2 us -> 25.3 us
    ppermute x14, waiting for transfers between devices: 16.1 us -> 15.4 us  [swap(): lax.ppermute(value, axis, [(place, place ^ mask) for place in range(size)])]
    pallas_call x1 -> x2, Pallas kernels: 1.14 us -> 1.72 us  [on_device(): pl.pallas_call(functools.partial(finish_kernel, part_order), in_specs=[pl...]
  transfers between devices with their start and end apart: 18 -> 18, of which waited for: 8 -> 8; matrix products, arithmetic and copies ran while one was open for 0% -> 0% of each run, Pallas kernels for 35% -> 36%
where the time goes in v11:
time: 62.9 us; the launch traced here: 62.5 us
  waiting for transfers between devices  25.3 us (40%)
  Pallas kernels  23.1 us (37%)
  starting transfers between devices  13.8 us (22%)
    pallas_call x14, Pallas kernels, kernel_call(): pl.pallas_call(kernel, in_specs=[pl.BlockSpec(memory_space=pltpu.VMEM)] *...  16.9 us
    ppermute x14, waiting for transfers between devices, swap(): lax.ppermute(value, axis, [(place, place ^ mask) for place in range(size)])  15.4 us
    ppermute x3, waiting for transfers between devices, exchange(): return lax.ppermute(message, 'ctx', pairs)  9.85 us
    ppermute x14, starting transfers between devices, swap(): lax.ppermute(value, axis, [(place, place ^ mask) for place in range(size)])  7.19 us
    ppermute x3, starting transfers between devices, exchange(): return lax.ppermute(message, 'ctx', pairs)  5.06 us
    pallas_call x1, Pallas kernels, loading_call(): pl.pallas_call(kernel, in_specs=[pl.BlockSpec(memory_space=pltpu.HBM)] *...  4.44 us
    pallas_call x2, Pallas kernels, on_device(): pl.pallas_call(functools.partial(finish_kernel, part_order), in_specs=[pl...  1.72 us
    ppermute x1, starting transfers between devices, on_device(): out_mine = lax.ppermute(for_partner, ('tp', 'fsdp'), pairs)  1.55 us
  transfers between devices with their start and end apart: 18, of which 8 were waited for; matrix products, arithmetic and copies ran while one was open for 0% of the time, Pallas kernels for 36%

profile of v11, /device:TPU:24, one launch (start us, length us, event | category | flops | bytes accessed | tf_op | source)
XLA Modules:
  0.0 62.5 jit_solution(14746791865137586094)
XLA Ops:
  0.0 0.5 collective-permute-start.2
  0.5 4.4 %key_value_own.1 = (bf16[1024,1024]{1,0:T(8,128)(2,1)S(1)}, bf16[1024,1024]{1,0:T(8,128)(2,1)S(1)}, f32[1024,512]{1,0:T(8,128)S(1)}, f32[1024,512]{1,0:T(8,128)S...) custom-call(bf16[1024,2048]{1,0:T(8,128)(2,1)} %bitcast.4, ...), custom_call_target="tpu_custom_call" | custom-call | flops 1 | bytes 1 | tf_op jit(solution)/shard_map/key_value_own/pallas_call | solution.py:56
  5.0 0.5 collective-permute-start.3
  5.6 3.3 %key_value.1 = (bf16[1024,512]{1,0:T(8,128)(2,1)S(1)}, bf16[1024,512]{1,0:T(8,128)(2,1)S(1)}, bf16[2,512,256]{2,1,0:T(8,128)(2,1)S(1)}, f32[512,256]{1,0:T(8,128)S(1)}, bf16[528,256]{1,0:T(8,128)(2,1)S(1)}) custom-call(bf16[1024,1024]{1,0:T(8,128)(2,1)S(1)} %get-tuple-element.44.x.x_other, bf16[1024,512]{1,0:T(8,128)(2,1)S(1)} %collective-permute-done.1.wk, ...), custom_call_target="tpu_custom_call" | custom-call | flops 1 | bytes 1 | tf_op jit(solution)/shard_map/key_value/pallas_call | solution.py:40
  9.0 1.6 %collective-permute-start.9 = (bf16[512,1024]{1,0:T(8,128)(2,1)S(1)}, bf16[512,1024]{1,0:T(8,128)(2,1)S(1)}, u32[]{:S(2)}, u32[]{:S(2)}) collective-permute-start(bf16[512,1024]{1,0:T(8,128)(2,1)S(1)} %columns.1), channel_id=1, source_target_pairs={{0,2},{1,5},{2,0},{3,7},{4,6},{5,1},{6,4},{7,3},{8,10},{9,13},{10,... | collective-permute-start | bytes 3145736 | tf_op jit(solution)/shard_map/ppermute | solution.py:494
  10.6 1.3 %collective-permute-start.5 = (bf16[528,256]{1,0:T(8,128)(2,1)S(1)}, bf16[528,256]{1,0:T(8,128)(2,1)S(1)}, u32[]{:S(2)}, u32[]{:S(2)}) collective-permute-start(bf16[528,256]{1,0:T(8,128)(2,1)S(1)} %get-tuple-element.58.sent), channel_id=1, source_target_pairs={{0,8},{8,16},{16,24},{1,9},{9,17},{17,25},{2,10},{10,18},{18,26},{... | collective-permute-start | bytes 811016 | tf_op jit(solution)/shard_map/ppermute | solution.py:463
  11.9 0.7 %collective-permute-start.7 = (bf16[528,256]{1,0:T(8,128)(2,1)S(1)}, bf16[528,256]{1,0:T(8,128)(2,1)S(1)}, u32[]{:S(2)}, u32[]{:S(2)}) collective-permute-start(bf16[528,256]{1,0:T(8,128)(2,1)S(1)} %get-tuple-element.58.sent), channel_id=1, source_target_pairs={{0,16},{16,0},{1,17},{17,1},{2,18},{18,2},{3,19},{19,3},{4,20},{20... | collective-permute-start | bytes 811016 | tf_op jit(solution)/shard_map/ppermute | solution.py:463
  12.6 3.0 %query_gate.2 = (bf16[512,512]{1,0:T(8,128)(2,1)S(1)}, f32[512,512]{1,0:T(8,128)S(1)}, f32[512,512]{1,0:T(8,128)S(1)}) custom-call(bf16[1024,1024]{1,0:T(8,128)(2,1)S(1)} %get-tuple-element.51.x_own, bf16[1024,1024]{1,0:T(8,128)(2,1)S(1)} %get-tuple-element.44.x.x_other, bf16[1024,512]{1,0:T(8,128)(2,1)S(1)} %get-tuple-element.52.wq, ...), custom_call_target="tpu_custom_call" | custom-call | flops 1 | bytes 1 | tf_op jit(solution)/shard_map/query_gate/pallas_call | solution.py:40
  15.6 5.5 %collective-permute-done.5.refs_0_ = bf16[528,256]{1,0:T(8,128)(2,1)S(1)} collective-permute-done((bf16[528,256]{1,0:T(8,128)(2,1)S(1)}, bf16[528,256]{1,0:T(8,128)(2,1)S(1)}, u32[]{:S(2)}, u32[]{:S(2)}) %collective-permute-start.5) | collective-permute-done | bytes 270368 | tf_op jit(solution)/shard_map/ppermute | solution.py:463
  21.1 0.9 %combine.1 = (f32[512,256]{1,0:T(8,128)}, f32[520,256]{1,0:T(8,128)S(1)}, bf16[528,256]{1,0:T(8,128)(2,1)S(1)}) custom-call(f32[512,256]{1,0:T(8,128)S(1)} %get-tuple-element.57.state, bf16[528,256]{1,0:T(8,128)(2,1)S(1)} %get-tuple-element.58.sent, bf16[528,256]{1,0:T(8,128)(2,1)S(1)} %collective-permute-done.5.refs_0_), custom_call_target="tpu_custom_call" | custom-call | flops 1 | bytes 1 | tf_op jit(solution)/shard_map/combine/pallas_call | solution.py:40
  22.0 3.1 %collective-permute-start.6 = (bf16[528,256]{1,0:T(8,128)(2,1)S(1)}, bf16[528,256]{1,0:T(8,128)(2,1)S(1)}, u32[]{:S(2)}, u32[]{:S(2)}) collective-permute-start(bf16[528,256]{1,0:T(8,128)(2,1)S(1)} %get-tuple-element.60), channel_id=1, source_target_pairs={{8,24},{24,8},{9,25},{25,9},{10,26},{26,10},{11,27},{27,11},{12,28... | collective-permute-start | bytes 811016 | tf_op jit(solution)/shard_map/ppermute | solution.py:463
  25.1 3.1 %query_gate.3 = (bf16[512,512]{1,0:T(8,128)(2,1)S(1)}, f32[512,512]{1,0:T(8,128)S(1)}, f32[512,512]{1,0:T(8,128)S(1)}) custom-call(bf16[1024,1024]{1,0:T(8,128)(2,1)S(1)} %get-tuple-element.51.x_own, bf16[1024,1024]{1,0:T(8,128)(2,1)S(1)} %get-tuple-element.44.x.x_other, bf16[1024,512]{1,0:T(8,128)(2,1)S(1)} %get-tuple-element.52.wq, ...), custom_call_target="tpu_custom_call" | custom-call | flops 1 | bytes 1 | tf_op jit(solution)/shard_map/query_gate/pallas_call | solution.py:40
  28.2 4.4 %collective-permute-done.6.refs_0_ = bf16[528,256]{1,0:T(8,128)(2,1)S(1)} collective-permute-done((bf16[528,256]{1,0:T(8,128)(2,1)S(1)}, bf16[528,256]{1,0:T(8,128)(2,1)S(1)}, u32[]{:S(2)}, u32[]{:S(2)}) %collective-permute-start.6) | collective-permute-done | bytes 270368 | tf_op jit(solution)/shard_map/ppermute | solution.py:463
  32.6 1.5 %hidden.3 = (bf16[256,512]{1,0:T(8,128)(2,1)S(1)}, bf16[256,512]{1,0:T(8,128)(2,1)S(1)}, bf16[16,128]{1,0:T(8,128)(2,1)}) custom-call(f32[8,1024]{1,0:T(8,128)S(1)} %get-tuple-element.63.decay, bf16[2,512,256]{2,1,0:T(8,128)(2,1)S(1)} %get-tuple-element.49.before, f32[520,256]{1,0:T(8,128)S(1)} %get-tuple-element.59.entering, ...), custom_call_target="tpu_custom_call" | custom-call | flops 1 | bytes 1 | tf_op jit(solution)/shard_map/hidden/pallas_call | solution.py:40
  34.2 2.0 %collective-permute-start.15 = (bf16[256,512]{1,0:T(8,128)(2,1)S(1)}, bf16[256,512]{1,0:T(8,128)(2,1)S(1)}, u32[]{:S(2)}, u32[]{:S(2)}) collective-permute-start(bf16[256,512]{1,0:T(8,128)(2,1)S(1)} %get-tuple-element.70.refs_3_), channel_id=1, source_target_pairs={{0,2},{2,0},{4,6},{6,4},{1,3},{3,1},{5,7},{7,5},{8,10},{10,8},{12,... | collective-permute-start | bytes 786440 | tf_op jit(solution)/shard_map/ppermute | solution.py:35
  36.2 1.5 %hidden.2 = (bf16[256,512]{1,0:T(8,128)(2,1)S(1)}, bf16[256,512]{1,0:T(8,128)(2,1)S(1)}, bf16[16,128]{1,0:T(8,128)(2,1)}) custom-call(f32[8,1024]{1,0:T(8,128)S(1)} %get-tuple-element.63.decay, bf16[2,512,256]{2,1,0:T(8,128)(2,1)S(1)} %get-tuple-element.49.before, f32[520,256]{1,0:T(8,128)S(1)} %get-tuple-element.59.entering, ...), custom_call_target="tpu_custom_call" | custom-call | flops 1 | bytes 1 | tf_op jit(solution)/shard_map/hidden/pallas_call | solution.py:40
  37.7 0.6 collective-permute-start.12
  38.3 1.6 %collective-permute-start.8 = (bf16[256,512]{1,0:T(8,128)(2,1)S(1)}, bf16[256,512]{1,0:T(8,128)(2,1)S(1)}, u32[]{:S(2)}, u32[]{:S(2)}) collective-permute-start(bf16[256,512]{1,0:T(8,128)(2,1)S(1)} %get-tuple-element.67.refs_0_), channel_id=1, source_target_pairs={{0,4},{2,6},{4,0},{6,2},{1,5},{3,7},{5,1},{7,3},{8,12},{10,14},{12... | collective-permute-start | bytes 786440 | tf_op jit(solution)/shard_map/ppermute | solution.py:35
  39.9 1.3 %own_products.1 = (f32[512,1024]{1,0:T(8,128)S(1)}, f32[512,1024]{1,0:T(8,128)S(1)}) custom-call(bf16[512,1024]{1,0:T(8,128)(2,1)S(1)} %get-tuple-element.72.own_first.first, bf16[512,1024]{1,0:T(8,128)(2,1)S(1)} %collective-permute-done.own_second.second, bf16[256,512]{1,0:T(8,128)(2,1)S(1)} %get-tuple-element.67.refs_0_, ...), custom_call_target="tpu_custom_call" | custom-call | flops 1 | bytes 1 | tf_op jit(solution)/shard_map/own_products/pallas_call | solution.py:40
  41.5 1.9 %collective-permute-done.15.refs_3_.far = bf16[256,512]{1,0:T(8,128)(2,1)S(1)} collective-permute-done((bf16[256,512]{1,0:T(8,128)(2,1)S(1)}, bf16[256,512]{1,0:T(8,128)(2,1)S(1)}, u32[]{:S(2)}, u32[]{:S(2)}) %collective-permute-start.15) | collective-permute-done | bytes 262176 | tf_op jit(solution)/shard_map/ppermute | solution.py:35
  43.7 0.5 collective-permute-start.17
  44.2 1.2 %collective-permute-done.14.refs_2_.far = bf16[256,512]{1,0:T(8,128)(2,1)S(1)} collective-permute-done((bf16[256,512]{1,0:T(8,128)(2,1)S(1)}, bf16[256,512]{1,0:T(8,128)(2,1)S(1)}, u32[]{:S(2)}, u32[]{:S(2)}) %collective-permute-start.14) | collective-permute-done | bytes 262176 | tf_op jit(solution)/shard_map/ppermute | solution.py:35
  45.7 0.4 collective-permute-start.16
  46.1 2.9 %collective-permute-done.12.far.refs_1_ = bf16[256,512]{1,0:T(8,128)(2,1)S(1)} collective-permute-done((bf16[256,512]{1,0:T(8,128)(2,1)S(1)}, bf16[256,512]{1,0:T(8,128)(2,1)S(1)}, u32[]{:S(2)}, u32[]{:S(2)}) %collective-permute-start.12) | collective-permute-done | bytes 262176 | tf_op jit(solution)/shard_map/ppermute | solution.py:35
  49.4 0.5 collective-permute-start.13
  49.8 1.2 %collective-permute-done.8.far.refs_0_ = bf16[256,512]{1,0:T(8,128)(2,1)S(1)} collective-permute-done((bf16[256,512]{1,0:T(8,128)(2,1)S(1)}, bf16[256,512]{1,0:T(8,128)(2,1)S(1)}, u32[]{:S(2)}, u32[]{:S(2)}) %collective-permute-start.8) | collective-permute-done | bytes 262176 | tf_op jit(solution)/shard_map/ppermute | solution.py:35
  51.3 0.4 collective-permute-start.11
  51.7 0.7 %keep.1 = (f32[512,512]{1,0:T(8,128)S(1)}, f32[512,512]{1,0:T(8,128)S(1)}) custom-call(bf16[256,512]{1,0:T(8,128)(2,1)S(1)} %collective-permute-done.8.far.refs_0_, bf16[256,512]{1,0:T(8,128)(2,1)S(1)} %collective-permute-done.12.far.refs_1_, bf16[256,512]{1,0:T(8,128)(2,1)S(1)} %collective-permute-done.14.refs_2_.far, ...), custom_call_target="tpu_custom_call" | custom-call | flops 1 | bytes 1 | tf_op jit(solution)/shard_map/keep/pallas_call | solution.py:40
  52.5 4.2 %collective-permute-done.17.refs_1_ = bf16[256,512]{1,0:T(8,128)(2,1)S(1)} collective-permute-done((bf16[256,512]{1,0:T(8,128)(2,1)S(1)}, bf16[256,512]{1,0:T(8,128)(2,1)S(1)}, u32[]{:S(2)}, u32[]{:S(2)}) %collective-permute-start.17) | collective-permute-done | bytes 262176 | tf_op jit(solution)/shard_map/ppermute | solution.py:35
  56.6 0.9 %finish.2.refs_4_ = bf16[1,1024,512]{2,1,0:T(8,128)(2,1)} custom-call(bf16[256,512]{1,0:T(8,128)(2,1)S(1)} %collective-permute-done.16.refs_0_, bf16[256,512]{1,0:T(8,128)(2,1)S(1)} %collective-permute-done.17.refs_1_, f32[512,512]{1,0:T(8,128)S(1)} %get-tuple-element.77.refs_2_, f32[512,512]{1,0:T(8,128)S(1)} %get-tuple-element.78.refs_3_), custom_call_target="tpu_custom_call" | custom-call | tf_op jit(solution)/shard_map/finish/pallas_call | solution.py:548
  57.5 4.0 %collective-permute-done.13.refs_1_ = bf16[256,512]{1,0:T(8,128)(2,1)S(1)} collective-permute-done((bf16[256,512]{1,0:T(8,128)(2,1)S(1)}, bf16[256,512]{1,0:T(8,128)(2,1)S(1)}, u32[]{:S(2)}, u32[]{:S(2)}) %collective-permute-start.13) | collective-permute-done | bytes 262176 | tf_op jit(solution)/shard_map/ppermute | solution.py:35
  61.5 0.9 %finish.3 = bf16[1,1024,512]{2,1,0:T(8,128)(2,1)} custom-call(bf16[256,512]{1,0:T(8,128)(2,1)S(1)} %collective-permute-done.11.refs_0_, bf16[256,512]{1,0:T(8,128)(2,1)S(1)} %collective-permute-done.13.refs_1_, f32[512,512]{1,0:T(8,128)S(1)} %get-tuple-element.77.refs_2_, f32[512,512]{1,0:T(8,128)S(1)} %get-tuple-element.78.refs_3_, ...), custom_call_target="tpu_custom_call", output_to_operand_aliasing={{}: (4, {})} | custom-call | tf_op jit(solution)/shard_map/finish/pallas_call | solution.py:548
  (21 shorter events, 1.8 us)
Async XLA Ops:
  0.0 5.6 %collective-permute-start.1 = (bf16[1024,512]{1,0:T(8,128)(2,1)}, bf16[1024,512]{1,0:T(8,128)(2,1)S(1)}, u32[]{:S(2)}, u32[]{:S(2)}) collective-permute-start(bf16[1024,512]{1,0:T(8,128)(2,1)} %wk_far.1), channel_id=1, source_target_pairs={{0,1},{1,0},{2,3},{3,2},{4,5},{5,4},{6,7},{7,6},{8,9},{9,8},{10,11... | collective-permute-start | bytes 3145736 | tf_op jit(solution)/shard_map/ppermute | solution.py:35
  0.0 5.6 %collective-permute-start.2 = (bf16[1024,512]{1,0:T(8,128)(2,1)}, bf16[1024,512]{1,0:T(8,128)(2,1)S(1)}, u32[]{:S(2)}, u32[]{:S(2)}) collective-permute-start(bf16[1024,512]{1,0:T(8,128)(2,1)} %wv_far.1), channel_id=1, source_target_pairs={{0,1},{1,0},{2,3},{3,2},{4,5},{5,4},{6,7},{7,6},{8,9},{9,8},{10,11... | collective-permute-start | bytes 3145736 | tf_op jit(solution)/shard_map/ppermute | solution.py:35
  5.0 3.9 %collective-permute-start = (bf16[512,1024]{1,0:T(8,128)(2,1)S(1)}, bf16[512,1024]{1,0:T(8,128)(2,1)S(1)}, u32[]{:S(2)}, u32[]{:S(2)}) collective-permute-start(bf16[512,1024]{1,0:T(8,128)(2,1)S(1)} %get-tuple-element.72.own_first.first), channel_id=1, source_target_pairs={{0,1},{1,0},{2,3},{3,2},{4,5},{5,4},{6,7},{7,6},{8,9},{9,8},{10,11... | collective-permute-start | bytes 3145736 | tf_op jit(solution)/shard_map/ppermute | solution.py:35
  5.0 7.5 %collective-permute-start.3 = (bf16[1024,512]{1,0:T(8,128)(2,1)S(1)}, bf16[1024,512]{1,0:T(8,128)(2,1)S(1)}, u32[]{:S(2)}, u32[]{:S(2)}) collective-permute-start(bf16[1024,512]{1,0:T(8,128)(2,1)S(1)} %get-tuple-element.52.wq), channel_id=1, source_target_pairs={{0,1},{1,0},{2,3},{3,2},{4,5},{5,4},{6,7},{7,6},{8,9},{9,8},{10,11... | collective-permute-start | bytes 3145736 | tf_op jit(solution)/shard_map/ppermute | solution.py:35
  5.5 7.0 %collective-permute-start.4 = (bf16[1024,512]{1,0:T(8,128)(2,1)S(1)}, bf16[1024,512]{1,0:T(8,128)(2,1)S(1)}, u32[]{:S(2)}, u32[]{:S(2)}) collective-permute-start(bf16[1024,512]{1,0:T(8,128)(2,1)S(1)} %get-tuple-element.53.wg), channel_id=1, source_target_pairs={{0,1},{1,0},{2,3},{3,2},{4,5},{5,4},{6,7},{7,6},{8,9},{9,8},{10,11... | collective-permute-start | bytes 3145736 | tf_op jit(solution)/shard_map/ppermute | solution.py:35
  9.0 25.1 %collective-permute-start.9 = (bf16[512,1024]{1,0:T(8,128)(2,1)S(1)}, bf16[512,1024]{1,0:T(8,128)(2,1)S(1)}, u32[]{:S(2)}, u32[]{:S(2)}) collective-permute-start(bf16[512,1024]{1,0:T(8,128)(2,1)S(1)} %columns.1), channel_id=1, source_target_pairs={{0,2},{1,5},{2,0},{3,7},{4,6},{5,1},{6,4},{7,3},{8,10},{9,13},{10,... | collective-permute-start | bytes 3145736 | tf_op jit(solution)/shard_map/ppermute | solution.py:494
  10.6 10.5 %collective-permute-start.5 = (bf16[528,256]{1,0:T(8,128)(2,1)S(1)}, bf16[528,256]{1,0:T(8,128)(2,1)S(1)}, u32[]{:S(2)}, u32[]{:S(2)}) collective-permute-start(bf16[528,256]{1,0:T(8,128)(2,1)S(1)} %get-tuple-element.58.sent), channel_id=1, source_target_pairs={{0,8},{8,16},{16,24},{1,9},{9,17},{17,25},{2,10},{10,18},{18,26},{... | collective-permute-start | bytes 811016 | tf_op jit(solution)/shard_map/ppermute | solution.py:463
  11.9 13.3 %collective-permute-start.7 = (bf16[528,256]{1,0:T(8,128)(2,1)S(1)}, bf16[528,256]{1,0:T(8,128)(2,1)S(1)}, u32[]{:S(2)}, u32[]{:S(2)}) collective-permute-start(bf16[528,256]{1,0:T(8,128)(2,1)S(1)} %get-tuple-element.58.sent), channel_id=1, source_target_pairs={{0,16},{16,0},{1,17},{17,1},{2,18},{18,2},{3,19},{19,3},{4,20},{20... | collective-permute-start | bytes 811016 | tf_op jit(solution)/shard_map/ppermute | solution.py:463
  22.0 10.6 %collective-permute-start.6 = (bf16[528,256]{1,0:T(8,128)(2,1)S(1)}, bf16[528,256]{1,0:T(8,128)(2,1)S(1)}, u32[]{:S(2)}, u32[]{:S(2)}) collective-permute-start(bf16[528,256]{1,0:T(8,128)(2,1)S(1)} %get-tuple-element.60), channel_id=1, source_target_pairs={{8,24},{24,8},{9,25},{25,9},{10,26},{26,10},{11,27},{27,11},{12,28... | collective-permute-start | bytes 811016 | tf_op jit(solution)/shard_map/ppermute | solution.py:463
  34.1 7.1 %collective-permute-start.10 = (bf16[512,1024]{1,0:T(8,128)(2,1)S(1)}, bf16[512,1024]{1,0:T(8,128)(2,1)S(1)}, u32[]{:S(2)}, u32[]{:S(2)}) collective-permute-start(bf16[512,1024]{1,0:T(8,128)(2,1)S(1)} %collective-permute-done.9.mine), channel_id=1, source_target_pairs={{0,1},{1,0},{2,3},{3,2},{4,5},{5,4},{6,7},{7,6},{8,9},{9,8},{10,11... | collective-permute-start | bytes 3145736 | tf_op jit(solution)/shard_map/ppermute | solution.py:35
  34.2 9.2 %collective-permute-start.15 = (bf16[256,512]{1,0:T(8,128)(2,1)S(1)}, bf16[256,512]{1,0:T(8,128)(2,1)S(1)}, u32[]{:S(2)}, u32[]{:S(2)}) collective-permute-start(bf16[256,512]{1,0:T(8,128)(2,1)S(1)} %get-tuple-element.70.refs_3_), channel_id=1, source_target_pairs={{0,2},{2,0},{4,6},{6,4},{1,3},{3,1},{5,7},{7,5},{8,10},{10,8},{12,... | collective-permute-start | bytes 786440 | tf_op jit(solution)/shard_map/ppermute | solution.py:35
  36.2 9.2 %collective-permute-start.14 = (bf16[256,512]{1,0:T(8,128)(2,1)S(1)}, bf16[256,512]{1,0:T(8,128)(2,1)S(1)}, u32[]{:S(2)}, u32[]{:S(2)}) collective-permute-start(bf16[256,512]{1,0:T(8,128)(2,1)S(1)} %get-tuple-element.69.refs_2_), channel_id=1, source_target_pairs={{0,4},{2,6},{4,0},{6,2},{1,5},{3,7},{5,1},{7,3},{8,12},{10,14},{12... | collective-permute-start | bytes 786440 | tf_op jit(solution)/shard_map/ppermute | solution.py:35
  37.7 11.3 %collective-permute-start.12 = (bf16[256,512]{1,0:T(8,128)(2,1)S(1)}, bf16[256,512]{1,0:T(8,128)(2,1)S(1)}, u32[]{:S(2)}, u32[]{:S(2)}) collective-permute-start(bf16[256,512]{1,0:T(8,128)(2,1)S(1)} %get-tuple-element.68.refs_1_), channel_id=1, source_target_pairs={{0,2},{2,0},{4,6},{6,4},{1,3},{3,1},{5,7},{7,5},{8,10},{10,8},{12,... | collective-permute-start | bytes 786440 | tf_op jit(solution)/shard_map/ppermute | solution.py:35
  38.3 12.7 %collective-permute-start.8 = (bf16[256,512]{1,0:T(8,128)(2,1)S(1)}, bf16[256,512]{1,0:T(8,128)(2,1)S(1)}, u32[]{:S(2)}, u32[]{:S(2)}) collective-permute-start(bf16[256,512]{1,0:T(8,128)(2,1)S(1)} %get-tuple-element.67.refs_0_), channel_id=1, source_target_pairs={{0,4},{2,6},{4,0},{6,2},{1,5},{3,7},{5,1},{7,3},{8,12},{10,14},{12... | collective-permute-start | bytes 786440 | tf_op jit(solution)/shard_map/ppermute | solution.py:35
  43.7 12.9 %collective-permute-start.17 = (bf16[256,512]{1,0:T(8,128)(2,1)S(1)}, bf16[256,512]{1,0:T(8,128)(2,1)S(1)}, u32[]{:S(2)}, u32[]{:S(2)}) collective-permute-start(bf16[256,512]{1,0:T(8,128)(2,1)S(1)} %give.7), channel_id=1, source_target_pairs={{0,4},{2,6},{4,0},{6,2},{1,5},{3,7},{5,1},{7,3},{8,12},{10,14},{12... | collective-permute-start | bytes 786440 | tf_op jit(solution)/shard_map/ppermute | solution.py:35
  45.7 10.9 %collective-permute-start.16 = (bf16[256,512]{1,0:T(8,128)(2,1)S(1)}, bf16[256,512]{1,0:T(8,128)(2,1)S(1)}, u32[]{:S(2)}, u32[]{:S(2)}) collective-permute-start(bf16[256,512]{1,0:T(8,128)(2,1)S(1)} %give.6), channel_id=1, source_target_pairs={{0,2},{2,0},{4,6},{6,4},{1,3},{3,1},{5,7},{7,5},{8,10},{10,8},{12,... | collective-permute-start | bytes 786440 | tf_op jit(solution)/shard_map/ppermute | solution.py:35
  49.4 12.1 %collective-permute-start.13 = (bf16[256,512]{1,0:T(8,128)(2,1)S(1)}, bf16[256,512]{1,0:T(8,128)(2,1)S(1)}, u32[]{:S(2)}, u32[]{:S(2)}) collective-permute-start(bf16[256,512]{1,0:T(8,128)(2,1)S(1)} %give.5), channel_id=1, source_target_pairs={{0,4},{2,6},{4,0},{6,2},{1,5},{3,7},{5,1},{7,3},{8,12},{10,14},{12... | collective-permute-start | bytes 786440 | tf_op jit(solution)/shard_map/ppermute | solution.py:35
  51.3 10.2 %collective-permute-start.11 = (bf16[256,512]{1,0:T(8,128)(2,1)S(1)}, bf16[256,512]{1,0:T(8,128)(2,1)S(1)}, u32[]{:S(2)}, u32[]{:S(2)}) collective-permute-start(bf16[256,512]{1,0:T(8,128)(2,1)S(1)} %give.4), channel_id=1, source_target_pairs={{0,2},{2,0},{4,6},{6,4},{1,3},{3,1},{5,7},{7,5},{8,10},{10,8},{12,... | collective-permute-start | bytes 786440 | tf_op jit(solution)/shard_map/ppermute | solution.py:35

commit v12 on v11

--- a/solution.py
+++ b/solution.py
@@ -256,11 +256,11 @@
     pack_message(message, states, [totals[:, head : head + 1] for head in range(heads)])
 
 
-def combine_kernel(heads, hop, sets, first, state, sent, *refs):
+def combine_kernel(heads, hop, sets, first, last, state, sent, *refs):
     if not first:
         old_entering, refs = refs[0], refs[1:]
-    arrivals = refs[: len(sets)]
-    window, entering, message = refs[len(sets) :]
+    arrivals, entering = refs[: len(sets)], refs[len(sets)]
+    outs = refs[len(sets) + 1 :]
     states, logs = [], []
     for head in range(heads):
         span = slice(head * DH, (head + 1) * DH)
@@ -277,10 +277,14 @@
             entering_log = before_log + log
         entering[row, :] = jnp.broadcast_to(entering_log, (1, DH))
         new = state[span, :] + jnp.exp(window_log) * arrived
-        window[span, :] = new
+        if last:
+            outs[head][...] = new.astype(BF16)
+        else:
+            outs[0][span, :] = new
         states.append(new)
         logs.append(window_log + log)
-    pack_message(message, states, logs)
+    if not last:
+        pack_message(outs[1], states, logs)
 
 
 def query_gate_kernel(
@@ -308,28 +312,33 @@
             intra_out[low:last, span] = mm((scores * weights).astype(BF16), v[start : start + last, span])
 
 
-def hidden_kernel(heads, hop, sets, starts, decay, before, entering, *refs):
-    arrivals, refs, token = refs[: len(sets)], refs[len(sets) : -1], refs[-1]
-    projected, outs = refs[: -len(starts)], refs[-len(starts) :]
+def hidden_kernel(heads, head, hop, early_sets, late_sets, pieces, decay, before, entering, *refs):
+    early, refs = refs[: len(early_sets)], refs[len(early_sets) :]
+    late, refs = refs[: len(late_sets)], refs[len(late_sets) :]
+    projected, outs, token = refs[: -len(pieces) - 1], refs[-len(pieces) - 1 : -1], refs[-1]
     token[...] = jnp.zeros_like(token)
-    for head in range(heads):
-        span = slice(head * DH, (head + 1) * DH)
-        entering_log = entering[heads * DH + head : heads * DH + head + 1, :1]
-        state = entering[span, :] + jnp.exp(entering_log) * arrived_state(arrivals, sets, hop, span)
-        for start, out in zip(starts, outs):
-            block = start // BLOCK
-            q, gate, intra = projected[3 * block : 3 * block + 3]
-            at = slice(start % BLOCK, start % BLOCK + TILE)
-            column = jnp.exp(decay[:, start : start + TILE].T[:, head : head + 1])
-            scale_log = jnp.zeros((1, 1), F32)
-            for earlier in range(block):
-                end = (earlier + 1) * BLOCK
-                scale_log = scale_log + decay[head : head + 1, end - 1 : end]
-            prior = (jnp.exp(scale_log) * state + before[block, span, :].astype(F32)).astype(BF16)
+    span = slice(head * DH, (head + 1) * DH)
+    arrived = arrived_state(late, late_sets, hop, slice(0, DH))
+    if early_sets:
+        arrived = arrived + arrived_state(early, early_sets, hop, span)
+    entering_log = entering[heads * DH + head : heads * DH + head + 1, :1]
+    state = entering[span, :] + jnp.exp(entering_log) * arrived
+    for (start, count), out in zip(pieces, outs):
+        block = start // BLOCK
+        q, gate, intra = projected[3 * block : 3 * block + 3]
+        scale_log = jnp.zeros((1, 1), F32)
+        for earlier in range(block):
+            end = (earlier + 1) * BLOCK
+            scale_log = scale_log + decay[head : head + 1, end - 1 : end]
+        prior = (jnp.exp(scale_log) * state + before[block, span, :].astype(F32)).astype(BF16)
+        for low in range(0, count, TILE):
+            first = start % BLOCK + low
+            at = slice(first, first + TILE)
+            column = jnp.exp(decay[:, start + low : start + low + TILE].T[:, head : head + 1])
             retained = intra[at, span] + column * mm(q[at, span], prior)
             center = retained - jnp.mean(retained, axis=1, keepdims=True)
             spread = jnp.mean(center * center, axis=1, keepdims=True)
-            out[:, span] = (gate[at, span] * center * lax.rsqrt(spread + 1e-5)).astype(BF16)
+            out[low : low + TILE, :] = (gate[at, span] * center * lax.rsqrt(spread + 1e-5)).astype(BF16)
 
 
 def columns_kernel(first, second, out):
@@ -360,7 +369,7 @@
 
 def own_kernel(order, own_first, own_second, *refs):
     pieces, outs = refs[: len(order)], refs[len(order) :]
-    cols = pieces[0].shape[1]
+    cols = outs[0].shape[1] // 2
     place, core = lax.axis_index("tp"), lax.axis_index("fsdp")
     high, low = place // 2, place % 2
     here = core == high
@@ -371,36 +380,54 @@
         jnp.where(here, own_second[:, mine], own_first[:, mine]),
         jnp.where(here, own_first[:, flipped], own_second[:, flipped]),
     ]
-    for (half, number), piece in zip(order, pieces):
-        at = slice(number * TILE, (number + 1) * TILE)
-        outs[half][at, :cols] = mm(piece[...], gives[half])
-        outs[half][at, cols:] = mm(piece[...], keep)
-
-
-def give_kernel(number, own, far, weight, out):
+    for half in range(2):
+        for (head, first, count), piece in sorted(
+            ((key[1:], ref) for key, ref in zip(order, pieces) if key[0] == half), key=lambda pair: pair[0]
+        ):
+            at, span = slice(first, first + count), slice(head * DH, (head + 1) * DH)
+            for target, weight in ((slice(0, cols), gives[half]), (slice(cols, 2 * cols), keep)):
+                term = mm(piece[...], weight[span, :])
+                outs[half][at, target] = term if head == 0 else outs[half][at, target] + term
+
+
+def far_product(first, keys, fars, weight, columns):
+    total = None
+    for (head, start, count), far in zip(keys, fars):
+        if start <= first < start + count:
+            term = mm(far[first - start : first - start + TILE, :], weight[head * DH : (head + 1) * DH, columns])
+            total = term if total is None else total + term
+    return total
+
+
+def give_kernel(first, keys, own, weight, *refs):
+    fars, out = refs[:-1], refs[-1]
     cols = out.shape[1]
-    at = slice(number * TILE, (number + 1) * TILE)
-    out[...] = (own[at, :cols] + mm(far[...], weight[:, :cols])).astype(BF16)
+    at = slice(first, first + TILE)
+    out[...] = (own[at, :cols] + far_product(first, keys, fars, weight, slice(0, cols))).astype(BF16)
 
 
 def keep_kernel(order, *refs):
     count = len(order)
     fars, owns, weights, outs = refs[:count], refs[count : count + 2], refs[count + 2 : count + 4], refs[count + 4 :]
-    for (half, number), far in zip(order, fars):
-        cols = far.shape[1]
-        at = slice(number * TILE, (number + 1) * TILE)
-        outs[half][at, :] = owns[half][at, cols:] + mm(far[...], weights[half][:, cols:])
+    for half in range(2):
+        mine = [(key[1:], far) for key, far in zip(order, fars) if key[0] == half]
+        keys, pieces = [key for key, _ in mine], [far for _, far in mine]
+        cols = outs[half].shape[1]
+        for first in range(0, outs[half].shape[0], TILE):
+            at = slice(first, first + TILE)
+            term = far_product(first, keys, pieces, weights[half], slice(cols, 2 * cols))
+            outs[half][at, :] = owns[half][at, cols:] + term
 
 
 def finish_kernel(order, *refs):
     count = len(order)
     gots, keeps, out, ready, written = refs[:count], refs[count : count + 2], refs[-3], refs[-2], refs[-1]
     copies = []
-    for slot, ((half, number), got) in enumerate(zip(order, gots)):
+    for slot, ((half, first), got) in enumerate(zip(order, gots)):
         keep = keeps[half]
-        at = slice(number * TILE, (number + 1) * TILE)
+        at = slice(first, first + TILE)
         ready[slot] = (keep[at, :] + got[...].astype(F32)).astype(BF16)
-        start = half * keep.shape[0] + number * TILE
+        start = half * keep.shape[0] + first
         copies.append(pltpu.make_async_copy(ready.at[slot], out.at[0, pl.ds(start, TILE)], written.at[slot]))
         copies[-1].start()
     for copy in copies:
@@ -466,24 +493,31 @@
     window = after(window, projected[0])
     entering, hop, early, first_message = None, 1, [], message
     while True:
-        first_set, *later_sets = exchanges(ctx, hop)
-        later_sets = [lowers for lowers in later_sets if lowers]
-        sets = later_sets + ([first_set] if first_set else [])
-        arrivals = [exchange(message, lowers, hop) for lowers in later_sets] + early
+        early_sets, late_sets = [], []
+        first_set, *late_sets = exchanges(ctx, hop)
+        late_sets = [lowers for lowers in late_sets if lowers]
+        early_sets = [first_set] if first_set else []
         if 2 * hop >= ctx:
             break
+        arrivals = [exchange(message, lowers, hop) for lowers in late_sets] + early
         unchanged = exchanges(ctx, 2 * hop)[0]
         early = [exchange(message, unchanged, 2 * hop)]
         old = [] if entering is None else [entering]
-        window, entering, message = kernel_call(
-            functools.partial(combine_kernel, heads, hop, sets, entering is None),
-            [(state_shape, F32), ((heads * DH + 8, DH), F32), (message_shape, BF16)],
+        last = 4 * hop >= ctx
+        combined = [((heads * DH + 8, DH), F32)]
+        combined += [((DH, DH), BF16)] * heads if last else [(state_shape, F32), (message_shape, BF16)]
+        entering, *outs = kernel_call(
+            functools.partial(combine_kernel, heads, hop, late_sets + early_sets, entering is None, last),
+            combined,
             [window, message, *old, *arrivals],
             "combine",
         )
+        if not last:
+            window, message = outs
         hop *= 2
-
     own_second = swap(out_first, "fsdp", 1)
+    late = [[exchange(state, lowers, hop) for lowers in late_sets] for state in outs]
+
     [for_partner] = kernel_call(
         columns_kernel,
         [(out_weight.shape, BF16)],
@@ -493,56 +527,60 @@
     pairs = [(at * cores + at_core, (at ^ mask) * cores + at_core) for at in range(tp) for at_core, mask in enumerate((near_mask, far_mask))]
     out_mine = lax.ppermute(for_partner, ("tp", "fsdp"), pairs)
 
-    held = after(decay, message, *early)
+    held = after(decay, *outs, *early)
     for block in range(1, blocks):
         projected += query_gate(block, held)
 
-    count = rows // 2 // TILE
-    masks = (near_mask, far_mask)
-    hidden, far = [[], []], [[], []]
-    for number in range(count):
-        held = after(decay, swap(pair[2], "fsdp", 1)) if number else decay
-        pair = kernel_call(
-            functools.partial(hidden_kernel, heads, hop, sets, [(half * count + number) * TILE for half in range(2)]),
-            [((TILE, cols), BF16)] * 2 + [((16, 128), BF16)],
-            [held, before, entering, *arrivals, *projected],
+    masks, middle = (near_mask, far_mask), rows // 2
+    out_other = swap(after(out_mine, outs[0], *early), "fsdp", 1)
+    cuts = [(head, 0, middle) for head in range(heads - 1)]
+    cuts += [(heads - 1, first, TILE) for first in range(0, middle, TILE)]
+    hidden, far, token = {}, {}, None
+    for head, first, count in cuts:
+        held = decay if token is None else after(decay, swap(token, "fsdp", 1))
+        *pair, token = kernel_call(
+            functools.partial(
+                hidden_kernel, heads, head, hop, early_sets, late_sets, [(half * middle + first, count) for half in range(2)]
+            ),
+            [((count, DH), BF16)] * 2 + [((16, 128), BF16)],
+            [held, before, entering, *early, *late[head], *projected],
             "hidden",
         )
-        if number == 0:
-            out_other = swap(after(out_mine, pair[0]), "fsdp", 1)
         for half in range(2):
-            hidden[half].append(pair[half])
-            far[half].append(swap(pair[half], "tp", masks[half]))
+            key = half, head, first, count
+            hidden[key], far[key] = pair[half], swap(pair[half], "tp", masks[half])
     weights = kernel_call(
         arrange_kernel,
         [((cols, 2 * cols), BF16)] * 2,
         [out_mine, out_other],
         "arrange",
     )
-    order = [(half, number) for number in reversed(range(count)) for half in (1, 0)]
+    order = [(half, *cut) for cut in reversed(cuts) for half in (1, 0)]
     owns = kernel_call(
         functools.partial(own_kernel, order),
-        [((count * TILE, 2 * cols), F32)] * 2,
-        [out_first, own_second, *(hidden[half][number] for half, number in order)],
+        [((middle, 2 * cols), F32)] * 2,
+        [out_first, own_second, *(hidden[key] for key in order)],
         "own_products",
     )
+    tiles = [(half, first) for first in reversed(range(0, middle, TILE)) for half in (1, 0)]
     gots = []
-    for half, number in order:
+    for half, first in tiles:
+        keys = [key for key in order if key[0] == half and key[2] <= first < key[2] + key[3]]
         [give] = kernel_call(
-            functools.partial(give_kernel, number),
+            functools.partial(give_kernel, first, [key[1:] for key in keys]),
             [((TILE, cols), BF16)],
-            [owns[half], far[half][number], weights[half]],
+            [owns[half], weights[half], *(far[key] for key in keys)],
             "give",
         )
         gots.append(swap(give, "tp", masks[1 - half]))
     keeps = kernel_call(
         functools.partial(keep_kernel, order),
-        [((count * TILE, cols), F32)] * 2,
-        [*(far[half][number] for half, number in order), *owns, *weights],
+        [((middle, cols), F32)] * 2,
+        [*(far[key] for key in order), *owns, *weights],
         "keep",
     )
     result = None
-    for part_order, part_gots in ((order[2:], gots[2:]), (order[:2], gots[:2])):
+    for part_order, part_gots in ((tiles[2:], gots[2:]), (tiles[:2], gots[:2])):
         arrays = [pltpu.with_memory_space_constraint(array, pltpu.VMEM) for array in (*part_gots, *keeps)]
         held = [] if result is None else [result]
         result = pl.pallas_call(

time: 62.9 us -> 66.1 us (1.051)
  starting transfers between devices: 13.8 us -> 23 us
  waiting for transfers between devices: 25.3 us -> 19.6 us
    ppermute x14 -> x16, starting transfers between devices: 7.19 us -> 12.5 us  [swap(): lax.ppermute(value, axis, [(place, place ^ mask) for place in range(size)])]
    ppermute x3 -> x4, waiting for transfers between devices: 9.85 us -> 5.46 us  [exchange(): return lax.ppermute(message, 'ctx', pairs)]
    ppermute x14 -> x16, waiting for transfers between devices: 15.4 us -> 11.5 us  [swap(): lax.ppermute(value, axis, [(place, place ^ mask) for place in range(size)])]
    ppermute x3 -> x4, starting transfers between devices: 5.06 us -> 8.87 us  [exchange(): return lax.ppermute(message, 'ctx', pairs)]
    ppermute x1, waiting for transfers between devices: 0.01 us -> 2.64 us  [on_device(): out_mine = lax.ppermute(for_partner, ('tp', 'fsdp'), pairs)]
    pallas_call x14 -> x15, Pallas kernels: 16.9 us -> 16.9 us  [kernel_call(): pl.pallas_call(kernel, in_specs=[pl.BlockSpec(memory_space=pltpu.VMEM)] *...]
  transfers between devices with their start and end apart: 18 -> 21, of which waited for: 8 -> 7; matrix products, arithmetic and copies ran while one was open for 0% -> 0% of each run, Pallas kernels for 36% -> 34%
where the time goes in v12:
time: 66.1 us; the launch traced here: 65.9 us
  starting transfers between devices  23 us (35%)
  Pallas kernels  23 us (35%)
  waiting for transfers between devices  19.6 us (30%)
    pallas_call x15, Pallas kernels, kernel_call(): pl.pallas_call(kernel, in_specs=[pl.BlockSpec(memory_space=pltpu.VMEM)] *...  16.9 us
    ppermute x16, starting transfers between devices, swap(): lax.ppermute(value, axis, [(place, place ^ mask) for place in range(size)])  12.5 us
    ppermute x16, waiting for transfers between devices, swap(): lax.ppermute(value, axis, [(place, place ^ mask) for place in range(size)])  11.5 us
    ppermute x4, starting transfers between devices, exchange(): return lax.ppermute(message, 'ctx', pairs)  8.87 us
    ppermute x4, waiting for transfers between devices, exchange(): return lax.ppermute(message, 'ctx', pairs)  5.46 us
    pallas_call x1, Pallas kernels, loading_call(): pl.pallas_call(kernel, in_specs=[pl.BlockSpec(memory_space=pltpu.HBM)] *...  4.44 us
    ppermute x1, waiting for transfers between devices, on_device(): out_mine = lax.ppermute(for_partner, ('tp', 'fsdp'), pairs)  2.64 us
    pallas_call x2, Pallas kernels, on_device(): pl.pallas_call(functools.partial(finish_kernel, part_order), in_specs=[pl...  1.7 us
  transfers between devices with their start and end apart: 21, of which 7 were waited for; matrix products, arithmetic and copies ran while one was open for 0% of the time, Pallas kernels for 34%

profile of v12, /device:TPU:24, one launch (start us, length us, event | category | flops | bytes accessed | tf_op | source)
XLA Modules:
  0.0 65.9 jit_solution(9978257351718419660)
XLA Ops:
  0.0 0.5 collective-permute-start.2
  0.5 4.4 %key_value_own.1 = (bf16[1024,1024]{1,0:T(8,128)(2,1)S(1)}, bf16[1024,1024]{1,0:T(8,128)(2,1)S(1)}, f32[1024,512]{1,0:T(8,128)S(1)}, f32[1024,512]{1,0:T(8,128)S...) custom-call(bf16[1024,2048]{1,0:T(8,128)(2,1)} %bitcast.4, ...), custom_call_target="tpu_custom_call" | custom-call | flops 1 | bytes 1 | tf_op jit(solution)/shard_map/key_value_own/pallas_call | solution.py:56
  5.6 3.3 %key_value.1 = (bf16[1024,512]{1,0:T(8,128)(2,1)S(1)}, bf16[1024,512]{1,0:T(8,128)(2,1)S(1)}, bf16[2,512,256]{2,1,0:T(8,128)(2,1)S(1)}, f32[512,256]{1,0:T(8,128)S(1)}, bf16[528,256]{1,0:T(8,128)(2,1)S(1)}) custom-call(bf16[1024,1024]{1,0:T(8,128)(2,1)S(1)} %get-tuple-element.47.x.x_other, bf16[1024,512]{1,0:T(8,128)(2,1)S(1)} %collective-permute-done.1.wk, ...), custom_call_target="tpu_custom_call" | custom-call | flops 1 | bytes 1 | tf_op jit(solution)/shard_map/key_value/pallas_call | solution.py:40
  9.0 1.6 %collective-permute-start.9 = (bf16[512,1024]{1,0:T(8,128)(2,1)S(1)}, bf16[512,1024]{1,0:T(8,128)(2,1)S(1)}, u32[]{:S(2)}, u32[]{:S(2)}) collective-permute-start(bf16[512,1024]{1,0:T(8,128)(2,1)S(1)} %columns.1), channel_id=1, source_target_pairs={{0,2},{1,5},{2,0},{3,7},{4,6},{5,1},{6,4},{7,3},{8,10},{9,13},{10,... | collective-permute-start | bytes 3145736 | tf_op jit(solution)/shard_map/ppermute | solution.py:528
  10.6 1.3 %collective-permute-start.5 = (bf16[528,256]{1,0:T(8,128)(2,1)S(1)}, bf16[528,256]{1,0:T(8,128)(2,1)S(1)}, u32[]{:S(2)}, u32[]{:S(2)}) collective-permute-start(bf16[528,256]{1,0:T(8,128)(2,1)S(1)} %get-tuple-element.61.sent), channel_id=1, source_target_pairs={{0,8},{8,16},{16,24},{1,9},{9,17},{17,25},{2,10},{10,18},{18,26},{... | collective-permute-start | bytes 811016 | tf_op jit(solution)/shard_map/ppermute | solution.py:490
  11.9 0.7 %collective-permute-start.6 = (bf16[528,256]{1,0:T(8,128)(2,1)S(1)}, bf16[528,256]{1,0:T(8,128)(2,1)S(1)}, u32[]{:S(2)}, u32[]{:S(2)}) collective-permute-start(bf16[528,256]{1,0:T(8,128)(2,1)S(1)} %get-tuple-element.61.sent), channel_id=1, source_target_pairs={{0,16},{16,0},{1,17},{17,1},{2,18},{18,2},{3,19},{19,3},{4,20},{20... | collective-permute-start | bytes 811016 | tf_op jit(solution)/shard_map/ppermute | solution.py:490
  12.6 3.0 %query_gate.2 = (bf16[512,512]{1,0:T(8,128)(2,1)S(1)}, f32[512,512]{1,0:T(8,128)S(1)}, f32[512,512]{1,0:T(8,128)S(1)}) custom-call(bf16[1024,1024]{1,0:T(8,128)(2,1)S(1)} %get-tuple-element.54.x_own, bf16[1024,1024]{1,0:T(8,128)(2,1)S(1)} %get-tuple-element.47.x.x_other, bf16[1024,512]{1,0:T(8,128)(2,1)S(1)} %get-tuple-element.55.wq, ...), custom_call_target="tpu_custom_call" | custom-call | flops 1 | bytes 1 | tf_op jit(solution)/shard_map/query_gate/pallas_call | solution.py:40
  15.6 5.5 %collective-permute-done.5.refs_0_ = bf16[528,256]{1,0:T(8,128)(2,1)S(1)} collective-permute-done((bf16[528,256]{1,0:T(8,128)(2,1)S(1)}, bf16[528,256]{1,0:T(8,128)(2,1)S(1)}, u32[]{:S(2)}, u32[]{:S(2)}) %collective-permute-start.5) | collective-permute-done | bytes 270368 | tf_op jit(solution)/shard_map/ppermute | solution.py:490
  21.2 2.6 %collective-permute-done.9.mine = bf16[512,1024]{1,0:T(8,128)(2,1)S(1)} collective-permute-done((bf16[512,1024]{1,0:T(8,128)(2,1)S(1)}, bf16[512,1024]{1,0:T(8,128)(2,1)S(1)}, u32[]{:S(2)}, u32[]{:S(2)}) %collective-permute-start.9) | collective-permute-done | bytes 1048608 | tf_op jit(solution)/shard_map/ppermute | solution.py:528
  23.9 2.2 %collective-permute-start.8 = (bf16[256,256]{1,0:T(8,128)(2,1)S(1)}, bf16[256,256]{1,0:T(8,128)(2,1)S(1)}, u32[]{:S(2)}, u32[]{:S(2)}) collective-permute-start(bf16[256,256]{1,0:T(8,128)(2,1)S(1)} %get-tuple-element.66), channel_id=1, source_target_pairs={{8,24},{24,8},{9,25},{25,9},{10,26},{26,10},{11,27},{27,11},{12,28... | collective-permute-start | bytes 393224 | tf_op jit(solution)/shard_map/ppermute | solution.py:490
  26.1 4.7 %collective-permute-start.7 = (bf16[256,256]{1,0:T(8,128)(2,1)S(1)}, bf16[256,256]{1,0:T(8,128)(2,1)S(1)}, u32[]{:S(2)}, u32[]{:S(2)}) collective-permute-start(bf16[256,256]{1,0:T(8,128)(2,1)S(1)} %get-tuple-element.63), channel_id=1, source_target_pairs={{8,24},{24,8},{9,25},{25,9},{10,26},{26,10},{11,27},{27,11},{12,28... | collective-permute-start | bytes 393224 | tf_op jit(solution)/shard_map/ppermute | solution.py:490
  30.8 3.1 %query_gate.3 = (bf16[512,512]{1,0:T(8,128)(2,1)S(1)}, f32[512,512]{1,0:T(8,128)S(1)}, f32[512,512]{1,0:T(8,128)S(1)}) custom-call(bf16[1024,1024]{1,0:T(8,128)(2,1)S(1)} %get-tuple-element.54.x_own, bf16[1024,1024]{1,0:T(8,128)(2,1)S(1)} %get-tuple-element.47.x.x_other, bf16[1024,512]{1,0:T(8,128)(2,1)S(1)} %get-tuple-element.55.wq, ...), custom_call_target="tpu_custom_call" | custom-call | flops 1 | bytes 1 | tf_op jit(solution)/shard_map/query_gate/pallas_call | solution.py:40
  33.9 2.1 %hidden.5 = (bf16[512,256]{1,0:T(8,128)(2,1)S(1)}, bf16[512,256]{1,0:T(8,128)(2,1)S(1)}, bf16[16,128]{1,0:T(8,128)(2,1)}) custom-call(f32[8,1024]{1,0:T(8,128)S(1)} %get-tuple-element.67.decay, bf16[2,512,256]{2,1,0:T(8,128)(2,1)S(1)} %get-tuple-element.52.before, f32[520,256]{1,0:T(8,128)S(1)} %get-tuple-element.62.entering, ...), custom_call_target="tpu_custom_call" | custom-call | flops 1 | bytes 1 | tf_op jit(solution)/shard_map/hidden/pallas_call | solution.py:40
  36.0 1.5 %collective-permute-start.12 = (bf16[512,256]{1,0:T(8,128)(2,1)S(1)}, bf16[512,256]{1,0:T(8,128)(2,1)S(1)}, u32[]{:S(2)}, u32[]{:S(2)}) collective-permute-start(bf16[512,256]{1,0:T(8,128)(2,1)S(1)} %get-tuple-element.75.refs_4_), channel_id=1, source_target_pairs={{0,4},{2,6},{4,0},{6,2},{1,5},{3,7},{5,1},{7,3},{8,12},{10,14},{12... | collective-permute-start | bytes 786440 | tf_op jit(solution)/shard_map/ppermute | solution.py:35
  37.5 1.5 %collective-permute-start.15 = (bf16[512,256]{1,0:T(8,128)(2,1)S(1)}, bf16[512,256]{1,0:T(8,128)(2,1)S(1)}, u32[]{:S(2)}, u32[]{:S(2)}) collective-permute-start(bf16[512,256]{1,0:T(8,128)(2,1)S(1)} %get-tuple-element.76.refs_5_), channel_id=1, source_target_pairs={{0,2},{2,0},{4,6},{6,4},{1,3},{3,1},{5,7},{7,5},{8,10},{10,8},{12,... | collective-permute-start | bytes 786440 | tf_op jit(solution)/shard_map/ppermute | solution.py:35
  39.0 0.8 %hidden.4 = (bf16[256,256]{1,0:T(8,128)(2,1)S(1)}, bf16[256,256]{1,0:T(8,128)(2,1)S(1)}, bf16[16,128]{1,0:T(8,128)(2,1)}) custom-call(f32[8,1024]{1,0:T(8,128)S(1)} %get-tuple-element.67.decay, bf16[2,512,256]{2,1,0:T(8,128)(2,1)S(1)} %get-tuple-element.52.before, f32[520,256]{1,0:T(8,128)S(1)} %get-tuple-element.62.entering, ...), custom_call_target="tpu_custom_call" | custom-call | flops 1 | bytes 1 | tf_op jit(solution)/shard_map/hidden/pallas_call | solution.py:40
  40.3 0.5 collective-permute-start.18
  40.9 0.8 %hidden.3 = (bf16[256,256]{1,0:T(8,128)(2,1)S(1)}, bf16[256,256]{1,0:T(8,128)(2,1)S(1)}, bf16[16,128]{1,0:T(8,128)(2,1)}) custom-call(f32[8,1024]{1,0:T(8,128)S(1)} %get-tuple-element.67.decay, bf16[2,512,256]{2,1,0:T(8,128)(2,1)S(1)} %get-tuple-element.52.before, f32[520,256]{1,0:T(8,128)S(1)} %get-tuple-element.62.entering, ...), custom_call_target="tpu_custom_call" | custom-call | flops 1 | bytes 1 | tf_op jit(solution)/shard_map/hidden/pallas_call | solution.py:40
  41.7 5.2 %collective-permute-done.17.refs_2_.refs_0_ = bf16[256,256]{1,0:T(8,128)(2,1)S(1)} collective-permute-done((bf16[256,256]{1,0:T(8,128)(2,1)S(1)}, bf16[256,256]{1,0:T(8,128)(2,1)S(1)}, u32[]{:S(2)}, u32[]{:S(2)}) %collective-permute-start.17) | collective-permute-done | bytes 131104 | tf_op jit(solution)/shard_map/ppermute | solution.py:35
  46.9 1.5 %collective-permute-start.11 = (bf16[256,256]{1,0:T(8,128)(2,1)S(1)}, bf16[256,256]{1,0:T(8,128)(2,1)S(1)}, u32[]{:S(2)}, u32[]{:S(2)}) collective-permute-start(bf16[256,256]{1,0:T(8,128)(2,1)S(1)} %get-tuple-element.71.refs_0_), channel_id=1, source_target_pairs={{0,4},{2,6},{4,0},{6,2},{1,5},{3,7},{5,1},{7,3},{8,12},{10,14},{12... | collective-permute-start | bytes 393224 | tf_op jit(solution)/shard_map/ppermute | solution.py:35
  48.5 1.5 %collective-permute-start.14 = (bf16[256,256]{1,0:T(8,128)(2,1)S(1)}, bf16[256,256]{1,0:T(8,128)(2,1)S(1)}, u32[]{:S(2)}, u32[]{:S(2)}) collective-permute-start(bf16[256,256]{1,0:T(8,128)(2,1)S(1)} %get-tuple-element.72.refs_1_), channel_id=1, source_target_pairs={{0,2},{2,0},{4,6},{6,4},{1,3},{3,1},{5,7},{7,5},{8,10},{10,8},{12,... | collective-permute-start | bytes 393224 | tf_op jit(solution)/shard_map/ppermute | solution.py:35
  49.9 1.3 %own_products.1 = (f32[512,1024]{1,0:T(8,128)S(1)}, f32[512,1024]{1,0:T(8,128)S(1)}) custom-call(bf16[512,1024]{1,0:T(8,128)(2,1)S(1)} %get-tuple-element.78.own_first.first, bf16[512,1024]{1,0:T(8,128)(2,1)S(1)} %collective-permute-done.own_second.second, bf16[256,256]{1,0:T(8,128)(2,1)S(1)} %get-tuple-element.71.refs_0_, ...), custom_call_target="tpu_custom_call" | custom-call | flops 1 | bytes 1 | tf_op jit(solution)/shard_map/own_products/pallas_call | solution.py:40
  51.8 0.6 collective-permute-start.19
  52.8 0.6 collective-permute-start.20
  53.6 1.6 %collective-permute-start.13 = (bf16[256,512]{1,0:T(8,128)(2,1)S(1)}, bf16[256,512]{1,0:T(8,128)(2,1)S(1)}, u32[]{:S(2)}, u32[]{:S(2)}) collective-permute-start(bf16[256,512]{1,0:T(8,128)(2,1)S(1)} %give.4), channel_id=1, source_target_pairs={{0,2},{2,0},{4,6},{6,4},{1,3},{3,1},{5,7},{7,5},{8,10},{10,8},{12,... | collective-permute-start | bytes 786440 | tf_op jit(solution)/shard_map/ppermute | solution.py:35
  55.5 1.6 %collective-permute-start.16 = (bf16[256,512]{1,0:T(8,128)(2,1)S(1)}, bf16[256,512]{1,0:T(8,128)(2,1)S(1)}, u32[]{:S(2)}, u32[]{:S(2)}) collective-permute-start(bf16[256,512]{1,0:T(8,128)(2,1)S(1)} %give.5), channel_id=1, source_target_pairs={{0,4},{2,6},{4,0},{6,2},{1,5},{3,7},{5,1},{7,3},{8,12},{10,14},{12... | collective-permute-start | bytes 786440 | tf_op jit(solution)/shard_map/ppermute | solution.py:35
  57.1 0.7 %keep.1 = (f32[512,512]{1,0:T(8,128)S(1)}, f32[512,512]{1,0:T(8,128)S(1)}) custom-call(bf16[256,256]{1,0:T(8,128)(2,1)S(1)} %collective-permute-done.11.refs_0_, bf16[256,256]{1,0:T(8,128)(2,1)S(1)} %collective-permute-done.14.refs_0_.refs_1_, bf16[256,256]{1,0:T(8,128)(2,1)S(1)} %collective-permute-done.17.refs_2_.refs_0_, ...), custom_call_target="tpu_custom_call" | custom-call | flops 1 | bytes 1 | tf_op jit(solution)/shard_map/keep/pallas_call | solution.py:40
  57.8 3.3 %collective-permute-done.19.refs_0_ = bf16[256,512]{1,0:T(8,128)(2,1)S(1)} collective-permute-done((bf16[256,512]{1,0:T(8,128)(2,1)S(1)}, bf16[256,512]{1,0:T(8,128)(2,1)S(1)}, u32[]{:S(2)}, u32[]{:S(2)}) %collective-permute-start.19) | collective-permute-done | bytes 262176 | tf_op jit(solution)/shard_map/ppermute | solution.py:35
  61.2 0.9 %collective-permute-done.20.refs_1_ = bf16[256,512]{1,0:T(8,128)(2,1)S(1)} collective-permute-done((bf16[256,512]{1,0:T(8,128)(2,1)S(1)}, bf16[256,512]{1,0:T(8,128)(2,1)S(1)}, u32[]{:S(2)}, u32[]{:S(2)}) %collective-permute-start.20) | collective-permute-done | bytes 262176 | tf_op jit(solution)/shard_map/ppermute | solution.py:35
  62.1 0.9 %finish.2.refs_4_ = bf16[1,1024,512]{2,1,0:T(8,128)(2,1)} custom-call(bf16[256,512]{1,0:T(8,128)(2,1)S(1)} %collective-permute-done.19.refs_0_, bf16[256,512]{1,0:T(8,128)(2,1)S(1)} %collective-permute-done.20.refs_1_, f32[512,512]{1,0:T(8,128)S(1)} %get-tuple-element.83.refs_2_, f32[512,512]{1,0:T(8,128)S(1)} %get-tuple-element.84.refs_3_), custom_call_target="tpu_custom_call" | custom-call | tf_op jit(solution)/shard_map/finish/pallas_call | solution.py:586
  62.9 1.7 %collective-permute-done.13.refs_0_ = bf16[256,512]{1,0:T(8,128)(2,1)S(1)} collective-permute-done((bf16[256,512]{1,0:T(8,128)(2,1)S(1)}, bf16[256,512]{1,0:T(8,128)(2,1)S(1)}, u32[]{:S(2)}, u32[]{:S(2)}) %collective-permute-start.13) | collective-permute-done | bytes 262176 | tf_op jit(solution)/shard_map/ppermute | solution.py:35
  64.9 0.9 %finish.3 = bf16[1,1024,512]{2,1,0:T(8,128)(2,1)} custom-call(bf16[256,512]{1,0:T(8,128)(2,1)S(1)} %collective-permute-done.13.refs_0_, bf16[256,512]{1,0:T(8,128)(2,1)S(1)} %collective-permute-done.16.refs_1_, f32[512,512]{1,0:T(8,128)S(1)} %get-tuple-element.83.refs_2_, f32[512,512]{1,0:T(8,128)S(1)} %get-tuple-element.84.refs_3_, ...), custom_call_target="tpu_custom_call", output_to_operand_aliasing={{}: (4, {})} | custom-call | tf_op jit(solution)/shard_map/finish/pallas_call | solution.py:586
  (28 shorter events, 3.2 us)
Async XLA Ops:
  0.0 5.6 %collective-permute-start.1 = (bf16[1024,512]{1,0:T(8,128)(2,1)}, bf16[1024,512]{1,0:T(8,128)(2,1)S(1)}, u32[]{:S(2)}, u32[]{:S(2)}) collective-permute-start(bf16[1024,512]{1,0:T(8,128)(2,1)} %wk_far.1), channel_id=1, source_target_pairs={{0,1},{1,0},{2,3},{3,2},{4,5},{5,4},{6,7},{7,6},{8,9},{9,8},{10,11... | collective-permute-start | bytes 3145736 | tf_op jit(solution)/shard_map/ppermute | solution.py:35
  0.0 5.6 %collective-permute-start.2 = (bf16[1024,512]{1,0:T(8,128)(2,1)}, bf16[1024,512]{1,0:T(8,128)(2,1)S(1)}, u32[]{:S(2)}, u32[]{:S(2)}) collective-permute-start(bf16[1024,512]{1,0:T(8,128)(2,1)} %wv_far.1), channel_id=1, source_target_pairs={{0,1},{1,0},{2,3},{3,2},{4,5},{5,4},{6,7},{7,6},{8,9},{9,8},{10,11... | collective-permute-start | bytes 3145736 | tf_op jit(solution)/shard_map/ppermute | solution.py:35
  5.0 3.9 %collective-permute-start = (bf16[512,1024]{1,0:T(8,128)(2,1)S(1)}, bf16[512,1024]{1,0:T(8,128)(2,1)S(1)}, u32[]{:S(2)}, u32[]{:S(2)}) collective-permute-start(bf16[512,1024]{1,0:T(8,128)(2,1)S(1)} %get-tuple-element.78.own_first.first), channel_id=1, source_target_pairs={{0,1},{1,0},{2,3},{3,2},{4,5},{5,4},{6,7},{7,6},{8,9},{9,8},{10,11... | collective-permute-start | bytes 3145736 | tf_op jit(solution)/shard_map/ppermute | solution.py:35
  5.0 7.5 %collective-permute-start.3 = (bf16[1024,512]{1,0:T(8,128)(2,1)S(1)}, bf16[1024,512]{1,0:T(8,128)(2,1)S(1)}, u32[]{:S(2)}, u32[]{:S(2)}) collective-permute-start(bf16[1024,512]{1,0:T(8,128)(2,1)S(1)} %get-tuple-element.55.wq), channel_id=1, source_target_pairs={{0,1},{1,0},{2,3},{3,2},{4,5},{5,4},{6,7},{7,6},{8,9},{9,8},{10,11... | collective-permute-start | bytes 3145736 | tf_op jit(solution)/shard_map/ppermute | solution.py:35
  5.5 7.0 %collective-permute-start.4 = (bf16[1024,512]{1,0:T(8,128)(2,1)S(1)}, bf16[1024,512]{1,0:T(8,128)(2,1)S(1)}, u32[]{:S(2)}, u32[]{:S(2)}) collective-permute-start(bf16[1024,512]{1,0:T(8,128)(2,1)S(1)} %get-tuple-element.56.wg), channel_id=1, source_target_pairs={{0,1},{1,0},{2,3},{3,2},{4,5},{5,4},{6,7},{7,6},{8,9},{9,8},{10,11... | collective-permute-start | bytes 3145736 | tf_op jit(solution)/shard_map/ppermute | solution.py:35
  9.0 14.9 %collective-permute-start.9 = (bf16[512,1024]{1,0:T(8,128)(2,1)S(1)}, bf16[512,1024]{1,0:T(8,128)(2,1)S(1)}, u32[]{:S(2)}, u32[]{:S(2)}) collective-permute-start(bf16[512,1024]{1,0:T(8,128)(2,1)S(1)} %columns.1), channel_id=1, source_target_pairs={{0,2},{1,5},{2,0},{3,7},{4,6},{5,1},{6,4},{7,3},{8,10},{9,13},{10,... | collective-permute-start | bytes 3145736 | tf_op jit(solution)/shard_map/ppermute | solution.py:528
  10.6 10.5 %collective-permute-start.5 = (bf16[528,256]{1,0:T(8,128)(2,1)S(1)}, bf16[528,256]{1,0:T(8,128)(2,1)S(1)}, u32[]{:S(2)}, u32[]{:S(2)}) collective-permute-start(bf16[528,256]{1,0:T(8,128)(2,1)S(1)} %get-tuple-element.61.sent), channel_id=1, source_target_pairs={{0,8},{8,16},{16,24},{1,9},{9,17},{17,25},{2,10},{10,18},{18,26},{... | collective-permute-start | bytes 811016 | tf_op jit(solution)/shard_map/ppermute | solution.py:490
  11.9 9.4 %collective-permute-start.6 = (bf16[528,256]{1,0:T(8,128)(2,1)S(1)}, bf16[528,256]{1,0:T(8,128)(2,1)S(1)}, u32[]{:S(2)}, u32[]{:S(2)}) collective-permute-start(bf16[528,256]{1,0:T(8,128)(2,1)S(1)} %get-tuple-element.61.sent), channel_id=1, source_target_pairs={{0,16},{16,0},{1,17},{17,1},{2,18},{18,2},{3,19},{19,3},{4,20},{20... | collective-permute-start | bytes 811016 | tf_op jit(solution)/shard_map/ppermute | solution.py:490
  23.9 24.6 %collective-permute-start.10 = (bf16[512,1024]{1,0:T(8,128)(2,1)S(1)}, bf16[512,1024]{1,0:T(8,128)(2,1)S(1)}, u32[]{:S(2)}, u32[]{:S(2)}) collective-permute-start(bf16[512,1024]{1,0:T(8,128)(2,1)S(1)} %collective-permute-done.9.mine), channel_id=1, source_target_pairs={{0,1},{1,0},{2,3},{3,2},{4,5},{5,4},{6,7},{7,6},{8,9},{9,8},{10,11... | collective-permute-start | bytes 3145736 | tf_op jit(solution)/shard_map/ppermute | solution.py:35
  23.9 10.0 %collective-permute-start.8 = (bf16[256,256]{1,0:T(8,128)(2,1)S(1)}, bf16[256,256]{1,0:T(8,128)(2,1)S(1)}, u32[]{:S(2)}, u32[]{:S(2)}) collective-permute-start(bf16[256,256]{1,0:T(8,128)(2,1)S(1)} %get-tuple-element.66), channel_id=1, source_target_pairs={{8,24},{24,8},{9,25},{25,9},{10,26},{26,10},{11,27},{27,11},{12,28... | collective-permute-start | bytes 393224 | tf_op jit(solution)/shard_map/ppermute | solution.py:490
  26.1 12.9 %collective-permute-start.7 = (bf16[256,256]{1,0:T(8,128)(2,1)S(1)}, bf16[256,256]{1,0:T(8,128)(2,1)S(1)}, u32[]{:S(2)}, u32[]{:S(2)}) collective-permute-start(bf16[256,256]{1,0:T(8,128)(2,1)S(1)} %get-tuple-element.63), channel_id=1, source_target_pairs={{8,24},{24,8},{9,25},{25,9},{10,26},{26,10},{11,27},{27,11},{12,28... | collective-permute-start | bytes 393224 | tf_op jit(solution)/shard_map/ppermute | solution.py:490
  36.0 15.6 %collective-permute-start.12 = (bf16[512,256]{1,0:T(8,128)(2,1)S(1)}, bf16[512,256]{1,0:T(8,128)(2,1)S(1)}, u32[]{:S(2)}, u32[]{:S(2)}) collective-permute-start(bf16[512,256]{1,0:T(8,128)(2,1)S(1)} %get-tuple-element.75.refs_4_), channel_id=1, source_target_pairs={{0,4},{2,6},{4,0},{6,2},{1,5},{3,7},{5,1},{7,3},{8,12},{10,14},{12... | collective-permute-start | bytes 786440 | tf_op jit(solution)/shard_map/ppermute | solution.py:35
  37.5 15.0 %collective-permute-start.15 = (bf16[512,256]{1,0:T(8,128)(2,1)S(1)}, bf16[512,256]{1,0:T(8,128)(2,1)S(1)}, u32[]{:S(2)}, u32[]{:S(2)}) collective-permute-start(bf16[512,256]{1,0:T(8,128)(2,1)S(1)} %get-tuple-element.76.refs_5_), channel_id=1, source_target_pairs={{0,2},{2,0},{4,6},{6,4},{1,3},{3,1},{5,7},{7,5},{8,10},{10,8},{12,... | collective-permute-start | bytes 786440 | tf_op jit(solution)/shard_map/ppermute | solution.py:35
  39.8 7.1 %collective-permute-start.17 = (bf16[256,256]{1,0:T(8,128)(2,1)S(1)}, bf16[256,256]{1,0:T(8,128)(2,1)S(1)}, u32[]{:S(2)}, u32[]{:S(2)}) collective-permute-start(bf16[256,256]{1,0:T(8,128)(2,1)S(1)} %get-tuple-element.73.refs_2_), channel_id=1, source_target_pairs={{0,4},{2,6},{4,0},{6,2},{1,5},{3,7},{5,1},{7,3},{8,12},{10,14},{12... | collective-permute-start | bytes 393224 | tf_op jit(solution)/shard_map/ppermute | solution.py:35
  40.3 12.1 %collective-permute-start.18 = (bf16[256,256]{1,0:T(8,128)(2,1)S(1)}, bf16[256,256]{1,0:T(8,128)(2,1)S(1)}, u32[]{:S(2)}, u32[]{:S(2)}) collective-permute-start(bf16[256,256]{1,0:T(8,128)(2,1)S(1)} %get-tuple-element.74.refs_3_), channel_id=1, source_target_pairs={{0,2},{2,0},{4,6},{6,4},{1,3},{3,1},{5,7},{7,5},{8,10},{10,8},{12,... | collective-permute-start | bytes 393224 | tf_op jit(solution)/shard_map/ppermute | solution.py:35
  46.9 6.4 %collective-permute-start.11 = (bf16[256,256]{1,0:T(8,128)(2,1)S(1)}, bf16[256,256]{1,0:T(8,128)(2,1)S(1)}, u32[]{:S(2)}, u32[]{:S(2)}) collective-permute-start(bf16[256,256]{1,0:T(8,128)(2,1)S(1)} %get-tuple-element.71.refs_0_), channel_id=1, source_target_pairs={{0,4},{2,6},{4,0},{6,2},{1,5},{3,7},{5,1},{7,3},{8,12},{10,14},{12... | collective-permute-start | bytes 393224 | tf_op jit(solution)/shard_map/ppermute | solution.py:35
  48.5 6.7 %collective-permute-start.14 = (bf16[256,256]{1,0:T(8,128)(2,1)S(1)}, bf16[256,256]{1,0:T(8,128)(2,1)S(1)}, u32[]{:S(2)}, u32[]{:S(2)}) collective-permute-start(bf16[256,256]{1,0:T(8,128)(2,1)S(1)} %get-tuple-element.72.refs_1_), channel_id=1, source_target_pairs={{0,2},{2,0},{4,6},{6,4},{1,3},{3,1},{5,7},{7,5},{8,10},{10,8},{12,... | collective-permute-start | bytes 393224 | tf_op jit(solution)/shard_map/ppermute | solution.py:35
  51.8 9.3 %collective-permute-start.19 = (bf16[256,512]{1,0:T(8,128)(2,1)S(1)}, bf16[256,512]{1,0:T(8,128)(2,1)S(1)}, u32[]{:S(2)}, u32[]{:S(2)}) collective-permute-start(bf16[256,512]{1,0:T(8,128)(2,1)S(1)} %give.6), channel_id=1, source_target_pairs={{0,2},{2,0},{4,6},{6,4},{1,3},{3,1},{5,7},{7,5},{8,10},{10,8},{12,... | collective-permute-start | bytes 786440 | tf_op jit(solution)/shard_map/ppermute | solution.py:35
  52.8 9.3 %collective-permute-start.20 = (bf16[256,512]{1,0:T(8,128)(2,1)S(1)}, bf16[256,512]{1,0:T(8,128)(2,1)S(1)}, u32[]{:S(2)}, u32[]{:S(2)}) collective-permute-start(bf16[256,512]{1,0:T(8,128)(2,1)S(1)} %give.7), channel_id=1, source_target_pairs={{0,4},{2,6},{4,0},{6,2},{1,5},{3,7},{5,1},{7,3},{8,12},{10,14},{12... | collective-permute-start | bytes 786440 | tf_op jit(solution)/shard_map/ppermute | solution.py:35
  53.6 11.0 %collective-permute-start.13 = (bf16[256,512]{1,0:T(8,128)(2,1)S(1)}, bf16[256,512]{1,0:T(8,128)(2,1)S(1)}, u32[]{:S(2)}, u32[]{:S(2)}) collective-permute-start(bf16[256,512]{1,0:T(8,128)(2,1)S(1)} %give.4), channel_id=1, source_target_pairs={{0,2},{2,0},{4,6},{6,4},{1,3},{3,1},{5,7},{7,5},{8,10},{10,8},{12,... | collective-permute-start | bytes 786440 | tf_op jit(solution)/shard_map/ppermute | solution.py:35
  55.5 9.4 %collective-permute-start.16 = (bf16[256,512]{1,0:T(8,128)(2,1)S(1)}, bf16[256,512]{1,0:T(8,128)(2,1)S(1)}, u32[]{:S(2)}, u32[]{:S(2)}) collective-permute-start(bf16[256,512]{1,0:T(8,128)(2,1)S(1)} %give.5), channel_id=1, source_target_pairs={{0,4},{2,6},{4,0},{6,2},{1,5},{3,7},{5,1},{7,3},{8,12},{10,14},{12... | collective-permute-start | bytes 786440 | tf_op jit(solution)/shard_map/ppermute | solution.py:35

commit v13 on v11

--- a/solution.py
+++ b/solution.py
@@ -159,21 +159,22 @@
 
     starts = range(0, rows, BLOCK)
     logs, key = loads.start(log_decay_far, log_decay), loads.start(wk_far, wk)
-    tiles = [tile(x_own, core, start) for start in starts]
+    tiles = [tile(x_own, core, 0)]
+    logs.wait()
+    tiles += [tile(x_own, core, start) for start in starts[1:]]
     value = loads.start(wv_far, wv)
-    others = [tile(x_other, 1 - core, start) for start in starts]
-    others += [loads.start(wo_far, wo), loads.start(wq_far, wq), loads.start(wg_far, wg)]
+    angle_tables(coarse, fine)
+    decay_sums(log_decay, decay)
     key.wait()
     tiles[0].wait()
+    others = [tile(x_other, 1 - core, 0)]
+    others += [loads.start(far, near) for far, near in ((wo_far, wo), (wq_far, wq), (wg_far, wg))]
     for number, start in enumerate(starts):
         at = slice(start, start + BLOCK)
         if number:
             tiles[number].wait()
         acc_k[at, :] = mm(x_own[at, :], wk[...])
     value.wait()
-    logs.wait()
-    angle_tables(coarse, fine)
-    decay_sums(log_decay, decay)
     for start in starts:
         at = slice(start, start + BLOCK)
         acc_v[at, :] = mm(x_own[at, :], wv[...])
@@ -181,23 +182,22 @@
         copy.wait()
 
 
+def block_ends(decay, start, stop):
+    ends = [decay[:, end - 1 : end] for end in range(start + BLOCK, stop + 1, BLOCK)]
+    return functools.reduce(lambda a, b: a + b, ends, jnp.zeros((decay.shape[0], 1), F32))
+
+
 def pack_message(message, states, logs):
-    heads = len(states)
-    place = lax.broadcasted_iota(jnp.int32, (EXTRA, DH), 0)
-    tail = jnp.zeros((EXTRA, DH), F32)
-    for head in range(heads):
-        message[head * DH : (head + 1) * DH, :] = states[head].astype(BF16)
-        rest = logs[head]
-        for number in range(3):
-            piece = rest.astype(BF16).astype(F32)
-            tail = jnp.where(place == 3 * head + number, piece, tail)
-            rest = rest - piece
-    message[heads * DH :, :] = tail.astype(BF16)
-
-
-def message_log(message, heads, head):
+    for head, state in enumerate(states):
+        message[head * DH : (head + 1) * DH, :] = state.astype(BF16)
+    large = logs.astype(BF16).astype(F32)
+    parts = jnp.concatenate([large, logs - large], axis=0)
+    message[len(states) * DH :, :] = jnp.broadcast_to(parts, (EXTRA, DH)).astype(BF16)
+
+
+def message_log(message, heads):
     tail = message[heads * DH :, :].astype(F32)
-    return (tail[3 * head : 3 * head + 1] + tail[3 * head + 1 : 3 * head + 2] + tail[3 * head + 2 : 3 * head + 3])[:, :1]
+    return (tail[: EXTRA // 2] + tail[EXTRA // 2 :])[:, :1]
 
 
 def exchanges(ctx, hop):
@@ -223,27 +223,37 @@
     return functools.reduce(lambda a, b: a + b, parts)
 
 
-def arrived_log(arrivals, sets, hop, heads, head):
-    parts = [jnp.where(is_upper(lowers, hop), message_log(ref, heads, head), 0.0) for ref, lowers in zip(arrivals, sets)]
+def arrived_log(arrivals, sets, hop, heads):
+    parts = [jnp.where(is_upper(lowers, hop), message_log(ref, heads), 0.0) for ref, lowers in zip(arrivals, sets)]
     return functools.reduce(lambda a, b: a + b, parts)
 
 
 def key_value_kernel(
-    heads, x, wk, wv, acc_k, acc_v, decay, coarse, fine, k_out, v_out, before_out, state_out, message
+    heads, x_far, x_first, wk, wv, acc_k, acc_v, decay, coarse, fine,
+    x_rest, k_out, v_out, before_out, state_out, message, arrived,
 ):
+    part = wk.shape[0]
+    blocks = acc_k.shape[0] // BLOCK
+    loads = Loads(arrived)
+    columns = pl.ds(pl.multiple_of((1 - lax.axis_index("fsdp")) * part, part), part)
+    rest = [
+        loads.start(x_far.at[pl.ds(block * BLOCK, BLOCK), columns], x_rest.at[pl.ds((block - 1) * BLOCK, BLOCK)])
+        for block in range(1, blocks)
+    ]
     state_out[...] = jnp.zeros_like(state_out)
-
-    totals = jnp.zeros((1, 8), F32)
-    for block in range(x.shape[0] // BLOCK):
+    for block in range(blocks):
         start = block * BLOCK
-        columns = decay[:, slice(start, start + BLOCK)].T
+        at = slice(start, start + BLOCK)
+        columns = decay[:, at].T
         ending = columns[BLOCK - 1 : BLOCK, :]
         faded = jnp.exp(ending - columns)
-        at = slice(start, start + BLOCK)
+        if block:
+            rest[block - 1].wait()
+        x = x_rest[start - BLOCK : start, :] if block else x_first[...]
         cosine, sine = angles(coarse, fine, start, BLOCK)
-        keys = turned(acc_k[at, :] + mm(x[at, :], wk[...]), cosine, sine)
+        keys = turned(acc_k[at, :] + mm(x, wk[...]), cosine, sine)
         k_out[at, :] = keys
-        values = (acc_v[at, :] + mm(x[at, :], wv[...])).astype(BF16)
+        values = (acc_v[at, :] + mm(x, wv[...])).astype(BF16)
         v_out[at, :] = values
         for head in range(heads):
             span = slice(head * DH, (head + 1) * DH)
@@ -251,36 +261,32 @@
             old = state_out[span, :]
             before_out[block, span, :] = old.astype(BF16)
             state_out[span, :] = jnp.exp(ending[:, head : head + 1]) * old + mm_tn(weighted, values[:, span])
-        totals = totals + ending
     states = [state_out[head * DH : (head + 1) * DH, :] for head in range(heads)]
-    pack_message(message, states, [totals[:, head : head + 1] for head in range(heads)])
-
-
-def combine_kernel(heads, hop, sets, first, state, sent, *refs):
+    pack_message(message, states, block_ends(decay, 0, acc_k.shape[0]))
+
+
+def combine_kernel(heads, hop, sets, first, last, state, sent, *refs):
     if not first:
         old_entering, refs = refs[0], refs[1:]
-    arrivals = refs[: len(sets)]
-    window, entering, message = refs[len(sets) :]
-    states, logs = [], []
+    arrivals, entering, message = refs[: len(sets)], refs[len(sets)], refs[len(sets) + 1]
+    window_log, log = message_log(sent, heads), arrived_log(arrivals, sets, hop, heads)
+    before_log = jnp.zeros_like(log) if first else old_entering[heads * DH :, :1]
+    states = []
     for head in range(heads):
-        span = slice(head * DH, (head + 1) * DH)
-        row = slice(heads * DH + head, heads * DH + head + 1)
+        span, row = slice(head * DH, (head + 1) * DH), slice(head, head + 1)
         arrived = arrived_state(arrivals, sets, hop, span)
-        log = arrived_log(arrivals, sets, hop, heads, head)
-        window_log = message_log(sent, heads, head)
         if first:
             entering[span, :] = arrived
-            entering_log = log
         else:
-            before_log = old_entering[row, :1]
-            entering[span, :] = old_entering[span, :] + jnp.exp(before_log) * arrived
-            entering_log = before_log + log
-        entering[row, :] = jnp.broadcast_to(entering_log, (1, DH))
-        new = state[span, :] + jnp.exp(window_log) * arrived
-        window[span, :] = new
-        states.append(new)
-        logs.append(window_log + log)
-    pack_message(message, states, logs)
+            entering[span, :] = old_entering[span, :] + jnp.exp(before_log[row]) * arrived
+        states.append(state[span, :] + jnp.exp(window_log[row]) * arrived)
+        if last:
+            message[span, :] = states[-1].astype(BF16)
+        else:
+            refs[len(sets) + 2][span, :] = states[-1]
+    entering[heads * DH :, :] = jnp.broadcast_to(before_log + log, (8, DH))
+    if not last:
+        pack_message(message, states, window_log + log)
 
 
 def query_gate_kernel(
@@ -292,8 +298,11 @@
 
     at = slice(start, start + BLOCK)
     cosine, sine = angles(coarse, fine, start, BLOCK)
-    q_out[...] = turned(mm(x_own[at, :], wq[...]) + mm(x_other[at, :], wq_far[...]), cosine, sine)
-    gates = (mm(x_own[at, :], wg[...]) + mm(x_other[at, :], wg_far[...])).astype(BF16).astype(F32)
+    far = slice(max(start - BLOCK, 0), max(start - BLOCK, 0) + BLOCK)
+    queries = mm(x_own[at, :], wq[...]) + mm(x_other[far, :], wq_far[...])
+    q_out[...] = turned(queries, cosine, sine)
+    gates = mm(x_own[at, :], wg[...]) + mm(x_other[far, :], wg_far[...])
+    gates = gates.astype(BF16).astype(F32)
     g_out[...] = gates / (1.0 + jnp.exp(-gates))
     for piece in range(BLOCK // TILE):
         low, last = piece * TILE, (piece + 1) * TILE
@@ -425,25 +434,27 @@
     key_far = swap(key_weight, "fsdp", 1)
     value_far = swap(value_weight, "fsdp", 1)
 
-    x_own, x_other, acc_k, acc_v, decay, coarse, fine, out_first, own_q, own_g = loading_call(
+    x_own, x_first, acc_k, acc_v, decay, coarse, fine, out_first, own_q, own_g = loading_call(
         key_value_own_kernel,
-        [((rows, part), BF16)] * 2
-        + [((rows, cols), F32)] * 2
-        + [((8, rows), F32)]
+        [((rows, part), BF16), ((BLOCK, part), BF16), ((rows, cols), F32), ((rows, cols), F32), ((8, rows), F32)]
         + tables
         + [(out_weight.shape, BF16), ((part, cols), BF16), ((part, cols), BF16)],
         [x, key_weight, value_weight, log_decay[0].T, out_weight, query_weight, gate_weight],
         [],
         [pltpu.VMEM((part, cols), BF16)] * 2 + [pltpu.VMEM((heads, rows), F32)],
-        2 * (rows // BLOCK) + 6,
+        rows // BLOCK + 7,
         "key_value_own",
     )
     state_shape, message_shape = (heads * DH, DH), (heads * DH + EXTRA, DH)
-    keys, values, before, window, message = kernel_call(
+    x_rest, keys, values, before, window, message = loading_call(
         functools.partial(key_value_kernel, heads),
-        [((rows, cols), BF16)] * 2
+        [((rows - BLOCK, part), BF16)]
+        + [((rows, cols), BF16)] * 2
         + [((blocks, heads * DH, DH), BF16), (state_shape, F32), (message_shape, BF16)],
-        [x_other, key_far, value_far, acc_k, acc_v, decay, coarse, fine],
+        [x],
+        [x_first, key_far, value_far, acc_k, acc_v, decay, coarse, fine],
+        [],
+        rows // BLOCK - 1,
         "key_value",
     )
     far_q, far_g = swap(own_q, "fsdp", 1), swap(own_g, "fsdp", 1)
@@ -452,7 +463,7 @@
         return kernel_call(
             functools.partial(query_gate_kernel, heads, block),
             [((BLOCK, cols), BF16), ((BLOCK, cols), F32), ((BLOCK, cols), F32)],
-            [x_own, x_other, own_q, far_q, own_g, far_g, decay, coarse, fine, keys, values],
+            [x_own, x_rest if block else x_first, own_q, far_q, own_g, far_g, decay, coarse, fine, keys, values],
             "query_gate",
         )
 
@@ -475,12 +486,15 @@
         unchanged = exchanges(ctx, 2 * hop)[0]
         early = [exchange(message, unchanged, 2 * hop)]
         old = [] if entering is None else [entering]
-        window, entering, message = kernel_call(
-            functools.partial(combine_kernel, heads, hop, sets, entering is None),
-            [(state_shape, F32), ((heads * DH + 8, DH), F32), (message_shape, BF16)],
+        last = 4 * hop >= ctx
+        entering, message, *windows = kernel_call(
+            functools.partial(combine_kernel, heads, hop, sets, entering is None, last),
+            [((heads * DH + 8, DH), F32)]
+            + ([(state_shape, BF16)] if last else [(message_shape, BF16), (state_shape, F32)]),
             [window, message, *old, *arrivals],
             "combine",
         )
+        window = windows[0] if windows else None
         hop *= 2
 
     own_second = swap(out_first, "fsdp", 1)

time: 62.9 us -> 62.9 us (level)
  waiting for transfers between devices: 25.3 us -> 23.5 us
  starting transfers between devices: 13.8 us -> 15.4 us
    pallas_call x1 -> x2, Pallas kernels: 4.44 us -> 8.62 us  [loading_call(): pl.pallas_call(kernel, in_specs=[pl.BlockSpec(memory_space=pltpu.HBM)] *...]
    pallas_call x14 -> x13, Pallas kernels: 16.9 us -> 12.9 us  [kernel_call(): pl.pallas_call(kernel, in_specs=[pl.BlockSpec(memory_space=pltpu.VMEM)] *...]
    ppermute x14, waiting for transfers between devices: 15.4 us -> 13.2 us  [swap(): lax.ppermute(value, axis, [(place, place ^ mask) for place in range(size)])]
    ppermute x14, starting transfers between devices: 7.19 us -> 8.77 us  [swap(): lax.ppermute(value, axis, [(place, place ^ mask) for place in range(size)])]
where the time goes in v13:
time: 62.9 us; the launch traced here: 62.5 us
  waiting for transfers between devices  23.5 us (37%)
  Pallas kernels  23.2 us (37%)
  starting transfers between devices  15.4 us (24%)
    ppermute x14, waiting for transfers between devices, swap(): lax.ppermute(value, axis, [(place, place ^ mask) for place in range(size)])  13.2 us
    pallas_call x13, Pallas kernels, kernel_call(): pl.pallas_call(kernel, in_specs=[pl.BlockSpec(memory_space=pltpu.VMEM)] *...  12.9 us
    ppermute x3, waiting for transfers between devices, exchange(): return lax.ppermute(message, 'ctx', pairs)  10.3 us
    ppermute x14, starting transfers between devices, swap(): lax.ppermute(value, axis, [(place, place ^ mask) for place in range(size)])  8.77 us
    pallas_call x2, Pallas kernels, loading_call(): pl.pallas_call(kernel, in_specs=[pl.BlockSpec(memory_space=pltpu.HBM)] *...  8.62 us
    ppermute x3, starting transfers between devices, exchange(): return lax.ppermute(message, 'ctx', pairs)  5.1 us
    pallas_call x2, Pallas kernels, on_device(): pl.pallas_call(functools.partial(finish_kernel, part_order), in_specs=[pl...  1.7 us
    ppermute x1, starting transfers between devices, on_device(): out_mine = lax.ppermute(for_partner, ('tp', 'fsdp'), pairs)  1.55 us
  transfers between devices with their start and end apart: 18, of which 8 were waited for; matrix products, arithmetic and copies ran while one was open for 0% of the time, Pallas kernels for 36%

profile of v13, /device:TPU:24, one launch (start us, length us, event | category | flops | bytes accessed | tf_op | source)
XLA Modules:
  0.0 62.5 jit_solution(13386913703695882092)
XLA Ops:
  0.0 0.5 collective-permute-start.2
  0.5 4.3 %key_value_own.1 = (bf16[1024,1024]{1,0:T(8,128)(2,1)S(1)}, bf16[512,1024]{1,0:T(8,128)(2,1)S(1)}, f32[1024,512]{1,0:T(8,128)S(1)}, f32[1024,512]{1,0:T(8,128)S(...) custom-call(bf16[1024,2048]{1,0:T(8,128)(2,1)} %bitcast.4, ...), custom_call_target="tpu_custom_call" | custom-call | flops 1 | bytes 1 | tf_op jit(solution)/shard_map/key_value_own/pallas_call | solution.py:56
  4.9 0.5 collective-permute-start.3
  5.5 4.3 %key_value.1 = (bf16[512,1024]{1,0:T(8,128)(2,1)S(1)}, bf16[1024,512]{1,0:T(8,128)(2,1)S(1)}, bf16[1024,512]{1,0:T(8,128)(2,1)S(1)}, bf16[2,512,256]{2,1,0:T(8,1...) custom-call(bf16[1024,2048]{1,0:T(8,128)(2,1)} %bitcast.5, ...), custom_call_target="tpu_custom_call" | custom-call | flops 1 | bytes 1 | tf_op jit(solution)/shard_map/key_value/pallas_call | solution.py:56
  9.9 1.6 %collective-permute-start.9 = (bf16[512,1024]{1,0:T(8,128)(2,1)S(1)}, bf16[512,1024]{1,0:T(8,128)(2,1)S(1)}, u32[]{:S(2)}, u32[]{:S(2)}) collective-permute-start(bf16[512,1024]{1,0:T(8,128)(2,1)S(1)} %columns.1), channel_id=1, source_target_pairs={{0,2},{1,5},{2,0},{3,7},{4,6},{5,1},{6,4},{7,3},{8,10},{9,13},{10,... | collective-permute-start | bytes 3145736 | tf_op jit(solution)/shard_map/ppermute | solution.py:508
  11.5 1.3 %collective-permute-start.5 = (bf16[528,256]{1,0:T(8,128)(2,1)S(1)}, bf16[528,256]{1,0:T(8,128)(2,1)S(1)}, u32[]{:S(2)}, u32[]{:S(2)}) collective-permute-start(bf16[528,256]{1,0:T(8,128)(2,1)S(1)} %get-tuple-element.59.sent), channel_id=1, source_target_pairs={{0,8},{8,16},{16,24},{1,9},{9,17},{17,25},{2,10},{10,18},{18,26},{... | collective-permute-start | bytes 811016 | tf_op jit(solution)/shard_map/ppermute | solution.py:474
  12.8 0.7 %collective-permute-start.7 = (bf16[528,256]{1,0:T(8,128)(2,1)S(1)}, bf16[528,256]{1,0:T(8,128)(2,1)S(1)}, u32[]{:S(2)}, u32[]{:S(2)}) collective-permute-start(bf16[528,256]{1,0:T(8,128)(2,1)S(1)} %get-tuple-element.59.sent), channel_id=1, source_target_pairs={{0,16},{16,0},{1,17},{17,1},{2,18},{18,2},{3,19},{19,3},{4,20},{20... | collective-permute-start | bytes 811016 | tf_op jit(solution)/shard_map/ppermute | solution.py:474
  13.5 3.1 %query_gate.2 = (bf16[512,512]{1,0:T(8,128)(2,1)S(1)}, f32[512,512]{1,0:T(8,128)S(1)}, f32[512,512]{1,0:T(8,128)S(1)}) custom-call(bf16[1024,1024]{1,0:T(8,128)(2,1)S(1)} %get-tuple-element.52.x_own, bf16[512,1024]{1,0:T(8,128)(2,1)S(1)} %get-tuple-element.45.x_first.x_other, bf16[1024,512]{1,0:T(8,128)(2,1)S(1)} %get-tuple-element.53.wq, ...), custom_call_target="tpu_custom_call" | custom-call | flops 1 | bytes 1 | tf_op jit(solution)/shard_map/query_gate/pallas_call | solution.py:40
  16.5 5.4 %collective-permute-done.5.refs_0_ = bf16[528,256]{1,0:T(8,128)(2,1)S(1)} collective-permute-done((bf16[528,256]{1,0:T(8,128)(2,1)S(1)}, bf16[528,256]{1,0:T(8,128)(2,1)S(1)}, u32[]{:S(2)}, u32[]{:S(2)}) %collective-permute-start.5) | collective-permute-done | bytes 270368 | tf_op jit(solution)/shard_map/ppermute | solution.py:474
  22.1 3.1 %collective-permute-start.6 = (bf16[512,256]{1,0:T(8,128)(2,1)S(1)}, bf16[512,256]{1,0:T(8,128)(2,1)S(1)}, u32[]{:S(2)}, u32[]{:S(2)}) collective-permute-start(bf16[512,256]{1,0:T(8,128)(2,1)S(1)} %get-tuple-element.61), channel_id=1, source_target_pairs={{8,24},{24,8},{9,25},{25,9},{10,26},{26,10},{11,27},{27,11},{12,28... | collective-permute-start | bytes 786440 | tf_op jit(solution)/shard_map/ppermute | solution.py:474
  25.3 3.1 %query_gate.3 = (bf16[512,512]{1,0:T(8,128)(2,1)S(1)}, f32[512,512]{1,0:T(8,128)S(1)}, f32[512,512]{1,0:T(8,128)S(1)}) custom-call(bf16[1024,1024]{1,0:T(8,128)(2,1)S(1)} %get-tuple-element.52.x_own, bf16[512,1024]{1,0:T(8,128)(2,1)S(1)} %get-tuple-element.64.x_other, bf16[1024,512]{1,0:T(8,128)(2,1)S(1)} %get-tuple-element.53.wq, ...), custom_call_target="tpu_custom_call" | custom-call | flops 1 | bytes 1 | tf_op jit(solution)/shard_map/query_gate/pallas_call | solution.py:40
  28.3 4.9 %collective-permute-done.6.refs_0_ = bf16[512,256]{1,0:T(8,128)(2,1)S(1)} collective-permute-done((bf16[512,256]{1,0:T(8,128)(2,1)S(1)}, bf16[512,256]{1,0:T(8,128)(2,1)S(1)}, u32[]{:S(2)}, u32[]{:S(2)}) %collective-permute-start.6) | collective-permute-done | bytes 262176 | tf_op jit(solution)/shard_map/ppermute | solution.py:474
  33.3 1.5 %hidden.3 = (bf16[256,512]{1,0:T(8,128)(2,1)S(1)}, bf16[256,512]{1,0:T(8,128)(2,1)S(1)}, bf16[16,128]{1,0:T(8,128)(2,1)}) custom-call(f32[8,1024]{1,0:T(8,128)S(1)} %get-tuple-element.65.decay, bf16[2,512,256]{2,1,0:T(8,128)(2,1)S(1)} %get-tuple-element.50.before, f32[520,256]{1,0:T(8,128)S(1)} %get-tuple-element.60.entering, ...), custom_call_target="tpu_custom_call" | custom-call | flops 1 | bytes 1 | tf_op jit(solution)/shard_map/hidden/pallas_call | solution.py:40
  34.9 1.4 %collective-permute-start.15 = (bf16[256,512]{1,0:T(8,128)(2,1)S(1)}, bf16[256,512]{1,0:T(8,128)(2,1)S(1)}, u32[]{:S(2)}, u32[]{:S(2)}) collective-permute-start(bf16[256,512]{1,0:T(8,128)(2,1)S(1)} %get-tuple-element.72.refs_3_), channel_id=1, source_target_pairs={{0,2},{2,0},{4,6},{6,4},{1,3},{3,1},{5,7},{7,5},{8,10},{10,8},{12,... | collective-permute-start | bytes 786440 | tf_op jit(solution)/shard_map/ppermute | solution.py:35
  36.2 0.7 %collective-permute-start.14 = (bf16[256,512]{1,0:T(8,128)(2,1)S(1)}, bf16[256,512]{1,0:T(8,128)(2,1)S(1)}, u32[]{:S(2)}, u32[]{:S(2)}) collective-permute-start(bf16[256,512]{1,0:T(8,128)(2,1)S(1)} %get-tuple-element.71.refs_2_), channel_id=1, source_target_pairs={{0,4},{2,6},{4,0},{6,2},{1,5},{3,7},{5,1},{7,3},{8,12},{10,14},{12... | collective-permute-start | bytes 786440 | tf_op jit(solution)/shard_map/ppermute | solution.py:35
  36.9 1.5 %hidden.2 = (bf16[256,512]{1,0:T(8,128)(2,1)S(1)}, bf16[256,512]{1,0:T(8,128)(2,1)S(1)}, bf16[16,128]{1,0:T(8,128)(2,1)}) custom-call(f32[8,1024]{1,0:T(8,128)S(1)} %get-tuple-element.65.decay, bf16[2,512,256]{2,1,0:T(8,128)(2,1)S(1)} %get-tuple-element.50.before, f32[520,256]{1,0:T(8,128)S(1)} %get-tuple-element.60.entering, ...), custom_call_target="tpu_custom_call" | custom-call | flops 1 | bytes 1 | tf_op jit(solution)/shard_map/hidden/pallas_call | solution.py:40
  38.4 0.6 collective-permute-start.12
  39.0 1.5 %collective-permute-start.8 = (bf16[256,512]{1,0:T(8,128)(2,1)S(1)}, bf16[256,512]{1,0:T(8,128)(2,1)S(1)}, u32[]{:S(2)}, u32[]{:S(2)}) collective-permute-start(bf16[256,512]{1,0:T(8,128)(2,1)S(1)} %get-tuple-element.69.refs_0_), channel_id=1, source_target_pairs={{0,4},{2,6},{4,0},{6,2},{1,5},{3,7},{5,1},{7,3},{8,12},{10,14},{12... | collective-permute-start | bytes 786440 | tf_op jit(solution)/shard_map/ppermute | solution.py:35
  40.5 1.3 %own_products.1 = (f32[512,1024]{1,0:T(8,128)S(1)}, f32[512,1024]{1,0:T(8,128)S(1)}) custom-call(bf16[512,1024]{1,0:T(8,128)(2,1)S(1)} %get-tuple-element.74.own_first.first, bf16[512,1024]{1,0:T(8,128)(2,1)S(1)} %collective-permute-done.own_second.second, bf16[256,512]{1,0:T(8,128)(2,1)S(1)} %get-tuple-element.69.refs_0_, ...), custom_call_target="tpu_custom_call" | custom-call | flops 1 | bytes 1 | tf_op jit(solution)/shard_map/own_products/pallas_call | solution.py:40
  42.1 1.9 %collective-permute-done.15.refs_3_.far = bf16[256,512]{1,0:T(8,128)(2,1)S(1)} collective-permute-done((bf16[256,512]{1,0:T(8,128)(2,1)S(1)}, bf16[256,512]{1,0:T(8,128)(2,1)S(1)}, u32[]{:S(2)}, u32[]{:S(2)}) %collective-permute-start.15) | collective-permute-done | bytes 262176 | tf_op jit(solution)/shard_map/ppermute | solution.py:35
  44.3 0.6 collective-permute-start.17
  44.9 0.5 collective-permute-done.14.refs_2_.far
  45.7 1.1 %collective-permute-start.16 = (bf16[256,512]{1,0:T(8,128)(2,1)S(1)}, bf16[256,512]{1,0:T(8,128)(2,1)S(1)}, u32[]{:S(2)}, u32[]{:S(2)}) collective-permute-start(bf16[256,512]{1,0:T(8,128)(2,1)S(1)} %give.6), channel_id=1, source_target_pairs={{0,2},{2,0},{4,6},{6,4},{1,3},{3,1},{5,7},{7,5},{8,10},{10,8},{12,... | collective-permute-start | bytes 786440 | tf_op jit(solution)/shard_map/ppermute | solution.py:35
  46.8 2.9 %collective-permute-done.12.far.refs_1_ = bf16[256,512]{1,0:T(8,128)(2,1)S(1)} collective-permute-done((bf16[256,512]{1,0:T(8,128)(2,1)S(1)}, bf16[256,512]{1,0:T(8,128)(2,1)S(1)}, u32[]{:S(2)}, u32[]{:S(2)}) %collective-permute-start.12) | collective-permute-done | bytes 262176 | tf_op jit(solution)/shard_map/ppermute | solution.py:35
  50.0 0.6 collective-permute-start.13
  50.5 0.5 collective-permute-done.8.far.refs_0_
  51.3 1.1 %collective-permute-start.11 = (bf16[256,512]{1,0:T(8,128)(2,1)S(1)}, bf16[256,512]{1,0:T(8,128)(2,1)S(1)}, u32[]{:S(2)}, u32[]{:S(2)}) collective-permute-start(bf16[256,512]{1,0:T(8,128)(2,1)S(1)} %give.4), channel_id=1, source_target_pairs={{0,2},{2,0},{4,6},{6,4},{1,3},{3,1},{5,7},{7,5},{8,10},{10,8},{12,... | collective-permute-start | bytes 786440 | tf_op jit(solution)/shard_map/ppermute | solution.py:35
  52.4 0.7 %keep.1 = (f32[512,512]{1,0:T(8,128)S(1)}, f32[512,512]{1,0:T(8,128)S(1)}) custom-call(bf16[256,512]{1,0:T(8,128)(2,1)S(1)} %collective-permute-done.8.far.refs_0_, bf16[256,512]{1,0:T(8,128)(2,1)S(1)} %collective-permute-done.12.far.refs_1_, bf16[256,512]{1,0:T(8,128)(2,1)S(1)} %collective-permute-done.14.refs_2_.far, ...), custom_call_target="tpu_custom_call" | custom-call | flops 1 | bytes 1 | tf_op jit(solution)/shard_map/keep/pallas_call | solution.py:40
  53.1 3.5 %collective-permute-done.17.refs_1_ = bf16[256,512]{1,0:T(8,128)(2,1)S(1)} collective-permute-done((bf16[256,512]{1,0:T(8,128)(2,1)S(1)}, bf16[256,512]{1,0:T(8,128)(2,1)S(1)}, u32[]{:S(2)}, u32[]{:S(2)}) %collective-permute-start.17) | collective-permute-done | bytes 262176 | tf_op jit(solution)/shard_map/ppermute | solution.py:35
  56.6 0.9 %finish.2.refs_4_ = bf16[1,1024,512]{2,1,0:T(8,128)(2,1)} custom-call(bf16[256,512]{1,0:T(8,128)(2,1)S(1)} %collective-permute-done.16.refs_0_, bf16[256,512]{1,0:T(8,128)(2,1)S(1)} %collective-permute-done.17.refs_1_, f32[512,512]{1,0:T(8,128)S(1)} %get-tuple-element.79.refs_2_, f32[512,512]{1,0:T(8,128)S(1)} %get-tuple-element.80.refs_3_), custom_call_target="tpu_custom_call" | custom-call | tf_op jit(solution)/shard_map/finish/pallas_call | solution.py:562
  57.5 4.0 %collective-permute-done.13.refs_1_ = bf16[256,512]{1,0:T(8,128)(2,1)S(1)} collective-permute-done((bf16[256,512]{1,0:T(8,128)(2,1)S(1)}, bf16[256,512]{1,0:T(8,128)(2,1)S(1)}, u32[]{:S(2)}, u32[]{:S(2)}) %collective-permute-start.13) | collective-permute-done | bytes 262176 | tf_op jit(solution)/shard_map/ppermute | solution.py:35
  61.4 0.9 %finish.3 = bf16[1,1024,512]{2,1,0:T(8,128)(2,1)} custom-call(bf16[256,512]{1,0:T(8,128)(2,1)S(1)} %collective-permute-done.11.refs_0_, bf16[256,512]{1,0:T(8,128)(2,1)S(1)} %collective-permute-done.13.refs_1_, f32[512,512]{1,0:T(8,128)S(1)} %get-tuple-element.79.refs_2_, f32[512,512]{1,0:T(8,128)S(1)} %get-tuple-element.80.refs_3_, ...), custom_call_target="tpu_custom_call", output_to_operand_aliasing={{}: (4, {})} | custom-call | tf_op jit(solution)/shard_map/finish/pallas_call | solution.py:562
  (21 shorter events, 2.0 us)
Async XLA Ops:
  0.0 5.5 %collective-permute-start.1 = (bf16[1024,512]{1,0:T(8,128)(2,1)}, bf16[1024,512]{1,0:T(8,128)(2,1)S(1)}, u32[]{:S(2)}, u32[]{:S(2)}) collective-permute-start(bf16[1024,512]{1,0:T(8,128)(2,1)} %wk_far.1), channel_id=1, source_target_pairs={{0,1},{1,0},{2,3},{3,2},{4,5},{5,4},{6,7},{7,6},{8,9},{9,8},{10,11... | collective-permute-start | bytes 3145736 | tf_op jit(solution)/shard_map/ppermute | solution.py:35
  0.0 5.5 %collective-permute-start.2 = (bf16[1024,512]{1,0:T(8,128)(2,1)}, bf16[1024,512]{1,0:T(8,128)(2,1)S(1)}, u32[]{:S(2)}, u32[]{:S(2)}) collective-permute-start(bf16[1024,512]{1,0:T(8,128)(2,1)} %wv_far.1), channel_id=1, source_target_pairs={{0,1},{1,0},{2,3},{3,2},{4,5},{5,4},{6,7},{7,6},{8,9},{9,8},{10,11... | collective-permute-start | bytes 3145736 | tf_op jit(solution)/shard_map/ppermute | solution.py:35
  4.9 5.0 %collective-permute-start = (bf16[512,1024]{1,0:T(8,128)(2,1)S(1)}, bf16[512,1024]{1,0:T(8,128)(2,1)S(1)}, u32[]{:S(2)}, u32[]{:S(2)}) collective-permute-start(bf16[512,1024]{1,0:T(8,128)(2,1)S(1)} %get-tuple-element.74.own_first.first), channel_id=1, source_target_pairs={{0,1},{1,0},{2,3},{3,2},{4,5},{5,4},{6,7},{7,6},{8,9},{9,8},{10,11... | collective-permute-start | bytes 3145736 | tf_op jit(solution)/shard_map/ppermute | solution.py:35
  4.9 8.5 %collective-permute-start.3 = (bf16[1024,512]{1,0:T(8,128)(2,1)S(1)}, bf16[1024,512]{1,0:T(8,128)(2,1)S(1)}, u32[]{:S(2)}, u32[]{:S(2)}) collective-permute-start(bf16[1024,512]{1,0:T(8,128)(2,1)S(1)} %get-tuple-element.53.wq), channel_id=1, source_target_pairs={{0,1},{1,0},{2,3},{3,2},{4,5},{5,4},{6,7},{7,6},{8,9},{9,8},{10,11... | collective-permute-start | bytes 3145736 | tf_op jit(solution)/shard_map/ppermute | solution.py:35
  5.4 8.0 %collective-permute-start.4 = (bf16[1024,512]{1,0:T(8,128)(2,1)S(1)}, bf16[1024,512]{1,0:T(8,128)(2,1)S(1)}, u32[]{:S(2)}, u32[]{:S(2)}) collective-permute-start(bf16[1024,512]{1,0:T(8,128)(2,1)S(1)} %get-tuple-element.54.wg), channel_id=1, source_target_pairs={{0,1},{1,0},{2,3},{3,2},{4,5},{5,4},{6,7},{7,6},{8,9},{9,8},{10,11... | collective-permute-start | bytes 3145736 | tf_op jit(solution)/shard_map/ppermute | solution.py:35
  9.9 24.8 %collective-permute-start.9 = (bf16[512,1024]{1,0:T(8,128)(2,1)S(1)}, bf16[512,1024]{1,0:T(8,128)(2,1)S(1)}, u32[]{:S(2)}, u32[]{:S(2)}) collective-permute-start(bf16[512,1024]{1,0:T(8,128)(2,1)S(1)} %columns.1), channel_id=1, source_target_pairs={{0,2},{1,5},{2,0},{3,7},{4,6},{5,1},{6,4},{7,3},{8,10},{9,13},{10,... | collective-permute-start | bytes 3145736 | tf_op jit(solution)/shard_map/ppermute | solution.py:508
  11.5 10.5 %collective-permute-start.5 = (bf16[528,256]{1,0:T(8,128)(2,1)S(1)}, bf16[528,256]{1,0:T(8,128)(2,1)S(1)}, u32[]{:S(2)}, u32[]{:S(2)}) collective-permute-start(bf16[528,256]{1,0:T(8,128)(2,1)S(1)} %get-tuple-element.59.sent), channel_id=1, source_target_pairs={{0,8},{8,16},{16,24},{1,9},{9,17},{17,25},{2,10},{10,18},{18,26},{... | collective-permute-start | bytes 811016 | tf_op jit(solution)/shard_map/ppermute | solution.py:474
  12.8 12.5 %collective-permute-start.7 = (bf16[528,256]{1,0:T(8,128)(2,1)S(1)}, bf16[528,256]{1,0:T(8,128)(2,1)S(1)}, u32[]{:S(2)}, u32[]{:S(2)}) collective-permute-start(bf16[528,256]{1,0:T(8,128)(2,1)S(1)} %get-tuple-element.59.sent), channel_id=1, source_target_pairs={{0,16},{16,0},{1,17},{17,1},{2,18},{18,2},{3,19},{19,3},{4,20},{20... | collective-permute-start | bytes 811016 | tf_op jit(solution)/shard_map/ppermute | solution.py:474
  22.1 11.1 %collective-permute-start.6 = (bf16[512,256]{1,0:T(8,128)(2,1)S(1)}, bf16[512,256]{1,0:T(8,128)(2,1)S(1)}, u32[]{:S(2)}, u32[]{:S(2)}) collective-permute-start(bf16[512,256]{1,0:T(8,128)(2,1)S(1)} %get-tuple-element.61), channel_id=1, source_target_pairs={{8,24},{24,8},{9,25},{25,9},{10,26},{26,10},{11,27},{27,11},{12,28... | collective-permute-start | bytes 786440 | tf_op jit(solution)/shard_map/ppermute | solution.py:474
  34.8 7.1 %collective-permute-start.10 = (bf16[512,1024]{1,0:T(8,128)(2,1)S(1)}, bf16[512,1024]{1,0:T(8,128)(2,1)S(1)}, u32[]{:S(2)}, u32[]{:S(2)}) collective-permute-start(bf16[512,1024]{1,0:T(8,128)(2,1)S(1)} %collective-permute-done.9.mine), channel_id=1, source_target_pairs={{0,1},{1,0},{2,3},{3,2},{4,5},{5,4},{6,7},{7,6},{8,9},{9,8},{10,11... | collective-permute-start | bytes 3145736 | tf_op jit(solution)/shard_map/ppermute | solution.py:35
  34.9 9.2 %collective-permute-start.15 = (bf16[256,512]{1,0:T(8,128)(2,1)S(1)}, bf16[256,512]{1,0:T(8,128)(2,1)S(1)}, u32[]{:S(2)}, u32[]{:S(2)}) collective-permute-start(bf16[256,512]{1,0:T(8,128)(2,1)S(1)} %get-tuple-element.72.refs_3_), channel_id=1, source_target_pairs={{0,2},{2,0},{4,6},{6,4},{1,3},{3,1},{5,7},{7,5},{8,10},{10,8},{12,... | collective-permute-start | bytes 786440 | tf_op jit(solution)/shard_map/ppermute | solution.py:35
  36.2 9.2 %collective-permute-start.14 = (bf16[256,512]{1,0:T(8,128)(2,1)S(1)}, bf16[256,512]{1,0:T(8,128)(2,1)S(1)}, u32[]{:S(2)}, u32[]{:S(2)}) collective-permute-start(bf16[256,512]{1,0:T(8,128)(2,1)S(1)} %get-tuple-element.71.refs_2_), channel_id=1, source_target_pairs={{0,4},{2,6},{4,0},{6,2},{1,5},{3,7},{5,1},{7,3},{8,12},{10,14},{12... | collective-permute-start | bytes 786440 | tf_op jit(solution)/shard_map/ppermute | solution.py:35
  38.4 11.2 %collective-permute-start.12 = (bf16[256,512]{1,0:T(8,128)(2,1)S(1)}, bf16[256,512]{1,0:T(8,128)(2,1)S(1)}, u32[]{:S(2)}, u32[]{:S(2)}) collective-permute-start(bf16[256,512]{1,0:T(8,128)(2,1)S(1)} %get-tuple-element.70.refs_1_), channel_id=1, source_target_pairs={{0,2},{2,0},{4,6},{6,4},{1,3},{3,1},{5,7},{7,5},{8,10},{10,8},{12,... | collective-permute-start | bytes 786440 | tf_op jit(solution)/shard_map/ppermute | solution.py:35
  39.0 12.0 %collective-permute-start.8 = (bf16[256,512]{1,0:T(8,128)(2,1)S(1)}, bf16[256,512]{1,0:T(8,128)(2,1)S(1)}, u32[]{:S(2)}, u32[]{:S(2)}) collective-permute-start(bf16[256,512]{1,0:T(8,128)(2,1)S(1)} %get-tuple-element.69.refs_0_), channel_id=1, source_target_pairs={{0,4},{2,6},{4,0},{6,2},{1,5},{3,7},{5,1},{7,3},{8,12},{10,14},{12... | collective-permute-start | bytes 786440 | tf_op jit(solution)/shard_map/ppermute | solution.py:35
  44.3 12.3 %collective-permute-start.17 = (bf16[256,512]{1,0:T(8,128)(2,1)S(1)}, bf16[256,512]{1,0:T(8,128)(2,1)S(1)}, u32[]{:S(2)}, u32[]{:S(2)}) collective-permute-start(bf16[256,512]{1,0:T(8,128)(2,1)S(1)} %give.7), channel_id=1, source_target_pairs={{0,4},{2,6},{4,0},{6,2},{1,5},{3,7},{5,1},{7,3},{8,12},{10,14},{12... | collective-permute-start | bytes 786440 | tf_op jit(solution)/shard_map/ppermute | solution.py:35
  45.7 10.9 %collective-permute-start.16 = (bf16[256,512]{1,0:T(8,128)(2,1)S(1)}, bf16[256,512]{1,0:T(8,128)(2,1)S(1)}, u32[]{:S(2)}, u32[]{:S(2)}) collective-permute-start(bf16[256,512]{1,0:T(8,128)(2,1)S(1)} %give.6), channel_id=1, source_target_pairs={{0,2},{2,0},{4,6},{6,4},{1,3},{3,1},{5,7},{7,5},{8,10},{10,8},{12,... | collective-permute-start | bytes 786440 | tf_op jit(solution)/shard_map/ppermute | solution.py:35
  50.0 11.5 %collective-permute-start.13 = (bf16[256,512]{1,0:T(8,128)(2,1)S(1)}, bf16[256,512]{1,0:T(8,128)(2,1)S(1)}, u32[]{:S(2)}, u32[]{:S(2)}) collective-permute-start(bf16[256,512]{1,0:T(8,128)(2,1)S(1)} %give.5), channel_id=1, source_target_pairs={{0,4},{2,6},{4,0},{6,2},{1,5},{3,7},{5,1},{7,3},{8,12},{10,14},{12... | collective-permute-start | bytes 786440 | tf_op jit(solution)/shard_map/ppermute | solution.py:35
  51.3 10.2 %collective-permute-start.11 = (bf16[256,512]{1,0:T(8,128)(2,1)S(1)}, bf16[256,512]{1,0:T(8,128)(2,1)S(1)}, u32[]{:S(2)}, u32[]{:S(2)}) collective-permute-start(bf16[256,512]{1,0:T(8,128)(2,1)S(1)} %give.4), channel_id=1, source_target_pairs={{0,2},{2,0},{4,6},{6,4},{1,3},{3,1},{5,7},{7,5},{8,10},{10,8},{12,... | collective-permute-start | bytes 786440 | tf_op jit(solution)/shard_map/ppermute | solution.py:35

commit v14 on v13

--- a/solution.py
+++ b/solution.py
@@ -144,40 +144,37 @@
         return copy
 
 
+def half_of(x, rows, half):
+    part = x.shape[1] // 2
+    return x[rows, pl.ds(pl.multiple_of(half * part, part), part)]
+
+
 def key_value_own_kernel(
     x_far, wk_far, wv_far, log_decay_far, wo_far, wq_far, wg_far,
-    x_own, x_other, acc_k, acc_v, decay, coarse, fine, wo, wq, wg, wk, wv, log_decay, arrived,
+    x, acc_k, acc_v, decay, coarse, fine, wo, wq, wg, wk, wv, log_decay, arrived,
 ):
-    rows, part = x_own.shape
     core = lax.axis_index("fsdp")
     loads = Loads(arrived)
-
-    def tile(x, half, start):
-        at = pl.ds(start, BLOCK)
-        columns = pl.ds(pl.multiple_of(half * part, part), part)
-        return loads.start(x_far.at[at, columns], x.at[at])
-
-    starts = range(0, rows, BLOCK)
+    starts = range(0, x.shape[0], TILE)
     logs, key = loads.start(log_decay_far, log_decay), loads.start(wk_far, wk)
-    tiles = [tile(x_own, core, 0)]
+    tiles = [loads.start(x_far.at[pl.ds(0, TILE)], x.at[pl.ds(0, TILE)])]
     logs.wait()
-    tiles += [tile(x_own, core, start) for start in starts[1:]]
+    tiles += [loads.start(x_far.at[pl.ds(start, TILE)], x.at[pl.ds(start, TILE)]) for start in starts[1:]]
     value = loads.start(wv_far, wv)
     angle_tables(coarse, fine)
     decay_sums(log_decay, decay)
     key.wait()
     tiles[0].wait()
-    others = [tile(x_other, 1 - core, 0)]
-    others += [loads.start(far, near) for far, near in ((wo_far, wo), (wq_far, wq), (wg_far, wg))]
+    others = [loads.start(far, near) for far, near in ((wo_far, wo), (wq_far, wq), (wg_far, wg))]
     for number, start in enumerate(starts):
-        at = slice(start, start + BLOCK)
+        at = slice(start, start + TILE)
         if number:
             tiles[number].wait()
-        acc_k[at, :] = mm(x_own[at, :], wk[...])
+        acc_k[at, :] = mm(half_of(x, at, core), wk[...])
     value.wait()
-    for start in starts:
+    for start in range(0, x.shape[0], BLOCK):
         at = slice(start, start + BLOCK)
-        acc_v[at, :] = mm(x_own[at, :], wv[...])
+        acc_v[at, :] = mm(half_of(x, at, core), wv[...])
     for copy in others:
         copy.wait()
 
@@ -229,17 +226,9 @@
 
 
 def key_value_kernel(
-    heads, x_far, x_first, wk, wv, acc_k, acc_v, decay, coarse, fine,
-    x_rest, k_out, v_out, before_out, state_out, message, arrived,
+    heads, x, wk, wv, acc_k, acc_v, decay, coarse, fine, k_out, v_out, before_out, state_out, message
 ):
-    part = wk.shape[0]
-    blocks = acc_k.shape[0] // BLOCK
-    loads = Loads(arrived)
-    columns = pl.ds(pl.multiple_of((1 - lax.axis_index("fsdp")) * part, part), part)
-    rest = [
-        loads.start(x_far.at[pl.ds(block * BLOCK, BLOCK), columns], x_rest.at[pl.ds((block - 1) * BLOCK, BLOCK)])
-        for block in range(1, blocks)
-    ]
+    blocks, other = acc_k.shape[0] // BLOCK, 1 - lax.axis_index("fsdp")
     state_out[...] = jnp.zeros_like(state_out)
     for block in range(blocks):
         start = block * BLOCK
@@ -247,13 +236,11 @@
         columns = decay[:, at].T
         ending = columns[BLOCK - 1 : BLOCK, :]
         faded = jnp.exp(ending - columns)
-        if block:
-            rest[block - 1].wait()
-        x = x_rest[start - BLOCK : start, :] if block else x_first[...]
+        rows = half_of(x, at, other)
         cosine, sine = angles(coarse, fine, start, BLOCK)
-        keys = turned(acc_k[at, :] + mm(x, wk[...]), cosine, sine)
+        keys = turned(acc_k[at, :] + mm(rows, wk[...]), cosine, sine)
         k_out[at, :] = keys
-        values = (acc_v[at, :] + mm(x, wv[...])).astype(BF16)
+        values = (acc_v[at, :] + mm(rows, wv[...])).astype(BF16)
         v_out[at, :] = values
         for head in range(heads):
             span = slice(head * DH, (head + 1) * DH)
@@ -290,7 +277,7 @@
 
 
 def query_gate_kernel(
-    heads, block, x_own, x_other, wq, wq_far, wg, wg_far, decay, coarse, fine, k, v, q_out, g_out, intra_out
+    heads, block, x, wq, wq_far, wg, wg_far, decay, coarse, fine, k, v, q_out, g_out, intra_out
 ):
     start = block * BLOCK
     lines = decay[:, start : start + BLOCK]
@@ -298,10 +285,11 @@
 
     at = slice(start, start + BLOCK)
     cosine, sine = angles(coarse, fine, start, BLOCK)
-    far = slice(max(start - BLOCK, 0), max(start - BLOCK, 0) + BLOCK)
-    queries = mm(x_own[at, :], wq[...]) + mm(x_other[far, :], wq_far[...])
+    core = lax.axis_index("fsdp")
+    own, far = half_of(x, at, core), half_of(x, at, 1 - core)
+    queries = mm(own, wq[...]) + mm(far, wq_far[...])
     q_out[...] = turned(queries, cosine, sine)
-    gates = mm(x_own[at, :], wg[...]) + mm(x_other[far, :], wg_far[...])
+    gates = mm(own, wg[...]) + mm(far, wg_far[...])
     gates = gates.astype(BF16).astype(F32)
     g_out[...] = gates / (1.0 + jnp.exp(-gates))
     for piece in range(BLOCK // TILE):
@@ -434,27 +422,23 @@
     key_far = swap(key_weight, "fsdp", 1)
     value_far = swap(value_weight, "fsdp", 1)
 
-    x_own, x_first, acc_k, acc_v, decay, coarse, fine, out_first, own_q, own_g = loading_call(
+    x, acc_k, acc_v, decay, coarse, fine, out_first, own_q, own_g = loading_call(
         key_value_own_kernel,
-        [((rows, part), BF16), ((BLOCK, part), BF16), ((rows, cols), F32), ((rows, cols), F32), ((8, rows), F32)]
+        [((rows, width), BF16), ((rows, cols), F32), ((rows, cols), F32), ((8, rows), F32)]
         + tables
         + [(out_weight.shape, BF16), ((part, cols), BF16), ((part, cols), BF16)],
         [x, key_weight, value_weight, log_decay[0].T, out_weight, query_weight, gate_weight],
         [],
         [pltpu.VMEM((part, cols), BF16)] * 2 + [pltpu.VMEM((heads, rows), F32)],
-        rows // BLOCK + 7,
+        rows // TILE + 6,
         "key_value_own",
     )
     state_shape, message_shape = (heads * DH, DH), (heads * DH + EXTRA, DH)
-    x_rest, keys, values, before, window, message = loading_call(
+    keys, values, before, window, message = kernel_call(
         functools.partial(key_value_kernel, heads),
-        [((rows - BLOCK, part), BF16)]
-        + [((rows, cols), BF16)] * 2
+        [((rows, cols), BF16)] * 2
         + [((blocks, heads * DH, DH), BF16), (state_shape, F32), (message_shape, BF16)],
-        [x],
-        [x_first, key_far, value_far, acc_k, acc_v, decay, coarse, fine],
-        [],
-        rows // BLOCK - 1,
+        [x, key_far, value_far, acc_k, acc_v, decay, coarse, fine],
         "key_value",
     )
     far_q, far_g = swap(own_q, "fsdp", 1), swap(own_g, "fsdp", 1)
@@ -463,7 +447,7 @@
         return kernel_call(
             functools.partial(query_gate_kernel, heads, block),
             [((BLOCK, cols), BF16), ((BLOCK, cols), F32), ((BLOCK, cols), F32)],
-            [x_own, x_rest if block else x_first, own_q, far_q, own_g, far_g, decay, coarse, fine, keys, values],
+            [x, own_q, far_q, own_g, far_g, decay, coarse, fine, keys, values],
             "query_gate",
         )
 

time: 62.9 us -> 62.3 us (level)
    pallas_call x2 -> x1, Pallas kernels: 8.62 us -> 4.76 us  [loading_call(): pl.pallas_call(kernel, in_specs=[pl.BlockSpec(memory_space=pltpu.HBM)] *...]
    pallas_call x13 -> x14, Pallas kernels: 12.9 us -> 16.2 us  [kernel_call(): pl.pallas_call(kernel, in_specs=[pl.BlockSpec(memory_space=pltpu.VMEM)] *...]
  transfers between devices with their start and end apart: 18 -> 18, of which waited for: 8 -> 8; matrix products, arithmetic and copies ran while one was open for 0% -> 0% of each run, Pallas kernels for 36% -> 35%
where the time goes in v14:
time: 62.3 us; the launch traced here: 61.8 us
  waiting for transfers between devices  23.4 us (38%)
  Pallas kernels  22.7 us (36%)
  starting transfers between devices  15.4 us (25%)
    pallas_call x14, Pallas kernels, kernel_call(): pl.pallas_call(kernel, in_specs=[pl.BlockSpec(memory_space=pltpu.VMEM)] *...  16.2 us
    ppermute x14, waiting for transfers between devices, swap(): lax.ppermute(value, axis, [(place, place ^ mask) for place in range(size)])  13.1 us
    ppermute x3, waiting for transfers between devices, exchange(): return lax.ppermute(message, 'ctx', pairs)  10.2 us
    ppermute x14, starting transfers between devices, swap(): lax.ppermute(value, axis, [(place, place ^ mask) for place in range(size)])  8.75 us
    ppermute x3, starting transfers between devices, exchange(): return lax.ppermute(message, 'ctx', pairs)  5.1 us
    pallas_call x1, Pallas kernels, loading_call(): pl.pallas_call(kernel, in_specs=[pl.BlockSpec(memory_space=pltpu.HBM)] *...  4.76 us
    pallas_call x2, Pallas kernels, on_device(): pl.pallas_call(functools.partial(finish_kernel, part_order), in_specs=[pl...  1.7 us
    ppermute x1, starting transfers between devices, on_device(): out_mine = lax.ppermute(for_partner, ('tp', 'fsdp'), pairs)  1.56 us
  transfers between devices with their start and end apart: 18, of which 8 were waited for; matrix products, arithmetic and copies ran while one was open for 0% of the time, Pallas kernels for 35%

profile of v14, /device:TPU:24, one launch (start us, length us, event | category | flops | bytes accessed | tf_op | source)
XLA Modules:
  0.0 61.8 jit_solution(8056806227205973651)
XLA Ops:
  0.0 0.5 collective-permute-start.2
  0.5 4.8 %key_value_own.1 = (bf16[1024,2048]{1,0:T(8,128)(2,1)S(1)}, f32[1024,512]{1,0:T(8,128)S(1)}, f32[1024,512]{1,0:T(8,128)S(1)}, f32[8,1024]{1,0:T(8,128)S(1)}, f32...) custom-call(bf16[1024,2048]{1,0:T(8,128)(2,1)} %bitcast.4, ...), custom_call_target="tpu_custom_call" | custom-call | flops 1 | bytes 1 | tf_op jit(solution)/shard_map/key_value_own/pallas_call | solution.py:56
  5.4 0.5 collective-permute-start.3
  5.9 3.2 %key_value.1 = (bf16[1024,512]{1,0:T(8,128)(2,1)S(1)}, bf16[1024,512]{1,0:T(8,128)(2,1)S(1)}, bf16[2,512,256]{2,1,0:T(8,128)(2,1)S(1)}, f32[512,256]{1,0:T(8,128)S(1)}, bf16[528,256]{1,0:T(8,128)(2,1)S(1)}) custom-call(bf16[1024,2048]{1,0:T(8,128)(2,1)S(1)} %get-tuple-element.43.x, bf16[1024,512]{1,0:T(8,128)(2,1)S(1)} %collective-permute-done.1.wk, ...), custom_call_target="tpu_custom_call" | custom-call | flops 1 | bytes 1 | tf_op jit(solution)/shard_map/key_value/pallas_call | solution.py:40
  9.3 1.6 %collective-permute-start.9 = (bf16[512,1024]{1,0:T(8,128)(2,1)S(1)}, bf16[512,1024]{1,0:T(8,128)(2,1)S(1)}, u32[]{:S(2)}, u32[]{:S(2)}) collective-permute-start(bf16[512,1024]{1,0:T(8,128)(2,1)S(1)} %columns.1), channel_id=1, source_target_pairs={{0,2},{1,5},{2,0},{3,7},{4,6},{5,1},{6,4},{7,3},{8,10},{9,13},{10,... | collective-permute-start | bytes 3145736 | tf_op jit(solution)/shard_map/ppermute | solution.py:492
  10.8 1.3 %collective-permute-start.5 = (bf16[528,256]{1,0:T(8,128)(2,1)S(1)}, bf16[528,256]{1,0:T(8,128)(2,1)S(1)}, u32[]{:S(2)}, u32[]{:S(2)}) collective-permute-start(bf16[528,256]{1,0:T(8,128)(2,1)S(1)} %get-tuple-element.56.sent), channel_id=1, source_target_pairs={{0,8},{8,16},{16,24},{1,9},{9,17},{17,25},{2,10},{10,18},{18,26},{... | collective-permute-start | bytes 811016 | tf_op jit(solution)/shard_map/ppermute | solution.py:458
  12.1 0.7 %collective-permute-start.7 = (bf16[528,256]{1,0:T(8,128)(2,1)S(1)}, bf16[528,256]{1,0:T(8,128)(2,1)S(1)}, u32[]{:S(2)}, u32[]{:S(2)}) collective-permute-start(bf16[528,256]{1,0:T(8,128)(2,1)S(1)} %get-tuple-element.56.sent), channel_id=1, source_target_pairs={{0,16},{16,0},{1,17},{17,1},{2,18},{18,2},{3,19},{19,3},{4,20},{20... | collective-permute-start | bytes 811016 | tf_op jit(solution)/shard_map/ppermute | solution.py:458
  12.8 3.1 %query_gate.2 = (bf16[512,512]{1,0:T(8,128)(2,1)S(1)}, f32[512,512]{1,0:T(8,128)S(1)}, f32[512,512]{1,0:T(8,128)S(1)}) custom-call(bf16[1024,2048]{1,0:T(8,128)(2,1)S(1)} %get-tuple-element.43.x, bf16[1024,512]{1,0:T(8,128)(2,1)S(1)} %get-tuple-element.50.wq, bf16[1024,512]{1,0:T(8,128)(2,1)S(1)} %collective-permute-done.3.wq_far, ...), custom_call_target="tpu_custom_call" | custom-call | flops 1 | bytes 1 | tf_op jit(solution)/shard_map/query_gate/pallas_call | solution.py:40
  15.9 5.4 %collective-permute-done.5.refs_0_ = bf16[528,256]{1,0:T(8,128)(2,1)S(1)} collective-permute-done((bf16[528,256]{1,0:T(8,128)(2,1)S(1)}, bf16[528,256]{1,0:T(8,128)(2,1)S(1)}, u32[]{:S(2)}, u32[]{:S(2)}) %collective-permute-start.5) | collective-permute-done | bytes 270368 | tf_op jit(solution)/shard_map/ppermute | solution.py:458
  21.5 3.1 %collective-permute-start.6 = (bf16[512,256]{1,0:T(8,128)(2,1)S(1)}, bf16[512,256]{1,0:T(8,128)(2,1)S(1)}, u32[]{:S(2)}, u32[]{:S(2)}) collective-permute-start(bf16[512,256]{1,0:T(8,128)(2,1)S(1)} %get-tuple-element.58), channel_id=1, source_target_pairs={{8,24},{24,8},{9,25},{25,9},{10,26},{26,10},{11,27},{27,11},{12,28... | collective-permute-start | bytes 786440 | tf_op jit(solution)/shard_map/ppermute | solution.py:458
  24.6 3.1 %query_gate.3 = (bf16[512,512]{1,0:T(8,128)(2,1)S(1)}, f32[512,512]{1,0:T(8,128)S(1)}, f32[512,512]{1,0:T(8,128)S(1)}) custom-call(bf16[1024,2048]{1,0:T(8,128)(2,1)S(1)} %get-tuple-element.43.x, bf16[1024,512]{1,0:T(8,128)(2,1)S(1)} %get-tuple-element.50.wq, bf16[1024,512]{1,0:T(8,128)(2,1)S(1)} %collective-permute-done.3.wq_far, ...), custom_call_target="tpu_custom_call" | custom-call | flops 1 | bytes 1 | tf_op jit(solution)/shard_map/query_gate/pallas_call | solution.py:40
  27.7 4.9 %collective-permute-done.6.refs_0_ = bf16[512,256]{1,0:T(8,128)(2,1)S(1)} collective-permute-done((bf16[512,256]{1,0:T(8,128)(2,1)S(1)}, bf16[512,256]{1,0:T(8,128)(2,1)S(1)}, u32[]{:S(2)}, u32[]{:S(2)}) %collective-permute-start.6) | collective-permute-done | bytes 262176 | tf_op jit(solution)/shard_map/ppermute | solution.py:458
  32.6 1.5 %hidden.3 = (bf16[256,512]{1,0:T(8,128)(2,1)S(1)}, bf16[256,512]{1,0:T(8,128)(2,1)S(1)}, bf16[16,128]{1,0:T(8,128)(2,1)}) custom-call(f32[8,1024]{1,0:T(8,128)S(1)} %get-tuple-element.61.decay, bf16[2,512,256]{2,1,0:T(8,128)(2,1)S(1)} %get-tuple-element.48.before, f32[520,256]{1,0:T(8,128)S(1)} %get-tuple-element.57.entering, ...), custom_call_target="tpu_custom_call" | custom-call | flops 1 | bytes 1 | tf_op jit(solution)/shard_map/hidden/pallas_call | solution.py:40
  34.2 1.4 %collective-permute-start.15 = (bf16[256,512]{1,0:T(8,128)(2,1)S(1)}, bf16[256,512]{1,0:T(8,128)(2,1)S(1)}, u32[]{:S(2)}, u32[]{:S(2)}) collective-permute-start(bf16[256,512]{1,0:T(8,128)(2,1)S(1)} %get-tuple-element.68.refs_3_), channel_id=1, source_target_pairs={{0,2},{2,0},{4,6},{6,4},{1,3},{3,1},{5,7},{7,5},{8,10},{10,8},{12,... | collective-permute-start | bytes 786440 | tf_op jit(solution)/shard_map/ppermute | solution.py:35
  35.6 0.7 %collective-permute-start.14 = (bf16[256,512]{1,0:T(8,128)(2,1)S(1)}, bf16[256,512]{1,0:T(8,128)(2,1)S(1)}, u32[]{:S(2)}, u32[]{:S(2)}) collective-permute-start(bf16[256,512]{1,0:T(8,128)(2,1)S(1)} %get-tuple-element.67.refs_2_), channel_id=1, source_target_pairs={{0,4},{2,6},{4,0},{6,2},{1,5},{3,7},{5,1},{7,3},{8,12},{10,14},{12... | collective-permute-start | bytes 786440 | tf_op jit(solution)/shard_map/ppermute | solution.py:35
  36.3 1.5 %hidden.2 = (bf16[256,512]{1,0:T(8,128)(2,1)S(1)}, bf16[256,512]{1,0:T(8,128)(2,1)S(1)}, bf16[16,128]{1,0:T(8,128)(2,1)}) custom-call(f32[8,1024]{1,0:T(8,128)S(1)} %get-tuple-element.61.decay, bf16[2,512,256]{2,1,0:T(8,128)(2,1)S(1)} %get-tuple-element.48.before, f32[520,256]{1,0:T(8,128)S(1)} %get-tuple-element.57.entering, ...), custom_call_target="tpu_custom_call" | custom-call | flops 1 | bytes 1 | tf_op jit(solution)/shard_map/hidden/pallas_call | solution.py:40
  37.8 0.6 collective-permute-start.12
  38.4 1.5 %collective-permute-start.8 = (bf16[256,512]{1,0:T(8,128)(2,1)S(1)}, bf16[256,512]{1,0:T(8,128)(2,1)S(1)}, u32[]{:S(2)}, u32[]{:S(2)}) collective-permute-start(bf16[256,512]{1,0:T(8,128)(2,1)S(1)} %get-tuple-element.65.refs_0_), channel_id=1, source_target_pairs={{0,4},{2,6},{4,0},{6,2},{1,5},{3,7},{5,1},{7,3},{8,12},{10,14},{12... | collective-permute-start | bytes 786440 | tf_op jit(solution)/shard_map/ppermute | solution.py:35
  39.9 1.3 %own_products.1 = (f32[512,1024]{1,0:T(8,128)S(1)}, f32[512,1024]{1,0:T(8,128)S(1)}) custom-call(bf16[512,1024]{1,0:T(8,128)(2,1)S(1)} %get-tuple-element.70.own_first.first, bf16[512,1024]{1,0:T(8,128)(2,1)S(1)} %collective-permute-done.own_second.second, bf16[256,512]{1,0:T(8,128)(2,1)S(1)} %get-tuple-element.65.refs_0_, ...), custom_call_target="tpu_custom_call" | custom-call | flops 1 | bytes 1 | tf_op jit(solution)/shard_map/own_products/pallas_call | solution.py:40
  41.5 1.9 %collective-permute-done.15.refs_3_.far = bf16[256,512]{1,0:T(8,128)(2,1)S(1)} collective-permute-done((bf16[256,512]{1,0:T(8,128)(2,1)S(1)}, bf16[256,512]{1,0:T(8,128)(2,1)S(1)}, u32[]{:S(2)}, u32[]{:S(2)}) %collective-permute-start.15) | collective-permute-done | bytes 262176 | tf_op jit(solution)/shard_map/ppermute | solution.py:35
  43.7 0.6 collective-permute-start.17
  44.3 0.5 collective-permute-done.14.refs_2_.far
  45.0 1.1 %collective-permute-start.16 = (bf16[256,512]{1,0:T(8,128)(2,1)S(1)}, bf16[256,512]{1,0:T(8,128)(2,1)S(1)}, u32[]{:S(2)}, u32[]{:S(2)}) collective-permute-start(bf16[256,512]{1,0:T(8,128)(2,1)S(1)} %give.6), channel_id=1, source_target_pairs={{0,2},{2,0},{4,6},{6,4},{1,3},{3,1},{5,7},{7,5},{8,10},{10,8},{12,... | collective-permute-start | bytes 786440 | tf_op jit(solution)/shard_map/ppermute | solution.py:35
  46.1 2.9 %collective-permute-done.12.far.refs_1_ = bf16[256,512]{1,0:T(8,128)(2,1)S(1)} collective-permute-done((bf16[256,512]{1,0:T(8,128)(2,1)S(1)}, bf16[256,512]{1,0:T(8,128)(2,1)S(1)}, u32[]{:S(2)}, u32[]{:S(2)}) %collective-permute-start.12) | collective-permute-done | bytes 262176 | tf_op jit(solution)/shard_map/ppermute | solution.py:35
  49.3 0.6 collective-permute-start.13
  49.9 0.5 collective-permute-done.8.far.refs_0_
  50.7 1.1 %collective-permute-start.11 = (bf16[256,512]{1,0:T(8,128)(2,1)S(1)}, bf16[256,512]{1,0:T(8,128)(2,1)S(1)}, u32[]{:S(2)}, u32[]{:S(2)}) collective-permute-start(bf16[256,512]{1,0:T(8,128)(2,1)S(1)} %give.4), channel_id=1, source_target_pairs={{0,2},{2,0},{4,6},{6,4},{1,3},{3,1},{5,7},{7,5},{8,10},{10,8},{12,... | collective-permute-start | bytes 786440 | tf_op jit(solution)/shard_map/ppermute | solution.py:35
  51.8 0.7 %keep.1 = (f32[512,512]{1,0:T(8,128)S(1)}, f32[512,512]{1,0:T(8,128)S(1)}) custom-call(bf16[256,512]{1,0:T(8,128)(2,1)S(1)} %collective-permute-done.8.far.refs_0_, bf16[256,512]{1,0:T(8,128)(2,1)S(1)} %collective-permute-done.12.far.refs_1_, bf16[256,512]{1,0:T(8,128)(2,1)S(1)} %collective-permute-done.14.refs_2_.far, ...), custom_call_target="tpu_custom_call" | custom-call | flops 1 | bytes 1 | tf_op jit(solution)/shard_map/keep/pallas_call | solution.py:40
  52.5 3.5 %collective-permute-done.17.refs_1_ = bf16[256,512]{1,0:T(8,128)(2,1)S(1)} collective-permute-done((bf16[256,512]{1,0:T(8,128)(2,1)S(1)}, bf16[256,512]{1,0:T(8,128)(2,1)S(1)}, u32[]{:S(2)}, u32[]{:S(2)}) %collective-permute-start.17) | collective-permute-done | bytes 262176 | tf_op jit(solution)/shard_map/ppermute | solution.py:35
  56.0 0.9 %finish.2.refs_4_ = bf16[1,1024,512]{2,1,0:T(8,128)(2,1)} custom-call(bf16[256,512]{1,0:T(8,128)(2,1)S(1)} %collective-permute-done.16.refs_0_, bf16[256,512]{1,0:T(8,128)(2,1)S(1)} %collective-permute-done.17.refs_1_, f32[512,512]{1,0:T(8,128)S(1)} %get-tuple-element.75.refs_2_, f32[512,512]{1,0:T(8,128)S(1)} %get-tuple-element.76.refs_3_), custom_call_target="tpu_custom_call" | custom-call | tf_op jit(solution)/shard_map/finish/pallas_call | solution.py:546
  56.8 4.0 %collective-permute-done.13.refs_1_ = bf16[256,512]{1,0:T(8,128)(2,1)S(1)} collective-permute-done((bf16[256,512]{1,0:T(8,128)(2,1)S(1)}, bf16[256,512]{1,0:T(8,128)(2,1)S(1)}, u32[]{:S(2)}, u32[]{:S(2)}) %collective-permute-start.13) | collective-permute-done | bytes 262176 | tf_op jit(solution)/shard_map/ppermute | solution.py:35
  60.8 0.9 %finish.3 = bf16[1,1024,512]{2,1,0:T(8,128)(2,1)} custom-call(bf16[256,512]{1,0:T(8,128)(2,1)S(1)} %collective-permute-done.11.refs_0_, bf16[256,512]{1,0:T(8,128)(2,1)S(1)} %collective-permute-done.13.refs_1_, f32[512,512]{1,0:T(8,128)S(1)} %get-tuple-element.75.refs_2_, f32[512,512]{1,0:T(8,128)S(1)} %get-tuple-element.76.refs_3_, ...), custom_call_target="tpu_custom_call", output_to_operand_aliasing={{}: (4, {})} | custom-call | tf_op jit(solution)/shard_map/finish/pallas_call | solution.py:546
  (21 shorter events, 2.0 us)
Async XLA Ops:
  0.0 5.9 %collective-permute-start.1 = (bf16[1024,512]{1,0:T(8,128)(2,1)}, bf16[1024,512]{1,0:T(8,128)(2,1)S(1)}, u32[]{:S(2)}, u32[]{:S(2)}) collective-permute-start(bf16[1024,512]{1,0:T(8,128)(2,1)} %wk_far.1), channel_id=1, source_target_pairs={{0,1},{1,0},{2,3},{3,2},{4,5},{5,4},{6,7},{7,6},{8,9},{9,8},{10,11... | collective-permute-start | bytes 3145736 | tf_op jit(solution)/shard_map/ppermute | solution.py:35
  0.0 5.9 %collective-permute-start.2 = (bf16[1024,512]{1,0:T(8,128)(2,1)}, bf16[1024,512]{1,0:T(8,128)(2,1)S(1)}, u32[]{:S(2)}, u32[]{:S(2)}) collective-permute-start(bf16[1024,512]{1,0:T(8,128)(2,1)} %wv_far.1), channel_id=1, source_target_pairs={{0,1},{1,0},{2,3},{3,2},{4,5},{5,4},{6,7},{7,6},{8,9},{9,8},{10,11... | collective-permute-start | bytes 3145736 | tf_op jit(solution)/shard_map/ppermute | solution.py:35
  5.3 3.9 %collective-permute-start = (bf16[512,1024]{1,0:T(8,128)(2,1)S(1)}, bf16[512,1024]{1,0:T(8,128)(2,1)S(1)}, u32[]{:S(2)}, u32[]{:S(2)}) collective-permute-start(bf16[512,1024]{1,0:T(8,128)(2,1)S(1)} %get-tuple-element.70.own_first.first), channel_id=1, source_target_pairs={{0,1},{1,0},{2,3},{3,2},{4,5},{5,4},{6,7},{7,6},{8,9},{9,8},{10,11... | collective-permute-start | bytes 3145736 | tf_op jit(solution)/shard_map/ppermute | solution.py:35
  5.4 7.4 %collective-permute-start.3 = (bf16[1024,512]{1,0:T(8,128)(2,1)S(1)}, bf16[1024,512]{1,0:T(8,128)(2,1)S(1)}, u32[]{:S(2)}, u32[]{:S(2)}) collective-permute-start(bf16[1024,512]{1,0:T(8,128)(2,1)S(1)} %get-tuple-element.50.wq), channel_id=1, source_target_pairs={{0,1},{1,0},{2,3},{3,2},{4,5},{5,4},{6,7},{7,6},{8,9},{9,8},{10,11... | collective-permute-start | bytes 3145736 | tf_op jit(solution)/shard_map/ppermute | solution.py:35
  5.9 7.0 %collective-permute-start.4 = (bf16[1024,512]{1,0:T(8,128)(2,1)S(1)}, bf16[1024,512]{1,0:T(8,128)(2,1)S(1)}, u32[]{:S(2)}, u32[]{:S(2)}) collective-permute-start(bf16[1024,512]{1,0:T(8,128)(2,1)S(1)} %get-tuple-element.51.wg), channel_id=1, source_target_pairs={{0,1},{1,0},{2,3},{3,2},{4,5},{5,4},{6,7},{7,6},{8,9},{9,8},{10,11... | collective-permute-start | bytes 3145736 | tf_op jit(solution)/shard_map/ppermute | solution.py:35
  9.3 24.9 %collective-permute-start.9 = (bf16[512,1024]{1,0:T(8,128)(2,1)S(1)}, bf16[512,1024]{1,0:T(8,128)(2,1)S(1)}, u32[]{:S(2)}, u32[]{:S(2)}) collective-permute-start(bf16[512,1024]{1,0:T(8,128)(2,1)S(1)} %columns.1), channel_id=1, source_target_pairs={{0,2},{1,5},{2,0},{3,7},{4,6},{5,1},{6,4},{7,3},{8,10},{9,13},{10,... | collective-permute-start | bytes 3145736 | tf_op jit(solution)/shard_map/ppermute | solution.py:492
  10.8 10.5 %collective-permute-start.5 = (bf16[528,256]{1,0:T(8,128)(2,1)S(1)}, bf16[528,256]{1,0:T(8,128)(2,1)S(1)}, u32[]{:S(2)}, u32[]{:S(2)}) collective-permute-start(bf16[528,256]{1,0:T(8,128)(2,1)S(1)} %get-tuple-element.56.sent), channel_id=1, source_target_pairs={{0,8},{8,16},{16,24},{1,9},{9,17},{17,25},{2,10},{10,18},{18,26},{... | collective-permute-start | bytes 811016 | tf_op jit(solution)/shard_map/ppermute | solution.py:458
  12.1 12.5 %collective-permute-start.7 = (bf16[528,256]{1,0:T(8,128)(2,1)S(1)}, bf16[528,256]{1,0:T(8,128)(2,1)S(1)}, u32[]{:S(2)}, u32[]{:S(2)}) collective-permute-start(bf16[528,256]{1,0:T(8,128)(2,1)S(1)} %get-tuple-element.56.sent), channel_id=1, source_target_pairs={{0,16},{16,0},{1,17},{17,1},{2,18},{18,2},{3,19},{19,3},{4,20},{20... | collective-permute-start | bytes 811016 | tf_op jit(solution)/shard_map/ppermute | solution.py:458
  21.5 11.1 %collective-permute-start.6 = (bf16[512,256]{1,0:T(8,128)(2,1)S(1)}, bf16[512,256]{1,0:T(8,128)(2,1)S(1)}, u32[]{:S(2)}, u32[]{:S(2)}) collective-permute-start(bf16[512,256]{1,0:T(8,128)(2,1)S(1)} %get-tuple-element.58), channel_id=1, source_target_pairs={{8,24},{24,8},{9,25},{25,9},{10,26},{26,10},{11,27},{27,11},{12,28... | collective-permute-start | bytes 786440 | tf_op jit(solution)/shard_map/ppermute | solution.py:458
  34.2 7.1 %collective-permute-start.10 = (bf16[512,1024]{1,0:T(8,128)(2,1)S(1)}, bf16[512,1024]{1,0:T(8,128)(2,1)S(1)}, u32[]{:S(2)}, u32[]{:S(2)}) collective-permute-start(bf16[512,1024]{1,0:T(8,128)(2,1)S(1)} %collective-permute-done.9.mine), channel_id=1, source_target_pairs={{0,1},{1,0},{2,3},{3,2},{4,5},{5,4},{6,7},{7,6},{8,9},{9,8},{10,11... | collective-permute-start | bytes 3145736 | tf_op jit(solution)/shard_map/ppermute | solution.py:35
  34.2 9.2 %collective-permute-start.15 = (bf16[256,512]{1,0:T(8,128)(2,1)S(1)}, bf16[256,512]{1,0:T(8,128)(2,1)S(1)}, u32[]{:S(2)}, u32[]{:S(2)}) collective-permute-start(bf16[256,512]{1,0:T(8,128)(2,1)S(1)} %get-tuple-element.68.refs_3_), channel_id=1, source_target_pairs={{0,2},{2,0},{4,6},{6,4},{1,3},{3,1},{5,7},{7,5},{8,10},{10,8},{12,... | collective-permute-start | bytes 786440 | tf_op jit(solution)/shard_map/ppermute | solution.py:35
  35.6 9.2 %collective-permute-start.14 = (bf16[256,512]{1,0:T(8,128)(2,1)S(1)}, bf16[256,512]{1,0:T(8,128)(2,1)S(1)}, u32[]{:S(2)}, u32[]{:S(2)}) collective-permute-start(bf16[256,512]{1,0:T(8,128)(2,1)S(1)} %get-tuple-element.67.refs_2_), channel_id=1, source_target_pairs={{0,4},{2,6},{4,0},{6,2},{1,5},{3,7},{5,1},{7,3},{8,12},{10,14},{12... | collective-permute-start | bytes 786440 | tf_op jit(solution)/shard_map/ppermute | solution.py:35
  37.8 11.2 %collective-permute-start.12 = (bf16[256,512]{1,0:T(8,128)(2,1)S(1)}, bf16[256,512]{1,0:T(8,128)(2,1)S(1)}, u32[]{:S(2)}, u32[]{:S(2)}) collective-permute-start(bf16[256,512]{1,0:T(8,128)(2,1)S(1)} %get-tuple-element.66.refs_1_), channel_id=1, source_target_pairs={{0,2},{2,0},{4,6},{6,4},{1,3},{3,1},{5,7},{7,5},{8,10},{10,8},{12,... | collective-permute-start | bytes 786440 | tf_op jit(solution)/shard_map/ppermute | solution.py:35
  38.4 11.9 %collective-permute-start.8 = (bf16[256,512]{1,0:T(8,128)(2,1)S(1)}, bf16[256,512]{1,0:T(8,128)(2,1)S(1)}, u32[]{:S(2)}, u32[]{:S(2)}) collective-permute-start(bf16[256,512]{1,0:T(8,128)(2,1)S(1)} %get-tuple-element.65.refs_0_), channel_id=1, source_target_pairs={{0,4},{2,6},{4,0},{6,2},{1,5},{3,7},{5,1},{7,3},{8,12},{10,14},{12... | collective-permute-start | bytes 786440 | tf_op jit(solution)/shard_map/ppermute | solution.py:35
  43.7 12.3 %collective-permute-start.17 = (bf16[256,512]{1,0:T(8,128)(2,1)S(1)}, bf16[256,512]{1,0:T(8,128)(2,1)S(1)}, u32[]{:S(2)}, u32[]{:S(2)}) collective-permute-start(bf16[256,512]{1,0:T(8,128)(2,1)S(1)} %give.7), channel_id=1, source_target_pairs={{0,4},{2,6},{4,0},{6,2},{1,5},{3,7},{5,1},{7,3},{8,12},{10,14},{12... | collective-permute-start | bytes 786440 | tf_op jit(solution)/shard_map/ppermute | solution.py:35
  45.0 10.9 %collective-permute-start.16 = (bf16[256,512]{1,0:T(8,128)(2,1)S(1)}, bf16[256,512]{1,0:T(8,128)(2,1)S(1)}, u32[]{:S(2)}, u32[]{:S(2)}) collective-permute-start(bf16[256,512]{1,0:T(8,128)(2,1)S(1)} %give.6), channel_id=1, source_target_pairs={{0,2},{2,0},{4,6},{6,4},{1,3},{3,1},{5,7},{7,5},{8,10},{10,8},{12,... | collective-permute-start | bytes 786440 | tf_op jit(solution)/shard_map/ppermute | solution.py:35
  49.3 11.5 %collective-permute-start.13 = (bf16[256,512]{1,0:T(8,128)(2,1)S(1)}, bf16[256,512]{1,0:T(8,128)(2,1)S(1)}, u32[]{:S(2)}, u32[]{:S(2)}) collective-permute-start(bf16[256,512]{1,0:T(8,128)(2,1)S(1)} %give.5), channel_id=1, source_target_pairs={{0,4},{2,6},{4,0},{6,2},{1,5},{3,7},{5,1},{7,3},{8,12},{10,14},{12... | collective-permute-start | bytes 786440 | tf_op jit(solution)/shard_map/ppermute | solution.py:35
  50.7 10.2 %collective-permute-start.11 = (bf16[256,512]{1,0:T(8,128)(2,1)S(1)}, bf16[256,512]{1,0:T(8,128)(2,1)S(1)}, u32[]{:S(2)}, u32[]{:S(2)}) collective-permute-start(bf16[256,512]{1,0:T(8,128)(2,1)S(1)} %give.4), channel_id=1, source_target_pairs={{0,2},{2,0},{4,6},{6,4},{1,3},{3,1},{5,7},{7,5},{8,10},{10,8},{12,... | collective-permute-start | bytes 786440 | tf_op jit(solution)/shard_map/ppermute | solution.py:35

commit v15 on v14

--- a/solution.py
+++ b/solution.py
@@ -158,11 +158,10 @@
     starts = range(0, x.shape[0], TILE)
     logs, key = loads.start(log_decay_far, log_decay), loads.start(wk_far, wk)
     tiles = [loads.start(x_far.at[pl.ds(0, TILE)], x.at[pl.ds(0, TILE)])]
+    angle_tables(coarse, fine)
     logs.wait()
     tiles += [loads.start(x_far.at[pl.ds(start, TILE)], x.at[pl.ds(start, TILE)]) for start in starts[1:]]
     value = loads.start(wv_far, wv)
-    angle_tables(coarse, fine)
-    decay_sums(log_decay, decay)
     key.wait()
     tiles[0].wait()
     others = [loads.start(far, near) for far, near in ((wo_far, wo), (wq_far, wq), (wg_far, wg))]
@@ -175,6 +174,7 @@
     for start in range(0, x.shape[0], BLOCK):
         at = slice(start, start + BLOCK)
         acc_v[at, :] = mm(half_of(x, at, core), wv[...])
+    decay_sums(log_decay, decay)
     for copy in others:
         copy.wait()
 
@@ -329,30 +329,31 @@
             out[:, span] = (gate[at, span] * center * lax.rsqrt(spread + 1e-5)).astype(BF16)
 
 
-def columns_kernel(first, second, out):
-    cols = out.shape[1] // 2
+def columns_kernel(first, second, *outs):
+    cols = outs[0].shape[1]
     place, core = lax.axis_index("tp"), lax.axis_index("fsdp")
     high, low = place // 2, place % 2
 
     @pl.when(core == 0)
     def _():
         at = pl.ds(pl.multiple_of((1 - low) * cols, cols), cols)
-        out[:, :cols] = first[:, at]
-        out[:, cols:] = second[:, at]
+        outs[0][...] = first[:, at]
+        outs[1][...] = second[:, at]
 
     @pl.when(core == 1)
     def _():
-        out[...] = jnp.where(high == 0, first[...], second[...])
-
-
-def arrange_kernel(mine, other, low_out, high_out):
-    cols = mine.shape[1] // 2
+        for number, out in enumerate(outs):
+            at = slice(number * cols, (number + 1) * cols)
+            out[...] = jnp.where(high == 0, first[:, at], second[:, at])
+
+
+def arrange_kernel(mine_0, mine_1, other_0, other_1, low_out, high_out):
+    cols = mine_0.shape[1]
     place, core = lax.axis_index("tp"), lax.axis_index("fsdp")
     for gathered, bit, out in ((core == 0, place // 2, low_out), (core == 1, place % 2, high_out)):
-        give = pl.ds(pl.multiple_of((1 - bit) * cols, cols), cols)
-        keep = pl.ds(pl.multiple_of(bit * cols, cols), cols)
-        out[:, :cols] = jnp.where(gathered, mine[:, give], other[:, give])
-        out[:, cols:] = jnp.where(gathered, mine[:, keep], other[:, keep])
+        blocks = [jnp.where(gathered, mine[...], other[...]) for mine, other in ((mine_0, other_0), (mine_1, other_1))]
+        out[:, :cols] = jnp.where(bit == 0, blocks[1], blocks[0])
+        out[:, cols:] = jnp.where(bit == 0, blocks[0], blocks[1])
 
 
 def own_kernel(order, own_first, own_second, *refs):
@@ -482,16 +483,16 @@
         hop *= 2
 
     own_second = swap(out_first, "fsdp", 1)
-    [for_partner] = kernel_call(
+    for_partner = kernel_call(
         columns_kernel,
-        [(out_weight.shape, BF16)],
+        [((cols, cols), BF16)] * 2,
         [after(out_first, first_message), own_second],
         "columns",
     )
     pairs = [(at * cores + at_core, (at ^ mask) * cores + at_core) for at in range(tp) for at_core, mask in enumerate((near_mask, far_mask))]
-    out_mine = lax.ppermute(for_partner, ("tp", "fsdp"), pairs)
-
-    held = after(decay, message, *early)
+    out_mine = [lax.ppermute(block, ("tp", "fsdp"), pairs) for block in for_partner]
+
+    held = after(decay, message, *early, out_mine[0])
     for block in range(1, blocks):
         projected += query_gate(block, held)
 
@@ -507,14 +508,14 @@
             "hidden",
         )
         if number == 0:
-            out_other = swap(after(out_mine, pair[0]), "fsdp", 1)
+            out_other = [swap(after(block, pair[0]), "fsdp", 1) for block in out_mine]
         for half in range(2):
             hidden[half].append(pair[half])
             far[half].append(swap(pair[half], "tp", masks[half]))
     weights = kernel_call(
         arrange_kernel,
         [((cols, 2 * cols), BF16)] * 2,
-        [out_mine, out_other],
+        [*out_mine, *out_other],
         "arrange",
     )
     order = [(half, number) for number in reversed(range(count)) for half in (1, 0)]

time: 62.3 us -> 61 us (0.979)
  waiting for transfers between devices: 23.4 us -> 19 us
  starting transfers between devices: 15.4 us -> 18.7 us
    ppermute x14 -> x15, starting transfers between devices: 8.75 us -> 12.1 us  [swap(): lax.ppermute(value, axis, [(place, place ^ mask) for place in range(size)])]
    ppermute x14 -> x15, waiting for transfers between devices: 13.1 us -> 10.1 us  [swap(): lax.ppermute(value, axis, [(place, place ^ mask) for place in range(size)])]
    ppermute x3, waiting for transfers between devices: 10.2 us -> 8.87 us  [exchange(): return lax.ppermute(message, 'ctx', pairs)]
    ppermute x3, starting transfers between devices: 5.1 us -> 4.42 us  [exchange(): return lax.ppermute(message, 'ctx', pairs)]
    ppermute x1 -> x2, starting transfers between devices: 1.56 us -> 2.16 us  [on_device(): lax.ppermute(block, ('tp', 'fsdp'), pairs)]
  transfers between devices with their start and end apart: 18 -> 20, of which waited for: 8 -> 6; matrix products, arithmetic and copies ran while one was open for 0% -> 0% of each run, Pallas kernels for 35% -> 36%
where the time goes in v15:
time: 61 us; the launch traced here: 60.8 us
  Pallas kernels  22.7 us (37%)
  waiting for transfers between devices  19 us (31%)
  starting transfers between devices  18.7 us (31%)
    pallas_call x14, Pallas kernels, kernel_call(): pl.pallas_call(kernel, in_specs=[pl.BlockSpec(memory_space=pltpu.VMEM)] *...  16.2 us
    ppermute x15, starting transfers between devices, swap(): lax.ppermute(value, axis, [(place, place ^ mask) for place in range(size)])  12.1 us
    ppermute x15, waiting for transfers between devices, swap(): lax.ppermute(value, axis, [(place, place ^ mask) for place in range(size)])  10.1 us
    ppermute x3, waiting for transfers between devices, exchange(): return lax.ppermute(message, 'ctx', pairs)  8.87 us
    pallas_call x1, Pallas kernels, loading_call(): pl.pallas_call(kernel, in_specs=[pl.BlockSpec(memory_space=pltpu.HBM)] *...  4.86 us
    ppermute x3, starting transfers between devices, exchange(): return lax.ppermute(message, 'ctx', pairs)  4.42 us
    ppermute x2, starting transfers between devices, on_device(): lax.ppermute(block, ('tp', 'fsdp'), pairs)  2.16 us
    pallas_call x2, Pallas kernels, on_device(): pl.pallas_call(functools.partial(finish_kernel, part_order), in_specs=[pl...  1.7 us
  transfers between devices with their start and end apart: 20, of which 6 were waited for; matrix products, arithmetic and copies ran while one was open for 0% of the time, Pallas kernels for 36%

profile of v15, /device:TPU:24, one launch (start us, length us, event | category | flops | bytes accessed | tf_op | source)
XLA Modules:
  0.0 60.8 jit_solution(3493974011901296211)
XLA Ops:
  0.0 0.5 collective-permute-start.2
  0.5 4.9 %key_value_own.1 = (bf16[1024,2048]{1,0:T(8,128)(2,1)S(1)}, f32[1024,512]{1,0:T(8,128)S(1)}, f32[1024,512]{1,0:T(8,128)S(1)}, f32[8,1024]{1,0:T(8,128)S(1)}, f32...) custom-call(bf16[1024,2048]{1,0:T(8,128)(2,1)} %bitcast.4, ...), custom_call_target="tpu_custom_call" | custom-call | flops 1 | bytes 1 | tf_op jit(solution)/shard_map/key_value_own/pallas_call | solution.py:56
  5.5 0.5 collective-permute-start.3
  6.0 3.2 %key_value.1 = (bf16[1024,512]{1,0:T(8,128)(2,1)S(1)}, bf16[1024,512]{1,0:T(8,128)(2,1)S(1)}, bf16[2,512,256]{2,1,0:T(8,128)(2,1)S(1)}, f32[512,256]{1,0:T(8,128)S(1)}, bf16[528,256]{1,0:T(8,128)(2,1)S(1)}) custom-call(bf16[1024,2048]{1,0:T(8,128)(2,1)S(1)} %get-tuple-element.46.x, bf16[1024,512]{1,0:T(8,128)(2,1)S(1)} %collective-permute-done.1.wk, ...), custom_call_target="tpu_custom_call" | custom-call | flops 1 | bytes 1 | tf_op jit(solution)/shard_map/key_value/pallas_call | solution.py:40
  9.3 1.3 %collective-permute-start.5 = (bf16[528,256]{1,0:T(8,128)(2,1)S(1)}, bf16[528,256]{1,0:T(8,128)(2,1)S(1)}, u32[]{:S(2)}, u32[]{:S(2)}) collective-permute-start(bf16[528,256]{1,0:T(8,128)(2,1)S(1)} %get-tuple-element.59.sent), channel_id=1, source_target_pairs={{0,8},{8,16},{16,24},{1,9},{9,17},{17,25},{2,10},{10,18},{18,26},{... | collective-permute-start | bytes 811016 | tf_op jit(solution)/shard_map/ppermute | solution.py:459
  10.7 1.6 %collective-permute-start.8 = (bf16[512,512]{1,0:T(8,128)(2,1)S(1)}, bf16[512,512]{1,0:T(8,128)(2,1)S(1)}, u32[]{:S(2)}, u32[]{:S(2)}) collective-permute-start(bf16[512,512]{1,0:T(8,128)(2,1)S(1)} %get-tuple-element.65), channel_id=1, source_target_pairs={{0,2},{1,5},{2,0},{3,7},{4,6},{5,1},{6,4},{7,3},{8,10},{9,13},{10,... | collective-permute-start | bytes 1572872 | tf_op jit(solution)/shard_map/ppermute | solution.py:493
  12.2 0.7 %collective-permute-start.7 = (bf16[528,256]{1,0:T(8,128)(2,1)S(1)}, bf16[528,256]{1,0:T(8,128)(2,1)S(1)}, u32[]{:S(2)}, u32[]{:S(2)}) collective-permute-start(bf16[528,256]{1,0:T(8,128)(2,1)S(1)} %get-tuple-element.59.sent), channel_id=1, source_target_pairs={{0,16},{16,0},{1,17},{17,1},{2,18},{18,2},{3,19},{19,3},{4,20},{20... | collective-permute-start | bytes 811016 | tf_op jit(solution)/shard_map/ppermute | solution.py:459
  12.9 0.6 collective-permute-start.10
  13.5 3.1 %query_gate.2 = (bf16[512,512]{1,0:T(8,128)(2,1)S(1)}, f32[512,512]{1,0:T(8,128)S(1)}, f32[512,512]{1,0:T(8,128)S(1)}) custom-call(bf16[1024,2048]{1,0:T(8,128)(2,1)S(1)} %get-tuple-element.46.x, bf16[1024,512]{1,0:T(8,128)(2,1)S(1)} %get-tuple-element.53.wq, bf16[1024,512]{1,0:T(8,128)(2,1)S(1)} %collective-permute-done.3.wq_far, ...), custom_call_target="tpu_custom_call" | custom-call | flops 1 | bytes 1 | tf_op jit(solution)/shard_map/query_gate/pallas_call | solution.py:40
  16.6 3.4 %collective-permute-done.5.refs_0_ = bf16[528,256]{1,0:T(8,128)(2,1)S(1)} collective-permute-done((bf16[528,256]{1,0:T(8,128)(2,1)S(1)}, bf16[528,256]{1,0:T(8,128)(2,1)S(1)}, u32[]{:S(2)}, u32[]{:S(2)}) %collective-permute-start.5) | collective-permute-done | bytes 270368 | tf_op jit(solution)/shard_map/ppermute | solution.py:459
  20.2 2.5 %collective-permute-start.6 = (bf16[512,256]{1,0:T(8,128)(2,1)S(1)}, bf16[512,256]{1,0:T(8,128)(2,1)S(1)}, u32[]{:S(2)}, u32[]{:S(2)}) collective-permute-start(bf16[512,256]{1,0:T(8,128)(2,1)S(1)} %get-tuple-element.61), channel_id=1, source_target_pairs={{8,24},{24,8},{9,25},{25,9},{10,26},{26,10},{11,27},{27,11},{12,28... | collective-permute-start | bytes 786440 | tf_op jit(solution)/shard_map/ppermute | solution.py:459
  22.7 3.1 %query_gate.3 = (bf16[512,512]{1,0:T(8,128)(2,1)S(1)}, f32[512,512]{1,0:T(8,128)S(1)}, f32[512,512]{1,0:T(8,128)S(1)}) custom-call(bf16[1024,2048]{1,0:T(8,128)(2,1)S(1)} %get-tuple-element.46.x, bf16[1024,512]{1,0:T(8,128)(2,1)S(1)} %get-tuple-element.53.wq, bf16[1024,512]{1,0:T(8,128)(2,1)S(1)} %collective-permute-done.3.wq_far, ...), custom_call_target="tpu_custom_call" | custom-call | flops 1 | bytes 1 | tf_op jit(solution)/shard_map/query_gate/pallas_call | solution.py:40
  25.8 5.5 %collective-permute-done.6.refs_0_ = bf16[512,256]{1,0:T(8,128)(2,1)S(1)} collective-permute-done((bf16[512,256]{1,0:T(8,128)(2,1)S(1)}, bf16[512,256]{1,0:T(8,128)(2,1)S(1)}, u32[]{:S(2)}, u32[]{:S(2)}) %collective-permute-start.6) | collective-permute-done | bytes 262176 | tf_op jit(solution)/shard_map/ppermute | solution.py:459
  31.3 1.5 %hidden.3 = (bf16[256,512]{1,0:T(8,128)(2,1)S(1)}, bf16[256,512]{1,0:T(8,128)(2,1)S(1)}, bf16[16,128]{1,0:T(8,128)(2,1)}) custom-call(f32[8,1024]{1,0:T(8,128)S(1)} %get-tuple-element.66.decay, bf16[2,512,256]{2,1,0:T(8,128)(2,1)S(1)} %get-tuple-element.51.before, f32[520,256]{1,0:T(8,128)S(1)} %get-tuple-element.60.entering, ...), custom_call_target="tpu_custom_call" | custom-call | flops 1 | bytes 1 | tf_op jit(solution)/shard_map/hidden/pallas_call | solution.py:40
  32.9 0.5 collective-permute-start.12
  33.4 1.5 %collective-permute-start.17 = (bf16[256,512]{1,0:T(8,128)(2,1)S(1)}, bf16[256,512]{1,0:T(8,128)(2,1)S(1)}, u32[]{:S(2)}, u32[]{:S(2)}) collective-permute-start(bf16[256,512]{1,0:T(8,128)(2,1)S(1)} %get-tuple-element.73.refs_3_), channel_id=1, source_target_pairs={{0,2},{2,0},{4,6},{6,4},{1,3},{3,1},{5,7},{7,5},{8,10},{10,8},{12,... | collective-permute-start | bytes 786440 | tf_op jit(solution)/shard_map/ppermute | solution.py:35
  34.9 1.5 %collective-permute-start.16 = (bf16[256,512]{1,0:T(8,128)(2,1)S(1)}, bf16[256,512]{1,0:T(8,128)(2,1)S(1)}, u32[]{:S(2)}, u32[]{:S(2)}) collective-permute-start(bf16[256,512]{1,0:T(8,128)(2,1)S(1)} %get-tuple-element.72.refs_2_), channel_id=1, source_target_pairs={{0,4},{2,6},{4,0},{6,2},{1,5},{3,7},{5,1},{7,3},{8,12},{10,14},{12... | collective-permute-start | bytes 786440 | tf_op jit(solution)/shard_map/ppermute | solution.py:35
  36.4 1.5 %hidden.2 = (bf16[256,512]{1,0:T(8,128)(2,1)S(1)}, bf16[256,512]{1,0:T(8,128)(2,1)S(1)}, bf16[16,128]{1,0:T(8,128)(2,1)}) custom-call(f32[8,1024]{1,0:T(8,128)S(1)} %get-tuple-element.66.decay, bf16[2,512,256]{2,1,0:T(8,128)(2,1)S(1)} %get-tuple-element.51.before, f32[520,256]{1,0:T(8,128)S(1)} %get-tuple-element.60.entering, ...), custom_call_target="tpu_custom_call" | custom-call | flops 1 | bytes 1 | tf_op jit(solution)/shard_map/hidden/pallas_call | solution.py:40
  37.9 0.6 collective-permute-start.14
  38.5 0.5 collective-permute-start.9
  39.0 1.3 %own_products.1 = (f32[512,1024]{1,0:T(8,128)S(1)}, f32[512,1024]{1,0:T(8,128)S(1)}) custom-call(bf16[512,1024]{1,0:T(8,128)(2,1)S(1)} %get-tuple-element.64.first.own_first, bf16[512,1024]{1,0:T(8,128)(2,1)S(1)} %collective-permute-done.second.own_second, bf16[256,512]{1,0:T(8,128)(2,1)S(1)} %get-tuple-element.70.refs_0_, ...), custom_call_target="tpu_custom_call" | custom-call | flops 1 | bytes 1 | tf_op jit(solution)/shard_map/own_products/pallas_call | solution.py:40
  40.6 2.0 %collective-permute-done.17.refs_3_.far = bf16[256,512]{1,0:T(8,128)(2,1)S(1)} collective-permute-done((bf16[256,512]{1,0:T(8,128)(2,1)S(1)}, bf16[256,512]{1,0:T(8,128)(2,1)S(1)}, u32[]{:S(2)}, u32[]{:S(2)}) %collective-permute-start.17) | collective-permute-done | bytes 262176 | tf_op jit(solution)/shard_map/ppermute | solution.py:35
  42.9 1.6 %collective-permute-start.19 = (bf16[256,512]{1,0:T(8,128)(2,1)S(1)}, bf16[256,512]{1,0:T(8,128)(2,1)S(1)}, u32[]{:S(2)}, u32[]{:S(2)}) collective-permute-start(bf16[256,512]{1,0:T(8,128)(2,1)S(1)} %give.7), channel_id=1, source_target_pairs={{0,4},{2,6},{4,0},{6,2},{1,5},{3,7},{5,1},{7,3},{8,12},{10,14},{12... | collective-permute-start | bytes 786440 | tf_op jit(solution)/shard_map/ppermute | solution.py:35
  44.8 1.6 %collective-permute-start.18 = (bf16[256,512]{1,0:T(8,128)(2,1)S(1)}, bf16[256,512]{1,0:T(8,128)(2,1)S(1)}, u32[]{:S(2)}, u32[]{:S(2)}) collective-permute-start(bf16[256,512]{1,0:T(8,128)(2,1)S(1)} %give.6), channel_id=1, source_target_pairs={{0,2},{2,0},{4,6},{6,4},{1,3},{3,1},{5,7},{7,5},{8,10},{10,8},{12,... | collective-permute-start | bytes 786440 | tf_op jit(solution)/shard_map/ppermute | solution.py:35
  46.3 1.9 %collective-permute-done.14.far.refs_1_ = bf16[256,512]{1,0:T(8,128)(2,1)S(1)} collective-permute-done((bf16[256,512]{1,0:T(8,128)(2,1)S(1)}, bf16[256,512]{1,0:T(8,128)(2,1)S(1)}, u32[]{:S(2)}, u32[]{:S(2)}) %collective-permute-start.14) | collective-permute-done | bytes 262176 | tf_op jit(solution)/shard_map/ppermute | solution.py:35
  48.5 1.6 %collective-permute-start.15 = (bf16[256,512]{1,0:T(8,128)(2,1)S(1)}, bf16[256,512]{1,0:T(8,128)(2,1)S(1)}, u32[]{:S(2)}, u32[]{:S(2)}) collective-permute-start(bf16[256,512]{1,0:T(8,128)(2,1)S(1)} %give.5), channel_id=1, source_target_pairs={{0,4},{2,6},{4,0},{6,2},{1,5},{3,7},{5,1},{7,3},{8,12},{10,14},{12... | collective-permute-start | bytes 786440 | tf_op jit(solution)/shard_map/ppermute | solution.py:35
  50.4 1.6 %collective-permute-start.13 = (bf16[256,512]{1,0:T(8,128)(2,1)S(1)}, bf16[256,512]{1,0:T(8,128)(2,1)S(1)}, u32[]{:S(2)}, u32[]{:S(2)}) collective-permute-start(bf16[256,512]{1,0:T(8,128)(2,1)S(1)} %give.4), channel_id=1, source_target_pairs={{0,2},{2,0},{4,6},{6,4},{1,3},{3,1},{5,7},{7,5},{8,10},{10,8},{12,... | collective-permute-start | bytes 786440 | tf_op jit(solution)/shard_map/ppermute | solution.py:35
  51.9 0.7 %keep.1 = (f32[512,512]{1,0:T(8,128)S(1)}, f32[512,512]{1,0:T(8,128)S(1)}) custom-call(bf16[256,512]{1,0:T(8,128)(2,1)S(1)} %collective-permute-done.9.far.refs_0_, bf16[256,512]{1,0:T(8,128)(2,1)S(1)} %collective-permute-done.14.far.refs_1_, bf16[256,512]{1,0:T(8,128)(2,1)S(1)} %collective-permute-done.16.refs_2_.far, ...), custom_call_target="tpu_custom_call" | custom-call | flops 1 | bytes 1 | tf_op jit(solution)/shard_map/keep/pallas_call | solution.py:40
  52.7 2.7 %collective-permute-done.19.refs_1_ = bf16[256,512]{1,0:T(8,128)(2,1)S(1)} collective-permute-done((bf16[256,512]{1,0:T(8,128)(2,1)S(1)}, bf16[256,512]{1,0:T(8,128)(2,1)S(1)}, u32[]{:S(2)}, u32[]{:S(2)}) %collective-permute-start.19) | collective-permute-done | bytes 262176 | tf_op jit(solution)/shard_map/ppermute | solution.py:35
  55.3 0.9 %finish.2.refs_4_ = bf16[1,1024,512]{2,1,0:T(8,128)(2,1)} custom-call(bf16[256,512]{1,0:T(8,128)(2,1)S(1)} %collective-permute-done.18.refs_0_, bf16[256,512]{1,0:T(8,128)(2,1)S(1)} %collective-permute-done.19.refs_1_, f32[512,512]{1,0:T(8,128)S(1)} %get-tuple-element.81.refs_2_, f32[512,512]{1,0:T(8,128)S(1)} %get-tuple-element.82.refs_3_), custom_call_target="tpu_custom_call" | custom-call | tf_op jit(solution)/shard_map/finish/pallas_call | solution.py:547
  56.2 3.6 %collective-permute-done.15.refs_1_ = bf16[256,512]{1,0:T(8,128)(2,1)S(1)} collective-permute-done((bf16[256,512]{1,0:T(8,128)(2,1)S(1)}, bf16[256,512]{1,0:T(8,128)(2,1)S(1)}, u32[]{:S(2)}, u32[]{:S(2)}) %collective-permute-start.15) | collective-permute-done | bytes 262176 | tf_op jit(solution)/shard_map/ppermute | solution.py:35
  59.8 0.9 %finish.3 = bf16[1,1024,512]{2,1,0:T(8,128)(2,1)} custom-call(bf16[256,512]{1,0:T(8,128)(2,1)S(1)} %collective-permute-done.13.refs_0_, bf16[256,512]{1,0:T(8,128)(2,1)S(1)} %collective-permute-done.15.refs_1_, f32[512,512]{1,0:T(8,128)S(1)} %get-tuple-element.81.refs_2_, f32[512,512]{1,0:T(8,128)S(1)} %get-tuple-element.82.refs_3_, ...), custom_call_target="tpu_custom_call", output_to_operand_aliasing={{}: (4, {})} | custom-call | tf_op jit(solution)/shard_map/finish/pallas_call | solution.py:547
  (25 shorter events, 2.0 us)
Async XLA Ops:
  0.0 6.0 %collective-permute-start.1 = (bf16[1024,512]{1,0:T(8,128)(2,1)}, bf16[1024,512]{1,0:T(8,128)(2,1)S(1)}, u32[]{:S(2)}, u32[]{:S(2)}) collective-permute-start(bf16[1024,512]{1,0:T(8,128)(2,1)} %wk_far.1), channel_id=1, source_target_pairs={{0,1},{1,0},{2,3},{3,2},{4,5},{5,4},{6,7},{7,6},{8,9},{9,8},{10,11... | collective-permute-start | bytes 3145736 | tf_op jit(solution)/shard_map/ppermute | solution.py:35
  0.0 6.0 %collective-permute-start.2 = (bf16[1024,512]{1,0:T(8,128)(2,1)}, bf16[1024,512]{1,0:T(8,128)(2,1)S(1)}, u32[]{:S(2)}, u32[]{:S(2)}) collective-permute-start(bf16[1024,512]{1,0:T(8,128)(2,1)} %wv_far.1), channel_id=1, source_target_pairs={{0,1},{1,0},{2,3},{3,2},{4,5},{5,4},{6,7},{7,6},{8,9},{9,8},{10,11... | collective-permute-start | bytes 3145736 | tf_op jit(solution)/shard_map/ppermute | solution.py:35
  5.4 5.2 %collective-permute-start = (bf16[512,1024]{1,0:T(8,128)(2,1)S(1)}, bf16[512,1024]{1,0:T(8,128)(2,1)S(1)}, u32[]{:S(2)}, u32[]{:S(2)}) collective-permute-start(bf16[512,1024]{1,0:T(8,128)(2,1)S(1)} %get-tuple-element.64.first.own_first), channel_id=1, source_target_pairs={{0,1},{1,0},{2,3},{3,2},{4,5},{5,4},{6,7},{7,6},{8,9},{9,8},{10,11... | collective-permute-start | bytes 3145736 | tf_op jit(solution)/shard_map/ppermute | solution.py:35
  5.5 7.4 %collective-permute-start.3 = (bf16[1024,512]{1,0:T(8,128)(2,1)S(1)}, bf16[1024,512]{1,0:T(8,128)(2,1)S(1)}, u32[]{:S(2)}, u32[]{:S(2)}) collective-permute-start(bf16[1024,512]{1,0:T(8,128)(2,1)S(1)} %get-tuple-element.53.wq), channel_id=1, source_target_pairs={{0,1},{1,0},{2,3},{3,2},{4,5},{5,4},{6,7},{7,6},{8,9},{9,8},{10,11... | collective-permute-start | bytes 3145736 | tf_op jit(solution)/shard_map/ppermute | solution.py:35
  6.0 7.6 %collective-permute-start.4 = (bf16[1024,512]{1,0:T(8,128)(2,1)S(1)}, bf16[1024,512]{1,0:T(8,128)(2,1)S(1)}, u32[]{:S(2)}, u32[]{:S(2)}) collective-permute-start(bf16[1024,512]{1,0:T(8,128)(2,1)S(1)} %get-tuple-element.54.wg), channel_id=1, source_target_pairs={{0,1},{1,0},{2,3},{3,2},{4,5},{5,4},{6,7},{7,6},{8,9},{9,8},{10,11... | collective-permute-start | bytes 3145736 | tf_op jit(solution)/shard_map/ppermute | solution.py:35
  9.3 10.7 %collective-permute-start.5 = (bf16[528,256]{1,0:T(8,128)(2,1)S(1)}, bf16[528,256]{1,0:T(8,128)(2,1)S(1)}, u32[]{:S(2)}, u32[]{:S(2)}) collective-permute-start(bf16[528,256]{1,0:T(8,128)(2,1)S(1)} %get-tuple-element.59.sent), channel_id=1, source_target_pairs={{0,8},{8,16},{16,24},{1,9},{9,17},{17,25},{2,10},{10,18},{18,26},{... | collective-permute-start | bytes 811016 | tf_op jit(solution)/shard_map/ppermute | solution.py:459
  10.7 12.0 %collective-permute-start.8 = (bf16[512,512]{1,0:T(8,128)(2,1)S(1)}, bf16[512,512]{1,0:T(8,128)(2,1)S(1)}, u32[]{:S(2)}, u32[]{:S(2)}) collective-permute-start(bf16[512,512]{1,0:T(8,128)(2,1)S(1)} %get-tuple-element.65), channel_id=1, source_target_pairs={{0,2},{1,5},{2,0},{3,7},{4,6},{5,1},{6,4},{7,3},{8,10},{9,13},{10,... | collective-permute-start | bytes 1572872 | tf_op jit(solution)/shard_map/ppermute | solution.py:493
  12.2 10.4 %collective-permute-start.7 = (bf16[528,256]{1,0:T(8,128)(2,1)S(1)}, bf16[528,256]{1,0:T(8,128)(2,1)S(1)}, u32[]{:S(2)}, u32[]{:S(2)}) collective-permute-start(bf16[528,256]{1,0:T(8,128)(2,1)S(1)} %get-tuple-element.59.sent), channel_id=1, source_target_pairs={{0,16},{16,0},{1,17},{17,1},{2,18},{18,2},{3,19},{19,3},{4,20},{20... | collective-permute-start | bytes 811016 | tf_op jit(solution)/shard_map/ppermute | solution.py:459
  12.9 20.0 %collective-permute-start.10 = (bf16[512,512]{1,0:T(8,128)(2,1)S(1)}, bf16[512,512]{1,0:T(8,128)(2,1)S(1)}, u32[]{:S(2)}, u32[]{:S(2)}) collective-permute-start(bf16[512,512]{1,0:T(8,128)(2,1)S(1)} %get-tuple-element.75), channel_id=1, source_target_pairs={{0,2},{1,5},{2,0},{3,7},{4,6},{5,1},{6,4},{7,3},{8,10},{9,13},{10,... | collective-permute-start | bytes 1572872 | tf_op jit(solution)/shard_map/ppermute | solution.py:493
  20.2 11.1 %collective-permute-start.6 = (bf16[512,256]{1,0:T(8,128)(2,1)S(1)}, bf16[512,256]{1,0:T(8,128)(2,1)S(1)}, u32[]{:S(2)}, u32[]{:S(2)}) collective-permute-start(bf16[512,256]{1,0:T(8,128)(2,1)S(1)} %get-tuple-element.61), channel_id=1, source_target_pairs={{8,24},{24,8},{9,25},{25,9},{10,26},{26,10},{11,27},{27,11},{12,28... | collective-permute-start | bytes 786440 | tf_op jit(solution)/shard_map/ppermute | solution.py:459
  32.8 5.7 %collective-permute-start.11 = (bf16[512,512]{1,0:T(8,128)(2,1)S(1)}, bf16[512,512]{1,0:T(8,128)(2,1)S(1)}, u32[]{:S(2)}, u32[]{:S(2)}) collective-permute-start(bf16[512,512]{1,0:T(8,128)(2,1)S(1)} %collective-permute-done.8.mine_0), channel_id=1, source_target_pairs={{0,1},{1,0},{2,3},{3,2},{4,5},{5,4},{6,7},{7,6},{8,9},{9,8},{10,11... | collective-permute-start | bytes 1572872 | tf_op jit(solution)/shard_map/ppermute | solution.py:35
  32.9 7.4 %collective-permute-start.12 = (bf16[512,512]{1,0:T(8,128)(2,1)S(1)}, bf16[512,512]{1,0:T(8,128)(2,1)S(1)}, u32[]{:S(2)}, u32[]{:S(2)}) collective-permute-start(bf16[512,512]{1,0:T(8,128)(2,1)S(1)} %collective-permute-done.10.mine_1), channel_id=1, source_target_pairs={{0,1},{1,0},{2,3},{3,2},{4,5},{5,4},{6,7},{7,6},{8,9},{9,8},{10,11... | collective-permute-start | bytes 1572872 | tf_op jit(solution)/shard_map/ppermute | solution.py:35
  33.4 9.2 %collective-permute-start.17 = (bf16[256,512]{1,0:T(8,128)(2,1)S(1)}, bf16[256,512]{1,0:T(8,128)(2,1)S(1)}, u32[]{:S(2)}, u32[]{:S(2)}) collective-permute-start(bf16[256,512]{1,0:T(8,128)(2,1)S(1)} %get-tuple-element.73.refs_3_), channel_id=1, source_target_pairs={{0,2},{2,0},{4,6},{6,4},{1,3},{3,1},{5,7},{7,5},{8,10},{10,8},{12,... | collective-permute-start | bytes 786440 | tf_op jit(solution)/shard_map/ppermute | solution.py:35
  34.9 9.6 %collective-permute-start.16 = (bf16[256,512]{1,0:T(8,128)(2,1)S(1)}, bf16[256,512]{1,0:T(8,128)(2,1)S(1)}, u32[]{:S(2)}, u32[]{:S(2)}) collective-permute-start(bf16[256,512]{1,0:T(8,128)(2,1)S(1)} %get-tuple-element.72.refs_2_), channel_id=1, source_target_pairs={{0,4},{2,6},{4,0},{6,2},{1,5},{3,7},{5,1},{7,3},{8,12},{10,14},{12... | collective-permute-start | bytes 786440 | tf_op jit(solution)/shard_map/ppermute | solution.py:35
  37.9 10.2 %collective-permute-start.14 = (bf16[256,512]{1,0:T(8,128)(2,1)S(1)}, bf16[256,512]{1,0:T(8,128)(2,1)S(1)}, u32[]{:S(2)}, u32[]{:S(2)}) collective-permute-start(bf16[256,512]{1,0:T(8,128)(2,1)S(1)} %get-tuple-element.71.refs_1_), channel_id=1, source_target_pairs={{0,2},{2,0},{4,6},{6,4},{1,3},{3,1},{5,7},{7,5},{8,10},{10,8},{12,... | collective-permute-start | bytes 786440 | tf_op jit(solution)/shard_map/ppermute | solution.py:35
  38.5 11.5 %collective-permute-start.9 = (bf16[256,512]{1,0:T(8,128)(2,1)S(1)}, bf16[256,512]{1,0:T(8,128)(2,1)S(1)}, u32[]{:S(2)}, u32[]{:S(2)}) collective-permute-start(bf16[256,512]{1,0:T(8,128)(2,1)S(1)} %get-tuple-element.70.refs_0_), channel_id=1, source_target_pairs={{0,4},{2,6},{4,0},{6,2},{1,5},{3,7},{5,1},{7,3},{8,12},{10,14},{12... | collective-permute-start | bytes 786440 | tf_op jit(solution)/shard_map/ppermute | solution.py:35
  42.9 12.5 %collective-permute-start.19 = (bf16[256,512]{1,0:T(8,128)(2,1)S(1)}, bf16[256,512]{1,0:T(8,128)(2,1)S(1)}, u32[]{:S(2)}, u32[]{:S(2)}) collective-permute-start(bf16[256,512]{1,0:T(8,128)(2,1)S(1)} %give.7), channel_id=1, source_target_pairs={{0,4},{2,6},{4,0},{6,2},{1,5},{3,7},{5,1},{7,3},{8,12},{10,14},{12... | collective-permute-start | bytes 786440 | tf_op jit(solution)/shard_map/ppermute | solution.py:35
  44.8 10.6 %collective-permute-start.18 = (bf16[256,512]{1,0:T(8,128)(2,1)S(1)}, bf16[256,512]{1,0:T(8,128)(2,1)S(1)}, u32[]{:S(2)}, u32[]{:S(2)}) collective-permute-start(bf16[256,512]{1,0:T(8,128)(2,1)S(1)} %give.6), channel_id=1, source_target_pairs={{0,2},{2,0},{4,6},{6,4},{1,3},{3,1},{5,7},{7,5},{8,10},{10,8},{12,... | collective-permute-start | bytes 786440 | tf_op jit(solution)/shard_map/ppermute | solution.py:35
  48.5 11.3 %collective-permute-start.15 = (bf16[256,512]{1,0:T(8,128)(2,1)S(1)}, bf16[256,512]{1,0:T(8,128)(2,1)S(1)}, u32[]{:S(2)}, u32[]{:S(2)}) collective-permute-start(bf16[256,512]{1,0:T(8,128)(2,1)S(1)} %give.5), channel_id=1, source_target_pairs={{0,4},{2,6},{4,0},{6,2},{1,5},{3,7},{5,1},{7,3},{8,12},{10,14},{12... | collective-permute-start | bytes 786440 | tf_op jit(solution)/shard_map/ppermute | solution.py:35
  50.4 9.4 %collective-permute-start.13 = (bf16[256,512]{1,0:T(8,128)(2,1)S(1)}, bf16[256,512]{1,0:T(8,128)(2,1)S(1)}, u32[]{:S(2)}, u32[]{:S(2)}) collective-permute-start(bf16[256,512]{1,0:T(8,128)(2,1)S(1)} %give.4), channel_id=1, source_target_pairs={{0,2},{2,0},{4,6},{6,4},{1,3},{3,1},{5,7},{7,5},{8,10},{10,8},{12,... | collective-permute-start | bytes 786440 | tf_op jit(solution)/shard_map/ppermute | solution.py:35

commit v16 on v15

--- a/solution.py
+++ b/solution.py
@@ -150,25 +150,24 @@
 
 
 def key_value_own_kernel(
-    x_far, wk_far, wv_far, log_decay_far, wo_far, wq_far, wg_far,
-    x, acc_k, acc_v, decay, coarse, fine, wo, wq, wg, wk, wv, log_decay, arrived,
+    x_far, wk_far, wv_far, log_decay_far, wo_far,
+    x, acc_k, acc_v, decay, coarse, fine, wo, wk, wv, log_decay, arrived,
 ):
     core = lax.axis_index("fsdp")
     loads = Loads(arrived)
     starts = range(0, x.shape[0], TILE)
     logs, key = loads.start(log_decay_far, log_decay), loads.start(wk_far, wk)
     tiles = [loads.start(x_far.at[pl.ds(0, TILE)], x.at[pl.ds(0, TILE)])]
+    tiles += [loads.start(x_far.at[pl.ds(start, TILE)], x.at[pl.ds(start, TILE)]) for start in starts[1:]]
+    value = loads.start(wv_far, wv)
+    others = [loads.start(far, near) for far, near in ((wo_far, wo),)]
     angle_tables(coarse, fine)
     logs.wait()
-    tiles += [loads.start(x_far.at[pl.ds(start, TILE)], x.at[pl.ds(start, TILE)]) for start in starts[1:]]
-    value = loads.start(wv_far, wv)
     key.wait()
-    tiles[0].wait()
-    others = [loads.start(far, near) for far, near in ((wo_far, wo), (wq_far, wq), (wg_far, wg))]
-    for number, start in enumerate(starts):
-        at = slice(start, start + TILE)
-        if number:
-            tiles[number].wait()
+    for start in range(0, x.shape[0], BLOCK):
+        at = slice(start, start + BLOCK)
+        for copy in tiles[start // TILE : (start + BLOCK) // TILE]:
+            copy.wait()
         acc_k[at, :] = mm(half_of(x, at, core), wk[...])
     value.wait()
     for start in range(0, x.shape[0], BLOCK):
@@ -226,8 +225,11 @@
 
 
 def key_value_kernel(
-    heads, x, wk, wv, acc_k, acc_v, decay, coarse, fine, k_out, v_out, before_out, state_out, message
+    heads, wq_far, wg_far, x, wk, wv, acc_k, acc_v, decay, coarse, fine,
+    wq, wg, k_out, v_out, before_out, state_out, message, arrived,
 ):
+    loads = Loads(arrived)
+    others = [loads.start(wq_far, wq), loads.start(wg_far, wg)]
     blocks, other = acc_k.shape[0] // BLOCK, 1 - lax.axis_index("fsdp")
     state_out[...] = jnp.zeros_like(state_out)
     for block in range(blocks):
@@ -250,6 +252,8 @@
             state_out[span, :] = jnp.exp(ending[:, head : head + 1]) * old + mm_tn(weighted, values[:, span])
     states = [state_out[head * DH : (head + 1) * DH, :] for head in range(heads)]
     pack_message(message, states, block_ends(decay, 0, acc_k.shape[0]))
+    for copy in others:
+        copy.wait()
 
 
 def combine_kernel(heads, hop, sets, first, last, state, sent, *refs):
@@ -423,23 +427,27 @@
     key_far = swap(key_weight, "fsdp", 1)
     value_far = swap(value_weight, "fsdp", 1)
 
-    x, acc_k, acc_v, decay, coarse, fine, out_first, own_q, own_g = loading_call(
+    x, acc_k, acc_v, decay, coarse, fine, out_first = loading_call(
         key_value_own_kernel,
         [((rows, width), BF16), ((rows, cols), F32), ((rows, cols), F32), ((8, rows), F32)]
         + tables
-        + [(out_weight.shape, BF16), ((part, cols), BF16), ((part, cols), BF16)],
-        [x, key_weight, value_weight, log_decay[0].T, out_weight, query_weight, gate_weight],
+        + [(out_weight.shape, BF16)],
+        [x, key_weight, value_weight, log_decay[0].T, out_weight],
         [],
         [pltpu.VMEM((part, cols), BF16)] * 2 + [pltpu.VMEM((heads, rows), F32)],
-        rows // TILE + 6,
+        rows // TILE + 4,
         "key_value_own",
     )
     state_shape, message_shape = (heads * DH, DH), (heads * DH + EXTRA, DH)
-    keys, values, before, window, message = kernel_call(
+    own_q, own_g, keys, values, before, window, message = loading_call(
         functools.partial(key_value_kernel, heads),
-        [((rows, cols), BF16)] * 2
+        [((part, cols), BF16)] * 2
+        + [((rows, cols), BF16)] * 2
         + [((blocks, heads * DH, DH), BF16), (state_shape, F32), (message_shape, BF16)],
+        [query_weight, gate_weight],
         [x, key_far, value_far, acc_k, acc_v, decay, coarse, fine],
+        [],
+        2,
         "key_value",
     )
     far_q, far_g = swap(own_q, "fsdp", 1), swap(own_g, "fsdp", 1)

time: 61 us -> 60.9 us (level)
    pallas_call x14 -> x13, Pallas kernels: 16.2 us -> 12.9 us  [kernel_call(): pl.pallas_call(kernel, in_specs=[pl.BlockSpec(memory_space=pltpu.VMEM)] *...]
    pallas_call x1 -> x2, Pallas kernels: 4.86 us -> 7.96 us  [loading_call(): pl.pallas_call(kernel, in_specs=[pl.BlockSpec(memory_space=pltpu.HBM)] *...]
where the time goes in v16:
time: 60.9 us; the launch traced here: 60.7 us
  Pallas kernels  22.6 us (37%)
  waiting for transfers between devices  19 us (31%)
  starting transfers between devices  18.7 us (31%)
    pallas_call x13, Pallas kernels, kernel_call(): pl.pallas_call(kernel, in_specs=[pl.BlockSpec(memory_space=pltpu.VMEM)] *...  12.9 us
    ppermute x15, starting transfers between devices, swap(): lax.ppermute(value, axis, [(place, place ^ mask) for place in range(size)])  12.2 us
    ppermute x15, waiting for transfers between devices, swap(): lax.ppermute(value, axis, [(place, place ^ mask) for place in range(size)])  10.1 us
    ppermute x3, waiting for transfers between devices, exchange(): return lax.ppermute(message, 'ctx', pairs)  8.91 us
    pallas_call x2, Pallas kernels, loading_call(): pl.pallas_call(kernel, in_specs=[pl.BlockSpec(memory_space=pltpu.HBM)] *...  7.96 us
    ppermute x3, starting transfers between devices, exchange(): return lax.ppermute(message, 'ctx', pairs)  4.4 us
    ppermute x2, starting transfers between devices, on_device(): lax.ppermute(block, ('tp', 'fsdp'), pairs)  2.16 us
    pallas_call x2, Pallas kernels, on_device(): pl.pallas_call(functools.partial(finish_kernel, part_order), in_specs=[pl...  1.7 us
  transfers between devices with their start and end apart: 20, of which 6 were waited for; matrix products, arithmetic and copies ran while one was open for 0% of the time, Pallas kernels for 36%

profile of v16, /device:TPU:24, one launch (start us, length us, event | category | flops | bytes accessed | tf_op | source)
XLA Modules:
  0.0 60.7 jit_solution(4118599919322733287)
XLA Ops:
  0.0 0.5 collective-permute-start.2
  0.5 4.7 %key_value_own.1 = (bf16[1024,2048]{1,0:T(8,128)(2,1)S(1)}, f32[1024,512]{1,0:T(8,128)S(1)}, f32[1024,512]{1,0:T(8,128)S(1)}, f32[8,1024]{1,0:T(8,128)S(1)}, f32...) custom-call(bf16[1024,2048]{1,0:T(8,128)(2,1)} %bitcast.4, ...), custom_call_target="tpu_custom_call" | custom-call | flops 1 | bytes 1 | tf_op jit(solution)/shard_map/key_value_own/pallas_call | solution.py:56
  5.3 3.3 %key_value.1 = (bf16[1024,512]{1,0:T(8,128)(2,1)S(1)}, bf16[1024,512]{1,0:T(8,128)(2,1)S(1)}, bf16[1024,512]{1,0:T(8,128)(2,1)S(1)}, bf16[1024,512]{1,0:T(8,128)...) custom-call(bf16[1024,512]{1,0:T(8,128)(2,1)} %wq_far.1, ...), custom_call_target="tpu_custom_call" | custom-call | flops 1 | bytes 1 | tf_op jit(solution)/shard_map/key_value/pallas_call | solution.py:56
  8.6 0.5 collective-permute-start.3
  9.2 1.3 %collective-permute-start.5 = (bf16[528,256]{1,0:T(8,128)(2,1)S(1)}, bf16[528,256]{1,0:T(8,128)(2,1)S(1)}, u32[]{:S(2)}, u32[]{:S(2)}) collective-permute-start(bf16[528,256]{1,0:T(8,128)(2,1)S(1)} %get-tuple-element.59.sent), channel_id=1, source_target_pairs={{0,8},{8,16},{16,24},{1,9},{9,17},{17,25},{2,10},{10,18},{18,26},{... | collective-permute-start | bytes 811016 | tf_op jit(solution)/shard_map/ppermute | solution.py:467
  10.6 1.6 %collective-permute-start.8 = (bf16[512,512]{1,0:T(8,128)(2,1)S(1)}, bf16[512,512]{1,0:T(8,128)(2,1)S(1)}, u32[]{:S(2)}, u32[]{:S(2)}) collective-permute-start(bf16[512,512]{1,0:T(8,128)(2,1)S(1)} %get-tuple-element.65), channel_id=1, source_target_pairs={{0,2},{1,5},{2,0},{3,7},{4,6},{5,1},{6,4},{7,3},{8,10},{9,13},{10,... | collective-permute-start | bytes 1572872 | tf_op jit(solution)/shard_map/ppermute | solution.py:501
  12.2 0.7 %collective-permute-start.7 = (bf16[528,256]{1,0:T(8,128)(2,1)S(1)}, bf16[528,256]{1,0:T(8,128)(2,1)S(1)}, u32[]{:S(2)}, u32[]{:S(2)}) collective-permute-start(bf16[528,256]{1,0:T(8,128)(2,1)S(1)} %get-tuple-element.59.sent), channel_id=1, source_target_pairs={{0,16},{16,0},{1,17},{17,1},{2,18},{18,2},{3,19},{19,3},{4,20},{20... | collective-permute-start | bytes 811016 | tf_op jit(solution)/shard_map/ppermute | solution.py:467
  12.9 0.6 collective-permute-start.10
  13.5 3.1 %query_gate.2 = (bf16[512,512]{1,0:T(8,128)(2,1)S(1)}, f32[512,512]{1,0:T(8,128)S(1)}, f32[512,512]{1,0:T(8,128)S(1)}) custom-call(bf16[1024,2048]{1,0:T(8,128)(2,1)S(1)} %get-tuple-element.46.x, bf16[1024,512]{1,0:T(8,128)(2,1)S(1)} %get-tuple-element.53.wq, bf16[1024,512]{1,0:T(8,128)(2,1)S(1)} %collective-permute-done.3.wq_far, ...), custom_call_target="tpu_custom_call" | custom-call | flops 1 | bytes 1 | tf_op jit(solution)/shard_map/query_gate/pallas_call | solution.py:40
  16.5 3.4 %collective-permute-done.5.refs_0_ = bf16[528,256]{1,0:T(8,128)(2,1)S(1)} collective-permute-done((bf16[528,256]{1,0:T(8,128)(2,1)S(1)}, bf16[528,256]{1,0:T(8,128)(2,1)S(1)}, u32[]{:S(2)}, u32[]{:S(2)}) %collective-permute-start.5) | collective-permute-done | bytes 270368 | tf_op jit(solution)/shard_map/ppermute | solution.py:467
  20.1 2.5 %collective-permute-start.6 = (bf16[512,256]{1,0:T(8,128)(2,1)S(1)}, bf16[512,256]{1,0:T(8,128)(2,1)S(1)}, u32[]{:S(2)}, u32[]{:S(2)}) collective-permute-start(bf16[512,256]{1,0:T(8,128)(2,1)S(1)} %get-tuple-element.61), channel_id=1, source_target_pairs={{8,24},{24,8},{9,25},{25,9},{10,26},{26,10},{11,27},{27,11},{12,28... | collective-permute-start | bytes 786440 | tf_op jit(solution)/shard_map/ppermute | solution.py:467
  22.6 3.1 %query_gate.3 = (bf16[512,512]{1,0:T(8,128)(2,1)S(1)}, f32[512,512]{1,0:T(8,128)S(1)}, f32[512,512]{1,0:T(8,128)S(1)}) custom-call(bf16[1024,2048]{1,0:T(8,128)(2,1)S(1)} %get-tuple-element.46.x, bf16[1024,512]{1,0:T(8,128)(2,1)S(1)} %get-tuple-element.53.wq, bf16[1024,512]{1,0:T(8,128)(2,1)S(1)} %collective-permute-done.3.wq_far, ...), custom_call_target="tpu_custom_call" | custom-call | flops 1 | bytes 1 | tf_op jit(solution)/shard_map/query_gate/pallas_call | solution.py:40
  25.7 5.5 %collective-permute-done.6.refs_0_ = bf16[512,256]{1,0:T(8,128)(2,1)S(1)} collective-permute-done((bf16[512,256]{1,0:T(8,128)(2,1)S(1)}, bf16[512,256]{1,0:T(8,128)(2,1)S(1)}, u32[]{:S(2)}, u32[]{:S(2)}) %collective-permute-start.6) | collective-permute-done | bytes 262176 | tf_op jit(solution)/shard_map/ppermute | solution.py:467
  31.2 1.5 %hidden.3 = (bf16[256,512]{1,0:T(8,128)(2,1)S(1)}, bf16[256,512]{1,0:T(8,128)(2,1)S(1)}, bf16[16,128]{1,0:T(8,128)(2,1)}) custom-call(f32[8,1024]{1,0:T(8,128)S(1)} %get-tuple-element.66.decay, bf16[2,512,256]{2,1,0:T(8,128)(2,1)S(1)} %get-tuple-element.51.before, f32[520,256]{1,0:T(8,128)S(1)} %get-tuple-element.60.entering, ...), custom_call_target="tpu_custom_call" | custom-call | flops 1 | bytes 1 | tf_op jit(solution)/shard_map/hidden/pallas_call | solution.py:40
  32.8 0.5 collective-permute-start.12
  33.3 1.5 %collective-permute-start.17 = (bf16[256,512]{1,0:T(8,128)(2,1)S(1)}, bf16[256,512]{1,0:T(8,128)(2,1)S(1)}, u32[]{:S(2)}, u32[]{:S(2)}) collective-permute-start(bf16[256,512]{1,0:T(8,128)(2,1)S(1)} %get-tuple-element.73.refs_3_), channel_id=1, source_target_pairs={{0,2},{2,0},{4,6},{6,4},{1,3},{3,1},{5,7},{7,5},{8,10},{10,8},{12,... | collective-permute-start | bytes 786440 | tf_op jit(solution)/shard_map/ppermute | solution.py:35
  34.8 1.5 %collective-permute-start.16 = (bf16[256,512]{1,0:T(8,128)(2,1)S(1)}, bf16[256,512]{1,0:T(8,128)(2,1)S(1)}, u32[]{:S(2)}, u32[]{:S(2)}) collective-permute-start(bf16[256,512]{1,0:T(8,128)(2,1)S(1)} %get-tuple-element.72.refs_2_), channel_id=1, source_target_pairs={{0,4},{2,6},{4,0},{6,2},{1,5},{3,7},{5,1},{7,3},{8,12},{10,14},{12... | collective-permute-start | bytes 786440 | tf_op jit(solution)/shard_map/ppermute | solution.py:35
  36.3 1.5 %hidden.2 = (bf16[256,512]{1,0:T(8,128)(2,1)S(1)}, bf16[256,512]{1,0:T(8,128)(2,1)S(1)}, bf16[16,128]{1,0:T(8,128)(2,1)}) custom-call(f32[8,1024]{1,0:T(8,128)S(1)} %get-tuple-element.66.decay, bf16[2,512,256]{2,1,0:T(8,128)(2,1)S(1)} %get-tuple-element.51.before, f32[520,256]{1,0:T(8,128)S(1)} %get-tuple-element.60.entering, ...), custom_call_target="tpu_custom_call" | custom-call | flops 1 | bytes 1 | tf_op jit(solution)/shard_map/hidden/pallas_call | solution.py:40
  37.8 0.6 collective-permute-start.14
  38.4 0.5 collective-permute-start.9
  38.9 1.3 %own_products.1 = (f32[512,1024]{1,0:T(8,128)S(1)}, f32[512,1024]{1,0:T(8,128)S(1)}) custom-call(bf16[512,1024]{1,0:T(8,128)(2,1)S(1)} %get-tuple-element.64.first.own_first, bf16[512,1024]{1,0:T(8,128)(2,1)S(1)} %collective-permute-done.second.own_second, bf16[256,512]{1,0:T(8,128)(2,1)S(1)} %get-tuple-element.70.refs_0_, ...), custom_call_target="tpu_custom_call" | custom-call | flops 1 | bytes 1 | tf_op jit(solution)/shard_map/own_products/pallas_call | solution.py:40
  40.5 2.0 %collective-permute-done.17.refs_3_.far = bf16[256,512]{1,0:T(8,128)(2,1)S(1)} collective-permute-done((bf16[256,512]{1,0:T(8,128)(2,1)S(1)}, bf16[256,512]{1,0:T(8,128)(2,1)S(1)}, u32[]{:S(2)}, u32[]{:S(2)}) %collective-permute-start.17) | collective-permute-done | bytes 262176 | tf_op jit(solution)/shard_map/ppermute | solution.py:35
  42.8 1.6 %collective-permute-start.19 = (bf16[256,512]{1,0:T(8,128)(2,1)S(1)}, bf16[256,512]{1,0:T(8,128)(2,1)S(1)}, u32[]{:S(2)}, u32[]{:S(2)}) collective-permute-start(bf16[256,512]{1,0:T(8,128)(2,1)S(1)} %give.7), channel_id=1, source_target_pairs={{0,4},{2,6},{4,0},{6,2},{1,5},{3,7},{5,1},{7,3},{8,12},{10,14},{12... | collective-permute-start | bytes 786440 | tf_op jit(solution)/shard_map/ppermute | solution.py:35
  44.7 1.6 %collective-permute-start.18 = (bf16[256,512]{1,0:T(8,128)(2,1)S(1)}, bf16[256,512]{1,0:T(8,128)(2,1)S(1)}, u32[]{:S(2)}, u32[]{:S(2)}) collective-permute-start(bf16[256,512]{1,0:T(8,128)(2,1)S(1)} %give.6), channel_id=1, source_target_pairs={{0,2},{2,0},{4,6},{6,4},{1,3},{3,1},{5,7},{7,5},{8,10},{10,8},{12,... | collective-permute-start | bytes 786440 | tf_op jit(solution)/shard_map/ppermute | solution.py:35
  46.2 1.9 %collective-permute-done.14.far.refs_1_ = bf16[256,512]{1,0:T(8,128)(2,1)S(1)} collective-permute-done((bf16[256,512]{1,0:T(8,128)(2,1)S(1)}, bf16[256,512]{1,0:T(8,128)(2,1)S(1)}, u32[]{:S(2)}, u32[]{:S(2)}) %collective-permute-start.14) | collective-permute-done | bytes 262176 | tf_op jit(solution)/shard_map/ppermute | solution.py:35
  48.4 1.6 %collective-permute-start.15 = (bf16[256,512]{1,0:T(8,128)(2,1)S(1)}, bf16[256,512]{1,0:T(8,128)(2,1)S(1)}, u32[]{:S(2)}, u32[]{:S(2)}) collective-permute-start(bf16[256,512]{1,0:T(8,128)(2,1)S(1)} %give.5), channel_id=1, source_target_pairs={{0,4},{2,6},{4,0},{6,2},{1,5},{3,7},{5,1},{7,3},{8,12},{10,14},{12... | collective-permute-start | bytes 786440 | tf_op jit(solution)/shard_map/ppermute | solution.py:35
  50.3 1.6 %collective-permute-start.13 = (bf16[256,512]{1,0:T(8,128)(2,1)S(1)}, bf16[256,512]{1,0:T(8,128)(2,1)S(1)}, u32[]{:S(2)}, u32[]{:S(2)}) collective-permute-start(bf16[256,512]{1,0:T(8,128)(2,1)S(1)} %give.4), channel_id=1, source_target_pairs={{0,2},{2,0},{4,6},{6,4},{1,3},{3,1},{5,7},{7,5},{8,10},{10,8},{12,... | collective-permute-start | bytes 786440 | tf_op jit(solution)/shard_map/ppermute | solution.py:35
  51.8 0.7 %keep.1 = (f32[512,512]{1,0:T(8,128)S(1)}, f32[512,512]{1,0:T(8,128)S(1)}) custom-call(bf16[256,512]{1,0:T(8,128)(2,1)S(1)} %collective-permute-done.9.far.refs_0_, bf16[256,512]{1,0:T(8,128)(2,1)S(1)} %collective-permute-done.14.far.refs_1_, bf16[256,512]{1,0:T(8,128)(2,1)S(1)} %collective-permute-done.16.refs_2_.far, ...), custom_call_target="tpu_custom_call" | custom-call | flops 1 | bytes 1 | tf_op jit(solution)/shard_map/keep/pallas_call | solution.py:40
  52.6 2.7 %collective-permute-done.19.refs_1_ = bf16[256,512]{1,0:T(8,128)(2,1)S(1)} collective-permute-done((bf16[256,512]{1,0:T(8,128)(2,1)S(1)}, bf16[256,512]{1,0:T(8,128)(2,1)S(1)}, u32[]{:S(2)}, u32[]{:S(2)}) %collective-permute-start.19) | collective-permute-done | bytes 262176 | tf_op jit(solution)/shard_map/ppermute | solution.py:35
  55.3 0.9 %finish.2.refs_4_ = bf16[1,1024,512]{2,1,0:T(8,128)(2,1)} custom-call(bf16[256,512]{1,0:T(8,128)(2,1)S(1)} %collective-permute-done.18.refs_0_, bf16[256,512]{1,0:T(8,128)(2,1)S(1)} %collective-permute-done.19.refs_1_, f32[512,512]{1,0:T(8,128)S(1)} %get-tuple-element.81.refs_2_, f32[512,512]{1,0:T(8,128)S(1)} %get-tuple-element.82.refs_3_), custom_call_target="tpu_custom_call" | custom-call | tf_op jit(solution)/shard_map/finish/pallas_call | solution.py:555
  56.1 3.6 %collective-permute-done.15.refs_1_ = bf16[256,512]{1,0:T(8,128)(2,1)S(1)} collective-permute-done((bf16[256,512]{1,0:T(8,128)(2,1)S(1)}, bf16[256,512]{1,0:T(8,128)(2,1)S(1)}, u32[]{:S(2)}, u32[]{:S(2)}) %collective-permute-start.15) | collective-permute-done | bytes 262176 | tf_op jit(solution)/shard_map/ppermute | solution.py:35
  59.7 0.9 %finish.3 = bf16[1,1024,512]{2,1,0:T(8,128)(2,1)} custom-call(bf16[256,512]{1,0:T(8,128)(2,1)S(1)} %collective-permute-done.13.refs_0_, bf16[256,512]{1,0:T(8,128)(2,1)S(1)} %collective-permute-done.15.refs_1_, f32[512,512]{1,0:T(8,128)S(1)} %get-tuple-element.81.refs_2_, f32[512,512]{1,0:T(8,128)S(1)} %get-tuple-element.82.refs_3_, ...), custom_call_target="tpu_custom_call", output_to_operand_aliasing={{}: (4, {})} | custom-call | tf_op jit(solution)/shard_map/finish/pallas_call | solution.py:555
  (25 shorter events, 2.0 us)
Async XLA Ops:
  0.0 5.3 %collective-permute-start.1 = (bf16[1024,512]{1,0:T(8,128)(2,1)}, bf16[1024,512]{1,0:T(8,128)(2,1)S(1)}, u32[]{:S(2)}, u32[]{:S(2)}) collective-permute-start(bf16[1024,512]{1,0:T(8,128)(2,1)} %wk_far.1), channel_id=1, source_target_pairs={{0,1},{1,0},{2,3},{3,2},{4,5},{5,4},{6,7},{7,6},{8,9},{9,8},{10,11... | collective-permute-start | bytes 3145736 | tf_op jit(solution)/shard_map/ppermute | solution.py:35
  0.0 5.3 %collective-permute-start.2 = (bf16[1024,512]{1,0:T(8,128)(2,1)}, bf16[1024,512]{1,0:T(8,128)(2,1)S(1)}, u32[]{:S(2)}, u32[]{:S(2)}) collective-permute-start(bf16[1024,512]{1,0:T(8,128)(2,1)} %wv_far.1), channel_id=1, source_target_pairs={{0,1},{1,0},{2,3},{3,2},{4,5},{5,4},{6,7},{7,6},{8,9},{9,8},{10,11... | collective-permute-start | bytes 3145736 | tf_op jit(solution)/shard_map/ppermute | solution.py:35
  5.2 5.3 %collective-permute-start = (bf16[512,1024]{1,0:T(8,128)(2,1)S(1)}, bf16[512,1024]{1,0:T(8,128)(2,1)S(1)}, u32[]{:S(2)}, u32[]{:S(2)}) collective-permute-start(bf16[512,1024]{1,0:T(8,128)(2,1)S(1)} %get-tuple-element.64.first.own_first), channel_id=1, source_target_pairs={{0,1},{1,0},{2,3},{3,2},{4,5},{5,4},{6,7},{7,6},{8,9},{9,8},{10,11... | collective-permute-start | bytes 3145736 | tf_op jit(solution)/shard_map/ppermute | solution.py:35
  8.6 4.3 %collective-permute-start.3 = (bf16[1024,512]{1,0:T(8,128)(2,1)S(1)}, bf16[1024,512]{1,0:T(8,128)(2,1)S(1)}, u32[]{:S(2)}, u32[]{:S(2)}) collective-permute-start(bf16[1024,512]{1,0:T(8,128)(2,1)S(1)} %get-tuple-element.53.wq), channel_id=1, source_target_pairs={{0,1},{1,0},{2,3},{3,2},{4,5},{5,4},{6,7},{7,6},{8,9},{9,8},{10,11... | collective-permute-start | bytes 3145736 | tf_op jit(solution)/shard_map/ppermute | solution.py:35
  9.1 4.3 %collective-permute-start.4 = (bf16[1024,512]{1,0:T(8,128)(2,1)S(1)}, bf16[1024,512]{1,0:T(8,128)(2,1)S(1)}, u32[]{:S(2)}, u32[]{:S(2)}) collective-permute-start(bf16[1024,512]{1,0:T(8,128)(2,1)S(1)} %get-tuple-element.54.wg), channel_id=1, source_target_pairs={{0,1},{1,0},{2,3},{3,2},{4,5},{5,4},{6,7},{7,6},{8,9},{9,8},{10,11... | collective-permute-start | bytes 3145736 | tf_op jit(solution)/shard_map/ppermute | solution.py:35
  9.2 10.7 %collective-permute-start.5 = (bf16[528,256]{1,0:T(8,128)(2,1)S(1)}, bf16[528,256]{1,0:T(8,128)(2,1)S(1)}, u32[]{:S(2)}, u32[]{:S(2)}) collective-permute-start(bf16[528,256]{1,0:T(8,128)(2,1)S(1)} %get-tuple-element.59.sent), channel_id=1, source_target_pairs={{0,8},{8,16},{16,24},{1,9},{9,17},{17,25},{2,10},{10,18},{18,26},{... | collective-permute-start | bytes 811016 | tf_op jit(solution)/shard_map/ppermute | solution.py:467
  10.6 12.0 %collective-permute-start.8 = (bf16[512,512]{1,0:T(8,128)(2,1)S(1)}, bf16[512,512]{1,0:T(8,128)(2,1)S(1)}, u32[]{:S(2)}, u32[]{:S(2)}) collective-permute-start(bf16[512,512]{1,0:T(8,128)(2,1)S(1)} %get-tuple-element.65), channel_id=1, source_target_pairs={{0,2},{1,5},{2,0},{3,7},{4,6},{5,1},{6,4},{7,3},{8,10},{9,13},{10,... | collective-permute-start | bytes 1572872 | tf_op jit(solution)/shard_map/ppermute | solution.py:501
  12.2 10.4 %collective-permute-start.7 = (bf16[528,256]{1,0:T(8,128)(2,1)S(1)}, bf16[528,256]{1,0:T(8,128)(2,1)S(1)}, u32[]{:S(2)}, u32[]{:S(2)}) collective-permute-start(bf16[528,256]{1,0:T(8,128)(2,1)S(1)} %get-tuple-element.59.sent), channel_id=1, source_target_pairs={{0,16},{16,0},{1,17},{17,1},{2,18},{18,2},{3,19},{19,3},{4,20},{20... | collective-permute-start | bytes 811016 | tf_op jit(solution)/shard_map/ppermute | solution.py:467
  12.9 20.0 %collective-permute-start.10 = (bf16[512,512]{1,0:T(8,128)(2,1)S(1)}, bf16[512,512]{1,0:T(8,128)(2,1)S(1)}, u32[]{:S(2)}, u32[]{:S(2)}) collective-permute-start(bf16[512,512]{1,0:T(8,128)(2,1)S(1)} %get-tuple-element.75), channel_id=1, source_target_pairs={{0,2},{1,5},{2,0},{3,7},{4,6},{5,1},{6,4},{7,3},{8,10},{9,13},{10,... | collective-permute-start | bytes 1572872 | tf_op jit(solution)/shard_map/ppermute | solution.py:501
  20.1 11.1 %collective-permute-start.6 = (bf16[512,256]{1,0:T(8,128)(2,1)S(1)}, bf16[512,256]{1,0:T(8,128)(2,1)S(1)}, u32[]{:S(2)}, u32[]{:S(2)}) collective-permute-start(bf16[512,256]{1,0:T(8,128)(2,1)S(1)} %get-tuple-element.61), channel_id=1, source_target_pairs={{8,24},{24,8},{9,25},{25,9},{10,26},{26,10},{11,27},{27,11},{12,28... | collective-permute-start | bytes 786440 | tf_op jit(solution)/shard_map/ppermute | solution.py:467
  32.7 5.7 %collective-permute-start.11 = (bf16[512,512]{1,0:T(8,128)(2,1)S(1)}, bf16[512,512]{1,0:T(8,128)(2,1)S(1)}, u32[]{:S(2)}, u32[]{:S(2)}) collective-permute-start(bf16[512,512]{1,0:T(8,128)(2,1)S(1)} %collective-permute-done.8.mine_0), channel_id=1, source_target_pairs={{0,1},{1,0},{2,3},{3,2},{4,5},{5,4},{6,7},{7,6},{8,9},{9,8},{10,11... | collective-permute-start | bytes 1572872 | tf_op jit(solution)/shard_map/ppermute | solution.py:35
  32.8 7.4 %collective-permute-start.12 = (bf16[512,512]{1,0:T(8,128)(2,1)S(1)}, bf16[512,512]{1,0:T(8,128)(2,1)S(1)}, u32[]{:S(2)}, u32[]{:S(2)}) collective-permute-start(bf16[512,512]{1,0:T(8,128)(2,1)S(1)} %collective-permute-done.10.mine_1), channel_id=1, source_target_pairs={{0,1},{1,0},{2,3},{3,2},{4,5},{5,4},{6,7},{7,6},{8,9},{9,8},{10,11... | collective-permute-start | bytes 1572872 | tf_op jit(solution)/shard_map/ppermute | solution.py:35
  33.3 9.2 %collective-permute-start.17 = (bf16[256,512]{1,0:T(8,128)(2,1)S(1)}, bf16[256,512]{1,0:T(8,128)(2,1)S(1)}, u32[]{:S(2)}, u32[]{:S(2)}) collective-permute-start(bf16[256,512]{1,0:T(8,128)(2,1)S(1)} %get-tuple-element.73.refs_3_), channel_id=1, source_target_pairs={{0,2},{2,0},{4,6},{6,4},{1,3},{3,1},{5,7},{7,5},{8,10},{10,8},{12,... | collective-permute-start | bytes 786440 | tf_op jit(solution)/shard_map/ppermute | solution.py:35
  34.8 9.6 %collective-permute-start.16 = (bf16[256,512]{1,0:T(8,128)(2,1)S(1)}, bf16[256,512]{1,0:T(8,128)(2,1)S(1)}, u32[]{:S(2)}, u32[]{:S(2)}) collective-permute-start(bf16[256,512]{1,0:T(8,128)(2,1)S(1)} %get-tuple-element.72.refs_2_), channel_id=1, source_target_pairs={{0,4},{2,6},{4,0},{6,2},{1,5},{3,7},{5,1},{7,3},{8,12},{10,14},{12... | collective-permute-start | bytes 786440 | tf_op jit(solution)/shard_map/ppermute | solution.py:35
  37.8 10.3 %collective-permute-start.14 = (bf16[256,512]{1,0:T(8,128)(2,1)S(1)}, bf16[256,512]{1,0:T(8,128)(2,1)S(1)}, u32[]{:S(2)}, u32[]{:S(2)}) collective-permute-start(bf16[256,512]{1,0:T(8,128)(2,1)S(1)} %get-tuple-element.71.refs_1_), channel_id=1, source_target_pairs={{0,2},{2,0},{4,6},{6,4},{1,3},{3,1},{5,7},{7,5},{8,10},{10,8},{12,... | collective-permute-start | bytes 786440 | tf_op jit(solution)/shard_map/ppermute | solution.py:35
  38.4 11.6 %collective-permute-start.9 = (bf16[256,512]{1,0:T(8,128)(2,1)S(1)}, bf16[256,512]{1,0:T(8,128)(2,1)S(1)}, u32[]{:S(2)}, u32[]{:S(2)}) collective-permute-start(bf16[256,512]{1,0:T(8,128)(2,1)S(1)} %get-tuple-element.70.refs_0_), channel_id=1, source_target_pairs={{0,4},{2,6},{4,0},{6,2},{1,5},{3,7},{5,1},{7,3},{8,12},{10,14},{12... | collective-permute-start | bytes 786440 | tf_op jit(solution)/shard_map/ppermute | solution.py:35
  42.8 12.5 %collective-permute-start.19 = (bf16[256,512]{1,0:T(8,128)(2,1)S(1)}, bf16[256,512]{1,0:T(8,128)(2,1)S(1)}, u32[]{:S(2)}, u32[]{:S(2)}) collective-permute-start(bf16[256,512]{1,0:T(8,128)(2,1)S(1)} %give.7), channel_id=1, source_target_pairs={{0,4},{2,6},{4,0},{6,2},{1,5},{3,7},{5,1},{7,3},{8,12},{10,14},{12... | collective-permute-start | bytes 786440 | tf_op jit(solution)/shard_map/ppermute | solution.py:35
  44.7 10.6 %collective-permute-start.18 = (bf16[256,512]{1,0:T(8,128)(2,1)S(1)}, bf16[256,512]{1,0:T(8,128)(2,1)S(1)}, u32[]{:S(2)}, u32[]{:S(2)}) collective-permute-start(bf16[256,512]{1,0:T(8,128)(2,1)S(1)} %give.6), channel_id=1, source_target_pairs={{0,2},{2,0},{4,6},{6,4},{1,3},{3,1},{5,7},{7,5},{8,10},{10,8},{12,... | collective-permute-start | bytes 786440 | tf_op jit(solution)/shard_map/ppermute | solution.py:35
  48.4 11.3 %collective-permute-start.15 = (bf16[256,512]{1,0:T(8,128)(2,1)S(1)}, bf16[256,512]{1,0:T(8,128)(2,1)S(1)}, u32[]{:S(2)}, u32[]{:S(2)}) collective-permute-start(bf16[256,512]{1,0:T(8,128)(2,1)S(1)} %give.5), channel_id=1, source_target_pairs={{0,4},{2,6},{4,0},{6,2},{1,5},{3,7},{5,1},{7,3},{8,12},{10,14},{12... | collective-permute-start | bytes 786440 | tf_op jit(solution)/shard_map/ppermute | solution.py:35
  50.3 9.4 %collective-permute-start.13 = (bf16[256,512]{1,0:T(8,128)(2,1)S(1)}, bf16[256,512]{1,0:T(8,128)(2,1)S(1)}, u32[]{:S(2)}, u32[]{:S(2)}) collective-permute-start(bf16[256,512]{1,0:T(8,128)(2,1)S(1)} %give.4), channel_id=1, source_target_pairs={{0,2},{2,0},{4,6},{6,4},{1,3},{3,1},{5,7},{7,5},{8,10},{10,8},{12,... | collective-permute-start | bytes 786440 | tf_op jit(solution)/shard_map/ppermute | solution.py:35

commit v17 on v16

--- a/solution.py
+++ b/solution.py
@@ -144,36 +144,36 @@
         return copy
 
 
-def half_of(x, rows, half):
-    part = x.shape[1] // 2
-    return x[rows, pl.ds(pl.multiple_of(half * part, part), part)]
-
-
 def key_value_own_kernel(
     x_far, wk_far, wv_far, log_decay_far, wo_far,
-    x, acc_k, acc_v, decay, coarse, fine, wo, wk, wv, log_decay, arrived,
+    x_own, x_other, acc_k, acc_v, decay, coarse, fine, wo, wk, wv, log_decay, arrived,
 ):
+    rows, part = x_own.shape
     core = lax.axis_index("fsdp")
     loads = Loads(arrived)
-    starts = range(0, x.shape[0], TILE)
-    logs, key = loads.start(log_decay_far, log_decay), loads.start(wk_far, wk)
-    tiles = [loads.start(x_far.at[pl.ds(0, TILE)], x.at[pl.ds(0, TILE)])]
-    tiles += [loads.start(x_far.at[pl.ds(start, TILE)], x.at[pl.ds(start, TILE)]) for start in starts[1:]]
+
+    def tile(x, half, start):
+        at = pl.ds(start, BLOCK)
+        columns = pl.ds(pl.multiple_of(half * part, part), part)
+        return loads.start(x_far.at[at, columns], x.at[at])
+
+    starts = range(0, rows, BLOCK)
+    key, logs = loads.start(wk_far, wk), loads.start(log_decay_far, log_decay)
+    tiles = [tile(x_own, core, start) for start in starts]
     value = loads.start(wv_far, wv)
-    others = [loads.start(far, near) for far, near in ((wo_far, wo),)]
+    others = [tile(x_other, 1 - core, start) for start in starts] + [loads.start(wo_far, wo)]
     angle_tables(coarse, fine)
     logs.wait()
+    decay_sums(log_decay, decay)
     key.wait()
-    for start in range(0, x.shape[0], BLOCK):
+    for copy, start in zip(tiles, starts):
         at = slice(start, start + BLOCK)
-        for copy in tiles[start // TILE : (start + BLOCK) // TILE]:
-            copy.wait()
-        acc_k[at, :] = mm(half_of(x, at, core), wk[...])
+        copy.wait()
+        acc_k[at, :] = mm(x_own[at, :], wk[...])
     value.wait()
-    for start in range(0, x.shape[0], BLOCK):
+    for start in starts:
         at = slice(start, start + BLOCK)
-        acc_v[at, :] = mm(half_of(x, at, core), wv[...])
-    decay_sums(log_decay, decay)
+        acc_v[at, :] = mm(x_own[at, :], wv[...])
     for copy in others:
         copy.wait()
 
@@ -230,7 +230,7 @@
 ):
     loads = Loads(arrived)
     others = [loads.start(wq_far, wq), loads.start(wg_far, wg)]
-    blocks, other = acc_k.shape[0] // BLOCK, 1 - lax.axis_index("fsdp")
+    blocks = acc_k.shape[0] // BLOCK
     state_out[...] = jnp.zeros_like(state_out)
     for block in range(blocks):
         start = block * BLOCK
@@ -238,7 +238,7 @@
         columns = decay[:, at].T
         ending = columns[BLOCK - 1 : BLOCK, :]
         faded = jnp.exp(ending - columns)
-        rows = half_of(x, at, other)
+        rows = x[at, :]
         cosine, sine = angles(coarse, fine, start, BLOCK)
         keys = turned(acc_k[at, :] + mm(rows, wk[...]), cosine, sine)
         k_out[at, :] = keys
@@ -281,7 +281,7 @@
 
 
 def query_gate_kernel(
-    heads, block, x, wq, wq_far, wg, wg_far, decay, coarse, fine, k, v, q_out, g_out, intra_out
+    heads, block, x_own, x_other, wq, wq_far, wg, wg_far, decay, coarse, fine, k, v, q_out, g_out, intra_out
 ):
     start = block * BLOCK
     lines = decay[:, start : start + BLOCK]
@@ -289,8 +289,7 @@
 
     at = slice(start, start + BLOCK)
     cosine, sine = angles(coarse, fine, start, BLOCK)
-    core = lax.axis_index("fsdp")
-    own, far = half_of(x, at, core), half_of(x, at, 1 - core)
+    own, far = x_own[at, :], x_other[at, :]
     queries = mm(own, wq[...]) + mm(far, wq_far[...])
     q_out[...] = turned(queries, cosine, sine)
     gates = mm(own, wg[...]) + mm(far, wg_far[...])
@@ -427,15 +426,15 @@
     key_far = swap(key_weight, "fsdp", 1)
     value_far = swap(value_weight, "fsdp", 1)
 
-    x, acc_k, acc_v, decay, coarse, fine, out_first = loading_call(
+    x_own, x_other, acc_k, acc_v, decay, coarse, fine, out_first = loading_call(
         key_value_own_kernel,
-        [((rows, width), BF16), ((rows, cols), F32), ((rows, cols), F32), ((8, rows), F32)]
+        [((rows, part), BF16)] * 2 + [((rows, cols), F32)] * 2 + [((8, rows), F32)]
         + tables
         + [(out_weight.shape, BF16)],
         [x, key_weight, value_weight, log_decay[0].T, out_weight],
         [],
         [pltpu.VMEM((part, cols), BF16)] * 2 + [pltpu.VMEM((heads, rows), F32)],
-        rows // TILE + 4,
+        2 * (rows // BLOCK) + 4,
         "key_value_own",
     )
     state_shape, message_shape = (heads * DH, DH), (heads * DH + EXTRA, DH)
@@ -445,7 +444,7 @@
         + [((rows, cols), BF16)] * 2
         + [((blocks, heads * DH, DH), BF16), (state_shape, F32), (message_shape, BF16)],
         [query_weight, gate_weight],
-        [x, key_far, value_far, acc_k, acc_v, decay, coarse, fine],
+        [x_other, key_far, value_far, acc_k, acc_v, decay, coarse, fine],
         [],
         2,
         "key_value",
@@ -456,7 +455,7 @@
         return kernel_call(
             functools.partial(query_gate_kernel, heads, block),
             [((BLOCK, cols), BF16), ((BLOCK, cols), F32), ((BLOCK, cols), F32)],
-            [x, own_q, far_q, own_g, far_g, decay, coarse, fine, keys, values],
+            [x_own, x_other, own_q, far_q, own_g, far_g, decay, coarse, fine, keys, values],
             "query_gate",
         )
 

time: 60.9 us -> 60.4 us (level)
  transfers between devices with their start and end apart: 20 -> 20, of which waited for: 6 -> 6; matrix products, arithmetic and copies ran while one was open for 0% -> 0% of each run, Pallas kernels for 36% -> 35%
where the time goes in v17:
time: 60.4 us; the launch traced here: 60.2 us
  Pallas kernels  22.1 us (37%)
  waiting for transfers between devices  19 us (31%)
  starting transfers between devices  18.7 us (31%)
    pallas_call x13, Pallas kernels, kernel_call(): pl.pallas_call(kernel, in_specs=[pl.BlockSpec(memory_space=pltpu.VMEM)] *...  12.9 us
    ppermute x15, starting transfers between devices, swap(): lax.ppermute(value, axis, [(place, place ^ mask) for place in range(size)])  12.2 us
    ppermute x15, waiting for transfers between devices, swap(): lax.ppermute(value, axis, [(place, place ^ mask) for place in range(size)])  10.1 us
    ppermute x3, waiting for transfers between devices, exchange(): return lax.ppermute(message, 'ctx', pairs)  8.91 us
    pallas_call x2, Pallas kernels, loading_call(): pl.pallas_call(kernel, in_specs=[pl.BlockSpec(memory_space=pltpu.HBM)] *...  7.48 us
    ppermute x3, starting transfers between devices, exchange(): return lax.ppermute(message, 'ctx', pairs)  4.4 us
    ppermute x2, starting transfers between devices, on_device(): lax.ppermute(block, ('tp', 'fsdp'), pairs)  2.16 us
    pallas_call x2, Pallas kernels, on_device(): pl.pallas_call(functools.partial(finish_kernel, part_order), in_specs=[pl...  1.7 us
  transfers between devices with their start and end apart: 20, of which 6 were waited for; matrix products, arithmetic and copies ran while one was open for 0% of the time, Pallas kernels for 35%

profile of v17, /device:TPU:24, one launch (start us, length us, event | category | flops | bytes accessed | tf_op | source)
XLA Modules:
  0.0 60.2 jit_solution(17783045384522888431)
XLA Ops:
  0.0 0.5 collective-permute-start.2
  0.5 4.3 %key_value_own.1 = (bf16[1024,1024]{1,0:T(8,128)(2,1)S(1)}, bf16[1024,1024]{1,0:T(8,128)(2,1)S(1)}, f32[1024,512]{1,0:T(8,128)S(1)}, f32[1024,512]{1,0:T(8,128)S...) custom-call(bf16[1024,2048]{1,0:T(8,128)(2,1)} %bitcast.4, ...), custom_call_target="tpu_custom_call" | custom-call | flops 1 | bytes 1 | tf_op jit(solution)/shard_map/key_value_own/pallas_call | solution.py:56
  4.9 3.2 %key_value.1 = (bf16[1024,512]{1,0:T(8,128)(2,1)S(1)}, bf16[1024,512]{1,0:T(8,128)(2,1)S(1)}, bf16[1024,512]{1,0:T(8,128)(2,1)S(1)}, bf16[1024,512]{1,0:T(8,128)...) custom-call(bf16[1024,512]{1,0:T(8,128)(2,1)} %wq_far.1, ...), custom_call_target="tpu_custom_call" | custom-call | flops 1 | bytes 1 | tf_op jit(solution)/shard_map/key_value/pallas_call | solution.py:56
  8.1 0.5 collective-permute-start.3
  8.7 1.3 %collective-permute-start.5 = (bf16[528,256]{1,0:T(8,128)(2,1)S(1)}, bf16[528,256]{1,0:T(8,128)(2,1)S(1)}, u32[]{:S(2)}, u32[]{:S(2)}) collective-permute-start(bf16[528,256]{1,0:T(8,128)(2,1)S(1)} %get-tuple-element.61.sent), channel_id=1, source_target_pairs={{0,8},{8,16},{16,24},{1,9},{9,17},{17,25},{2,10},{10,18},{18,26},{... | collective-permute-start | bytes 811016 | tf_op jit(solution)/shard_map/ppermute | solution.py:466
  10.1 1.6 %collective-permute-start.8 = (bf16[512,512]{1,0:T(8,128)(2,1)S(1)}, bf16[512,512]{1,0:T(8,128)(2,1)S(1)}, u32[]{:S(2)}, u32[]{:S(2)}) collective-permute-start(bf16[512,512]{1,0:T(8,128)(2,1)S(1)} %get-tuple-element.67), channel_id=1, source_target_pairs={{0,2},{1,5},{2,0},{3,7},{4,6},{5,1},{6,4},{7,3},{8,10},{9,13},{10,... | collective-permute-start | bytes 1572872 | tf_op jit(solution)/shard_map/ppermute | solution.py:500
  11.7 0.7 %collective-permute-start.7 = (bf16[528,256]{1,0:T(8,128)(2,1)S(1)}, bf16[528,256]{1,0:T(8,128)(2,1)S(1)}, u32[]{:S(2)}, u32[]{:S(2)}) collective-permute-start(bf16[528,256]{1,0:T(8,128)(2,1)S(1)} %get-tuple-element.61.sent), channel_id=1, source_target_pairs={{0,16},{16,0},{1,17},{17,1},{2,18},{18,2},{3,19},{19,3},{4,20},{20... | collective-permute-start | bytes 811016 | tf_op jit(solution)/shard_map/ppermute | solution.py:466
  12.4 0.6 collective-permute-start.10
  13.0 3.1 %query_gate.2 = (bf16[512,512]{1,0:T(8,128)(2,1)S(1)}, f32[512,512]{1,0:T(8,128)S(1)}, f32[512,512]{1,0:T(8,128)S(1)}) custom-call(bf16[1024,1024]{1,0:T(8,128)(2,1)S(1)} %get-tuple-element.54.x_own, bf16[1024,1024]{1,0:T(8,128)(2,1)S(1)} %get-tuple-element.47.x.x_other, bf16[1024,512]{1,0:T(8,128)(2,1)S(1)} %get-tuple-element.55.wq, ...), custom_call_target="tpu_custom_call" | custom-call | flops 1 | bytes 1 | tf_op jit(solution)/shard_map/query_gate/pallas_call | solution.py:40
  16.1 3.4 %collective-permute-done.5.refs_0_ = bf16[528,256]{1,0:T(8,128)(2,1)S(1)} collective-permute-done((bf16[528,256]{1,0:T(8,128)(2,1)S(1)}, bf16[528,256]{1,0:T(8,128)(2,1)S(1)}, u32[]{:S(2)}, u32[]{:S(2)}) %collective-permute-start.5) | collective-permute-done | bytes 270368 | tf_op jit(solution)/shard_map/ppermute | solution.py:466
  19.6 2.5 %collective-permute-start.6 = (bf16[512,256]{1,0:T(8,128)(2,1)S(1)}, bf16[512,256]{1,0:T(8,128)(2,1)S(1)}, u32[]{:S(2)}, u32[]{:S(2)}) collective-permute-start(bf16[512,256]{1,0:T(8,128)(2,1)S(1)} %get-tuple-element.63), channel_id=1, source_target_pairs={{8,24},{24,8},{9,25},{25,9},{10,26},{26,10},{11,27},{27,11},{12,28... | collective-permute-start | bytes 786440 | tf_op jit(solution)/shard_map/ppermute | solution.py:466
  22.1 3.1 %query_gate.3 = (bf16[512,512]{1,0:T(8,128)(2,1)S(1)}, f32[512,512]{1,0:T(8,128)S(1)}, f32[512,512]{1,0:T(8,128)S(1)}) custom-call(bf16[1024,1024]{1,0:T(8,128)(2,1)S(1)} %get-tuple-element.54.x_own, bf16[1024,1024]{1,0:T(8,128)(2,1)S(1)} %get-tuple-element.47.x.x_other, bf16[1024,512]{1,0:T(8,128)(2,1)S(1)} %get-tuple-element.55.wq, ...), custom_call_target="tpu_custom_call" | custom-call | flops 1 | bytes 1 | tf_op jit(solution)/shard_map/query_gate/pallas_call | solution.py:40
  25.2 5.5 %collective-permute-done.6.refs_0_ = bf16[512,256]{1,0:T(8,128)(2,1)S(1)} collective-permute-done((bf16[512,256]{1,0:T(8,128)(2,1)S(1)}, bf16[512,256]{1,0:T(8,128)(2,1)S(1)}, u32[]{:S(2)}, u32[]{:S(2)}) %collective-permute-start.6) | collective-permute-done | bytes 262176 | tf_op jit(solution)/shard_map/ppermute | solution.py:466
  30.7 1.5 %hidden.3 = (bf16[256,512]{1,0:T(8,128)(2,1)S(1)}, bf16[256,512]{1,0:T(8,128)(2,1)S(1)}, bf16[16,128]{1,0:T(8,128)(2,1)}) custom-call(f32[8,1024]{1,0:T(8,128)S(1)} %get-tuple-element.68.decay, bf16[2,512,256]{2,1,0:T(8,128)(2,1)S(1)} %get-tuple-element.52.before, f32[520,256]{1,0:T(8,128)S(1)} %get-tuple-element.62.entering, ...), custom_call_target="tpu_custom_call" | custom-call | flops 1 | bytes 1 | tf_op jit(solution)/shard_map/hidden/pallas_call | solution.py:40
  32.3 0.5 collective-permute-start.12
  32.8 1.5 %collective-permute-start.17 = (bf16[256,512]{1,0:T(8,128)(2,1)S(1)}, bf16[256,512]{1,0:T(8,128)(2,1)S(1)}, u32[]{:S(2)}, u32[]{:S(2)}) collective-permute-start(bf16[256,512]{1,0:T(8,128)(2,1)S(1)} %get-tuple-element.75.refs_3_), channel_id=1, source_target_pairs={{0,2},{2,0},{4,6},{6,4},{1,3},{3,1},{5,7},{7,5},{8,10},{10,8},{12,... | collective-permute-start | bytes 786440 | tf_op jit(solution)/shard_map/ppermute | solution.py:35
  34.3 1.5 %collective-permute-start.16 = (bf16[256,512]{1,0:T(8,128)(2,1)S(1)}, bf16[256,512]{1,0:T(8,128)(2,1)S(1)}, u32[]{:S(2)}, u32[]{:S(2)}) collective-permute-start(bf16[256,512]{1,0:T(8,128)(2,1)S(1)} %get-tuple-element.74.refs_2_), channel_id=1, source_target_pairs={{0,4},{2,6},{4,0},{6,2},{1,5},{3,7},{5,1},{7,3},{8,12},{10,14},{12... | collective-permute-start | bytes 786440 | tf_op jit(solution)/shard_map/ppermute | solution.py:35
  35.9 1.5 %hidden.2 = (bf16[256,512]{1,0:T(8,128)(2,1)S(1)}, bf16[256,512]{1,0:T(8,128)(2,1)S(1)}, bf16[16,128]{1,0:T(8,128)(2,1)}) custom-call(f32[8,1024]{1,0:T(8,128)S(1)} %get-tuple-element.68.decay, bf16[2,512,256]{2,1,0:T(8,128)(2,1)S(1)} %get-tuple-element.52.before, f32[520,256]{1,0:T(8,128)S(1)} %get-tuple-element.62.entering, ...), custom_call_target="tpu_custom_call" | custom-call | flops 1 | bytes 1 | tf_op jit(solution)/shard_map/hidden/pallas_call | solution.py:40
  37.4 0.6 collective-permute-start.14
  38.0 0.5 collective-permute-start.9
  38.5 1.3 %own_products.1 = (f32[512,1024]{1,0:T(8,128)S(1)}, f32[512,1024]{1,0:T(8,128)S(1)}) custom-call(bf16[512,1024]{1,0:T(8,128)(2,1)S(1)} %get-tuple-element.66.first.own_first, bf16[512,1024]{1,0:T(8,128)(2,1)S(1)} %collective-permute-done.second.own_second, bf16[256,512]{1,0:T(8,128)(2,1)S(1)} %get-tuple-element.72.refs_0_, ...), custom_call_target="tpu_custom_call" | custom-call | flops 1 | bytes 1 | tf_op jit(solution)/shard_map/own_products/pallas_call | solution.py:40
  40.0 2.0 %collective-permute-done.17.refs_3_.far = bf16[256,512]{1,0:T(8,128)(2,1)S(1)} collective-permute-done((bf16[256,512]{1,0:T(8,128)(2,1)S(1)}, bf16[256,512]{1,0:T(8,128)(2,1)S(1)}, u32[]{:S(2)}, u32[]{:S(2)}) %collective-permute-start.17) | collective-permute-done | bytes 262176 | tf_op jit(solution)/shard_map/ppermute | solution.py:35
  42.3 1.6 %collective-permute-start.19 = (bf16[256,512]{1,0:T(8,128)(2,1)S(1)}, bf16[256,512]{1,0:T(8,128)(2,1)S(1)}, u32[]{:S(2)}, u32[]{:S(2)}) collective-permute-start(bf16[256,512]{1,0:T(8,128)(2,1)S(1)} %give.7), channel_id=1, source_target_pairs={{0,4},{2,6},{4,0},{6,2},{1,5},{3,7},{5,1},{7,3},{8,12},{10,14},{12... | collective-permute-start | bytes 786440 | tf_op jit(solution)/shard_map/ppermute | solution.py:35
  44.2 1.6 %collective-permute-start.18 = (bf16[256,512]{1,0:T(8,128)(2,1)S(1)}, bf16[256,512]{1,0:T(8,128)(2,1)S(1)}, u32[]{:S(2)}, u32[]{:S(2)}) collective-permute-start(bf16[256,512]{1,0:T(8,128)(2,1)S(1)} %give.6), channel_id=1, source_target_pairs={{0,2},{2,0},{4,6},{6,4},{1,3},{3,1},{5,7},{7,5},{8,10},{10,8},{12,... | collective-permute-start | bytes 786440 | tf_op jit(solution)/shard_map/ppermute | solution.py:35
  45.8 1.9 %collective-permute-done.14.far.refs_1_ = bf16[256,512]{1,0:T(8,128)(2,1)S(1)} collective-permute-done((bf16[256,512]{1,0:T(8,128)(2,1)S(1)}, bf16[256,512]{1,0:T(8,128)(2,1)S(1)}, u32[]{:S(2)}, u32[]{:S(2)}) %collective-permute-start.14) | collective-permute-done | bytes 262176 | tf_op jit(solution)/shard_map/ppermute | solution.py:35
  47.9 1.6 %collective-permute-start.15 = (bf16[256,512]{1,0:T(8,128)(2,1)S(1)}, bf16[256,512]{1,0:T(8,128)(2,1)S(1)}, u32[]{:S(2)}, u32[]{:S(2)}) collective-permute-start(bf16[256,512]{1,0:T(8,128)(2,1)S(1)} %give.5), channel_id=1, source_target_pairs={{0,4},{2,6},{4,0},{6,2},{1,5},{3,7},{5,1},{7,3},{8,12},{10,14},{12... | collective-permute-start | bytes 786440 | tf_op jit(solution)/shard_map/ppermute | solution.py:35
  49.8 1.6 %collective-permute-start.13 = (bf16[256,512]{1,0:T(8,128)(2,1)S(1)}, bf16[256,512]{1,0:T(8,128)(2,1)S(1)}, u32[]{:S(2)}, u32[]{:S(2)}) collective-permute-start(bf16[256,512]{1,0:T(8,128)(2,1)S(1)} %give.4), channel_id=1, source_target_pairs={{0,2},{2,0},{4,6},{6,4},{1,3},{3,1},{5,7},{7,5},{8,10},{10,8},{12,... | collective-permute-start | bytes 786440 | tf_op jit(solution)/shard_map/ppermute | solution.py:35
  51.4 0.7 %keep.1 = (f32[512,512]{1,0:T(8,128)S(1)}, f32[512,512]{1,0:T(8,128)S(1)}) custom-call(bf16[256,512]{1,0:T(8,128)(2,1)S(1)} %collective-permute-done.9.far.refs_0_, bf16[256,512]{1,0:T(8,128)(2,1)S(1)} %collective-permute-done.14.far.refs_1_, bf16[256,512]{1,0:T(8,128)(2,1)S(1)} %collective-permute-done.16.refs_2_.far, ...), custom_call_target="tpu_custom_call" | custom-call | flops 1 | bytes 1 | tf_op jit(solution)/shard_map/keep/pallas_call | solution.py:40
  52.1 2.7 %collective-permute-done.19.refs_1_ = bf16[256,512]{1,0:T(8,128)(2,1)S(1)} collective-permute-done((bf16[256,512]{1,0:T(8,128)(2,1)S(1)}, bf16[256,512]{1,0:T(8,128)(2,1)S(1)}, u32[]{:S(2)}, u32[]{:S(2)}) %collective-permute-start.19) | collective-permute-done | bytes 262176 | tf_op jit(solution)/shard_map/ppermute | solution.py:35
  54.8 0.9 %finish.2.refs_4_ = bf16[1,1024,512]{2,1,0:T(8,128)(2,1)} custom-call(bf16[256,512]{1,0:T(8,128)(2,1)S(1)} %collective-permute-done.18.refs_0_, bf16[256,512]{1,0:T(8,128)(2,1)S(1)} %collective-permute-done.19.refs_1_, f32[512,512]{1,0:T(8,128)S(1)} %get-tuple-element.83.refs_2_, f32[512,512]{1,0:T(8,128)S(1)} %get-tuple-element.84.refs_3_), custom_call_target="tpu_custom_call" | custom-call | tf_op jit(solution)/shard_map/finish/pallas_call | solution.py:554
  55.6 3.6 %collective-permute-done.15.refs_1_ = bf16[256,512]{1,0:T(8,128)(2,1)S(1)} collective-permute-done((bf16[256,512]{1,0:T(8,128)(2,1)S(1)}, bf16[256,512]{1,0:T(8,128)(2,1)S(1)}, u32[]{:S(2)}, u32[]{:S(2)}) %collective-permute-start.15) | collective-permute-done | bytes 262176 | tf_op jit(solution)/shard_map/ppermute | solution.py:35
  59.2 0.9 %finish.3 = bf16[1,1024,512]{2,1,0:T(8,128)(2,1)} custom-call(bf16[256,512]{1,0:T(8,128)(2,1)S(1)} %collective-permute-done.13.refs_0_, bf16[256,512]{1,0:T(8,128)(2,1)S(1)} %collective-permute-done.15.refs_1_, f32[512,512]{1,0:T(8,128)S(1)} %get-tuple-element.83.refs_2_, f32[512,512]{1,0:T(8,128)S(1)} %get-tuple-element.84.refs_3_, ...), custom_call_target="tpu_custom_call", output_to_operand_aliasing={{}: (4, {})} | custom-call | tf_op jit(solution)/shard_map/finish/pallas_call | solution.py:554
  (25 shorter events, 2.0 us)
Async XLA Ops:
  0.0 4.9 %collective-permute-start.1 = (bf16[1024,512]{1,0:T(8,128)(2,1)}, bf16[1024,512]{1,0:T(8,128)(2,1)S(1)}, u32[]{:S(2)}, u32[]{:S(2)}) collective-permute-start(bf16[1024,512]{1,0:T(8,128)(2,1)} %wk_far.1), channel_id=1, source_target_pairs={{0,1},{1,0},{2,3},{3,2},{4,5},{5,4},{6,7},{7,6},{8,9},{9,8},{10,11... | collective-permute-start | bytes 3145736 | tf_op jit(solution)/shard_map/ppermute | solution.py:35
  0.0 4.9 %collective-permute-start.2 = (bf16[1024,512]{1,0:T(8,128)(2,1)}, bf16[1024,512]{1,0:T(8,128)(2,1)S(1)}, u32[]{:S(2)}, u32[]{:S(2)}) collective-permute-start(bf16[1024,512]{1,0:T(8,128)(2,1)} %wv_far.1), channel_id=1, source_target_pairs={{0,1},{1,0},{2,3},{3,2},{4,5},{5,4},{6,7},{7,6},{8,9},{9,8},{10,11... | collective-permute-start | bytes 3145736 | tf_op jit(solution)/shard_map/ppermute | solution.py:35
  4.8 5.2 %collective-permute-start = (bf16[512,1024]{1,0:T(8,128)(2,1)S(1)}, bf16[512,1024]{1,0:T(8,128)(2,1)S(1)}, u32[]{:S(2)}, u32[]{:S(2)}) collective-permute-start(bf16[512,1024]{1,0:T(8,128)(2,1)S(1)} %get-tuple-element.66.first.own_first), channel_id=1, source_target_pairs={{0,1},{1,0},{2,3},{3,2},{4,5},{5,4},{6,7},{7,6},{8,9},{9,8},{10,11... | collective-permute-start | bytes 3145736 | tf_op jit(solution)/shard_map/ppermute | solution.py:35
  8.1 4.3 %collective-permute-start.3 = (bf16[1024,512]{1,0:T(8,128)(2,1)S(1)}, bf16[1024,512]{1,0:T(8,128)(2,1)S(1)}, u32[]{:S(2)}, u32[]{:S(2)}) collective-permute-start(bf16[1024,512]{1,0:T(8,128)(2,1)S(1)} %get-tuple-element.55.wq), channel_id=1, source_target_pairs={{0,1},{1,0},{2,3},{3,2},{4,5},{5,4},{6,7},{7,6},{8,9},{9,8},{10,11... | collective-permute-start | bytes 3145736 | tf_op jit(solution)/shard_map/ppermute | solution.py:35
  8.6 4.3 %collective-permute-start.4 = (bf16[1024,512]{1,0:T(8,128)(2,1)S(1)}, bf16[1024,512]{1,0:T(8,128)(2,1)S(1)}, u32[]{:S(2)}, u32[]{:S(2)}) collective-permute-start(bf16[1024,512]{1,0:T(8,128)(2,1)S(1)} %get-tuple-element.56.wg), channel_id=1, source_target_pairs={{0,1},{1,0},{2,3},{3,2},{4,5},{5,4},{6,7},{7,6},{8,9},{9,8},{10,11... | collective-permute-start | bytes 3145736 | tf_op jit(solution)/shard_map/ppermute | solution.py:35
  8.7 10.7 %collective-permute-start.5 = (bf16[528,256]{1,0:T(8,128)(2,1)S(1)}, bf16[528,256]{1,0:T(8,128)(2,1)S(1)}, u32[]{:S(2)}, u32[]{:S(2)}) collective-permute-start(bf16[528,256]{1,0:T(8,128)(2,1)S(1)} %get-tuple-element.61.sent), channel_id=1, source_target_pairs={{0,8},{8,16},{16,24},{1,9},{9,17},{17,25},{2,10},{10,18},{18,26},{... | collective-permute-start | bytes 811016 | tf_op jit(solution)/shard_map/ppermute | solution.py:466
  10.1 12.0 %collective-permute-start.8 = (bf16[512,512]{1,0:T(8,128)(2,1)S(1)}, bf16[512,512]{1,0:T(8,128)(2,1)S(1)}, u32[]{:S(2)}, u32[]{:S(2)}) collective-permute-start(bf16[512,512]{1,0:T(8,128)(2,1)S(1)} %get-tuple-element.67), channel_id=1, source_target_pairs={{0,2},{1,5},{2,0},{3,7},{4,6},{5,1},{6,4},{7,3},{8,10},{9,13},{10,... | collective-permute-start | bytes 1572872 | tf_op jit(solution)/shard_map/ppermute | solution.py:500
  11.7 10.4 %collective-permute-start.7 = (bf16[528,256]{1,0:T(8,128)(2,1)S(1)}, bf16[528,256]{1,0:T(8,128)(2,1)S(1)}, u32[]{:S(2)}, u32[]{:S(2)}) collective-permute-start(bf16[528,256]{1,0:T(8,128)(2,1)S(1)} %get-tuple-element.61.sent), channel_id=1, source_target_pairs={{0,16},{16,0},{1,17},{17,1},{2,18},{18,2},{3,19},{19,3},{4,20},{20... | collective-permute-start | bytes 811016 | tf_op jit(solution)/shard_map/ppermute | solution.py:466
  12.4 20.0 %collective-permute-start.10 = (bf16[512,512]{1,0:T(8,128)(2,1)S(1)}, bf16[512,512]{1,0:T(8,128)(2,1)S(1)}, u32[]{:S(2)}, u32[]{:S(2)}) collective-permute-start(bf16[512,512]{1,0:T(8,128)(2,1)S(1)} %get-tuple-element.77), channel_id=1, source_target_pairs={{0,2},{1,5},{2,0},{3,7},{4,6},{5,1},{6,4},{7,3},{8,10},{9,13},{10,... | collective-permute-start | bytes 1572872 | tf_op jit(solution)/shard_map/ppermute | solution.py:500
  19.6 11.1 %collective-permute-start.6 = (bf16[512,256]{1,0:T(8,128)(2,1)S(1)}, bf16[512,256]{1,0:T(8,128)(2,1)S(1)}, u32[]{:S(2)}, u32[]{:S(2)}) collective-permute-start(bf16[512,256]{1,0:T(8,128)(2,1)S(1)} %get-tuple-element.63), channel_id=1, source_target_pairs={{8,24},{24,8},{9,25},{25,9},{10,26},{26,10},{11,27},{27,11},{12,28... | collective-permute-start | bytes 786440 | tf_op jit(solution)/shard_map/ppermute | solution.py:466
  32.3 5.7 %collective-permute-start.11 = (bf16[512,512]{1,0:T(8,128)(2,1)S(1)}, bf16[512,512]{1,0:T(8,128)(2,1)S(1)}, u32[]{:S(2)}, u32[]{:S(2)}) collective-permute-start(bf16[512,512]{1,0:T(8,128)(2,1)S(1)} %collective-permute-done.8.mine_0), channel_id=1, source_target_pairs={{0,1},{1,0},{2,3},{3,2},{4,5},{5,4},{6,7},{7,6},{8,9},{9,8},{10,11... | collective-permute-start | bytes 1572872 | tf_op jit(solution)/shard_map/ppermute | solution.py:35
  32.3 7.4 %collective-permute-start.12 = (bf16[512,512]{1,0:T(8,128)(2,1)S(1)}, bf16[512,512]{1,0:T(8,128)(2,1)S(1)}, u32[]{:S(2)}, u32[]{:S(2)}) collective-permute-start(bf16[512,512]{1,0:T(8,128)(2,1)S(1)} %collective-permute-done.10.mine_1), channel_id=1, source_target_pairs={{0,1},{1,0},{2,3},{3,2},{4,5},{5,4},{6,7},{7,6},{8,9},{9,8},{10,11... | collective-permute-start | bytes 1572872 | tf_op jit(solution)/shard_map/ppermute | solution.py:35
  32.8 9.2 %collective-permute-start.17 = (bf16[256,512]{1,0:T(8,128)(2,1)S(1)}, bf16[256,512]{1,0:T(8,128)(2,1)S(1)}, u32[]{:S(2)}, u32[]{:S(2)}) collective-permute-start(bf16[256,512]{1,0:T(8,128)(2,1)S(1)} %get-tuple-element.75.refs_3_), channel_id=1, source_target_pairs={{0,2},{2,0},{4,6},{6,4},{1,3},{3,1},{5,7},{7,5},{8,10},{10,8},{12,... | collective-permute-start | bytes 786440 | tf_op jit(solution)/shard_map/ppermute | solution.py:35
  34.3 9.6 %collective-permute-start.16 = (bf16[256,512]{1,0:T(8,128)(2,1)S(1)}, bf16[256,512]{1,0:T(8,128)(2,1)S(1)}, u32[]{:S(2)}, u32[]{:S(2)}) collective-permute-start(bf16[256,512]{1,0:T(8,128)(2,1)S(1)} %get-tuple-element.74.refs_2_), channel_id=1, source_target_pairs={{0,4},{2,6},{4,0},{6,2},{1,5},{3,7},{5,1},{7,3},{8,12},{10,14},{12... | collective-permute-start | bytes 786440 | tf_op jit(solution)/shard_map/ppermute | solution.py:35
  37.4 10.2 %collective-permute-start.14 = (bf16[256,512]{1,0:T(8,128)(2,1)S(1)}, bf16[256,512]{1,0:T(8,128)(2,1)S(1)}, u32[]{:S(2)}, u32[]{:S(2)}) collective-permute-start(bf16[256,512]{1,0:T(8,128)(2,1)S(1)} %get-tuple-element.73.refs_1_), channel_id=1, source_target_pairs={{0,2},{2,0},{4,6},{6,4},{1,3},{3,1},{5,7},{7,5},{8,10},{10,8},{12,... | collective-permute-start | bytes 786440 | tf_op jit(solution)/shard_map/ppermute | solution.py:35
  38.0 11.5 %collective-permute-start.9 = (bf16[256,512]{1,0:T(8,128)(2,1)S(1)}, bf16[256,512]{1,0:T(8,128)(2,1)S(1)}, u32[]{:S(2)}, u32[]{:S(2)}) collective-permute-start(bf16[256,512]{1,0:T(8,128)(2,1)S(1)} %get-tuple-element.72.refs_0_), channel_id=1, source_target_pairs={{0,4},{2,6},{4,0},{6,2},{1,5},{3,7},{5,1},{7,3},{8,12},{10,14},{12... | collective-permute-start | bytes 786440 | tf_op jit(solution)/shard_map/ppermute | solution.py:35
  42.3 12.5 %collective-permute-start.19 = (bf16[256,512]{1,0:T(8,128)(2,1)S(1)}, bf16[256,512]{1,0:T(8,128)(2,1)S(1)}, u32[]{:S(2)}, u32[]{:S(2)}) collective-permute-start(bf16[256,512]{1,0:T(8,128)(2,1)S(1)} %give.7), channel_id=1, source_target_pairs={{0,4},{2,6},{4,0},{6,2},{1,5},{3,7},{5,1},{7,3},{8,12},{10,14},{12... | collective-permute-start | bytes 786440 | tf_op jit(solution)/shard_map/ppermute | solution.py:35
  44.2 10.6 %collective-permute-start.18 = (bf16[256,512]{1,0:T(8,128)(2,1)S(1)}, bf16[256,512]{1,0:T(8,128)(2,1)S(1)}, u32[]{:S(2)}, u32[]{:S(2)}) collective-permute-start(bf16[256,512]{1,0:T(8,128)(2,1)S(1)} %give.6), channel_id=1, source_target_pairs={{0,2},{2,0},{4,6},{6,4},{1,3},{3,1},{5,7},{7,5},{8,10},{10,8},{12,... | collective-permute-start | bytes 786440 | tf_op jit(solution)/shard_map/ppermute | solution.py:35
  47.9 11.3 %collective-permute-start.15 = (bf16[256,512]{1,0:T(8,128)(2,1)S(1)}, bf16[256,512]{1,0:T(8,128)(2,1)S(1)}, u32[]{:S(2)}, u32[]{:S(2)}) collective-permute-start(bf16[256,512]{1,0:T(8,128)(2,1)S(1)} %give.5), channel_id=1, source_target_pairs={{0,4},{2,6},{4,0},{6,2},{1,5},{3,7},{5,1},{7,3},{8,12},{10,14},{12... | collective-permute-start | bytes 786440 | tf_op jit(solution)/shard_map/ppermute | solution.py:35
  49.8 9.4 %collective-permute-start.13 = (bf16[256,512]{1,0:T(8,128)(2,1)S(1)}, bf16[256,512]{1,0:T(8,128)(2,1)S(1)}, u32[]{:S(2)}, u32[]{:S(2)}) collective-permute-start(bf16[256,512]{1,0:T(8,128)(2,1)S(1)} %give.4), channel_id=1, source_target_pairs={{0,2},{2,0},{4,6},{6,4},{1,3},{3,1},{5,7},{7,5},{8,10},{10,8},{12,... | collective-permute-start | bytes 786440 | tf_op jit(solution)/shard_map/ppermute | solution.py:35

commit v18 on v17

--- a/solution.py
+++ b/solution.py
@@ -312,11 +312,13 @@
     arrivals, refs, token = refs[: len(sets)], refs[len(sets) : -1], refs[-1]
     projected, outs = refs[: -len(starts)], refs[-len(starts) :]
     token[...] = jnp.zeros_like(token)
+    core = lax.axis_index("fsdp")
     for head in range(heads):
         span = slice(head * DH, (head + 1) * DH)
         entering_log = entering[heads * DH + head : heads * DH + head + 1, :1]
         state = entering[span, :] + jnp.exp(entering_log) * arrived_state(arrivals, sets, hop, span)
-        for start, out in zip(starts, outs):
+        pieces = []
+        for start in starts:
             block = start // BLOCK
             q, gate, intra = projected[3 * block : 3 * block + 3]
             at = slice(start % BLOCK, start % BLOCK + TILE)
@@ -329,7 +331,9 @@
             retained = intra[at, span] + column * mm(q[at, span], prior)
             center = retained - jnp.mean(retained, axis=1, keepdims=True)
             spread = jnp.mean(center * center, axis=1, keepdims=True)
-            out[:, span] = (gate[at, span] * center * lax.rsqrt(spread + 1e-5)).astype(BF16)
+            pieces.append((gate[at, span] * center * lax.rsqrt(spread + 1e-5)).astype(BF16))
+        for role, out in enumerate(outs):
+            out[:, span] = jnp.where(core == 0, pieces[role], pieces[1 - role])
 
 
 def columns_kernel(first, second, *outs):
@@ -350,13 +354,13 @@
             out[...] = jnp.where(high == 0, first[:, at], second[:, at])
 
 
-def arrange_kernel(mine_0, mine_1, other_0, other_1, low_out, high_out):
+def arrange_kernel(mine_0, mine_1, other_0, other_1, *outs):
     cols = mine_0.shape[1]
     place, core = lax.axis_index("tp"), lax.axis_index("fsdp")
-    for gathered, bit, out in ((core == 0, place // 2, low_out), (core == 1, place % 2, high_out)):
-        blocks = [jnp.where(gathered, mine[...], other[...]) for mine, other in ((mine_0, other_0), (mine_1, other_1))]
-        out[:, :cols] = jnp.where(bit == 0, blocks[1], blocks[0])
-        out[:, cols:] = jnp.where(bit == 0, blocks[0], blocks[1])
+    for role, (blocks, out) in enumerate(zip(((mine_0, mine_1), (other_0, other_1)), outs)):
+        bit = jnp.where(core == role, place // 2, place % 2)
+        out[:, :cols] = jnp.where(bit == 0, blocks[1][...], blocks[0][...])
+        out[:, cols:] = jnp.where(bit == 0, blocks[0][...], blocks[1][...])
 
 
 def own_kernel(order, own_first, own_second, *refs):
@@ -368,14 +372,13 @@
     mine = pl.ds(pl.multiple_of(low * cols, cols), cols)
     flipped = pl.ds(pl.multiple_of((1 - low) * cols, cols), cols)
     keep = jnp.where(here, own_first[:, mine], own_second[:, mine])
-    gives = [
-        jnp.where(here, own_second[:, mine], own_first[:, mine]),
-        jnp.where(here, own_first[:, flipped], own_second[:, flipped]),
-    ]
-    for (half, number), piece in zip(order, pieces):
+    low_give = jnp.where(here, own_second[:, mine], own_first[:, mine])
+    high_give = jnp.where(here, own_first[:, flipped], own_second[:, flipped])
+    gives = [jnp.where(core == role, low_give, high_give) for role in range(2)]
+    for (role, number), piece in zip(order, pieces):
         at = slice(number * TILE, (number + 1) * TILE)
-        outs[half][at, :cols] = mm(piece[...], gives[half])
-        outs[half][at, cols:] = mm(piece[...], keep)
+        outs[role][at, :cols] = mm(piece[...], gives[role])
+        outs[role][at, cols:] = mm(piece[...], keep)
 
 
 def give_kernel(number, own, far, weight, out):
@@ -387,21 +390,21 @@
 def keep_kernel(order, *refs):
     count = len(order)
     fars, owns, weights, outs = refs[:count], refs[count : count + 2], refs[count + 2 : count + 4], refs[count + 4 :]
-    for (half, number), far in zip(order, fars):
+    for (role, number), far in zip(order, fars):
         cols = far.shape[1]
         at = slice(number * TILE, (number + 1) * TILE)
-        outs[half][at, :] = owns[half][at, cols:] + mm(far[...], weights[half][:, cols:])
+        outs[role][at, :] = owns[role][at, cols:] + mm(far[...], weights[role][:, cols:])
 
 
 def finish_kernel(order, *refs):
     count = len(order)
     gots, keeps, out, ready, written = refs[:count], refs[count : count + 2], refs[-3], refs[-2], refs[-1]
-    copies = []
-    for slot, ((half, number), got) in enumerate(zip(order, gots)):
-        keep = keeps[half]
+    core, copies = lax.axis_index("fsdp"), []
+    for slot, ((role, number), got) in enumerate(zip(order, gots)):
+        keep = keeps[role]
         at = slice(number * TILE, (number + 1) * TILE)
         ready[slot] = (keep[at, :] + got[...].astype(F32)).astype(BF16)
-        start = half * keep.shape[0] + number * TILE
+        start = pl.multiple_of((role + core) % 2 * keep.shape[0] + number * TILE, TILE)
         copies.append(pltpu.make_async_copy(ready.at[slot], out.at[0, pl.ds(start, TILE)], written.at[slot]))
         copies[-1].start()
     for copy in copies:
@@ -420,7 +423,14 @@
     blocks = rows // BLOCK
     ctx, tp, cores = lax.axis_size("ctx"), lax.axis_size("tp"), lax.axis_size("fsdp")
     assert tp == 4 and cores == 2 and ctx >= 4 and ctx & (ctx - 1) == 0
-    near_mask, far_mask = 1, 2
+    partners = [
+        [(at * cores + core, (at ^ (1 << (role + core) % 2)) * cores + core) for at in range(tp) for core in range(cores)]
+        for role in range(2)
+    ]
+
+    def trade(value, role):
+        return lax.ppermute(value, ("tp", "fsdp"), partners[role])
+
     tables = [((2, rows // FINE, DH // 2), F32), ((2, FINE, DH // 2), F32)]
 
     key_far = swap(key_weight, "fsdp", 1)
@@ -496,15 +506,13 @@
         [after(out_first, first_message), own_second],
         "columns",
     )
-    pairs = [(at * cores + at_core, (at ^ mask) * cores + at_core) for at in range(tp) for at_core, mask in enumerate((near_mask, far_mask))]
-    out_mine = [lax.ppermute(block, ("tp", "fsdp"), pairs) for block in for_partner]
+    out_mine = [trade(block, 0) for block in for_partner]
 
     held = after(decay, message, *early, out_mine[0])
     for block in range(1, blocks):
         projected += query_gate(block, held)
 
     count = rows // 2 // TILE
-    masks = (near_mask, far_mask)
     hidden, far = [[], []], [[], []]
     for number in range(count):
         held = after(decay, swap(pair[2], "fsdp", 1)) if number else decay
@@ -516,35 +524,35 @@
         )
         if number == 0:
             out_other = [swap(after(block, pair[0]), "fsdp", 1) for block in out_mine]
-        for half in range(2):
-            hidden[half].append(pair[half])
-            far[half].append(swap(pair[half], "tp", masks[half]))
+        for role in range(2):
+            hidden[role].append(pair[role])
+            far[role].append(trade(pair[role], role))
     weights = kernel_call(
         arrange_kernel,
         [((cols, 2 * cols), BF16)] * 2,
         [*out_mine, *out_other],
         "arrange",
     )
-    order = [(half, number) for number in reversed(range(count)) for half in (1, 0)]
+    order = [(role, number) for number in reversed(range(count)) for role in (1, 0)]
     owns = kernel_call(
         functools.partial(own_kernel, order),
         [((count * TILE, 2 * cols), F32)] * 2,
-        [out_first, own_second, *(hidden[half][number] for half, number in order)],
+        [out_first, own_second, *(hidden[role][number] for role, number in order)],
         "own_products",
     )
     gots = []
-    for half, number in order:
+    for role, number in order:
         [give] = kernel_call(
             functools.partial(give_kernel, number),
             [((TILE, cols), BF16)],
-            [owns[half], far[half][number], weights[half]],
+            [owns[role], far[role][number], weights[role]],
             "give",
         )
-        gots.append(swap(give, "tp", masks[1 - half]))
+        gots.append(trade(give, 1 - role))
     keeps = kernel_call(
         functools.partial(keep_kernel, order),
         [((count * TILE, cols), F32)] * 2,
-        [*(far[half][number] for half, number in order), *owns, *weights],
+        [*(far[role][number] for role, number in order), *owns, *weights],
         "keep",
     )
     result = None

time: 60.4 us -> 60.5 us (level)
  waiting for transfers between devices: 19 us -> 17.8 us
  Pallas kernels: 22.1 us -> 23 us
    ppermute x2 -> x10, starting transfers between devices: 2.16 us -> 13 us  [trade(): return lax.ppermute(value, ('tp', 'fsdp'), partners[role])]
    ppermute x15 -> x7, starting transfers between devices: 12.2 us -> 1.71 us  [swap(): lax.ppermute(value, axis, [(place, place ^ mask) for place in range(size)])]
    ppermute x15 -> x7, waiting for transfers between devices: 10.1 us -> 0.02 us  [swap(): lax.ppermute(value, axis, [(place, place ^ mask) for place in range(size)])]
    ppermute x2 -> x10, waiting for transfers between devices: 0.01 us -> 8.9 us  [trade(): return lax.ppermute(value, ('tp', 'fsdp'), partners[role])]
    pallas_call x13, Pallas kernels: 12.9 us -> 13.8 us  [kernel_call(): pl.pallas_call(kernel, in_specs=[pl.BlockSpec(memory_space=pltpu.VMEM)] *...]
  transfers between devices with their start and end apart: 20 -> 20, of which waited for: 6 -> 7; matrix products, arithmetic and copies ran while one was open for 0% -> 0% of each run, Pallas kernels for 35% -> 37%
where the time goes in v18:
time: 60.5 us; the launch traced here: 60.2 us
  Pallas kernels  23 us (38%)
  starting transfers between devices  19.1 us (32%)
  waiting for transfers between devices  17.8 us (29%)
    pallas_call x13, Pallas kernels, kernel_call(): pl.pallas_call(kernel, in_specs=[pl.BlockSpec(memory_space=pltpu.VMEM)] *...  13.8 us
    ppermute x10, starting transfers between devices, trade(): return lax.ppermute(value, ('tp', 'fsdp'), partners[role])  13 us
    ppermute x3, waiting for transfers between devices, exchange(): return lax.ppermute(message, 'ctx', pairs)  8.91 us
    ppermute x10, waiting for transfers between devices, trade(): return lax.ppermute(value, ('tp', 'fsdp'), partners[role])  8.9 us
    pallas_call x2, Pallas kernels, loading_call(): pl.pallas_call(kernel, in_specs=[pl.BlockSpec(memory_space=pltpu.HBM)] *...  7.48 us
    ppermute x3, starting transfers between devices, exchange(): return lax.ppermute(message, 'ctx', pairs)  4.4 us
    ppermute x7, starting transfers between devices, swap(): lax.ppermute(value, axis, [(place, place ^ mask) for place in range(size)])  1.71 us
    pallas_call x2, Pallas kernels, on_device(): pl.pallas_call(functools.partial(finish_kernel, part_order), in_specs=[pl...  1.7 us
  transfers between devices with their start and end apart: 20, of which 7 were waited for; matrix products, arithmetic and copies ran while one was open for 0% of the time, Pallas kernels for 37%

profile of v18, /device:TPU:24, one launch (start us, length us, event | category | flops | bytes accessed | tf_op | source)
XLA Modules:
  0.0 60.2 jit_solution(17155217523968078657)
XLA Ops:
  0.5 4.3 %key_value_own.1 = (bf16[1024,1024]{1,0:T(8,128)(2,1)S(1)}, bf16[1024,1024]{1,0:T(8,128)(2,1)S(1)}, f32[1024,512]{1,0:T(8,128)S(1)}, f32[1024,512]{1,0:T(8,128)S...) custom-call(bf16[1024,2048]{1,0:T(8,128)(2,1)} %bitcast.4, ...), custom_call_target="tpu_custom_call" | custom-call | flops 1 | bytes 1 | tf_op jit(solution)/shard_map/key_value_own/pallas_call | solution.py:56
  4.9 3.2 %key_value.1 = (bf16[1024,512]{1,0:T(8,128)(2,1)S(1)}, bf16[1024,512]{1,0:T(8,128)(2,1)S(1)}, bf16[1024,512]{1,0:T(8,128)(2,1)S(1)}, bf16[1024,512]{1,0:T(8,128)...) custom-call(bf16[1024,512]{1,0:T(8,128)(2,1)} %wq_far.1, ...), custom_call_target="tpu_custom_call" | custom-call | flops 1 | bytes 1 | tf_op jit(solution)/shard_map/key_value/pallas_call | solution.py:56
  8.1 0.5 collective-permute-start.3
  8.7 1.3 %collective-permute-start.5 = (bf16[528,256]{1,0:T(8,128)(2,1)S(1)}, bf16[528,256]{1,0:T(8,128)(2,1)S(1)}, u32[]{:S(2)}, u32[]{:S(2)}) collective-permute-start(bf16[528,256]{1,0:T(8,128)(2,1)S(1)} %get-tuple-element.61.sent), channel_id=1, source_target_pairs={{0,8},{8,16},{16,24},{1,9},{9,17},{17,25},{2,10},{10,18},{18,26},{... | collective-permute-start | bytes 811016 | tf_op jit(solution)/shard_map/ppermute | solution.py:476
  10.1 1.6 %collective-permute-start.8 = (bf16[512,512]{1,0:T(8,128)(2,1)S(1)}, bf16[512,512]{1,0:T(8,128)(2,1)S(1)}, u32[]{:S(2)}, u32[]{:S(2)}) collective-permute-start(bf16[512,512]{1,0:T(8,128)(2,1)S(1)} %get-tuple-element.67), channel_id=1, source_target_pairs={{0,2},{1,5},{2,0},{3,7},{4,6},{5,1},{6,4},{7,3},{8,10},{9,13},{10,... | collective-permute-start | bytes 1572872 | tf_op jit(solution)/shard_map/ppermute | solution.py:432
  11.7 0.7 %collective-permute-start.7 = (bf16[528,256]{1,0:T(8,128)(2,1)S(1)}, bf16[528,256]{1,0:T(8,128)(2,1)S(1)}, u32[]{:S(2)}, u32[]{:S(2)}) collective-permute-start(bf16[528,256]{1,0:T(8,128)(2,1)S(1)} %get-tuple-element.61.sent), channel_id=1, source_target_pairs={{0,16},{16,0},{1,17},{17,1},{2,18},{18,2},{3,19},{19,3},{4,20},{20... | collective-permute-start | bytes 811016 | tf_op jit(solution)/shard_map/ppermute | solution.py:476
  12.4 0.6 collective-permute-start.10
  13.0 3.1 %query_gate.2 = (bf16[512,512]{1,0:T(8,128)(2,1)S(1)}, f32[512,512]{1,0:T(8,128)S(1)}, f32[512,512]{1,0:T(8,128)S(1)}) custom-call(bf16[1024,1024]{1,0:T(8,128)(2,1)S(1)} %get-tuple-element.54.x_own, bf16[1024,1024]{1,0:T(8,128)(2,1)S(1)} %get-tuple-element.47.x.x_other, bf16[1024,512]{1,0:T(8,128)(2,1)S(1)} %get-tuple-element.55.wq, ...), custom_call_target="tpu_custom_call" | custom-call | flops 1 | bytes 1 | tf_op jit(solution)/shard_map/query_gate/pallas_call | solution.py:40
  16.1 3.4 %collective-permute-done.5.refs_0_ = bf16[528,256]{1,0:T(8,128)(2,1)S(1)} collective-permute-done((bf16[528,256]{1,0:T(8,128)(2,1)S(1)}, bf16[528,256]{1,0:T(8,128)(2,1)S(1)}, u32[]{:S(2)}, u32[]{:S(2)}) %collective-permute-start.5) | collective-permute-done | bytes 270368 | tf_op jit(solution)/shard_map/ppermute | solution.py:476
  19.6 2.5 %collective-permute-start.6 = (bf16[512,256]{1,0:T(8,128)(2,1)S(1)}, bf16[512,256]{1,0:T(8,128)(2,1)S(1)}, u32[]{:S(2)}, u32[]{:S(2)}) collective-permute-start(bf16[512,256]{1,0:T(8,128)(2,1)S(1)} %get-tuple-element.63), channel_id=1, source_target_pairs={{8,24},{24,8},{9,25},{25,9},{10,26},{26,10},{11,27},{27,11},{12,28... | collective-permute-start | bytes 786440 | tf_op jit(solution)/shard_map/ppermute | solution.py:476
  22.1 3.1 %query_gate.3 = (bf16[512,512]{1,0:T(8,128)(2,1)S(1)}, f32[512,512]{1,0:T(8,128)S(1)}, f32[512,512]{1,0:T(8,128)S(1)}) custom-call(bf16[1024,1024]{1,0:T(8,128)(2,1)S(1)} %get-tuple-element.54.x_own, bf16[1024,1024]{1,0:T(8,128)(2,1)S(1)} %get-tuple-element.47.x.x_other, bf16[1024,512]{1,0:T(8,128)(2,1)S(1)} %get-tuple-element.55.wq, ...), custom_call_target="tpu_custom_call" | custom-call | flops 1 | bytes 1 | tf_op jit(solution)/shard_map/query_gate/pallas_call | solution.py:40
  25.2 5.5 %collective-permute-done.6.refs_0_ = bf16[512,256]{1,0:T(8,128)(2,1)S(1)} collective-permute-done((bf16[512,256]{1,0:T(8,128)(2,1)S(1)}, bf16[512,256]{1,0:T(8,128)(2,1)S(1)}, u32[]{:S(2)}, u32[]{:S(2)}) %collective-permute-start.6) | collective-permute-done | bytes 262176 | tf_op jit(solution)/shard_map/ppermute | solution.py:476
  30.7 1.9 %hidden.3 = (bf16[256,512]{1,0:T(8,128)(2,1)S(1)}, bf16[256,512]{1,0:T(8,128)(2,1)S(1)}, bf16[16,128]{1,0:T(8,128)(2,1)}) custom-call(f32[8,1024]{1,0:T(8,128)S(1)} %get-tuple-element.68.decay, bf16[2,512,256]{2,1,0:T(8,128)(2,1)S(1)} %get-tuple-element.52.before, f32[520,256]{1,0:T(8,128)S(1)} %get-tuple-element.62.entering, ...), custom_call_target="tpu_custom_call" | custom-call | flops 1 | bytes 1 | tf_op jit(solution)/shard_map/hidden/pallas_call | solution.py:40
  32.7 0.5 collective-permute-start.12
  33.2 1.5 %collective-permute-start.17 = (bf16[256,512]{1,0:T(8,128)(2,1)S(1)}, bf16[256,512]{1,0:T(8,128)(2,1)S(1)}, u32[]{:S(2)}, u32[]{:S(2)}) collective-permute-start(bf16[256,512]{1,0:T(8,128)(2,1)S(1)} %get-tuple-element.75.refs_3_), channel_id=1, source_target_pairs={{0,2},{1,5},{2,0},{3,7},{4,6},{5,1},{6,4},{7,3},{8,10},{9,13},{10,... | collective-permute-start | bytes 786440 | tf_op jit(solution)/shard_map/ppermute | solution.py:432
  34.7 1.5 %collective-permute-start.16 = (bf16[256,512]{1,0:T(8,128)(2,1)S(1)}, bf16[256,512]{1,0:T(8,128)(2,1)S(1)}, u32[]{:S(2)}, u32[]{:S(2)}) collective-permute-start(bf16[256,512]{1,0:T(8,128)(2,1)S(1)} %get-tuple-element.74.refs_2_), channel_id=1, source_target_pairs={{0,4},{1,3},{2,6},{3,1},{4,0},{5,7},{6,2},{7,5},{8,12},{9,11},{10,... | collective-permute-start | bytes 786440 | tf_op jit(solution)/shard_map/ppermute | solution.py:432
  36.2 1.9 %hidden.2 = (bf16[256,512]{1,0:T(8,128)(2,1)S(1)}, bf16[256,512]{1,0:T(8,128)(2,1)S(1)}, bf16[16,128]{1,0:T(8,128)(2,1)}) custom-call(f32[8,1024]{1,0:T(8,128)S(1)} %get-tuple-element.68.decay, bf16[2,512,256]{2,1,0:T(8,128)(2,1)S(1)} %get-tuple-element.52.before, f32[520,256]{1,0:T(8,128)S(1)} %get-tuple-element.62.entering, ...), custom_call_target="tpu_custom_call" | custom-call | flops 1 | bytes 1 | tf_op jit(solution)/shard_map/hidden/pallas_call | solution.py:40
  38.1 0.5 collective-permute-start.14
  38.7 0.5 collective-permute-start.9
  39.2 1.3 %own_products.1 = (f32[512,1024]{1,0:T(8,128)S(1)}, f32[512,1024]{1,0:T(8,128)S(1)}) custom-call(bf16[512,1024]{1,0:T(8,128)(2,1)S(1)} %get-tuple-element.66.first.own_first, bf16[512,1024]{1,0:T(8,128)(2,1)S(1)} %collective-permute-done.second.own_second, bf16[256,512]{1,0:T(8,128)(2,1)S(1)} %get-tuple-element.72.refs_0_, ...), custom_call_target="tpu_custom_call" | custom-call | flops 1 | bytes 1 | tf_op jit(solution)/shard_map/own_products/pallas_call | solution.py:40
  40.8 1.3 %collective-permute-done.17.refs_3_.far = bf16[256,512]{1,0:T(8,128)(2,1)S(1)} collective-permute-done((bf16[256,512]{1,0:T(8,128)(2,1)S(1)}, bf16[256,512]{1,0:T(8,128)(2,1)S(1)}, u32[]{:S(2)}, u32[]{:S(2)}) %collective-permute-start.17) | collective-permute-done | bytes 262176 | tf_op jit(solution)/shard_map/ppermute | solution.py:432
  42.4 1.8 %collective-permute-start.19 = (bf16[256,512]{1,0:T(8,128)(2,1)S(1)}, bf16[256,512]{1,0:T(8,128)(2,1)S(1)}, u32[]{:S(2)}, u32[]{:S(2)}) collective-permute-start(bf16[256,512]{1,0:T(8,128)(2,1)S(1)} %give.7), channel_id=1, source_target_pairs={{0,4},{1,3},{2,6},{3,1},{4,0},{5,7},{6,2},{7,5},{8,12},{9,11},{10,... | collective-permute-start | bytes 786440 | tf_op jit(solution)/shard_map/ppermute | solution.py:432
  44.5 1.6 %collective-permute-start.18 = (bf16[256,512]{1,0:T(8,128)(2,1)S(1)}, bf16[256,512]{1,0:T(8,128)(2,1)S(1)}, u32[]{:S(2)}, u32[]{:S(2)}) collective-permute-start(bf16[256,512]{1,0:T(8,128)(2,1)S(1)} %give.6), channel_id=1, source_target_pairs={{0,2},{1,5},{2,0},{3,7},{4,6},{5,1},{6,4},{7,3},{8,10},{9,13},{10,... | collective-permute-start | bytes 786440 | tf_op jit(solution)/shard_map/ppermute | solution.py:432
  46.1 1.6 %collective-permute-done.14.far.refs_1_ = bf16[256,512]{1,0:T(8,128)(2,1)S(1)} collective-permute-done((bf16[256,512]{1,0:T(8,128)(2,1)S(1)}, bf16[256,512]{1,0:T(8,128)(2,1)S(1)}, u32[]{:S(2)}, u32[]{:S(2)}) %collective-permute-start.14) | collective-permute-done | bytes 262176 | tf_op jit(solution)/shard_map/ppermute | solution.py:432
  48.0 1.8 %collective-permute-start.15 = (bf16[256,512]{1,0:T(8,128)(2,1)S(1)}, bf16[256,512]{1,0:T(8,128)(2,1)S(1)}, u32[]{:S(2)}, u32[]{:S(2)}) collective-permute-start(bf16[256,512]{1,0:T(8,128)(2,1)S(1)} %give.5), channel_id=1, source_target_pairs={{0,4},{1,3},{2,6},{3,1},{4,0},{5,7},{6,2},{7,5},{8,12},{9,11},{10,... | collective-permute-start | bytes 786440 | tf_op jit(solution)/shard_map/ppermute | solution.py:432
  50.1 1.6 %collective-permute-start.13 = (bf16[256,512]{1,0:T(8,128)(2,1)S(1)}, bf16[256,512]{1,0:T(8,128)(2,1)S(1)}, u32[]{:S(2)}, u32[]{:S(2)}) collective-permute-start(bf16[256,512]{1,0:T(8,128)(2,1)S(1)} %give.4), channel_id=1, source_target_pairs={{0,2},{1,5},{2,0},{3,7},{4,6},{5,1},{6,4},{7,3},{8,10},{9,13},{10,... | collective-permute-start | bytes 786440 | tf_op jit(solution)/shard_map/ppermute | solution.py:432
  51.7 0.7 %keep.1 = (f32[512,512]{1,0:T(8,128)S(1)}, f32[512,512]{1,0:T(8,128)S(1)}) custom-call(bf16[256,512]{1,0:T(8,128)(2,1)S(1)} %collective-permute-done.9.far.refs_0_, bf16[256,512]{1,0:T(8,128)(2,1)S(1)} %collective-permute-done.14.far.refs_1_, bf16[256,512]{1,0:T(8,128)(2,1)S(1)} %collective-permute-done.16.refs_2_.far, ...), custom_call_target="tpu_custom_call" | custom-call | flops 1 | bytes 1 | tf_op jit(solution)/shard_map/keep/pallas_call | solution.py:40
  52.4 1.5 %collective-permute-done.19.refs_1_ = bf16[256,512]{1,0:T(8,128)(2,1)S(1)} collective-permute-done((bf16[256,512]{1,0:T(8,128)(2,1)S(1)}, bf16[256,512]{1,0:T(8,128)(2,1)S(1)}, u32[]{:S(2)}, u32[]{:S(2)}) %collective-permute-start.19) | collective-permute-done | bytes 262176 | tf_op jit(solution)/shard_map/ppermute | solution.py:432
  53.9 0.9 %finish.2.refs_4_ = bf16[1,1024,512]{2,1,0:T(8,128)(2,1)} custom-call(bf16[256,512]{1,0:T(8,128)(2,1)S(1)} %collective-permute-done.18.refs_0_, bf16[256,512]{1,0:T(8,128)(2,1)S(1)} %collective-permute-done.19.refs_1_, f32[512,512]{1,0:T(8,128)S(1)} %get-tuple-element.83.refs_2_, f32[512,512]{1,0:T(8,128)S(1)} %get-tuple-element.84.refs_3_), custom_call_target="tpu_custom_call" | custom-call | tf_op jit(solution)/shard_map/finish/pallas_call | solution.py:562
  54.8 3.5 %collective-permute-done.15.refs_1_ = bf16[256,512]{1,0:T(8,128)(2,1)S(1)} collective-permute-done((bf16[256,512]{1,0:T(8,128)(2,1)S(1)}, bf16[256,512]{1,0:T(8,128)(2,1)S(1)}, u32[]{:S(2)}, u32[]{:S(2)}) %collective-permute-start.15) | collective-permute-done | bytes 262176 | tf_op jit(solution)/shard_map/ppermute | solution.py:432
  58.3 1.0 %collective-permute-done.13.refs_0_ = bf16[256,512]{1,0:T(8,128)(2,1)S(1)} collective-permute-done((bf16[256,512]{1,0:T(8,128)(2,1)S(1)}, bf16[256,512]{1,0:T(8,128)(2,1)S(1)}, u32[]{:S(2)}, u32[]{:S(2)}) %collective-permute-start.13) | collective-permute-done | bytes 262176 | tf_op jit(solution)/shard_map/ppermute | solution.py:432
  59.2 0.9 %finish.3 = bf16[1,1024,512]{2,1,0:T(8,128)(2,1)} custom-call(bf16[256,512]{1,0:T(8,128)(2,1)S(1)} %collective-permute-done.13.refs_0_, bf16[256,512]{1,0:T(8,128)(2,1)S(1)} %collective-permute-done.15.refs_1_, f32[512,512]{1,0:T(8,128)S(1)} %get-tuple-element.83.refs_2_, f32[512,512]{1,0:T(8,128)S(1)} %get-tuple-element.84.refs_3_, ...), custom_call_target="tpu_custom_call", output_to_operand_aliasing={{}: (4, {})} | custom-call | tf_op jit(solution)/shard_map/finish/pallas_call | solution.py:562
  (25 shorter events, 2.4 us)
Async XLA Ops:
  0.0 4.9 %collective-permute-start.1 = (bf16[1024,512]{1,0:T(8,128)(2,1)}, bf16[1024,512]{1,0:T(8,128)(2,1)S(1)}, u32[]{:S(2)}, u32[]{:S(2)}) collective-permute-start(bf16[1024,512]{1,0:T(8,128)(2,1)} %wk_far.1), channel_id=1, source_target_pairs={{0,1},{1,0},{2,3},{3,2},{4,5},{5,4},{6,7},{7,6},{8,9},{9,8},{10,11... | collective-permute-start | bytes 3145736 | tf_op jit(solution)/shard_map/ppermute | solution.py:35
  0.0 4.9 %collective-permute-start.2 = (bf16[1024,512]{1,0:T(8,128)(2,1)}, bf16[1024,512]{1,0:T(8,128)(2,1)S(1)}, u32[]{:S(2)}, u32[]{:S(2)}) collective-permute-start(bf16[1024,512]{1,0:T(8,128)(2,1)} %wv_far.1), channel_id=1, source_target_pairs={{0,1},{1,0},{2,3},{3,2},{4,5},{5,4},{6,7},{7,6},{8,9},{9,8},{10,11... | collective-permute-start | bytes 3145736 | tf_op jit(solution)/shard_map/ppermute | solution.py:35
  4.8 5.2 %collective-permute-start = (bf16[512,1024]{1,0:T(8,128)(2,1)S(1)}, bf16[512,1024]{1,0:T(8,128)(2,1)S(1)}, u32[]{:S(2)}, u32[]{:S(2)}) collective-permute-start(bf16[512,1024]{1,0:T(8,128)(2,1)S(1)} %get-tuple-element.66.first.own_first), channel_id=1, source_target_pairs={{0,1},{1,0},{2,3},{3,2},{4,5},{5,4},{6,7},{7,6},{8,9},{9,8},{10,11... | collective-permute-start | bytes 3145736 | tf_op jit(solution)/shard_map/ppermute | solution.py:35
  8.1 4.3 %collective-permute-start.3 = (bf16[1024,512]{1,0:T(8,128)(2,1)S(1)}, bf16[1024,512]{1,0:T(8,128)(2,1)S(1)}, u32[]{:S(2)}, u32[]{:S(2)}) collective-permute-start(bf16[1024,512]{1,0:T(8,128)(2,1)S(1)} %get-tuple-element.55.wq), channel_id=1, source_target_pairs={{0,1},{1,0},{2,3},{3,2},{4,5},{5,4},{6,7},{7,6},{8,9},{9,8},{10,11... | collective-permute-start | bytes 3145736 | tf_op jit(solution)/shard_map/ppermute | solution.py:35
  8.6 4.3 %collective-permute-start.4 = (bf16[1024,512]{1,0:T(8,128)(2,1)S(1)}, bf16[1024,512]{1,0:T(8,128)(2,1)S(1)}, u32[]{:S(2)}, u32[]{:S(2)}) collective-permute-start(bf16[1024,512]{1,0:T(8,128)(2,1)S(1)} %get-tuple-element.56.wg), channel_id=1, source_target_pairs={{0,1},{1,0},{2,3},{3,2},{4,5},{5,4},{6,7},{7,6},{8,9},{9,8},{10,11... | collective-permute-start | bytes 3145736 | tf_op jit(solution)/shard_map/ppermute | solution.py:35
  8.7 10.7 %collective-permute-start.5 = (bf16[528,256]{1,0:T(8,128)(2,1)S(1)}, bf16[528,256]{1,0:T(8,128)(2,1)S(1)}, u32[]{:S(2)}, u32[]{:S(2)}) collective-permute-start(bf16[528,256]{1,0:T(8,128)(2,1)S(1)} %get-tuple-element.61.sent), channel_id=1, source_target_pairs={{0,8},{8,16},{16,24},{1,9},{9,17},{17,25},{2,10},{10,18},{18,26},{... | collective-permute-start | bytes 811016 | tf_op jit(solution)/shard_map/ppermute | solution.py:476
  10.1 12.0 %collective-permute-start.8 = (bf16[512,512]{1,0:T(8,128)(2,1)S(1)}, bf16[512,512]{1,0:T(8,128)(2,1)S(1)}, u32[]{:S(2)}, u32[]{:S(2)}) collective-permute-start(bf16[512,512]{1,0:T(8,128)(2,1)S(1)} %get-tuple-element.67), channel_id=1, source_target_pairs={{0,2},{1,5},{2,0},{3,7},{4,6},{5,1},{6,4},{7,3},{8,10},{9,13},{10,... | collective-permute-start | bytes 1572872 | tf_op jit(solution)/shard_map/ppermute | solution.py:432
  11.7 10.4 %collective-permute-start.7 = (bf16[528,256]{1,0:T(8,128)(2,1)S(1)}, bf16[528,256]{1,0:T(8,128)(2,1)S(1)}, u32[]{:S(2)}, u32[]{:S(2)}) collective-permute-start(bf16[528,256]{1,0:T(8,128)(2,1)S(1)} %get-tuple-element.61.sent), channel_id=1, source_target_pairs={{0,16},{16,0},{1,17},{17,1},{2,18},{18,2},{3,19},{19,3},{4,20},{20... | collective-permute-start | bytes 811016 | tf_op jit(solution)/shard_map/ppermute | solution.py:476
  12.4 20.3 %collective-permute-start.10 = (bf16[512,512]{1,0:T(8,128)(2,1)S(1)}, bf16[512,512]{1,0:T(8,128)(2,1)S(1)}, u32[]{:S(2)}, u32[]{:S(2)}) collective-permute-start(bf16[512,512]{1,0:T(8,128)(2,1)S(1)} %get-tuple-element.77), channel_id=1, source_target_pairs={{0,2},{1,5},{2,0},{3,7},{4,6},{5,1},{6,4},{7,3},{8,10},{9,13},{10,... | collective-permute-start | bytes 1572872 | tf_op jit(solution)/shard_map/ppermute | solution.py:432
  19.6 11.1 %collective-permute-start.6 = (bf16[512,256]{1,0:T(8,128)(2,1)S(1)}, bf16[512,256]{1,0:T(8,128)(2,1)S(1)}, u32[]{:S(2)}, u32[]{:S(2)}) collective-permute-start(bf16[512,256]{1,0:T(8,128)(2,1)S(1)} %get-tuple-element.63), channel_id=1, source_target_pairs={{8,24},{24,8},{9,25},{25,9},{10,26},{26,10},{11,27},{27,11},{12,28... | collective-permute-start | bytes 786440 | tf_op jit(solution)/shard_map/ppermute | solution.py:476
  32.7 6.0 %collective-permute-start.11 = (bf16[512,512]{1,0:T(8,128)(2,1)S(1)}, bf16[512,512]{1,0:T(8,128)(2,1)S(1)}, u32[]{:S(2)}, u32[]{:S(2)}) collective-permute-start(bf16[512,512]{1,0:T(8,128)(2,1)S(1)} %collective-permute-done.8.mine_0), channel_id=1, source_target_pairs={{0,1},{1,0},{2,3},{3,2},{4,5},{5,4},{6,7},{7,6},{8,9},{9,8},{10,11... | collective-permute-start | bytes 1572872 | tf_op jit(solution)/shard_map/ppermute | solution.py:35
  32.7 7.8 %collective-permute-start.12 = (bf16[512,512]{1,0:T(8,128)(2,1)S(1)}, bf16[512,512]{1,0:T(8,128)(2,1)S(1)}, u32[]{:S(2)}, u32[]{:S(2)}) collective-permute-start(bf16[512,512]{1,0:T(8,128)(2,1)S(1)} %collective-permute-done.10.mine_1), channel_id=1, source_target_pairs={{0,1},{1,0},{2,3},{3,2},{4,5},{5,4},{6,7},{7,6},{8,9},{9,8},{10,11... | collective-permute-start | bytes 1572872 | tf_op jit(solution)/shard_map/ppermute | solution.py:35
  33.2 8.9 %collective-permute-start.17 = (bf16[256,512]{1,0:T(8,128)(2,1)S(1)}, bf16[256,512]{1,0:T(8,128)(2,1)S(1)}, u32[]{:S(2)}, u32[]{:S(2)}) collective-permute-start(bf16[256,512]{1,0:T(8,128)(2,1)S(1)} %get-tuple-element.75.refs_3_), channel_id=1, source_target_pairs={{0,2},{1,5},{2,0},{3,7},{4,6},{5,1},{6,4},{7,3},{8,10},{9,13},{10,... | collective-permute-start | bytes 786440 | tf_op jit(solution)/shard_map/ppermute | solution.py:432
  34.7 9.5 %collective-permute-start.16 = (bf16[256,512]{1,0:T(8,128)(2,1)S(1)}, bf16[256,512]{1,0:T(8,128)(2,1)S(1)}, u32[]{:S(2)}, u32[]{:S(2)}) collective-permute-start(bf16[256,512]{1,0:T(8,128)(2,1)S(1)} %get-tuple-element.74.refs_2_), channel_id=1, source_target_pairs={{0,4},{1,3},{2,6},{3,1},{4,0},{5,7},{6,2},{7,5},{8,12},{9,11},{10,... | collective-permute-start | bytes 786440 | tf_op jit(solution)/shard_map/ppermute | solution.py:432
  38.1 9.6 %collective-permute-start.14 = (bf16[256,512]{1,0:T(8,128)(2,1)S(1)}, bf16[256,512]{1,0:T(8,128)(2,1)S(1)}, u32[]{:S(2)}, u32[]{:S(2)}) collective-permute-start(bf16[256,512]{1,0:T(8,128)(2,1)S(1)} %get-tuple-element.73.refs_1_), channel_id=1, source_target_pairs={{0,2},{1,5},{2,0},{3,7},{4,6},{5,1},{6,4},{7,3},{8,10},{9,13},{10,... | collective-permute-start | bytes 786440 | tf_op jit(solution)/shard_map/ppermute | solution.py:432
  38.7 11.2 %collective-permute-start.9 = (bf16[256,512]{1,0:T(8,128)(2,1)S(1)}, bf16[256,512]{1,0:T(8,128)(2,1)S(1)}, u32[]{:S(2)}, u32[]{:S(2)}) collective-permute-start(bf16[256,512]{1,0:T(8,128)(2,1)S(1)} %get-tuple-element.72.refs_0_), channel_id=1, source_target_pairs={{0,4},{1,3},{2,6},{3,1},{4,0},{5,7},{6,2},{7,5},{8,12},{9,11},{10,... | collective-permute-start | bytes 786440 | tf_op jit(solution)/shard_map/ppermute | solution.py:432
  42.4 11.5 %collective-permute-start.19 = (bf16[256,512]{1,0:T(8,128)(2,1)S(1)}, bf16[256,512]{1,0:T(8,128)(2,1)S(1)}, u32[]{:S(2)}, u32[]{:S(2)}) collective-permute-start(bf16[256,512]{1,0:T(8,128)(2,1)S(1)} %give.7), channel_id=1, source_target_pairs={{0,4},{1,3},{2,6},{3,1},{4,0},{5,7},{6,2},{7,5},{8,12},{9,11},{10,... | collective-permute-start | bytes 786440 | tf_op jit(solution)/shard_map/ppermute | solution.py:432
  44.5 9.4 %collective-permute-start.18 = (bf16[256,512]{1,0:T(8,128)(2,1)S(1)}, bf16[256,512]{1,0:T(8,128)(2,1)S(1)}, u32[]{:S(2)}, u32[]{:S(2)}) collective-permute-start(bf16[256,512]{1,0:T(8,128)(2,1)S(1)} %give.6), channel_id=1, source_target_pairs={{0,2},{1,5},{2,0},{3,7},{4,6},{5,1},{6,4},{7,3},{8,10},{9,13},{10,... | collective-permute-start | bytes 786440 | tf_op jit(solution)/shard_map/ppermute | solution.py:432
  48.0 10.2 %collective-permute-start.15 = (bf16[256,512]{1,0:T(8,128)(2,1)S(1)}, bf16[256,512]{1,0:T(8,128)(2,1)S(1)}, u32[]{:S(2)}, u32[]{:S(2)}) collective-permute-start(bf16[256,512]{1,0:T(8,128)(2,1)S(1)} %give.5), channel_id=1, source_target_pairs={{0,4},{1,3},{2,6},{3,1},{4,0},{5,7},{6,2},{7,5},{8,12},{9,11},{10,... | collective-permute-start | bytes 786440 | tf_op jit(solution)/shard_map/ppermute | solution.py:432
  50.1 9.1 %collective-permute-start.13 = (bf16[256,512]{1,0:T(8,128)(2,1)S(1)}, bf16[256,512]{1,0:T(8,128)(2,1)S(1)}, u32[]{:S(2)}, u32[]{:S(2)}) collective-permute-start(bf16[256,512]{1,0:T(8,128)(2,1)S(1)} %give.4), channel_id=1, source_target_pairs={{0,2},{1,5},{2,0},{3,7},{4,6},{5,1},{6,4},{7,3},{8,10},{9,13},{10,... | collective-permute-start | bytes 786440 | tf_op jit(solution)/shard_map/ppermute | solution.py:432

commit v19 on v18

--- a/solution.py
+++ b/solution.py
@@ -308,32 +308,29 @@
             intra_out[low:last, span] = mm((scores * weights).astype(BF16), v[start : start + last, span])
 
 
-def hidden_kernel(heads, hop, sets, starts, decay, before, entering, *refs):
-    arrivals, refs, token = refs[: len(sets)], refs[len(sets) : -1], refs[-1]
-    projected, outs = refs[: -len(starts)], refs[-len(starts) :]
+def hidden_kernel(heads, hop, sets, role, first, decay, before, entering, *refs):
+    arrivals, projected, out, token = refs[: len(sets)], refs[len(sets) : -2], refs[-2], refs[-1]
     token[...] = jnp.zeros_like(token)
-    core = lax.axis_index("fsdp")
-    for head in range(heads):
-        span = slice(head * DH, (head + 1) * DH)
-        entering_log = entering[heads * DH + head : heads * DH + head + 1, :1]
-        state = entering[span, :] + jnp.exp(entering_log) * arrived_state(arrivals, sets, hop, span)
-        pieces = []
-        for start in starts:
-            block = start // BLOCK
-            q, gate, intra = projected[3 * block : 3 * block + 3]
-            at = slice(start % BLOCK, start % BLOCK + TILE)
-            column = jnp.exp(decay[:, start : start + TILE].T[:, head : head + 1])
-            scale_log = jnp.zeros((1, 1), F32)
-            for earlier in range(block):
-                end = (earlier + 1) * BLOCK
-                scale_log = scale_log + decay[head : head + 1, end - 1 : end]
-            prior = (jnp.exp(scale_log) * state + before[block, span, :].astype(F32)).astype(BF16)
-            retained = intra[at, span] + column * mm(q[at, span], prior)
+
+    def piece(start):
+        block = start // BLOCK
+        q, gate, intra = projected[3 * block : 3 * block + 3]
+        at = slice(start % BLOCK, start % BLOCK + TILE)
+        columns = jnp.exp(decay[:, start : start + TILE].T)
+        scales = jnp.exp(block_ends(decay, 0, block * BLOCK))
+        for head in range(heads):
+            span, row = slice(head * DH, (head + 1) * DH), slice(head, head + 1)
+            fade = jnp.exp(entering[heads * DH + head : heads * DH + head + 1, :1])
+            state = entering[span, :] + fade * arrived_state(arrivals, sets, hop, span)
+            prior = (scales[row] * state + before[block, span, :].astype(F32)).astype(BF16)
+            retained = intra[at, span] + columns[:, row] * mm(q[at, span], prior)
             center = retained - jnp.mean(retained, axis=1, keepdims=True)
             spread = jnp.mean(center * center, axis=1, keepdims=True)
-            pieces.append((gate[at, span] * center * lax.rsqrt(spread + 1e-5)).astype(BF16))
-        for role, out in enumerate(outs):
-            out[:, span] = jnp.where(core == 0, pieces[role], pieces[1 - role])
+            out[:, span] = (gate[at, span] * center * lax.rsqrt(spread + 1e-5)).astype(BF16)
+
+    core, middle = lax.axis_index("fsdp"), decay.shape[1] // 2
+    pl.when(core == role)(lambda: piece(first))
+    pl.when(core != role)(lambda: piece(middle + first))
 
 
 def columns_kernel(first, second, *outs):
@@ -514,19 +511,19 @@
 
     count = rows // 2 // TILE
     hidden, far = [[], []], [[], []]
-    for number in range(count):
-        held = after(decay, swap(pair[2], "fsdp", 1)) if number else decay
-        pair = kernel_call(
-            functools.partial(hidden_kernel, heads, hop, sets, [(half * count + number) * TILE for half in range(2)]),
-            [((TILE, cols), BF16)] * 2 + [((16, 128), BF16)],
+    token = None
+    for number, role in [(number, role) for number in range(count) for role in range(2)]:
+        held = decay if token is None else after(decay, swap(token, "fsdp", 1))
+        piece, token = kernel_call(
+            functools.partial(hidden_kernel, heads, hop, sets, role, number * TILE),
+            [((TILE, cols), BF16), ((16, 128), BF16)],
             [held, before, entering, *arrivals, *projected],
             "hidden",
         )
-        if number == 0:
-            out_other = [swap(after(block, pair[0]), "fsdp", 1) for block in out_mine]
-        for role in range(2):
-            hidden[role].append(pair[role])
-            far[role].append(trade(pair[role], role))
+        if number == 0 and role == 0:
+            out_other = [swap(after(block, piece), "fsdp", 1) for block in out_mine]
+        hidden[role].append(piece)
+        far[role].append(trade(piece, role))
     weights = kernel_call(
         arrange_kernel,
         [((cols, 2 * cols), BF16)] * 2,

time: 60.5 us -> 60 us (level)
  starting transfers between devices: 19.1 us -> 17.6 us
  Pallas kernels: 23 us -> 24 us
    ppermute x10, starting transfers between devices: 13 us -> 11.6 us  [trade(): return lax.ppermute(value, ('tp', 'fsdp'), partners[role])]
    pallas_call x13 -> x15, Pallas kernels: 13.8 us -> 14.8 us  [kernel_call(): pl.pallas_call(kernel, in_specs=[pl.BlockSpec(memory_space=pltpu.VMEM)] *...]
  transfers between devices with their start and end apart: 20 -> 20, of which waited for: 7 -> 7; matrix products, arithmetic and copies ran while one was open for 0% -> 0% of each run, Pallas kernels for 37% -> 39%
where the time goes in v19:
time: 60 us; the launch traced here: 59.6 us
  Pallas kernels  24 us (40%)
  starting transfers between devices  17.6 us (29%)
  waiting for transfers between devices  17.6 us (29%)
    pallas_call x15, Pallas kernels, kernel_call(): pl.pallas_call(kernel, in_specs=[pl.BlockSpec(memory_space=pltpu.VMEM)] *...  14.8 us
    ppermute x10, starting transfers between devices, trade(): return lax.ppermute(value, ('tp', 'fsdp'), partners[role])  11.6 us
    ppermute x3, waiting for transfers between devices, exchange(): return lax.ppermute(message, 'ctx', pairs)  9.12 us
    ppermute x10, waiting for transfers between devices, trade(): return lax.ppermute(value, ('tp', 'fsdp'), partners[role])  8.47 us
    pallas_call x2, Pallas kernels, loading_call(): pl.pallas_call(kernel, in_specs=[pl.BlockSpec(memory_space=pltpu.HBM)] *...  7.53 us
    ppermute x3, starting transfers between devices, exchange(): return lax.ppermute(message, 'ctx', pairs)  4.23 us
    ppermute x7, starting transfers between devices, swap(): lax.ppermute(value, axis, [(place, place ^ mask) for place in range(size)])  1.71 us
    pallas_call x2, Pallas kernels, on_device(): pl.pallas_call(functools.partial(finish_kernel, part_order), in_specs=[pl...  1.7 us
  transfers between devices with their start and end apart: 20, of which 7 were waited for; matrix products, arithmetic and copies ran while one was open for 0% of the time, Pallas kernels for 39%

profile of v19, /device:TPU:24, one launch (start us, length us, event | category | flops | bytes accessed | tf_op | source)
XLA Modules:
  0.0 59.6 jit_solution(17551524048728518391)
XLA Ops:
  0.0 0.5 collective-permute-start.2
  0.5 4.3 %key_value_own.1 = (bf16[1024,1024]{1,0:T(8,128)(2,1)S(1)}, bf16[1024,1024]{1,0:T(8,128)(2,1)S(1)}, f32[1024,512]{1,0:T(8,128)S(1)}, f32[1024,512]{1,0:T(8,128)S...) custom-call(bf16[1024,2048]{1,0:T(8,128)(2,1)} %bitcast.4, ...), custom_call_target="tpu_custom_call" | custom-call | flops 1 | bytes 1 | tf_op jit(solution)/shard_map/key_value_own/pallas_call | solution.py:56
  4.9 3.2 %key_value.1 = (bf16[1024,512]{1,0:T(8,128)(2,1)S(1)}, bf16[1024,512]{1,0:T(8,128)(2,1)S(1)}, bf16[1024,512]{1,0:T(8,128)(2,1)S(1)}, bf16[1024,512]{1,0:T(8,128)...) custom-call(bf16[1024,512]{1,0:T(8,128)(2,1)} %wq_far.1, ...), custom_call_target="tpu_custom_call" | custom-call | flops 1 | bytes 1 | tf_op jit(solution)/shard_map/key_value/pallas_call | solution.py:56
  8.2 0.5 collective-permute-start.3
  8.8 1.3 %collective-permute-start.5 = (bf16[528,256]{1,0:T(8,128)(2,1)S(1)}, bf16[528,256]{1,0:T(8,128)(2,1)S(1)}, u32[]{:S(2)}, u32[]{:S(2)}) collective-permute-start(bf16[528,256]{1,0:T(8,128)(2,1)S(1)} %get-tuple-element.61.sent), channel_id=1, source_target_pairs={{0,8},{8,16},{16,24},{1,9},{9,17},{17,25},{2,10},{10,18},{18,26},{... | collective-permute-start | bytes 811016 | tf_op jit(solution)/shard_map/ppermute | solution.py:473
  10.2 1.6 %collective-permute-start.8 = (bf16[512,512]{1,0:T(8,128)(2,1)S(1)}, bf16[512,512]{1,0:T(8,128)(2,1)S(1)}, u32[]{:S(2)}, u32[]{:S(2)}) collective-permute-start(bf16[512,512]{1,0:T(8,128)(2,1)S(1)} %get-tuple-element.67), channel_id=1, source_target_pairs={{0,2},{1,5},{2,0},{3,7},{4,6},{5,1},{6,4},{7,3},{8,10},{9,13},{10,... | collective-permute-start | bytes 1572872 | tf_op jit(solution)/shard_map/ppermute | solution.py:429
  11.7 0.7 %collective-permute-start.7 = (bf16[528,256]{1,0:T(8,128)(2,1)S(1)}, bf16[528,256]{1,0:T(8,128)(2,1)S(1)}, u32[]{:S(2)}, u32[]{:S(2)}) collective-permute-start(bf16[528,256]{1,0:T(8,128)(2,1)S(1)} %get-tuple-element.61.sent), channel_id=1, source_target_pairs={{0,16},{16,0},{1,17},{17,1},{2,18},{18,2},{3,19},{19,3},{4,20},{20... | collective-permute-start | bytes 811016 | tf_op jit(solution)/shard_map/ppermute | solution.py:473
  12.4 0.6 collective-permute-start.10
  13.0 3.1 %query_gate.2 = (bf16[512,512]{1,0:T(8,128)(2,1)S(1)}, f32[512,512]{1,0:T(8,128)S(1)}, f32[512,512]{1,0:T(8,128)S(1)}) custom-call(bf16[1024,1024]{1,0:T(8,128)(2,1)S(1)} %get-tuple-element.54.x_own, bf16[1024,1024]{1,0:T(8,128)(2,1)S(1)} %get-tuple-element.47.x.x_other, bf16[1024,512]{1,0:T(8,128)(2,1)S(1)} %get-tuple-element.55.wq, ...), custom_call_target="tpu_custom_call" | custom-call | flops 1 | bytes 1 | tf_op jit(solution)/shard_map/query_gate/pallas_call | solution.py:40
  16.1 3.4 %collective-permute-done.5.refs_0_ = bf16[528,256]{1,0:T(8,128)(2,1)S(1)} collective-permute-done((bf16[528,256]{1,0:T(8,128)(2,1)S(1)}, bf16[528,256]{1,0:T(8,128)(2,1)S(1)}, u32[]{:S(2)}, u32[]{:S(2)}) %collective-permute-start.5) | collective-permute-done | bytes 270368 | tf_op jit(solution)/shard_map/ppermute | solution.py:473
  19.7 2.3 %collective-permute-start.6 = (bf16[512,256]{1,0:T(8,128)(2,1)S(1)}, bf16[512,256]{1,0:T(8,128)(2,1)S(1)}, u32[]{:S(2)}, u32[]{:S(2)}) collective-permute-start(bf16[512,256]{1,0:T(8,128)(2,1)S(1)} %get-tuple-element.63), channel_id=1, source_target_pairs={{8,24},{24,8},{9,25},{25,9},{10,26},{26,10},{11,27},{27,11},{12,28... | collective-permute-start | bytes 786440 | tf_op jit(solution)/shard_map/ppermute | solution.py:473
  22.0 3.1 %query_gate.3 = (bf16[512,512]{1,0:T(8,128)(2,1)S(1)}, f32[512,512]{1,0:T(8,128)S(1)}, f32[512,512]{1,0:T(8,128)S(1)}) custom-call(bf16[1024,1024]{1,0:T(8,128)(2,1)S(1)} %get-tuple-element.54.x_own, bf16[1024,1024]{1,0:T(8,128)(2,1)S(1)} %get-tuple-element.47.x.x_other, bf16[1024,512]{1,0:T(8,128)(2,1)S(1)} %get-tuple-element.55.wq, ...), custom_call_target="tpu_custom_call" | custom-call | flops 1 | bytes 1 | tf_op jit(solution)/shard_map/query_gate/pallas_call | solution.py:40
  25.1 5.7 %collective-permute-done.6.refs_0_ = bf16[512,256]{1,0:T(8,128)(2,1)S(1)} collective-permute-done((bf16[512,256]{1,0:T(8,128)(2,1)S(1)}, bf16[512,256]{1,0:T(8,128)(2,1)S(1)}, u32[]{:S(2)}, u32[]{:S(2)}) %collective-permute-start.6) | collective-permute-done | bytes 262176 | tf_op jit(solution)/shard_map/ppermute | solution.py:473
  30.8 1.2 %hidden.7 = (bf16[256,512]{1,0:T(8,128)(2,1)S(1)}, bf16[16,128]{1,0:T(8,128)(2,1)}) custom-call(f32[8,1024]{1,0:T(8,128)S(1)} %get-tuple-element.68.decay, bf16[2,512,256]{2,1,0:T(8,128)(2,1)S(1)} %get-tuple-element.52.before, f32[520,256]{1,0:T(8,128)S(1)} %get-tuple-element.62.entering, bf16[512,256]{1,0:T(8,128)(2,1)S(1)} %collective-permute-done.6.refs_0_, ...), custom_call_target="tpu_custom_call" | custom-call | flops 1 | bytes 1 | tf_op jit(solution)/shard_map/hidden/pallas_call | solution.py:40
  32.0 0.5 collective-permute-start.12
  32.5 1.5 %collective-permute-start.17 = (bf16[256,512]{1,0:T(8,128)(2,1)S(1)}, bf16[256,512]{1,0:T(8,128)(2,1)S(1)}, u32[]{:S(2)}, u32[]{:S(2)}) collective-permute-start(bf16[256,512]{1,0:T(8,128)(2,1)S(1)} %get-tuple-element.75.refs_3_), channel_id=1, source_target_pairs={{0,2},{1,5},{2,0},{3,7},{4,6},{5,1},{6,4},{7,3},{8,10},{9,13},{10,... | collective-permute-start | bytes 786440 | tf_op jit(solution)/shard_map/ppermute | solution.py:429
  34.0 1.2 %hidden.6 = (bf16[256,512]{1,0:T(8,128)(2,1)S(1)}, bf16[16,128]{1,0:T(8,128)(2,1)}) custom-call(f32[8,1024]{1,0:T(8,128)S(1)} %get-tuple-element.68.decay, bf16[2,512,256]{2,1,0:T(8,128)(2,1)S(1)} %get-tuple-element.52.before, f32[520,256]{1,0:T(8,128)S(1)} %get-tuple-element.62.entering, bf16[512,256]{1,0:T(8,128)(2,1)S(1)} %collective-permute-done.6.refs_0_, ...), custom_call_target="tpu_custom_call" | custom-call | flops 1 | bytes 1 | tf_op jit(solution)/shard_map/hidden/pallas_call | solution.py:40
  35.2 1.5 %collective-permute-start.16 = (bf16[256,512]{1,0:T(8,128)(2,1)S(1)}, bf16[256,512]{1,0:T(8,128)(2,1)S(1)}, u32[]{:S(2)}, u32[]{:S(2)}) collective-permute-start(bf16[256,512]{1,0:T(8,128)(2,1)S(1)} %get-tuple-element.74.refs_2_), channel_id=1, source_target_pairs={{0,4},{1,3},{2,6},{3,1},{4,0},{5,7},{6,2},{7,5},{8,12},{9,11},{10,... | collective-permute-start | bytes 786440 | tf_op jit(solution)/shard_map/ppermute | solution.py:429
  36.8 1.2 %hidden.5 = (bf16[256,512]{1,0:T(8,128)(2,1)S(1)}, bf16[16,128]{1,0:T(8,128)(2,1)}) custom-call(f32[8,1024]{1,0:T(8,128)S(1)} %get-tuple-element.68.decay, bf16[2,512,256]{2,1,0:T(8,128)(2,1)S(1)} %get-tuple-element.52.before, f32[520,256]{1,0:T(8,128)S(1)} %get-tuple-element.62.entering, bf16[512,256]{1,0:T(8,128)(2,1)S(1)} %collective-permute-done.6.refs_0_, ...), custom_call_target="tpu_custom_call" | custom-call | flops 1 | bytes 1 | tf_op jit(solution)/shard_map/hidden/pallas_call | solution.py:40
  38.0 0.5 collective-permute-start.14
  38.5 1.2 %hidden.4 = (bf16[256,512]{1,0:T(8,128)(2,1)S(1)}, bf16[16,128]{1,0:T(8,128)(2,1)}) custom-call(f32[8,1024]{1,0:T(8,128)S(1)} %get-tuple-element.68.decay, bf16[2,512,256]{2,1,0:T(8,128)(2,1)S(1)} %get-tuple-element.52.before, f32[520,256]{1,0:T(8,128)S(1)} %get-tuple-element.62.entering, bf16[512,256]{1,0:T(8,128)(2,1)S(1)} %collective-permute-done.6.refs_0_, ...), custom_call_target="tpu_custom_call" | custom-call | flops 1 | bytes 1 | tf_op jit(solution)/shard_map/hidden/pallas_call | solution.py:40
  40.2 1.3 %own_products.1 = (f32[512,1024]{1,0:T(8,128)S(1)}, f32[512,1024]{1,0:T(8,128)S(1)}) custom-call(bf16[512,1024]{1,0:T(8,128)(2,1)S(1)} %get-tuple-element.66.first.own_first, bf16[512,1024]{1,0:T(8,128)(2,1)S(1)} %collective-permute-done.second.own_second, bf16[256,512]{1,0:T(8,128)(2,1)S(1)} %get-tuple-element.72.refs_0_, ...), custom_call_target="tpu_custom_call" | custom-call | flops 1 | bytes 1 | tf_op jit(solution)/shard_map/own_products/pallas_call | solution.py:40
  42.2 1.6 %collective-permute-start.19 = (bf16[256,512]{1,0:T(8,128)(2,1)S(1)}, bf16[256,512]{1,0:T(8,128)(2,1)S(1)}, u32[]{:S(2)}, u32[]{:S(2)}) collective-permute-start(bf16[256,512]{1,0:T(8,128)(2,1)S(1)} %give.7), channel_id=1, source_target_pairs={{0,4},{1,3},{2,6},{3,1},{4,0},{5,7},{6,2},{7,5},{8,12},{9,11},{10,... | collective-permute-start | bytes 786440 | tf_op jit(solution)/shard_map/ppermute | solution.py:429
  44.1 1.6 %collective-permute-start.18 = (bf16[256,512]{1,0:T(8,128)(2,1)S(1)}, bf16[256,512]{1,0:T(8,128)(2,1)S(1)}, u32[]{:S(2)}, u32[]{:S(2)}) collective-permute-start(bf16[256,512]{1,0:T(8,128)(2,1)S(1)} %give.6), channel_id=1, source_target_pairs={{0,2},{1,5},{2,0},{3,7},{4,6},{5,1},{6,4},{7,3},{8,10},{9,13},{10,... | collective-permute-start | bytes 786440 | tf_op jit(solution)/shard_map/ppermute | solution.py:429
  45.6 1.6 %collective-permute-done.14.far.refs_1_ = bf16[256,512]{1,0:T(8,128)(2,1)S(1)} collective-permute-done((bf16[256,512]{1,0:T(8,128)(2,1)S(1)}, bf16[256,512]{1,0:T(8,128)(2,1)S(1)}, u32[]{:S(2)}, u32[]{:S(2)}) %collective-permute-start.14) | collective-permute-done | bytes 262176 | tf_op jit(solution)/shard_map/ppermute | solution.py:429
  47.5 1.1 %collective-permute-start.15 = (bf16[256,512]{1,0:T(8,128)(2,1)S(1)}, bf16[256,512]{1,0:T(8,128)(2,1)S(1)}, u32[]{:S(2)}, u32[]{:S(2)}) collective-permute-start(bf16[256,512]{1,0:T(8,128)(2,1)S(1)} %give.5), channel_id=1, source_target_pairs={{0,4},{1,3},{2,6},{3,1},{4,0},{5,7},{6,2},{7,5},{8,12},{9,11},{10,... | collective-permute-start | bytes 786440 | tf_op jit(solution)/shard_map/ppermute | solution.py:429
  49.3 1.2 %collective-permute-start.13 = (bf16[256,512]{1,0:T(8,128)(2,1)S(1)}, bf16[256,512]{1,0:T(8,128)(2,1)S(1)}, u32[]{:S(2)}, u32[]{:S(2)}) collective-permute-start(bf16[256,512]{1,0:T(8,128)(2,1)S(1)} %give.4), channel_id=1, source_target_pairs={{0,2},{1,5},{2,0},{3,7},{4,6},{5,1},{6,4},{7,3},{8,10},{9,13},{10,... | collective-permute-start | bytes 786440 | tf_op jit(solution)/shard_map/ppermute | solution.py:429
  50.5 0.7 %keep.1 = (f32[512,512]{1,0:T(8,128)S(1)}, f32[512,512]{1,0:T(8,128)S(1)}) custom-call(bf16[256,512]{1,0:T(8,128)(2,1)S(1)} %collective-permute-done.9.far.refs_0_, bf16[256,512]{1,0:T(8,128)(2,1)S(1)} %collective-permute-done.14.far.refs_1_, bf16[256,512]{1,0:T(8,128)(2,1)S(1)} %collective-permute-done.16.refs_2_.far, ...), custom_call_target="tpu_custom_call" | custom-call | flops 1 | bytes 1 | tf_op jit(solution)/shard_map/keep/pallas_call | solution.py:40
  51.2 3.4 %collective-permute-done.19.refs_1_ = bf16[256,512]{1,0:T(8,128)(2,1)S(1)} collective-permute-done((bf16[256,512]{1,0:T(8,128)(2,1)S(1)}, bf16[256,512]{1,0:T(8,128)(2,1)S(1)}, u32[]{:S(2)}, u32[]{:S(2)}) %collective-permute-start.19) | collective-permute-done | bytes 262176 | tf_op jit(solution)/shard_map/ppermute | solution.py:429
  54.6 0.9 %finish.2.refs_4_ = bf16[1,1024,512]{2,1,0:T(8,128)(2,1)} custom-call(bf16[256,512]{1,0:T(8,128)(2,1)S(1)} %collective-permute-done.18.refs_0_, bf16[256,512]{1,0:T(8,128)(2,1)S(1)} %collective-permute-done.19.refs_1_, f32[512,512]{1,0:T(8,128)S(1)} %get-tuple-element.83.refs_2_, f32[512,512]{1,0:T(8,128)S(1)} %get-tuple-element.84.refs_3_), custom_call_target="tpu_custom_call" | custom-call | tf_op jit(solution)/shard_map/finish/pallas_call | solution.py:559
  55.5 3.0 %collective-permute-done.15.refs_1_ = bf16[256,512]{1,0:T(8,128)(2,1)S(1)} collective-permute-done((bf16[256,512]{1,0:T(8,128)(2,1)S(1)}, bf16[256,512]{1,0:T(8,128)(2,1)S(1)}, u32[]{:S(2)}, u32[]{:S(2)}) %collective-permute-start.15) | collective-permute-done | bytes 262176 | tf_op jit(solution)/shard_map/ppermute | solution.py:429
  58.5 0.9 %finish.3 = bf16[1,1024,512]{2,1,0:T(8,128)(2,1)} custom-call(bf16[256,512]{1,0:T(8,128)(2,1)S(1)} %collective-permute-done.13.refs_0_, bf16[256,512]{1,0:T(8,128)(2,1)S(1)} %collective-permute-done.15.refs_1_, f32[512,512]{1,0:T(8,128)S(1)} %get-tuple-element.83.refs_2_, f32[512,512]{1,0:T(8,128)S(1)} %get-tuple-element.84.refs_3_, ...), custom_call_target="tpu_custom_call", output_to_operand_aliasing={{}: (4, {})} | custom-call | tf_op jit(solution)/shard_map/finish/pallas_call | solution.py:559
  (27 shorter events, 2.9 us)
Async XLA Ops:
  0.0 4.9 %collective-permute-start.1 = (bf16[1024,512]{1,0:T(8,128)(2,1)}, bf16[1024,512]{1,0:T(8,128)(2,1)S(1)}, u32[]{:S(2)}, u32[]{:S(2)}) collective-permute-start(bf16[1024,512]{1,0:T(8,128)(2,1)} %wk_far.1), channel_id=1, source_target_pairs={{0,1},{1,0},{2,3},{3,2},{4,5},{5,4},{6,7},{7,6},{8,9},{9,8},{10,11... | collective-permute-start | bytes 3145736 | tf_op jit(solution)/shard_map/ppermute | solution.py:35
  0.0 4.9 %collective-permute-start.2 = (bf16[1024,512]{1,0:T(8,128)(2,1)}, bf16[1024,512]{1,0:T(8,128)(2,1)S(1)}, u32[]{:S(2)}, u32[]{:S(2)}) collective-permute-start(bf16[1024,512]{1,0:T(8,128)(2,1)} %wv_far.1), channel_id=1, source_target_pairs={{0,1},{1,0},{2,3},{3,2},{4,5},{5,4},{6,7},{7,6},{8,9},{9,8},{10,11... | collective-permute-start | bytes 3145736 | tf_op jit(solution)/shard_map/ppermute | solution.py:35
  4.8 5.2 %collective-permute-start = (bf16[512,1024]{1,0:T(8,128)(2,1)S(1)}, bf16[512,1024]{1,0:T(8,128)(2,1)S(1)}, u32[]{:S(2)}, u32[]{:S(2)}) collective-permute-start(bf16[512,1024]{1,0:T(8,128)(2,1)S(1)} %get-tuple-element.66.first.own_first), channel_id=1, source_target_pairs={{0,1},{1,0},{2,3},{3,2},{4,5},{5,4},{6,7},{7,6},{8,9},{9,8},{10,11... | collective-permute-start | bytes 3145736 | tf_op jit(solution)/shard_map/ppermute | solution.py:35
  8.2 4.3 %collective-permute-start.3 = (bf16[1024,512]{1,0:T(8,128)(2,1)S(1)}, bf16[1024,512]{1,0:T(8,128)(2,1)S(1)}, u32[]{:S(2)}, u32[]{:S(2)}) collective-permute-start(bf16[1024,512]{1,0:T(8,128)(2,1)S(1)} %get-tuple-element.55.wq), channel_id=1, source_target_pairs={{0,1},{1,0},{2,3},{3,2},{4,5},{5,4},{6,7},{7,6},{8,9},{9,8},{10,11... | collective-permute-start | bytes 3145736 | tf_op jit(solution)/shard_map/ppermute | solution.py:35
  8.7 4.3 %collective-permute-start.4 = (bf16[1024,512]{1,0:T(8,128)(2,1)S(1)}, bf16[1024,512]{1,0:T(8,128)(2,1)S(1)}, u32[]{:S(2)}, u32[]{:S(2)}) collective-permute-start(bf16[1024,512]{1,0:T(8,128)(2,1)S(1)} %get-tuple-element.56.wg), channel_id=1, source_target_pairs={{0,1},{1,0},{2,3},{3,2},{4,5},{5,4},{6,7},{7,6},{8,9},{9,8},{10,11... | collective-permute-start | bytes 3145736 | tf_op jit(solution)/shard_map/ppermute | solution.py:35
  8.8 10.7 %collective-permute-start.5 = (bf16[528,256]{1,0:T(8,128)(2,1)S(1)}, bf16[528,256]{1,0:T(8,128)(2,1)S(1)}, u32[]{:S(2)}, u32[]{:S(2)}) collective-permute-start(bf16[528,256]{1,0:T(8,128)(2,1)S(1)} %get-tuple-element.61.sent), channel_id=1, source_target_pairs={{0,8},{8,16},{16,24},{1,9},{9,17},{17,25},{2,10},{10,18},{18,26},{... | collective-permute-start | bytes 811016 | tf_op jit(solution)/shard_map/ppermute | solution.py:473
  10.2 11.8 %collective-permute-start.8 = (bf16[512,512]{1,0:T(8,128)(2,1)S(1)}, bf16[512,512]{1,0:T(8,128)(2,1)S(1)}, u32[]{:S(2)}, u32[]{:S(2)}) collective-permute-start(bf16[512,512]{1,0:T(8,128)(2,1)S(1)} %get-tuple-element.67), channel_id=1, source_target_pairs={{0,2},{1,5},{2,0},{3,7},{4,6},{5,1},{6,4},{7,3},{8,10},{9,13},{10,... | collective-permute-start | bytes 1572872 | tf_op jit(solution)/shard_map/ppermute | solution.py:429
  11.7 10.2 %collective-permute-start.7 = (bf16[528,256]{1,0:T(8,128)(2,1)S(1)}, bf16[528,256]{1,0:T(8,128)(2,1)S(1)}, u32[]{:S(2)}, u32[]{:S(2)}) collective-permute-start(bf16[528,256]{1,0:T(8,128)(2,1)S(1)} %get-tuple-element.61.sent), channel_id=1, source_target_pairs={{0,16},{16,0},{1,17},{17,1},{2,18},{18,2},{3,19},{19,3},{4,20},{20... | collective-permute-start | bytes 811016 | tf_op jit(solution)/shard_map/ppermute | solution.py:473
  12.4 19.6 %collective-permute-start.10 = (bf16[512,512]{1,0:T(8,128)(2,1)S(1)}, bf16[512,512]{1,0:T(8,128)(2,1)S(1)}, u32[]{:S(2)}, u32[]{:S(2)}) collective-permute-start(bf16[512,512]{1,0:T(8,128)(2,1)S(1)} %get-tuple-element.77), channel_id=1, source_target_pairs={{0,2},{1,5},{2,0},{3,7},{4,6},{5,1},{6,4},{7,3},{8,10},{9,13},{10,... | collective-permute-start | bytes 1572872 | tf_op jit(solution)/shard_map/ppermute | solution.py:429
  19.7 11.1 %collective-permute-start.6 = (bf16[512,256]{1,0:T(8,128)(2,1)S(1)}, bf16[512,256]{1,0:T(8,128)(2,1)S(1)}, u32[]{:S(2)}, u32[]{:S(2)}) collective-permute-start(bf16[512,256]{1,0:T(8,128)(2,1)S(1)} %get-tuple-element.63), channel_id=1, source_target_pairs={{8,24},{24,8},{9,25},{25,9},{10,26},{26,10},{11,27},{27,11},{12,28... | collective-permute-start | bytes 786440 | tf_op jit(solution)/shard_map/ppermute | solution.py:473
  32.0 7.7 %collective-permute-start.11 = (bf16[512,512]{1,0:T(8,128)(2,1)S(1)}, bf16[512,512]{1,0:T(8,128)(2,1)S(1)}, u32[]{:S(2)}, u32[]{:S(2)}) collective-permute-start(bf16[512,512]{1,0:T(8,128)(2,1)S(1)} %collective-permute-done.8.mine_0), channel_id=1, source_target_pairs={{0,1},{1,0},{2,3},{3,2},{4,5},{5,4},{6,7},{7,6},{8,9},{9,8},{10,11... | collective-permute-start | bytes 1572872 | tf_op jit(solution)/shard_map/ppermute | solution.py:35
  32.0 9.6 %collective-permute-start.12 = (bf16[512,512]{1,0:T(8,128)(2,1)S(1)}, bf16[512,512]{1,0:T(8,128)(2,1)S(1)}, u32[]{:S(2)}, u32[]{:S(2)}) collective-permute-start(bf16[512,512]{1,0:T(8,128)(2,1)S(1)} %collective-permute-done.10.mine_1), channel_id=1, source_target_pairs={{0,1},{1,0},{2,3},{3,2},{4,5},{5,4},{6,7},{7,6},{8,9},{9,8},{10,11... | collective-permute-start | bytes 1572872 | tf_op jit(solution)/shard_map/ppermute | solution.py:35
  32.5 9.3 %collective-permute-start.17 = (bf16[256,512]{1,0:T(8,128)(2,1)S(1)}, bf16[256,512]{1,0:T(8,128)(2,1)S(1)}, u32[]{:S(2)}, u32[]{:S(2)}) collective-permute-start(bf16[256,512]{1,0:T(8,128)(2,1)S(1)} %get-tuple-element.75.refs_3_), channel_id=1, source_target_pairs={{0,2},{1,5},{2,0},{3,7},{4,6},{5,1},{6,4},{7,3},{8,10},{9,13},{10,... | collective-permute-start | bytes 786440 | tf_op jit(solution)/shard_map/ppermute | solution.py:429
  35.2 8.5 %collective-permute-start.16 = (bf16[256,512]{1,0:T(8,128)(2,1)S(1)}, bf16[256,512]{1,0:T(8,128)(2,1)S(1)}, u32[]{:S(2)}, u32[]{:S(2)}) collective-permute-start(bf16[256,512]{1,0:T(8,128)(2,1)S(1)} %get-tuple-element.74.refs_2_), channel_id=1, source_target_pairs={{0,4},{1,3},{2,6},{3,1},{4,0},{5,7},{6,2},{7,5},{8,12},{9,11},{10,... | collective-permute-start | bytes 786440 | tf_op jit(solution)/shard_map/ppermute | solution.py:429
  38.0 9.2 %collective-permute-start.14 = (bf16[256,512]{1,0:T(8,128)(2,1)S(1)}, bf16[256,512]{1,0:T(8,128)(2,1)S(1)}, u32[]{:S(2)}, u32[]{:S(2)}) collective-permute-start(bf16[256,512]{1,0:T(8,128)(2,1)S(1)} %get-tuple-element.73.refs_1_), channel_id=1, source_target_pairs={{0,2},{1,5},{2,0},{3,7},{4,6},{5,1},{6,4},{7,3},{8,10},{9,13},{10,... | collective-permute-start | bytes 786440 | tf_op jit(solution)/shard_map/ppermute | solution.py:429
  39.7 9.2 %collective-permute-start.9 = (bf16[256,512]{1,0:T(8,128)(2,1)S(1)}, bf16[256,512]{1,0:T(8,128)(2,1)S(1)}, u32[]{:S(2)}, u32[]{:S(2)}) collective-permute-start(bf16[256,512]{1,0:T(8,128)(2,1)S(1)} %get-tuple-element.72.refs_0_), channel_id=1, source_target_pairs={{0,4},{1,3},{2,6},{3,1},{4,0},{5,7},{6,2},{7,5},{8,12},{9,11},{10,... | collective-permute-start | bytes 786440 | tf_op jit(solution)/shard_map/ppermute | solution.py:429
  42.2 12.4 %collective-permute-start.19 = (bf16[256,512]{1,0:T(8,128)(2,1)S(1)}, bf16[256,512]{1,0:T(8,128)(2,1)S(1)}, u32[]{:S(2)}, u32[]{:S(2)}) collective-permute-start(bf16[256,512]{1,0:T(8,128)(2,1)S(1)} %give.7), channel_id=1, source_target_pairs={{0,4},{1,3},{2,6},{3,1},{4,0},{5,7},{6,2},{7,5},{8,12},{9,11},{10,... | collective-permute-start | bytes 786440 | tf_op jit(solution)/shard_map/ppermute | solution.py:429
  44.1 10.5 %collective-permute-start.18 = (bf16[256,512]{1,0:T(8,128)(2,1)S(1)}, bf16[256,512]{1,0:T(8,128)(2,1)S(1)}, u32[]{:S(2)}, u32[]{:S(2)}) collective-permute-start(bf16[256,512]{1,0:T(8,128)(2,1)S(1)} %give.6), channel_id=1, source_target_pairs={{0,2},{1,5},{2,0},{3,7},{4,6},{5,1},{6,4},{7,3},{8,10},{9,13},{10,... | collective-permute-start | bytes 786440 | tf_op jit(solution)/shard_map/ppermute | solution.py:429
  47.5 11.0 %collective-permute-start.15 = (bf16[256,512]{1,0:T(8,128)(2,1)S(1)}, bf16[256,512]{1,0:T(8,128)(2,1)S(1)}, u32[]{:S(2)}, u32[]{:S(2)}) collective-permute-start(bf16[256,512]{1,0:T(8,128)(2,1)S(1)} %give.5), channel_id=1, source_target_pairs={{0,4},{1,3},{2,6},{3,1},{4,0},{5,7},{6,2},{7,5},{8,12},{9,11},{10,... | collective-permute-start | bytes 786440 | tf_op jit(solution)/shard_map/ppermute | solution.py:429
  49.3 9.3 %collective-permute-start.13 = (bf16[256,512]{1,0:T(8,128)(2,1)S(1)}, bf16[256,512]{1,0:T(8,128)(2,1)S(1)}, u32[]{:S(2)}, u32[]{:S(2)}) collective-permute-start(bf16[256,512]{1,0:T(8,128)(2,1)S(1)} %give.4), channel_id=1, source_target_pairs={{0,2},{1,5},{2,0},{3,7},{4,6},{5,1},{6,4},{7,3},{8,10},{9,13},{10,... | collective-permute-start | bytes 786440 | tf_op jit(solution)/shard_map/ppermute | solution.py:429

commit v20 on v19

--- a/solution.py
+++ b/solution.py
@@ -35,17 +35,16 @@
     return lax.ppermute(value, axis, [(place, place ^ mask) for place in range(size)])
 
 
-def kernel_call(kernel, outs, operands, name):
+def kernel_call(kernel, outs, operands, name, scratch=()):
     arrays = [pltpu.with_memory_space_constraint(array, pltpu.VMEM) for array in operands]
     return pl.pallas_call(
         kernel,
         in_specs=[pl.BlockSpec(memory_space=pltpu.VMEM)] * len(operands),
         out_specs=[pl.BlockSpec(memory_space=pltpu.VMEM)] * len(outs),
         out_shape=[pltpu.VMEM(shape, dtype) for shape, dtype in outs],
+        scratch_shapes=list(scratch),
         compiler_params=pltpu.CompilerParams(vmem_limit_bytes=VMEM_LIMIT),
-        cost_estimate=pl.CostEstimate(
-            flops=1, bytes_accessed=1, transcendentals=0
-        ),
+        cost_estimate=pl.CostEstimate(flops=1, bytes_accessed=1, transcendentals=0),
         name=name,
     )(*arrays)
 
@@ -171,9 +170,7 @@
         copy.wait()
         acc_k[at, :] = mm(x_own[at, :], wk[...])
     value.wait()
-    for start in starts:
-        at = slice(start, start + BLOCK)
-        acc_v[at, :] = mm(x_own[at, :], wv[...])
+    acc_v[...] = mm(x_own[...], wv[...])
     for copy in others:
         copy.wait()
 
@@ -281,7 +278,7 @@
 
 
 def query_gate_kernel(
-    heads, block, x_own, x_other, wq, wq_far, wg, wg_far, decay, coarse, fine, k, v, q_out, g_out, intra_out
+    heads, block, x_own, x_other, wq, wq_far, wg, wg_far, decay, coarse, fine, k, v, q_out, g_out, intra_out, q
 ):
     start = block * BLOCK
     lines = decay[:, start : start + BLOCK]
@@ -291,7 +288,11 @@
     cosine, sine = angles(coarse, fine, start, BLOCK)
     own, far = x_own[at, :], x_other[at, :]
     queries = mm(own, wq[...]) + mm(far, wq_far[...])
-    q_out[...] = turned(queries, cosine, sine)
+    q[...] = turned(queries, cosine, sine)
+    faded = jnp.exp(columns)
+    for head in range(heads):
+        span = slice(head * DH, (head + 1) * DH)
+        q_out[:, span] = (q[:, span].astype(F32) * faded[:, head : head + 1]).astype(BF16)
     gates = mm(own, wg[...]) + mm(far, wg_far[...])
     gates = gates.astype(BF16).astype(F32)
     g_out[...] = gates / (1.0 + jnp.exp(-gates))
@@ -302,7 +303,7 @@
         causal = place_t >= place_s
         for head in range(heads):
             span = slice(head * DH, (head + 1) * DH)
-            scores = mm_nt(q_out[low:last, span], k[start : start + last, span])
+            scores = mm_nt(q[low:last, span], k[start : start + last, span])
             differ = columns[low:last, head : head + 1] - lines[head : head + 1, :last]
             weights = jnp.where(causal, jnp.exp(jnp.where(causal, differ, 0.0)), 0.0)
             intra_out[low:last, span] = mm((scores * weights).astype(BF16), v[start : start + last, span])
@@ -316,14 +317,13 @@
         block = start // BLOCK
         q, gate, intra = projected[3 * block : 3 * block + 3]
         at = slice(start % BLOCK, start % BLOCK + TILE)
-        columns = jnp.exp(decay[:, start : start + TILE].T)
         scales = jnp.exp(block_ends(decay, 0, block * BLOCK))
         for head in range(heads):
             span, row = slice(head * DH, (head + 1) * DH), slice(head, head + 1)
             fade = jnp.exp(entering[heads * DH + head : heads * DH + head + 1, :1])
             state = entering[span, :] + fade * arrived_state(arrivals, sets, hop, span)
             prior = (scales[row] * state + before[block, span, :].astype(F32)).astype(BF16)
-            retained = intra[at, span] + columns[:, row] * mm(q[at, span], prior)
+            retained = intra[at, span] + mm(q[at, span], prior)
             center = retained - jnp.mean(retained, axis=1, keepdims=True)
             spread = jnp.mean(center * center, axis=1, keepdims=True)
             out[:, span] = (gate[at, span] * center * lax.rsqrt(spread + 1e-5)).astype(BF16)
@@ -464,6 +464,7 @@
             [((BLOCK, cols), BF16), ((BLOCK, cols), F32), ((BLOCK, cols), F32)],
             [x_own, x_other, own_q, far_q, own_g, far_g, decay, coarse, fine, keys, values],
             "query_gate",
+            [pltpu.VMEM((BLOCK, cols), BF16)],
         )
 
     def exchange(message, lowers, hop):

time: 60 us -> 60 us (level)
  no operation moved by 1% of the time
where the time goes in v20:
time: 60 us; the launch traced here: 59.5 us
  Pallas kernels  23.9 us (40%)
  starting transfers between devices  17.9 us (30%)
  waiting for transfers between devices  17.4 us (29%)
    pallas_call x15, Pallas kernels, kernel_call(): pl.pallas_call(kernel, in_specs=[pl.BlockSpec(memory_space=pltpu.VMEM)] *...  14.6 us
    ppermute x10, starting transfers between devices, trade(): return lax.ppermute(value, ('tp', 'fsdp'), partners[role])  11.9 us
    ppermute x3, waiting for transfers between devices, exchange(): return lax.ppermute(message, 'ctx', pairs)  9.11 us
    ppermute x10, waiting for transfers between devices, trade(): return lax.ppermute(value, ('tp', 'fsdp'), partners[role])  8.27 us
    pallas_call x2, Pallas kernels, loading_call(): pl.pallas_call(kernel, in_specs=[pl.BlockSpec(memory_space=pltpu.HBM)] *...  7.53 us
    ppermute x3, starting transfers between devices, exchange(): return lax.ppermute(message, 'ctx', pairs)  4.22 us
    ppermute x7, starting transfers between devices, swap(): lax.ppermute(value, axis, [(place, place ^ mask) for place in range(size)])  1.71 us
    pallas_call x2, Pallas kernels, on_device(): pl.pallas_call(functools.partial(finish_kernel, part_order), in_specs=[pl...  1.7 us
  transfers between devices with their start and end apart: 20, of which 7 were waited for; matrix products, arithmetic and copies ran while one was open for 0% of the time, Pallas kernels for 39%

profile of v20, /device:TPU:24, one launch (start us, length us, event | category | flops | bytes accessed | tf_op | source)
XLA Modules:
  0.0 59.5 jit_solution(9454599030269387645)
XLA Ops:
  0.5 4.3 %key_value_own.1 = (bf16[1024,1024]{1,0:T(8,128)(2,1)S(1)}, bf16[1024,1024]{1,0:T(8,128)(2,1)S(1)}, f32[1024,512]{1,0:T(8,128)S(1)}, f32[1024,512]{1,0:T(8,128)S...) custom-call(bf16[1024,2048]{1,0:T(8,128)(2,1)} %bitcast.4, ...), custom_call_target="tpu_custom_call" | custom-call | flops 1 | bytes 1 | tf_op jit(solution)/shard_map/key_value_own/pallas_call | solution.py:55
  4.9 3.2 %key_value.1 = (bf16[1024,512]{1,0:T(8,128)(2,1)S(1)}, bf16[1024,512]{1,0:T(8,128)(2,1)S(1)}, bf16[1024,512]{1,0:T(8,128)(2,1)S(1)}, bf16[1024,512]{1,0:T(8,128)...) custom-call(bf16[1024,512]{1,0:T(8,128)(2,1)} %wq_far.1, ...), custom_call_target="tpu_custom_call" | custom-call | flops 1 | bytes 1 | tf_op jit(solution)/shard_map/key_value/pallas_call | solution.py:55
  8.2 0.5 collective-permute-start.3
  8.8 1.3 %collective-permute-start.5 = (bf16[528,256]{1,0:T(8,128)(2,1)S(1)}, bf16[528,256]{1,0:T(8,128)(2,1)S(1)}, u32[]{:S(2)}, u32[]{:S(2)}) collective-permute-start(bf16[528,256]{1,0:T(8,128)(2,1)S(1)} %get-tuple-element.61.sent), channel_id=1, source_target_pairs={{0,8},{8,16},{16,24},{1,9},{9,17},{17,25},{2,10},{10,18},{18,26},{... | collective-permute-start | bytes 811016 | tf_op jit(solution)/shard_map/ppermute | solution.py:474
  10.2 1.6 %collective-permute-start.8 = (bf16[512,512]{1,0:T(8,128)(2,1)S(1)}, bf16[512,512]{1,0:T(8,128)(2,1)S(1)}, u32[]{:S(2)}, u32[]{:S(2)}) collective-permute-start(bf16[512,512]{1,0:T(8,128)(2,1)S(1)} %get-tuple-element.67), channel_id=1, source_target_pairs={{0,2},{1,5},{2,0},{3,7},{4,6},{5,1},{6,4},{7,3},{8,10},{9,13},{10,... | collective-permute-start | bytes 1572872 | tf_op jit(solution)/shard_map/ppermute | solution.py:429
  11.7 0.7 %collective-permute-start.7 = (bf16[528,256]{1,0:T(8,128)(2,1)S(1)}, bf16[528,256]{1,0:T(8,128)(2,1)S(1)}, u32[]{:S(2)}, u32[]{:S(2)}) collective-permute-start(bf16[528,256]{1,0:T(8,128)(2,1)S(1)} %get-tuple-element.61.sent), channel_id=1, source_target_pairs={{0,16},{16,0},{1,17},{17,1},{2,18},{18,2},{3,19},{19,3},{4,20},{20... | collective-permute-start | bytes 811016 | tf_op jit(solution)/shard_map/ppermute | solution.py:474
  12.4 0.6 %collective-permute-start.10 = (bf16[512,512]{1,0:T(8,128)(2,1)S(1)}, bf16[512,512]{1,0:T(8,128)(2,1)S(1)}, u32[]{:S(2)}, u32[]{:S(2)}) collective-permute-start(bf16[512,512]{1,0:T(8,128)(2,1)S(1)} %get-tuple-element.77), channel_id=1, source_target_pairs={{0,2},{1,5},{2,0},{3,7},{4,6},{5,1},{6,4},{7,3},{8,10},{9,13},{10,... | collective-permute-start | bytes 1572872 | tf_op jit(solution)/shard_map/ppermute | solution.py:429
  13.0 3.1 %query_gate.2 = (bf16[512,512]{1,0:T(8,128)(2,1)S(1)}, f32[512,512]{1,0:T(8,128)S(1)}, f32[512,512]{1,0:T(8,128)S(1)}) custom-call(bf16[1024,1024]{1,0:T(8,128)(2,1)S(1)} %get-tuple-element.54.x_own, bf16[1024,1024]{1,0:T(8,128)(2,1)S(1)} %get-tuple-element.47.x.x_other, bf16[1024,512]{1,0:T(8,128)(2,1)S(1)} %get-tuple-element.55.wq, ...), custom_call_target="tpu_custom_call" | custom-call | flops 1 | bytes 1 | tf_op jit(solution)/shard_map/query_gate/pallas_call | solution.py:40
  16.1 3.4 %collective-permute-done.5.refs_0_ = bf16[528,256]{1,0:T(8,128)(2,1)S(1)} collective-permute-done((bf16[528,256]{1,0:T(8,128)(2,1)S(1)}, bf16[528,256]{1,0:T(8,128)(2,1)S(1)}, u32[]{:S(2)}, u32[]{:S(2)}) %collective-permute-start.5) | collective-permute-done | bytes 270368 | tf_op jit(solution)/shard_map/ppermute | solution.py:474
  19.7 2.3 %collective-permute-start.6 = (bf16[512,256]{1,0:T(8,128)(2,1)S(1)}, bf16[512,256]{1,0:T(8,128)(2,1)S(1)}, u32[]{:S(2)}, u32[]{:S(2)}) collective-permute-start(bf16[512,256]{1,0:T(8,128)(2,1)S(1)} %get-tuple-element.63), channel_id=1, source_target_pairs={{8,24},{24,8},{9,25},{25,9},{10,26},{26,10},{11,27},{27,11},{12,28... | collective-permute-start | bytes 786440 | tf_op jit(solution)/shard_map/ppermute | solution.py:474
  22.0 3.1 %query_gate.3 = (bf16[512,512]{1,0:T(8,128)(2,1)S(1)}, f32[512,512]{1,0:T(8,128)S(1)}, f32[512,512]{1,0:T(8,128)S(1)}) custom-call(bf16[1024,1024]{1,0:T(8,128)(2,1)S(1)} %get-tuple-element.54.x_own, bf16[1024,1024]{1,0:T(8,128)(2,1)S(1)} %get-tuple-element.47.x.x_other, bf16[1024,512]{1,0:T(8,128)(2,1)S(1)} %get-tuple-element.55.wq, ...), custom_call_target="tpu_custom_call" | custom-call | flops 1 | bytes 1 | tf_op jit(solution)/shard_map/query_gate/pallas_call | solution.py:40
  25.1 5.7 %collective-permute-done.6.refs_0_ = bf16[512,256]{1,0:T(8,128)(2,1)S(1)} collective-permute-done((bf16[512,256]{1,0:T(8,128)(2,1)S(1)}, bf16[512,256]{1,0:T(8,128)(2,1)S(1)}, u32[]{:S(2)}, u32[]{:S(2)}) %collective-permute-start.6) | collective-permute-done | bytes 262176 | tf_op jit(solution)/shard_map/ppermute | solution.py:474
  30.8 1.2 %hidden.7 = (bf16[256,512]{1,0:T(8,128)(2,1)S(1)}, bf16[16,128]{1,0:T(8,128)(2,1)}) custom-call(f32[8,1024]{1,0:T(8,128)S(1)} %get-tuple-element.68.decay, bf16[2,512,256]{2,1,0:T(8,128)(2,1)S(1)} %get-tuple-element.52.before, f32[520,256]{1,0:T(8,128)S(1)} %get-tuple-element.62.entering, bf16[512,256]{1,0:T(8,128)(2,1)S(1)} %collective-permute-done.6.refs_0_, ...), custom_call_target="tpu_custom_call" | custom-call | flops 1 | bytes 1 | tf_op jit(solution)/shard_map/hidden/pallas_call | solution.py:40
  31.9 0.5 collective-permute-start.12
  32.5 1.5 %collective-permute-start.17 = (bf16[256,512]{1,0:T(8,128)(2,1)S(1)}, bf16[256,512]{1,0:T(8,128)(2,1)S(1)}, u32[]{:S(2)}, u32[]{:S(2)}) collective-permute-start(bf16[256,512]{1,0:T(8,128)(2,1)S(1)} %get-tuple-element.75.refs_3_), channel_id=1, source_target_pairs={{0,2},{1,5},{2,0},{3,7},{4,6},{5,1},{6,4},{7,3},{8,10},{9,13},{10,... | collective-permute-start | bytes 786440 | tf_op jit(solution)/shard_map/ppermute | solution.py:429
  33.9 1.2 %hidden.6 = (bf16[256,512]{1,0:T(8,128)(2,1)S(1)}, bf16[16,128]{1,0:T(8,128)(2,1)}) custom-call(f32[8,1024]{1,0:T(8,128)S(1)} %get-tuple-element.68.decay, bf16[2,512,256]{2,1,0:T(8,128)(2,1)S(1)} %get-tuple-element.52.before, f32[520,256]{1,0:T(8,128)S(1)} %get-tuple-element.62.entering, bf16[512,256]{1,0:T(8,128)(2,1)S(1)} %collective-permute-done.6.refs_0_, ...), custom_call_target="tpu_custom_call" | custom-call | flops 1 | bytes 1 | tf_op jit(solution)/shard_map/hidden/pallas_call | solution.py:40
  35.1 1.5 %collective-permute-start.16 = (bf16[256,512]{1,0:T(8,128)(2,1)S(1)}, bf16[256,512]{1,0:T(8,128)(2,1)S(1)}, u32[]{:S(2)}, u32[]{:S(2)}) collective-permute-start(bf16[256,512]{1,0:T(8,128)(2,1)S(1)} %get-tuple-element.74.refs_2_), channel_id=1, source_target_pairs={{0,4},{1,3},{2,6},{3,1},{4,0},{5,7},{6,2},{7,5},{8,12},{9,11},{10,... | collective-permute-start | bytes 786440 | tf_op jit(solution)/shard_map/ppermute | solution.py:429
  36.7 1.2 %hidden.5 = (bf16[256,512]{1,0:T(8,128)(2,1)S(1)}, bf16[16,128]{1,0:T(8,128)(2,1)}) custom-call(f32[8,1024]{1,0:T(8,128)S(1)} %get-tuple-element.68.decay, bf16[2,512,256]{2,1,0:T(8,128)(2,1)S(1)} %get-tuple-element.52.before, f32[520,256]{1,0:T(8,128)S(1)} %get-tuple-element.62.entering, bf16[512,256]{1,0:T(8,128)(2,1)S(1)} %collective-permute-done.6.refs_0_, ...), custom_call_target="tpu_custom_call" | custom-call | flops 1 | bytes 1 | tf_op jit(solution)/shard_map/hidden/pallas_call | solution.py:40
  37.8 0.5 collective-permute-start.14
  38.4 1.2 %hidden.4 = (bf16[256,512]{1,0:T(8,128)(2,1)S(1)}, bf16[16,128]{1,0:T(8,128)(2,1)}) custom-call(f32[8,1024]{1,0:T(8,128)S(1)} %get-tuple-element.68.decay, bf16[2,512,256]{2,1,0:T(8,128)(2,1)S(1)} %get-tuple-element.52.before, f32[520,256]{1,0:T(8,128)S(1)} %get-tuple-element.62.entering, bf16[512,256]{1,0:T(8,128)(2,1)S(1)} %collective-permute-done.6.refs_0_, ...), custom_call_target="tpu_custom_call" | custom-call | flops 1 | bytes 1 | tf_op jit(solution)/shard_map/hidden/pallas_call | solution.py:40
  39.5 0.5 collective-permute-start.9
  40.1 1.3 %own_products.1 = (f32[512,1024]{1,0:T(8,128)S(1)}, f32[512,1024]{1,0:T(8,128)S(1)}) custom-call(bf16[512,1024]{1,0:T(8,128)(2,1)S(1)} %get-tuple-element.66.first.own_first, bf16[512,1024]{1,0:T(8,128)(2,1)S(1)} %collective-permute-done.second.own_second, bf16[256,512]{1,0:T(8,128)(2,1)S(1)} %get-tuple-element.72.refs_0_, ...), custom_call_target="tpu_custom_call" | custom-call | flops 1 | bytes 1 | tf_op jit(solution)/shard_map/own_products/pallas_call | solution.py:40
  42.0 1.6 %collective-permute-start.19 = (bf16[256,512]{1,0:T(8,128)(2,1)S(1)}, bf16[256,512]{1,0:T(8,128)(2,1)S(1)}, u32[]{:S(2)}, u32[]{:S(2)}) collective-permute-start(bf16[256,512]{1,0:T(8,128)(2,1)S(1)} %give.7), channel_id=1, source_target_pairs={{0,4},{1,3},{2,6},{3,1},{4,0},{5,7},{6,2},{7,5},{8,12},{9,11},{10,... | collective-permute-start | bytes 786440 | tf_op jit(solution)/shard_map/ppermute | solution.py:429
  43.9 1.6 %collective-permute-start.18 = (bf16[256,512]{1,0:T(8,128)(2,1)S(1)}, bf16[256,512]{1,0:T(8,128)(2,1)S(1)}, u32[]{:S(2)}, u32[]{:S(2)}) collective-permute-start(bf16[256,512]{1,0:T(8,128)(2,1)S(1)} %give.6), channel_id=1, source_target_pairs={{0,2},{1,5},{2,0},{3,7},{4,6},{5,1},{6,4},{7,3},{8,10},{9,13},{10,... | collective-permute-start | bytes 786440 | tf_op jit(solution)/shard_map/ppermute | solution.py:429
  45.4 1.6 %collective-permute-done.14.far.refs_1_ = bf16[256,512]{1,0:T(8,128)(2,1)S(1)} collective-permute-done((bf16[256,512]{1,0:T(8,128)(2,1)S(1)}, bf16[256,512]{1,0:T(8,128)(2,1)S(1)}, u32[]{:S(2)}, u32[]{:S(2)}) %collective-permute-start.14) | collective-permute-done | bytes 262176 | tf_op jit(solution)/shard_map/ppermute | solution.py:429
  47.4 1.2 %collective-permute-start.15 = (bf16[256,512]{1,0:T(8,128)(2,1)S(1)}, bf16[256,512]{1,0:T(8,128)(2,1)S(1)}, u32[]{:S(2)}, u32[]{:S(2)}) collective-permute-start(bf16[256,512]{1,0:T(8,128)(2,1)S(1)} %give.5), channel_id=1, source_target_pairs={{0,4},{1,3},{2,6},{3,1},{4,0},{5,7},{6,2},{7,5},{8,12},{9,11},{10,... | collective-permute-start | bytes 786440 | tf_op jit(solution)/shard_map/ppermute | solution.py:429
  49.1 1.4 %collective-permute-start.13 = (bf16[256,512]{1,0:T(8,128)(2,1)S(1)}, bf16[256,512]{1,0:T(8,128)(2,1)S(1)}, u32[]{:S(2)}, u32[]{:S(2)}) collective-permute-start(bf16[256,512]{1,0:T(8,128)(2,1)S(1)} %give.4), channel_id=1, source_target_pairs={{0,2},{1,5},{2,0},{3,7},{4,6},{5,1},{6,4},{7,3},{8,10},{9,13},{10,... | collective-permute-start | bytes 786440 | tf_op jit(solution)/shard_map/ppermute | solution.py:429
  50.5 0.7 %keep.1 = (f32[512,512]{1,0:T(8,128)S(1)}, f32[512,512]{1,0:T(8,128)S(1)}) custom-call(bf16[256,512]{1,0:T(8,128)(2,1)S(1)} %collective-permute-done.9.far.refs_0_, bf16[256,512]{1,0:T(8,128)(2,1)S(1)} %collective-permute-done.14.far.refs_1_, bf16[256,512]{1,0:T(8,128)(2,1)S(1)} %collective-permute-done.16.refs_2_.far, ...), custom_call_target="tpu_custom_call" | custom-call | flops 1 | bytes 1 | tf_op jit(solution)/shard_map/keep/pallas_call | solution.py:40
  51.2 3.2 %collective-permute-done.19.refs_1_ = bf16[256,512]{1,0:T(8,128)(2,1)S(1)} collective-permute-done((bf16[256,512]{1,0:T(8,128)(2,1)S(1)}, bf16[256,512]{1,0:T(8,128)(2,1)S(1)}, u32[]{:S(2)}, u32[]{:S(2)}) %collective-permute-start.19) | collective-permute-done | bytes 262176 | tf_op jit(solution)/shard_map/ppermute | solution.py:429
  54.4 0.9 %finish.2.refs_4_ = bf16[1,1024,512]{2,1,0:T(8,128)(2,1)} custom-call(bf16[256,512]{1,0:T(8,128)(2,1)S(1)} %collective-permute-done.18.refs_0_, bf16[256,512]{1,0:T(8,128)(2,1)S(1)} %collective-permute-done.19.refs_1_, f32[512,512]{1,0:T(8,128)S(1)} %get-tuple-element.83.refs_2_, f32[512,512]{1,0:T(8,128)S(1)} %get-tuple-element.84.refs_3_), custom_call_target="tpu_custom_call" | custom-call | tf_op jit(solution)/shard_map/finish/pallas_call | solution.py:560
  55.3 3.1 %collective-permute-done.15.refs_1_ = bf16[256,512]{1,0:T(8,128)(2,1)S(1)} collective-permute-done((bf16[256,512]{1,0:T(8,128)(2,1)S(1)}, bf16[256,512]{1,0:T(8,128)(2,1)S(1)}, u32[]{:S(2)}, u32[]{:S(2)}) %collective-permute-start.15) | collective-permute-done | bytes 262176 | tf_op jit(solution)/shard_map/ppermute | solution.py:429
  58.5 0.9 %finish.3 = bf16[1,1024,512]{2,1,0:T(8,128)(2,1)} custom-call(bf16[256,512]{1,0:T(8,128)(2,1)S(1)} %collective-permute-done.13.refs_0_, bf16[256,512]{1,0:T(8,128)(2,1)S(1)} %collective-permute-done.15.refs_1_, f32[512,512]{1,0:T(8,128)S(1)} %get-tuple-element.83.refs_2_, f32[512,512]{1,0:T(8,128)S(1)} %get-tuple-element.84.refs_3_, ...), custom_call_target="tpu_custom_call", output_to_operand_aliasing={{}: (4, {})} | custom-call | tf_op jit(solution)/shard_map/finish/pallas_call | solution.py:560
  (27 shorter events, 2.7 us)
Async XLA Ops:
  0.0 4.9 %collective-permute-start.1 = (bf16[1024,512]{1,0:T(8,128)(2,1)}, bf16[1024,512]{1,0:T(8,128)(2,1)S(1)}, u32[]{:S(2)}, u32[]{:S(2)}) collective-permute-start(bf16[1024,512]{1,0:T(8,128)(2,1)} %wk_far.1), channel_id=1, source_target_pairs={{0,1},{1,0},{2,3},{3,2},{4,5},{5,4},{6,7},{7,6},{8,9},{9,8},{10,11... | collective-permute-start | bytes 3145736 | tf_op jit(solution)/shard_map/ppermute | solution.py:35
  0.0 4.9 %collective-permute-start.2 = (bf16[1024,512]{1,0:T(8,128)(2,1)}, bf16[1024,512]{1,0:T(8,128)(2,1)S(1)}, u32[]{:S(2)}, u32[]{:S(2)}) collective-permute-start(bf16[1024,512]{1,0:T(8,128)(2,1)} %wv_far.1), channel_id=1, source_target_pairs={{0,1},{1,0},{2,3},{3,2},{4,5},{5,4},{6,7},{7,6},{8,9},{9,8},{10,11... | collective-permute-start | bytes 3145736 | tf_op jit(solution)/shard_map/ppermute | solution.py:35
  4.8 5.2 %collective-permute-start = (bf16[512,1024]{1,0:T(8,128)(2,1)S(1)}, bf16[512,1024]{1,0:T(8,128)(2,1)S(1)}, u32[]{:S(2)}, u32[]{:S(2)}) collective-permute-start(bf16[512,1024]{1,0:T(8,128)(2,1)S(1)} %get-tuple-element.66.first.own_first), channel_id=1, source_target_pairs={{0,1},{1,0},{2,3},{3,2},{4,5},{5,4},{6,7},{7,6},{8,9},{9,8},{10,11... | collective-permute-start | bytes 3145736 | tf_op jit(solution)/shard_map/ppermute | solution.py:35
  8.2 4.2 %collective-permute-start.3 = (bf16[1024,512]{1,0:T(8,128)(2,1)S(1)}, bf16[1024,512]{1,0:T(8,128)(2,1)S(1)}, u32[]{:S(2)}, u32[]{:S(2)}) collective-permute-start(bf16[1024,512]{1,0:T(8,128)(2,1)S(1)} %get-tuple-element.55.wq), channel_id=1, source_target_pairs={{0,1},{1,0},{2,3},{3,2},{4,5},{5,4},{6,7},{7,6},{8,9},{9,8},{10,11... | collective-permute-start | bytes 3145736 | tf_op jit(solution)/shard_map/ppermute | solution.py:35
  8.7 4.3 %collective-permute-start.4 = (bf16[1024,512]{1,0:T(8,128)(2,1)S(1)}, bf16[1024,512]{1,0:T(8,128)(2,1)S(1)}, u32[]{:S(2)}, u32[]{:S(2)}) collective-permute-start(bf16[1024,512]{1,0:T(8,128)(2,1)S(1)} %get-tuple-element.56.wg), channel_id=1, source_target_pairs={{0,1},{1,0},{2,3},{3,2},{4,5},{5,4},{6,7},{7,6},{8,9},{9,8},{10,11... | collective-permute-start | bytes 3145736 | tf_op jit(solution)/shard_map/ppermute | solution.py:35
  8.8 10.7 %collective-permute-start.5 = (bf16[528,256]{1,0:T(8,128)(2,1)S(1)}, bf16[528,256]{1,0:T(8,128)(2,1)S(1)}, u32[]{:S(2)}, u32[]{:S(2)}) collective-permute-start(bf16[528,256]{1,0:T(8,128)(2,1)S(1)} %get-tuple-element.61.sent), channel_id=1, source_target_pairs={{0,8},{8,16},{16,24},{1,9},{9,17},{17,25},{2,10},{10,18},{18,26},{... | collective-permute-start | bytes 811016 | tf_op jit(solution)/shard_map/ppermute | solution.py:474
  10.2 11.8 %collective-permute-start.8 = (bf16[512,512]{1,0:T(8,128)(2,1)S(1)}, bf16[512,512]{1,0:T(8,128)(2,1)S(1)}, u32[]{:S(2)}, u32[]{:S(2)}) collective-permute-start(bf16[512,512]{1,0:T(8,128)(2,1)S(1)} %get-tuple-element.67), channel_id=1, source_target_pairs={{0,2},{1,5},{2,0},{3,7},{4,6},{5,1},{6,4},{7,3},{8,10},{9,13},{10,... | collective-permute-start | bytes 1572872 | tf_op jit(solution)/shard_map/ppermute | solution.py:429
  11.7 10.2 %collective-permute-start.7 = (bf16[528,256]{1,0:T(8,128)(2,1)S(1)}, bf16[528,256]{1,0:T(8,128)(2,1)S(1)}, u32[]{:S(2)}, u32[]{:S(2)}) collective-permute-start(bf16[528,256]{1,0:T(8,128)(2,1)S(1)} %get-tuple-element.61.sent), channel_id=1, source_target_pairs={{0,16},{16,0},{1,17},{17,1},{2,18},{18,2},{3,19},{19,3},{4,20},{20... | collective-permute-start | bytes 811016 | tf_op jit(solution)/shard_map/ppermute | solution.py:474
  12.4 19.5 %collective-permute-start.10 = (bf16[512,512]{1,0:T(8,128)(2,1)S(1)}, bf16[512,512]{1,0:T(8,128)(2,1)S(1)}, u32[]{:S(2)}, u32[]{:S(2)}) collective-permute-start(bf16[512,512]{1,0:T(8,128)(2,1)S(1)} %get-tuple-element.77), channel_id=1, source_target_pairs={{0,2},{1,5},{2,0},{3,7},{4,6},{5,1},{6,4},{7,3},{8,10},{9,13},{10,... | collective-permute-start | bytes 1572872 | tf_op jit(solution)/shard_map/ppermute | solution.py:429
  19.7 11.1 %collective-permute-start.6 = (bf16[512,256]{1,0:T(8,128)(2,1)S(1)}, bf16[512,256]{1,0:T(8,128)(2,1)S(1)}, u32[]{:S(2)}, u32[]{:S(2)}) collective-permute-start(bf16[512,256]{1,0:T(8,128)(2,1)S(1)} %get-tuple-element.63), channel_id=1, source_target_pairs={{8,24},{24,8},{9,25},{25,9},{10,26},{26,10},{11,27},{27,11},{12,28... | collective-permute-start | bytes 786440 | tf_op jit(solution)/shard_map/ppermute | solution.py:474
  31.9 7.6 %collective-permute-start.11 = (bf16[512,512]{1,0:T(8,128)(2,1)S(1)}, bf16[512,512]{1,0:T(8,128)(2,1)S(1)}, u32[]{:S(2)}, u32[]{:S(2)}) collective-permute-start(bf16[512,512]{1,0:T(8,128)(2,1)S(1)} %collective-permute-done.8.mine_0), channel_id=1, source_target_pairs={{0,1},{1,0},{2,3},{3,2},{4,5},{5,4},{6,7},{7,6},{8,9},{9,8},{10,11... | collective-permute-start | bytes 1572872 | tf_op jit(solution)/shard_map/ppermute | solution.py:35
  31.9 9.5 %collective-permute-start.12 = (bf16[512,512]{1,0:T(8,128)(2,1)S(1)}, bf16[512,512]{1,0:T(8,128)(2,1)S(1)}, u32[]{:S(2)}, u32[]{:S(2)}) collective-permute-start(bf16[512,512]{1,0:T(8,128)(2,1)S(1)} %collective-permute-done.10.mine_1), channel_id=1, source_target_pairs={{0,1},{1,0},{2,3},{3,2},{4,5},{5,4},{6,7},{7,6},{8,9},{9,8},{10,11... | collective-permute-start | bytes 1572872 | tf_op jit(solution)/shard_map/ppermute | solution.py:35
  32.5 9.2 %collective-permute-start.17 = (bf16[256,512]{1,0:T(8,128)(2,1)S(1)}, bf16[256,512]{1,0:T(8,128)(2,1)S(1)}, u32[]{:S(2)}, u32[]{:S(2)}) collective-permute-start(bf16[256,512]{1,0:T(8,128)(2,1)S(1)} %get-tuple-element.75.refs_3_), channel_id=1, source_target_pairs={{0,2},{1,5},{2,0},{3,7},{4,6},{5,1},{6,4},{7,3},{8,10},{9,13},{10,... | collective-permute-start | bytes 786440 | tf_op jit(solution)/shard_map/ppermute | solution.py:429
  35.1 8.4 %collective-permute-start.16 = (bf16[256,512]{1,0:T(8,128)(2,1)S(1)}, bf16[256,512]{1,0:T(8,128)(2,1)S(1)}, u32[]{:S(2)}, u32[]{:S(2)}) collective-permute-start(bf16[256,512]{1,0:T(8,128)(2,1)S(1)} %get-tuple-element.74.refs_2_), channel_id=1, source_target_pairs={{0,4},{1,3},{2,6},{3,1},{4,0},{5,7},{6,2},{7,5},{8,12},{9,11},{10,... | collective-permute-start | bytes 786440 | tf_op jit(solution)/shard_map/ppermute | solution.py:429
  37.8 9.2 %collective-permute-start.14 = (bf16[256,512]{1,0:T(8,128)(2,1)S(1)}, bf16[256,512]{1,0:T(8,128)(2,1)S(1)}, u32[]{:S(2)}, u32[]{:S(2)}) collective-permute-start(bf16[256,512]{1,0:T(8,128)(2,1)S(1)} %get-tuple-element.73.refs_1_), channel_id=1, source_target_pairs={{0,2},{1,5},{2,0},{3,7},{4,6},{5,1},{6,4},{7,3},{8,10},{9,13},{10,... | collective-permute-start | bytes 786440 | tf_op jit(solution)/shard_map/ppermute | solution.py:429
  39.5 9.2 %collective-permute-start.9 = (bf16[256,512]{1,0:T(8,128)(2,1)S(1)}, bf16[256,512]{1,0:T(8,128)(2,1)S(1)}, u32[]{:S(2)}, u32[]{:S(2)}) collective-permute-start(bf16[256,512]{1,0:T(8,128)(2,1)S(1)} %get-tuple-element.72.refs_0_), channel_id=1, source_target_pairs={{0,4},{1,3},{2,6},{3,1},{4,0},{5,7},{6,2},{7,5},{8,12},{9,11},{10,... | collective-permute-start | bytes 786440 | tf_op jit(solution)/shard_map/ppermute | solution.py:429
  42.0 12.4 %collective-permute-start.19 = (bf16[256,512]{1,0:T(8,128)(2,1)S(1)}, bf16[256,512]{1,0:T(8,128)(2,1)S(1)}, u32[]{:S(2)}, u32[]{:S(2)}) collective-permute-start(bf16[256,512]{1,0:T(8,128)(2,1)S(1)} %give.7), channel_id=1, source_target_pairs={{0,4},{1,3},{2,6},{3,1},{4,0},{5,7},{6,2},{7,5},{8,12},{9,11},{10,... | collective-permute-start | bytes 786440 | tf_op jit(solution)/shard_map/ppermute | solution.py:429
  43.9 10.5 %collective-permute-start.18 = (bf16[256,512]{1,0:T(8,128)(2,1)S(1)}, bf16[256,512]{1,0:T(8,128)(2,1)S(1)}, u32[]{:S(2)}, u32[]{:S(2)}) collective-permute-start(bf16[256,512]{1,0:T(8,128)(2,1)S(1)} %give.6), channel_id=1, source_target_pairs={{0,2},{1,5},{2,0},{3,7},{4,6},{5,1},{6,4},{7,3},{8,10},{9,13},{10,... | collective-permute-start | bytes 786440 | tf_op jit(solution)/shard_map/ppermute | solution.py:429
  47.4 11.0 %collective-permute-start.15 = (bf16[256,512]{1,0:T(8,128)(2,1)S(1)}, bf16[256,512]{1,0:T(8,128)(2,1)S(1)}, u32[]{:S(2)}, u32[]{:S(2)}) collective-permute-start(bf16[256,512]{1,0:T(8,128)(2,1)S(1)} %give.5), channel_id=1, source_target_pairs={{0,4},{1,3},{2,6},{3,1},{4,0},{5,7},{6,2},{7,5},{8,12},{9,11},{10,... | collective-permute-start | bytes 786440 | tf_op jit(solution)/shard_map/ppermute | solution.py:429
  49.1 9.4 %collective-permute-start.13 = (bf16[256,512]{1,0:T(8,128)(2,1)S(1)}, bf16[256,512]{1,0:T(8,128)(2,1)S(1)}, u32[]{:S(2)}, u32[]{:S(2)}) collective-permute-start(bf16[256,512]{1,0:T(8,128)(2,1)S(1)} %give.4), channel_id=1, source_target_pairs={{0,2},{1,5},{2,0},{3,7},{4,6},{5,1},{6,4},{7,3},{8,10},{9,13},{10,... | collective-permute-start | bytes 786440 | tf_op jit(solution)/shard_map/ppermute | solution.py:429

commit v21 on v19

--- a/solution.py
+++ b/solution.py
@@ -468,8 +468,7 @@
 
     def exchange(message, lowers, hop):
         pairs = [(at, at + hop) for at in lowers]
-        if hop > 1:
-            pairs += [(upper, at) for at, upper in pairs]
+        pairs += [(upper, at) for at, upper in pairs] if hop > 1 else [(ctx - 1, 0)]
         return lax.ppermute(message, "ctx", pairs)
 
     projected = list(query_gate(0, decay))

time: 60 us -> 64.4 us (1.073)
  the two profiles are of different devices: /device:TPU:24 before, /device:TPU:0 now
where the time goes in v21:
time: 64.4 us; the launch traced here: 64.2 us
  Pallas kernels  24.1 us (37%)
  starting transfers between devices  21.4 us (33%)
  waiting for transfers between devices  18.4 us (29%)
    pallas_call x15, Pallas kernels, kernel_call(): pl.pallas_call(kernel, in_specs=[pl.BlockSpec(memory_space=pltpu.VMEM)] *...  14.8 us
    ppermute x10, starting transfers between devices, trade(): return lax.ppermute(value, ('tp', 'fsdp'), partners[role])  11.5 us
    ppermute x3, waiting for transfers between devices, exchange(): return lax.ppermute(message, 'ctx', pairs)  9.8 us
    ppermute x10, waiting for transfers between devices, trade(): return lax.ppermute(value, ('tp', 'fsdp'), partners[role])  8.56 us
    ppermute x3, starting transfers between devices, exchange(): return lax.ppermute(message, 'ctx', pairs)  7.81 us
    pallas_call x2, Pallas kernels, loading_call(): pl.pallas_call(kernel, in_specs=[pl.BlockSpec(memory_space=pltpu.HBM)] *...  7.53 us
    ppermute x7, starting transfers between devices, swap(): lax.ppermute(value, axis, [(place, place ^ mask) for place in range(size)])  2.11 us
    pallas_call x2, Pallas kernels, on_device(): pl.pallas_call(functools.partial(finish_kernel, part_order), in_specs=[pl...  1.7 us
  transfers between devices with their start and end apart: 20, of which 6 were waited for; matrix products, arithmetic and copies ran while one was open for 0% of the time, Pallas kernels for 36%

profile of v21, /device:TPU:0, one launch (start us, length us, event | category | flops | bytes accessed | tf_op | source)
XLA Modules:
  0.0 64.2 jit_solution(10190159392376987150)
XLA Ops:
  0.5 4.3 %key_value_own.1 = (bf16[1024,1024]{1,0:T(8,128)(2,1)S(1)}, bf16[1024,1024]{1,0:T(8,128)(2,1)S(1)}, f32[1024,512]{1,0:T(8,128)S(1)}, f32[1024,512]{1,0:T(8,128)S...) custom-call(bf16[1024,2048]{1,0:T(8,128)(2,1)} %bitcast.4, ...), custom_call_target="tpu_custom_call" | custom-call | flops 1 | bytes 1 | tf_op jit(solution)/shard_map/key_value_own/pallas_call | solution.py:56
  4.8 0.5 collective-permute-start
  5.4 3.2 %key_value.1 = (bf16[1024,512]{1,0:T(8,128)(2,1)S(1)}, bf16[1024,512]{1,0:T(8,128)(2,1)S(1)}, bf16[1024,512]{1,0:T(8,128)(2,1)S(1)}, bf16[1024,512]{1,0:T(8,128)...) custom-call(bf16[1024,512]{1,0:T(8,128)(2,1)} %wq_far.1, ...), custom_call_target="tpu_custom_call" | custom-call | flops 1 | bytes 1 | tf_op jit(solution)/shard_map/key_value/pallas_call | solution.py:56
  8.7 0.5 collective-permute-start.4
  9.2 2.6 %collective-permute-start.5 = (bf16[528,256]{1,0:T(8,128)(2,1)S(1)}, bf16[528,256]{1,0:T(8,128)(2,1)S(1)}, u32[]{:S(2)}, u32[]{:S(2)}) collective-permute-start(bf16[528,256]{1,0:T(8,128)(2,1)S(1)} %get-tuple-element.61.sent), channel_id=1, source_target_pairs={{0,8},{8,16},{16,24},{24,0},{1,9},{9,17},{17,25},{25,1},{2,10},{10... | collective-permute-start | bytes 811016 | tf_op jit(solution)/shard_map/ppermute | solution.py:472
  11.9 1.6 %collective-permute-start.8 = (bf16[512,512]{1,0:T(8,128)(2,1)S(1)}, bf16[512,512]{1,0:T(8,128)(2,1)S(1)}, u32[]{:S(2)}, u32[]{:S(2)}) collective-permute-start(bf16[512,512]{1,0:T(8,128)(2,1)S(1)} %get-tuple-element.67), channel_id=1, source_target_pairs={{0,2},{1,5},{2,0},{3,7},{4,6},{5,1},{6,4},{7,3},{8,10},{9,13},{10,... | collective-permute-start | bytes 1572872 | tf_op jit(solution)/shard_map/ppermute | solution.py:429
  13.4 4.5 %collective-permute-start.7 = (bf16[528,256]{1,0:T(8,128)(2,1)S(1)}, bf16[528,256]{1,0:T(8,128)(2,1)S(1)}, u32[]{:S(2)}, u32[]{:S(2)}) collective-permute-start(bf16[528,256]{1,0:T(8,128)(2,1)S(1)} %get-tuple-element.61.sent), channel_id=1, source_target_pairs={{0,16},{16,0},{1,17},{17,1},{2,18},{18,2},{3,19},{19,3},{4,20},{20... | collective-permute-start | bytes 811016 | tf_op jit(solution)/shard_map/ppermute | solution.py:472
  17.9 0.6 collective-permute-start.10
  18.5 3.1 %query_gate.2 = (bf16[512,512]{1,0:T(8,128)(2,1)S(1)}, f32[512,512]{1,0:T(8,128)S(1)}, f32[512,512]{1,0:T(8,128)S(1)}) custom-call(bf16[1024,1024]{1,0:T(8,128)(2,1)S(1)} %get-tuple-element.54.x_own, bf16[1024,1024]{1,0:T(8,128)(2,1)S(1)} %get-tuple-element.47.x.x_other, bf16[1024,512]{1,0:T(8,128)(2,1)S(1)} %get-tuple-element.55.wq, ...), custom_call_target="tpu_custom_call" | custom-call | flops 1 | bytes 1 | tf_op jit(solution)/shard_map/query_gate/pallas_call | solution.py:40
  21.8 0.7 %collective-permute-start.6 = (bf16[512,256]{1,0:T(8,128)(2,1)S(1)}, bf16[512,256]{1,0:T(8,128)(2,1)S(1)}, u32[]{:S(2)}, u32[]{:S(2)}) collective-permute-start(bf16[512,256]{1,0:T(8,128)(2,1)S(1)} %get-tuple-element.63), channel_id=1, source_target_pairs={{8,24},{24,8},{9,25},{25,9},{10,26},{26,10},{11,27},{27,11},{12,28... | collective-permute-start | bytes 786440 | tf_op jit(solution)/shard_map/ppermute | solution.py:472
  22.5 9.8 %collective-permute-done.7.refs_1_ = bf16[528,256]{1,0:T(8,128)(2,1)S(1)} collective-permute-done((bf16[528,256]{1,0:T(8,128)(2,1)S(1)}, bf16[528,256]{1,0:T(8,128)(2,1)S(1)}, u32[]{:S(2)}, u32[]{:S(2)}) %collective-permute-start.7) | collective-permute-done | bytes 270368 | tf_op jit(solution)/shard_map/ppermute | solution.py:472
  32.3 3.1 %query_gate.3 = (bf16[512,512]{1,0:T(8,128)(2,1)S(1)}, f32[512,512]{1,0:T(8,128)S(1)}, f32[512,512]{1,0:T(8,128)S(1)}) custom-call(bf16[1024,1024]{1,0:T(8,128)(2,1)S(1)} %get-tuple-element.54.x_own, bf16[1024,1024]{1,0:T(8,128)(2,1)S(1)} %get-tuple-element.47.x.x_other, bf16[1024,512]{1,0:T(8,128)(2,1)S(1)} %get-tuple-element.55.wq, ...), custom_call_target="tpu_custom_call" | custom-call | flops 1 | bytes 1 | tf_op jit(solution)/shard_map/query_gate/pallas_call | solution.py:40
  35.4 1.2 %hidden.7 = (bf16[256,512]{1,0:T(8,128)(2,1)S(1)}, bf16[16,128]{1,0:T(8,128)(2,1)}) custom-call(f32[8,1024]{1,0:T(8,128)S(1)} %get-tuple-element.68.decay, bf16[2,512,256]{2,1,0:T(8,128)(2,1)S(1)} %get-tuple-element.52.before, f32[520,256]{1,0:T(8,128)S(1)} %get-tuple-element.62.entering, bf16[512,256]{1,0:T(8,128)(2,1)S(1)} %collective-permute-done.6.refs_0_, ...), custom_call_target="tpu_custom_call" | custom-call | flops 1 | bytes 1 | tf_op jit(solution)/shard_map/hidden/pallas_call | solution.py:40
  36.7 0.5 collective-permute-start.12
  37.2 1.5 %collective-permute-start.17 = (bf16[256,512]{1,0:T(8,128)(2,1)S(1)}, bf16[256,512]{1,0:T(8,128)(2,1)S(1)}, u32[]{:S(2)}, u32[]{:S(2)}) collective-permute-start(bf16[256,512]{1,0:T(8,128)(2,1)S(1)} %get-tuple-element.75.refs_3_), channel_id=1, source_target_pairs={{0,2},{1,5},{2,0},{3,7},{4,6},{5,1},{6,4},{7,3},{8,10},{9,13},{10,... | collective-permute-start | bytes 786440 | tf_op jit(solution)/shard_map/ppermute | solution.py:429
  38.7 1.2 %hidden.6 = (bf16[256,512]{1,0:T(8,128)(2,1)S(1)}, bf16[16,128]{1,0:T(8,128)(2,1)}) custom-call(f32[8,1024]{1,0:T(8,128)S(1)} %get-tuple-element.68.decay, bf16[2,512,256]{2,1,0:T(8,128)(2,1)S(1)} %get-tuple-element.52.before, f32[520,256]{1,0:T(8,128)S(1)} %get-tuple-element.62.entering, bf16[512,256]{1,0:T(8,128)(2,1)S(1)} %collective-permute-done.6.refs_0_, ...), custom_call_target="tpu_custom_call" | custom-call | flops 1 | bytes 1 | tf_op jit(solution)/shard_map/hidden/pallas_call | solution.py:40
  39.9 1.5 %collective-permute-start.16 = (bf16[256,512]{1,0:T(8,128)(2,1)S(1)}, bf16[256,512]{1,0:T(8,128)(2,1)S(1)}, u32[]{:S(2)}, u32[]{:S(2)}) collective-permute-start(bf16[256,512]{1,0:T(8,128)(2,1)S(1)} %get-tuple-element.74.refs_2_), channel_id=1, source_target_pairs={{0,4},{1,3},{2,6},{3,1},{4,0},{5,7},{6,2},{7,5},{8,12},{9,11},{10,... | collective-permute-start | bytes 786440 | tf_op jit(solution)/shard_map/ppermute | solution.py:429
  41.4 1.2 %hidden.5 = (bf16[256,512]{1,0:T(8,128)(2,1)S(1)}, bf16[16,128]{1,0:T(8,128)(2,1)}) custom-call(f32[8,1024]{1,0:T(8,128)S(1)} %get-tuple-element.68.decay, bf16[2,512,256]{2,1,0:T(8,128)(2,1)S(1)} %get-tuple-element.52.before, f32[520,256]{1,0:T(8,128)S(1)} %get-tuple-element.62.entering, bf16[512,256]{1,0:T(8,128)(2,1)S(1)} %collective-permute-done.6.refs_0_, ...), custom_call_target="tpu_custom_call" | custom-call | flops 1 | bytes 1 | tf_op jit(solution)/shard_map/hidden/pallas_call | solution.py:40
  42.6 0.5 collective-permute-start.14
  43.1 1.2 %hidden.4 = (bf16[256,512]{1,0:T(8,128)(2,1)S(1)}, bf16[16,128]{1,0:T(8,128)(2,1)}) custom-call(f32[8,1024]{1,0:T(8,128)S(1)} %get-tuple-element.68.decay, bf16[2,512,256]{2,1,0:T(8,128)(2,1)S(1)} %get-tuple-element.52.before, f32[520,256]{1,0:T(8,128)S(1)} %get-tuple-element.62.entering, bf16[512,256]{1,0:T(8,128)(2,1)S(1)} %collective-permute-done.6.refs_0_, ...), custom_call_target="tpu_custom_call" | custom-call | flops 1 | bytes 1 | tf_op jit(solution)/shard_map/hidden/pallas_call | solution.py:40
  44.4 0.5 collective-permute-start.9
  44.9 1.3 %own_products.1 = (f32[512,1024]{1,0:T(8,128)S(1)}, f32[512,1024]{1,0:T(8,128)S(1)}) custom-call(bf16[512,1024]{1,0:T(8,128)(2,1)S(1)} %get-tuple-element.66.first.own_first, bf16[512,1024]{1,0:T(8,128)(2,1)S(1)} %collective-permute-done.second.own_second, bf16[256,512]{1,0:T(8,128)(2,1)S(1)} %get-tuple-element.72.refs_0_, ...), custom_call_target="tpu_custom_call" | custom-call | flops 1 | bytes 1 | tf_op jit(solution)/shard_map/own_products/pallas_call | solution.py:40
  46.8 1.6 %collective-permute-start.19 = (bf16[256,512]{1,0:T(8,128)(2,1)S(1)}, bf16[256,512]{1,0:T(8,128)(2,1)S(1)}, u32[]{:S(2)}, u32[]{:S(2)}) collective-permute-start(bf16[256,512]{1,0:T(8,128)(2,1)S(1)} %give.7), channel_id=1, source_target_pairs={{0,4},{1,3},{2,6},{3,1},{4,0},{5,7},{6,2},{7,5},{8,12},{9,11},{10,... | collective-permute-start | bytes 786440 | tf_op jit(solution)/shard_map/ppermute | solution.py:429
  48.7 1.5 %collective-permute-start.18 = (bf16[256,512]{1,0:T(8,128)(2,1)S(1)}, bf16[256,512]{1,0:T(8,128)(2,1)S(1)}, u32[]{:S(2)}, u32[]{:S(2)}) collective-permute-start(bf16[256,512]{1,0:T(8,128)(2,1)S(1)} %give.6), channel_id=1, source_target_pairs={{0,2},{1,5},{2,0},{3,7},{4,6},{5,1},{6,4},{7,3},{8,10},{9,13},{10,... | collective-permute-start | bytes 786440 | tf_op jit(solution)/shard_map/ppermute | solution.py:429
  50.3 1.6 %collective-permute-done.14.far.refs_1_ = bf16[256,512]{1,0:T(8,128)(2,1)S(1)} collective-permute-done((bf16[256,512]{1,0:T(8,128)(2,1)S(1)}, bf16[256,512]{1,0:T(8,128)(2,1)S(1)}, u32[]{:S(2)}, u32[]{:S(2)}) %collective-permute-start.14) | collective-permute-done | bytes 262176 | tf_op jit(solution)/shard_map/ppermute | solution.py:429
  52.1 1.0 %collective-permute-start.15 = (bf16[256,512]{1,0:T(8,128)(2,1)S(1)}, bf16[256,512]{1,0:T(8,128)(2,1)S(1)}, u32[]{:S(2)}, u32[]{:S(2)}) collective-permute-start(bf16[256,512]{1,0:T(8,128)(2,1)S(1)} %give.5), channel_id=1, source_target_pairs={{0,4},{1,3},{2,6},{3,1},{4,0},{5,7},{6,2},{7,5},{8,12},{9,11},{10,... | collective-permute-start | bytes 786440 | tf_op jit(solution)/shard_map/ppermute | solution.py:429
  53.8 1.2 %collective-permute-start.13 = (bf16[256,512]{1,0:T(8,128)(2,1)S(1)}, bf16[256,512]{1,0:T(8,128)(2,1)S(1)}, u32[]{:S(2)}, u32[]{:S(2)}) collective-permute-start(bf16[256,512]{1,0:T(8,128)(2,1)S(1)} %give.4), channel_id=1, source_target_pairs={{0,2},{1,5},{2,0},{3,7},{4,6},{5,1},{6,4},{7,3},{8,10},{9,13},{10,... | collective-permute-start | bytes 786440 | tf_op jit(solution)/shard_map/ppermute | solution.py:429
  54.9 0.7 %keep.1 = (f32[512,512]{1,0:T(8,128)S(1)}, f32[512,512]{1,0:T(8,128)S(1)}) custom-call(bf16[256,512]{1,0:T(8,128)(2,1)S(1)} %collective-permute-done.9.far.refs_0_, bf16[256,512]{1,0:T(8,128)(2,1)S(1)} %collective-permute-done.14.far.refs_1_, bf16[256,512]{1,0:T(8,128)(2,1)S(1)} %collective-permute-done.16.refs_2_.far, ...), custom_call_target="tpu_custom_call" | custom-call | flops 1 | bytes 1 | tf_op jit(solution)/shard_map/keep/pallas_call | solution.py:40
  55.6 3.4 %collective-permute-done.19.refs_1_ = bf16[256,512]{1,0:T(8,128)(2,1)S(1)} collective-permute-done((bf16[256,512]{1,0:T(8,128)(2,1)S(1)}, bf16[256,512]{1,0:T(8,128)(2,1)S(1)}, u32[]{:S(2)}, u32[]{:S(2)}) %collective-permute-start.19) | collective-permute-done | bytes 262176 | tf_op jit(solution)/shard_map/ppermute | solution.py:429
  59.1 0.9 %finish.2.refs_4_ = bf16[1,1024,512]{2,1,0:T(8,128)(2,1)} custom-call(bf16[256,512]{1,0:T(8,128)(2,1)S(1)} %collective-permute-done.18.refs_0_, bf16[256,512]{1,0:T(8,128)(2,1)S(1)} %collective-permute-done.19.refs_1_, f32[512,512]{1,0:T(8,128)S(1)} %get-tuple-element.83.refs_2_, f32[512,512]{1,0:T(8,128)S(1)} %get-tuple-element.84.refs_3_), custom_call_target="tpu_custom_call" | custom-call | tf_op jit(solution)/shard_map/finish/pallas_call | solution.py:558
  59.9 3.2 %collective-permute-done.15.refs_1_ = bf16[256,512]{1,0:T(8,128)(2,1)S(1)} collective-permute-done((bf16[256,512]{1,0:T(8,128)(2,1)S(1)}, bf16[256,512]{1,0:T(8,128)(2,1)S(1)}, u32[]{:S(2)}, u32[]{:S(2)}) %collective-permute-start.15) | collective-permute-done | bytes 262176 | tf_op jit(solution)/shard_map/ppermute | solution.py:429
  63.2 0.9 %finish.3 = bf16[1,1024,512]{2,1,0:T(8,128)(2,1)} custom-call(bf16[256,512]{1,0:T(8,128)(2,1)S(1)} %collective-permute-done.13.refs_0_, bf16[256,512]{1,0:T(8,128)(2,1)S(1)} %collective-permute-done.15.refs_1_, f32[512,512]{1,0:T(8,128)S(1)} %get-tuple-element.83.refs_2_, f32[512,512]{1,0:T(8,128)S(1)} %get-tuple-element.84.refs_3_, ...), custom_call_target="tpu_custom_call", output_to_operand_aliasing={{}: (4, {})} | custom-call | tf_op jit(solution)/shard_map/finish/pallas_call | solution.py:558
  (27 shorter events, 2.8 us)
Async XLA Ops:
  0.0 5.4 %collective-permute-start.1 = (bf16[1024,512]{1,0:T(8,128)(2,1)}, bf16[1024,512]{1,0:T(8,128)(2,1)S(1)}, u32[]{:S(2)}, u32[]{:S(2)}) collective-permute-start(bf16[1024,512]{1,0:T(8,128)(2,1)} %wk_far.1), channel_id=1, source_target_pairs={{0,1},{1,0},{2,3},{3,2},{4,5},{5,4},{6,7},{7,6},{8,9},{9,8},{10,11... | collective-permute-start | bytes 3145736 | tf_op jit(solution)/shard_map/ppermute | solution.py:35
  0.5 4.9 %collective-permute-start.2 = (bf16[1024,512]{1,0:T(8,128)(2,1)}, bf16[1024,512]{1,0:T(8,128)(2,1)S(1)}, u32[]{:S(2)}, u32[]{:S(2)}) collective-permute-start(bf16[1024,512]{1,0:T(8,128)(2,1)} %wv_far.1), channel_id=1, source_target_pairs={{0,1},{1,0},{2,3},{3,2},{4,5},{5,4},{6,7},{7,6},{8,9},{9,8},{10,11... | collective-permute-start | bytes 3145736 | tf_op jit(solution)/shard_map/ppermute | solution.py:35
  4.8 7.0 %collective-permute-start = (bf16[512,1024]{1,0:T(8,128)(2,1)S(1)}, bf16[512,1024]{1,0:T(8,128)(2,1)S(1)}, u32[]{:S(2)}, u32[]{:S(2)}) collective-permute-start(bf16[512,1024]{1,0:T(8,128)(2,1)S(1)} %get-tuple-element.66.first.own_first), channel_id=1, source_target_pairs={{0,1},{1,0},{2,3},{3,2},{4,5},{5,4},{6,7},{7,6},{8,9},{9,8},{10,11... | collective-permute-start | bytes 3145736 | tf_op jit(solution)/shard_map/ppermute | solution.py:35
  8.6 9.4 %collective-permute-start.3 = (bf16[1024,512]{1,0:T(8,128)(2,1)S(1)}, bf16[1024,512]{1,0:T(8,128)(2,1)S(1)}, u32[]{:S(2)}, u32[]{:S(2)}) collective-permute-start(bf16[1024,512]{1,0:T(8,128)(2,1)S(1)} %get-tuple-element.55.wq), channel_id=1, source_target_pairs={{0,1},{1,0},{2,3},{3,2},{4,5},{5,4},{6,7},{7,6},{8,9},{9,8},{10,11... | collective-permute-start | bytes 3145736 | tf_op jit(solution)/shard_map/ppermute | solution.py:35
  8.7 9.8 %collective-permute-start.4 = (bf16[1024,512]{1,0:T(8,128)(2,1)S(1)}, bf16[1024,512]{1,0:T(8,128)(2,1)S(1)}, u32[]{:S(2)}, u32[]{:S(2)}) collective-permute-start(bf16[1024,512]{1,0:T(8,128)(2,1)S(1)} %get-tuple-element.56.wg), channel_id=1, source_target_pairs={{0,1},{1,0},{2,3},{3,2},{4,5},{5,4},{6,7},{7,6},{8,9},{9,8},{10,11... | collective-permute-start | bytes 3145736 | tf_op jit(solution)/shard_map/ppermute | solution.py:35
  9.2 12.5 %collective-permute-start.5 = (bf16[528,256]{1,0:T(8,128)(2,1)S(1)}, bf16[528,256]{1,0:T(8,128)(2,1)S(1)}, u32[]{:S(2)}, u32[]{:S(2)}) collective-permute-start(bf16[528,256]{1,0:T(8,128)(2,1)S(1)} %get-tuple-element.61.sent), channel_id=1, source_target_pairs={{0,8},{8,16},{16,24},{24,0},{1,9},{9,17},{17,25},{25,1},{2,10},{10... | collective-permute-start | bytes 811016 | tf_op jit(solution)/shard_map/ppermute | solution.py:472
  11.9 20.4 %collective-permute-start.8 = (bf16[512,512]{1,0:T(8,128)(2,1)S(1)}, bf16[512,512]{1,0:T(8,128)(2,1)S(1)}, u32[]{:S(2)}, u32[]{:S(2)}) collective-permute-start(bf16[512,512]{1,0:T(8,128)(2,1)S(1)} %get-tuple-element.67), channel_id=1, source_target_pairs={{0,2},{1,5},{2,0},{3,7},{4,6},{5,1},{6,4},{7,3},{8,10},{9,13},{10,... | collective-permute-start | bytes 1572872 | tf_op jit(solution)/shard_map/ppermute | solution.py:429
  13.4 18.9 %collective-permute-start.7 = (bf16[528,256]{1,0:T(8,128)(2,1)S(1)}, bf16[528,256]{1,0:T(8,128)(2,1)S(1)}, u32[]{:S(2)}, u32[]{:S(2)}) collective-permute-start(bf16[528,256]{1,0:T(8,128)(2,1)S(1)} %get-tuple-element.61.sent), channel_id=1, source_target_pairs={{0,16},{16,0},{1,17},{17,1},{2,18},{18,2},{3,19},{19,3},{4,20},{20... | collective-permute-start | bytes 811016 | tf_op jit(solution)/shard_map/ppermute | solution.py:472
  17.9 18.7 %collective-permute-start.10 = (bf16[512,512]{1,0:T(8,128)(2,1)S(1)}, bf16[512,512]{1,0:T(8,128)(2,1)S(1)}, u32[]{:S(2)}, u32[]{:S(2)}) collective-permute-start(bf16[512,512]{1,0:T(8,128)(2,1)S(1)} %get-tuple-element.77), channel_id=1, source_target_pairs={{0,2},{1,5},{2,0},{3,7},{4,6},{5,1},{6,4},{7,3},{8,10},{9,13},{10,... | collective-permute-start | bytes 1572872 | tf_op jit(solution)/shard_map/ppermute | solution.py:429
  21.8 13.6 %collective-permute-start.6 = (bf16[512,256]{1,0:T(8,128)(2,1)S(1)}, bf16[512,256]{1,0:T(8,128)(2,1)S(1)}, u32[]{:S(2)}, u32[]{:S(2)}) collective-permute-start(bf16[512,256]{1,0:T(8,128)(2,1)S(1)} %get-tuple-element.63), channel_id=1, source_target_pairs={{8,24},{24,8},{9,25},{25,9},{10,26},{26,10},{11,27},{27,11},{12,28... | collective-permute-start | bytes 786440 | tf_op jit(solution)/shard_map/ppermute | solution.py:472
  36.6 7.7 %collective-permute-start.11 = (bf16[512,512]{1,0:T(8,128)(2,1)S(1)}, bf16[512,512]{1,0:T(8,128)(2,1)S(1)}, u32[]{:S(2)}, u32[]{:S(2)}) collective-permute-start(bf16[512,512]{1,0:T(8,128)(2,1)S(1)} %collective-permute-done.8.mine_0), channel_id=1, source_target_pairs={{0,1},{1,0},{2,3},{3,2},{4,5},{5,4},{6,7},{7,6},{8,9},{9,8},{10,11... | collective-permute-start | bytes 1572872 | tf_op jit(solution)/shard_map/ppermute | solution.py:35
  36.7 9.5 %collective-permute-start.12 = (bf16[512,512]{1,0:T(8,128)(2,1)S(1)}, bf16[512,512]{1,0:T(8,128)(2,1)S(1)}, u32[]{:S(2)}, u32[]{:S(2)}) collective-permute-start(bf16[512,512]{1,0:T(8,128)(2,1)S(1)} %collective-permute-done.10.mine_1), channel_id=1, source_target_pairs={{0,1},{1,0},{2,3},{3,2},{4,5},{5,4},{6,7},{7,6},{8,9},{9,8},{10,11... | collective-permute-start | bytes 1572872 | tf_op jit(solution)/shard_map/ppermute | solution.py:35
  37.2 9.4 %collective-permute-start.17 = (bf16[256,512]{1,0:T(8,128)(2,1)S(1)}, bf16[256,512]{1,0:T(8,128)(2,1)S(1)}, u32[]{:S(2)}, u32[]{:S(2)}) collective-permute-start(bf16[256,512]{1,0:T(8,128)(2,1)S(1)} %get-tuple-element.75.refs_3_), channel_id=1, source_target_pairs={{0,2},{1,5},{2,0},{3,7},{4,6},{5,1},{6,4},{7,3},{8,10},{9,13},{10,... | collective-permute-start | bytes 786440 | tf_op jit(solution)/shard_map/ppermute | solution.py:429
  39.9 8.5 %collective-permute-start.16 = (bf16[256,512]{1,0:T(8,128)(2,1)S(1)}, bf16[256,512]{1,0:T(8,128)(2,1)S(1)}, u32[]{:S(2)}, u32[]{:S(2)}) collective-permute-start(bf16[256,512]{1,0:T(8,128)(2,1)S(1)} %get-tuple-element.74.refs_2_), channel_id=1, source_target_pairs={{0,4},{1,3},{2,6},{3,1},{4,0},{5,7},{6,2},{7,5},{8,12},{9,11},{10,... | collective-permute-start | bytes 786440 | tf_op jit(solution)/shard_map/ppermute | solution.py:429
  42.6 9.2 %collective-permute-start.14 = (bf16[256,512]{1,0:T(8,128)(2,1)S(1)}, bf16[256,512]{1,0:T(8,128)(2,1)S(1)}, u32[]{:S(2)}, u32[]{:S(2)}) collective-permute-start(bf16[256,512]{1,0:T(8,128)(2,1)S(1)} %get-tuple-element.73.refs_1_), channel_id=1, source_target_pairs={{0,2},{1,5},{2,0},{3,7},{4,6},{5,1},{6,4},{7,3},{8,10},{9,13},{10,... | collective-permute-start | bytes 786440 | tf_op jit(solution)/shard_map/ppermute | solution.py:429
  44.4 9.1 %collective-permute-start.9 = (bf16[256,512]{1,0:T(8,128)(2,1)S(1)}, bf16[256,512]{1,0:T(8,128)(2,1)S(1)}, u32[]{:S(2)}, u32[]{:S(2)}) collective-permute-start(bf16[256,512]{1,0:T(8,128)(2,1)S(1)} %get-tuple-element.72.refs_0_), channel_id=1, source_target_pairs={{0,4},{1,3},{2,6},{3,1},{4,0},{5,7},{6,2},{7,5},{8,12},{9,11},{10,... | collective-permute-start | bytes 786440 | tf_op jit(solution)/shard_map/ppermute | solution.py:429
  46.8 12.2 %collective-permute-start.19 = (bf16[256,512]{1,0:T(8,128)(2,1)S(1)}, bf16[256,512]{1,0:T(8,128)(2,1)S(1)}, u32[]{:S(2)}, u32[]{:S(2)}) collective-permute-start(bf16[256,512]{1,0:T(8,128)(2,1)S(1)} %give.7), channel_id=1, source_target_pairs={{0,4},{1,3},{2,6},{3,1},{4,0},{5,7},{6,2},{7,5},{8,12},{9,11},{10,... | collective-permute-start | bytes 786440 | tf_op jit(solution)/shard_map/ppermute | solution.py:429
  48.7 10.4 %collective-permute-start.18 = (bf16[256,512]{1,0:T(8,128)(2,1)S(1)}, bf16[256,512]{1,0:T(8,128)(2,1)S(1)}, u32[]{:S(2)}, u32[]{:S(2)}) collective-permute-start(bf16[256,512]{1,0:T(8,128)(2,1)S(1)} %give.6), channel_id=1, source_target_pairs={{0,2},{1,5},{2,0},{3,7},{4,6},{5,1},{6,4},{7,3},{8,10},{9,13},{10,... | collective-permute-start | bytes 786440 | tf_op jit(solution)/shard_map/ppermute | solution.py:429
  52.1 11.0 %collective-permute-start.15 = (bf16[256,512]{1,0:T(8,128)(2,1)S(1)}, bf16[256,512]{1,0:T(8,128)(2,1)S(1)}, u32[]{:S(2)}, u32[]{:S(2)}) collective-permute-start(bf16[256,512]{1,0:T(8,128)(2,1)S(1)} %give.5), channel_id=1, source_target_pairs={{0,4},{1,3},{2,6},{3,1},{4,0},{5,7},{6,2},{7,5},{8,12},{9,11},{10,... | collective-permute-start | bytes 786440 | tf_op jit(solution)/shard_map/ppermute | solution.py:429
  53.8 9.4 %collective-permute-start.13 = (bf16[256,512]{1,0:T(8,128)(2,1)S(1)}, bf16[256,512]{1,0:T(8,128)(2,1)S(1)}, u32[]{:S(2)}, u32[]{:S(2)}) collective-permute-start(bf16[256,512]{1,0:T(8,128)(2,1)S(1)} %give.4), channel_id=1, source_target_pairs={{0,2},{1,5},{2,0},{3,7},{4,6},{5,1},{6,4},{7,3},{8,10},{9,13},{10,... | collective-permute-start | bytes 786440 | tf_op jit(solution)/shard_map/ppermute | solution.py:429

commit v22 on v21

--- a/solution.py
+++ b/solution.py
@@ -466,9 +466,10 @@
             "query_gate",
         )
 
-    def exchange(message, lowers, hop):
+    def exchange(message, lowers, hop, two_way=True):
         pairs = [(at, at + hop) for at in lowers]
-        pairs += [(upper, at) for at, upper in pairs] if hop > 1 else [(ctx - 1, 0)]
+        if two_way:
+            pairs += [(upper, at) for at, upper in pairs] if hop > 1 else [(ctx - 1, 0)]
         return lax.ppermute(message, "ctx", pairs)
 
     projected = list(query_gate(0, decay))
@@ -482,7 +483,7 @@
         if 2 * hop >= ctx:
             break
         unchanged = exchanges(ctx, 2 * hop)[0]
-        early = [exchange(message, unchanged, 2 * hop)]
+        early = [exchange(message, unchanged, 2 * hop, two_way=False)]
         old = [] if entering is None else [entering]
         last = 4 * hop >= ctx
         entering, message, *windows = kernel_call(

time: 64.4 us -> 58.1 us (0.902)
  the two profiles are of different devices: /device:TPU:0 before, /device:TPU:24 now
where the time goes in v22:
time: 58.1 us; the launch traced here: 57.7 us
  Pallas kernels  24 us (41%)
  starting transfers between devices  17.1 us (29%)
  waiting for transfers between devices  16.2 us (28%)
    pallas_call x15, Pallas kernels, kernel_call(): pl.pallas_call(kernel, in_specs=[pl.BlockSpec(memory_space=pltpu.VMEM)] *...  14.8 us
    ppermute x10, starting transfers between devices, trade(): return lax.ppermute(value, ('tp', 'fsdp'), partners[role])  12.4 us
    ppermute x10, waiting for transfers between devices, trade(): return lax.ppermute(value, ('tp', 'fsdp'), partners[role])  8.47 us
    ppermute x3, waiting for transfers between devices, exchange(): return lax.ppermute(message, 'ctx', pairs)  7.72 us
    pallas_call x2, Pallas kernels, loading_call(): pl.pallas_call(kernel, in_specs=[pl.BlockSpec(memory_space=pltpu.HBM)] *...  7.53 us
    ppermute x3, starting transfers between devices, exchange(): return lax.ppermute(message, 'ctx', pairs)  3.01 us
    ppermute x7, starting transfers between devices, swap(): lax.ppermute(value, axis, [(place, place ^ mask) for place in range(size)])  1.71 us
    pallas_call x2, Pallas kernels, on_device(): pl.pallas_call(functools.partial(finish_kernel, part_order), in_specs=[pl...  1.7 us
  transfers between devices with their start and end apart: 20, of which 7 were waited for; matrix products, arithmetic and copies ran while one was open for 0% of the time, Pallas kernels for 40%

profile of v22, /device:TPU:24, one launch (start us, length us, event | category | flops | bytes accessed | tf_op | source)
XLA Modules:
  0.0 57.7 jit_solution(5195995718772848163)
XLA Ops:
  0.0 0.5 collective-permute-start.2
  0.5 4.3 %key_value_own.1 = (bf16[1024,1024]{1,0:T(8,128)(2,1)S(1)}, bf16[1024,1024]{1,0:T(8,128)(2,1)S(1)}, f32[1024,512]{1,0:T(8,128)S(1)}, f32[1024,512]{1,0:T(8,128)S...) custom-call(bf16[1024,2048]{1,0:T(8,128)(2,1)} %bitcast.4, ...), custom_call_target="tpu_custom_call" | custom-call | flops 1 | bytes 1 | tf_op jit(solution)/shard_map/key_value_own/pallas_call | solution.py:56
  4.9 3.2 %key_value.1 = (bf16[1024,512]{1,0:T(8,128)(2,1)S(1)}, bf16[1024,512]{1,0:T(8,128)(2,1)S(1)}, bf16[1024,512]{1,0:T(8,128)(2,1)S(1)}, bf16[1024,512]{1,0:T(8,128)...) custom-call(bf16[1024,512]{1,0:T(8,128)(2,1)} %wq_far.1, ...), custom_call_target="tpu_custom_call" | custom-call | flops 1 | bytes 1 | tf_op jit(solution)/shard_map/key_value/pallas_call | solution.py:56
  8.2 0.5 collective-permute-start.3
  8.9 1.8 %collective-permute-start.8 = (bf16[512,512]{1,0:T(8,128)(2,1)S(1)}, bf16[512,512]{1,0:T(8,128)(2,1)S(1)}, u32[]{:S(2)}, u32[]{:S(2)}) collective-permute-start(bf16[512,512]{1,0:T(8,128)(2,1)S(1)} %get-tuple-element.67), channel_id=1, source_target_pairs={{0,2},{1,5},{2,0},{3,7},{4,6},{5,1},{6,4},{7,3},{8,10},{9,13},{10,... | collective-permute-start | bytes 1572872 | tf_op jit(solution)/shard_map/ppermute | solution.py:429
  10.6 0.7 %collective-permute-start.7 = (bf16[528,256]{1,0:T(8,128)(2,1)S(1)}, bf16[528,256]{1,0:T(8,128)(2,1)S(1)}, u32[]{:S(2)}, u32[]{:S(2)}) collective-permute-start(bf16[528,256]{1,0:T(8,128)(2,1)S(1)} %get-tuple-element.61.sent), channel_id=1, source_target_pairs={{0,16},{1,17},{2,18},{3,19},{4,20},{5,21},{6,22},{7,23}} | collective-permute-start | bytes 811016 | tf_op jit(solution)/shard_map/ppermute | solution.py:473
  11.3 1.2 %collective-permute-start.10 = (bf16[512,512]{1,0:T(8,128)(2,1)S(1)}, bf16[512,512]{1,0:T(8,128)(2,1)S(1)}, u32[]{:S(2)}, u32[]{:S(2)}) collective-permute-start(bf16[512,512]{1,0:T(8,128)(2,1)S(1)} %get-tuple-element.77), channel_id=1, source_target_pairs={{0,2},{1,5},{2,0},{3,7},{4,6},{5,1},{6,4},{7,3},{8,10},{9,13},{10,... | collective-permute-start | bytes 1572872 | tf_op jit(solution)/shard_map/ppermute | solution.py:429
  12.5 3.1 %query_gate.2 = (bf16[512,512]{1,0:T(8,128)(2,1)S(1)}, f32[512,512]{1,0:T(8,128)S(1)}, f32[512,512]{1,0:T(8,128)S(1)}) custom-call(bf16[1024,1024]{1,0:T(8,128)(2,1)S(1)} %get-tuple-element.54.x_own, bf16[1024,1024]{1,0:T(8,128)(2,1)S(1)} %get-tuple-element.47.x.x_other, bf16[1024,512]{1,0:T(8,128)(2,1)S(1)} %get-tuple-element.55.wq, ...), custom_call_target="tpu_custom_call" | custom-call | flops 1 | bytes 1 | tf_op jit(solution)/shard_map/query_gate/pallas_call | solution.py:40
  15.6 2.0 %collective-permute-done.5.refs_0_ = bf16[528,256]{1,0:T(8,128)(2,1)S(1)} collective-permute-done((bf16[528,256]{1,0:T(8,128)(2,1)S(1)}, bf16[528,256]{1,0:T(8,128)(2,1)S(1)}, u32[]{:S(2)}, u32[]{:S(2)}) %collective-permute-start.5) | collective-permute-done | bytes 270368 | tf_op jit(solution)/shard_map/ppermute | solution.py:473
  17.8 2.3 %collective-permute-start.6 = (bf16[512,256]{1,0:T(8,128)(2,1)S(1)}, bf16[512,256]{1,0:T(8,128)(2,1)S(1)}, u32[]{:S(2)}, u32[]{:S(2)}) collective-permute-start(bf16[512,256]{1,0:T(8,128)(2,1)S(1)} %get-tuple-element.63), channel_id=1, source_target_pairs={{8,24},{24,8},{9,25},{25,9},{10,26},{26,10},{11,27},{27,11},{12,28... | collective-permute-start | bytes 786440 | tf_op jit(solution)/shard_map/ppermute | solution.py:473
  20.1 3.1 %query_gate.3 = (bf16[512,512]{1,0:T(8,128)(2,1)S(1)}, f32[512,512]{1,0:T(8,128)S(1)}, f32[512,512]{1,0:T(8,128)S(1)}) custom-call(bf16[1024,1024]{1,0:T(8,128)(2,1)S(1)} %get-tuple-element.54.x_own, bf16[1024,1024]{1,0:T(8,128)(2,1)S(1)} %get-tuple-element.47.x.x_other, bf16[1024,512]{1,0:T(8,128)(2,1)S(1)} %get-tuple-element.55.wq, ...), custom_call_target="tpu_custom_call" | custom-call | flops 1 | bytes 1 | tf_op jit(solution)/shard_map/query_gate/pallas_call | solution.py:40
  23.2 5.7 %collective-permute-done.6.refs_0_ = bf16[512,256]{1,0:T(8,128)(2,1)S(1)} collective-permute-done((bf16[512,256]{1,0:T(8,128)(2,1)S(1)}, bf16[512,256]{1,0:T(8,128)(2,1)S(1)}, u32[]{:S(2)}, u32[]{:S(2)}) %collective-permute-start.6) | collective-permute-done | bytes 262176 | tf_op jit(solution)/shard_map/ppermute | solution.py:473
  28.9 1.2 %hidden.7 = (bf16[256,512]{1,0:T(8,128)(2,1)S(1)}, bf16[16,128]{1,0:T(8,128)(2,1)}) custom-call(f32[8,1024]{1,0:T(8,128)S(1)} %get-tuple-element.68.decay, bf16[2,512,256]{2,1,0:T(8,128)(2,1)S(1)} %get-tuple-element.52.before, f32[520,256]{1,0:T(8,128)S(1)} %get-tuple-element.62.entering, bf16[512,256]{1,0:T(8,128)(2,1)S(1)} %collective-permute-done.6.refs_0_, ...), custom_call_target="tpu_custom_call" | custom-call | flops 1 | bytes 1 | tf_op jit(solution)/shard_map/hidden/pallas_call | solution.py:40
  30.1 0.5 collective-permute-start.12
  30.6 1.5 %collective-permute-start.17 = (bf16[256,512]{1,0:T(8,128)(2,1)S(1)}, bf16[256,512]{1,0:T(8,128)(2,1)S(1)}, u32[]{:S(2)}, u32[]{:S(2)}) collective-permute-start(bf16[256,512]{1,0:T(8,128)(2,1)S(1)} %get-tuple-element.75.refs_3_), channel_id=1, source_target_pairs={{0,2},{1,5},{2,0},{3,7},{4,6},{5,1},{6,4},{7,3},{8,10},{9,13},{10,... | collective-permute-start | bytes 786440 | tf_op jit(solution)/shard_map/ppermute | solution.py:429
  32.1 1.2 %hidden.6 = (bf16[256,512]{1,0:T(8,128)(2,1)S(1)}, bf16[16,128]{1,0:T(8,128)(2,1)}) custom-call(f32[8,1024]{1,0:T(8,128)S(1)} %get-tuple-element.68.decay, bf16[2,512,256]{2,1,0:T(8,128)(2,1)S(1)} %get-tuple-element.52.before, f32[520,256]{1,0:T(8,128)S(1)} %get-tuple-element.62.entering, bf16[512,256]{1,0:T(8,128)(2,1)S(1)} %collective-permute-done.6.refs_0_, ...), custom_call_target="tpu_custom_call" | custom-call | flops 1 | bytes 1 | tf_op jit(solution)/shard_map/hidden/pallas_call | solution.py:40
  33.4 1.5 %collective-permute-start.16 = (bf16[256,512]{1,0:T(8,128)(2,1)S(1)}, bf16[256,512]{1,0:T(8,128)(2,1)S(1)}, u32[]{:S(2)}, u32[]{:S(2)}) collective-permute-start(bf16[256,512]{1,0:T(8,128)(2,1)S(1)} %get-tuple-element.74.refs_2_), channel_id=1, source_target_pairs={{0,4},{1,3},{2,6},{3,1},{4,0},{5,7},{6,2},{7,5},{8,12},{9,11},{10,... | collective-permute-start | bytes 786440 | tf_op jit(solution)/shard_map/ppermute | solution.py:429
  34.9 1.2 %hidden.5 = (bf16[256,512]{1,0:T(8,128)(2,1)S(1)}, bf16[16,128]{1,0:T(8,128)(2,1)}) custom-call(f32[8,1024]{1,0:T(8,128)S(1)} %get-tuple-element.68.decay, bf16[2,512,256]{2,1,0:T(8,128)(2,1)S(1)} %get-tuple-element.52.before, f32[520,256]{1,0:T(8,128)S(1)} %get-tuple-element.62.entering, bf16[512,256]{1,0:T(8,128)(2,1)S(1)} %collective-permute-done.6.refs_0_, ...), custom_call_target="tpu_custom_call" | custom-call | flops 1 | bytes 1 | tf_op jit(solution)/shard_map/hidden/pallas_call | solution.py:40
  36.1 0.5 collective-permute-start.14
  36.6 1.2 %hidden.4 = (bf16[256,512]{1,0:T(8,128)(2,1)S(1)}, bf16[16,128]{1,0:T(8,128)(2,1)}) custom-call(f32[8,1024]{1,0:T(8,128)S(1)} %get-tuple-element.68.decay, bf16[2,512,256]{2,1,0:T(8,128)(2,1)S(1)} %get-tuple-element.52.before, f32[520,256]{1,0:T(8,128)S(1)} %get-tuple-element.62.entering, bf16[512,256]{1,0:T(8,128)(2,1)S(1)} %collective-permute-done.6.refs_0_, ...), custom_call_target="tpu_custom_call" | custom-call | flops 1 | bytes 1 | tf_op jit(solution)/shard_map/hidden/pallas_call | solution.py:40
  37.9 0.5 collective-permute-start.9
  38.4 1.3 %own_products.1 = (f32[512,1024]{1,0:T(8,128)S(1)}, f32[512,1024]{1,0:T(8,128)S(1)}) custom-call(bf16[512,1024]{1,0:T(8,128)(2,1)S(1)} %get-tuple-element.66.first.own_first, bf16[512,1024]{1,0:T(8,128)(2,1)S(1)} %collective-permute-done.second.own_second, bf16[256,512]{1,0:T(8,128)(2,1)S(1)} %get-tuple-element.72.refs_0_, ...), custom_call_target="tpu_custom_call" | custom-call | flops 1 | bytes 1 | tf_op jit(solution)/shard_map/own_products/pallas_call | solution.py:40
  40.3 1.6 %collective-permute-start.19 = (bf16[256,512]{1,0:T(8,128)(2,1)S(1)}, bf16[256,512]{1,0:T(8,128)(2,1)S(1)}, u32[]{:S(2)}, u32[]{:S(2)}) collective-permute-start(bf16[256,512]{1,0:T(8,128)(2,1)S(1)} %give.7), channel_id=1, source_target_pairs={{0,4},{1,3},{2,6},{3,1},{4,0},{5,7},{6,2},{7,5},{8,12},{9,11},{10,... | collective-permute-start | bytes 786440 | tf_op jit(solution)/shard_map/ppermute | solution.py:429
  42.2 1.5 %collective-permute-start.18 = (bf16[256,512]{1,0:T(8,128)(2,1)S(1)}, bf16[256,512]{1,0:T(8,128)(2,1)S(1)}, u32[]{:S(2)}, u32[]{:S(2)}) collective-permute-start(bf16[256,512]{1,0:T(8,128)(2,1)S(1)} %give.6), channel_id=1, source_target_pairs={{0,2},{1,5},{2,0},{3,7},{4,6},{5,1},{6,4},{7,3},{8,10},{9,13},{10,... | collective-permute-start | bytes 786440 | tf_op jit(solution)/shard_map/ppermute | solution.py:429
  43.7 1.6 %collective-permute-done.14.far.refs_1_ = bf16[256,512]{1,0:T(8,128)(2,1)S(1)} collective-permute-done((bf16[256,512]{1,0:T(8,128)(2,1)S(1)}, bf16[256,512]{1,0:T(8,128)(2,1)S(1)}, u32[]{:S(2)}, u32[]{:S(2)}) %collective-permute-start.14) | collective-permute-done | bytes 262176 | tf_op jit(solution)/shard_map/ppermute | solution.py:429
  45.6 1.1 %collective-permute-start.15 = (bf16[256,512]{1,0:T(8,128)(2,1)S(1)}, bf16[256,512]{1,0:T(8,128)(2,1)S(1)}, u32[]{:S(2)}, u32[]{:S(2)}) collective-permute-start(bf16[256,512]{1,0:T(8,128)(2,1)S(1)} %give.5), channel_id=1, source_target_pairs={{0,4},{1,3},{2,6},{3,1},{4,0},{5,7},{6,2},{7,5},{8,12},{9,11},{10,... | collective-permute-start | bytes 786440 | tf_op jit(solution)/shard_map/ppermute | solution.py:429
  47.4 1.2 %collective-permute-start.13 = (bf16[256,512]{1,0:T(8,128)(2,1)S(1)}, bf16[256,512]{1,0:T(8,128)(2,1)S(1)}, u32[]{:S(2)}, u32[]{:S(2)}) collective-permute-start(bf16[256,512]{1,0:T(8,128)(2,1)S(1)} %give.4), channel_id=1, source_target_pairs={{0,2},{1,5},{2,0},{3,7},{4,6},{5,1},{6,4},{7,3},{8,10},{9,13},{10,... | collective-permute-start | bytes 786440 | tf_op jit(solution)/shard_map/ppermute | solution.py:429
  48.6 0.7 %keep.1 = (f32[512,512]{1,0:T(8,128)S(1)}, f32[512,512]{1,0:T(8,128)S(1)}) custom-call(bf16[256,512]{1,0:T(8,128)(2,1)S(1)} %collective-permute-done.9.far.refs_0_, bf16[256,512]{1,0:T(8,128)(2,1)S(1)} %collective-permute-done.14.far.refs_1_, bf16[256,512]{1,0:T(8,128)(2,1)S(1)} %collective-permute-done.16.refs_2_.far, ...), custom_call_target="tpu_custom_call" | custom-call | flops 1 | bytes 1 | tf_op jit(solution)/shard_map/keep/pallas_call | solution.py:40
  49.3 3.4 %collective-permute-done.19.refs_1_ = bf16[256,512]{1,0:T(8,128)(2,1)S(1)} collective-permute-done((bf16[256,512]{1,0:T(8,128)(2,1)S(1)}, bf16[256,512]{1,0:T(8,128)(2,1)S(1)}, u32[]{:S(2)}, u32[]{:S(2)}) %collective-permute-start.19) | collective-permute-done | bytes 262176 | tf_op jit(solution)/shard_map/ppermute | solution.py:429
  52.7 0.9 %finish.2.refs_4_ = bf16[1,1024,512]{2,1,0:T(8,128)(2,1)} custom-call(bf16[256,512]{1,0:T(8,128)(2,1)S(1)} %collective-permute-done.18.refs_0_, bf16[256,512]{1,0:T(8,128)(2,1)S(1)} %collective-permute-done.19.refs_1_, f32[512,512]{1,0:T(8,128)S(1)} %get-tuple-element.83.refs_2_, f32[512,512]{1,0:T(8,128)S(1)} %get-tuple-element.84.refs_3_), custom_call_target="tpu_custom_call" | custom-call | tf_op jit(solution)/shard_map/finish/pallas_call | solution.py:559
  53.6 3.0 %collective-permute-done.15.refs_1_ = bf16[256,512]{1,0:T(8,128)(2,1)S(1)} collective-permute-done((bf16[256,512]{1,0:T(8,128)(2,1)S(1)}, bf16[256,512]{1,0:T(8,128)(2,1)S(1)}, u32[]{:S(2)}, u32[]{:S(2)}) %collective-permute-start.15) | collective-permute-done | bytes 262176 | tf_op jit(solution)/shard_map/ppermute | solution.py:429
  56.7 0.9 %finish.3 = bf16[1,1024,512]{2,1,0:T(8,128)(2,1)} custom-call(bf16[256,512]{1,0:T(8,128)(2,1)S(1)} %collective-permute-done.13.refs_0_, bf16[256,512]{1,0:T(8,128)(2,1)S(1)} %collective-permute-done.15.refs_1_, f32[512,512]{1,0:T(8,128)S(1)} %get-tuple-element.83.refs_2_, f32[512,512]{1,0:T(8,128)S(1)} %get-tuple-element.84.refs_3_, ...), custom_call_target="tpu_custom_call", output_to_operand_aliasing={{}: (4, {})} | custom-call | tf_op jit(solution)/shard_map/finish/pallas_call | solution.py:559
  (27 shorter events, 2.3 us)
Async XLA Ops:
  0.0 4.9 %collective-permute-start.1 = (bf16[1024,512]{1,0:T(8,128)(2,1)}, bf16[1024,512]{1,0:T(8,128)(2,1)S(1)}, u32[]{:S(2)}, u32[]{:S(2)}) collective-permute-start(bf16[1024,512]{1,0:T(8,128)(2,1)} %wk_far.1), channel_id=1, source_target_pairs={{0,1},{1,0},{2,3},{3,2},{4,5},{5,4},{6,7},{7,6},{8,9},{9,8},{10,11... | collective-permute-start | bytes 3145736 | tf_op jit(solution)/shard_map/ppermute | solution.py:35
  0.0 4.9 %collective-permute-start.2 = (bf16[1024,512]{1,0:T(8,128)(2,1)}, bf16[1024,512]{1,0:T(8,128)(2,1)S(1)}, u32[]{:S(2)}, u32[]{:S(2)}) collective-permute-start(bf16[1024,512]{1,0:T(8,128)(2,1)} %wv_far.1), channel_id=1, source_target_pairs={{0,1},{1,0},{2,3},{3,2},{4,5},{5,4},{6,7},{7,6},{8,9},{9,8},{10,11... | collective-permute-start | bytes 3145736 | tf_op jit(solution)/shard_map/ppermute | solution.py:35
  4.8 3.9 %collective-permute-start = (bf16[512,1024]{1,0:T(8,128)(2,1)S(1)}, bf16[512,1024]{1,0:T(8,128)(2,1)S(1)}, u32[]{:S(2)}, u32[]{:S(2)}) collective-permute-start(bf16[512,1024]{1,0:T(8,128)(2,1)S(1)} %get-tuple-element.66.first.own_first), channel_id=1, source_target_pairs={{0,1},{1,0},{2,3},{3,2},{4,5},{5,4},{6,7},{7,6},{8,9},{9,8},{10,11... | collective-permute-start | bytes 3145736 | tf_op jit(solution)/shard_map/ppermute | solution.py:35
  8.2 3.2 %collective-permute-start.3 = (bf16[1024,512]{1,0:T(8,128)(2,1)S(1)}, bf16[1024,512]{1,0:T(8,128)(2,1)S(1)}, u32[]{:S(2)}, u32[]{:S(2)}) collective-permute-start(bf16[1024,512]{1,0:T(8,128)(2,1)S(1)} %get-tuple-element.55.wq), channel_id=1, source_target_pairs={{0,1},{1,0},{2,3},{3,2},{4,5},{5,4},{6,7},{7,6},{8,9},{9,8},{10,11... | collective-permute-start | bytes 3145736 | tf_op jit(solution)/shard_map/ppermute | solution.py:35
  8.7 3.8 %collective-permute-start.4 = (bf16[1024,512]{1,0:T(8,128)(2,1)S(1)}, bf16[1024,512]{1,0:T(8,128)(2,1)S(1)}, u32[]{:S(2)}, u32[]{:S(2)}) collective-permute-start(bf16[1024,512]{1,0:T(8,128)(2,1)S(1)} %get-tuple-element.56.wg), channel_id=1, source_target_pairs={{0,1},{1,0},{2,3},{3,2},{4,5},{5,4},{6,7},{7,6},{8,9},{9,8},{10,11... | collective-permute-start | bytes 3145736 | tf_op jit(solution)/shard_map/ppermute | solution.py:35
  8.8 8.8 %collective-permute-start.5 = (bf16[528,256]{1,0:T(8,128)(2,1)S(1)}, bf16[528,256]{1,0:T(8,128)(2,1)S(1)}, u32[]{:S(2)}, u32[]{:S(2)}) collective-permute-start(bf16[528,256]{1,0:T(8,128)(2,1)S(1)} %get-tuple-element.61.sent), channel_id=1, source_target_pairs={{0,8},{8,16},{16,24},{24,0},{1,9},{9,17},{17,25},{25,1},{2,10},{10... | collective-permute-start | bytes 811016 | tf_op jit(solution)/shard_map/ppermute | solution.py:473
  8.9 11.3 %collective-permute-start.8 = (bf16[512,512]{1,0:T(8,128)(2,1)S(1)}, bf16[512,512]{1,0:T(8,128)(2,1)S(1)}, u32[]{:S(2)}, u32[]{:S(2)}) collective-permute-start(bf16[512,512]{1,0:T(8,128)(2,1)S(1)} %get-tuple-element.67), channel_id=1, source_target_pairs={{0,2},{1,5},{2,0},{3,7},{4,6},{5,1},{6,4},{7,3},{8,10},{9,13},{10,... | collective-permute-start | bytes 1572872 | tf_op jit(solution)/shard_map/ppermute | solution.py:429
  10.6 9.5 %collective-permute-start.7 = (bf16[528,256]{1,0:T(8,128)(2,1)S(1)}, bf16[528,256]{1,0:T(8,128)(2,1)S(1)}, u32[]{:S(2)}, u32[]{:S(2)}) collective-permute-start(bf16[528,256]{1,0:T(8,128)(2,1)S(1)} %get-tuple-element.61.sent), channel_id=1, source_target_pairs={{0,16},{1,17},{2,18},{3,19},{4,20},{5,21},{6,22},{7,23}} | collective-permute-start | bytes 811016 | tf_op jit(solution)/shard_map/ppermute | solution.py:473
  11.3 18.8 %collective-permute-start.10 = (bf16[512,512]{1,0:T(8,128)(2,1)S(1)}, bf16[512,512]{1,0:T(8,128)(2,1)S(1)}, u32[]{:S(2)}, u32[]{:S(2)}) collective-permute-start(bf16[512,512]{1,0:T(8,128)(2,1)S(1)} %get-tuple-element.77), channel_id=1, source_target_pairs={{0,2},{1,5},{2,0},{3,7},{4,6},{5,1},{6,4},{7,3},{8,10},{9,13},{10,... | collective-permute-start | bytes 1572872 | tf_op jit(solution)/shard_map/ppermute | solution.py:429
  17.8 11.1 %collective-permute-start.6 = (bf16[512,256]{1,0:T(8,128)(2,1)S(1)}, bf16[512,256]{1,0:T(8,128)(2,1)S(1)}, u32[]{:S(2)}, u32[]{:S(2)}) collective-permute-start(bf16[512,256]{1,0:T(8,128)(2,1)S(1)} %get-tuple-element.63), channel_id=1, source_target_pairs={{8,24},{24,8},{9,25},{25,9},{10,26},{26,10},{11,27},{27,11},{12,28... | collective-permute-start | bytes 786440 | tf_op jit(solution)/shard_map/ppermute | solution.py:473
  30.1 7.7 %collective-permute-start.11 = (bf16[512,512]{1,0:T(8,128)(2,1)S(1)}, bf16[512,512]{1,0:T(8,128)(2,1)S(1)}, u32[]{:S(2)}, u32[]{:S(2)}) collective-permute-start(bf16[512,512]{1,0:T(8,128)(2,1)S(1)} %collective-permute-done.8.mine_0), channel_id=1, source_target_pairs={{0,1},{1,0},{2,3},{3,2},{4,5},{5,4},{6,7},{7,6},{8,9},{9,8},{10,11... | collective-permute-start | bytes 1572872 | tf_op jit(solution)/shard_map/ppermute | solution.py:35
  30.1 9.6 %collective-permute-start.12 = (bf16[512,512]{1,0:T(8,128)(2,1)S(1)}, bf16[512,512]{1,0:T(8,128)(2,1)S(1)}, u32[]{:S(2)}, u32[]{:S(2)}) collective-permute-start(bf16[512,512]{1,0:T(8,128)(2,1)S(1)} %collective-permute-done.10.mine_1), channel_id=1, source_target_pairs={{0,1},{1,0},{2,3},{3,2},{4,5},{5,4},{6,7},{7,6},{8,9},{9,8},{10,11... | collective-permute-start | bytes 1572872 | tf_op jit(solution)/shard_map/ppermute | solution.py:35
  30.6 9.4 %collective-permute-start.17 = (bf16[256,512]{1,0:T(8,128)(2,1)S(1)}, bf16[256,512]{1,0:T(8,128)(2,1)S(1)}, u32[]{:S(2)}, u32[]{:S(2)}) collective-permute-start(bf16[256,512]{1,0:T(8,128)(2,1)S(1)} %get-tuple-element.75.refs_3_), channel_id=1, source_target_pairs={{0,2},{1,5},{2,0},{3,7},{4,6},{5,1},{6,4},{7,3},{8,10},{9,13},{10,... | collective-permute-start | bytes 786440 | tf_op jit(solution)/shard_map/ppermute | solution.py:429
  33.4 8.5 %collective-permute-start.16 = (bf16[256,512]{1,0:T(8,128)(2,1)S(1)}, bf16[256,512]{1,0:T(8,128)(2,1)S(1)}, u32[]{:S(2)}, u32[]{:S(2)}) collective-permute-start(bf16[256,512]{1,0:T(8,128)(2,1)S(1)} %get-tuple-element.74.refs_2_), channel_id=1, source_target_pairs={{0,4},{1,3},{2,6},{3,1},{4,0},{5,7},{6,2},{7,5},{8,12},{9,11},{10,... | collective-permute-start | bytes 786440 | tf_op jit(solution)/shard_map/ppermute | solution.py:429
  36.1 9.2 %collective-permute-start.14 = (bf16[256,512]{1,0:T(8,128)(2,1)S(1)}, bf16[256,512]{1,0:T(8,128)(2,1)S(1)}, u32[]{:S(2)}, u32[]{:S(2)}) collective-permute-start(bf16[256,512]{1,0:T(8,128)(2,1)S(1)} %get-tuple-element.73.refs_1_), channel_id=1, source_target_pairs={{0,2},{1,5},{2,0},{3,7},{4,6},{5,1},{6,4},{7,3},{8,10},{9,13},{10,... | collective-permute-start | bytes 786440 | tf_op jit(solution)/shard_map/ppermute | solution.py:429
  37.9 9.2 %collective-permute-start.9 = (bf16[256,512]{1,0:T(8,128)(2,1)S(1)}, bf16[256,512]{1,0:T(8,128)(2,1)S(1)}, u32[]{:S(2)}, u32[]{:S(2)}) collective-permute-start(bf16[256,512]{1,0:T(8,128)(2,1)S(1)} %get-tuple-element.72.refs_0_), channel_id=1, source_target_pairs={{0,4},{1,3},{2,6},{3,1},{4,0},{5,7},{6,2},{7,5},{8,12},{9,11},{10,... | collective-permute-start | bytes 786440 | tf_op jit(solution)/shard_map/ppermute | solution.py:429
  40.3 12.4 %collective-permute-start.19 = (bf16[256,512]{1,0:T(8,128)(2,1)S(1)}, bf16[256,512]{1,0:T(8,128)(2,1)S(1)}, u32[]{:S(2)}, u32[]{:S(2)}) collective-permute-start(bf16[256,512]{1,0:T(8,128)(2,1)S(1)} %give.7), channel_id=1, source_target_pairs={{0,4},{1,3},{2,6},{3,1},{4,0},{5,7},{6,2},{7,5},{8,12},{9,11},{10,... | collective-permute-start | bytes 786440 | tf_op jit(solution)/shard_map/ppermute | solution.py:429
  42.2 10.5 %collective-permute-start.18 = (bf16[256,512]{1,0:T(8,128)(2,1)S(1)}, bf16[256,512]{1,0:T(8,128)(2,1)S(1)}, u32[]{:S(2)}, u32[]{:S(2)}) collective-permute-start(bf16[256,512]{1,0:T(8,128)(2,1)S(1)} %give.6), channel_id=1, source_target_pairs={{0,2},{1,5},{2,0},{3,7},{4,6},{5,1},{6,4},{7,3},{8,10},{9,13},{10,... | collective-permute-start | bytes 786440 | tf_op jit(solution)/shard_map/ppermute | solution.py:429
  45.6 11.0 %collective-permute-start.15 = (bf16[256,512]{1,0:T(8,128)(2,1)S(1)}, bf16[256,512]{1,0:T(8,128)(2,1)S(1)}, u32[]{:S(2)}, u32[]{:S(2)}) collective-permute-start(bf16[256,512]{1,0:T(8,128)(2,1)S(1)} %give.5), channel_id=1, source_target_pairs={{0,4},{1,3},{2,6},{3,1},{4,0},{5,7},{6,2},{7,5},{8,12},{9,11},{10,... | collective-permute-start | bytes 786440 | tf_op jit(solution)/shard_map/ppermute | solution.py:429
  47.4 9.3 %collective-permute-start.13 = (bf16[256,512]{1,0:T(8,128)(2,1)S(1)}, bf16[256,512]{1,0:T(8,128)(2,1)S(1)}, u32[]{:S(2)}, u32[]{:S(2)}) collective-permute-start(bf16[256,512]{1,0:T(8,128)(2,1)S(1)} %give.4), channel_id=1, source_target_pairs={{0,2},{1,5},{2,0},{3,7},{4,6},{5,1},{6,4},{7,3},{8,10},{9,13},{10,... | collective-permute-start | bytes 786440 | tf_op jit(solution)/shard_map/ppermute | solution.py:429

commit v23 on v19

--- a/solution.py
+++ b/solution.py
@@ -466,10 +466,14 @@
             "query_gate",
         )
 
-    def exchange(message, lowers, hop):
+    def exchange(message, lowers, hop, everyone=False):
         pairs = [(at, at + hop) for at in lowers]
-        if hop > 1:
+        if everyone and hop == 1:
+            pairs += [(ctx - 1, 0)]
+        elif everyone:
             pairs += [(upper, at) for at, upper in pairs]
+            busy = {at for pair in pairs for at in pair}
+            pairs += [(at, at) for at in range(ctx) if at not in busy]
         return lax.ppermute(message, "ctx", pairs)
 
     projected = list(query_gate(0, decay))
@@ -479,11 +483,11 @@
         first_set, *later_sets = exchanges(ctx, hop)
         later_sets = [lowers for lowers in later_sets if lowers]
         sets = later_sets + ([first_set] if first_set else [])
-        arrivals = [exchange(message, lowers, hop) for lowers in later_sets] + early
+        arrivals = [exchange(message, lowers, hop, everyone=hop == 1) for lowers in later_sets] + early
         if 2 * hop >= ctx:
             break
         unchanged = exchanges(ctx, 2 * hop)[0]
-        early = [exchange(message, unchanged, 2 * hop)]
+        early = [exchange(message, unchanged, 2 * hop, everyone=True)]
         old = [] if entering is None else [entering]
         last = 4 * hop >= ctx
         entering, message, *windows = kernel_call(

time: 60 us -> 58.8 us (0.980); the launches traced: 59.6 us -> 57.7 us
  starting transfers between devices: 17.6 us -> 16.1 us
    ppermute x3, starting transfers between devices: 4.23 us -> 1.96 us  [exchange(): return lax.ppermute(message, 'ctx', pairs)]
    ppermute x10, starting transfers between devices: 11.6 us -> 12.4 us  [trade(): return lax.ppermute(value, ('tp', 'fsdp'), partners[role])]
  transfers between devices with their start and end apart: 20 -> 20, of which waited for: 7 -> 7; matrix products, arithmetic and copies ran while one was open for 0% -> 0% of each run, Pallas kernels for 39% -> 40%
where the time goes in v23:
time: 58.8 us; the launch traced here: 57.7 us
  Pallas kernels  24 us (41%)
  waiting for transfers between devices  17.2 us (29%)
  starting transfers between devices  16.1 us (27%)
    pallas_call x15, Pallas kernels, kernel_call(): pl.pallas_call(kernel, in_specs=[pl.BlockSpec(memory_space=pltpu.VMEM)] *...  14.8 us
    ppermute x10, starting transfers between devices, trade(): return lax.ppermute(value, ('tp', 'fsdp'), partners[role])  12.4 us
    ppermute x3, waiting for transfers between devices, exchange(): return lax.ppermute(message, 'ctx', pairs)  8.74 us
    ppermute x10, waiting for transfers between devices, trade(): return lax.ppermute(value, ('tp', 'fsdp'), partners[role])  8.47 us
    pallas_call x2, Pallas kernels, loading_call(): pl.pallas_call(kernel, in_specs=[pl.BlockSpec(memory_space=pltpu.HBM)] *...  7.53 us
    ppermute x3, starting transfers between devices, exchange(): return lax.ppermute(message, 'ctx', pairs)  1.96 us
    ppermute x7, starting transfers between devices, swap(): lax.ppermute(value, axis, [(place, place ^ mask) for place in range(size)])  1.71 us
    pallas_call x2, Pallas kernels, on_device(): pl.pallas_call(functools.partial(finish_kernel, part_order), in_specs=[pl...  1.7 us
  transfers between devices with their start and end apart: 20, of which 7 were waited for; matrix products, arithmetic and copies ran while one was open for 0% of the time, Pallas kernels for 40%

profile of v23, /device:TPU:24, one launch (start us, length us, event | category | flops | bytes accessed | tf_op | source)
XLA Modules:
  0.0 57.7 jit_solution(18411822697127764651)
XLA Ops:
  0.0 0.5 collective-permute-start.2
  0.5 4.3 %key_value_own.1 = (bf16[1024,1024]{1,0:T(8,128)(2,1)S(1)}, bf16[1024,1024]{1,0:T(8,128)(2,1)S(1)}, f32[1024,512]{1,0:T(8,128)S(1)}, f32[1024,512]{1,0:T(8,128)S...) custom-call(bf16[1024,2048]{1,0:T(8,128)(2,1)} %bitcast.4, ...), custom_call_target="tpu_custom_call" | custom-call | flops 1 | bytes 1 | tf_op jit(solution)/shard_map/key_value_own/pallas_call | solution.py:56
  4.9 3.2 %key_value.1 = (bf16[1024,512]{1,0:T(8,128)(2,1)S(1)}, bf16[1024,512]{1,0:T(8,128)(2,1)S(1)}, bf16[1024,512]{1,0:T(8,128)(2,1)S(1)}, bf16[1024,512]{1,0:T(8,128)...) custom-call(bf16[1024,512]{1,0:T(8,128)(2,1)} %wq_far.1, ...), custom_call_target="tpu_custom_call" | custom-call | flops 1 | bytes 1 | tf_op jit(solution)/shard_map/key_value/pallas_call | solution.py:56
  8.2 0.5 collective-permute-start.3
  8.9 1.8 %collective-permute-start.8 = (bf16[512,512]{1,0:T(8,128)(2,1)S(1)}, bf16[512,512]{1,0:T(8,128)(2,1)S(1)}, u32[]{:S(2)}, u32[]{:S(2)}) collective-permute-start(bf16[512,512]{1,0:T(8,128)(2,1)S(1)} %get-tuple-element.67), channel_id=1, source_target_pairs={{0,2},{1,5},{2,0},{3,7},{4,6},{5,1},{6,4},{7,3},{8,10},{9,13},{10,... | collective-permute-start | bytes 1572872 | tf_op jit(solution)/shard_map/ppermute | solution.py:429
  10.6 0.7 %collective-permute-start.7 = (bf16[528,256]{1,0:T(8,128)(2,1)S(1)}, bf16[528,256]{1,0:T(8,128)(2,1)S(1)}, u32[]{:S(2)}, u32[]{:S(2)}) collective-permute-start(bf16[528,256]{1,0:T(8,128)(2,1)S(1)} %get-tuple-element.61.sent), channel_id=1, source_target_pairs={{0,16},{16,0},{8,8},{24,24},{1,17},{17,1},{9,9},{25,25},{2,18},{18... | collective-permute-start | bytes 811016 | tf_op jit(solution)/shard_map/ppermute | solution.py:477
  11.3 1.2 %collective-permute-start.10 = (bf16[512,512]{1,0:T(8,128)(2,1)S(1)}, bf16[512,512]{1,0:T(8,128)(2,1)S(1)}, u32[]{:S(2)}, u32[]{:S(2)}) collective-permute-start(bf16[512,512]{1,0:T(8,128)(2,1)S(1)} %get-tuple-element.77), channel_id=1, source_target_pairs={{0,2},{1,5},{2,0},{3,7},{4,6},{5,1},{6,4},{7,3},{8,10},{9,13},{10,... | collective-permute-start | bytes 1572872 | tf_op jit(solution)/shard_map/ppermute | solution.py:429
  12.5 3.1 %query_gate.2 = (bf16[512,512]{1,0:T(8,128)(2,1)S(1)}, f32[512,512]{1,0:T(8,128)S(1)}, f32[512,512]{1,0:T(8,128)S(1)}) custom-call(bf16[1024,1024]{1,0:T(8,128)(2,1)S(1)} %get-tuple-element.54.x_own, bf16[1024,1024]{1,0:T(8,128)(2,1)S(1)} %get-tuple-element.47.x.x_other, bf16[1024,512]{1,0:T(8,128)(2,1)S(1)} %get-tuple-element.55.wq, ...), custom_call_target="tpu_custom_call" | custom-call | flops 1 | bytes 1 | tf_op jit(solution)/shard_map/query_gate/pallas_call | solution.py:40
  15.6 2.0 %collective-permute-done.5.refs_0_ = bf16[528,256]{1,0:T(8,128)(2,1)S(1)} collective-permute-done((bf16[528,256]{1,0:T(8,128)(2,1)S(1)}, bf16[528,256]{1,0:T(8,128)(2,1)S(1)}, u32[]{:S(2)}, u32[]{:S(2)}) %collective-permute-start.5) | collective-permute-done | bytes 270368 | tf_op jit(solution)/shard_map/ppermute | solution.py:477
  17.8 1.3 %collective-permute-start.6 = (bf16[512,256]{1,0:T(8,128)(2,1)S(1)}, bf16[512,256]{1,0:T(8,128)(2,1)S(1)}, u32[]{:S(2)}, u32[]{:S(2)}) collective-permute-start(bf16[512,256]{1,0:T(8,128)(2,1)S(1)} %get-tuple-element.63), channel_id=1, source_target_pairs={{8,24},{9,25},{10,26},{11,27},{12,28},{13,29},{14,30},{15,31}} | collective-permute-start | bytes 786440 | tf_op jit(solution)/shard_map/ppermute | solution.py:477
  19.1 3.1 %query_gate.3 = (bf16[512,512]{1,0:T(8,128)(2,1)S(1)}, f32[512,512]{1,0:T(8,128)S(1)}, f32[512,512]{1,0:T(8,128)S(1)}) custom-call(bf16[1024,1024]{1,0:T(8,128)(2,1)S(1)} %get-tuple-element.54.x_own, bf16[1024,1024]{1,0:T(8,128)(2,1)S(1)} %get-tuple-element.47.x.x_other, bf16[1024,512]{1,0:T(8,128)(2,1)S(1)} %get-tuple-element.55.wq, ...), custom_call_target="tpu_custom_call" | custom-call | flops 1 | bytes 1 | tf_op jit(solution)/shard_map/query_gate/pallas_call | solution.py:40
  22.2 6.7 %collective-permute-done.6.refs_0_ = bf16[512,256]{1,0:T(8,128)(2,1)S(1)} collective-permute-done((bf16[512,256]{1,0:T(8,128)(2,1)S(1)}, bf16[512,256]{1,0:T(8,128)(2,1)S(1)}, u32[]{:S(2)}, u32[]{:S(2)}) %collective-permute-start.6) | collective-permute-done | bytes 262176 | tf_op jit(solution)/shard_map/ppermute | solution.py:477
  28.9 1.2 %hidden.7 = (bf16[256,512]{1,0:T(8,128)(2,1)S(1)}, bf16[16,128]{1,0:T(8,128)(2,1)}) custom-call(f32[8,1024]{1,0:T(8,128)S(1)} %get-tuple-element.68.decay, bf16[2,512,256]{2,1,0:T(8,128)(2,1)S(1)} %get-tuple-element.52.before, f32[520,256]{1,0:T(8,128)S(1)} %get-tuple-element.62.entering, bf16[512,256]{1,0:T(8,128)(2,1)S(1)} %collective-permute-done.6.refs_0_, ...), custom_call_target="tpu_custom_call" | custom-call | flops 1 | bytes 1 | tf_op jit(solution)/shard_map/hidden/pallas_call | solution.py:40
  30.1 0.5 collective-permute-start.12
  30.6 1.5 %collective-permute-start.17 = (bf16[256,512]{1,0:T(8,128)(2,1)S(1)}, bf16[256,512]{1,0:T(8,128)(2,1)S(1)}, u32[]{:S(2)}, u32[]{:S(2)}) collective-permute-start(bf16[256,512]{1,0:T(8,128)(2,1)S(1)} %get-tuple-element.75.refs_3_), channel_id=1, source_target_pairs={{0,2},{1,5},{2,0},{3,7},{4,6},{5,1},{6,4},{7,3},{8,10},{9,13},{10,... | collective-permute-start | bytes 786440 | tf_op jit(solution)/shard_map/ppermute | solution.py:429
  32.1 1.2 %hidden.6 = (bf16[256,512]{1,0:T(8,128)(2,1)S(1)}, bf16[16,128]{1,0:T(8,128)(2,1)}) custom-call(f32[8,1024]{1,0:T(8,128)S(1)} %get-tuple-element.68.decay, bf16[2,512,256]{2,1,0:T(8,128)(2,1)S(1)} %get-tuple-element.52.before, f32[520,256]{1,0:T(8,128)S(1)} %get-tuple-element.62.entering, bf16[512,256]{1,0:T(8,128)(2,1)S(1)} %collective-permute-done.6.refs_0_, ...), custom_call_target="tpu_custom_call" | custom-call | flops 1 | bytes 1 | tf_op jit(solution)/shard_map/hidden/pallas_call | solution.py:40
  33.4 1.5 %collective-permute-start.16 = (bf16[256,512]{1,0:T(8,128)(2,1)S(1)}, bf16[256,512]{1,0:T(8,128)(2,1)S(1)}, u32[]{:S(2)}, u32[]{:S(2)}) collective-permute-start(bf16[256,512]{1,0:T(8,128)(2,1)S(1)} %get-tuple-element.74.refs_2_), channel_id=1, source_target_pairs={{0,4},{1,3},{2,6},{3,1},{4,0},{5,7},{6,2},{7,5},{8,12},{9,11},{10,... | collective-permute-start | bytes 786440 | tf_op jit(solution)/shard_map/ppermute | solution.py:429
  34.9 1.2 %hidden.5 = (bf16[256,512]{1,0:T(8,128)(2,1)S(1)}, bf16[16,128]{1,0:T(8,128)(2,1)}) custom-call(f32[8,1024]{1,0:T(8,128)S(1)} %get-tuple-element.68.decay, bf16[2,512,256]{2,1,0:T(8,128)(2,1)S(1)} %get-tuple-element.52.before, f32[520,256]{1,0:T(8,128)S(1)} %get-tuple-element.62.entering, bf16[512,256]{1,0:T(8,128)(2,1)S(1)} %collective-permute-done.6.refs_0_, ...), custom_call_target="tpu_custom_call" | custom-call | flops 1 | bytes 1 | tf_op jit(solution)/shard_map/hidden/pallas_call | solution.py:40
  36.1 0.5 collective-permute-start.14
  36.6 1.2 %hidden.4 = (bf16[256,512]{1,0:T(8,128)(2,1)S(1)}, bf16[16,128]{1,0:T(8,128)(2,1)}) custom-call(f32[8,1024]{1,0:T(8,128)S(1)} %get-tuple-element.68.decay, bf16[2,512,256]{2,1,0:T(8,128)(2,1)S(1)} %get-tuple-element.52.before, f32[520,256]{1,0:T(8,128)S(1)} %get-tuple-element.62.entering, bf16[512,256]{1,0:T(8,128)(2,1)S(1)} %collective-permute-done.6.refs_0_, ...), custom_call_target="tpu_custom_call" | custom-call | flops 1 | bytes 1 | tf_op jit(solution)/shard_map/hidden/pallas_call | solution.py:40
  37.9 0.5 collective-permute-start.9
  38.4 1.3 %own_products.1 = (f32[512,1024]{1,0:T(8,128)S(1)}, f32[512,1024]{1,0:T(8,128)S(1)}) custom-call(bf16[512,1024]{1,0:T(8,128)(2,1)S(1)} %get-tuple-element.66.first.own_first, bf16[512,1024]{1,0:T(8,128)(2,1)S(1)} %collective-permute-done.second.own_second, bf16[256,512]{1,0:T(8,128)(2,1)S(1)} %get-tuple-element.72.refs_0_, ...), custom_call_target="tpu_custom_call" | custom-call | flops 1 | bytes 1 | tf_op jit(solution)/shard_map/own_products/pallas_call | solution.py:40
  40.3 1.6 %collective-permute-start.19 = (bf16[256,512]{1,0:T(8,128)(2,1)S(1)}, bf16[256,512]{1,0:T(8,128)(2,1)S(1)}, u32[]{:S(2)}, u32[]{:S(2)}) collective-permute-start(bf16[256,512]{1,0:T(8,128)(2,1)S(1)} %give.7), channel_id=1, source_target_pairs={{0,4},{1,3},{2,6},{3,1},{4,0},{5,7},{6,2},{7,5},{8,12},{9,11},{10,... | collective-permute-start | bytes 786440 | tf_op jit(solution)/shard_map/ppermute | solution.py:429
  42.2 1.5 %collective-permute-start.18 = (bf16[256,512]{1,0:T(8,128)(2,1)S(1)}, bf16[256,512]{1,0:T(8,128)(2,1)S(1)}, u32[]{:S(2)}, u32[]{:S(2)}) collective-permute-start(bf16[256,512]{1,0:T(8,128)(2,1)S(1)} %give.6), channel_id=1, source_target_pairs={{0,2},{1,5},{2,0},{3,7},{4,6},{5,1},{6,4},{7,3},{8,10},{9,13},{10,... | collective-permute-start | bytes 786440 | tf_op jit(solution)/shard_map/ppermute | solution.py:429
  43.7 1.6 %collective-permute-done.14.far.refs_1_ = bf16[256,512]{1,0:T(8,128)(2,1)S(1)} collective-permute-done((bf16[256,512]{1,0:T(8,128)(2,1)S(1)}, bf16[256,512]{1,0:T(8,128)(2,1)S(1)}, u32[]{:S(2)}, u32[]{:S(2)}) %collective-permute-start.14) | collective-permute-done | bytes 262176 | tf_op jit(solution)/shard_map/ppermute | solution.py:429
  45.6 1.1 %collective-permute-start.15 = (bf16[256,512]{1,0:T(8,128)(2,1)S(1)}, bf16[256,512]{1,0:T(8,128)(2,1)S(1)}, u32[]{:S(2)}, u32[]{:S(2)}) collective-permute-start(bf16[256,512]{1,0:T(8,128)(2,1)S(1)} %give.5), channel_id=1, source_target_pairs={{0,4},{1,3},{2,6},{3,1},{4,0},{5,7},{6,2},{7,5},{8,12},{9,11},{10,... | collective-permute-start | bytes 786440 | tf_op jit(solution)/shard_map/ppermute | solution.py:429
  47.4 1.2 %collective-permute-start.13 = (bf16[256,512]{1,0:T(8,128)(2,1)S(1)}, bf16[256,512]{1,0:T(8,128)(2,1)S(1)}, u32[]{:S(2)}, u32[]{:S(2)}) collective-permute-start(bf16[256,512]{1,0:T(8,128)(2,1)S(1)} %give.4), channel_id=1, source_target_pairs={{0,2},{1,5},{2,0},{3,7},{4,6},{5,1},{6,4},{7,3},{8,10},{9,13},{10,... | collective-permute-start | bytes 786440 | tf_op jit(solution)/shard_map/ppermute | solution.py:429
  48.6 0.7 %keep.1 = (f32[512,512]{1,0:T(8,128)S(1)}, f32[512,512]{1,0:T(8,128)S(1)}) custom-call(bf16[256,512]{1,0:T(8,128)(2,1)S(1)} %collective-permute-done.9.far.refs_0_, bf16[256,512]{1,0:T(8,128)(2,1)S(1)} %collective-permute-done.14.far.refs_1_, bf16[256,512]{1,0:T(8,128)(2,1)S(1)} %collective-permute-done.16.refs_2_.far, ...), custom_call_target="tpu_custom_call" | custom-call | flops 1 | bytes 1 | tf_op jit(solution)/shard_map/keep/pallas_call | solution.py:40
  49.3 3.4 %collective-permute-done.19.refs_1_ = bf16[256,512]{1,0:T(8,128)(2,1)S(1)} collective-permute-done((bf16[256,512]{1,0:T(8,128)(2,1)S(1)}, bf16[256,512]{1,0:T(8,128)(2,1)S(1)}, u32[]{:S(2)}, u32[]{:S(2)}) %collective-permute-start.19) | collective-permute-done | bytes 262176 | tf_op jit(solution)/shard_map/ppermute | solution.py:429
  52.7 0.9 %finish.2.refs_4_ = bf16[1,1024,512]{2,1,0:T(8,128)(2,1)} custom-call(bf16[256,512]{1,0:T(8,128)(2,1)S(1)} %collective-permute-done.18.refs_0_, bf16[256,512]{1,0:T(8,128)(2,1)S(1)} %collective-permute-done.19.refs_1_, f32[512,512]{1,0:T(8,128)S(1)} %get-tuple-element.83.refs_2_, f32[512,512]{1,0:T(8,128)S(1)} %get-tuple-element.84.refs_3_), custom_call_target="tpu_custom_call" | custom-call | tf_op jit(solution)/shard_map/finish/pallas_call | solution.py:563
  53.6 3.0 %collective-permute-done.15.refs_1_ = bf16[256,512]{1,0:T(8,128)(2,1)S(1)} collective-permute-done((bf16[256,512]{1,0:T(8,128)(2,1)S(1)}, bf16[256,512]{1,0:T(8,128)(2,1)S(1)}, u32[]{:S(2)}, u32[]{:S(2)}) %collective-permute-start.15) | collective-permute-done | bytes 262176 | tf_op jit(solution)/shard_map/ppermute | solution.py:429
  56.7 0.9 %finish.3 = bf16[1,1024,512]{2,1,0:T(8,128)(2,1)} custom-call(bf16[256,512]{1,0:T(8,128)(2,1)S(1)} %collective-permute-done.13.refs_0_, bf16[256,512]{1,0:T(8,128)(2,1)S(1)} %collective-permute-done.15.refs_1_, f32[512,512]{1,0:T(8,128)S(1)} %get-tuple-element.83.refs_2_, f32[512,512]{1,0:T(8,128)S(1)} %get-tuple-element.84.refs_3_, ...), custom_call_target="tpu_custom_call", output_to_operand_aliasing={{}: (4, {})} | custom-call | tf_op jit(solution)/shard_map/finish/pallas_call | solution.py:563
  (27 shorter events, 2.3 us)
Async XLA Ops:
  0.0 4.9 %collective-permute-start.1 = (bf16[1024,512]{1,0:T(8,128)(2,1)}, bf16[1024,512]{1,0:T(8,128)(2,1)S(1)}, u32[]{:S(2)}, u32[]{:S(2)}) collective-permute-start(bf16[1024,512]{1,0:T(8,128)(2,1)} %wk_far.1), channel_id=1, source_target_pairs={{0,1},{1,0},{2,3},{3,2},{4,5},{5,4},{6,7},{7,6},{8,9},{9,8},{10,11... | collective-permute-start | bytes 3145736 | tf_op jit(solution)/shard_map/ppermute | solution.py:35
  0.0 4.9 %collective-permute-start.2 = (bf16[1024,512]{1,0:T(8,128)(2,1)}, bf16[1024,512]{1,0:T(8,128)(2,1)S(1)}, u32[]{:S(2)}, u32[]{:S(2)}) collective-permute-start(bf16[1024,512]{1,0:T(8,128)(2,1)} %wv_far.1), channel_id=1, source_target_pairs={{0,1},{1,0},{2,3},{3,2},{4,5},{5,4},{6,7},{7,6},{8,9},{9,8},{10,11... | collective-permute-start | bytes 3145736 | tf_op jit(solution)/shard_map/ppermute | solution.py:35
  4.8 3.9 %collective-permute-start = (bf16[512,1024]{1,0:T(8,128)(2,1)S(1)}, bf16[512,1024]{1,0:T(8,128)(2,1)S(1)}, u32[]{:S(2)}, u32[]{:S(2)}) collective-permute-start(bf16[512,1024]{1,0:T(8,128)(2,1)S(1)} %get-tuple-element.66.first.own_first), channel_id=1, source_target_pairs={{0,1},{1,0},{2,3},{3,2},{4,5},{5,4},{6,7},{7,6},{8,9},{9,8},{10,11... | collective-permute-start | bytes 3145736 | tf_op jit(solution)/shard_map/ppermute | solution.py:35
  8.2 3.2 %collective-permute-start.3 = (bf16[1024,512]{1,0:T(8,128)(2,1)S(1)}, bf16[1024,512]{1,0:T(8,128)(2,1)S(1)}, u32[]{:S(2)}, u32[]{:S(2)}) collective-permute-start(bf16[1024,512]{1,0:T(8,128)(2,1)S(1)} %get-tuple-element.55.wq), channel_id=1, source_target_pairs={{0,1},{1,0},{2,3},{3,2},{4,5},{5,4},{6,7},{7,6},{8,9},{9,8},{10,11... | collective-permute-start | bytes 3145736 | tf_op jit(solution)/shard_map/ppermute | solution.py:35
  8.7 3.8 %collective-permute-start.4 = (bf16[1024,512]{1,0:T(8,128)(2,1)S(1)}, bf16[1024,512]{1,0:T(8,128)(2,1)S(1)}, u32[]{:S(2)}, u32[]{:S(2)}) collective-permute-start(bf16[1024,512]{1,0:T(8,128)(2,1)S(1)} %get-tuple-element.56.wg), channel_id=1, source_target_pairs={{0,1},{1,0},{2,3},{3,2},{4,5},{5,4},{6,7},{7,6},{8,9},{9,8},{10,11... | collective-permute-start | bytes 3145736 | tf_op jit(solution)/shard_map/ppermute | solution.py:35
  8.8 8.8 %collective-permute-start.5 = (bf16[528,256]{1,0:T(8,128)(2,1)S(1)}, bf16[528,256]{1,0:T(8,128)(2,1)S(1)}, u32[]{:S(2)}, u32[]{:S(2)}) collective-permute-start(bf16[528,256]{1,0:T(8,128)(2,1)S(1)} %get-tuple-element.61.sent), channel_id=1, source_target_pairs={{0,8},{8,16},{16,24},{24,0},{1,9},{9,17},{17,25},{25,1},{2,10},{10... | collective-permute-start | bytes 811016 | tf_op jit(solution)/shard_map/ppermute | solution.py:477
  8.9 10.2 %collective-permute-start.8 = (bf16[512,512]{1,0:T(8,128)(2,1)S(1)}, bf16[512,512]{1,0:T(8,128)(2,1)S(1)}, u32[]{:S(2)}, u32[]{:S(2)}) collective-permute-start(bf16[512,512]{1,0:T(8,128)(2,1)S(1)} %get-tuple-element.67), channel_id=1, source_target_pairs={{0,2},{1,5},{2,0},{3,7},{4,6},{5,1},{6,4},{7,3},{8,10},{9,13},{10,... | collective-permute-start | bytes 1572872 | tf_op jit(solution)/shard_map/ppermute | solution.py:429
  10.6 8.4 %collective-permute-start.7 = (bf16[528,256]{1,0:T(8,128)(2,1)S(1)}, bf16[528,256]{1,0:T(8,128)(2,1)S(1)}, u32[]{:S(2)}, u32[]{:S(2)}) collective-permute-start(bf16[528,256]{1,0:T(8,128)(2,1)S(1)} %get-tuple-element.61.sent), channel_id=1, source_target_pairs={{0,16},{16,0},{8,8},{24,24},{1,17},{17,1},{9,9},{25,25},{2,18},{18... | collective-permute-start | bytes 811016 | tf_op jit(solution)/shard_map/ppermute | solution.py:477
  11.3 18.8 %collective-permute-start.10 = (bf16[512,512]{1,0:T(8,128)(2,1)S(1)}, bf16[512,512]{1,0:T(8,128)(2,1)S(1)}, u32[]{:S(2)}, u32[]{:S(2)}) collective-permute-start(bf16[512,512]{1,0:T(8,128)(2,1)S(1)} %get-tuple-element.77), channel_id=1, source_target_pairs={{0,2},{1,5},{2,0},{3,7},{4,6},{5,1},{6,4},{7,3},{8,10},{9,13},{10,... | collective-permute-start | bytes 1572872 | tf_op jit(solution)/shard_map/ppermute | solution.py:429
  17.8 11.1 %collective-permute-start.6 = (bf16[512,256]{1,0:T(8,128)(2,1)S(1)}, bf16[512,256]{1,0:T(8,128)(2,1)S(1)}, u32[]{:S(2)}, u32[]{:S(2)}) collective-permute-start(bf16[512,256]{1,0:T(8,128)(2,1)S(1)} %get-tuple-element.63), channel_id=1, source_target_pairs={{8,24},{9,25},{10,26},{11,27},{12,28},{13,29},{14,30},{15,31}} | collective-permute-start | bytes 786440 | tf_op jit(solution)/shard_map/ppermute | solution.py:477
  30.1 7.7 %collective-permute-start.11 = (bf16[512,512]{1,0:T(8,128)(2,1)S(1)}, bf16[512,512]{1,0:T(8,128)(2,1)S(1)}, u32[]{:S(2)}, u32[]{:S(2)}) collective-permute-start(bf16[512,512]{1,0:T(8,128)(2,1)S(1)} %collective-permute-done.8.mine_0), channel_id=1, source_target_pairs={{0,1},{1,0},{2,3},{3,2},{4,5},{5,4},{6,7},{7,6},{8,9},{9,8},{10,11... | collective-permute-start | bytes 1572872 | tf_op jit(solution)/shard_map/ppermute | solution.py:35
  30.1 9.6 %collective-permute-start.12 = (bf16[512,512]{1,0:T(8,128)(2,1)S(1)}, bf16[512,512]{1,0:T(8,128)(2,1)S(1)}, u32[]{:S(2)}, u32[]{:S(2)}) collective-permute-start(bf16[512,512]{1,0:T(8,128)(2,1)S(1)} %collective-permute-done.10.mine_1), channel_id=1, source_target_pairs={{0,1},{1,0},{2,3},{3,2},{4,5},{5,4},{6,7},{7,6},{8,9},{9,8},{10,11... | collective-permute-start | bytes 1572872 | tf_op jit(solution)/shard_map/ppermute | solution.py:35
  30.6 9.4 %collective-permute-start.17 = (bf16[256,512]{1,0:T(8,128)(2,1)S(1)}, bf16[256,512]{1,0:T(8,128)(2,1)S(1)}, u32[]{:S(2)}, u32[]{:S(2)}) collective-permute-start(bf16[256,512]{1,0:T(8,128)(2,1)S(1)} %get-tuple-element.75.refs_3_), channel_id=1, source_target_pairs={{0,2},{1,5},{2,0},{3,7},{4,6},{5,1},{6,4},{7,3},{8,10},{9,13},{10,... | collective-permute-start | bytes 786440 | tf_op jit(solution)/shard_map/ppermute | solution.py:429
  33.4 8.5 %collective-permute-start.16 = (bf16[256,512]{1,0:T(8,128)(2,1)S(1)}, bf16[256,512]{1,0:T(8,128)(2,1)S(1)}, u32[]{:S(2)}, u32[]{:S(2)}) collective-permute-start(bf16[256,512]{1,0:T(8,128)(2,1)S(1)} %get-tuple-element.74.refs_2_), channel_id=1, source_target_pairs={{0,4},{1,3},{2,6},{3,1},{4,0},{5,7},{6,2},{7,5},{8,12},{9,11},{10,... | collective-permute-start | bytes 786440 | tf_op jit(solution)/shard_map/ppermute | solution.py:429
  36.1 9.2 %collective-permute-start.14 = (bf16[256,512]{1,0:T(8,128)(2,1)S(1)}, bf16[256,512]{1,0:T(8,128)(2,1)S(1)}, u32[]{:S(2)}, u32[]{:S(2)}) collective-permute-start(bf16[256,512]{1,0:T(8,128)(2,1)S(1)} %get-tuple-element.73.refs_1_), channel_id=1, source_target_pairs={{0,2},{1,5},{2,0},{3,7},{4,6},{5,1},{6,4},{7,3},{8,10},{9,13},{10,... | collective-permute-start | bytes 786440 | tf_op jit(solution)/shard_map/ppermute | solution.py:429
  37.9 9.2 %collective-permute-start.9 = (bf16[256,512]{1,0:T(8,128)(2,1)S(1)}, bf16[256,512]{1,0:T(8,128)(2,1)S(1)}, u32[]{:S(2)}, u32[]{:S(2)}) collective-permute-start(bf16[256,512]{1,0:T(8,128)(2,1)S(1)} %get-tuple-element.72.refs_0_), channel_id=1, source_target_pairs={{0,4},{1,3},{2,6},{3,1},{4,0},{5,7},{6,2},{7,5},{8,12},{9,11},{10,... | collective-permute-start | bytes 786440 | tf_op jit(solution)/shard_map/ppermute | solution.py:429
  40.3 12.4 %collective-permute-start.19 = (bf16[256,512]{1,0:T(8,128)(2,1)S(1)}, bf16[256,512]{1,0:T(8,128)(2,1)S(1)}, u32[]{:S(2)}, u32[]{:S(2)}) collective-permute-start(bf16[256,512]{1,0:T(8,128)(2,1)S(1)} %give.7), channel_id=1, source_target_pairs={{0,4},{1,3},{2,6},{3,1},{4,0},{5,7},{6,2},{7,5},{8,12},{9,11},{10,... | collective-permute-start | bytes 786440 | tf_op jit(solution)/shard_map/ppermute | solution.py:429
  42.2 10.5 %collective-permute-start.18 = (bf16[256,512]{1,0:T(8,128)(2,1)S(1)}, bf16[256,512]{1,0:T(8,128)(2,1)S(1)}, u32[]{:S(2)}, u32[]{:S(2)}) collective-permute-start(bf16[256,512]{1,0:T(8,128)(2,1)S(1)} %give.6), channel_id=1, source_target_pairs={{0,2},{1,5},{2,0},{3,7},{4,6},{5,1},{6,4},{7,3},{8,10},{9,13},{10,... | collective-permute-start | bytes 786440 | tf_op jit(solution)/shard_map/ppermute | solution.py:429
  45.6 11.0 %collective-permute-start.15 = (bf16[256,512]{1,0:T(8,128)(2,1)S(1)}, bf16[256,512]{1,0:T(8,128)(2,1)S(1)}, u32[]{:S(2)}, u32[]{:S(2)}) collective-permute-start(bf16[256,512]{1,0:T(8,128)(2,1)S(1)} %give.5), channel_id=1, source_target_pairs={{0,4},{1,3},{2,6},{3,1},{4,0},{5,7},{6,2},{7,5},{8,12},{9,11},{10,... | collective-permute-start | bytes 786440 | tf_op jit(solution)/shard_map/ppermute | solution.py:429
  47.4 9.3 %collective-permute-start.13 = (bf16[256,512]{1,0:T(8,128)(2,1)S(1)}, bf16[256,512]{1,0:T(8,128)(2,1)S(1)}, u32[]{:S(2)}, u32[]{:S(2)}) collective-permute-start(bf16[256,512]{1,0:T(8,128)(2,1)S(1)} %give.4), channel_id=1, source_target_pairs={{0,2},{1,5},{2,0},{3,7},{4,6},{5,1},{6,4},{7,3},{8,10},{9,13},{10,... | collective-permute-start | bytes 786440 | tf_op jit(solution)/shard_map/ppermute | solution.py:429

commit v24 on v22

--- a/solution.py
+++ b/solution.py
@@ -479,7 +479,8 @@
         first_set, *later_sets = exchanges(ctx, hop)
         later_sets = [lowers for lowers in later_sets if lowers]
         sets = later_sets + ([first_set] if first_set else [])
-        arrivals = [exchange(message, lowers, hop) for lowers in later_sets] + early
+        late = after(message, *early) if early else message
+        arrivals = [exchange(late, lowers, hop) for lowers in later_sets] + early
         if 2 * hop >= ctx:
             break
         unchanged = exchanges(ctx, 2 * hop)[0]

time: 58.1 us -> 58.5 us (level)
  no operation moved by 1% of the time
where the time goes in v24:
time: 58.5 us; the launch traced here: 57.7 us
  Pallas kernels  24 us (41%)
  starting transfers between devices  17.5 us (30%)
  waiting for transfers between devices  15.8 us (27%)
    pallas_call x15, Pallas kernels, kernel_call(): pl.pallas_call(kernel, in_specs=[pl.BlockSpec(memory_space=pltpu.VMEM)] *...  14.8 us
    ppermute x10, starting transfers between devices, trade(): return lax.ppermute(value, ('tp', 'fsdp'), partners[role])  12.4 us
    ppermute x10, waiting for transfers between devices, trade(): return lax.ppermute(value, ('tp', 'fsdp'), partners[role])  8.47 us
    pallas_call x2, Pallas kernels, loading_call(): pl.pallas_call(kernel, in_specs=[pl.BlockSpec(memory_space=pltpu.HBM)] *...  7.53 us
    ppermute x3, waiting for transfers between devices, exchange(): return lax.ppermute(message, 'ctx', pairs)  7.34 us
    ppermute x3, starting transfers between devices, exchange(): return lax.ppermute(message, 'ctx', pairs)  3.37 us
    ppermute x7, starting transfers between devices, swap(): lax.ppermute(value, axis, [(place, place ^ mask) for place in range(size)])  1.71 us
    pallas_call x2, Pallas kernels, on_device(): pl.pallas_call(functools.partial(finish_kernel, part_order), in_specs=[pl...  1.7 us
  transfers between devices with their start and end apart: 20, of which 7 were waited for; matrix products, arithmetic and copies ran while one was open for 0% of the time, Pallas kernels for 40%

profile of v24, /device:TPU:24, one launch (start us, length us, event | category | flops | bytes accessed | tf_op | source)
XLA Modules:
  0.0 57.7 jit_solution(9388597171213625552)
XLA Ops:
  0.0 0.5 collective-permute-start.2
  0.5 4.3 %key_value_own.1 = (bf16[1024,1024]{1,0:T(8,128)(2,1)S(1)}, bf16[1024,1024]{1,0:T(8,128)(2,1)S(1)}, f32[1024,512]{1,0:T(8,128)S(1)}, f32[1024,512]{1,0:T(8,128)S...) custom-call(bf16[1024,2048]{1,0:T(8,128)(2,1)} %bitcast.4, ...), custom_call_target="tpu_custom_call" | custom-call | flops 1 | bytes 1 | tf_op jit(solution)/shard_map/key_value_own/pallas_call | solution.py:56
  4.9 3.2 %key_value.1 = (bf16[1024,512]{1,0:T(8,128)(2,1)S(1)}, bf16[1024,512]{1,0:T(8,128)(2,1)S(1)}, bf16[1024,512]{1,0:T(8,128)(2,1)S(1)}, bf16[1024,512]{1,0:T(8,128)...) custom-call(bf16[1024,512]{1,0:T(8,128)(2,1)} %wq_far.1, ...), custom_call_target="tpu_custom_call" | custom-call | flops 1 | bytes 1 | tf_op jit(solution)/shard_map/key_value/pallas_call | solution.py:56
  8.2 0.5 collective-permute-start.3
  8.8 0.7 %collective-permute-start.6 = (bf16[528,256]{1,0:T(8,128)(2,1)S(1)}, bf16[528,256]{1,0:T(8,128)(2,1)S(1)}, u32[]{:S(2)}, u32[]{:S(2)}) collective-permute-start(bf16[528,256]{1,0:T(8,128)(2,1)S(1)} %get-tuple-element.62.sent), channel_id=1, source_target_pairs={{0,16},{1,17},{2,18},{3,19},{4,20},{5,21},{6,22},{7,23}} | collective-permute-start | bytes 811016 | tf_op jit(solution)/shard_map/ppermute | solution.py:473
  9.6 1.8 %collective-permute-start.8 = (bf16[512,512]{1,0:T(8,128)(2,1)S(1)}, bf16[512,512]{1,0:T(8,128)(2,1)S(1)}, u32[]{:S(2)}, u32[]{:S(2)}) collective-permute-start(bf16[512,512]{1,0:T(8,128)(2,1)S(1)} %get-tuple-element.69), channel_id=1, source_target_pairs={{0,2},{1,5},{2,0},{3,7},{4,6},{5,1},{6,4},{7,3},{8,10},{9,13},{10,... | collective-permute-start | bytes 1572872 | tf_op jit(solution)/shard_map/ppermute | solution.py:429
  11.3 1.1 %collective-permute-start.10 = (bf16[512,512]{1,0:T(8,128)(2,1)S(1)}, bf16[512,512]{1,0:T(8,128)(2,1)S(1)}, u32[]{:S(2)}, u32[]{:S(2)}) collective-permute-start(bf16[512,512]{1,0:T(8,128)(2,1)S(1)} %get-tuple-element.79), channel_id=1, source_target_pairs={{0,2},{1,5},{2,0},{3,7},{4,6},{5,1},{6,4},{7,3},{8,10},{9,13},{10,... | collective-permute-start | bytes 1572872 | tf_op jit(solution)/shard_map/ppermute | solution.py:429
  12.5 3.1 %query_gate.2 = (bf16[512,512]{1,0:T(8,128)(2,1)S(1)}, f32[512,512]{1,0:T(8,128)S(1)}, f32[512,512]{1,0:T(8,128)S(1)}) custom-call(bf16[1024,1024]{1,0:T(8,128)(2,1)S(1)} %get-tuple-element.55.x_own, bf16[1024,1024]{1,0:T(8,128)(2,1)S(1)} %get-tuple-element.48.x.x_other, bf16[1024,512]{1,0:T(8,128)(2,1)S(1)} %get-tuple-element.56.wq, ...), custom_call_target="tpu_custom_call" | custom-call | flops 1 | bytes 1 | tf_op jit(solution)/shard_map/query_gate/pallas_call | solution.py:40
  15.6 2.0 %collective-permute-done.5.refs_0_ = bf16[528,256]{1,0:T(8,128)(2,1)S(1)} collective-permute-done((bf16[528,256]{1,0:T(8,128)(2,1)S(1)}, bf16[528,256]{1,0:T(8,128)(2,1)S(1)}, u32[]{:S(2)}, u32[]{:S(2)}) %collective-permute-start.5) | collective-permute-done | bytes 270368 | tf_op jit(solution)/shard_map/ppermute | solution.py:473
  17.8 2.7 %collective-permute-start.7 = (bf16[512,256]{1,0:T(8,128)(2,1)S(1)}, bf16[512,256]{1,0:T(8,128)(2,1)S(1)}, u32[]{:S(2)}, u32[]{:S(2)}) collective-permute-start(bf16[512,256]{1,0:T(8,128)(2,1)S(1)} %get-tuple-element.65), channel_id=1, source_target_pairs={{8,24},{24,8},{9,25},{25,9},{10,26},{26,10},{11,27},{27,11},{12,28... | collective-permute-start | bytes 786440 | tf_op jit(solution)/shard_map/ppermute | solution.py:473
  20.5 3.1 %query_gate.3 = (bf16[512,512]{1,0:T(8,128)(2,1)S(1)}, f32[512,512]{1,0:T(8,128)S(1)}, f32[512,512]{1,0:T(8,128)S(1)}) custom-call(bf16[1024,1024]{1,0:T(8,128)(2,1)S(1)} %get-tuple-element.55.x_own, bf16[1024,1024]{1,0:T(8,128)(2,1)S(1)} %get-tuple-element.48.x.x_other, bf16[1024,512]{1,0:T(8,128)(2,1)S(1)} %get-tuple-element.56.wq, ...), custom_call_target="tpu_custom_call" | custom-call | flops 1 | bytes 1 | tf_op jit(solution)/shard_map/query_gate/pallas_call | solution.py:40
  23.6 5.3 %collective-permute-done.7.refs_0_ = bf16[512,256]{1,0:T(8,128)(2,1)S(1)} collective-permute-done((bf16[512,256]{1,0:T(8,128)(2,1)S(1)}, bf16[512,256]{1,0:T(8,128)(2,1)S(1)}, u32[]{:S(2)}, u32[]{:S(2)}) %collective-permute-start.7) | collective-permute-done | bytes 262176 | tf_op jit(solution)/shard_map/ppermute | solution.py:473
  28.9 1.2 %hidden.7 = (bf16[256,512]{1,0:T(8,128)(2,1)S(1)}, bf16[16,128]{1,0:T(8,128)(2,1)}) custom-call(f32[8,1024]{1,0:T(8,128)S(1)} %get-tuple-element.70.decay, bf16[2,512,256]{2,1,0:T(8,128)(2,1)S(1)} %get-tuple-element.53.before, f32[520,256]{1,0:T(8,128)S(1)} %get-tuple-element.63.entering, bf16[512,256]{1,0:T(8,128)(2,1)S(1)} %collective-permute-done.7.refs_0_, ...), custom_call_target="tpu_custom_call" | custom-call | flops 1 | bytes 1 | tf_op jit(solution)/shard_map/hidden/pallas_call | solution.py:40
  30.1 0.5 collective-permute-start.12
  30.6 1.5 %collective-permute-start.17 = (bf16[256,512]{1,0:T(8,128)(2,1)S(1)}, bf16[256,512]{1,0:T(8,128)(2,1)S(1)}, u32[]{:S(2)}, u32[]{:S(2)}) collective-permute-start(bf16[256,512]{1,0:T(8,128)(2,1)S(1)} %get-tuple-element.77.refs_3_), channel_id=1, source_target_pairs={{0,2},{1,5},{2,0},{3,7},{4,6},{5,1},{6,4},{7,3},{8,10},{9,13},{10,... | collective-permute-start | bytes 786440 | tf_op jit(solution)/shard_map/ppermute | solution.py:429
  32.1 1.2 %hidden.6 = (bf16[256,512]{1,0:T(8,128)(2,1)S(1)}, bf16[16,128]{1,0:T(8,128)(2,1)}) custom-call(f32[8,1024]{1,0:T(8,128)S(1)} %get-tuple-element.70.decay, bf16[2,512,256]{2,1,0:T(8,128)(2,1)S(1)} %get-tuple-element.53.before, f32[520,256]{1,0:T(8,128)S(1)} %get-tuple-element.63.entering, bf16[512,256]{1,0:T(8,128)(2,1)S(1)} %collective-permute-done.7.refs_0_, ...), custom_call_target="tpu_custom_call" | custom-call | flops 1 | bytes 1 | tf_op jit(solution)/shard_map/hidden/pallas_call | solution.py:40
  33.4 1.5 %collective-permute-start.16 = (bf16[256,512]{1,0:T(8,128)(2,1)S(1)}, bf16[256,512]{1,0:T(8,128)(2,1)S(1)}, u32[]{:S(2)}, u32[]{:S(2)}) collective-permute-start(bf16[256,512]{1,0:T(8,128)(2,1)S(1)} %get-tuple-element.76.refs_2_), channel_id=1, source_target_pairs={{0,4},{1,3},{2,6},{3,1},{4,0},{5,7},{6,2},{7,5},{8,12},{9,11},{10,... | collective-permute-start | bytes 786440 | tf_op jit(solution)/shard_map/ppermute | solution.py:429
  34.9 1.2 %hidden.5 = (bf16[256,512]{1,0:T(8,128)(2,1)S(1)}, bf16[16,128]{1,0:T(8,128)(2,1)}) custom-call(f32[8,1024]{1,0:T(8,128)S(1)} %get-tuple-element.70.decay, bf16[2,512,256]{2,1,0:T(8,128)(2,1)S(1)} %get-tuple-element.53.before, f32[520,256]{1,0:T(8,128)S(1)} %get-tuple-element.63.entering, bf16[512,256]{1,0:T(8,128)(2,1)S(1)} %collective-permute-done.7.refs_0_, ...), custom_call_target="tpu_custom_call" | custom-call | flops 1 | bytes 1 | tf_op jit(solution)/shard_map/hidden/pallas_call | solution.py:40
  36.1 0.5 collective-permute-start.14
  36.6 1.2 %hidden.4 = (bf16[256,512]{1,0:T(8,128)(2,1)S(1)}, bf16[16,128]{1,0:T(8,128)(2,1)}) custom-call(f32[8,1024]{1,0:T(8,128)S(1)} %get-tuple-element.70.decay, bf16[2,512,256]{2,1,0:T(8,128)(2,1)S(1)} %get-tuple-element.53.before, f32[520,256]{1,0:T(8,128)S(1)} %get-tuple-element.63.entering, bf16[512,256]{1,0:T(8,128)(2,1)S(1)} %collective-permute-done.7.refs_0_, ...), custom_call_target="tpu_custom_call" | custom-call | flops 1 | bytes 1 | tf_op jit(solution)/shard_map/hidden/pallas_call | solution.py:40
  37.9 0.5 collective-permute-start.9
  38.4 1.3 %own_products.1 = (f32[512,1024]{1,0:T(8,128)S(1)}, f32[512,1024]{1,0:T(8,128)S(1)}) custom-call(bf16[512,1024]{1,0:T(8,128)(2,1)S(1)} %get-tuple-element.68.first.own_first, bf16[512,1024]{1,0:T(8,128)(2,1)S(1)} %collective-permute-done.second.own_second, bf16[256,512]{1,0:T(8,128)(2,1)S(1)} %get-tuple-element.74.refs_0_, ...), custom_call_target="tpu_custom_call" | custom-call | flops 1 | bytes 1 | tf_op jit(solution)/shard_map/own_products/pallas_call | solution.py:40
  40.3 1.6 %collective-permute-start.19 = (bf16[256,512]{1,0:T(8,128)(2,1)S(1)}, bf16[256,512]{1,0:T(8,128)(2,1)S(1)}, u32[]{:S(2)}, u32[]{:S(2)}) collective-permute-start(bf16[256,512]{1,0:T(8,128)(2,1)S(1)} %give.7), channel_id=1, source_target_pairs={{0,4},{1,3},{2,6},{3,1},{4,0},{5,7},{6,2},{7,5},{8,12},{9,11},{10,... | collective-permute-start | bytes 786440 | tf_op jit(solution)/shard_map/ppermute | solution.py:429
  42.2 1.5 %collective-permute-start.18 = (bf16[256,512]{1,0:T(8,128)(2,1)S(1)}, bf16[256,512]{1,0:T(8,128)(2,1)S(1)}, u32[]{:S(2)}, u32[]{:S(2)}) collective-permute-start(bf16[256,512]{1,0:T(8,128)(2,1)S(1)} %give.6), channel_id=1, source_target_pairs={{0,2},{1,5},{2,0},{3,7},{4,6},{5,1},{6,4},{7,3},{8,10},{9,13},{10,... | collective-permute-start | bytes 786440 | tf_op jit(solution)/shard_map/ppermute | solution.py:429
  43.7 1.6 %collective-permute-done.14.far.refs_1_ = bf16[256,512]{1,0:T(8,128)(2,1)S(1)} collective-permute-done((bf16[256,512]{1,0:T(8,128)(2,1)S(1)}, bf16[256,512]{1,0:T(8,128)(2,1)S(1)}, u32[]{:S(2)}, u32[]{:S(2)}) %collective-permute-start.14) | collective-permute-done | bytes 262176 | tf_op jit(solution)/shard_map/ppermute | solution.py:429
  45.6 1.1 %collective-permute-start.15 = (bf16[256,512]{1,0:T(8,128)(2,1)S(1)}, bf16[256,512]{1,0:T(8,128)(2,1)S(1)}, u32[]{:S(2)}, u32[]{:S(2)}) collective-permute-start(bf16[256,512]{1,0:T(8,128)(2,1)S(1)} %give.5), channel_id=1, source_target_pairs={{0,4},{1,3},{2,6},{3,1},{4,0},{5,7},{6,2},{7,5},{8,12},{9,11},{10,... | collective-permute-start | bytes 786440 | tf_op jit(solution)/shard_map/ppermute | solution.py:429
  47.4 1.2 %collective-permute-start.13 = (bf16[256,512]{1,0:T(8,128)(2,1)S(1)}, bf16[256,512]{1,0:T(8,128)(2,1)S(1)}, u32[]{:S(2)}, u32[]{:S(2)}) collective-permute-start(bf16[256,512]{1,0:T(8,128)(2,1)S(1)} %give.4), channel_id=1, source_target_pairs={{0,2},{1,5},{2,0},{3,7},{4,6},{5,1},{6,4},{7,3},{8,10},{9,13},{10,... | collective-permute-start | bytes 786440 | tf_op jit(solution)/shard_map/ppermute | solution.py:429
  48.6 0.7 %keep.1 = (f32[512,512]{1,0:T(8,128)S(1)}, f32[512,512]{1,0:T(8,128)S(1)}) custom-call(bf16[256,512]{1,0:T(8,128)(2,1)S(1)} %collective-permute-done.9.far.refs_0_, bf16[256,512]{1,0:T(8,128)(2,1)S(1)} %collective-permute-done.14.far.refs_1_, bf16[256,512]{1,0:T(8,128)(2,1)S(1)} %collective-permute-done.16.refs_2_.far, ...), custom_call_target="tpu_custom_call" | custom-call | flops 1 | bytes 1 | tf_op jit(solution)/shard_map/keep/pallas_call | solution.py:40
  49.3 3.4 %collective-permute-done.19.refs_1_ = bf16[256,512]{1,0:T(8,128)(2,1)S(1)} collective-permute-done((bf16[256,512]{1,0:T(8,128)(2,1)S(1)}, bf16[256,512]{1,0:T(8,128)(2,1)S(1)}, u32[]{:S(2)}, u32[]{:S(2)}) %collective-permute-start.19) | collective-permute-done | bytes 262176 | tf_op jit(solution)/shard_map/ppermute | solution.py:429
  52.7 0.9 %finish.2.refs_4_ = bf16[1,1024,512]{2,1,0:T(8,128)(2,1)} custom-call(bf16[256,512]{1,0:T(8,128)(2,1)S(1)} %collective-permute-done.18.refs_0_, bf16[256,512]{1,0:T(8,128)(2,1)S(1)} %collective-permute-done.19.refs_1_, f32[512,512]{1,0:T(8,128)S(1)} %get-tuple-element.85.refs_2_, f32[512,512]{1,0:T(8,128)S(1)} %get-tuple-element.86.refs_3_), custom_call_target="tpu_custom_call" | custom-call | tf_op jit(solution)/shard_map/finish/pallas_call | solution.py:560
  53.6 3.0 %collective-permute-done.15.refs_1_ = bf16[256,512]{1,0:T(8,128)(2,1)S(1)} collective-permute-done((bf16[256,512]{1,0:T(8,128)(2,1)S(1)}, bf16[256,512]{1,0:T(8,128)(2,1)S(1)}, u32[]{:S(2)}, u32[]{:S(2)}) %collective-permute-start.15) | collective-permute-done | bytes 262176 | tf_op jit(solution)/shard_map/ppermute | solution.py:429
  56.7 0.9 %finish.3 = bf16[1,1024,512]{2,1,0:T(8,128)(2,1)} custom-call(bf16[256,512]{1,0:T(8,128)(2,1)S(1)} %collective-permute-done.13.refs_0_, bf16[256,512]{1,0:T(8,128)(2,1)S(1)} %collective-permute-done.15.refs_1_, f32[512,512]{1,0:T(8,128)S(1)} %get-tuple-element.85.refs_2_, f32[512,512]{1,0:T(8,128)S(1)} %get-tuple-element.86.refs_3_, ...), custom_call_target="tpu_custom_call", output_to_operand_aliasing={{}: (4, {})} | custom-call | tf_op jit(solution)/shard_map/finish/pallas_call | solution.py:560
  (27 shorter events, 2.4 us)
Async XLA Ops:
  0.0 4.9 %collective-permute-start.1 = (bf16[1024,512]{1,0:T(8,128)(2,1)}, bf16[1024,512]{1,0:T(8,128)(2,1)S(1)}, u32[]{:S(2)}, u32[]{:S(2)}) collective-permute-start(bf16[1024,512]{1,0:T(8,128)(2,1)} %wk_far.1), channel_id=1, source_target_pairs={{0,1},{1,0},{2,3},{3,2},{4,5},{5,4},{6,7},{7,6},{8,9},{9,8},{10,11... | collective-permute-start | bytes 3145736 | tf_op jit(solution)/shard_map/ppermute | solution.py:35
  0.0 4.9 %collective-permute-start.2 = (bf16[1024,512]{1,0:T(8,128)(2,1)}, bf16[1024,512]{1,0:T(8,128)(2,1)S(1)}, u32[]{:S(2)}, u32[]{:S(2)}) collective-permute-start(bf16[1024,512]{1,0:T(8,128)(2,1)} %wv_far.1), channel_id=1, source_target_pairs={{0,1},{1,0},{2,3},{3,2},{4,5},{5,4},{6,7},{7,6},{8,9},{9,8},{10,11... | collective-permute-start | bytes 3145736 | tf_op jit(solution)/shard_map/ppermute | solution.py:35
  4.8 4.6 %collective-permute-start = (bf16[512,1024]{1,0:T(8,128)(2,1)S(1)}, bf16[512,1024]{1,0:T(8,128)(2,1)S(1)}, u32[]{:S(2)}, u32[]{:S(2)}) collective-permute-start(bf16[512,1024]{1,0:T(8,128)(2,1)S(1)} %get-tuple-element.68.first.own_first), channel_id=1, source_target_pairs={{0,1},{1,0},{2,3},{3,2},{4,5},{5,4},{6,7},{7,6},{8,9},{9,8},{10,11... | collective-permute-start | bytes 3145736 | tf_op jit(solution)/shard_map/ppermute | solution.py:35
  8.2 3.2 %collective-permute-start.3 = (bf16[1024,512]{1,0:T(8,128)(2,1)S(1)}, bf16[1024,512]{1,0:T(8,128)(2,1)S(1)}, u32[]{:S(2)}, u32[]{:S(2)}) collective-permute-start(bf16[1024,512]{1,0:T(8,128)(2,1)S(1)} %get-tuple-element.56.wq), channel_id=1, source_target_pairs={{0,1},{1,0},{2,3},{3,2},{4,5},{5,4},{6,7},{7,6},{8,9},{9,8},{10,11... | collective-permute-start | bytes 3145736 | tf_op jit(solution)/shard_map/ppermute | solution.py:35
  8.7 3.8 %collective-permute-start.4 = (bf16[1024,512]{1,0:T(8,128)(2,1)S(1)}, bf16[1024,512]{1,0:T(8,128)(2,1)S(1)}, u32[]{:S(2)}, u32[]{:S(2)}) collective-permute-start(bf16[1024,512]{1,0:T(8,128)(2,1)S(1)} %get-tuple-element.57.wg), channel_id=1, source_target_pairs={{0,1},{1,0},{2,3},{3,2},{4,5},{5,4},{6,7},{7,6},{8,9},{9,8},{10,11... | collective-permute-start | bytes 3145736 | tf_op jit(solution)/shard_map/ppermute | solution.py:35
  8.8 8.8 %collective-permute-start.5 = (bf16[528,256]{1,0:T(8,128)(2,1)S(1)}, bf16[528,256]{1,0:T(8,128)(2,1)S(1)}, u32[]{:S(2)}, u32[]{:S(2)}) collective-permute-start(bf16[528,256]{1,0:T(8,128)(2,1)S(1)} %get-tuple-element.62.sent), channel_id=1, source_target_pairs={{0,8},{8,16},{16,24},{24,0},{1,9},{9,17},{17,25},{25,1},{2,10},{10... | collective-permute-start | bytes 811016 | tf_op jit(solution)/shard_map/ppermute | solution.py:473
  8.8 9.0 %collective-permute-start.6 = (bf16[528,256]{1,0:T(8,128)(2,1)S(1)}, bf16[528,256]{1,0:T(8,128)(2,1)S(1)}, u32[]{:S(2)}, u32[]{:S(2)}) collective-permute-start(bf16[528,256]{1,0:T(8,128)(2,1)S(1)} %get-tuple-element.62.sent), channel_id=1, source_target_pairs={{0,16},{1,17},{2,18},{3,19},{4,20},{5,21},{6,22},{7,23}} | collective-permute-start | bytes 811016 | tf_op jit(solution)/shard_map/ppermute | solution.py:473
  9.6 10.9 %collective-permute-start.8 = (bf16[512,512]{1,0:T(8,128)(2,1)S(1)}, bf16[512,512]{1,0:T(8,128)(2,1)S(1)}, u32[]{:S(2)}, u32[]{:S(2)}) collective-permute-start(bf16[512,512]{1,0:T(8,128)(2,1)S(1)} %get-tuple-element.69), channel_id=1, source_target_pairs={{0,2},{1,5},{2,0},{3,7},{4,6},{5,1},{6,4},{7,3},{8,10},{9,13},{10,... | collective-permute-start | bytes 1572872 | tf_op jit(solution)/shard_map/ppermute | solution.py:429
  11.3 18.8 %collective-permute-start.10 = (bf16[512,512]{1,0:T(8,128)(2,1)S(1)}, bf16[512,512]{1,0:T(8,128)(2,1)S(1)}, u32[]{:S(2)}, u32[]{:S(2)}) collective-permute-start(bf16[512,512]{1,0:T(8,128)(2,1)S(1)} %get-tuple-element.79), channel_id=1, source_target_pairs={{0,2},{1,5},{2,0},{3,7},{4,6},{5,1},{6,4},{7,3},{8,10},{9,13},{10,... | collective-permute-start | bytes 1572872 | tf_op jit(solution)/shard_map/ppermute | solution.py:429
  17.8 11.1 %collective-permute-start.7 = (bf16[512,256]{1,0:T(8,128)(2,1)S(1)}, bf16[512,256]{1,0:T(8,128)(2,1)S(1)}, u32[]{:S(2)}, u32[]{:S(2)}) collective-permute-start(bf16[512,256]{1,0:T(8,128)(2,1)S(1)} %get-tuple-element.65), channel_id=1, source_target_pairs={{8,24},{24,8},{9,25},{25,9},{10,26},{26,10},{11,27},{27,11},{12,28... | collective-permute-start | bytes 786440 | tf_op jit(solution)/shard_map/ppermute | solution.py:473
  30.1 7.7 %collective-permute-start.11 = (bf16[512,512]{1,0:T(8,128)(2,1)S(1)}, bf16[512,512]{1,0:T(8,128)(2,1)S(1)}, u32[]{:S(2)}, u32[]{:S(2)}) collective-permute-start(bf16[512,512]{1,0:T(8,128)(2,1)S(1)} %collective-permute-done.8.mine_0), channel_id=1, source_target_pairs={{0,1},{1,0},{2,3},{3,2},{4,5},{5,4},{6,7},{7,6},{8,9},{9,8},{10,11... | collective-permute-start | bytes 1572872 | tf_op jit(solution)/shard_map/ppermute | solution.py:35
  30.1 9.6 %collective-permute-start.12 = (bf16[512,512]{1,0:T(8,128)(2,1)S(1)}, bf16[512,512]{1,0:T(8,128)(2,1)S(1)}, u32[]{:S(2)}, u32[]{:S(2)}) collective-permute-start(bf16[512,512]{1,0:T(8,128)(2,1)S(1)} %collective-permute-done.10.mine_1), channel_id=1, source_target_pairs={{0,1},{1,0},{2,3},{3,2},{4,5},{5,4},{6,7},{7,6},{8,9},{9,8},{10,11... | collective-permute-start | bytes 1572872 | tf_op jit(solution)/shard_map/ppermute | solution.py:35
  30.6 9.4 %collective-permute-start.17 = (bf16[256,512]{1,0:T(8,128)(2,1)S(1)}, bf16[256,512]{1,0:T(8,128)(2,1)S(1)}, u32[]{:S(2)}, u32[]{:S(2)}) collective-permute-start(bf16[256,512]{1,0:T(8,128)(2,1)S(1)} %get-tuple-element.77.refs_3_), channel_id=1, source_target_pairs={{0,2},{1,5},{2,0},{3,7},{4,6},{5,1},{6,4},{7,3},{8,10},{9,13},{10,... | collective-permute-start | bytes 786440 | tf_op jit(solution)/shard_map/ppermute | solution.py:429
  33.4 8.5 %collective-permute-start.16 = (bf16[256,512]{1,0:T(8,128)(2,1)S(1)}, bf16[256,512]{1,0:T(8,128)(2,1)S(1)}, u32[]{:S(2)}, u32[]{:S(2)}) collective-permute-start(bf16[256,512]{1,0:T(8,128)(2,1)S(1)} %get-tuple-element.76.refs_2_), channel_id=1, source_target_pairs={{0,4},{1,3},{2,6},{3,1},{4,0},{5,7},{6,2},{7,5},{8,12},{9,11},{10,... | collective-permute-start | bytes 786440 | tf_op jit(solution)/shard_map/ppermute | solution.py:429
  36.1 9.2 %collective-permute-start.14 = (bf16[256,512]{1,0:T(8,128)(2,1)S(1)}, bf16[256,512]{1,0:T(8,128)(2,1)S(1)}, u32[]{:S(2)}, u32[]{:S(2)}) collective-permute-start(bf16[256,512]{1,0:T(8,128)(2,1)S(1)} %get-tuple-element.75.refs_1_), channel_id=1, source_target_pairs={{0,2},{1,5},{2,0},{3,7},{4,6},{5,1},{6,4},{7,3},{8,10},{9,13},{10,... | collective-permute-start | bytes 786440 | tf_op jit(solution)/shard_map/ppermute | solution.py:429
  37.9 9.2 %collective-permute-start.9 = (bf16[256,512]{1,0:T(8,128)(2,1)S(1)}, bf16[256,512]{1,0:T(8,128)(2,1)S(1)}, u32[]{:S(2)}, u32[]{:S(2)}) collective-permute-start(bf16[256,512]{1,0:T(8,128)(2,1)S(1)} %get-tuple-element.74.refs_0_), channel_id=1, source_target_pairs={{0,4},{1,3},{2,6},{3,1},{4,0},{5,7},{6,2},{7,5},{8,12},{9,11},{10,... | collective-permute-start | bytes 786440 | tf_op jit(solution)/shard_map/ppermute | solution.py:429
  40.3 12.4 %collective-permute-start.19 = (bf16[256,512]{1,0:T(8,128)(2,1)S(1)}, bf16[256,512]{1,0:T(8,128)(2,1)S(1)}, u32[]{:S(2)}, u32[]{:S(2)}) collective-permute-start(bf16[256,512]{1,0:T(8,128)(2,1)S(1)} %give.7), channel_id=1, source_target_pairs={{0,4},{1,3},{2,6},{3,1},{4,0},{5,7},{6,2},{7,5},{8,12},{9,11},{10,... | collective-permute-start | bytes 786440 | tf_op jit(solution)/shard_map/ppermute | solution.py:429
  42.2 10.5 %collective-permute-start.18 = (bf16[256,512]{1,0:T(8,128)(2,1)S(1)}, bf16[256,512]{1,0:T(8,128)(2,1)S(1)}, u32[]{:S(2)}, u32[]{:S(2)}) collective-permute-start(bf16[256,512]{1,0:T(8,128)(2,1)S(1)} %give.6), channel_id=1, source_target_pairs={{0,2},{1,5},{2,0},{3,7},{4,6},{5,1},{6,4},{7,3},{8,10},{9,13},{10,... | collective-permute-start | bytes 786440 | tf_op jit(solution)/shard_map/ppermute | solution.py:429
  45.6 11.0 %collective-permute-start.15 = (bf16[256,512]{1,0:T(8,128)(2,1)S(1)}, bf16[256,512]{1,0:T(8,128)(2,1)S(1)}, u32[]{:S(2)}, u32[]{:S(2)}) collective-permute-start(bf16[256,512]{1,0:T(8,128)(2,1)S(1)} %give.5), channel_id=1, source_target_pairs={{0,4},{1,3},{2,6},{3,1},{4,0},{5,7},{6,2},{7,5},{8,12},{9,11},{10,... | collective-permute-start | bytes 786440 | tf_op jit(solution)/shard_map/ppermute | solution.py:429
  47.4 9.3 %collective-permute-start.13 = (bf16[256,512]{1,0:T(8,128)(2,1)S(1)}, bf16[256,512]{1,0:T(8,128)(2,1)S(1)}, u32[]{:S(2)}, u32[]{:S(2)}) collective-permute-start(bf16[256,512]{1,0:T(8,128)(2,1)S(1)} %give.4), channel_id=1, source_target_pairs={{0,2},{1,5},{2,0},{3,7},{4,6},{5,1},{6,4},{7,3},{8,10},{9,13},{10,... | collective-permute-start | bytes 786440 | tf_op jit(solution)/shard_map/ppermute | solution.py:429

commit v25 on v24

--- a/solution.py
+++ b/solution.py
@@ -506,7 +506,7 @@
     )
     out_mine = [trade(block, 0) for block in for_partner]
 
-    held = after(decay, message, *early, out_mine[0])
+    held = after(decay, message, *early)
     for block in range(1, blocks):
         projected += query_gate(block, held)
 

time: 58.5 us -> 58.5 us (level)
  no operation moved by 1% of the time
where the time goes in v25:
time: 58.5 us; the launch traced here: 57.7 us
  Pallas kernels  24 us (41%)
  starting transfers between devices  17.4 us (30%)
  waiting for transfers between devices  15.9 us (27%)
    pallas_call x15, Pallas kernels, kernel_call(): pl.pallas_call(kernel, in_specs=[pl.BlockSpec(memory_space=pltpu.VMEM)] *...  14.8 us
    ppermute x10, starting transfers between devices, trade(): return lax.ppermute(value, ('tp', 'fsdp'), partners[role])  12.3 us
    ppermute x10, waiting for transfers between devices, trade(): return lax.ppermute(value, ('tp', 'fsdp'), partners[role])  8.55 us
    pallas_call x2, Pallas kernels, loading_call(): pl.pallas_call(kernel, in_specs=[pl.BlockSpec(memory_space=pltpu.HBM)] *...  7.53 us
    ppermute x3, waiting for transfers between devices, exchange(): return lax.ppermute(message, 'ctx', pairs)  7.34 us
    ppermute x3, starting transfers between devices, exchange(): return lax.ppermute(message, 'ctx', pairs)  3.37 us
    ppermute x7, starting transfers between devices, swap(): lax.ppermute(value, axis, [(place, place ^ mask) for place in range(size)])  1.71 us
    pallas_call x2, Pallas kernels, on_device(): pl.pallas_call(functools.partial(finish_kernel, part_order), in_specs=[pl...  1.7 us
  transfers between devices with their start and end apart: 20, of which 7 were waited for; matrix products, arithmetic and copies ran while one was open for 0% of the time, Pallas kernels for 40%

profile of v25, /device:TPU:24, one launch (start us, length us, event | category | flops | bytes accessed | tf_op | source)
XLA Modules:
  0.0 57.7 jit_solution(4870871290009098029)
XLA Ops:
  0.0 0.5 collective-permute-start.2
  0.5 4.3 %key_value_own.1 = (bf16[1024,1024]{1,0:T(8,128)(2,1)S(1)}, bf16[1024,1024]{1,0:T(8,128)(2,1)S(1)}, f32[1024,512]{1,0:T(8,128)S(1)}, f32[1024,512]{1,0:T(8,128)S...) custom-call(bf16[1024,2048]{1,0:T(8,128)(2,1)} %bitcast.4, ...), custom_call_target="tpu_custom_call" | custom-call | flops 1 | bytes 1 | tf_op jit(solution)/shard_map/key_value_own/pallas_call | solution.py:56
  4.9 3.2 %key_value.1 = (bf16[1024,512]{1,0:T(8,128)(2,1)S(1)}, bf16[1024,512]{1,0:T(8,128)(2,1)S(1)}, bf16[1024,512]{1,0:T(8,128)(2,1)S(1)}, bf16[1024,512]{1,0:T(8,128)...) custom-call(bf16[1024,512]{1,0:T(8,128)(2,1)} %wq_far.1, ...), custom_call_target="tpu_custom_call" | custom-call | flops 1 | bytes 1 | tf_op jit(solution)/shard_map/key_value/pallas_call | solution.py:56
  8.2 0.5 collective-permute-start.3
  8.8 0.7 %collective-permute-start.6 = (bf16[528,256]{1,0:T(8,128)(2,1)S(1)}, bf16[528,256]{1,0:T(8,128)(2,1)S(1)}, u32[]{:S(2)}, u32[]{:S(2)}) collective-permute-start(bf16[528,256]{1,0:T(8,128)(2,1)S(1)} %get-tuple-element.62.sent), channel_id=1, source_target_pairs={{0,16},{1,17},{2,18},{3,19},{4,20},{5,21},{6,22},{7,23}} | collective-permute-start | bytes 811016 | tf_op jit(solution)/shard_map/ppermute | solution.py:473
  9.6 1.8 %collective-permute-start.10 = (bf16[512,512]{1,0:T(8,128)(2,1)S(1)}, bf16[512,512]{1,0:T(8,128)(2,1)S(1)}, u32[]{:S(2)}, u32[]{:S(2)}) collective-permute-start(bf16[512,512]{1,0:T(8,128)(2,1)S(1)} %get-tuple-element.79), channel_id=1, source_target_pairs={{0,2},{1,5},{2,0},{3,7},{4,6},{5,1},{6,4},{7,3},{8,10},{9,13},{10,... | collective-permute-start | bytes 1572872 | tf_op jit(solution)/shard_map/ppermute | solution.py:429
  11.3 1.1 %collective-permute-start.9 = (bf16[512,512]{1,0:T(8,128)(2,1)S(1)}, bf16[512,512]{1,0:T(8,128)(2,1)S(1)}, u32[]{:S(2)}, u32[]{:S(2)}) collective-permute-start(bf16[512,512]{1,0:T(8,128)(2,1)S(1)} %get-tuple-element.78), channel_id=1, source_target_pairs={{0,2},{1,5},{2,0},{3,7},{4,6},{5,1},{6,4},{7,3},{8,10},{9,13},{10,... | collective-permute-start | bytes 1572872 | tf_op jit(solution)/shard_map/ppermute | solution.py:429
  12.5 3.1 %query_gate.2 = (bf16[512,512]{1,0:T(8,128)(2,1)S(1)}, f32[512,512]{1,0:T(8,128)S(1)}, f32[512,512]{1,0:T(8,128)S(1)}) custom-call(bf16[1024,1024]{1,0:T(8,128)(2,1)S(1)} %get-tuple-element.55.x_own, bf16[1024,1024]{1,0:T(8,128)(2,1)S(1)} %get-tuple-element.48.x.x_other, bf16[1024,512]{1,0:T(8,128)(2,1)S(1)} %get-tuple-element.56.wq, ...), custom_call_target="tpu_custom_call" | custom-call | flops 1 | bytes 1 | tf_op jit(solution)/shard_map/query_gate/pallas_call | solution.py:40
  15.6 2.0 %collective-permute-done.5.refs_0_ = bf16[528,256]{1,0:T(8,128)(2,1)S(1)} collective-permute-done((bf16[528,256]{1,0:T(8,128)(2,1)S(1)}, bf16[528,256]{1,0:T(8,128)(2,1)S(1)}, u32[]{:S(2)}, u32[]{:S(2)}) %collective-permute-start.5) | collective-permute-done | bytes 270368 | tf_op jit(solution)/shard_map/ppermute | solution.py:473
  17.8 2.7 %collective-permute-start.7 = (bf16[512,256]{1,0:T(8,128)(2,1)S(1)}, bf16[512,256]{1,0:T(8,128)(2,1)S(1)}, u32[]{:S(2)}, u32[]{:S(2)}) collective-permute-start(bf16[512,256]{1,0:T(8,128)(2,1)S(1)} %get-tuple-element.65), channel_id=1, source_target_pairs={{8,24},{24,8},{9,25},{25,9},{10,26},{26,10},{11,27},{27,11},{12,28... | collective-permute-start | bytes 786440 | tf_op jit(solution)/shard_map/ppermute | solution.py:473
  20.5 3.1 %query_gate.3 = (bf16[512,512]{1,0:T(8,128)(2,1)S(1)}, f32[512,512]{1,0:T(8,128)S(1)}, f32[512,512]{1,0:T(8,128)S(1)}) custom-call(bf16[1024,1024]{1,0:T(8,128)(2,1)S(1)} %get-tuple-element.55.x_own, bf16[1024,1024]{1,0:T(8,128)(2,1)S(1)} %get-tuple-element.48.x.x_other, bf16[1024,512]{1,0:T(8,128)(2,1)S(1)} %get-tuple-element.56.wq, ...), custom_call_target="tpu_custom_call" | custom-call | flops 1 | bytes 1 | tf_op jit(solution)/shard_map/query_gate/pallas_call | solution.py:40
  23.6 5.3 %collective-permute-done.7.refs_0_ = bf16[512,256]{1,0:T(8,128)(2,1)S(1)} collective-permute-done((bf16[512,256]{1,0:T(8,128)(2,1)S(1)}, bf16[512,256]{1,0:T(8,128)(2,1)S(1)}, u32[]{:S(2)}, u32[]{:S(2)}) %collective-permute-start.7) | collective-permute-done | bytes 262176 | tf_op jit(solution)/shard_map/ppermute | solution.py:473
  28.9 1.2 %hidden.7 = (bf16[256,512]{1,0:T(8,128)(2,1)S(1)}, bf16[16,128]{1,0:T(8,128)(2,1)}) custom-call(f32[8,1024]{1,0:T(8,128)S(1)} %get-tuple-element.68.decay, bf16[2,512,256]{2,1,0:T(8,128)(2,1)S(1)} %get-tuple-element.53.before, f32[520,256]{1,0:T(8,128)S(1)} %get-tuple-element.63.entering, bf16[512,256]{1,0:T(8,128)(2,1)S(1)} %collective-permute-done.7.refs_0_, ...), custom_call_target="tpu_custom_call" | custom-call | flops 1 | bytes 1 | tf_op jit(solution)/shard_map/hidden/pallas_call | solution.py:40
  30.1 0.5 collective-permute-start.11
  30.6 1.5 %collective-permute-start.17 = (bf16[256,512]{1,0:T(8,128)(2,1)S(1)}, bf16[256,512]{1,0:T(8,128)(2,1)S(1)}, u32[]{:S(2)}, u32[]{:S(2)}) collective-permute-start(bf16[256,512]{1,0:T(8,128)(2,1)S(1)} %get-tuple-element.75.refs_3_), channel_id=1, source_target_pairs={{0,2},{1,5},{2,0},{3,7},{4,6},{5,1},{6,4},{7,3},{8,10},{9,13},{10,... | collective-permute-start | bytes 786440 | tf_op jit(solution)/shard_map/ppermute | solution.py:429
  32.1 1.2 %hidden.6 = (bf16[256,512]{1,0:T(8,128)(2,1)S(1)}, bf16[16,128]{1,0:T(8,128)(2,1)}) custom-call(f32[8,1024]{1,0:T(8,128)S(1)} %get-tuple-element.68.decay, bf16[2,512,256]{2,1,0:T(8,128)(2,1)S(1)} %get-tuple-element.53.before, f32[520,256]{1,0:T(8,128)S(1)} %get-tuple-element.63.entering, bf16[512,256]{1,0:T(8,128)(2,1)S(1)} %collective-permute-done.7.refs_0_, ...), custom_call_target="tpu_custom_call" | custom-call | flops 1 | bytes 1 | tf_op jit(solution)/shard_map/hidden/pallas_call | solution.py:40
  33.4 1.5 %collective-permute-start.16 = (bf16[256,512]{1,0:T(8,128)(2,1)S(1)}, bf16[256,512]{1,0:T(8,128)(2,1)S(1)}, u32[]{:S(2)}, u32[]{:S(2)}) collective-permute-start(bf16[256,512]{1,0:T(8,128)(2,1)S(1)} %get-tuple-element.74.refs_2_), channel_id=1, source_target_pairs={{0,4},{1,3},{2,6},{3,1},{4,0},{5,7},{6,2},{7,5},{8,12},{9,11},{10,... | collective-permute-start | bytes 786440 | tf_op jit(solution)/shard_map/ppermute | solution.py:429
  34.9 1.2 %hidden.5 = (bf16[256,512]{1,0:T(8,128)(2,1)S(1)}, bf16[16,128]{1,0:T(8,128)(2,1)}) custom-call(f32[8,1024]{1,0:T(8,128)S(1)} %get-tuple-element.68.decay, bf16[2,512,256]{2,1,0:T(8,128)(2,1)S(1)} %get-tuple-element.53.before, f32[520,256]{1,0:T(8,128)S(1)} %get-tuple-element.63.entering, bf16[512,256]{1,0:T(8,128)(2,1)S(1)} %collective-permute-done.7.refs_0_, ...), custom_call_target="tpu_custom_call" | custom-call | flops 1 | bytes 1 | tf_op jit(solution)/shard_map/hidden/pallas_call | solution.py:40
  36.1 0.5 collective-permute-start.14
  36.6 1.2 %hidden.4 = (bf16[256,512]{1,0:T(8,128)(2,1)S(1)}, bf16[16,128]{1,0:T(8,128)(2,1)}) custom-call(f32[8,1024]{1,0:T(8,128)S(1)} %get-tuple-element.68.decay, bf16[2,512,256]{2,1,0:T(8,128)(2,1)S(1)} %get-tuple-element.53.before, f32[520,256]{1,0:T(8,128)S(1)} %get-tuple-element.63.entering, bf16[512,256]{1,0:T(8,128)(2,1)S(1)} %collective-permute-done.7.refs_0_, ...), custom_call_target="tpu_custom_call" | custom-call | flops 1 | bytes 1 | tf_op jit(solution)/shard_map/hidden/pallas_call | solution.py:40
  37.9 0.5 collective-permute-start.8
  38.4 1.3 %own_products.1 = (f32[512,1024]{1,0:T(8,128)S(1)}, f32[512,1024]{1,0:T(8,128)S(1)}) custom-call(bf16[512,1024]{1,0:T(8,128)(2,1)S(1)} %get-tuple-element.77.own_first.first, bf16[512,1024]{1,0:T(8,128)(2,1)S(1)} %collective-permute-done.own_second.second, bf16[256,512]{1,0:T(8,128)(2,1)S(1)} %get-tuple-element.72.refs_0_, ...), custom_call_target="tpu_custom_call" | custom-call | flops 1 | bytes 1 | tf_op jit(solution)/shard_map/own_products/pallas_call | solution.py:40
  40.3 1.6 %collective-permute-start.19 = (bf16[256,512]{1,0:T(8,128)(2,1)S(1)}, bf16[256,512]{1,0:T(8,128)(2,1)S(1)}, u32[]{:S(2)}, u32[]{:S(2)}) collective-permute-start(bf16[256,512]{1,0:T(8,128)(2,1)S(1)} %give.7), channel_id=1, source_target_pairs={{0,4},{1,3},{2,6},{3,1},{4,0},{5,7},{6,2},{7,5},{8,12},{9,11},{10,... | collective-permute-start | bytes 786440 | tf_op jit(solution)/shard_map/ppermute | solution.py:429
  42.2 1.6 %collective-permute-start.18 = (bf16[256,512]{1,0:T(8,128)(2,1)S(1)}, bf16[256,512]{1,0:T(8,128)(2,1)S(1)}, u32[]{:S(2)}, u32[]{:S(2)}) collective-permute-start(bf16[256,512]{1,0:T(8,128)(2,1)S(1)} %give.6), channel_id=1, source_target_pairs={{0,2},{1,5},{2,0},{3,7},{4,6},{5,1},{6,4},{7,3},{8,10},{9,13},{10,... | collective-permute-start | bytes 786440 | tf_op jit(solution)/shard_map/ppermute | solution.py:429
  43.7 1.6 %collective-permute-done.14.far.refs_1_ = bf16[256,512]{1,0:T(8,128)(2,1)S(1)} collective-permute-done((bf16[256,512]{1,0:T(8,128)(2,1)S(1)}, bf16[256,512]{1,0:T(8,128)(2,1)S(1)}, u32[]{:S(2)}, u32[]{:S(2)}) %collective-permute-start.14) | collective-permute-done | bytes 262176 | tf_op jit(solution)/shard_map/ppermute | solution.py:429
  45.6 1.0 %collective-permute-start.15 = (bf16[256,512]{1,0:T(8,128)(2,1)S(1)}, bf16[256,512]{1,0:T(8,128)(2,1)S(1)}, u32[]{:S(2)}, u32[]{:S(2)}) collective-permute-start(bf16[256,512]{1,0:T(8,128)(2,1)S(1)} %give.5), channel_id=1, source_target_pairs={{0,4},{1,3},{2,6},{3,1},{4,0},{5,7},{6,2},{7,5},{8,12},{9,11},{10,... | collective-permute-start | bytes 786440 | tf_op jit(solution)/shard_map/ppermute | solution.py:429
  47.3 1.2 %collective-permute-start.13 = (bf16[256,512]{1,0:T(8,128)(2,1)S(1)}, bf16[256,512]{1,0:T(8,128)(2,1)S(1)}, u32[]{:S(2)}, u32[]{:S(2)}) collective-permute-start(bf16[256,512]{1,0:T(8,128)(2,1)S(1)} %give.4), channel_id=1, source_target_pairs={{0,2},{1,5},{2,0},{3,7},{4,6},{5,1},{6,4},{7,3},{8,10},{9,13},{10,... | collective-permute-start | bytes 786440 | tf_op jit(solution)/shard_map/ppermute | solution.py:429
  48.5 0.7 %keep.1 = (f32[512,512]{1,0:T(8,128)S(1)}, f32[512,512]{1,0:T(8,128)S(1)}) custom-call(bf16[256,512]{1,0:T(8,128)(2,1)S(1)} %collective-permute-done.8.far.refs_0_, bf16[256,512]{1,0:T(8,128)(2,1)S(1)} %collective-permute-done.14.far.refs_1_, bf16[256,512]{1,0:T(8,128)(2,1)S(1)} %collective-permute-done.16.refs_2_.far, ...), custom_call_target="tpu_custom_call" | custom-call | flops 1 | bytes 1 | tf_op jit(solution)/shard_map/keep/pallas_call | solution.py:40
  49.2 3.4 %collective-permute-done.19.refs_1_ = bf16[256,512]{1,0:T(8,128)(2,1)S(1)} collective-permute-done((bf16[256,512]{1,0:T(8,128)(2,1)S(1)}, bf16[256,512]{1,0:T(8,128)(2,1)S(1)}, u32[]{:S(2)}, u32[]{:S(2)}) %collective-permute-start.19) | collective-permute-done | bytes 262176 | tf_op jit(solution)/shard_map/ppermute | solution.py:429
  52.6 0.9 %finish.2.refs_4_ = bf16[1,1024,512]{2,1,0:T(8,128)(2,1)} custom-call(bf16[256,512]{1,0:T(8,128)(2,1)S(1)} %collective-permute-done.18.refs_0_, bf16[256,512]{1,0:T(8,128)(2,1)S(1)} %collective-permute-done.19.refs_1_, f32[512,512]{1,0:T(8,128)S(1)} %get-tuple-element.85.refs_2_, f32[512,512]{1,0:T(8,128)S(1)} %get-tuple-element.86.refs_3_), custom_call_target="tpu_custom_call" | custom-call | tf_op jit(solution)/shard_map/finish/pallas_call | solution.py:560
  53.5 3.1 %collective-permute-done.15.refs_1_ = bf16[256,512]{1,0:T(8,128)(2,1)S(1)} collective-permute-done((bf16[256,512]{1,0:T(8,128)(2,1)S(1)}, bf16[256,512]{1,0:T(8,128)(2,1)S(1)}, u32[]{:S(2)}, u32[]{:S(2)}) %collective-permute-start.15) | collective-permute-done | bytes 262176 | tf_op jit(solution)/shard_map/ppermute | solution.py:429
  56.7 0.9 %finish.3 = bf16[1,1024,512]{2,1,0:T(8,128)(2,1)} custom-call(bf16[256,512]{1,0:T(8,128)(2,1)S(1)} %collective-permute-done.13.refs_0_, bf16[256,512]{1,0:T(8,128)(2,1)S(1)} %collective-permute-done.15.refs_1_, f32[512,512]{1,0:T(8,128)S(1)} %get-tuple-element.85.refs_2_, f32[512,512]{1,0:T(8,128)S(1)} %get-tuple-element.86.refs_3_, ...), custom_call_target="tpu_custom_call", output_to_operand_aliasing={{}: (4, {})} | custom-call | tf_op jit(solution)/shard_map/finish/pallas_call | solution.py:560
  (27 shorter events, 2.3 us)
Async XLA Ops:
  0.0 4.9 %collective-permute-start.1 = (bf16[1024,512]{1,0:T(8,128)(2,1)}, bf16[1024,512]{1,0:T(8,128)(2,1)S(1)}, u32[]{:S(2)}, u32[]{:S(2)}) collective-permute-start(bf16[1024,512]{1,0:T(8,128)(2,1)} %wk_far.1), channel_id=1, source_target_pairs={{0,1},{1,0},{2,3},{3,2},{4,5},{5,4},{6,7},{7,6},{8,9},{9,8},{10,11... | collective-permute-start | bytes 3145736 | tf_op jit(solution)/shard_map/ppermute | solution.py:35
  0.0 4.9 %collective-permute-start.2 = (bf16[1024,512]{1,0:T(8,128)(2,1)}, bf16[1024,512]{1,0:T(8,128)(2,1)S(1)}, u32[]{:S(2)}, u32[]{:S(2)}) collective-permute-start(bf16[1024,512]{1,0:T(8,128)(2,1)} %wv_far.1), channel_id=1, source_target_pairs={{0,1},{1,0},{2,3},{3,2},{4,5},{5,4},{6,7},{7,6},{8,9},{9,8},{10,11... | collective-permute-start | bytes 3145736 | tf_op jit(solution)/shard_map/ppermute | solution.py:35
  4.8 4.6 %collective-permute-start = (bf16[512,1024]{1,0:T(8,128)(2,1)S(1)}, bf16[512,1024]{1,0:T(8,128)(2,1)S(1)}, u32[]{:S(2)}, u32[]{:S(2)}) collective-permute-start(bf16[512,1024]{1,0:T(8,128)(2,1)S(1)} %get-tuple-element.77.own_first.first), channel_id=1, source_target_pairs={{0,1},{1,0},{2,3},{3,2},{4,5},{5,4},{6,7},{7,6},{8,9},{9,8},{10,11... | collective-permute-start | bytes 3145736 | tf_op jit(solution)/shard_map/ppermute | solution.py:35
  8.2 3.2 %collective-permute-start.3 = (bf16[1024,512]{1,0:T(8,128)(2,1)S(1)}, bf16[1024,512]{1,0:T(8,128)(2,1)S(1)}, u32[]{:S(2)}, u32[]{:S(2)}) collective-permute-start(bf16[1024,512]{1,0:T(8,128)(2,1)S(1)} %get-tuple-element.56.wq), channel_id=1, source_target_pairs={{0,1},{1,0},{2,3},{3,2},{4,5},{5,4},{6,7},{7,6},{8,9},{9,8},{10,11... | collective-permute-start | bytes 3145736 | tf_op jit(solution)/shard_map/ppermute | solution.py:35
  8.7 3.8 %collective-permute-start.4 = (bf16[1024,512]{1,0:T(8,128)(2,1)S(1)}, bf16[1024,512]{1,0:T(8,128)(2,1)S(1)}, u32[]{:S(2)}, u32[]{:S(2)}) collective-permute-start(bf16[1024,512]{1,0:T(8,128)(2,1)S(1)} %get-tuple-element.57.wg), channel_id=1, source_target_pairs={{0,1},{1,0},{2,3},{3,2},{4,5},{5,4},{6,7},{7,6},{8,9},{9,8},{10,11... | collective-permute-start | bytes 3145736 | tf_op jit(solution)/shard_map/ppermute | solution.py:35
  8.8 8.8 %collective-permute-start.5 = (bf16[528,256]{1,0:T(8,128)(2,1)S(1)}, bf16[528,256]{1,0:T(8,128)(2,1)S(1)}, u32[]{:S(2)}, u32[]{:S(2)}) collective-permute-start(bf16[528,256]{1,0:T(8,128)(2,1)S(1)} %get-tuple-element.62.sent), channel_id=1, source_target_pairs={{0,8},{8,16},{16,24},{24,0},{1,9},{9,17},{17,25},{25,1},{2,10},{10... | collective-permute-start | bytes 811016 | tf_op jit(solution)/shard_map/ppermute | solution.py:473
  8.8 9.0 %collective-permute-start.6 = (bf16[528,256]{1,0:T(8,128)(2,1)S(1)}, bf16[528,256]{1,0:T(8,128)(2,1)S(1)}, u32[]{:S(2)}, u32[]{:S(2)}) collective-permute-start(bf16[528,256]{1,0:T(8,128)(2,1)S(1)} %get-tuple-element.62.sent), channel_id=1, source_target_pairs={{0,16},{1,17},{2,18},{3,19},{4,20},{5,21},{6,22},{7,23}} | collective-permute-start | bytes 811016 | tf_op jit(solution)/shard_map/ppermute | solution.py:473
  9.6 20.6 %collective-permute-start.10 = (bf16[512,512]{1,0:T(8,128)(2,1)S(1)}, bf16[512,512]{1,0:T(8,128)(2,1)S(1)}, u32[]{:S(2)}, u32[]{:S(2)}) collective-permute-start(bf16[512,512]{1,0:T(8,128)(2,1)S(1)} %get-tuple-element.79), channel_id=1, source_target_pairs={{0,2},{1,5},{2,0},{3,7},{4,6},{5,1},{6,4},{7,3},{8,10},{9,13},{10,... | collective-permute-start | bytes 1572872 | tf_op jit(solution)/shard_map/ppermute | solution.py:429
  11.3 18.8 %collective-permute-start.9 = (bf16[512,512]{1,0:T(8,128)(2,1)S(1)}, bf16[512,512]{1,0:T(8,128)(2,1)S(1)}, u32[]{:S(2)}, u32[]{:S(2)}) collective-permute-start(bf16[512,512]{1,0:T(8,128)(2,1)S(1)} %get-tuple-element.78), channel_id=1, source_target_pairs={{0,2},{1,5},{2,0},{3,7},{4,6},{5,1},{6,4},{7,3},{8,10},{9,13},{10,... | collective-permute-start | bytes 1572872 | tf_op jit(solution)/shard_map/ppermute | solution.py:429
  17.8 11.1 %collective-permute-start.7 = (bf16[512,256]{1,0:T(8,128)(2,1)S(1)}, bf16[512,256]{1,0:T(8,128)(2,1)S(1)}, u32[]{:S(2)}, u32[]{:S(2)}) collective-permute-start(bf16[512,256]{1,0:T(8,128)(2,1)S(1)} %get-tuple-element.65), channel_id=1, source_target_pairs={{8,24},{24,8},{9,25},{25,9},{10,26},{26,10},{11,27},{27,11},{12,28... | collective-permute-start | bytes 786440 | tf_op jit(solution)/shard_map/ppermute | solution.py:473
  30.1 7.7 %collective-permute-start.12 = (bf16[512,512]{1,0:T(8,128)(2,1)S(1)}, bf16[512,512]{1,0:T(8,128)(2,1)S(1)}, u32[]{:S(2)}, u32[]{:S(2)}) collective-permute-start(bf16[512,512]{1,0:T(8,128)(2,1)S(1)} %collective-permute-done.10.mine_1), channel_id=1, source_target_pairs={{0,1},{1,0},{2,3},{3,2},{4,5},{5,4},{6,7},{7,6},{8,9},{9,8},{10,11... | collective-permute-start | bytes 1572872 | tf_op jit(solution)/shard_map/ppermute | solution.py:35
  30.1 9.6 %collective-permute-start.11 = (bf16[512,512]{1,0:T(8,128)(2,1)S(1)}, bf16[512,512]{1,0:T(8,128)(2,1)S(1)}, u32[]{:S(2)}, u32[]{:S(2)}) collective-permute-start(bf16[512,512]{1,0:T(8,128)(2,1)S(1)} %collective-permute-done.9.mine_0), channel_id=1, source_target_pairs={{0,1},{1,0},{2,3},{3,2},{4,5},{5,4},{6,7},{7,6},{8,9},{9,8},{10,11... | collective-permute-start | bytes 1572872 | tf_op jit(solution)/shard_map/ppermute | solution.py:35
  30.6 9.3 %collective-permute-start.17 = (bf16[256,512]{1,0:T(8,128)(2,1)S(1)}, bf16[256,512]{1,0:T(8,128)(2,1)S(1)}, u32[]{:S(2)}, u32[]{:S(2)}) collective-permute-start(bf16[256,512]{1,0:T(8,128)(2,1)S(1)} %get-tuple-element.75.refs_3_), channel_id=1, source_target_pairs={{0,2},{1,5},{2,0},{3,7},{4,6},{5,1},{6,4},{7,3},{8,10},{9,13},{10,... | collective-permute-start | bytes 786440 | tf_op jit(solution)/shard_map/ppermute | solution.py:429
  33.4 8.5 %collective-permute-start.16 = (bf16[256,512]{1,0:T(8,128)(2,1)S(1)}, bf16[256,512]{1,0:T(8,128)(2,1)S(1)}, u32[]{:S(2)}, u32[]{:S(2)}) collective-permute-start(bf16[256,512]{1,0:T(8,128)(2,1)S(1)} %get-tuple-element.74.refs_2_), channel_id=1, source_target_pairs={{0,4},{1,3},{2,6},{3,1},{4,0},{5,7},{6,2},{7,5},{8,12},{9,11},{10,... | collective-permute-start | bytes 786440 | tf_op jit(solution)/shard_map/ppermute | solution.py:429
  36.1 9.2 %collective-permute-start.14 = (bf16[256,512]{1,0:T(8,128)(2,1)S(1)}, bf16[256,512]{1,0:T(8,128)(2,1)S(1)}, u32[]{:S(2)}, u32[]{:S(2)}) collective-permute-start(bf16[256,512]{1,0:T(8,128)(2,1)S(1)} %get-tuple-element.73.refs_1_), channel_id=1, source_target_pairs={{0,2},{1,5},{2,0},{3,7},{4,6},{5,1},{6,4},{7,3},{8,10},{9,13},{10,... | collective-permute-start | bytes 786440 | tf_op jit(solution)/shard_map/ppermute | solution.py:429
  37.9 9.2 %collective-permute-start.8 = (bf16[256,512]{1,0:T(8,128)(2,1)S(1)}, bf16[256,512]{1,0:T(8,128)(2,1)S(1)}, u32[]{:S(2)}, u32[]{:S(2)}) collective-permute-start(bf16[256,512]{1,0:T(8,128)(2,1)S(1)} %get-tuple-element.72.refs_0_), channel_id=1, source_target_pairs={{0,4},{1,3},{2,6},{3,1},{4,0},{5,7},{6,2},{7,5},{8,12},{9,11},{10,... | collective-permute-start | bytes 786440 | tf_op jit(solution)/shard_map/ppermute | solution.py:429
  40.3 12.4 %collective-permute-start.19 = (bf16[256,512]{1,0:T(8,128)(2,1)S(1)}, bf16[256,512]{1,0:T(8,128)(2,1)S(1)}, u32[]{:S(2)}, u32[]{:S(2)}) collective-permute-start(bf16[256,512]{1,0:T(8,128)(2,1)S(1)} %give.7), channel_id=1, source_target_pairs={{0,4},{1,3},{2,6},{3,1},{4,0},{5,7},{6,2},{7,5},{8,12},{9,11},{10,... | collective-permute-start | bytes 786440 | tf_op jit(solution)/shard_map/ppermute | solution.py:429
  42.2 10.5 %collective-permute-start.18 = (bf16[256,512]{1,0:T(8,128)(2,1)S(1)}, bf16[256,512]{1,0:T(8,128)(2,1)S(1)}, u32[]{:S(2)}, u32[]{:S(2)}) collective-permute-start(bf16[256,512]{1,0:T(8,128)(2,1)S(1)} %give.6), channel_id=1, source_target_pairs={{0,2},{1,5},{2,0},{3,7},{4,6},{5,1},{6,4},{7,3},{8,10},{9,13},{10,... | collective-permute-start | bytes 786440 | tf_op jit(solution)/shard_map/ppermute | solution.py:429
  45.6 11.0 %collective-permute-start.15 = (bf16[256,512]{1,0:T(8,128)(2,1)S(1)}, bf16[256,512]{1,0:T(8,128)(2,1)S(1)}, u32[]{:S(2)}, u32[]{:S(2)}) collective-permute-start(bf16[256,512]{1,0:T(8,128)(2,1)S(1)} %give.5), channel_id=1, source_target_pairs={{0,4},{1,3},{2,6},{3,1},{4,0},{5,7},{6,2},{7,5},{8,12},{9,11},{10,... | collective-permute-start | bytes 786440 | tf_op jit(solution)/shard_map/ppermute | solution.py:429
  47.3 9.3 %collective-permute-start.13 = (bf16[256,512]{1,0:T(8,128)(2,1)S(1)}, bf16[256,512]{1,0:T(8,128)(2,1)S(1)}, u32[]{:S(2)}, u32[]{:S(2)}) collective-permute-start(bf16[256,512]{1,0:T(8,128)(2,1)S(1)} %give.4), channel_id=1, source_target_pairs={{0,2},{1,5},{2,0},{3,7},{4,6},{5,1},{6,4},{7,3},{8,10},{9,13},{10,... | collective-permute-start | bytes 786440 | tf_op jit(solution)/shard_map/ppermute | solution.py:429
